TPU v7x, 32 devices: a whole 2x2x4 slice. The times are simulated.
32 devices in a mesh: groups: 2 (over x), gx: 8 (over z, y), gy: 2 (over core).
Axes of the slice: x: 2, y: 2, z: 4, core: 2. Of those that a mesh axis runs over, the one named last changes fastest.
Arguments:
- frames: bfloat16 [16, 384, 1280], P(('groups', 'gx')), parts along dimension 0, may hold values from -6 to 6
- out_grad: bfloat16 [16, 384, 1280], P(('groups', 'gx')), parts along dimension 0, may hold values from -6 to 6
- ln_gain: float32 [1280], replicated, may hold values from 0.1 to 1.9
- w_up: bfloat16 [1280, 2560], P('gx', 'gy'), may hold values from -0.15625 to 0.15625
- w_down: bfloat16 [1280, 2560], P('gx', 'gy'), may hold values from -0.15625 to 0.15625
- lengths: int32 [16], P('groups'), parts along dimension 0, may hold values from 1 to 384, 1024 in all
Outputs:
- input_grad: bfloat16 [16, 384, 1280], P(('groups', 'gx'), None, 'gy'), parts along dimension 0
- up_grad: float32 [2560, 2560], P(('groups', 'gx'), 'gy'), parts along dimension 0
There are 2 independent parts, one for each index of `groups`. A program takes and returns all parts, laid end to end along the dimension named above; an argument that names none is the same for every part. Nothing has to cross between parts.
Inputs may be any that keep to these rules, and one draw needn't show every extreme that they name: The lengths of one replica sum to 1024, and the largest equals 384.
All inputs are finite; a program needn't handle non-finite values.
Results may differ from a plain program's by a relative error of at most 0.0055.
Values may be sent and summed in bfloat16 or wider, within the bound.
No kernel may reach another device: no remote copies, remote signals or barrier semaphores. Data moves between devices by JAX's collectives and lax.ppermute only.
A program may use at most 64 MiB of HBM per device.

v0:
```python
import jax
import jax.numpy as jnp
from jax import lax
from jax.sharding import PartitionSpec as P


def norm_rows(rows, gain):
    values = rows.astype(jnp.float32)
    centre = jnp.mean(values, axis=-1, keepdims=True)
    shifted = values - centre
    variance = jnp.mean(shifted * shifted, axis=-1, keepdims=True)
    inv_std = lax.rsqrt(variance + 1e-05)
    centred = shifted * inv_std
    normed = (centred * gain).astype(jnp.bfloat16)
    return (centred, inv_std, normed)


def gelu_slope(values):
    return (
        0.5 * (1.0 + lax.erf(values * 0.7071067811865476))
        + values * jnp.exp(-0.5 * values * values) * 0.3989422804014327
    )


def row_product(left, right):
    return lax.dot_general(
        left, right, (((0,), (0,)), ((), ())), preferred_element_type=jnp.float32
    )


def shards(frames, out_grad, ln_gain, w_up, w_down, lengths):
    peers = lax.axis_size("gx")
    own_index = lax.axis_index("gx")
    frame_len = frames.shape[1]
    model_width = frames.shape[2]
    slot_rows = frame_len // peers
    owned = frame_len // 3 + peers
    my_length = lax.dynamic_index_in_dim(lengths, own_index, 0, keepdims=False)
    keep_rows = (jnp.arange(frame_len, dtype=jnp.int32) < my_length)[:, None]
    send_frames = jnp.where(keep_rows, frames[0], 0).reshape(slot_rows, peers, model_width)
    send_grads = jnp.where(keep_rows, out_grad[0], 0).reshape(slot_rows, peers, model_width)
    recv_frames, recv_grads = (
        lax.all_to_all(send_frames, "gx", split_axis=1, concat_axis=1, tiled=True),
        lax.all_to_all(send_grads, "gx", split_axis=1, concat_axis=1, tiled=True),
    )
    position = jnp.arange(slot_rows, dtype=jnp.int32)[:, None] * peers + own_index
    valid_slots = (position < lengths[None, :]).reshape(-1).astype(jnp.int32)
    running = jnp.cumsum(valid_slots)
    row_ids = jnp.arange(owned, dtype=jnp.int32)
    pick_rows = jnp.sum((running[None, :] <= row_ids[:, None]).astype(jnp.int32), axis=1)
    pick_rows = jnp.minimum(pick_rows, peers * slot_rows - 1)
    live_rows = (row_ids < running[-1])[:, None]
    own_frames = jnp.where(
        live_rows, jnp.take(recv_frames.reshape(-1, model_width), pick_rows, axis=0), 0
    )
    own_grads = jnp.where(
        live_rows, jnp.take(recv_grads.reshape(-1, model_width), pick_rows, axis=0), 0
    )
    full_up, full_down = (
        lax.all_gather(w_up, "gx", axis=0, tiled=True),
        lax.all_gather(w_down, "gx", axis=0, tiled=True),
    )
    centred, inv_std, normed = norm_rows(own_frames, ln_gain)
    pre_act = jnp.dot(normed, full_up, preferred_element_type=jnp.float32)
    d_act = jnp.dot(own_grads, full_down, preferred_element_type=jnp.float32)
    d_pre = (d_act * gelu_slope(pre_act)).astype(jnp.bfloat16)
    partial_value = lax.dot_general(
        d_pre, full_up, (((1,), (1,)), ((), ())), preferred_element_type=jnp.float32
    )
    up_grad = lax.psum_scatter(row_product(normed, d_pre), "gx", scatter_dimension=0, tiled=True)
    half_width = model_width // lax.axis_size("gy")
    offset_half = lax.axis_index("gy") * half_width
    d_norm = lax.psum(partial_value, "gy")
    scaled = d_norm * ln_gain
    first_mean = jnp.mean(scaled, axis=-1, keepdims=True)
    second_mean = jnp.mean(scaled * centred, axis=-1, keepdims=True)
    input_full = own_grads.astype(jnp.float32) + inv_std * (
        scaled - first_mean - centred * second_mean
    )
    input_rows = lax.dynamic_slice_in_dim(input_full, offset_half, half_width, 1).astype(
        jnp.bfloat16
    )
    back_index = jnp.clip(running - 1, 0, owned - 1)
    send_back = jnp.where(valid_slots[:, None] > 0, jnp.take(input_rows, back_index, axis=0), 0)
    send_back = send_back.reshape(slot_rows, peers, half_width)
    arrived = lax.all_to_all(send_back, "gx", split_axis=1, concat_axis=1, tiled=True)
    mine = arrived.reshape(frame_len, half_width)
    return (mine[None], up_grad)


def solution(mesh):
    placed = (
        P(("groups", "gx"), None, None),
        P(("groups", "gx"), None, None),
        P(),
        P("gx", "gy"),
        P("gx", "gy"),
        P("groups"),
    )
    return jax.shard_map(
        shards,
        mesh=mesh,
        in_specs=placed,
        out_specs=(P(("groups", "gx"), None, "gy"), P(("groups", "gx"), "gy")),
        check_vma=False,
    )
```

profile of v0, /device:TPU:0, one launch (start us, length us, event | category | flops | bytes accessed | tf_op | source)
XLA Modules:
  0.0 340.3 jit_solution(3063255427212198251)
XLA Ops:
  7.9 0.7 all-gather.3.cloned.1.call-update
  8.7 1.2 dynamic_slice.7
  10.6 1.7 bitcast_select_fusion.1
  12.3 1.1 copy.32
  13.4 7.4 %all-to-all-start.1 = ((bf16[48,8,1280]{2,0,1:T(8,128)(2,1)}), bf16[48,8,1280]{2,0,1:T(8,128)(2,1)S(1)}, u32[]{:S(2)}, u32[]{:S(2)}) async-start(bf16[48,8,1280]{2,0,1:T(8,128)(2,1)} %copy.32), calls=%async_computation.1 | async-start | bytes 1966080 | tf_op jit(solution)/shard_map/all_to_all | solution.py:43
  20.8 1.1 copy.30
  22.0 36.3 %all-to-all-done.1 = bf16[48,8,1280]{2,0,1:T(8,128)(2,1)S(1)} async-done(((bf16[48,8,1280]{2,0,1:T(8,128)(2,1)}), bf16[48,8,1280]{2,0,1:T(8,128)(2,1)S(1)}, u32[]{:S(2)}, u32[]{:S(2)}) %all-to-all-start.1) | async-done | bytes 983072 | tf_op jit(solution)/shard_map/all_to_all | solution.py:43
  58.3 3.6 %all-to-all-start = ((bf16[48,8,1280]{2,0,1:T(8,128)(2,1)}), bf16[48,8,1280]{2,0,1:T(8,128)(2,1)S(1)}, u32[]{:S(2)}, u32[]{:S(2)}) async-start(bf16[48,8,1280]{2,0,1:T(8,128)(2,1)} %copy.30), calls=%async_computation | async-start | bytes 1966080 | tf_op jit(solution)/shard_map/all_to_all | solution.py:44
  64.6 0.9 gather_fusion.2
  65.5 43.6 %all-to-all-done = bf16[48,8,1280]{2,0,1:T(8,128)(2,1)S(1)} async-done(((bf16[48,8,1280]{2,0,1:T(8,128)(2,1)}), bf16[48,8,1280]{2,0,1:T(8,128)(2,1)S(1)}, u32[]{:S(2)}, u32[]{:S(2)}) %all-to-all-start) | async-done | bytes 983072 | tf_op jit(solution)/shard_map/all_to_all | solution.py:44
  109.4 0.9 gather_fusion.1
  110.9 0.9 select_select_fusion.1
  111.7 3.5 %fusion.14 = f32[136,1280]{1,0:T(8,128)} fusion(bf16[1280,1280]{1,0:T(8,128)(2,1)} %all-gather.5.cloned.1.call-done, f32[1280]{0:T(1024)S(1)} %copy-done.5, bf16[136,1280]{1,0:T(8,128)(2,1)S(1)} %get-tuple-element.7, f32[136]{0:T(256)S(1)} %add_rsqrt_fusion, f32[136]{0:T(256)S(1)} %broadcast_multiply_fusion.3), kind=kOutput, calls=%fused_computation.36 | convolution fusion | flops 446515200 | bytes 4327488 | tf_op jit(solution)/shard_map/dot_general | solution.py:64
  115.2 58.1 %all-gather.3.cloned.1.call-done = bf16[1280,1280]{1,0:T(8,128)(2,1)} async-done(((bf16[160,1280]{1,0:T(8,128)(2,1)}), bf16[1280,1280]{1,0:T(8,128)(2,1)}) %all-gather.3.cloned.1.call-update) | async-done | bytes 3276816 | tf_op jit(solution)/shard_map/all_gather | solution.py:61
  173.3 2.9 fusion
  176.3 0.7 copy-done.3
  177.0 2.1 fusion.19
  179.1 5.1 %fusion.13 = f32[1280,1280]{1,0:T(8,128)} fusion(bf16[136,1280]{1,0:T(8,128)(2,1)} %copy-done.3, f32[1280]{0:T(1024)S(1)} %copy-done.5, bf16[136,1280]{1,0:T(8,128)(2,1)} %copy-done.1, f32[136]{0:T(256)S(1)} %add_rsqrt_fusion, f32[136]{0:T(256)S(1)} %broadcast_multiply_fusion.3), kind=kOutput, calls=%fused_computation.35 | convolution fusion | flops 446515200 | bytes 7256128 | tf_op jit(solution)/shard_map/dot_general | solution.py:26
  184.6 12.2 %all-reduce.2.cloned.1.call-done = f32[136,1280]{1,0:T(8,128)} async-done(((f32[136,1280]{1,0:T(8,128)}), f32[136,1280]{1,0:T(8,128)}) %all-reduce.2.cloned.1.call-update) | async-done | bytes 696336 | tf_op jit(solution)/shard_map/psum | solution.py:73
  196.8 1.4 fusion.18
  198.4 2.2 gather_fusion
  200.8 30.6 %all_to_all.15 = bf16[48,8,640]{2,0,1:T(8,128)(2,1)S(1)} all-to-all(bf16[48,8,640]{2,0,1:T(8,128)(2,1)S(1)} %fusion.8), channel_id=1, replica_groups=mesh['groups'=2,'gx'=8,'gy'=2] {'gx'}, dimensions={1} | all-to-all | bytes 983040 | tf_op jit(solution)/shard_map/all_to_all | solution.py:86
  231.5 0.9 copy.46
  232.3 101.4 %reduce-scatter.2.cloned.1.call-done = f32[160,1280]{1,0:T(8,128)} async-done(((f32[1280,1280]{1,0:T(8,128)}), f32[160,1280]{1,0:T(8,128)}) %reduce-scatter.2.cloned.1.call-update) | async-done | bytes 819216 | tf_op jit(solution)/shard_map/reduce_scatter | solution.py:70
  (56 shorter events, 5.7 us)
Async XLA Ops:
  7.2 104.6 %all-gather.5.cloned.1.call-start = ((), (), s32[]{:S(2)}) async-start(), calls=%async_computation.5 | async-start | bytes 3686400 | tf_op jit(solution)/shard_map/all_gather | solution.py:60
  7.9 165.4 %all-gather.3.cloned.1.call-start = ((), (), s32[]{:S(2)}) async-start(), calls=%async_computation.4 | async-start | bytes 3686400 | tf_op jit(solution)/shard_map/all_gather | solution.py:61
  13.4 48.8 %copy-start.6 = (s32[8]{0:T(128)S(1)}, s32[8]{0:T(128)}, u32[]{:S(2)}) copy-start(s32[8]{0:T(128)} %param.13) | copy-start | bytes 100
  13.4 44.9 %all-to-all-start.1 = ((bf16[48,8,1280]{2,0,1:T(8,128)(2,1)}), bf16[48,8,1280]{2,0,1:T(8,128)(2,1)S(1)}, u32[]{:S(2)}, u32[]{:S(2)}) async-start(bf16[48,8,1280]{2,0,1:T(8,128)(2,1)} %copy.32), calls=%async_computation.1 | async-start | bytes 1966080 | tf_op jit(solution)/shard_map/all_to_all | solution.py:43
  58.3 50.8 %all-to-all-start = ((bf16[48,8,1280]{2,0,1:T(8,128)(2,1)}), bf16[48,8,1280]{2,0,1:T(8,128)(2,1)S(1)}, u32[]{:S(2)}, u32[]{:S(2)}) async-start(bf16[48,8,1280]{2,0,1:T(8,128)(2,1)} %copy.30), calls=%async_computation | async-start | bytes 1966080 | tf_op jit(solution)/shard_map/all_to_all | solution.py:44
  61.9 134.9 %all-reduce.2.cloned.1.call-start = ((), (), s32[]{:S(2)}) async-start(), calls=%async_computation.6 | async-start | bytes 1392640 | tf_op jit(solution)/shard_map/psum | solution.py:73
  65.5 46.2 %copy-start.5 = (f32[1280]{0:T(1024)S(1)}, f32[1280]{0:T(1024)}, u32[]{:S(2)}) copy-start(f32[1280]{0:T(1024)} %param.10) | copy-start | bytes 15364
  110.6 1.1 copy-start.1
  115.2 61.7 %copy-start = (bf16[1280,1280]{1,0:T(8,128)(2,1)S(1)}, bf16[1280,1280]{1,0:T(8,128)(2,1)}, u32[]{:S(2)}) copy-start(bf16[1280,1280]{1,0:T(8,128)(2,1)} %all-gather.5.cloned.1.call-done) | copy-start | bytes 9830404
  176.2 0.7 copy-start.3
  179.1 154.7 %reduce-scatter.2.cloned.1.call-start = ((), (), s32[]{:S(2)}) async-start(), calls=%async_computation.7 | async-start | bytes 7372800 | tf_op jit(solution)/shard_map/reduce_scatter | solution.py:70
  184.2 12.7 %copy-start.2 = (bf16[136,1280]{1,0:T(8,128)(2,1)S(1)}, bf16[136,1280]{1,0:T(8,128)(2,1)}, u32[]{:S(2)}) copy-start(bf16[136,1280]{1,0:T(8,128)(2,1)} %copy-done.1) | copy-start | bytes 1044484
  184.2 14.1 %copy-start.4 = (bf16[136,1280]{1,0:T(8,128)(2,1)S(1)}, bf16[136,1280]{1,0:T(8,128)(2,1)}, u32[]{:S(2)}) copy-start(bf16[136,1280]{1,0:T(8,128)(2,1)} %select_select_fusion.1) | copy-start | bytes 1044484
Sparse Core Ops, SparseCore 0:
  10.2 99.8 all-gather.4
  112.3 60.9 all-gather.2
  179.2 17.5 all-reduce.1
  201.3 132.3 reduce-scatter.1
where the time goes:
time: 341 us; the launch traced here: 340 us
  waiting for transfers between devices  253 us (74%)
  blocking collectives  30.6 us (9%)
  between operations  14 us (4%)
  matrix products  13.5 us (4%)
  starting transfers between devices  11.2 us (3%)
  local copies, waits for them, and re-layouts  11.1 us (3%)
  other arithmetic  6.81 us (2%)
    reduce_scatter x1, waiting for transfers between devices, shards(): lax.psum_scatter(row_product(normed, d_pre), 'gx', scatter_dimension=0, t...  101 us
    all_gather x1, waiting for transfers between devices, shards(): lax.all_gather(w_down, 'gx', axis=0, tiled=True)  58.1 us
    all_to_all x1, waiting for transfers between devices, shards(): lax.all_to_all(send_grads, 'gx', split_axis=1, concat_axis=1, tiled=True)  43.6 us
    all_to_all x1, waiting for transfers between devices, shards(): lax.all_to_all(send_frames, 'gx', split_axis=1, concat_axis=1, tiled=True)  36.3 us
    all_to_all x1, blocking collectives, shards(): lax.all_to_all(send_back, 'gx', split_axis=1, concat_axis=1, tiled=True)  30.6 us
    psum x1, waiting for transfers between devices, shards(): d_norm = lax.psum(partial_value, 'gy')  12.2 us
    all_to_all x1, starting transfers between devices, shards(): lax.all_to_all(send_frames, 'gx', split_axis=1, concat_axis=1, tiled=True)  7.41 us
  transfers between devices with their start and end apart: 6, of which 5 were waited for; matrix products, arithmetic and copies ran while one was open for 8% of the time, Pallas kernels for 0%

commit v1 on v0

v1 whole, which is shorter than its diff:
```python
import jax
import jax.numpy as jnp
from jax import lax
from jax.sharding import PartitionSpec as P


def norm_rows(rows):
    values = rows.astype(jnp.float32)
    centre = jnp.mean(values, axis=-1, keepdims=True)
    shifted = values - centre
    variance = jnp.mean(shifted * shifted, axis=-1, keepdims=True)
    inv_std = lax.rsqrt(variance + 1e-05)
    return shifted * inv_std, inv_std


def gelu_slope(values):
    return (
        0.5 * (1.0 + lax.erf(values * 0.7071067811865476))
        + values * jnp.exp(-0.5 * values * values) * 0.3989422804014327
    )


def ring_member(place, count):
    place = place % count
    return jnp.where(place < count // 2, 2 * place, 2 * (count - 1 - place) + 1)


def shards(frames, out_grad, ln_gain, w_up, w_down, lengths):
    peers = lax.axis_size("gx")
    half = peers // 2
    own = lax.axis_index("gx")
    side = lax.axis_index("groups")
    core = lax.axis_index("gy")
    frame_len, width = frames.shape[1:]
    depth, hidden = w_up.shape
    quarter = hidden // 2
    half_width = width // 2
    bf16, f32 = jnp.bfloat16, jnp.float32

    order = list(range(0, peers, 2)) + list(range(peers - 1, 0, -2))
    ahead = [(order[i], order[(i + 1) % peers]) for i in range(peers)]
    behind = [(b, a) for a, b in ahead]
    place = jnp.where(own % 2 == 0, own // 2, peers - 1 - own // 2)
    swap = [(0, 1), (1, 0)]
    wire = bf16 if half <= 8 else f32

    mine = jnp.stack(
        [lax.dynamic_slice_in_dim(w, side * quarter, quarter, 1) for w in (w_up, w_down)]
    )

    centred, inv_std = norm_rows(frames[0])
    normed = (centred * ln_gain).astype(bf16)
    length = lax.dynamic_index_in_dim(lengths, own, 0, keepdims=False)
    keep = (jnp.arange(frame_len, dtype=jnp.int32) < length)[:, None]
    grads = jnp.where(keep, out_grad[0], 0)
    first = core == 0
    fetched = lax.ppermute(jnp.where(first, normed, grads), "groups", swap)
    sibling = lax.ppermute(fetched, "gy", swap)
    other_normed = jnp.where(first, fetched, sibling)
    other_grads = jnp.where(first, sibling, fetched)

    full = jnp.zeros((2, depth * peers, quarter), bf16)

    def put(full, block, step, at=0):
        row = ring_member(place + step + peers, peers) * depth
        return lax.dynamic_update_slice(full, block, (at, row, 0))

    full = put(full, mine, 0)
    up, down = mine, mine
    for step in range(1, half):
        up = lax.ppermute(up, "gx", ahead)
        down = lax.ppermute(down, "gx", behind)
        full = put(full, up, -step)
        full = put(full, down, step)
    full = put(full, lax.ppermute(up[:1], "gx", ahead), half)
    full = put(full, lax.ppermute(down[1:], "gx", behind), half, 1)
    full_up, full_down = full[0], full[1]

    normed_all = jnp.concatenate([normed, other_normed])
    grads_all = jnp.concatenate([grads, other_grads])
    pre_act = jnp.dot(normed_all, full_up, preferred_element_type=f32)
    d_act = jnp.dot(grads_all, full_down, preferred_element_type=f32)
    d_pre = (d_act * gelu_slope(pre_act)).astype(bf16)

    partial = jnp.stack(
        [
            lax.dot_general(
                normed_all[i * frame_len : (i + 1) * frame_len],
                d_pre[i * frame_len : (i + 1) * frame_len],
                (((0,), (0,)), ((), ())),
                preferred_element_type=f32,
            )
            for i in range(2)
        ]
    )

    def term(step):
        row = ring_member(place + step + peers, peers) * depth
        return lax.dynamic_slice_in_dim(partial, row, depth, 1)

    far = term(half)
    up = lax.ppermute(far[0].astype(wire), "gx", ahead)
    down = lax.ppermute(far[1].astype(wire), "gx", behind)
    for step in range(half - 1, 0, -1):
        up_term, down_term = term(step), term(-step)
        if step == half - 1:
            up = jnp.stack([up_term[0] + up.astype(f32), up_term[1]])
            down = jnp.stack([down_term[0], down_term[1] + down.astype(f32)])
        else:
            up = up_term + up.astype(f32)
            down = down_term + down.astype(f32)
        up = lax.ppermute(up.astype(wire), "gx", ahead)
        down = lax.ppermute(down.astype(wire), "gx", behind)
    total = term(0) + up.astype(f32) + down.astype(f32)
    passed = lax.ppermute(total[1].astype(wire), "groups", swap).astype(f32)
    low = jnp.where(side == 0, total[0], passed)
    high = jnp.where(side == 0, passed, total[0])
    up_grad = jnp.concatenate([low, high], axis=1)

    d_norm = lax.dot_general(
        d_pre, full_up, (((1,), (1,)), ((), ())), preferred_element_type=f32
    )
    first_sum = jnp.sum(d_norm * ln_gain, axis=-1)
    second_sum = jnp.sum(d_pre.astype(f32) * pre_act, axis=-1)
    sums = jnp.stack([first_sum, second_sum])
    sums = sums + lax.ppermute(sums, "gy", swap)
    sums = sums[:, :frame_len] + lax.ppermute(sums[:, frame_len:], "groups", swap)
    means = (sums / width)[:, :, None]
    keep_cols = lax.dynamic_slice_in_dim(d_norm, core * half_width, half_width, 1)
    send_cols = lax.dynamic_slice_in_dim(d_norm, (1 - core) * half_width, half_width, 1)
    cols = keep_cols + lax.ppermute(send_cols.astype(bf16), "gy", swap).astype(f32)
    back = lax.ppermute(cols[frame_len:].astype(bf16), "groups", swap)
    d_norm = cols[:frame_len] + back.astype(f32)

    def own_cols(array):
        return lax.dynamic_slice_in_dim(array, core * half_width, half_width, array.ndim - 1)

    scaled = d_norm * own_cols(ln_gain)
    input_grad = own_cols(grads).astype(f32) + inv_std * (
        scaled - means[0] - own_cols(centred) * means[1]
    )
    return (input_grad.astype(bf16)[None], up_grad)


def solution(mesh):
    placed = (
        P(("groups", "gx"), None, None),
        P(("groups", "gx"), None, None),
        P(),
        P("gx", "gy"),
        P("gx", "gy"),
        P("groups"),
    )
    return jax.shard_map(
        shards,
        mesh=mesh,
        in_specs=placed,
        out_specs=(P(("groups", "gx"), None, "gy"), P(("groups", "gx"), "gy")),
        check_vma=False,
    )
```

time: 341 us -> 113 us (0.33)
  waiting for transfers between devices: 253 us -> 51.1 us
  blocking collectives: 30.6 us -> 0 us
  starting transfers between devices: 11.2 us -> 24.2 us
  between operations: 14 us -> 1.04 us
  other arithmetic: 6.81 us -> 18.8 us
  matrix products: 13.5 us -> 7.7 us
    reduce_scatter x1 -> x0, waiting for transfers between devices: 101 us -> none  [shards(): lax.psum_scatter(row_product(normed, d_pre), 'gx', scatter_dimension=0, t...]
    all_to_all x2 -> x0, waiting for transfers between devices: 79.9 us -> none  [the longest x1 43.6 us: shards(): lax.all_to_all(send_grads, 'gx', split_axis=1, concat_axis=1, tiled=True)]
    all_gather x2 -> x0, waiting for transfers between devices: 58.1 us -> none  [the longest x1 58.1 us: shards(): lax.all_gather(w_down, 'gx', axis=0, tiled=True)]
    ppermute x0 -> x23, waiting for transfers between devices: none -> 51.1 us  [the longest x3 14.9 us: shards(): up = lax.ppermute(up, 'gx', ahead)]
    all_to_all x1 -> x0, blocking collectives: 30.6 us -> none  [shards(): lax.all_to_all(send_back, 'gx', split_axis=1, concat_axis=1, tiled=True)]
    ppermute x0 -> x23, starting transfers between devices: none -> 24.2 us  [the longest x3 4.9 us: shards(): up = lax.ppermute(up.astype(wire), 'gx', ahead)]
    psum x1 -> x0, waiting for transfers between devices: 12.2 us -> none  [shards(): d_norm = lax.psum(partial_value, 'gy')]
    all_to_all x2 -> x0, starting transfers between devices: 11 us -> none  [the longest x1 7.41 us: shards(): lax.all_to_all(send_frames, 'gx', split_axis=1, concat_axis=1, tiled=True)]
  transfers between devices with their start and end apart: 6 -> 23, of which waited for: 5 -> 15; matrix products, arithmetic and copies ran while one was open for 8% -> 14% of each run, Pallas kernels for 0% -> 0%
where the time goes in v1:
time: 113 us
  waiting for transfers between devices  51.1 us (45%)
  starting transfers between devices  24.2 us (21%)
  other arithmetic  18.8 us (17%)
  local copies, waits for them, and re-layouts  10.1 us (9%)
  matrix products  7.7 us (7%)
    ppermute x3, waiting for transfers between devices, shards(): up = lax.ppermute(up, 'gx', ahead)  14.9 us
    ppermute x3, waiting for transfers between devices, shards(): down = lax.ppermute(down.astype(wire), 'gx', behind)  10.3 us
    ppermute x1, waiting for transfers between devices, shards(): fetched = lax.ppermute(jnp.where(first, normed, grads), 'groups', swap)  7.19 us
    ppermute x3, waiting for transfers between devices, shards(): up = lax.ppermute(up.astype(wire), 'gx', ahead)  4.97 us
    ppermute x3, starting transfers between devices, shards(): up = lax.ppermute(up.astype(wire), 'gx', ahead)  4.9 us
    ppermute x3, starting transfers between devices, shards(): up = lax.ppermute(up, 'gx', ahead)  4.78 us
    dynamic_update_slice x8, local copies, waits for them, and re-layouts, put(): return lax.dynamic_update_slice(full, block, (at, row, 0))  4.38 us
    ppermute x1, waiting for transfers between devices, shards(): down = lax.ppermute(far[1].astype(wire), 'gx', behind)  3.82 us
  transfers between devices with their start and end apart: 23, of which 15 were waited for; matrix products, arithmetic and copies ran while one was open for 14% of the time, Pallas kernels for 0%

profile of v1, /device:TPU:0, one launch (start us, length us, event | category | flops | bytes accessed | tf_op | source)
XLA Modules:
  0.0 112.9 jit_solution(10659672525268471446)
XLA Ops:
  4.1 1.6 %fusion.3 = f32[384]{0:T(512)S(1)} fusion(bf16[1,384,1280]{2,1,0:T(8,128)(2,1)} %param.6, f32[384]{0:T(512)S(1)} %broadcast_multiply_fusion), kind=kLoop, calls=%fused_computation.25 | loop fusion | flops 1965696 | bytes 986112 | tf_op jit(solution)/shard_map/reduce_sum | solution.py:11
  5.7 3.8 %broadcast_select_fusion.2 = (bf16[384,1280]{1,0:T(8,128)(2,1)}, bf16[384,1280]{1,0:T(8,128)(2,1)}, bf16[384,1280]{1,0:T(8,128)(2,1)}) fusion(pred[]{:T(512)S(6)} %eq.29, bf16[1,384,1280]{2,1,0:T(8,128)(2,1)} %param.7, pred[384]{0:T(512)(128)(4,1)S(1)} %iota_compare_fusion, f32[1280]{0:T(1024)} %param.8, f32[384]{0:T(512)S(1)} %add_rsqrt_fusion, ...), kind=kLoop, calls=%fused_computation.58 | loop fusion | flops 3440640 | bytes 4923777 | tf_op jit(solution)/shard_map/jit(_where)/select_n | solution.py:57
  9.4 2.9 %collective-permute-start = (bf16[384,1280]{1,0:T(8,128)(2,1)}, bf16[384,1280]{1,0:T(8,128)(2,1)}, u32[]{:S(2)}, u32[]{:S(2)}) collective-permute-start(bf16[384,1280]{1,0:T(8,128)(2,1)} %get-tuple-element.4), channel_id=1, source_target_pairs={{0,16},{16,0},{1,17},{17,1},{2,18},{18,2},{3,19},{19,3},{4,20},{20... | collective-permute-start | bytes 2949128 | tf_op jit(solution)/shard_map/ppermute | solution.py:57
  14.1 1.6 %collective-permute-start.2 = (bf16[2,160,640]{2,1,0:T(8,128)(2,1)S(1)}, bf16[2,160,640]{2,1,0:T(8,128)(2,1)}, u32[]{:S(2)}, u32[]{:S(2)}) collective-permute-start(bf16[2,160,640]{2,1,0:T(8,128)(2,1)S(1)} %get-tuple-element.19), channel_id=1, source_target_pairs={{0,4},{4,8},{8,12},{12,14},{14,10},{10,6},{6,2},{2,0},{1,5},{5,9},... | collective-permute-start | bytes 1228808 | tf_op jit(solution)/shard_map/ppermute | solution.py:71
  16.2 9.0 %collective-permute-done.2 = bf16[2,160,640]{2,1,0:T(8,128)(2,1)} collective-permute-done((bf16[2,160,640]{2,1,0:T(8,128)(2,1)S(1)}, bf16[2,160,640]{2,1,0:T(8,128)(2,1)}, u32[]{:S(2)}, u32[]{:S(2)}) %collective-permute-start.2) | collective-permute-done | bytes 409632 | tf_op jit(solution)/shard_map/ppermute | solution.py:71
  27.2 7.2 %collective-permute-done = bf16[384,1280]{1,0:T(8,128)(2,1)} collective-permute-done((bf16[384,1280]{1,0:T(8,128)(2,1)}, bf16[384,1280]{1,0:T(8,128)(2,1)}, u32[]{:S(2)}, u32[]{:S(2)}) %collective-permute-start) | collective-permute-done | bytes 983072 | tf_op jit(solution)/shard_map/ppermute | solution.py:57
  41.8 4.7 %collective-permute-done.6 = bf16[2,160,640]{2,1,0:T(8,128)(2,1)S(1)} collective-permute-done((bf16[2,160,640]{2,1,0:T(8,128)(2,1)}, bf16[2,160,640]{2,1,0:T(8,128)(2,1)S(1)}, u32[]{:S(2)}, u32[]{:S(2)}) %collective-permute-start.6) | collective-permute-done | bytes 409632 | tf_op jit(solution)/shard_map/ppermute | solution.py:71
  46.6 1.9 %collective-permute-start.8 = (bf16[1,160,640]{2,1,0:T(8,128)(2,1)S(1)}, bf16[1,160,640]{2,1,0:T(8,128)(2,1)S(1)}, u32[]{:S(2)}, u32[]{:S(2)}) collective-permute-start(bf16[1,160,640]{2,1,0:T(8,128)(2,1)S(1)} %slice.89), channel_id=1, source_target_pairs={{0,4},{4,8},{8,12},{12,14},{14,10},{10,6},{6,2},{2,0},{1,5},{5,9},... | collective-permute-start | bytes 614408 | tf_op jit(solution)/shard_map/ppermute | solution.py:75
  48.9 3.5 %collective-permute-done.8 = bf16[1,160,640]{2,1,0:T(8,128)(2,1)S(1)} collective-permute-done((bf16[1,160,640]{2,1,0:T(8,128)(2,1)S(1)}, bf16[1,160,640]{2,1,0:T(8,128)(2,1)S(1)}, u32[]{:S(2)}, u32[]{:S(2)}) %collective-permute-start.8) | collective-permute-done | bytes 204832 | tf_op jit(solution)/shard_map/ppermute | solution.py:75
  52.4 1.9 %collective-permute-done.9 = bf16[1,160,640]{2,1,0:T(8,128)(2,1)S(1)} collective-permute-done((bf16[1,160,640]{2,1,0:T(8,128)(2,1)S(1)}, bf16[1,160,640]{2,1,0:T(8,128)(2,1)S(1)}, u32[]{:S(2)}, u32[]{:S(2)}) %collective-permute-start.9) | collective-permute-done | bytes 204832 | tf_op jit(solution)/shard_map/ppermute | solution.py:76
  54.3 2.8 %broadcast_select_fusion.1 = (bf16[384,1280]{1,0:T(8,128)(2,1)S(1)}, bf16[384,1280]{1,0:T(8,128)(2,1)S(1)}) fusion(bf16[384,1280]{1,0:T(8,128)(2,1)} %collective-permute-done.1, bf16[384,1280]{1,0:T(8,128)(2,1)} %collective-permute-done, pred[]{:T(512)S(6)} %eq.29), kind=kLoop, calls=%fused_computation.57 | loop fusion | flops 983040 | bytes 3932161 | tf_op jit(solution)/shard_map/jit(_where)/select_n | solution.py:60
  58.7 2.1 %multiply_reduce_fusion.1 = (f32[768]{0:T(1024)S(1)}, bf16[768,640]{0,1:T(8,128)(2,1)S(1)}) fusion(f32[768,640]{0,1:T(8,128)S(1)} %fusion.14, bf16[2,1280,640]{2,1,0:T(8,128)(2,1)S(1)} %constant_dynamic-update-slice_fusion, bf16[384,1280]{1,0:T(8,128)(2,1)S(1)} %get-tuple-element.13, bf16[384,1280]{1,0:T(8,128)(2,1)S(1)} %copy-done.6), kind=kOutput, calls=%fused_computation.40 | convolution fusion | flops 1268612352 | bytes 6556672 | tf_op jit(solution)/shard_map/dot_general | solution.py:82
  63.2 1.6 %collective-permute-start.14 = (bf16[160,640]{1,0:T(8,128)(2,1)S(1)}, bf16[160,640]{1,0:T(8,128)(2,1)S(1)}, u32[]{:S(2)}, u32[]{:S(2)}) collective-permute-start(bf16[160,640]{1,0:T(8,128)(2,1)S(1)} %get-tuple-element.17), channel_id=1, source_target_pairs={{0,4},{4,8},{8,12},{12,14},{14,10},{10,6},{6,2},{2,0},{1,5},{5,9},... | collective-permute-start | bytes 614408 | tf_op jit(solution)/shard_map/ppermute | solution.py:102
  66.2 1.8 %multiply_reduce_fusion = (f32[768]{0:T(1024)S(1)}, f32[768,1280]{1,0:T(8,128)S(1)}) fusion(f32[1280]{0:T(1024)S(1)} %copy-done.14, bf16[768,640]{0,1:T(8,128)(2,1)S(1)} %get-tuple-element.22, bf16[2,1280,640]{2,1,0:T(8,128)(2,1)S(1)} %copy-done.5), kind=kOutput, calls=%fused_computation.16 | convolution fusion | flops 1260256512 | bytes 6564864 | tf_op jit(solution)/shard_map/dot_general | solution.py:120
  69.2 1.7 %collective-permute-start.15 = (bf16[2,160,640]{2,1,0:T(8,128)(2,1)S(1)}, bf16[2,160,640]{2,1,0:T(8,128)(2,1)S(1)}, u32[]{:S(2)}, u32[]{:S(2)}) collective-permute-start(bf16[2,160,640]{2,1,0:T(8,128)(2,1)S(1)} %pad_maximum_fusion.2), channel_id=1, source_target_pairs={{0,4},{4,8},{8,12},{12,14},{14,10},{10,6},{6,2},{2,0},{1,5},{5,9},... | collective-permute-start | bytes 1228808 | tf_op jit(solution)/shard_map/ppermute | solution.py:112
  70.9 3.8 %collective-permute-done.18 = bf16[160,640]{1,0:T(8,128)(2,1)S(1)} collective-permute-done((bf16[160,640]{1,0:T(8,128)(2,1)S(1)}, bf16[160,640]{1,0:T(8,128)(2,1)S(1)}, u32[]{:S(2)}, u32[]{:S(2)}) %collective-permute-start.18) | collective-permute-done | bytes 204832 | tf_op jit(solution)/shard_map/ppermute | solution.py:103
  76.8 1.8 %collective-permute-start.13 = (f32[2,384]{1,0:T(2,128)S(1)}, f32[2,384]{1,0:T(2,128)S(1)}, u32[]{:S(2)}, u32[]{:S(2)}) collective-permute-start(f32[2,384]{1,0:T(2,128)S(1)} %slice.96), channel_id=1, source_target_pairs={{0,16},{16,0},{1,17},{17,1},{2,18},{18,2},{3,19},{19,3},{4,20},{20... | collective-permute-start | bytes 9224 | tf_op jit(solution)/shard_map/ppermute | solution.py:127
  78.6 4.3 %collective-permute-done.19 = bf16[2,160,640]{2,1,0:T(8,128)(2,1)S(1)} collective-permute-done((bf16[2,160,640]{2,1,0:T(8,128)(2,1)S(1)}, bf16[2,160,640]{2,1,0:T(8,128)(2,1)S(1)}, u32[]{:S(2)}, u32[]{:S(2)}) %collective-permute-start.19) | collective-permute-done | bytes 409632 | tf_op jit(solution)/shard_map/ppermute | solution.py:113
  84.0 1.6 %collective-permute-start.16 = (bf16[2,160,640]{2,1,0:T(8,128)(2,1)}, bf16[2,160,640]{2,1,0:T(8,128)(2,1)}, u32[]{:S(2)}, u32[]{:S(2)}) collective-permute-start(bf16[2,160,640]{2,1,0:T(8,128)(2,1)} %get-tuple-element.9), channel_id=1, source_target_pairs={{0,4},{4,8},{8,12},{12,14},{14,10},{10,6},{6,2},{2,0},{1,5},{5,9},... | collective-permute-start | bytes 1228808 | tf_op jit(solution)/shard_map/ppermute | solution.py:112
  86.0 1.6 %fusion.1 = f32[384,1280]{1,0:T(8,128)} fusion(bf16[1,384,1280]{2,1,0:T(8,128)(2,1)S(1)} %copy-done.2, f32[384]{0:T(512)S(1)} %add_rsqrt_fusion, f32[384]{0:T(512)S(1)} %broadcast_multiply_fusion), kind=kLoop, calls=%fused_computation.23 | loop fusion | flops 1474560 | bytes 2952192 | tf_op jit(solution)/shard_map/mul | solution.py:13
  87.7 4.5 %collective-permute-done.16 = bf16[2,160,640]{2,1,0:T(8,128)(2,1)} collective-permute-done((bf16[2,160,640]{2,1,0:T(8,128)(2,1)}, bf16[2,160,640]{2,1,0:T(8,128)(2,1)}, u32[]{:S(2)}, u32[]{:S(2)}) %collective-permute-start.16) | collective-permute-done | bytes 409632 | tf_op jit(solution)/shard_map/ppermute | solution.py:112
  92.3 2.9 %collective-permute-done.20 = bf16[2,160,640]{2,1,0:T(8,128)(2,1)} collective-permute-done((bf16[2,160,640]{2,1,0:T(8,128)(2,1)}, bf16[2,160,640]{2,1,0:T(8,128)(2,1)}, u32[]{:S(2)}, u32[]{:S(2)}) %collective-permute-start.20) | collective-permute-done | bytes 409632 | tf_op jit(solution)/shard_map/ppermute | solution.py:113
  101.6 3.1 %collective-permute-done.21 = bf16[2,160,640]{2,1,0:T(8,128)(2,1)S(1)} collective-permute-done((bf16[2,160,640]{2,1,0:T(8,128)(2,1)S(1)}, bf16[2,160,640]{2,1,0:T(8,128)(2,1)S(1)}, u32[]{:S(2)}, u32[]{:S(2)}) %collective-permute-start.21) | collective-permute-done | bytes 409632 | tf_op jit(solution)/shard_map/ppermute | solution.py:113
  106.6 3.0 %collective-permute-done.11 = bf16[384,640]{1,0:T(8,128)(2,1)S(1)} collective-permute-done((bf16[384,640]{1,0:T(8,128)(2,1)S(1)}, bf16[384,640]{1,0:T(8,128)(2,1)S(1)}, u32[]{:S(2)}, u32[]{:S(2)}) %collective-permute-start.11) | collective-permute-done | bytes 491552 | tf_op jit(solution)/shard_map/ppermute | solution.py:132
  (106 shorter events, 37.0 us)
Async XLA Ops:
  9.4 25.0 %collective-permute-start = (bf16[384,1280]{1,0:T(8,128)(2,1)}, bf16[384,1280]{1,0:T(8,128)(2,1)}, u32[]{:S(2)}, u32[]{:S(2)}) collective-permute-start(bf16[384,1280]{1,0:T(8,128)(2,1)} %get-tuple-element.4), channel_id=1, source_target_pairs={{0,16},{16,0},{1,17},{17,1},{2,18},{18,2},{3,19},{19,3},{4,20},{20... | collective-permute-start | bytes 2949128 | tf_op jit(solution)/shard_map/ppermute | solution.py:57
  14.1 11.1 %collective-permute-start.2 = (bf16[2,160,640]{2,1,0:T(8,128)(2,1)S(1)}, bf16[2,160,640]{2,1,0:T(8,128)(2,1)}, u32[]{:S(2)}, u32[]{:S(2)}) collective-permute-start(bf16[2,160,640]{2,1,0:T(8,128)(2,1)S(1)} %get-tuple-element.19), channel_id=1, source_target_pairs={{0,4},{4,8},{8,12},{12,14},{14,10},{10,6},{6,2},{2,0},{1,5},{5,9},... | collective-permute-start | bytes 1228808 | tf_op jit(solution)/shard_map/ppermute | solution.py:71
  15.8 11.0 %collective-permute-start.3 = (bf16[2,160,640]{2,1,0:T(8,128)(2,1)S(1)}, bf16[2,160,640]{2,1,0:T(8,128)(2,1)}, u32[]{:S(2)}, u32[]{:S(2)}) collective-permute-start(bf16[2,160,640]{2,1,0:T(8,128)(2,1)S(1)} %get-tuple-element.19), channel_id=1, source_target_pairs={{4,0},{8,4},{12,8},{14,12},{10,14},{6,10},{2,6},{0,2},{5,1},{9,5},... | collective-permute-start | bytes 1228808 | tf_op jit(solution)/shard_map/ppermute | solution.py:72
  25.2 10.3 %collective-permute-start.4 = (bf16[2,160,640]{2,1,0:T(8,128)(2,1)}, bf16[2,160,640]{2,1,0:T(8,128)(2,1)}, u32[]{:S(2)}, u32[]{:S(2)}) collective-permute-start(bf16[2,160,640]{2,1,0:T(8,128)(2,1)} %collective-permute-done.2), channel_id=1, source_target_pairs={{0,4},{4,8},{8,12},{12,14},{14,10},{10,6},{6,2},{2,0},{1,5},{5,9},... | collective-permute-start | bytes 1228808 | tf_op jit(solution)/shard_map/ppermute | solution.py:71
  26.8 10.3 %collective-permute-start.5 = (bf16[2,160,640]{2,1,0:T(8,128)(2,1)}, bf16[2,160,640]{2,1,0:T(8,128)(2,1)}, u32[]{:S(2)}, u32[]{:S(2)}) collective-permute-start(bf16[2,160,640]{2,1,0:T(8,128)(2,1)} %collective-permute-done.3), channel_id=1, source_target_pairs={{4,0},{8,4},{12,8},{14,12},{10,14},{6,10},{2,6},{0,2},{5,1},{9,5},... | collective-permute-start | bytes 1228808 | tf_op jit(solution)/shard_map/ppermute | solution.py:72
  34.4 19.9 %collective-permute-start.1 = (bf16[384,1280]{1,0:T(8,128)(2,1)}, bf16[384,1280]{1,0:T(8,128)(2,1)}, u32[]{:S(2)}, u32[]{:S(2)}) collective-permute-start(bf16[384,1280]{1,0:T(8,128)(2,1)} %collective-permute-done), channel_id=1, source_target_pairs={{0,1},{1,0},{2,3},{3,2},{4,5},{5,4},{6,7},{7,6},{8,9},{9,8},{10,11... | collective-permute-start | bytes 2949128 | tf_op jit(solution)/shard_map/ppermute | solution.py:58
  35.6 11.0 %collective-permute-start.6 = (bf16[2,160,640]{2,1,0:T(8,128)(2,1)}, bf16[2,160,640]{2,1,0:T(8,128)(2,1)S(1)}, u32[]{:S(2)}, u32[]{:S(2)}) collective-permute-start(bf16[2,160,640]{2,1,0:T(8,128)(2,1)} %collective-permute-done.4), channel_id=1, source_target_pairs={{0,4},{4,8},{8,12},{12,14},{14,10},{10,6},{6,2},{2,0},{1,5},{5,9},... | collective-permute-start | bytes 1228808 | tf_op jit(solution)/shard_map/ppermute | solution.py:71
  37.1 11.3 %collective-permute-start.7 = (bf16[2,160,640]{2,1,0:T(8,128)(2,1)}, bf16[2,160,640]{2,1,0:T(8,128)(2,1)S(1)}, u32[]{:S(2)}, u32[]{:S(2)}) collective-permute-start(bf16[2,160,640]{2,1,0:T(8,128)(2,1)} %collective-permute-done.5), channel_id=1, source_target_pairs={{4,0},{8,4},{12,8},{14,12},{10,14},{6,10},{2,6},{0,2},{5,1},{9,5},... | collective-permute-start | bytes 1228808 | tf_op jit(solution)/shard_map/ppermute | solution.py:72
  46.6 5.8 %collective-permute-start.8 = (bf16[1,160,640]{2,1,0:T(8,128)(2,1)S(1)}, bf16[1,160,640]{2,1,0:T(8,128)(2,1)S(1)}, u32[]{:S(2)}, u32[]{:S(2)}) collective-permute-start(bf16[1,160,640]{2,1,0:T(8,128)(2,1)S(1)} %slice.89), channel_id=1, source_target_pairs={{0,4},{4,8},{8,12},{12,14},{14,10},{10,6},{6,2},{2,0},{1,5},{5,9},... | collective-permute-start | bytes 614408 | tf_op jit(solution)/shard_map/ppermute | solution.py:75
  48.5 5.8 %collective-permute-start.9 = (bf16[1,160,640]{2,1,0:T(8,128)(2,1)S(1)}, bf16[1,160,640]{2,1,0:T(8,128)(2,1)S(1)}, u32[]{:S(2)}, u32[]{:S(2)}) collective-permute-start(bf16[1,160,640]{2,1,0:T(8,128)(2,1)S(1)} %slice.90), channel_id=1, source_target_pairs={{4,0},{8,4},{12,8},{14,12},{10,14},{6,10},{2,6},{0,2},{5,1},{9,5},... | collective-permute-start | bytes 614408 | tf_op jit(solution)/shard_map/ppermute | solution.py:76
  63.1 19.8 %copy-start = (f32[1,1280,640]{2,1,0:T(8,128)}, f32[1,1280,640]{2,1,0:T(8,128)S(1)}, u32[]{:S(2)}) copy-start(f32[1,1280,640]{2,1,0:T(8,128)S(1)} %convolution_bitcast_fusion) | copy-start | bytes 9830404
  63.2 5.9 %collective-permute-start.14 = (bf16[160,640]{1,0:T(8,128)(2,1)S(1)}, bf16[160,640]{1,0:T(8,128)(2,1)S(1)}, u32[]{:S(2)}, u32[]{:S(2)}) collective-permute-start(bf16[160,640]{1,0:T(8,128)(2,1)S(1)} %get-tuple-element.17), channel_id=1, source_target_pairs={{0,4},{4,8},{8,12},{12,14},{14,10},{10,6},{6,2},{2,0},{1,5},{5,9},... | collective-permute-start | bytes 614408 | tf_op jit(solution)/shard_map/ppermute | solution.py:102
  68.2 6.5 %collective-permute-start.18 = (bf16[160,640]{1,0:T(8,128)(2,1)S(1)}, bf16[160,640]{1,0:T(8,128)(2,1)S(1)}, u32[]{:S(2)}, u32[]{:S(2)}) collective-permute-start(bf16[160,640]{1,0:T(8,128)(2,1)S(1)} %get-tuple-element.18), channel_id=1, source_target_pairs={{4,0},{8,4},{12,8},{14,12},{10,14},{6,10},{2,6},{0,2},{5,1},{9,5},... | collective-permute-start | bytes 614408 | tf_op jit(solution)/shard_map/ppermute | solution.py:103
  69.2 9.4 %collective-permute-start.15 = (bf16[2,160,640]{2,1,0:T(8,128)(2,1)S(1)}, bf16[2,160,640]{2,1,0:T(8,128)(2,1)S(1)}, u32[]{:S(2)}, u32[]{:S(2)}) collective-permute-start(bf16[2,160,640]{2,1,0:T(8,128)(2,1)S(1)} %pad_maximum_fusion.2), channel_id=1, source_target_pairs={{0,4},{4,8},{8,12},{12,14},{14,10},{10,6},{6,2},{2,0},{1,5},{5,9},... | collective-permute-start | bytes 1228808 | tf_op jit(solution)/shard_map/ppermute | solution.py:112
  74.9 8.0 %collective-permute-start.19 = (bf16[2,160,640]{2,1,0:T(8,128)(2,1)S(1)}, bf16[2,160,640]{2,1,0:T(8,128)(2,1)S(1)}, u32[]{:S(2)}, u32[]{:S(2)}) collective-permute-start(bf16[2,160,640]{2,1,0:T(8,128)(2,1)S(1)} %pad_maximum_fusion.3), channel_id=1, source_target_pairs={{4,0},{8,4},{12,8},{14,12},{10,14},{6,10},{2,6},{0,2},{5,1},{9,5},... | collective-permute-start | bytes 1228808 | tf_op jit(solution)/shard_map/ppermute | solution.py:113
  75.1 1.6 %collective-permute-start.12 = (f32[2,768]{1,0:T(2,128)S(1)}, f32[2,768]{1,0:T(2,128)S(1)}, u32[]{:S(2)}, u32[]{:S(2)}) collective-permute-start(f32[2,768]{1,0:T(2,128)S(1)} %pad_maximum_fusion.4), channel_id=1, source_target_pairs={{0,1},{1,0},{2,3},{3,2},{4,5},{5,4},{6,7},{7,6},{8,9},{9,8},{10,11... | collective-permute-start | bytes 18440 | tf_op jit(solution)/shard_map/ppermute | solution.py:126
  76.3 22.5 %collective-permute-start.10 = (bf16[768,640]{1,0:T(8,128)(2,1)}, bf16[768,640]{1,0:T(8,128)(2,1)}, u32[]{:S(2)}, u32[]{:S(2)}) collective-permute-start(bf16[768,640]{1,0:T(8,128)(2,1)} %dynamic-slice_convert_fusion), channel_id=1, source_target_pairs={{0,1},{1,0},{2,3},{3,2},{4,5},{5,4},{6,7},{7,6},{8,9},{9,8},{10,11... | collective-permute-start | bytes 2949128 | tf_op jit(solution)/shard_map/ppermute | solution.py:131
  76.8 11.0 %collective-permute-start.13 = (f32[2,384]{1,0:T(2,128)S(1)}, f32[2,384]{1,0:T(2,128)S(1)}, u32[]{:S(2)}, u32[]{:S(2)}) collective-permute-start(f32[2,384]{1,0:T(2,128)S(1)} %slice.96), channel_id=1, source_target_pairs={{0,16},{16,0},{1,17},{17,1},{2,18},{18,2},{3,19},{19,3},{4,20},{20... | collective-permute-start | bytes 9224 | tf_op jit(solution)/shard_map/ppermute | solution.py:127
  84.0 8.3 %collective-permute-start.16 = (bf16[2,160,640]{2,1,0:T(8,128)(2,1)}, bf16[2,160,640]{2,1,0:T(8,128)(2,1)}, u32[]{:S(2)}, u32[]{:S(2)}) collective-permute-start(bf16[2,160,640]{2,1,0:T(8,128)(2,1)} %get-tuple-element.9), channel_id=1, source_target_pairs={{0,4},{4,8},{8,12},{12,14},{14,10},{10,6},{6,2},{2,0},{1,5},{5,9},... | collective-permute-start | bytes 1228808 | tf_op jit(solution)/shard_map/ppermute | solution.py:112
  85.6 9.6 %collective-permute-start.20 = (bf16[2,160,640]{2,1,0:T(8,128)(2,1)}, bf16[2,160,640]{2,1,0:T(8,128)(2,1)}, u32[]{:S(2)}, u32[]{:S(2)}) collective-permute-start(bf16[2,160,640]{2,1,0:T(8,128)(2,1)} %get-tuple-element.10), channel_id=1, source_target_pairs={{4,0},{8,4},{12,8},{14,12},{10,14},{6,10},{2,6},{0,2},{5,1},{9,5},... | collective-permute-start | bytes 1228808 | tf_op jit(solution)/shard_map/ppermute | solution.py:113
  96.7 8.0 %collective-permute-start.21 = (bf16[2,160,640]{2,1,0:T(8,128)(2,1)S(1)}, bf16[2,160,640]{2,1,0:T(8,128)(2,1)S(1)}, u32[]{:S(2)}, u32[]{:S(2)}) collective-permute-start(bf16[2,160,640]{2,1,0:T(8,128)(2,1)S(1)} %get-tuple-element.8), channel_id=1, source_target_pairs={{4,0},{8,4},{12,8},{14,12},{10,14},{6,10},{2,6},{0,2},{5,1},{9,5},... | collective-permute-start | bytes 1228808 | tf_op jit(solution)/shard_map/ppermute | solution.py:113
  97.2 8.0 %collective-permute-start.17 = (bf16[2,160,640]{2,1,0:T(8,128)(2,1)S(1)}, bf16[2,160,640]{2,1,0:T(8,128)(2,1)S(1)}, u32[]{:S(2)}, u32[]{:S(2)}) collective-permute-start(bf16[2,160,640]{2,1,0:T(8,128)(2,1)S(1)} %get-tuple-element.7), channel_id=1, source_target_pairs={{0,4},{4,8},{8,12},{12,14},{14,10},{10,6},{6,2},{2,0},{1,5},{5,9},... | collective-permute-start | bytes 1228808 | tf_op jit(solution)/shard_map/ppermute | solution.py:112
  100.3 9.4 %collective-permute-start.11 = (bf16[384,640]{1,0:T(8,128)(2,1)S(1)}, bf16[384,640]{1,0:T(8,128)(2,1)S(1)}, u32[]{:S(2)}, u32[]{:S(2)}) collective-permute-start(bf16[384,640]{1,0:T(8,128)(2,1)S(1)} %slice.167), channel_id=1, source_target_pairs={{0,16},{16,0},{1,17},{17,1},{2,18},{18,2},{3,19},{19,3},{4,20},{20... | collective-permute-start | bytes 1474568 | tf_op jit(solution)/shard_map/ppermute | solution.py:132
  105.3 6.5 %collective-permute-start.22 = (bf16[160,640]{1,0:T(8,128)(2,1)S(1)}, bf16[160,640]{1,0:T(8,128)(2,1)S(1)}, u32[]{:S(2)}, u32[]{:S(2)}) collective-permute-start(bf16[160,640]{1,0:T(8,128)(2,1)S(1)} %fusion.55), channel_id=1, source_target_pairs={{0,16},{16,0},{1,17},{17,1},{2,18},{18,2},{3,19},{19,3},{4,20},{20... | collective-permute-start | bytes 614408 | tf_op jit(solution)/shard_map/ppermute | solution.py:115
  (14 other events, 96.0 us)

commit v2 on v1

v2 whole, which is shorter than its diff:
```python
import jax
import jax.numpy as jnp
from jax import lax
from jax.sharding import PartitionSpec as P


def norm_rows(rows):
    values = rows.astype(jnp.float32)
    centre = jnp.mean(values, axis=-1, keepdims=True)
    shifted = values - centre
    variance = jnp.mean(shifted * shifted, axis=-1, keepdims=True)
    inv_std = lax.rsqrt(variance + 1e-05)
    return shifted * inv_std, inv_std


def gelu_slope(values):
    return (
        0.5 * (1.0 + lax.erf(values * 0.7071067811865476))
        + values * jnp.exp(-0.5 * values * values) * 0.3989422804014327
    )


def ring_member(place, count):
    place = place % count
    return jnp.where(place < count // 2, 2 * place, 2 * (count - 1 - place) + 1)


def shards(frames, out_grad, ln_gain, w_up, w_down, lengths):
    peers = lax.axis_size("gx")
    half = peers // 2
    own = lax.axis_index("gx")
    side = lax.axis_index("groups")
    core = lax.axis_index("gy")
    frame_len, width = frames.shape[1:]
    depth, hidden = w_up.shape
    quarter = hidden // 2
    half_width = width // 2
    bf16, f32 = jnp.bfloat16, jnp.float32

    order = list(range(0, peers, 2)) + list(range(peers - 1, 0, -2))
    ahead = [(order[i], order[(i + 1) % peers]) for i in range(peers)]
    behind = [(b, a) for a, b in ahead]
    place = jnp.where(own % 2 == 0, own // 2, peers - 1 - own // 2)
    swap = [(0, 1), (1, 0)]
    wire = bf16 if half <= 8 else f32

    mine = [lax.dynamic_slice_in_dim(w, side * quarter, quarter, 1) for w in (w_up, w_down)]
    mine, frames, out_grad = lax.optimization_barrier((mine, frames, out_grad))

    half_rows = frame_len // 2

    def fetch(rows):
        part = lax.dynamic_slice_in_dim(rows, core * half_rows, half_rows, 0)
        part = lax.ppermute(part, "groups", swap)
        return jnp.concatenate([part, lax.ppermute(part, "gy", swap)])

    length = lax.dynamic_index_in_dim(lengths, own, 0, keepdims=False)
    keep = (jnp.arange(frame_len, dtype=jnp.int32) < length)[:, None]
    grads = jnp.where(keep, out_grad[0], 0)
    other_grads = fetch(grads)
    centred, inv_std = norm_rows(frames[0])
    normed = (centred * ln_gain).astype(bf16)
    other_normed = fetch(normed)

    def put(full, block, step):
        row = ring_member(place + step + peers, peers) * depth
        return lax.dynamic_update_slice(full, block, (row, 0))

    blank = jnp.zeros((depth * peers, quarter), bf16)
    full = [put(blank, block, 0) for block in mine]
    up, down = list(mine), list(mine)
    for step in range(1, half):
        for i in range(2):
            up[i] = lax.ppermute(up[i], "gx", ahead)
            down[i] = lax.ppermute(down[i], "gx", behind)
        for i in range(2):
            full[i] = put(put(full[i], up[i], -step), down[i], step)
    full_up = put(full[0], lax.ppermute(up[0], "gx", ahead), half)
    full_down = put(full[1], lax.ppermute(down[1], "gx", behind), half)

    rows = [(normed, grads), (other_normed, other_grads)]
    d_pre, partial, second_sum = [None] * 2, [None] * 2, [None] * 2
    for i in (1, 0):
        pre_act = jnp.dot(rows[i][0], full_up, preferred_element_type=f32)
        d_act = jnp.dot(rows[i][1], full_down, preferred_element_type=f32)
        d_pre[i] = (d_act * gelu_slope(pre_act)).astype(bf16)
        second_sum[i] = jnp.sum(d_pre[i].astype(f32) * pre_act, axis=-1)
        partial[i] = lax.dot_general(
            rows[i][0], d_pre[i], (((0,), (0,)), ((), ())), preferred_element_type=f32
        )

    def term(i, step):
        row = ring_member(place + step + peers, peers) * depth
        return lax.dynamic_slice_in_dim(partial[i], row, depth, 0)

    up, down = [None] * 2, [None] * 2
    down[1] = lax.ppermute(term(1, half).astype(wire), "gx", behind)
    up[0] = lax.ppermute(term(0, half).astype(wire), "gx", ahead)
    for step in range(half - 1, 0, -1):
        for i in (1, 0):
            for way, at, pairs in ((up, step, ahead), (down, -step, behind)):
                value = term(i, at)
                if way[i] is not None:
                    value = value + way[i].astype(f32)
                way[i] = lax.ppermute(value.astype(wire), "gx", pairs)
    total = [term(i, 0) + up[i].astype(f32) + down[i].astype(f32) for i in range(2)]
    passed = lax.ppermute(total[1].astype(wire), "groups", swap).astype(f32)
    low = jnp.where(side == 0, total[0], passed)
    high = jnp.where(side == 0, passed, total[0])
    up_grad = jnp.concatenate([low, high], axis=1)

    def swap_halves(array):
        return jnp.concatenate([array[half_rows:], array[:half_rows]])

    cols, sums = [None] * 2, [None] * 2
    for i in (1, 0):
        d_norm = lax.dot_general(
            d_pre[i], full_up, (((1,), (1,)), ((), ())), preferred_element_type=f32
        )
        first_sum = jnp.sum(d_norm * ln_gain, axis=-1)
        sums[i] = jnp.stack([first_sum, second_sum[i]], axis=1)
        mine_cols = lax.dynamic_slice_in_dim(d_norm, core * half_width, half_width, 1)
        send = lax.dynamic_slice_in_dim(d_norm, (1 - core) * half_width, half_width, 1)
        came = lax.ppermute(send.astype(bf16), "gy", swap)
        came_sums = lax.ppermute(sums[i], "gy", swap)
        if i == 1:
            came, came_sums = swap_halves(came), swap_halves(came_sums)
        cols[i] = mine_cols + came.astype(f32)
        sums[i] = sums[i] + came_sums

    def in_order(array):
        return jnp.where(core == 0, array, swap_halves(array))

    back = lax.ppermute(in_order(cols[1].astype(bf16)), "groups", swap)
    means = (sums[0] + lax.ppermute(in_order(sums[1]), "groups", swap)) / width

    def own_cols(array):
        return lax.dynamic_slice_in_dim(array, core * half_width, half_width, array.ndim - 1)

    scaled = (cols[0] + back.astype(f32)) * own_cols(ln_gain)
    input_grad = own_cols(grads).astype(f32) + inv_std * (
        scaled - means[:, :1] - own_cols(centred) * means[:, 1:]
    )
    return (input_grad.astype(bf16)[None], up_grad)


def solution(mesh):
    placed = (
        P(("groups", "gx"), None, None),
        P(("groups", "gx"), None, None),
        P(),
        P("gx", "gy"),
        P("gx", "gy"),
        P("groups"),
    )
    return jax.shard_map(
        shards,
        mesh=mesh,
        in_specs=placed,
        out_specs=(P(("groups", "gx"), None, "gy"), P(("groups", "gx"), "gy")),
        check_vma=False,
    )
```

time: 113 us -> 117 us (1.035)
  starting transfers between devices: 24.2 us -> 38.3 us
  other arithmetic: 18.8 us -> 8.72 us
  waiting for transfers between devices: 51.1 us -> 42.5 us
  local copies, waits for them, and re-layouts: 10.1 us -> 14.5 us
  matrix products: 7.7 us -> 11.5 us
    ppermute x22 -> x38, starting transfers between devices: 22.8 us -> 36.9 us  [the longest x12 14.1 us: shards(): way[i] = lax.ppermute(value.astype(wire), 'gx', pairs)]
    ppermute x22 -> x38, waiting for transfers between devices: 50.1 us -> 40.1 us  [the longest x12 28.3 us: shards(): way[i] = lax.ppermute(value.astype(wire), 'gx', pairs)]
    dynamic_update_slice x8 -> x16, local copies, waits for them, and re-layouts: 4.38 us -> 9.64 us  [put(): return lax.dynamic_update_slice(full, block, (row, 0))]
    select_n x2 -> x3, other arithmetic: 6.58 us -> 1.53 us  [the longest x1 1.33 us: shards(): grads = jnp.where(keep, out_grad[0], 0)]
    dot_general x5 -> x8, matrix products: 7.7 us -> 11.5 us  [the longest x2 5.22 us: shards(): d_act = jnp.dot(rows[i][1], full_down, preferred_element_type=f32)]
    convert_element_type x2 -> x10, other arithmetic: 2.65 us -> 0.69 us  [the longest x8 0.48 us: shards(): way[i] = lax.ppermute(value.astype(wire), 'gx', pairs)]
    add x3 -> x1, other arithmetic: 1.55 us -> 0.08 us  [shards(): sums[i] = sums[i] + came_sums]
    ppermute x1, waiting for transfers between devices: 1.04 us -> 2.43 us  [shards(): passed = lax.ppermute(total[1].astype(wire), 'groups', swap).astype(f32)]
  transfers between devices with their start and end apart: 23 -> 39, of which waited for: 15 -> 14; matrix products, arithmetic and copies ran while one was open for 14% -> 28% of each run, Pallas kernels for 0% -> 0%
where the time goes in v2:
time: 117 us
  waiting for transfers between devices  42.5 us (36%)
  starting transfers between devices  38.3 us (33%)
  local copies, waits for them, and re-layouts  14.5 us (12%)
  matrix products  11.5 us (10%)
  other arithmetic  8.72 us (7%)
    ppermute x12, waiting for transfers between devices, shards(): way[i] = lax.ppermute(value.astype(wire), 'gx', pairs)  28.3 us
    ppermute x12, starting transfers between devices, shards(): way[i] = lax.ppermute(value.astype(wire), 'gx', pairs)  14.1 us
    ppermute x6, starting transfers between devices, shards(): down[i] = lax.ppermute(down[i], 'gx', behind)  9.94 us
    dynamic_update_slice x16, local copies, waits for them, and re-layouts, put(): return lax.dynamic_update_slice(full, block, (row, 0))  9.64 us
    dot_general x2, matrix products, shards(): d_act = jnp.dot(rows[i][1], full_down, preferred_element_type=f32)  5.22 us
    ppermute x1, waiting for transfers between devices, shards(): full_up = put(full[0], lax.ppermute(up[0], 'gx', ahead), half)  4.04 us
    ppermute x2, waiting for transfers between devices, fetch(): part = lax.ppermute(part, 'groups', swap)  3.52 us
    ppermute x6, starting transfers between devices, shards(): up[i] = lax.ppermute(up[i], 'gx', ahead)  3.38 us
  transfers between devices with their start and end apart: 39, of which 14 were waited for; matrix products, arithmetic and copies ran while one was open for 28% of the time, Pallas kernels for 0%

profile of v2, /device:TPU:0, one launch (start us, length us, event | category | flops | bytes accessed | tf_op | source)
XLA Modules:
  0.0 116.6 jit_solution(15719178534504215972)
XLA Ops:
  1.8 3.0 %collective-permute-start.1 = (bf16[160,640]{1,0:T(8,128)(2,1)S(1)}, bf16[160,640]{1,0:T(8,128)(2,1)}, u32[]{:S(2)}, u32[]{:S(2)}) collective-permute-start(bf16[160,640]{1,0:T(8,128)(2,1)S(1)} %get-tuple-element.8), channel_id=1, source_target_pairs={{4,0},{8,4},{12,8},{14,12},{10,14},{6,10},{2,6},{0,2},{5,1},{9,5},... | collective-permute-start | bytes 614408 | tf_op jit(solution)/shard_map/ppermute | solution.py:75
  5.0 1.9 %collective-permute-start.8 = (bf16[160,640]{1,0:T(8,128)(2,1)S(1)}, bf16[160,640]{1,0:T(8,128)(2,1)}, u32[]{:S(2)}, u32[]{:S(2)}) collective-permute-start(bf16[160,640]{1,0:T(8,128)(2,1)S(1)} %get-tuple-element.9), channel_id=1, source_target_pairs={{4,0},{8,4},{12,8},{14,12},{10,14},{6,10},{2,6},{0,2},{5,1},{9,5},... | collective-permute-start | bytes 614408 | tf_op jit(solution)/shard_map/ppermute | solution.py:75
  8.8 1.7 %fusion.1 = (f32[384,1280]{1,0:T(8,128)}, bf16[384,1280]{1,0:T(8,128)(2,1)S(1)}) fusion(bf16[1,384,1280]{2,1,0:T(8,128)(2,1)S(1)} %copy-done, f32[384]{0:T(512)S(1)} %add_rsqrt_fusion, f32[384]{0:T(512)S(1)} %broadcast_multiply_fusion, f32[1280]{0:T(1024)S(1)} %copy-done.2), kind=kLoop, calls=%fused_computation.3 | loop fusion | flops 2457600 | bytes 3940352 | tf_op jit(solution)/shard_map/mul | solution.py:13
  10.5 1.9 %collective-permute-start.17 = (bf16[192,1280]{1,0:T(8,128)(2,1)S(1)}, bf16[192,1280]{1,0:T(8,128)(2,1)}, u32[]{:S(2)}, u32[]{:S(2)}) collective-permute-start(bf16[192,1280]{1,0:T(8,128)(2,1)S(1)} %constant_dynamic-slice_fusion), channel_id=1, source_target_pairs={{0,16},{16,0},{1,17},{17,1},{2,18},{18,2},{3,19},{19,3},{4,20},{20... | collective-permute-start | bytes 1474568 | tf_op jit(solution)/shard_map/ppermute | solution.py:54
  17.4 1.6 %collective-permute-start.3 = (bf16[160,640]{1,0:T(8,128)(2,1)}, bf16[160,640]{1,0:T(8,128)(2,1)S(1)}, u32[]{:S(2)}, u32[]{:S(2)}) collective-permute-start(bf16[160,640]{1,0:T(8,128)(2,1)} %collective-permute-done.1), channel_id=1, source_target_pairs={{4,0},{8,4},{12,8},{14,12},{10,14},{6,10},{2,6},{0,2},{5,1},{9,5},... | collective-permute-start | bytes 614408 | tf_op jit(solution)/shard_map/ppermute | solution.py:75
  22.5 1.6 %constant_dynamic-update-slice_fusion.14 = bf16[1280,640]{1,0:T(8,128)(2,1)} fusion(bf16[1280,640]{1,0:T(8,128)(2,1)} %constant_dynamic-update-slice_fusion.15, bf16[160,640]{1,0:T(8,128)(2,1)} %collective-permute-done, s32[]{:T(128)S(6)} %select_n.258), kind=kLoop, calls=%fused_computation.70 | loop fusion | bytes 409604 | tf_op jit(solution)/shard_map/dynamic_update_slice | solution.py:67
  25.1 1.7 %constant_dynamic-update-slice_fusion.13 = bf16[1280,640]{1,0:T(8,128)(2,1)} fusion(bf16[1280,640]{1,0:T(8,128)(2,1)} %constant_dynamic-update-slice_fusion.14, bf16[160,640]{1,0:T(8,128)(2,1)} %collective-permute-done.1, s32[]{:T(128)S(6)} %select_n.261), kind=kLoop, calls=%fused_computation.69 | loop fusion | bytes 409604 | tf_op jit(solution)/shard_map/dynamic_update_slice | solution.py:67
  27.7 1.8 %collective-permute-start.4 = (bf16[160,640]{1,0:T(8,128)(2,1)S(1)}, bf16[160,640]{1,0:T(8,128)(2,1)S(1)}, u32[]{:S(2)}, u32[]{:S(2)}) collective-permute-start(bf16[160,640]{1,0:T(8,128)(2,1)S(1)} %collective-permute-done.2), channel_id=1, source_target_pairs={{0,4},{4,8},{8,12},{12,14},{14,10},{10,6},{6,2},{2,0},{1,5},{5,9},... | collective-permute-start | bytes 614408 | tf_op jit(solution)/shard_map/ppermute | solution.py:74
  29.8 1.7 %collective-permute-start.12 = (bf16[160,640]{1,0:T(8,128)(2,1)S(1)}, bf16[160,640]{1,0:T(8,128)(2,1)S(1)}, u32[]{:S(2)}, u32[]{:S(2)}) collective-permute-start(bf16[160,640]{1,0:T(8,128)(2,1)S(1)} %collective-permute-done.10), channel_id=1, source_target_pairs={{4,0},{8,4},{12,8},{14,12},{10,14},{6,10},{2,6},{0,2},{5,1},{9,5},... | collective-permute-start | bytes 614408 | tf_op jit(solution)/shard_map/ppermute | solution.py:75
  33.6 3.5 %collective-permute-done.15 = bf16[192,1280]{1,0:T(8,128)(2,1)S(1)} collective-permute-done((bf16[192,1280]{1,0:T(8,128)(2,1)S(1)}, bf16[192,1280]{1,0:T(8,128)(2,1)S(1)}, u32[]{:S(2)}, u32[]{:S(2)}) %collective-permute-start.15) | collective-permute-done | bytes 491552 | tf_op jit(solution)/shard_map/ppermute | solution.py:54
  41.6 4.0 %collective-permute-done.13 = bf16[160,640]{1,0:T(8,128)(2,1)S(1)} collective-permute-done((bf16[160,640]{1,0:T(8,128)(2,1)S(1)}, bf16[160,640]{1,0:T(8,128)(2,1)S(1)}, u32[]{:S(2)}, u32[]{:S(2)}) %collective-permute-start.13) | collective-permute-done | bytes 204832 | tf_op jit(solution)/shard_map/ppermute | solution.py:78
  47.3 2.6 %multiply_reduce_fusion.3 = (f32[384]{0:T(512)S(1)}, bf16[384,640]{1,0:T(8,128)(2,1)S(1)}) fusion(f32[384,640]{1,0:T(8,128)S(1)} %fusion.23, bf16[384,1280]{1,0:T(8,128)(2,1)S(1)} %bitcast_select_fusion, bf16[1280,640]{1,0:T(8,128)(2,1)} %constant_dynamic-update-slice_fusion.8), kind=kOutput, calls=%fused_computation.29 | convolution fusion | flops 632340096 | bytes 4097536 | tf_op jit(solution)/shard_map/dot_general | solution.py:85
  54.3 2.6 %multiply_reduce_fusion.2 = (f32[384]{0:T(512)S(1)}, bf16[384,640]{1,0:T(8,128)(2,1)S(1)}) fusion(f32[384,640]{1,0:T(8,128)S(1)} %fusion.24, bf16[1280,640]{1,0:T(8,128)(2,1)} %constant_dynamic-update-slice_fusion.8, bf16[192,1280]{1,0:T(8,128)(2,1)S(1)} %collective-permute-done.16, bf16[192,1280]{1,0:T(8,128)(2,1)S(1)} %collective-permute-done.15), kind=kOutput, calls=%fused_computation.28 | convolution fusion | flops 634306176 | bytes 4097536 | tf_op jit(solution)/shard_map/dot_general | solution.py:85
  63.7 1.9 %collective-permute-done.23 = f32[384,2]{0,1:T(2,128)S(1)} collective-permute-done((f32[384,2]{0,1:T(2,128)S(1)}, f32[384,2]{0,1:T(2,128)S(1)}, u32[]{:S(2)}, u32[]{:S(2)}) %collective-permute-start.23) | collective-permute-done | bytes 3104 | tf_op jit(solution)/shard_map/ppermute | solution.py:135
  67.7 4.0 %collective-permute-done.31 = bf16[160,640]{1,0:T(8,128)(2,1)S(1)} collective-permute-done((bf16[160,640]{1,0:T(8,128)(2,1)S(1)}, bf16[160,640]{1,0:T(8,128)(2,1)S(1)}, u32[]{:S(2)}, u32[]{:S(2)}) %collective-permute-start.31) | collective-permute-done | bytes 204832 | tf_op jit(solution)/shard_map/ppermute | solution.py:105
  72.8 4.9 %collective-permute-done.25 = bf16[160,640]{1,0:T(8,128)(2,1)S(1)} collective-permute-done((bf16[160,640]{1,0:T(8,128)(2,1)S(1)}, bf16[160,640]{1,0:T(8,128)(2,1)S(1)}, u32[]{:S(2)}, u32[]{:S(2)}) %collective-permute-start.25) | collective-permute-done | bytes 204832 | tf_op jit(solution)/shard_map/ppermute | solution.py:105
  78.8 1.7 %collective-permute-start.26 = (bf16[160,640]{1,0:T(8,128)(2,1)S(1)}, bf16[160,640]{1,0:T(8,128)(2,1)S(1)}, u32[]{:S(2)}, u32[]{:S(2)}) collective-permute-start(bf16[160,640]{1,0:T(8,128)(2,1)S(1)} %add_convert_fusion.11), channel_id=1, source_target_pairs={{0,4},{4,8},{8,12},{12,14},{14,10},{10,6},{6,2},{2,0},{1,5},{5,9},... | collective-permute-start | bytes 614408 | tf_op jit(solution)/shard_map/ppermute | solution.py:105
  80.4 5.3 %collective-permute-done.32 = bf16[160,640]{1,0:T(8,128)(2,1)S(1)} collective-permute-done((bf16[160,640]{1,0:T(8,128)(2,1)S(1)}, bf16[160,640]{1,0:T(8,128)(2,1)S(1)}, u32[]{:S(2)}, u32[]{:S(2)}) %collective-permute-start.32) | collective-permute-done | bytes 204832 | tf_op jit(solution)/shard_map/ppermute | solution.py:105
  87.9 2.2 %collective-permute-done.26 = bf16[160,640]{1,0:T(8,128)(2,1)S(1)} collective-permute-done((bf16[160,640]{1,0:T(8,128)(2,1)S(1)}, bf16[160,640]{1,0:T(8,128)(2,1)S(1)}, u32[]{:S(2)}, u32[]{:S(2)}) %collective-permute-start.26) | collective-permute-done | bytes 204832 | tf_op jit(solution)/shard_map/ppermute | solution.py:105
  92.7 1.5 %collective-permute-start.36 = (bf16[160,640]{1,0:T(8,128)(2,1)S(1)}, bf16[160,640]{1,0:T(8,128)(2,1)S(1)}, u32[]{:S(2)}, u32[]{:S(2)}) collective-permute-start(bf16[160,640]{1,0:T(8,128)(2,1)S(1)} %add_convert_fusion.4), channel_id=1, source_target_pairs={{4,0},{8,4},{12,8},{14,12},{10,14},{6,10},{2,6},{0,2},{5,1},{9,5},... | collective-permute-start | bytes 614408 | tf_op jit(solution)/shard_map/ppermute | solution.py:105
  94.4 8.7 %collective-permute-done.36 = bf16[160,640]{1,0:T(8,128)(2,1)S(1)} collective-permute-done((bf16[160,640]{1,0:T(8,128)(2,1)S(1)}, bf16[160,640]{1,0:T(8,128)(2,1)S(1)}, u32[]{:S(2)}, u32[]{:S(2)}) %collective-permute-start.36) | collective-permute-done | bytes 204832 | tf_op jit(solution)/shard_map/ppermute | solution.py:105
  104.9 1.6 %collective-permute-start.30 = (bf16[160,640]{1,0:T(8,128)(2,1)S(1)}, bf16[160,640]{1,0:T(8,128)(2,1)S(1)}, u32[]{:S(2)}, u32[]{:S(2)}) collective-permute-start(bf16[160,640]{1,0:T(8,128)(2,1)S(1)} %add_convert_fusion.8), channel_id=1, source_target_pairs={{4,0},{8,4},{12,8},{14,12},{10,14},{6,10},{2,6},{0,2},{5,1},{9,5},... | collective-permute-start | bytes 614408 | tf_op jit(solution)/shard_map/ppermute | solution.py:105
  106.6 3.0 %collective-permute-done.37 = bf16[160,640]{1,0:T(8,128)(2,1)S(1)} collective-permute-done((bf16[160,640]{1,0:T(8,128)(2,1)S(1)}, bf16[160,640]{1,0:T(8,128)(2,1)S(1)}, u32[]{:S(2)}, u32[]{:S(2)}) %collective-permute-start.37) | collective-permute-done | bytes 204832 | tf_op jit(solution)/shard_map/ppermute | solution.py:105
  113.1 2.4 %collective-permute-done.38 = bf16[160,640]{1,0:T(8,128)(2,1)S(1)} collective-permute-done((bf16[160,640]{1,0:T(8,128)(2,1)S(1)}, bf16[160,640]{1,0:T(8,128)(2,1)S(1)}, u32[]{:S(2)}, u32[]{:S(2)}) %collective-permute-start.38) | collective-permute-done | bytes 204832 | tf_op jit(solution)/shard_map/ppermute | solution.py:107
  (134 shorter events, 48.6 us)
Async XLA Ops:
  1.8 15.5 %collective-permute-start.1 = (bf16[160,640]{1,0:T(8,128)(2,1)S(1)}, bf16[160,640]{1,0:T(8,128)(2,1)}, u32[]{:S(2)}, u32[]{:S(2)}) collective-permute-start(bf16[160,640]{1,0:T(8,128)(2,1)S(1)} %get-tuple-element.8), channel_id=1, source_target_pairs={{4,0},{8,4},{12,8},{14,12},{10,14},{6,10},{2,6},{0,2},{5,1},{9,5},... | collective-permute-start | bytes 614408 | tf_op jit(solution)/shard_map/ppermute | solution.py:75
  4.8 14.1 %collective-permute-start = (bf16[160,640]{1,0:T(8,128)(2,1)S(1)}, bf16[160,640]{1,0:T(8,128)(2,1)}, u32[]{:S(2)}, u32[]{:S(2)}) collective-permute-start(bf16[160,640]{1,0:T(8,128)(2,1)S(1)} %get-tuple-element.8), channel_id=1, source_target_pairs={{0,4},{4,8},{8,12},{12,14},{14,10},{10,6},{6,2},{2,0},{1,5},{5,9},... | collective-permute-start | bytes 614408 | tf_op jit(solution)/shard_map/ppermute | solution.py:74
  5.0 14.5 %collective-permute-start.8 = (bf16[160,640]{1,0:T(8,128)(2,1)S(1)}, bf16[160,640]{1,0:T(8,128)(2,1)}, u32[]{:S(2)}, u32[]{:S(2)}) collective-permute-start(bf16[160,640]{1,0:T(8,128)(2,1)S(1)} %get-tuple-element.9), channel_id=1, source_target_pairs={{4,0},{8,4},{12,8},{14,12},{10,14},{6,10},{2,6},{0,2},{5,1},{9,5},... | collective-permute-start | bytes 614408 | tf_op jit(solution)/shard_map/ppermute | solution.py:75
  6.9 14.1 %collective-permute-start.7 = (bf16[160,640]{1,0:T(8,128)(2,1)S(1)}, bf16[160,640]{1,0:T(8,128)(2,1)}, u32[]{:S(2)}, u32[]{:S(2)}) collective-permute-start(bf16[160,640]{1,0:T(8,128)(2,1)S(1)} %get-tuple-element.9), channel_id=1, source_target_pairs={{0,4},{4,8},{8,12},{12,14},{14,10},{10,6},{6,2},{2,0},{1,5},{5,9},... | collective-permute-start | bytes 614408 | tf_op jit(solution)/shard_map/ppermute | solution.py:74
  10.5 21.8 %collective-permute-start.17 = (bf16[192,1280]{1,0:T(8,128)(2,1)S(1)}, bf16[192,1280]{1,0:T(8,128)(2,1)}, u32[]{:S(2)}, u32[]{:S(2)}) collective-permute-start(bf16[192,1280]{1,0:T(8,128)(2,1)S(1)} %constant_dynamic-slice_fusion), channel_id=1, source_target_pairs={{0,16},{16,0},{1,17},{17,1},{2,18},{18,2},{3,19},{19,3},{4,20},{20... | collective-permute-start | bytes 1474568 | tf_op jit(solution)/shard_map/ppermute | solution.py:54
  17.4 10.4 %collective-permute-start.3 = (bf16[160,640]{1,0:T(8,128)(2,1)}, bf16[160,640]{1,0:T(8,128)(2,1)S(1)}, u32[]{:S(2)}, u32[]{:S(2)}) collective-permute-start(bf16[160,640]{1,0:T(8,128)(2,1)} %collective-permute-done.1), channel_id=1, source_target_pairs={{4,0},{8,4},{12,8},{14,12},{10,14},{6,10},{2,6},{0,2},{5,1},{9,5},... | collective-permute-start | bytes 614408 | tf_op jit(solution)/shard_map/ppermute | solution.py:75
  19.4 10.1 %collective-permute-start.10 = (bf16[160,640]{1,0:T(8,128)(2,1)}, bf16[160,640]{1,0:T(8,128)(2,1)S(1)}, u32[]{:S(2)}, u32[]{:S(2)}) collective-permute-start(bf16[160,640]{1,0:T(8,128)(2,1)} %collective-permute-done.8), channel_id=1, source_target_pairs={{4,0},{8,4},{12,8},{14,12},{10,14},{6,10},{2,6},{0,2},{5,1},{9,5},... | collective-permute-start | bytes 614408 | tf_op jit(solution)/shard_map/ppermute | solution.py:75
  21.0 8.8 %collective-permute-start.9 = (bf16[160,640]{1,0:T(8,128)(2,1)}, bf16[160,640]{1,0:T(8,128)(2,1)S(1)}, u32[]{:S(2)}, u32[]{:S(2)}) collective-permute-start(bf16[160,640]{1,0:T(8,128)(2,1)} %collective-permute-done.7), channel_id=1, source_target_pairs={{0,4},{4,8},{8,12},{12,14},{14,10},{10,6},{6,2},{2,0},{1,5},{5,9},... | collective-permute-start | bytes 614408 | tf_op jit(solution)/shard_map/ppermute | solution.py:74
  26.7 10.4 %collective-permute-start.15 = (bf16[192,1280]{1,0:T(8,128)(2,1)S(1)}, bf16[192,1280]{1,0:T(8,128)(2,1)S(1)}, u32[]{:S(2)}, u32[]{:S(2)}) collective-permute-start(bf16[192,1280]{1,0:T(8,128)(2,1)S(1)} %constant_dynamic-slice_fusion.1), channel_id=1, source_target_pairs={{0,16},{16,0},{1,17},{17,1},{2,18},{18,2},{3,19},{19,3},{4,20},{20... | collective-permute-start | bytes 1474568 | tf_op jit(solution)/shard_map/ppermute | solution.py:54
  27.7 11.6 %collective-permute-start.4 = (bf16[160,640]{1,0:T(8,128)(2,1)S(1)}, bf16[160,640]{1,0:T(8,128)(2,1)S(1)}, u32[]{:S(2)}, u32[]{:S(2)}) collective-permute-start(bf16[160,640]{1,0:T(8,128)(2,1)S(1)} %collective-permute-done.2), channel_id=1, source_target_pairs={{0,4},{4,8},{8,12},{12,14},{14,10},{10,6},{6,2},{2,0},{1,5},{5,9},... | collective-permute-start | bytes 614408 | tf_op jit(solution)/shard_map/ppermute | solution.py:74
  29.8 11.8 %collective-permute-start.12 = (bf16[160,640]{1,0:T(8,128)(2,1)S(1)}, bf16[160,640]{1,0:T(8,128)(2,1)S(1)}, u32[]{:S(2)}, u32[]{:S(2)}) collective-permute-start(bf16[160,640]{1,0:T(8,128)(2,1)S(1)} %collective-permute-done.10), channel_id=1, source_target_pairs={{4,0},{8,4},{12,8},{14,12},{10,14},{6,10},{2,6},{0,2},{5,1},{9,5},... | collective-permute-start | bytes 614408 | tf_op jit(solution)/shard_map/ppermute | solution.py:75
  37.2 16.1 %collective-permute-start.18 = (bf16[192,1280]{1,0:T(8,128)(2,1)}, bf16[192,1280]{1,0:T(8,128)(2,1)S(1)}, u32[]{:S(2)}, u32[]{:S(2)}) collective-permute-start(bf16[192,1280]{1,0:T(8,128)(2,1)} %collective-permute-done.17), channel_id=1, source_target_pairs={{0,1},{1,0},{2,3},{3,2},{4,5},{5,4},{6,7},{7,6},{8,9},{9,8},{10,11... | collective-permute-start | bytes 1474568 | tf_op jit(solution)/shard_map/ppermute | solution.py:55
  38.0 16.2 %collective-permute-start.16 = (bf16[192,1280]{1,0:T(8,128)(2,1)S(1)}, bf16[192,1280]{1,0:T(8,128)(2,1)S(1)}, u32[]{:S(2)}, u32[]{:S(2)}) collective-permute-start(bf16[192,1280]{1,0:T(8,128)(2,1)S(1)} %collective-permute-done.15), channel_id=1, source_target_pairs={{0,1},{1,0},{2,3},{3,2},{4,5},{5,4},{6,7},{7,6},{8,9},{9,8},{10,11... | collective-permute-start | bytes 1474568 | tf_op jit(solution)/shard_map/ppermute | solution.py:55
  51.2 15.4 %collective-permute-start.24 = (bf16[160,640]{1,0:T(8,128)(2,1)S(1)}, bf16[160,640]{1,0:T(8,128)(2,1)S(1)}, u32[]{:S(2)}, u32[]{:S(2)}) collective-permute-start(bf16[160,640]{1,0:T(8,128)(2,1)S(1)} %get-tuple-element.18), channel_id=1, source_target_pairs={{0,4},{4,8},{8,12},{12,14},{14,10},{10,6},{6,2},{2,0},{1,5},{5,9},... | collective-permute-start | bytes 614408 | tf_op jit(solution)/shard_map/ppermute | solution.py:98
  52.2 34.7 %collective-permute-start.28 = (bf16[160,640]{1,0:T(8,128)(2,1)S(1)}, bf16[160,640]{1,0:T(8,128)(2,1)S(1)}, u32[]{:S(2)}, u32[]{:S(2)}) collective-permute-start(bf16[160,640]{1,0:T(8,128)(2,1)S(1)} %get-tuple-element.19), channel_id=1, source_target_pairs={{4,0},{8,4},{12,8},{14,12},{10,14},{6,10},{2,6},{0,2},{5,1},{9,5},... | collective-permute-start | bytes 614408 | tf_op jit(solution)/shard_map/ppermute | solution.py:105
  61.0 30.3 %collective-permute-start.19 = (bf16[384,640]{1,0:T(8,128)(2,1)S(1)}, bf16[384,640]{1,0:T(8,128)(2,1)S(1)}, u32[]{:S(2)}, u32[]{:S(2)}) collective-permute-start(bf16[384,640]{1,0:T(8,128)(2,1)S(1)} %dynamic-slice_convert_fusion), channel_id=1, source_target_pairs={{0,1},{1,0},{2,3},{3,2},{4,5},{5,4},{6,7},{7,6},{8,9},{9,8},{10,11... | collective-permute-start | bytes 1474568 | tf_op jit(solution)/shard_map/ppermute | solution.py:124
  63.5 47.6 %collective-permute-start.14 = (bf16[384,640]{1,0:T(8,128)(2,1)S(1)}, bf16[384,640]{1,0:T(8,128)(2,1)S(1)}, u32[]{:S(2)}, u32[]{:S(2)}) collective-permute-start(bf16[384,640]{1,0:T(8,128)(2,1)S(1)} %dynamic-slice_convert_fusion.1), channel_id=1, source_target_pairs={{0,1},{1,0},{2,3},{3,2},{4,5},{5,4},{6,7},{7,6},{8,9},{9,8},{10,11... | collective-permute-start | bytes 1474568 | tf_op jit(solution)/shard_map/ppermute | solution.py:124
  66.6 12.2 %collective-permute-start.34 = (bf16[160,640]{1,0:T(8,128)(2,1)S(1)}, bf16[160,640]{1,0:T(8,128)(2,1)S(1)}, u32[]{:S(2)}, u32[]{:S(2)}) collective-permute-start(bf16[160,640]{1,0:T(8,128)(2,1)S(1)} %get-tuple-element.23), channel_id=1, source_target_pairs={{4,0},{8,4},{12,8},{14,12},{10,14},{6,10},{2,6},{0,2},{5,1},{9,5},... | collective-permute-start | bytes 614408 | tf_op jit(solution)/shard_map/ppermute | solution.py:97
  78.8 11.3 %collective-permute-start.26 = (bf16[160,640]{1,0:T(8,128)(2,1)S(1)}, bf16[160,640]{1,0:T(8,128)(2,1)S(1)}, u32[]{:S(2)}, u32[]{:S(2)}) collective-permute-start(bf16[160,640]{1,0:T(8,128)(2,1)S(1)} %add_convert_fusion.11), channel_id=1, source_target_pairs={{0,4},{4,8},{8,12},{12,14},{14,10},{10,6},{6,2},{2,0},{1,5},{5,9},... | collective-permute-start | bytes 614408 | tf_op jit(solution)/shard_map/ppermute | solution.py:105
  85.8 19.1 %collective-permute-start.33 = (bf16[160,640]{1,0:T(8,128)(2,1)S(1)}, bf16[160,640]{1,0:T(8,128)(2,1)S(1)}, u32[]{:S(2)}, u32[]{:S(2)}) collective-permute-start(bf16[160,640]{1,0:T(8,128)(2,1)S(1)} %get-tuple-element.20), channel_id=1, source_target_pairs={{0,4},{4,8},{8,12},{12,14},{14,10},{10,6},{6,2},{2,0},{1,5},{5,9},... | collective-permute-start | bytes 614408 | tf_op jit(solution)/shard_map/ppermute | solution.py:105
  90.2 22.9 %collective-permute-start.27 = (bf16[160,640]{1,0:T(8,128)(2,1)S(1)}, bf16[160,640]{1,0:T(8,128)(2,1)S(1)}, u32[]{:S(2)}, u32[]{:S(2)}) collective-permute-start(bf16[160,640]{1,0:T(8,128)(2,1)S(1)} %get-tuple-element.16), channel_id=1, source_target_pairs={{0,4},{4,8},{8,12},{12,14},{14,10},{10,6},{6,2},{2,0},{1,5},{5,9},... | collective-permute-start | bytes 614408 | tf_op jit(solution)/shard_map/ppermute | solution.py:105
  91.3 12.5 %collective-permute-start.29 = (bf16[160,640]{1,0:T(8,128)(2,1)S(1)}, bf16[160,640]{1,0:T(8,128)(2,1)S(1)}, u32[]{:S(2)}, u32[]{:S(2)}) collective-permute-start(bf16[160,640]{1,0:T(8,128)(2,1)S(1)} %get-tuple-element.17), channel_id=1, source_target_pairs={{4,0},{8,4},{12,8},{14,12},{10,14},{6,10},{2,6},{0,2},{5,1},{9,5},... | collective-permute-start | bytes 614408 | tf_op jit(solution)/shard_map/ppermute | solution.py:105
  92.7 10.3 %collective-permute-start.36 = (bf16[160,640]{1,0:T(8,128)(2,1)S(1)}, bf16[160,640]{1,0:T(8,128)(2,1)S(1)}, u32[]{:S(2)}, u32[]{:S(2)}) collective-permute-start(bf16[160,640]{1,0:T(8,128)(2,1)S(1)} %add_convert_fusion.4), channel_id=1, source_target_pairs={{4,0},{8,4},{12,8},{14,12},{10,14},{6,10},{2,6},{0,2},{5,1},{9,5},... | collective-permute-start | bytes 614408 | tf_op jit(solution)/shard_map/ppermute | solution.py:105
  103.1 8.8 %collective-permute-start.20 = (bf16[384,640]{1,0:T(8,128)(2,1)S(1)}, bf16[384,640]{1,0:T(8,128)(2,1)S(1)}, u32[]{:S(2)}, u32[]{:S(2)}) collective-permute-start(bf16[384,640]{1,0:T(8,128)(2,1)S(1)} %maximum_select_fusion), channel_id=1, source_target_pairs={{0,16},{16,0},{1,17},{17,1},{2,18},{18,2},{3,19},{19,3},{4,20},{20... | collective-permute-start | bytes 1474568 | tf_op jit(solution)/shard_map/ppermute | solution.py:134
  (19 other events, 128.0 us)

commit v3 on v0

v3 whole, which is shorter than its diff:
```python
import functools

import jax
import jax.numpy as jnp
from jax import lax
from jax.experimental import pallas as pl
from jax.experimental.pallas import tpu as pltpu
from jax.sharding import PartitionSpec as P

BF16, F32 = jnp.bfloat16, jnp.float32
VMEM = pl.BlockSpec(memory_space=pltpu.VMEM)
SMEM = pl.BlockSpec(memory_space=pltpu.SMEM)


def shape(dims, kind):
    return jax.ShapeDtypeStruct(dims, kind)


def call(kernel, ins, out_shape, flops, scratch=(), vmem=32, aliases=None):
    outs = jax.tree.leaves(out_shape)
    moved = sum(x.size * x.dtype.itemsize for x in list(ins) + outs)
    return pl.pallas_call(
        kernel,
        out_shape=out_shape,
        in_specs=[SMEM if x.dtype == jnp.int32 else VMEM for x in ins],
        out_specs=jax.tree.map(lambda _: VMEM, out_shape),
        scratch_shapes=list(scratch),
        input_output_aliases=aliases or {},
        compiler_params=pltpu.CompilerParams(vmem_limit_bytes=vmem << 20),
        cost_estimate=pl.CostEstimate(flops=flops, bytes_accessed=moved, transcendentals=0),
    )(*ins)


def dot(left, right, left_dim=1, right_dim=0):
    return lax.dot_general(
        left, right, (((left_dim,), (right_dim,)), ((), ())), preferred_element_type=F32
    )


def gelu_slope(values):
    return (
        0.5 * (1.0 + lax.erf(values * 0.7071067811865476))
        + values * jnp.exp(-0.5 * values * values) * 0.3989422804014327
    )


def norm_kernel(meta, frames, out_grad, gain, normed, grads, share, stats):
    length, core = meta[0], meta[1]
    values = frames[...].astype(F32)
    centre = jnp.mean(values, axis=-1, keepdims=True)
    shifted = values - centre
    variance = jnp.mean(shifted * shifted, axis=-1, keepdims=True)
    inv_std = lax.rsqrt(variance + 1e-05)
    stats[:, 0:1] = centre
    stats[:, 1:2] = inv_std
    normed[...] = (shifted * inv_std * gain[...]).astype(BF16)
    keep = lax.broadcasted_iota(jnp.int32, (frames.shape[0], 1), 0) < length
    grads[...] = jnp.where(keep, out_grad[...].astype(F32), 0.0).astype(BF16)
    half = share.shape[1]
    rows = pl.ds(pl.multiple_of(core * half, half), half)
    share[0] = normed[rows, :]
    share[1] = grads[rows, :]


def back_through(normed, grads, up, down, d_pre, partial):
    pre_act = dot(normed[...], up[...])
    d_act = dot(grads[...], down[...])
    d_pre[...] = (d_act * gelu_slope(pre_act)).astype(BF16)
    partial[...] = dot(normed[...], d_pre[...], 0, 0)


def other_kernel(count, meta, first, second, *refs):
    blocks, refs = refs[: 2 * count], refs[2 * count :]
    d_pre, partial, up, down, normed, grads = refs
    half, depth = first.shape[1], blocks[0].shape[0]
    for i in range(count):
        rows = pl.ds(pl.multiple_of(meta[i] * depth, depth), depth)
        up[rows, :] = blocks[i][...]
        down[rows, :] = blocks[count + i][...]
    for at, part in ((0, first), (half, second)):
        normed[at : at + half, :] = part[0]
        grads[at : at + half, :] = part[1]
    back_through(normed, grads, up, down, d_pre, partial)


def own_kernel(normed, grads, up, down, d_pre, partial):
    back_through(normed, grads, up, down, d_pre, partial)


def d_norm_kernel(meta, d_pre_own, d_pre_other, up, keep, send):
    core = meta[1]
    rows, width = keep.shape[1:]
    mine = up[pl.ds(pl.multiple_of(core * width, width), width), :]
    theirs = up[pl.ds(pl.multiple_of((1 - core) * width, width), width), :]
    keep[0] = dot(d_pre_own[...], mine, 1, 1)
    keep[1] = dot(d_pre_other[...], mine, 1, 1)
    send[0] = dot(d_pre_own[...], theirs, 1, 1).astype(BF16)
    sent = dot(d_pre_other[...], theirs, 1, 1).astype(BF16)
    send[1, rows // 2 :, :] = sent[: rows // 2]
    send[1, : rows // 2, :] = sent[rows // 2 :]


def over_kernel(meta, keep, came, over):
    half = over.shape[0] // 2
    for i in range(2):
        at = lax.rem(i + meta[1], 2) * half
        rows = slice(i * half, (i + 1) * half)
        value = keep[1, rows, :] + came[1, rows, :].astype(F32)
        over[pl.ds(pl.multiple_of(at, half), half), :] = value.astype(BF16)


def own_columns(meta, ref, width):
    return ref[:, pl.ds(pl.multiple_of(meta[1] * width, width), width)]


def scale_kernel(meta, keep, came, back, frames, gain, stats, scaled, sums):
    width = scaled.shape[1]
    d_norm = keep[0] + came[0].astype(F32) + back[...].astype(F32)
    value = d_norm * own_columns(meta, gain, width)
    scaled[...] = value
    rows = own_columns(meta, frames, width).astype(F32)
    centred = (rows - stats[:, 0:1]) * stats[:, 1:2]
    sums[:, 0:1] = jnp.sum(value, axis=-1, keepdims=True)
    sums[:, 1:2] = jnp.sum(value * centred, axis=-1, keepdims=True)


def input_kernel(meta, scaled, sums, came, frames, grads, stats, out):
    width = scaled.shape[1]
    means = (sums[...] + came[...]) * (0.5 / width)
    rows = own_columns(meta, frames, width).astype(F32)
    inv_std = stats[:, 1:2]
    centred = (rows - stats[:, 0:1]) * inv_std
    value = inv_std * (scaled[...] - means[:, 0:1] - centred * means[:, 1:2])
    out[...] = (own_columns(meta, grads, width).astype(F32) + value).astype(BF16)


def ring_member(place, count):
    place = place % count
    return jnp.where(place < count // 2, 2 * place, 2 * (count - 1 - place) + 1)


def shards(frames, out_grad, ln_gain, w_up, w_down, lengths):
    peers = lax.axis_size("gx")
    half = peers // 2
    own = lax.axis_index("gx")
    side = lax.axis_index("groups")
    core = lax.axis_index("gy")
    frame_len, width = frames.shape[1:]
    depth, hidden = w_up.shape
    quarter = hidden // 2
    half_width = width // 2
    half_rows = frame_len // 2
    ringed = peers <= 16 and peers % 2 == 0 and depth % 16 == 0

    order = list(range(0, peers, 2)) + list(range(peers - 1, 0, -2))
    ahead = [(order[i], order[(i + 1) % peers]) for i in range(peers)]
    behind = [(b, a) for a, b in ahead]
    place = jnp.where(own % 2 == 0, own // 2, peers - 1 - own // 2)
    swap = [(0, 1), (1, 0)]

    mine = [lax.dynamic_slice_in_dim(w, side * quarter, quarter, 1) for w in (w_up, w_down)]
    mine, frames, out_grad = lax.optimization_barrier((mine, frames, out_grad))

    length = lax.dynamic_index_in_dim(lengths, own, 0, keepdims=False)
    meta = jnp.stack([length, core]).astype(jnp.int32)
    gain = ln_gain[None]
    frames, out_grad = frames[0], out_grad[0]
    rows_of = shape((frame_len, width), BF16)
    normed, grads, share, stats = call(
        norm_kernel,
        (meta, frames, out_grad, gain),
        (rows_of, rows_of, shape((2, half_rows, width), BF16), shape((frame_len, 2), F32)),
        10 * frame_len * width,
    )
    first = lax.ppermute(share, "groups", swap)
    second = lax.ppermute(first, "gy", swap)

    if ringed:
        blocks = {0: tuple(mine)}
        up, down = list(mine), list(mine)
        for step in range(1, half):
            for i in range(2):
                up[i] = lax.ppermute(up[i], "gx", ahead)
                down[i] = lax.ppermute(down[i], "gx", behind)
            blocks[-step], blocks[step] = tuple(up), tuple(down)
        blocks[half] = (lax.ppermute(up[0], "gx", ahead), lax.ppermute(down[1], "gx", behind))
        steps = list(blocks)
        index = jnp.stack([ring_member(place + step + peers, peers) for step in steps])
        blocks = [blocks[step][i] for i in range(2) for step in steps]
    else:
        blocks = [lax.all_gather(block, "gx", axis=0, tiled=True) for block in mine]
        index = jnp.zeros((1,), jnp.int32)

    weight = shape((depth * peers, quarter), BF16)
    d_pre_of, partial_of = shape((frame_len, quarter), BF16), shape((width, quarter), F32)
    flops = 6 * frame_len * width * quarter
    d_pre_other, partial_other, full_up, full_down = call(
        functools.partial(other_kernel, len(blocks) // 2),
        (index.astype(jnp.int32), first, second, *blocks),
        (d_pre_of, partial_of, weight, weight),
        flops,
        [pltpu.VMEM((frame_len, width), BF16)] * 2,
    )
    d_pre_own, partial_own = call(
        own_kernel, (normed, grads, full_up, full_down), (d_pre_of, partial_of), flops
    )
    partial = [partial_own, partial_other]

    if ringed:

        def term(i, step):
            row = ring_member(place + step + peers, peers) * depth
            return lax.dynamic_slice_in_dim(partial[i], row, depth, 0)

        up, down = [None] * 2, [None] * 2
        down[1] = lax.ppermute(term(1, half).astype(BF16), "gx", behind)
        up[0] = lax.ppermute(term(0, half).astype(BF16), "gx", ahead)
        for step in range(half - 1, 0, -1):
            for i in (1, 0):
                for way, at, pairs in ((up, step, ahead), (down, -step, behind)):
                    value = term(i, at)
                    if way[i] is not None:
                        value = value + way[i].astype(F32)
                    way[i] = lax.ppermute(value.astype(BF16), "gx", pairs)
        total = [term(i, 0) + up[i].astype(F32) + down[i].astype(F32) for i in range(2)]
    else:
        total = [lax.psum_scatter(p, "gx", scatter_dimension=0, tiled=True) for p in partial]
    passed = lax.ppermute(total[1].astype(BF16), "groups", swap).astype(F32)
    low = jnp.where(side == 0, total[0], passed)
    high = jnp.where(side == 0, passed, total[0])
    up_grad = jnp.concatenate([low, high], axis=1)

    keep, send = call(
        d_norm_kernel,
        (meta, d_pre_own, d_pre_other, full_up),
        (shape((2, frame_len, half_width), F32), shape((2, frame_len, half_width), BF16)),
        4 * frame_len * width * quarter,
    )
    came = lax.ppermute(send, "gy", swap)
    over = call(
        over_kernel, (meta, keep, came), shape((frame_len, half_width), BF16), frame_len * width
    )
    back = lax.ppermute(over, "groups", swap)
    scaled, sums = call(
        scale_kernel,
        (meta, keep, came, back, frames, gain, stats),
        (shape((frame_len, half_width), F32), shape((frame_len, 2), F32)),
        4 * frame_len * width,
    )
    input_grad = call(
        input_kernel,
        (meta, scaled, sums, lax.ppermute(sums, "gy", swap), frames, grads, stats),
        shape((frame_len, half_width), BF16),
        4 * frame_len * width,
    )
    return (input_grad[None], up_grad)


def solution(mesh):
    placed = (
        P(("groups", "gx"), None, None),
        P(("groups", "gx"), None, None),
        P(),
        P("gx", "gy"),
        P("gx", "gy"),
        P("groups"),
    )
    return jax.shard_map(
        shards,
        mesh=mesh,
        in_specs=placed,
        out_specs=(P(("groups", "gx"), None, "gy"), P(("groups", "gx"), "gy")),
        check_vma=False,
    )
```

time: 341 us -> 143 us (0.42)
  waiting for transfers between devices: 253 us -> 73 us
  blocking collectives: 30.6 us -> 0 us
  starting transfers between devices: 11.2 us -> 34.1 us
  Pallas kernels: 0 us -> 16.5 us
  matrix products: 13.5 us -> 0 us
  between operations: 14 us -> 0.83 us
    reduce_scatter x1 -> x0, waiting for transfers between devices: 101 us -> none  [shards(): lax.psum_scatter(row_product(normed, d_pre), 'gx', scatter_dimension=0, t...]
    all_to_all x2 -> x0, waiting for transfers between devices: 79.9 us -> none  [the longest x1 43.6 us: shards(): lax.all_to_all(send_grads, 'gx', split_axis=1, concat_axis=1, tiled=True)]
    ppermute x0 -> x34, waiting for transfers between devices: none -> 73 us  [the longest x1 21.9 us: shards(): first = lax.ppermute(share, 'groups', swap)]
    all_gather x2 -> x0, waiting for transfers between devices: 58.1 us -> none  [the longest x1 58.1 us: shards(): lax.all_gather(w_down, 'gx', axis=0, tiled=True)]
    ppermute x0 -> x34, starting transfers between devices: none -> 34.1 us  [the longest x12 12.4 us: shards(): way[i] = lax.ppermute(value.astype(BF16), 'gx', pairs)]
    all_to_all x1 -> x0, blocking collectives: 30.6 us -> none  [shards(): lax.all_to_all(send_back, 'gx', split_axis=1, concat_axis=1, tiled=True)]
    pallas_call x0 -> x7, Pallas kernels: none -> 16.5 us  [call(): pl.pallas_call(kernel, out_shape=out_shape, in_specs=[SMEM if x.dtype ==...]
    dot_general x4 -> x0, matrix products: 13.5 us -> none  [the longest x1 5.05 us: row_product(): lax.dot_general(left, right, (((0,), (0,)), ((), ())), preferred_element_...]
  transfers between devices with their start and end apart: 6 -> 34, of which waited for: 5 -> 16; matrix products, arithmetic and copies ran while one was open for 8% -> 4% of each run, Pallas kernels for 0% -> 5%
where the time goes in v3:
time: 143 us
  waiting for transfers between devices  73 us (51%)
  starting transfers between devices  34.1 us (24%)
  Pallas kernels  16.5 us (12%)
  local copies, waits for them, and re-layouts  12.6 us (9%)
  other arithmetic  5.65 us (4%)
    ppermute x1, waiting for transfers between devices, shards(): first = lax.ppermute(share, 'groups', swap)  21.9 us
    ppermute x12, waiting for transfers between devices, shards(): way[i] = lax.ppermute(value.astype(BF16), 'gx', pairs)  20.8 us
    pallas_call x7, Pallas kernels, call(): pl.pallas_call(kernel, out_shape=out_shape, in_specs=[SMEM if x.dtype ==...  16.5 us
    ppermute x12, starting transfers between devices, shards(): way[i] = lax.ppermute(value.astype(BF16), 'gx', pairs)  12.4 us
    ppermute x6, waiting for transfers between devices, shards(): down[i] = lax.ppermute(down[i], 'gx', behind)  11.1 us
    ppermute x1, waiting for transfers between devices, shards(): passed = lax.ppermute(total[1].astype(BF16), 'groups', swap).astype(F32)  10.8 us
    unnamed x28, local copies, waits for them, and re-layouts  9.41 us
    ppermute x6, starting transfers between devices, shards(): up[i] = lax.ppermute(up[i], 'gx', ahead)  9.22 us
  transfers between devices with their start and end apart: 34, of which 16 were waited for; matrix products, arithmetic and copies ran while one was open for 4% of the time, Pallas kernels for 5%

profile of v3, /device:TPU:0, one launch (start us, length us, event | category | flops | bytes accessed | tf_op | source)
XLA Modules:
  0.0 142.7 jit_solution(13221036856275042694)
XLA Ops:
  8.4 3.0 %collective-permute-start = (bf16[2,192,1280]{2,1,0:T(8,128)(2,1)S(1)}, bf16[2,192,1280]{2,1,0:T(8,128)(2,1)}, u32[]{:S(2)}, u32[]{:S(2)}) collective-permute-start(bf16[2,192,1280]{2,1,0:T(8,128)(2,1)S(1)} %get-tuple-element.24), channel_id=1, source_target_pairs={{0,16},{16,0},{1,17},{17,1},{2,18},{18,2},{3,19},{19,3},{4,20},{20... | collective-permute-start | bytes 2949128 | tf_op jit(solution)/shard_map/ppermute | solution.py:175
  11.4 21.9 %collective-permute-done.first = bf16[2,192,1280]{2,1,0:T(8,128)(2,1)} collective-permute-done((bf16[2,192,1280]{2,1,0:T(8,128)(2,1)S(1)}, bf16[2,192,1280]{2,1,0:T(8,128)(2,1)}, u32[]{:S(2)}, u32[]{:S(2)}) %collective-permute-start) | collective-permute-done | bytes 983072 | tf_op jit(solution)/shard_map/ppermute | solution.py:175
  33.2 1.8 %collective-permute-start.2 = (bf16[160,640]{1,0:T(8,128)(2,1)S(1)}, bf16[160,640]{1,0:T(8,128)(2,1)S(1)}, u32[]{:S(2)}, u32[]{:S(2)}) collective-permute-start(bf16[160,640]{1,0:T(8,128)(2,1)S(1)} %get-tuple-element.25.refs_0_), channel_id=1, source_target_pairs={{0,4},{4,8},{8,12},{12,14},{14,10},{10,6},{6,2},{2,0},{1,5},{5,9},... | collective-permute-start | bytes 614408 | tf_op jit(solution)/shard_map/ppermute | solution.py:183
  35.3 1.8 %collective-permute-start.3 = (bf16[160,640]{1,0:T(8,128)(2,1)S(1)}, bf16[160,640]{1,0:T(8,128)(2,1)S(1)}, u32[]{:S(2)}, u32[]{:S(2)}) collective-permute-start(bf16[160,640]{1,0:T(8,128)(2,1)S(1)} %get-tuple-element.25.refs_0_), channel_id=1, source_target_pairs={{4,0},{8,4},{12,8},{14,12},{10,14},{6,10},{2,6},{0,2},{5,1},{9,5},... | collective-permute-start | bytes 614408 | tf_op jit(solution)/shard_map/ppermute | solution.py:184
  37.3 3.8 %collective-permute-done.2.refs_1_ = bf16[160,640]{1,0:T(8,128)(2,1)S(1)} collective-permute-done((bf16[160,640]{1,0:T(8,128)(2,1)S(1)}, bf16[160,640]{1,0:T(8,128)(2,1)S(1)}, u32[]{:S(2)}, u32[]{:S(2)}) %collective-permute-start.2) | collective-permute-done | bytes 204832 | tf_op jit(solution)/shard_map/ppermute | solution.py:183
  41.1 1.8 %collective-permute-start.4 = (bf16[160,640]{1,0:T(8,128)(2,1)S(1)}, bf16[160,640]{1,0:T(8,128)(2,1)S(1)}, u32[]{:S(2)}, u32[]{:S(2)}) collective-permute-start(bf16[160,640]{1,0:T(8,128)(2,1)S(1)} %collective-permute-done.2.refs_1_), channel_id=1, source_target_pairs={{0,4},{4,8},{8,12},{12,14},{14,10},{10,6},{6,2},{2,0},{1,5},{5,9},... | collective-permute-start | bytes 614408 | tf_op jit(solution)/shard_map/ppermute | solution.py:183
  43.2 4.2 %collective-permute-done.3.refs_2_ = bf16[160,640]{1,0:T(8,128)(2,1)S(1)} collective-permute-done((bf16[160,640]{1,0:T(8,128)(2,1)S(1)}, bf16[160,640]{1,0:T(8,128)(2,1)S(1)}, u32[]{:S(2)}, u32[]{:S(2)}) %collective-permute-start.3) | collective-permute-done | bytes 204832 | tf_op jit(solution)/shard_map/ppermute | solution.py:184
  47.6 1.8 %collective-permute-start.11 = (bf16[160,640]{1,0:T(8,128)(2,1)S(1)}, bf16[160,640]{1,0:T(8,128)(2,1)}, u32[]{:S(2)}, u32[]{:S(2)}) collective-permute-start(bf16[160,640]{1,0:T(8,128)(2,1)S(1)} %collective-permute-done.9.refs_9_), channel_id=1, source_target_pairs={{0,4},{4,8},{8,12},{12,14},{14,10},{10,6},{6,2},{2,0},{1,5},{5,9},... | collective-permute-start | bytes 614408 | tf_op jit(solution)/shard_map/ppermute | solution.py:183
  53.5 2.8 %collective-permute-done.5.refs_4_ = bf16[160,640]{1,0:T(8,128)(2,1)} collective-permute-done((bf16[160,640]{1,0:T(8,128)(2,1)S(1)}, bf16[160,640]{1,0:T(8,128)(2,1)}, u32[]{:S(2)}, u32[]{:S(2)}) %collective-permute-start.5) | collective-permute-done | bytes 204832 | tf_op jit(solution)/shard_map/ppermute | solution.py:184
  56.5 1.8 %collective-permute-start.13 = (bf16[160,640]{1,0:T(8,128)(2,1)}, bf16[160,640]{1,0:T(8,128)(2,1)}, u32[]{:S(2)}, u32[]{:S(2)}) collective-permute-start(bf16[160,640]{1,0:T(8,128)(2,1)} %collective-permute-done.11.refs_11_), channel_id=1, source_target_pairs={{0,4},{4,8},{8,12},{12,14},{14,10},{10,6},{6,2},{2,0},{1,5},{5,9},... | collective-permute-start | bytes 614408 | tf_op jit(solution)/shard_map/ppermute | solution.py:183
  58.8 1.9 %collective-permute-start.8 = (bf16[160,640]{1,0:T(8,128)(2,1)}, bf16[160,640]{1,0:T(8,128)(2,1)}, u32[]{:S(2)}, u32[]{:S(2)}) collective-permute-start(bf16[160,640]{1,0:T(8,128)(2,1)} %collective-permute-done.6.refs_5_), channel_id=1, source_target_pairs={{0,4},{4,8},{8,12},{12,14},{14,10},{10,6},{6,2},{2,0},{1,5},{5,9},... | collective-permute-start | bytes 614408 | tf_op jit(solution)/shard_map/ppermute | solution.py:186
  61.0 4.0 %collective-permute-done.7.refs_6_ = bf16[160,640]{1,0:T(8,128)(2,1)} collective-permute-done((bf16[160,640]{1,0:T(8,128)(2,1)}, bf16[160,640]{1,0:T(8,128)(2,1)}, u32[]{:S(2)}, u32[]{:S(2)}) %collective-permute-start.7) | collective-permute-done | bytes 204832 | tf_op jit(solution)/shard_map/ppermute | solution.py:184
  65.0 2.2 %collective-permute-done.8.refs_7_ = bf16[160,640]{1,0:T(8,128)(2,1)} collective-permute-done((bf16[160,640]{1,0:T(8,128)(2,1)}, bf16[160,640]{1,0:T(8,128)(2,1)}, u32[]{:S(2)}, u32[]{:S(2)}) %collective-permute-start.8) | collective-permute-done | bytes 204832 | tf_op jit(solution)/shard_map/ppermute | solution.py:186
  71.5 4.9 %shard_map.78 = (bf16[384,640]{1,0:T(8,128)(2,1)S(1)}, f32[1280,640]{1,0:T(8,128)S(1)}, bf16[1280,640]{1,0:T(8,128)(2,1)S(1)}, bf16[1280,640]{1,0:T(8,128)(2,1)S(1)}) custom-call(s32[8]{0:T(128)S(1)} %stack.44.meta, bf16[2,192,1280]{2,1,0:T(8,128)(2,1)} %collective-permute-done.first, bf16[2,192,1280]{2,1,0:T(8,128)(2,1)} %collective-permute-done.1.second, ...), custom_call_target="tpu_custom_call" | custom-call | flops 1887436800 | bytes 12288032 | tf_op jit(solution)/shard_map/pallas_call | solution.py:22
  78.6 2.7 %shard_map.79 = (bf16[384,640]{1,0:T(8,128)(2,1)S(1)}, f32[1280,640]{1,0:T(8,128)S(1)}) custom-call(bf16[384,1280]{1,0:T(8,128)(2,1)S(1)} %get-tuple-element.22.normed, bf16[384,1280]{1,0:T(8,128)(2,1)S(1)} %get-tuple-element.23.grads, bf16[1280,640]{1,0:T(8,128)(2,1)S(1)} %get-tuple-element.27.up, bf16[1280,640]{1,0:T(8,128)(2,1)S(1)} %get-tuple-element.28.down), custom_call_target="tpu_custom_call" | custom-call | flops 1887436800 | bytes 9011200 | tf_op jit(solution)/shard_map/pallas_call | solution.py:22
  83.4 2.5 %shard_map.80 = (f32[2,384,640]{2,1,0:T(8,128)S(1)}, bf16[2,384,640]{2,1,0:T(8,128)(2,1)S(1)}) custom-call(s32[2]{0:T(128)S(1)} %pad_add_fusion.meta, bf16[384,640]{1,0:T(8,128)(2,1)S(1)} %get-tuple-element.29.d_pre_own, bf16[384,640]{1,0:T(8,128)(2,1)S(1)} %get-tuple-element.30.d_pre_other, bf16[1280,640]{1,0:T(8,128)(2,1)S(1)} %get-tuple-element.27.up), custom_call_target="tpu_custom_call" | custom-call | flops 1258291200 | bytes 5570568 | tf_op jit(solution)/shard_map/pallas_call | solution.py:22
  87.8 1.6 %collective-permute-start.20 = (bf16[160,640]{1,0:T(8,128)(2,1)S(1)}, bf16[160,640]{1,0:T(8,128)(2,1)S(1)}, u32[]{:S(2)}, u32[]{:S(2)}) collective-permute-start(bf16[160,640]{1,0:T(8,128)(2,1)S(1)} %add_convert_fusion.10), channel_id=1, source_target_pairs={{0,4},{4,8},{8,12},{12,14},{14,10},{10,6},{6,2},{2,0},{1,5},{5,9},... | collective-permute-start | bytes 614408 | tf_op jit(solution)/shard_map/ppermute | solution.py:224
  89.4 4.6 %collective-permute-done.27 = bf16[160,640]{1,0:T(8,128)(2,1)S(1)} collective-permute-done((bf16[160,640]{1,0:T(8,128)(2,1)S(1)}, bf16[160,640]{1,0:T(8,128)(2,1)S(1)}, u32[]{:S(2)}, u32[]{:S(2)}) %collective-permute-start.27) | collective-permute-done | bytes 204832 | tf_op jit(solution)/shard_map/ppermute | solution.py:224
  96.2 2.2 %collective-permute-done.20 = bf16[160,640]{1,0:T(8,128)(2,1)S(1)} collective-permute-done((bf16[160,640]{1,0:T(8,128)(2,1)S(1)}, bf16[160,640]{1,0:T(8,128)(2,1)S(1)}, u32[]{:S(2)}, u32[]{:S(2)}) %collective-permute-start.20) | collective-permute-done | bytes 204832 | tf_op jit(solution)/shard_map/ppermute | solution.py:224
  100.1 1.7 %collective-permute-done.30 = bf16[160,640]{1,0:T(8,128)(2,1)S(1)} collective-permute-done((bf16[160,640]{1,0:T(8,128)(2,1)S(1)}, bf16[160,640]{1,0:T(8,128)(2,1)S(1)}, u32[]{:S(2)}, u32[]{:S(2)}) %collective-permute-start.30) | collective-permute-done | bytes 204832 | tf_op jit(solution)/shard_map/ppermute | solution.py:224
  102.3 4.5 %collective-permute-done.21 = bf16[160,640]{1,0:T(8,128)(2,1)S(1)} collective-permute-done((bf16[160,640]{1,0:T(8,128)(2,1)S(1)}, bf16[160,640]{1,0:T(8,128)(2,1)S(1)}, u32[]{:S(2)}, u32[]{:S(2)}) %collective-permute-start.21) | collective-permute-done | bytes 204832 | tf_op jit(solution)/shard_map/ppermute | solution.py:224
  110.0 7.2 %collective-permute-done.24 = bf16[160,640]{1,0:T(8,128)(2,1)S(1)} collective-permute-done((bf16[160,640]{1,0:T(8,128)(2,1)S(1)}, bf16[160,640]{1,0:T(8,128)(2,1)S(1)}, u32[]{:S(2)}, u32[]{:S(2)}) %collective-permute-start.24) | collective-permute-done | bytes 204832 | tf_op jit(solution)/shard_map/ppermute | solution.py:224
  124.4 10.8 %collective-permute-done.33 = bf16[160,640]{1,0:T(8,128)(2,1)} collective-permute-done((bf16[160,640]{1,0:T(8,128)(2,1)}, bf16[160,640]{1,0:T(8,128)(2,1)}, u32[]{:S(2)}, u32[]{:S(2)}) %collective-permute-start.33) | collective-permute-done | bytes 204832 | tf_op jit(solution)/shard_map/ppermute | solution.py:228
  140.8 1.9 %shard_map.83 = bf16[384,640]{1,0:T(8,128)(2,1)} custom-call(s32[2]{0:T(128)S(1)} %pad_add_fusion.meta, f32[384,640]{1,0:T(8,128)S(1)} %get-tuple-element.34.scaled, f32[384,2]{1,0:T(8,128)S(1)} %get-tuple-element.35.sums, f32[384,2]{1,0:T(8,128)S(1)} %collective-permute-done.18.came, bf16[384,1280]{1,0:T(8,128)(2,1)S(1)} %bitcast.14, ...), custom_call_target="tpu_custom_call" | custom-call | flops 1966080 | bytes 3449864 | tf_op jit(solution)/shard_map/pallas_call | solution.py:22
  (97 shorter events, 44.4 us)
Async XLA Ops:
  8.4 24.9 %collective-permute-start = (bf16[2,192,1280]{2,1,0:T(8,128)(2,1)S(1)}, bf16[2,192,1280]{2,1,0:T(8,128)(2,1)}, u32[]{:S(2)}, u32[]{:S(2)}) collective-permute-start(bf16[2,192,1280]{2,1,0:T(8,128)(2,1)S(1)} %get-tuple-element.24), channel_id=1, source_target_pairs={{0,16},{16,0},{1,17},{17,1},{2,18},{18,2},{3,19},{19,3},{4,20},{20... | collective-permute-start | bytes 2949128 | tf_op jit(solution)/shard_map/ppermute | solution.py:175
  33.2 35.5 %collective-permute-start.1 = (bf16[2,192,1280]{2,1,0:T(8,128)(2,1)}, bf16[2,192,1280]{2,1,0:T(8,128)(2,1)}, u32[]{:S(2)}, u32[]{:S(2)}) collective-permute-start(bf16[2,192,1280]{2,1,0:T(8,128)(2,1)} %collective-permute-done.first), channel_id=1, source_target_pairs={{0,1},{1,0},{2,3},{3,2},{4,5},{5,4},{6,7},{7,6},{8,9},{9,8},{10,11... | collective-permute-start | bytes 2949128 | tf_op jit(solution)/shard_map/ppermute | solution.py:176
  35.3 12.1 %collective-permute-start.3 = (bf16[160,640]{1,0:T(8,128)(2,1)S(1)}, bf16[160,640]{1,0:T(8,128)(2,1)S(1)}, u32[]{:S(2)}, u32[]{:S(2)}) collective-permute-start(bf16[160,640]{1,0:T(8,128)(2,1)S(1)} %get-tuple-element.25.refs_0_), channel_id=1, source_target_pairs={{4,0},{8,4},{12,8},{14,12},{10,14},{6,10},{2,6},{0,2},{5,1},{9,5},... | collective-permute-start | bytes 614408 | tf_op jit(solution)/shard_map/ppermute | solution.py:184
  37.0 10.5 %collective-permute-start.9 = (bf16[160,640]{1,0:T(8,128)(2,1)S(1)}, bf16[160,640]{1,0:T(8,128)(2,1)S(1)}, u32[]{:S(2)}, u32[]{:S(2)}) collective-permute-start(bf16[160,640]{1,0:T(8,128)(2,1)S(1)} %get-tuple-element.26.refs_8_), channel_id=1, source_target_pairs={{0,4},{4,8},{8,12},{12,14},{14,10},{10,6},{6,2},{2,0},{1,5},{5,9},... | collective-permute-start | bytes 614408 | tf_op jit(solution)/shard_map/ppermute | solution.py:183
  41.1 9.0 %collective-permute-start.4 = (bf16[160,640]{1,0:T(8,128)(2,1)S(1)}, bf16[160,640]{1,0:T(8,128)(2,1)S(1)}, u32[]{:S(2)}, u32[]{:S(2)}) collective-permute-start(bf16[160,640]{1,0:T(8,128)(2,1)S(1)} %collective-permute-done.2.refs_1_), channel_id=1, source_target_pairs={{0,4},{4,8},{8,12},{12,14},{14,10},{10,6},{6,2},{2,0},{1,5},{5,9},... | collective-permute-start | bytes 614408 | tf_op jit(solution)/shard_map/ppermute | solution.py:183
  43.0 9.4 %collective-permute-start.12 = (bf16[160,640]{1,0:T(8,128)(2,1)S(1)}, bf16[160,640]{1,0:T(8,128)(2,1)S(1)}, u32[]{:S(2)}, u32[]{:S(2)}) collective-permute-start(bf16[160,640]{1,0:T(8,128)(2,1)S(1)} %collective-permute-done.10.refs_10_), channel_id=1, source_target_pairs={{4,0},{8,4},{12,8},{14,12},{10,14},{6,10},{2,6},{0,2},{5,1},{9,5},... | collective-permute-start | bytes 614408 | tf_op jit(solution)/shard_map/ppermute | solution.py:184
  47.4 8.9 %collective-permute-start.5 = (bf16[160,640]{1,0:T(8,128)(2,1)S(1)}, bf16[160,640]{1,0:T(8,128)(2,1)}, u32[]{:S(2)}, u32[]{:S(2)}) collective-permute-start(bf16[160,640]{1,0:T(8,128)(2,1)S(1)} %collective-permute-done.3.refs_2_), channel_id=1, source_target_pairs={{4,0},{8,4},{12,8},{14,12},{10,14},{6,10},{2,6},{0,2},{5,1},{9,5},... | collective-permute-start | bytes 614408 | tf_op jit(solution)/shard_map/ppermute | solution.py:184
  47.6 8.9 %collective-permute-start.11 = (bf16[160,640]{1,0:T(8,128)(2,1)S(1)}, bf16[160,640]{1,0:T(8,128)(2,1)}, u32[]{:S(2)}, u32[]{:S(2)}) collective-permute-start(bf16[160,640]{1,0:T(8,128)(2,1)S(1)} %collective-permute-done.9.refs_9_), channel_id=1, source_target_pairs={{0,4},{4,8},{8,12},{12,14},{14,10},{10,6},{6,2},{2,0},{1,5},{5,9},... | collective-permute-start | bytes 614408 | tf_op jit(solution)/shard_map/ppermute | solution.py:183
  50.1 8.7 %collective-permute-start.6 = (bf16[160,640]{1,0:T(8,128)(2,1)S(1)}, bf16[160,640]{1,0:T(8,128)(2,1)}, u32[]{:S(2)}, u32[]{:S(2)}) collective-permute-start(bf16[160,640]{1,0:T(8,128)(2,1)S(1)} %collective-permute-done.4.refs_3_), channel_id=1, source_target_pairs={{0,4},{4,8},{8,12},{12,14},{14,10},{10,6},{6,2},{2,0},{1,5},{5,9},... | collective-permute-start | bytes 614408 | tf_op jit(solution)/shard_map/ppermute | solution.py:183
  52.4 8.4 %collective-permute-start.14 = (bf16[160,640]{1,0:T(8,128)(2,1)S(1)}, bf16[160,640]{1,0:T(8,128)(2,1)}, u32[]{:S(2)}, u32[]{:S(2)}) collective-permute-start(bf16[160,640]{1,0:T(8,128)(2,1)S(1)} %collective-permute-done.12.refs_12_), channel_id=1, source_target_pairs={{4,0},{8,4},{12,8},{14,12},{10,14},{6,10},{2,6},{0,2},{5,1},{9,5},... | collective-permute-start | bytes 614408 | tf_op jit(solution)/shard_map/ppermute | solution.py:184
  56.3 8.8 %collective-permute-start.7 = (bf16[160,640]{1,0:T(8,128)(2,1)}, bf16[160,640]{1,0:T(8,128)(2,1)}, u32[]{:S(2)}, u32[]{:S(2)}) collective-permute-start(bf16[160,640]{1,0:T(8,128)(2,1)} %collective-permute-done.5.refs_4_), channel_id=1, source_target_pairs={{4,0},{8,4},{12,8},{14,12},{10,14},{6,10},{2,6},{0,2},{5,1},{9,5},... | collective-permute-start | bytes 614408 | tf_op jit(solution)/shard_map/ppermute | solution.py:184
  56.5 8.6 %collective-permute-start.13 = (bf16[160,640]{1,0:T(8,128)(2,1)}, bf16[160,640]{1,0:T(8,128)(2,1)}, u32[]{:S(2)}, u32[]{:S(2)}) collective-permute-start(bf16[160,640]{1,0:T(8,128)(2,1)} %collective-permute-done.11.refs_11_), channel_id=1, source_target_pairs={{0,4},{4,8},{8,12},{12,14},{14,10},{10,6},{6,2},{2,0},{1,5},{5,9},... | collective-permute-start | bytes 614408 | tf_op jit(solution)/shard_map/ppermute | solution.py:183
  58.8 8.4 %collective-permute-start.8 = (bf16[160,640]{1,0:T(8,128)(2,1)}, bf16[160,640]{1,0:T(8,128)(2,1)}, u32[]{:S(2)}, u32[]{:S(2)}) collective-permute-start(bf16[160,640]{1,0:T(8,128)(2,1)} %collective-permute-done.6.refs_5_), channel_id=1, source_target_pairs={{0,4},{4,8},{8,12},{12,14},{14,10},{10,6},{6,2},{2,0},{1,5},{5,9},... | collective-permute-start | bytes 614408 | tf_op jit(solution)/shard_map/ppermute | solution.py:186
  76.5 9.5 %collective-permute-start.26 = (bf16[160,640]{1,0:T(8,128)(2,1)S(1)}, bf16[160,640]{1,0:T(8,128)(2,1)S(1)}, u32[]{:S(2)}, u32[]{:S(2)}) collective-permute-start(bf16[160,640]{1,0:T(8,128)(2,1)S(1)} %get-tuple-element.46), channel_id=1, source_target_pairs={{0,4},{4,8},{8,12},{12,14},{14,10},{10,6},{6,2},{2,0},{1,5},{5,9},... | collective-permute-start | bytes 614408 | tf_op jit(solution)/shard_map/ppermute | solution.py:224
  78.1 11.3 %collective-permute-start.29 = (bf16[160,640]{1,0:T(8,128)(2,1)S(1)}, bf16[160,640]{1,0:T(8,128)(2,1)S(1)}, u32[]{:S(2)}, u32[]{:S(2)}) collective-permute-start(bf16[160,640]{1,0:T(8,128)(2,1)S(1)} %get-tuple-element.47), channel_id=1, source_target_pairs={{4,0},{8,4},{12,8},{14,12},{10,14},{6,10},{2,6},{0,2},{5,1},{9,5},... | collective-permute-start | bytes 614408 | tf_op jit(solution)/shard_map/ppermute | solution.py:216
  83.0 19.3 %collective-permute-start.23 = (bf16[160,640]{1,0:T(8,128)(2,1)S(1)}, bf16[160,640]{1,0:T(8,128)(2,1)S(1)}, u32[]{:S(2)}, u32[]{:S(2)}) collective-permute-start(bf16[160,640]{1,0:T(8,128)(2,1)S(1)} %get-tuple-element.43), channel_id=1, source_target_pairs={{4,0},{8,4},{12,8},{14,12},{10,14},{6,10},{2,6},{0,2},{5,1},{9,5},... | collective-permute-start | bytes 614408 | tf_op jit(solution)/shard_map/ppermute | solution.py:224
  86.0 32.4 %collective-permute-start.16 = (bf16[2,384,640]{2,1,0:T(8,128)(2,1)S(1)}, bf16[2,384,640]{2,1,0:T(8,128)(2,1)S(1)}, u32[]{:S(2)}, u32[]{:S(2)}) collective-permute-start(bf16[2,384,640]{2,1,0:T(8,128)(2,1)S(1)} %get-tuple-element.32), channel_id=1, source_target_pairs={{0,1},{1,0},{2,3},{3,2},{4,5},{5,4},{6,7},{7,6},{8,9},{9,8},{10,11... | collective-permute-start | bytes 2949128 | tf_op jit(solution)/shard_map/ppermute | solution.py:239
  87.8 10.7 %collective-permute-start.20 = (bf16[160,640]{1,0:T(8,128)(2,1)S(1)}, bf16[160,640]{1,0:T(8,128)(2,1)S(1)}, u32[]{:S(2)}, u32[]{:S(2)}) collective-permute-start(bf16[160,640]{1,0:T(8,128)(2,1)S(1)} %add_convert_fusion.10), channel_id=1, source_target_pairs={{0,4},{4,8},{8,12},{12,14},{14,10},{10,6},{6,2},{2,0},{1,5},{5,9},... | collective-permute-start | bytes 614408 | tf_op jit(solution)/shard_map/ppermute | solution.py:224
  94.1 28.1 %collective-permute-start.28 = (bf16[160,640]{1,0:T(8,128)(2,1)S(1)}, bf16[160,640]{1,0:T(8,128)(2,1)S(1)}, u32[]{:S(2)}, u32[]{:S(2)}) collective-permute-start(bf16[160,640]{1,0:T(8,128)(2,1)S(1)} %get-tuple-element.44), channel_id=1, source_target_pairs={{0,4},{4,8},{8,12},{12,14},{14,10},{10,6},{6,2},{2,0},{1,5},{5,9},... | collective-permute-start | bytes 614408 | tf_op jit(solution)/shard_map/ppermute | solution.py:224
  98.5 8.3 %collective-permute-start.21 = (bf16[160,640]{1,0:T(8,128)(2,1)S(1)}, bf16[160,640]{1,0:T(8,128)(2,1)S(1)}, u32[]{:S(2)}, u32[]{:S(2)}) collective-permute-start(bf16[160,640]{1,0:T(8,128)(2,1)S(1)} %add_convert_fusion.9), channel_id=1, source_target_pairs={{0,4},{4,8},{8,12},{12,14},{14,10},{10,6},{6,2},{2,0},{1,5},{5,9},... | collective-permute-start | bytes 614408 | tf_op jit(solution)/shard_map/ppermute | solution.py:224
  107.6 16.2 %collective-permute-start.22 = (bf16[160,640]{1,0:T(8,128)(2,1)}, bf16[160,640]{1,0:T(8,128)(2,1)S(1)}, u32[]{:S(2)}, u32[]{:S(2)}) collective-permute-start(bf16[160,640]{1,0:T(8,128)(2,1)} %get-tuple-element.40), channel_id=1, source_target_pairs={{0,4},{4,8},{8,12},{12,14},{14,10},{10,6},{6,2},{2,0},{1,5},{5,9},... | collective-permute-start | bytes 614408 | tf_op jit(solution)/shard_map/ppermute | solution.py:224
  109.7 12.6 %collective-permute-start.32 = (bf16[160,640]{1,0:T(8,128)(2,1)S(1)}, bf16[160,640]{1,0:T(8,128)(2,1)S(1)}, u32[]{:S(2)}, u32[]{:S(2)}) collective-permute-start(bf16[160,640]{1,0:T(8,128)(2,1)S(1)} %add_convert_fusion.1), channel_id=1, source_target_pairs={{4,0},{8,4},{12,8},{14,12},{10,14},{6,10},{2,6},{0,2},{5,1},{9,5},... | collective-permute-start | bytes 614408 | tf_op jit(solution)/shard_map/ppermute | solution.py:224
  120.7 15.8 %collective-permute-start.17 = (bf16[384,640]{1,0:T(8,128)(2,1)}, bf16[384,640]{1,0:T(8,128)(2,1)}, u32[]{:S(2)}, u32[]{:S(2)}) collective-permute-start(bf16[384,640]{1,0:T(8,128)(2,1)} %shard_map.81), channel_id=1, source_target_pairs={{0,16},{16,0},{1,17},{17,1},{2,18},{18,2},{3,19},{19,3},{4,20},{20... | collective-permute-start | bytes 1474568 | tf_op jit(solution)/shard_map/ppermute | solution.py:243
  123.0 12.2 %collective-permute-start.33 = (bf16[160,640]{1,0:T(8,128)(2,1)}, bf16[160,640]{1,0:T(8,128)(2,1)}, u32[]{:S(2)}, u32[]{:S(2)}) collective-permute-start(bf16[160,640]{1,0:T(8,128)(2,1)} %add_convert_fusion), channel_id=1, source_target_pairs={{0,16},{16,0},{1,17},{17,1},{2,18},{18,2},{3,19},{19,3},{4,20},{20... | collective-permute-start | bytes 614408 | tf_op jit(solution)/shard_map/ppermute | solution.py:228
  (24 other events, 207.8 us)

commit v4 on v3

--- a/solution.py
+++ b/solution.py
@@ -16,7 +16,7 @@
     return jax.ShapeDtypeStruct(dims, kind)
 
 
-def call(kernel, ins, out_shape, flops, scratch=(), vmem=32, aliases=None):
+def call(kernel, ins, out_shape, flops, scratch=(), vmem=16, aliases=None):
     outs = jax.tree.leaves(out_shape)
     moved = sum(x.size * x.dtype.itemsize for x in list(ins) + outs)
     return pl.pallas_call(
@@ -69,14 +69,22 @@
     partial[...] = dot(normed[...], d_pre[...], 0, 0)
 
 
-def other_kernel(count, meta, first, second, *refs):
-    blocks, refs = refs[: 2 * count], refs[2 * count :]
-    d_pre, partial, up, down, normed, grads = refs
-    half, depth = first.shape[1], blocks[0].shape[0]
-    for i in range(count):
-        rows = pl.ds(pl.multiple_of(meta[i] * depth, depth), depth)
-        up[rows, :] = blocks[i][...]
-        down[rows, :] = blocks[count + i][...]
+def place_kernel(index, *refs):
+    blocks, (up, down) = refs[:-2], refs[-2:]
+    depth = blocks[0].shape[1]
+    for i, block in enumerate(blocks):
+        rows = pl.ds(pl.multiple_of(index[i] * depth, depth), depth)
+        up[rows, :] = block[0]
+        down[rows, :] = block[1]
+
+
+def other_kernel(index, first, second, _, __, *refs):
+    d_pre, partial, up, down, normed, grads = refs[-6:]
+    half = first.shape[1]
+    for ref, block in zip((up, down), refs[:-6]):
+        depth = block.shape[0]
+        rows = pl.ds(pl.multiple_of(index[index.shape[0] - 1] * depth, depth), depth)
+        ref[rows, :] = block[...]
     for at, part in ((0, first), (half, second)):
         normed[at : at + half, :] = part[0]
         grads[at : at + half, :] = part[1]
@@ -132,6 +140,33 @@
     centred = (rows - stats[:, 0:1]) * inv_std
     value = inv_std * (scaled[...] - means[:, 0:1] - centred * means[:, 1:2])
     out[...] = (own_columns(meta, grads, width).astype(F32) + value).astype(BF16)
+
+
+def hop_kernel(at, given, index, *refs):
+    partial, came, out = refs[:2], refs[2:-1], refs[-1]
+    depth = out.shape[-2]
+    rows = pl.ds(pl.multiple_of(index[at] * depth, depth), depth)
+    for i in range(2):
+        value = partial[i][rows, :]
+        if i in given:
+            for ref in came:
+                value = value + (ref[i] if len(ref.shape) == 3 else ref[...]).astype(F32)
+        out[i] = value.astype(out.dtype)
+
+
+def total_kernel(index, own, other, up, down, total, passing):
+    depth = total.shape[0]
+    rows = pl.ds(pl.multiple_of(index[0] * depth, depth), depth)
+    total[...] = own[rows, :] + up[0].astype(F32) + down[0].astype(F32)
+    passing[...] = (other[rows, :] + up[1].astype(F32) + down[1].astype(F32)).astype(BF16)
+
+
+def join_kernel(meta, own, passed, out):
+    width = own.shape[1]
+    side = meta[2]
+    out[:, pl.ds(pl.multiple_of(side * width, width), width)] = own[...]
+    other = pl.ds(pl.multiple_of((1 - side) * width, width), width)
+    out[:, other] = passed[...].astype(F32)
 
 
 def ring_member(place, count):
@@ -157,12 +192,15 @@
     behind = [(b, a) for a, b in ahead]
     place = jnp.where(own % 2 == 0, own // 2, peers - 1 - own // 2)
     swap = [(0, 1), (1, 0)]
+    after = lax.optimization_barrier
 
     mine = [lax.dynamic_slice_in_dim(w, side * quarter, quarter, 1) for w in (w_up, w_down)]
-    mine, frames, out_grad = lax.optimization_barrier((mine, frames, out_grad))
+    mine, frames, out_grad, ln_gain, lengths = after(
+        (mine, frames, out_grad, ln_gain, lengths)
+    )
 
     length = lax.dynamic_index_in_dim(lengths, own, 0, keepdims=False)
-    meta = jnp.stack([length, core]).astype(jnp.int32)
+    meta = jnp.stack([length, core, side]).astype(jnp.int32)
     gain = ln_gain[None]
     frames, out_grad = frames[0], out_grad[0]
     rows_of = shape((frame_len, width), BF16)
@@ -173,62 +211,46 @@
         10 * frame_len * width,
     )
     first = lax.ppermute(share, "groups", swap)
+
+    weight = shape((depth * peers, quarter), BF16)
+    if ringed:
+        pair = jnp.stack(mine)
+        blocks = {0: pair}
+        up, down = pair, pair
+        for step in range(1, half):
+            up, down = lax.ppermute(up, "gx", ahead), lax.ppermute(down, "gx", behind)
+            if step == 1:
+                up, down, share = after((up, down, share))
+            else:
+                up, down = after((up, down))
+            blocks[-step], blocks[step] = up, down
+        far = lax.ppermute(up[0], "gx", ahead), lax.ppermute(down[1], "gx", behind)
+        steps = list(blocks)
+        index = jnp.stack([ring_member(place + step + peers, peers) for step in steps + [half]])
+        index = index.astype(jnp.int32)
+        first, up = after((first, up))
+        near = [blocks[step] for step in steps]
+        full_up, full_down = call(place_kernel, (index, *near), (weight, weight), 0)
+    else:
+        full_up, full_down = [lax.all_gather(w, "gx", axis=0, tiled=True) for w in mine]
+        index = own[None].astype(jnp.int32)
+        far = ()
     second = lax.ppermute(first, "gy", swap)
 
-    if ringed:
-        blocks = {0: tuple(mine)}
-        up, down = list(mine), list(mine)
-        for step in range(1, half):
-            for i in range(2):
-                up[i] = lax.ppermute(up[i], "gx", ahead)
-                down[i] = lax.ppermute(down[i], "gx", behind)
-            blocks[-step], blocks[step] = tuple(up), tuple(down)
-        blocks[half] = (lax.ppermute(up[0], "gx", ahead), lax.ppermute(down[1], "gx", behind))
-        steps = list(blocks)
-        index = jnp.stack([ring_member(place + step + peers, peers) for step in steps])
-        blocks = [blocks[step][i] for i in range(2) for step in steps]
-    else:
-        blocks = [lax.all_gather(block, "gx", axis=0, tiled=True) for block in mine]
-        index = jnp.zeros((1,), jnp.int32)
-
-    weight = shape((depth * peers, quarter), BF16)
     d_pre_of, partial_of = shape((frame_len, quarter), BF16), shape((width, quarter), F32)
     flops = 6 * frame_len * width * quarter
     d_pre_other, partial_other, full_up, full_down = call(
-        functools.partial(other_kernel, len(blocks) // 2),
-        (index.astype(jnp.int32), first, second, *blocks),
+        other_kernel,
+        (index, first, second, full_up, full_down, *far),
         (d_pre_of, partial_of, weight, weight),
         flops,
         [pltpu.VMEM((frame_len, width), BF16)] * 2,
+        aliases={3: 2, 4: 3},
     )
     d_pre_own, partial_own = call(
         own_kernel, (normed, grads, full_up, full_down), (d_pre_of, partial_of), flops
     )
     partial = [partial_own, partial_other]
-
-    if ringed:
-
-        def term(i, step):
-            row = ring_member(place + step + peers, peers) * depth
-            return lax.dynamic_slice_in_dim(partial[i], row, depth, 0)
-
-        up, down = [None] * 2, [None] * 2
-        down[1] = lax.ppermute(term(1, half).astype(BF16), "gx", behind)
-        up[0] = lax.ppermute(term(0, half).astype(BF16), "gx", ahead)
-        for step in range(half - 1, 0, -1):
-            for i in (1, 0):
-                for way, at, pairs in ((up, step, ahead), (down, -step, behind)):
-                    value = term(i, at)
-                    if way[i] is not None:
-                        value = value + way[i].astype(F32)
-                    way[i] = lax.ppermute(value.astype(BF16), "gx", pairs)
-        total = [term(i, 0) + up[i].astype(F32) + down[i].astype(F32) for i in range(2)]
-    else:
-        total = [lax.psum_scatter(p, "gx", scatter_dimension=0, tiled=True) for p in partial]
-    passed = lax.ppermute(total[1].astype(BF16), "groups", swap).astype(F32)
-    low = jnp.where(side == 0, total[0], passed)
-    high = jnp.where(side == 0, passed, total[0])
-    up_grad = jnp.concatenate([low, high], axis=1)
 
     keep, send = call(
         d_norm_kernel,
@@ -236,11 +258,57 @@
         (shape((2, frame_len, half_width), F32), shape((2, frame_len, half_width), BF16)),
         4 * frame_len * width * quarter,
     )
-    came = lax.ppermute(send, "gy", swap)
-    over = call(
-        over_kernel, (meta, keep, came), shape((frame_len, half_width), BF16), frame_len * width
-    )
-    back = lax.ppermute(over, "groups", swap)
+
+    def sum_cores(send):
+        came = lax.ppermute(send, "gy", swap)
+        over = call(
+            over_kernel, (meta, keep, came), shape((frame_len, half_width), BF16), frame_len * width
+        )
+        return came, over
+
+    if ringed:
+
+        pair_of = shape((2, depth, quarter), BF16)
+        place_of = {step: i for i, step in enumerate(steps + [half])}
+
+        def hop(step, given, *came):
+            kernel = functools.partial(hop_kernel, place_of[step], given)
+            return call(kernel, (index, *partial, *came), pair_of, 2 * depth * quarter)
+
+        far_row = ring_member(place + half, peers) * depth
+        far = [lax.dynamic_slice_in_dim(p, far_row, depth, 0).astype(BF16) for p in partial]
+        down = lax.ppermute(far[1], "gx", behind)
+        up = lax.ppermute(far[0], "gx", ahead)
+        for step in range(half - 1, 0, -1):
+            if step == half - 1:
+                up, down, send = after((up, down, send))
+            elif step == half - 2:
+                up, down, over = after((up, down, over))
+            else:
+                up, down, back = after((up, down, back))
+            up = hop(step, (0,) if step == half - 1 else (0, 1), up)
+            down = hop(-step, (1,) if step == half - 1 else (0, 1), down)
+            up, down = lax.ppermute(up, "gx", ahead), lax.ppermute(down, "gx", behind)
+            if step == half - 1:
+                came, over = sum_cores(send)
+            if step == half - 2:
+                back = lax.ppermute(over, "groups", swap)
+        total, passing = call(
+            total_kernel,
+            (index, *partial, up, down),
+            (shape((depth, quarter), F32), shape((depth, quarter), BF16)),
+            4 * depth * quarter,
+        )
+    else:
+        total, passing = [
+            lax.psum_scatter(p, "gx", scatter_dimension=0, tiled=True) for p in partial
+        ]
+        passing = passing.astype(BF16)
+        came, over = sum_cores(send)
+        back = lax.ppermute(over, "groups", swap)
+    passed = lax.ppermute(passing, "groups", swap)
+    up_grad = call(join_kernel, (meta, total, passed), shape((depth, hidden), F32), 0)
+
     scaled, sums = call(
         scale_kernel,
         (meta, keep, came, back, frames, gain, stats),

time: 143 us -> 111 us (0.78)
  waiting for transfers between devices: 73 us -> 51.8 us
  starting transfers between devices: 34.1 us -> 21.5 us
  Pallas kernels: 16.5 us -> 21.5 us
  other arithmetic: 5.65 us -> 0.76 us
    ppermute x1, waiting for transfers between devices: 21.9 us -> 0.01 us  [shards(): first = lax.ppermute(share, 'groups', swap)]
    ppermute x28 -> x16, starting transfers between devices: 27.5 us -> 16.3 us  [the longest x12 13.6 us: shards(): up, down = (lax.ppermute(up, 'gx', ahead), lax.ppermute(down, 'gx', behind))]
    pallas_call x7 -> x16, Pallas kernels: 16.5 us -> 21.5 us  [call(): pl.pallas_call(kernel, out_shape=out_shape, in_specs=[SMEM if x.dtype ==...]
    convert_element_type x9 -> x0, other arithmetic: 2.6 us -> none  [the longest x8 1.84 us: shards(): way[i] = lax.ppermute(value.astype(BF16), 'gx', pairs)]
    ppermute x28 -> x16, waiting for transfers between devices: 46.9 us -> 48.1 us  [the longest x12 45.4 us: shards(): up, down = (lax.ppermute(up, 'gx', ahead), lax.ppermute(down, 'gx', behind))]
    unnamed x28 -> x24, local copies, waits for them, and re-layouts: 9.41 us -> 9.16 us
  transfers between devices with their start and end apart: 34 -> 22, of which waited for: 16 -> 17; matrix products, arithmetic and copies ran while one was open for 4% -> 4% of each run, Pallas kernels for 5% -> 13%
where the time goes in v4:
time: 111 us; the launch traced here: 110 us
  waiting for transfers between devices  51.8 us (47%)
  starting transfers between devices  21.5 us (19%)
  Pallas kernels  21.5 us (19%)
  local copies, waits for them, and re-layouts  13.8 us (12%)
    ppermute x12, waiting for transfers between devices, shards(): up, down = (lax.ppermute(up, 'gx', ahead), lax.ppermute(down, 'gx', behind))  45.4 us
    pallas_call x16, Pallas kernels, call(): pl.pallas_call(kernel, out_shape=out_shape, in_specs=[SMEM if x.dtype ==...  21.5 us
    ppermute x12, starting transfers between devices, shards(): up, down = (lax.ppermute(up, 'gx', ahead), lax.ppermute(down, 'gx', behind))  13.6 us
    unnamed x24, local copies, waits for them, and re-layouts  9.16 us
  transfers between devices with their start and end apart: 22, of which 17 were waited for; matrix products, arithmetic and copies ran while one was open for 4% of the time, Pallas kernels for 13%

profile of v4, /device:TPU:0, one launch (start us, length us, event | category | flops | bytes accessed | tf_op | source)
XLA Modules:
  0.0 110.2 jit_solution(12544298919701282939)
XLA Ops:
  1.9 3.0 %collective-permute-start.2 = (bf16[2,160,640]{2,1,0:T(8,128)(2,1)S(1)}, bf16[2,160,640]{2,1,0:T(8,128)(2,1)S(1)}, u32[]{:S(2)}, u32[]{:S(2)}) collective-permute-start(bf16[2,160,640]{2,1,0:T(8,128)(2,1)S(1)} %pad_maximum_fusion.refs_0_), channel_id=1, source_target_pairs={{4,0},{8,4},{12,8},{14,12},{10,14},{6,10},{2,6},{0,2},{5,1},{9,5},... | collective-permute-start | bytes 1228808 | tf_op jit(solution)/shard_map/ppermute | solution.py:221
  8.9 1.6 %shard_map.77 = (bf16[384,1280]{1,0:T(8,128)(2,1)S(1)}, bf16[384,1280]{1,0:T(8,128)(2,1)S(1)}, bf16[2,192,1280]{2,1,0:T(8,128)(2,1)S(1)}, f32[384,2]{1,0:T(8,128)S(1)}) custom-call(s32[3]{0:T(128)S(1)} %pad_add_fusion.meta, bf16[384,1280]{1,0:T(8,128)(2,1)S(1)} %bitcast.19, bf16[384,1280]{1,0:T(8,128)(2,1)S(1)} %bitcast.22, f32[1,1280]{1,0:T(1,128)S(1)} %broadcast_in_dim.6.gain), custom_call_target="tpu_custom_call" | custom-call | flops 4915200 | bytes 4923404 | tf_op jit(solution)/shard_map/pallas_call | solution.py:22
  11.4 1.9 %collective-permute-start = (bf16[2,192,1280]{2,1,0:T(8,128)(2,1)S(1)}, bf16[2,192,1280]{2,1,0:T(8,128)(2,1)}, u32[]{:S(2)}, u32[]{:S(2)}) collective-permute-start(bf16[2,192,1280]{2,1,0:T(8,128)(2,1)S(1)} %get-tuple-element.48), channel_id=1, source_target_pairs={{0,16},{16,0},{1,17},{17,1},{2,18},{18,2},{3,19},{19,3},{4,20},{20... | collective-permute-start | bytes 2949128 | tf_op jit(solution)/shard_map/ppermute | solution.py:213
  17.0 1.6 %collective-permute-start.4 = (bf16[2,160,640]{2,1,0:T(8,128)(2,1)S(1)}, bf16[2,160,640]{2,1,0:T(8,128)(2,1)S(1)}, u32[]{:S(2)}, u32[]{:S(2)}) collective-permute-start(bf16[2,160,640]{2,1,0:T(8,128)(2,1)S(1)} %collective-permute-done.2.refs_2_), channel_id=1, source_target_pairs={{4,0},{8,4},{12,8},{14,12},{10,14},{6,10},{2,6},{0,2},{5,1},{9,5},... | collective-permute-start | bytes 1228808 | tf_op jit(solution)/shard_map/ppermute | solution.py:221
  19.3 6.5 %collective-permute-done.3.refs_3_ = bf16[2,160,640]{2,1,0:T(8,128)(2,1)S(1)} collective-permute-done((bf16[2,160,640]{2,1,0:T(8,128)(2,1)S(1)}, bf16[2,160,640]{2,1,0:T(8,128)(2,1)S(1)}, u32[]{:S(2)}, u32[]{:S(2)}) %collective-permute-start.3) | collective-permute-done | bytes 409632 | tf_op jit(solution)/shard_map/ppermute | solution.py:221
  27.0 1.5 %collective-permute-start.5 = (bf16[2,160,640]{2,1,0:T(8,128)(2,1)S(1)}, bf16[2,160,640]{2,1,0:T(8,128)(2,1)S(1)}, u32[]{:S(2)}, u32[]{:S(2)}) collective-permute-start(bf16[2,160,640]{2,1,0:T(8,128)(2,1)S(1)} %collective-permute-done.3.refs_3_), channel_id=1, source_target_pairs={{0,4},{4,8},{8,12},{12,14},{14,10},{10,6},{6,2},{2,0},{1,5},{5,9},... | collective-permute-start | bytes 1228808 | tf_op jit(solution)/shard_map/ppermute | solution.py:221
  30.5 5.7 %collective-permute-done.5.refs_5_ = bf16[2,160,640]{2,1,0:T(8,128)(2,1)S(1)} collective-permute-done((bf16[2,160,640]{2,1,0:T(8,128)(2,1)S(1)}, bf16[2,160,640]{2,1,0:T(8,128)(2,1)S(1)}, u32[]{:S(2)}, u32[]{:S(2)}) %collective-permute-start.5) | collective-permute-done | bytes 409632 | tf_op jit(solution)/shard_map/ppermute | solution.py:221
  36.2 1.8 %collective-permute-done.6.refs_6_ = bf16[2,160,640]{2,1,0:T(8,128)(2,1)S(1)} collective-permute-done((bf16[2,160,640]{2,1,0:T(8,128)(2,1)S(1)}, bf16[2,160,640]{2,1,0:T(8,128)(2,1)S(1)}, u32[]{:S(2)}, u32[]{:S(2)}) %collective-permute-start.6) | collective-permute-done | bytes 409632 | tf_op jit(solution)/shard_map/ppermute | solution.py:221
  39.5 1.6 %collective-permute-start.8 = (bf16[160,640]{1,0:T(8,128)(2,1)}, bf16[160,640]{1,0:T(8,128)(2,1)}, u32[]{:S(2)}, u32[]{:S(2)}) collective-permute-start(bf16[160,640]{1,0:T(8,128)(2,1)} %slice_bitcast_fusion.1), channel_id=1, source_target_pairs={{0,4},{4,8},{8,12},{12,14},{14,10},{10,6},{6,2},{2,0},{1,5},{5,9},... | collective-permute-start | bytes 614408 | tf_op jit(solution)/shard_map/ppermute | solution.py:227
  48.6 4.4 %shard_map.79 = (bf16[384,640]{1,0:T(8,128)(2,1)S(1)}, f32[1280,640]{1,0:T(8,128)S(1)}, bf16[1280,640]{1,0:T(8,128)(2,1)S(1)}, bf16[1280,640]{1,0:T(8,128)(2,1)S(1)}) custom-call(s32[8]{0:T(128)S(1)} %stack.57.index, bf16[2,192,1280]{2,1,0:T(8,128)(2,1)} %collective-permute-done.first, ...), custom_call_target="tpu_custom_call", output_to_operand_aliasing={{2}: (3, {}), {3}: (4, {})} | custom-call | flops 1887436800 | bytes 12697632 | tf_op jit(solution)/shard_map/pallas_call | solution.py:22
  53.5 2.7 %shard_map.80 = (bf16[384,640]{1,0:T(8,128)(2,1)S(1)}, f32[1280,640]{1,0:T(8,128)S(1)}) custom-call(bf16[384,1280]{1,0:T(8,128)(2,1)S(1)} %copy-done.11, bf16[384,1280]{1,0:T(8,128)(2,1)S(1)} %get-tuple-element.47.grads, bf16[1280,640]{1,0:T(8,128)(2,1)S(1)} %get-tuple-element.60.up, bf16[1280,640]{1,0:T(8,128)(2,1)S(1)} %get-tuple-element.61.down), custom_call_target="tpu_custom_call" | custom-call | flops 1887436800 | bytes 9011200 | tf_op jit(solution)/shard_map/pallas_call | solution.py:22
  56.2 1.6 %collective-permute-start.10 = (bf16[160,640]{1,0:T(8,128)(2,1)S(1)}, bf16[160,640]{1,0:T(8,128)(2,1)S(1)}, u32[]{:S(2)}, u32[]{:S(2)}) collective-permute-start(bf16[160,640]{1,0:T(8,128)(2,1)S(1)} %dynamic-slice_convert_fusion.1), channel_id=1, source_target_pairs={{0,4},{4,8},{8,12},{12,14},{14,10},{10,6},{6,2},{2,0},{1,5},{5,9},... | collective-permute-start | bytes 614408 | tf_op jit(solution)/shard_map/ppermute | solution.py:281
  57.9 2.5 %shard_map.81 = (f32[2,384,640]{2,1,0:T(8,128)S(1)}, bf16[2,384,640]{2,1,0:T(8,128)(2,1)S(1)}) custom-call(s32[3]{0:T(128)S(1)} %pad_add_fusion.meta, bf16[384,640]{1,0:T(8,128)(2,1)S(1)} %get-tuple-element.62.d_pre_own, bf16[384,640]{1,0:T(8,128)(2,1)S(1)} %get-tuple-element.63.d_pre_other, bf16[1280,640]{1,0:T(8,128)(2,1)S(1)} %get-tuple-element.60.up), custom_call_target="tpu_custom_call" | custom-call | flops 1258291200 | bytes 5570572 | tf_op jit(solution)/shard_map/pallas_call | solution.py:22
  60.4 2.0 %collective-permute-done.10.refs_2_ = bf16[160,640]{1,0:T(8,128)(2,1)S(1)} collective-permute-done((bf16[160,640]{1,0:T(8,128)(2,1)S(1)}, bf16[160,640]{1,0:T(8,128)(2,1)S(1)}, u32[]{:S(2)}, u32[]{:S(2)}) %collective-permute-start.10) | collective-permute-done | bytes 204832 | tf_op jit(solution)/shard_map/ppermute | solution.py:281
  66.4 8.5 %collective-permute-done.14.refs_2_ = bf16[2,160,640]{2,1,0:T(8,128)(2,1)S(1)} collective-permute-done((bf16[2,160,640]{2,1,0:T(8,128)(2,1)S(1)}, bf16[2,160,640]{2,1,0:T(8,128)(2,1)S(1)}, u32[]{:S(2)}, u32[]{:S(2)}) %collective-permute-start.14) | collective-permute-done | bytes 409632 | tf_op jit(solution)/shard_map/ppermute | solution.py:291
  77.9 1.4 %collective-permute-start.16 = (bf16[2,160,640]{2,1,0:T(8,128)(2,1)S(1)}, bf16[2,160,640]{2,1,0:T(8,128)(2,1)S(1)}, u32[]{:S(2)}, u32[]{:S(2)}) collective-permute-start(bf16[2,160,640]{2,1,0:T(8,128)(2,1)S(1)} %shard_map.86), channel_id=1, source_target_pairs={{4,0},{8,4},{12,8},{14,12},{10,14},{6,10},{2,6},{0,2},{5,1},{9,5},... | collective-permute-start | bytes 1228808 | tf_op jit(solution)/shard_map/ppermute | solution.py:291
  80.7 7.8 %collective-permute-done.16.refs_2_ = bf16[2,160,640]{2,1,0:T(8,128)(2,1)S(1)} collective-permute-done((bf16[2,160,640]{2,1,0:T(8,128)(2,1)S(1)}, bf16[2,160,640]{2,1,0:T(8,128)(2,1)S(1)}, u32[]{:S(2)}, u32[]{:S(2)}) %collective-permute-start.16) | collective-permute-done | bytes 409632 | tf_op jit(solution)/shard_map/ppermute | solution.py:291
  88.4 1.8 %collective-permute-done.15.refs_2_ = bf16[2,160,640]{2,1,0:T(8,128)(2,1)S(1)} collective-permute-done((bf16[2,160,640]{2,1,0:T(8,128)(2,1)S(1)}, bf16[2,160,640]{2,1,0:T(8,128)(2,1)S(1)}, u32[]{:S(2)}, u32[]{:S(2)}) %collective-permute-start.15) | collective-permute-done | bytes 409632 | tf_op jit(solution)/shard_map/ppermute | solution.py:291
  90.9 1.6 %collective-permute-start.20 = (bf16[2,160,640]{2,1,0:T(8,128)(2,1)S(1)}, bf16[2,160,640]{2,1,0:T(8,128)(2,1)S(1)}, u32[]{:S(2)}, u32[]{:S(2)}) collective-permute-start(bf16[2,160,640]{2,1,0:T(8,128)(2,1)S(1)} %shard_map.90), channel_id=1, source_target_pairs={{4,0},{8,4},{12,8},{14,12},{10,14},{6,10},{2,6},{0,2},{5,1},{9,5},... | collective-permute-start | bytes 1228808 | tf_op jit(solution)/shard_map/ppermute | solution.py:291
  93.6 6.6 %collective-permute-done.20.down = bf16[2,160,640]{2,1,0:T(8,128)(2,1)S(1)} collective-permute-done((bf16[2,160,640]{2,1,0:T(8,128)(2,1)S(1)}, bf16[2,160,640]{2,1,0:T(8,128)(2,1)S(1)}, u32[]{:S(2)}, u32[]{:S(2)}) %collective-permute-start.20) | collective-permute-done | bytes 409632 | tf_op jit(solution)/shard_map/ppermute | solution.py:291
  100.2 2.0 %collective-permute-done.19.up = bf16[2,160,640]{2,1,0:T(8,128)(2,1)S(1)} collective-permute-done((bf16[2,160,640]{2,1,0:T(8,128)(2,1)S(1)}, bf16[2,160,640]{2,1,0:T(8,128)(2,1)S(1)}, u32[]{:S(2)}, u32[]{:S(2)}) %collective-permute-start.19) | collective-permute-done | bytes 409632 | tf_op jit(solution)/shard_map/ppermute | solution.py:291
  104.7 1.4 %collective-permute-done.18.came = f32[384,2]{1,0:T(8,128)S(1)} collective-permute-done((f32[384,2]{1,0:T(8,128)S(1)}, f32[384,2]{1,0:T(8,128)S(1)}, u32[]{:S(2)}, u32[]{:S(2)}) %collective-permute-start.18) | collective-permute-done | bytes 3104 | tf_op jit(solution)/shard_map/ppermute | solution.py:320
  106.1 1.9 %shard_map.88 = bf16[384,640]{1,0:T(8,128)(2,1)} custom-call(s32[3]{0:T(128)S(1)} %pad_add_fusion.meta, f32[384,640]{1,0:T(8,128)S(1)} %get-tuple-element.76.scaled, f32[384,2]{1,0:T(8,128)S(1)} %get-tuple-element.77.sums, f32[384,2]{1,0:T(8,128)S(1)} %collective-permute-done.18.came, bf16[384,1280]{1,0:T(8,128)(2,1)S(1)} %bitcast.21, ...), custom_call_target="tpu_custom_call" | custom-call | flops 1966080 | bytes 3449868 | tf_op jit(solution)/shard_map/pallas_call | solution.py:22
  108.7 1.5 %shard_map.92 = f32[160,1280]{1,0:T(8,128)} custom-call(s32[3]{0:T(128)S(1)} %pad_add_fusion.meta, f32[160,640]{1,0:T(8,128)S(1)} %get-tuple-element.80.own, bf16[160,640]{1,0:T(8,128)(2,1)S(1)} %collective-permute-done.21.passed), custom_call_target="tpu_custom_call" | custom-call | bytes 1433612 | tf_op jit(solution)/shard_map/pallas_call | solution.py:22
  (70 shorter events, 36.4 us)
Async XLA Ops:
  0.6 7.0 %copy-start = (bf16[1,384,1280]{2,1,0:T(8,128)(2,1)S(1)}, bf16[1,384,1280]{2,1,0:T(8,128)(2,1)}, u32[]{:S(2)}) copy-start(bf16[1,384,1280]{2,1,0:T(8,128)(2,1)} %param.6) | copy-start | bytes 2949124
  1.9 12.5 %collective-permute-start.2 = (bf16[2,160,640]{2,1,0:T(8,128)(2,1)S(1)}, bf16[2,160,640]{2,1,0:T(8,128)(2,1)S(1)}, u32[]{:S(2)}, u32[]{:S(2)}) collective-permute-start(bf16[2,160,640]{2,1,0:T(8,128)(2,1)S(1)} %pad_maximum_fusion.refs_0_), channel_id=1, source_target_pairs={{4,0},{8,4},{12,8},{14,12},{10,14},{6,10},{2,6},{0,2},{5,1},{9,5},... | collective-permute-start | bytes 1228808 | tf_op jit(solution)/shard_map/ppermute | solution.py:221
  4.9 10.9 %collective-permute-start.1 = (bf16[2,160,640]{2,1,0:T(8,128)(2,1)S(1)}, bf16[2,160,640]{2,1,0:T(8,128)(2,1)S(1)}, u32[]{:S(2)}, u32[]{:S(2)}) collective-permute-start(bf16[2,160,640]{2,1,0:T(8,128)(2,1)S(1)} %pad_maximum_fusion.refs_0_), channel_id=1, source_target_pairs={{0,4},{4,8},{8,12},{12,14},{14,10},{10,6},{6,2},{2,0},{1,5},{5,9},... | collective-permute-start | bytes 1228808 | tf_op jit(solution)/shard_map/ppermute | solution.py:221
  11.4 26.7 %collective-permute-start = (bf16[2,192,1280]{2,1,0:T(8,128)(2,1)S(1)}, bf16[2,192,1280]{2,1,0:T(8,128)(2,1)}, u32[]{:S(2)}, u32[]{:S(2)}) collective-permute-start(bf16[2,192,1280]{2,1,0:T(8,128)(2,1)S(1)} %get-tuple-element.48), channel_id=1, source_target_pairs={{0,16},{16,0},{1,17},{17,1},{2,18},{18,2},{3,19},{19,3},{4,20},{20... | collective-permute-start | bytes 2949128 | tf_op jit(solution)/shard_map/ppermute | solution.py:213
  15.8 10.0 %collective-permute-start.3 = (bf16[2,160,640]{2,1,0:T(8,128)(2,1)S(1)}, bf16[2,160,640]{2,1,0:T(8,128)(2,1)S(1)}, u32[]{:S(2)}, u32[]{:S(2)}) collective-permute-start(bf16[2,160,640]{2,1,0:T(8,128)(2,1)S(1)} %collective-permute-done.1.refs_1_), channel_id=1, source_target_pairs={{0,4},{4,8},{8,12},{12,14},{14,10},{10,6},{6,2},{2,0},{1,5},{5,9},... | collective-permute-start | bytes 1228808 | tf_op jit(solution)/shard_map/ppermute | solution.py:221
  17.0 10.1 %collective-permute-start.4 = (bf16[2,160,640]{2,1,0:T(8,128)(2,1)S(1)}, bf16[2,160,640]{2,1,0:T(8,128)(2,1)S(1)}, u32[]{:S(2)}, u32[]{:S(2)}) collective-permute-start(bf16[2,160,640]{2,1,0:T(8,128)(2,1)S(1)} %collective-permute-done.2.refs_2_), channel_id=1, source_target_pairs={{4,0},{8,4},{12,8},{14,12},{10,14},{6,10},{2,6},{0,2},{5,1},{9,5},... | collective-permute-start | bytes 1228808 | tf_op jit(solution)/shard_map/ppermute | solution.py:221
  27.0 9.2 %collective-permute-start.5 = (bf16[2,160,640]{2,1,0:T(8,128)(2,1)S(1)}, bf16[2,160,640]{2,1,0:T(8,128)(2,1)S(1)}, u32[]{:S(2)}, u32[]{:S(2)}) collective-permute-start(bf16[2,160,640]{2,1,0:T(8,128)(2,1)S(1)} %collective-permute-done.3.refs_3_), channel_id=1, source_target_pairs={{0,4},{4,8},{8,12},{12,14},{14,10},{10,6},{6,2},{2,0},{1,5},{5,9},... | collective-permute-start | bytes 1228808 | tf_op jit(solution)/shard_map/ppermute | solution.py:221
  29.3 8.8 %collective-permute-start.6 = (bf16[2,160,640]{2,1,0:T(8,128)(2,1)S(1)}, bf16[2,160,640]{2,1,0:T(8,128)(2,1)S(1)}, u32[]{:S(2)}, u32[]{:S(2)}) collective-permute-start(bf16[2,160,640]{2,1,0:T(8,128)(2,1)S(1)} %collective-permute-done.4.refs_4_), channel_id=1, source_target_pairs={{4,0},{8,4},{12,8},{14,12},{10,14},{6,10},{2,6},{0,2},{5,1},{9,5},... | collective-permute-start | bytes 1228808 | tf_op jit(solution)/shard_map/ppermute | solution.py:221
  38.1 10.5 %collective-permute-start.7 = (bf16[2,192,1280]{2,1,0:T(8,128)(2,1)}, bf16[2,192,1280]{2,1,0:T(8,128)(2,1)}, u32[]{:S(2)}, u32[]{:S(2)}) collective-permute-start(bf16[2,192,1280]{2,1,0:T(8,128)(2,1)} %collective-permute-done.first), channel_id=1, source_target_pairs={{0,1},{1,0},{2,3},{3,2},{4,5},{5,4},{6,7},{7,6},{8,9},{9,8},{10,11... | collective-permute-start | bytes 2949128 | tf_op jit(solution)/shard_map/ppermute | solution.py:238
  39.5 7.8 %collective-permute-start.8 = (bf16[160,640]{1,0:T(8,128)(2,1)}, bf16[160,640]{1,0:T(8,128)(2,1)}, u32[]{:S(2)}, u32[]{:S(2)}) collective-permute-start(bf16[160,640]{1,0:T(8,128)(2,1)} %slice_bitcast_fusion.1), channel_id=1, source_target_pairs={{0,4},{4,8},{8,12},{12,14},{14,10},{10,6},{6,2},{2,0},{1,5},{5,9},... | collective-permute-start | bytes 614408 | tf_op jit(solution)/shard_map/ppermute | solution.py:227
  41.1 7.5 %collective-permute-start.9 = (bf16[160,640]{1,0:T(8,128)(2,1)}, bf16[160,640]{1,0:T(8,128)(2,1)}, u32[]{:S(2)}, u32[]{:S(2)}) collective-permute-start(bf16[160,640]{1,0:T(8,128)(2,1)} %slice_bitcast_fusion), channel_id=1, source_target_pairs={{4,0},{8,4},{12,8},{14,12},{10,14},{6,10},{2,6},{0,2},{5,1},{9,5},... | collective-permute-start | bytes 614408 | tf_op jit(solution)/shard_map/ppermute | solution.py:227
  48.6 4.9 %copy-start.11 = (bf16[384,1280]{1,0:T(8,128)(2,1)S(1)}, bf16[384,1280]{1,0:T(8,128)(2,1)}, u32[]{:S(2)}) copy-start(bf16[384,1280]{1,0:T(8,128)(2,1)} %copy-done.10) | copy-start | bytes 2949124
  53.0 7.4 %collective-permute-start.11 = (bf16[160,640]{1,0:T(8,128)(2,1)S(1)}, bf16[160,640]{1,0:T(8,128)(2,1)S(1)}, u32[]{:S(2)}, u32[]{:S(2)}) collective-permute-start(bf16[160,640]{1,0:T(8,128)(2,1)S(1)} %dynamic-slice_convert_fusion), channel_id=1, source_target_pairs={{4,0},{8,4},{12,8},{14,12},{10,14},{6,10},{2,6},{0,2},{5,1},{9,5},... | collective-permute-start | bytes 614408 | tf_op jit(solution)/shard_map/ppermute | solution.py:280
  56.2 6.2 %collective-permute-start.10 = (bf16[160,640]{1,0:T(8,128)(2,1)S(1)}, bf16[160,640]{1,0:T(8,128)(2,1)S(1)}, u32[]{:S(2)}, u32[]{:S(2)}) collective-permute-start(bf16[160,640]{1,0:T(8,128)(2,1)S(1)} %dynamic-slice_convert_fusion.1), channel_id=1, source_target_pairs={{0,4},{4,8},{8,12},{12,14},{14,10},{10,6},{6,2},{2,0},{1,5},{5,9},... | collective-permute-start | bytes 614408 | tf_op jit(solution)/shard_map/ppermute | solution.py:281
  62.4 3.4 %collective-permute-start.12 = (bf16[2,384,640]{2,1,0:T(8,128)(2,1)S(1)}, bf16[2,384,640]{2,1,0:T(8,128)(2,1)S(1)}, u32[]{:S(2)}, u32[]{:S(2)}) collective-permute-start(bf16[2,384,640]{2,1,0:T(8,128)(2,1)S(1)} %get-tuple-element.68), channel_id=1, source_target_pairs={{0,1},{1,0},{2,3},{3,2},{4,5},{5,4},{6,7},{7,6},{8,9},{9,8},{10,11... | collective-permute-start | bytes 2949128 | tf_op jit(solution)/shard_map/ppermute | solution.py:263
  63.0 11.9 %collective-permute-start.14 = (bf16[2,160,640]{2,1,0:T(8,128)(2,1)S(1)}, bf16[2,160,640]{2,1,0:T(8,128)(2,1)S(1)}, u32[]{:S(2)}, u32[]{:S(2)}) collective-permute-start(bf16[2,160,640]{2,1,0:T(8,128)(2,1)S(1)} %shard_map.83), channel_id=1, source_target_pairs={{4,0},{8,4},{12,8},{14,12},{10,14},{6,10},{2,6},{0,2},{5,1},{9,5},... | collective-permute-start | bytes 1228808 | tf_op jit(solution)/shard_map/ppermute | solution.py:291
  64.4 11.6 %collective-permute-start.13 = (bf16[2,160,640]{2,1,0:T(8,128)(2,1)S(1)}, bf16[2,160,640]{2,1,0:T(8,128)(2,1)S(1)}, u32[]{:S(2)}, u32[]{:S(2)}) collective-permute-start(bf16[2,160,640]{2,1,0:T(8,128)(2,1)S(1)} %shard_map.82), channel_id=1, source_target_pairs={{0,4},{4,8},{8,12},{12,14},{14,10},{10,6},{6,2},{2,0},{1,5},{5,9},... | collective-permute-start | bytes 1228808 | tf_op jit(solution)/shard_map/ppermute | solution.py:291
  76.0 14.2 %collective-permute-start.17 = (bf16[384,640]{1,0:T(8,128)(2,1)S(1)}, bf16[384,640]{1,0:T(8,128)(2,1)S(1)}, u32[]{:S(2)}, u32[]{:S(2)}) collective-permute-start(bf16[384,640]{1,0:T(8,128)(2,1)S(1)} %shard_map.84), channel_id=1, source_target_pairs={{0,16},{16,0},{1,17},{17,1},{2,18},{18,2},{3,19},{19,3},{4,20},{20... | collective-permute-start | bytes 1474568 | tf_op jit(solution)/shard_map/ppermute | solution.py:295
  77.9 10.6 %collective-permute-start.16 = (bf16[2,160,640]{2,1,0:T(8,128)(2,1)S(1)}, bf16[2,160,640]{2,1,0:T(8,128)(2,1)S(1)}, u32[]{:S(2)}, u32[]{:S(2)}) collective-permute-start(bf16[2,160,640]{2,1,0:T(8,128)(2,1)S(1)} %shard_map.86), channel_id=1, source_target_pairs={{4,0},{8,4},{12,8},{14,12},{10,14},{6,10},{2,6},{0,2},{5,1},{9,5},... | collective-permute-start | bytes 1228808 | tf_op jit(solution)/shard_map/ppermute | solution.py:291
  80.0 10.3 %collective-permute-start.15 = (bf16[2,160,640]{2,1,0:T(8,128)(2,1)S(1)}, bf16[2,160,640]{2,1,0:T(8,128)(2,1)S(1)}, u32[]{:S(2)}, u32[]{:S(2)}) collective-permute-start(bf16[2,160,640]{2,1,0:T(8,128)(2,1)S(1)} %shard_map.85), channel_id=1, source_target_pairs={{0,4},{4,8},{8,12},{12,14},{14,10},{10,6},{6,2},{2,0},{1,5},{5,9},... | collective-permute-start | bytes 1228808 | tf_op jit(solution)/shard_map/ppermute | solution.py:291
  90.9 9.3 %collective-permute-start.20 = (bf16[2,160,640]{2,1,0:T(8,128)(2,1)S(1)}, bf16[2,160,640]{2,1,0:T(8,128)(2,1)S(1)}, u32[]{:S(2)}, u32[]{:S(2)}) collective-permute-start(bf16[2,160,640]{2,1,0:T(8,128)(2,1)S(1)} %shard_map.90), channel_id=1, source_target_pairs={{4,0},{8,4},{12,8},{14,12},{10,14},{6,10},{2,6},{0,2},{5,1},{9,5},... | collective-permute-start | bytes 1228808 | tf_op jit(solution)/shard_map/ppermute | solution.py:291
  93.1 9.1 %collective-permute-start.19 = (bf16[2,160,640]{2,1,0:T(8,128)(2,1)S(1)}, bf16[2,160,640]{2,1,0:T(8,128)(2,1)S(1)}, u32[]{:S(2)}, u32[]{:S(2)}) collective-permute-start(bf16[2,160,640]{2,1,0:T(8,128)(2,1)S(1)} %shard_map.89), channel_id=1, source_target_pairs={{0,4},{4,8},{8,12},{12,14},{14,10},{10,6},{6,2},{2,0},{1,5},{5,9},... | collective-permute-start | bytes 1228808 | tf_op jit(solution)/shard_map/ppermute | solution.py:291
  102.9 5.8 %collective-permute-start.21 = (bf16[160,640]{1,0:T(8,128)(2,1)S(1)}, bf16[160,640]{1,0:T(8,128)(2,1)S(1)}, u32[]{:S(2)}, u32[]{:S(2)}) collective-permute-start(bf16[160,640]{1,0:T(8,128)(2,1)S(1)} %get-tuple-element.81), channel_id=1, source_target_pairs={{0,16},{16,0},{1,17},{17,1},{2,18},{18,2},{3,19},{19,3},{4,20},{20... | collective-permute-start | bytes 614408 | tf_op jit(solution)/shard_map/ppermute | solution.py:309
  104.6 1.5 %collective-permute-start.18 = (f32[384,2]{1,0:T(8,128)S(1)}, f32[384,2]{1,0:T(8,128)S(1)}, u32[]{:S(2)}, u32[]{:S(2)}) collective-permute-start(f32[384,2]{1,0:T(8,128)S(1)} %get-tuple-element.77.sums), channel_id=1, source_target_pairs={{0,1},{1,0},{2,3},{3,2},{4,5},{5,4},{6,7},{7,6},{8,9},{9,8},{10,11... | collective-permute-start | bytes 9224 | tf_op jit(solution)/shard_map/ppermute | solution.py:320
  (10 other events, 9.2 us)

commit v5 on v4

--- a/solution.py
+++ b/solution.py
@@ -9,6 +9,7 @@
 
 BF16, F32 = jnp.bfloat16, jnp.float32
 VMEM = pl.BlockSpec(memory_space=pltpu.VMEM)
+ANY = pl.BlockSpec(memory_space=pl.ANY)
 SMEM = pl.BlockSpec(memory_space=pltpu.SMEM)
 
 
@@ -16,14 +17,17 @@
     return jax.ShapeDtypeStruct(dims, kind)
 
 
-def call(kernel, ins, out_shape, flops, scratch=(), vmem=16, aliases=None):
+def call(kernel, ins, out_shape, flops, scratch=(), vmem=16, aliases=None, left=(), out=VMEM):
     outs = jax.tree.leaves(out_shape)
     moved = sum(x.size * x.dtype.itemsize for x in list(ins) + outs)
     return pl.pallas_call(
         kernel,
         out_shape=out_shape,
-        in_specs=[SMEM if x.dtype == jnp.int32 else VMEM for x in ins],
-        out_specs=jax.tree.map(lambda _: VMEM, out_shape),
+        in_specs=[
+            SMEM if x.dtype == jnp.int32 else ANY if i in left else VMEM
+            for i, x in enumerate(ins)
+        ],
+        out_specs=jax.tree.map(lambda _: out, out_shape),
         scratch_shapes=list(scratch),
         input_output_aliases=aliases or {},
         compiler_params=pltpu.CompilerParams(vmem_limit_bytes=vmem << 20),
@@ -44,22 +48,41 @@
     )
 
 
-def norm_kernel(meta, frames, out_grad, gain, normed, grads, share, stats):
-    length, core = meta[0], meta[1]
-    values = frames[...].astype(F32)
-    centre = jnp.mean(values, axis=-1, keepdims=True)
-    shifted = values - centre
-    variance = jnp.mean(shifted * shifted, axis=-1, keepdims=True)
-    inv_std = lax.rsqrt(variance + 1e-05)
-    stats[:, 0:1] = centre
-    stats[:, 1:2] = inv_std
-    normed[...] = (shifted * inv_std * gain[...]).astype(BF16)
-    keep = lax.broadcasted_iota(jnp.int32, (frames.shape[0], 1), 0) < length
-    grads[...] = jnp.where(keep, out_grad[...].astype(F32), 0.0).astype(BF16)
-    half = share.shape[1]
-    rows = pl.ds(pl.multiple_of(core * half, half), half)
-    share[0] = normed[rows, :]
-    share[1] = grads[rows, :]
+def norm_kernel(turn, lengths, frames_from, grads_from, gain, *refs):
+    outs, (frames, out_grad, normed, grads, stats, sems) = refs[-10:-6], refs[-6:]
+    normed_to, grads_to, share, stats_to = outs
+    core = lax.axis_index("gy")
+
+    @pl.when(core == turn)
+    def _():
+        def start(source, target, at):
+            copy = pltpu.make_async_copy(source, target, sems.at[at])
+            copy.start()
+            return copy
+
+        come = [start(frames_from, frames, 0), start(grads_from, out_grad, 1)]
+        half = share.shape[1]
+        rows = pl.ds(pl.multiple_of(core * half, half), half)
+        come[1].wait()
+        length = lengths[lax.axis_index("gx")]
+        keep = lax.broadcasted_iota(jnp.int32, (frames.shape[0], 1), 0) < length
+        grads[...] = jnp.where(keep, out_grad[...].astype(F32), 0.0).astype(BF16)
+        go = [start(grads.at[rows], share.at[1], 2), start(grads, grads_to, 3)]
+        come[0].wait()
+        values = frames[...].astype(F32)
+        centre = jnp.mean(values, axis=-1, keepdims=True)
+        shifted = values - centre
+        variance = jnp.mean(shifted * shifted, axis=-1, keepdims=True)
+        inv_std = lax.rsqrt(variance + 1e-05)
+        normed[...] = (shifted * inv_std * gain[...][None]).astype(BF16)
+        go += [start(normed.at[rows], share.at[0], 4), start(normed, normed_to, 5)]
+        stats[...] = jnp.concatenate(
+            [jnp.broadcast_to(centre, (len(centre), 128)), jnp.broadcast_to(inv_std, (len(centre), 128))],
+            axis=1,
+        )
+        go += [start(stats, stats_to, 6)]
+        for copy in go:
+            copy.wait()
 
 
 def back_through(normed, grads, up, down, d_pre, partial):
@@ -69,22 +92,18 @@
     partial[...] = dot(normed[...], d_pre[...], 0, 0)
 
 
-def place_kernel(index, *refs):
-    blocks, (up, down) = refs[:-2], refs[-2:]
-    depth = blocks[0].shape[1]
+def other_kernel(index, first, second, up_far, down_far, *refs):
+    blocks, (d_pre, partial, up, down, normed, grads) = refs[:-6], refs[-6:]
+    half, depth = first.shape[1], up_far.shape[0]
+
+    def rows(i):
+        return pl.ds(pl.multiple_of(index[i] * depth, depth), depth)
+
     for i, block in enumerate(blocks):
-        rows = pl.ds(pl.multiple_of(index[i] * depth, depth), depth)
-        up[rows, :] = block[0]
-        down[rows, :] = block[1]
-
-
-def other_kernel(index, first, second, _, __, *refs):
-    d_pre, partial, up, down, normed, grads = refs[-6:]
-    half = first.shape[1]
-    for ref, block in zip((up, down), refs[:-6]):
-        depth = block.shape[0]
-        rows = pl.ds(pl.multiple_of(index[index.shape[0] - 1] * depth, depth), depth)
-        ref[rows, :] = block[...]
+        up[rows(i), :] = block[0]
+        down[rows(i), :] = block[1]
+    up[rows(len(blocks)), :] = up_far[...]
+    down[rows(len(blocks)), :] = down_far[...]
     for at, part in ((0, first), (half, second)):
         normed[at : at + half, :] = part[0]
         grads[at : at + half, :] = part[1]
@@ -127,7 +146,7 @@
     value = d_norm * own_columns(meta, gain, width)
     scaled[...] = value
     rows = own_columns(meta, frames, width).astype(F32)
-    centred = (rows - stats[:, 0:1]) * stats[:, 1:2]
+    centred = (rows - stats[:, 0:1]) * stats[:, 128:129]
     sums[:, 0:1] = jnp.sum(value, axis=-1, keepdims=True)
     sums[:, 1:2] = jnp.sum(value * centred, axis=-1, keepdims=True)
 
@@ -136,7 +155,7 @@
     width = scaled.shape[1]
     means = (sums[...] + came[...]) * (0.5 / width)
     rows = own_columns(meta, frames, width).astype(F32)
-    inv_std = stats[:, 1:2]
+    inv_std = stats[:, 128:129]
     centred = (rows - stats[:, 0:1]) * inv_std
     value = inv_std * (scaled[...] - means[:, 0:1] - centred * means[:, 1:2])
     out[...] = (own_columns(meta, grads, width).astype(F32) + value).astype(BF16)
@@ -195,26 +214,36 @@
     after = lax.optimization_barrier
 
     mine = [lax.dynamic_slice_in_dim(w, side * quarter, quarter, 1) for w in (w_up, w_down)]
-    mine, frames, out_grad, ln_gain, lengths = after(
-        (mine, frames, out_grad, ln_gain, lengths)
-    )
-
-    length = lax.dynamic_index_in_dim(lengths, own, 0, keepdims=False)
-    meta = jnp.stack([length, core, side]).astype(jnp.int32)
-    gain = ln_gain[None]
+    meta = jnp.stack([own, core, side]).astype(jnp.int32)
     frames, out_grad = frames[0], out_grad[0]
+
     rows_of = shape((frame_len, width), BF16)
-    normed, grads, share, stats = call(
-        norm_kernel,
-        (meta, frames, out_grad, gain),
-        (rows_of, rows_of, shape((2, half_rows, width), BF16), shape((frame_len, 2), F32)),
-        10 * frame_len * width,
-    )
+    halves_of = shape((2, half_rows, width), BF16)
+    results = (rows_of, rows_of, halves_of, shape((frame_len, 256), F32))
+
+    def norm(turn, *given):
+        return call(
+            functools.partial(norm_kernel, turn),
+            (lengths, frames, out_grad, ln_gain, *given),
+            results,
+            10 * frame_len * width,
+            [pltpu.VMEM((frame_len, width), BF16)] * 4
+            + [pltpu.VMEM((frame_len, 256), F32), pltpu.SemaphoreType.DMA((7,))],
+            aliases={4 + i: i for i in range(len(given))},
+            vmem=56,
+            left=(1, 2, 4, 5, 6, 7),
+            out=ANY,
+        )
+
+    results_one = norm(1)
+    if ringed:
+        pair, results_one = after((jnp.stack(mine), results_one))
+    normed, grads, share, stats = norm(0, *results_one)
+
     first = lax.ppermute(share, "groups", swap)
 
     weight = shape((depth * peers, quarter), BF16)
     if ringed:
-        pair = jnp.stack(mine)
         blocks = {0: pair}
         up, down = pair, pair
         for step in range(1, half):
@@ -230,22 +259,19 @@
         index = index.astype(jnp.int32)
         first, up = after((first, up))
         near = [blocks[step] for step in steps]
-        full_up, full_down = call(place_kernel, (index, *near), (weight, weight), 0)
     else:
-        full_up, full_down = [lax.all_gather(w, "gx", axis=0, tiled=True) for w in mine]
-        index = own[None].astype(jnp.int32)
-        far = ()
+        far = [lax.all_gather(w, "gx", axis=0, tiled=True) for w in mine]
+        index, near = jnp.zeros((1,), jnp.int32), ()
     second = lax.ppermute(first, "gy", swap)
 
     d_pre_of, partial_of = shape((frame_len, quarter), BF16), shape((width, quarter), F32)
     flops = 6 * frame_len * width * quarter
     d_pre_other, partial_other, full_up, full_down = call(
         other_kernel,
-        (index, first, second, full_up, full_down, *far),
+        (index, first, second, *far, *near),
         (d_pre_of, partial_of, weight, weight),
         flops,
         [pltpu.VMEM((frame_len, width), BF16)] * 2,
-        aliases={3: 2, 4: 3},
     )
     d_pre_own, partial_own = call(
         own_kernel, (normed, grads, full_up, full_down), (d_pre_of, partial_of), flops
@@ -309,6 +335,7 @@
     passed = lax.ppermute(passing, "groups", swap)
     up_grad = call(join_kernel, (meta, total, passed), shape((depth, hidden), F32), 0)
 
+    gain = ln_gain[None]
     scaled, sums = call(
         scale_kernel,
         (meta, keep, came, back, frames, gain, stats),

time: 111 us -> 118 us (1.063)
  waiting for transfers between devices: 51.8 us -> 60.9 us
  local copies, waits for them, and re-layouts: 13.8 us -> 9.67 us
  Pallas kernels: 21.5 us -> 23.7 us
    ppermute x12, waiting for transfers between devices: 45.4 us -> 50.5 us  [shards(): up, down = (lax.ppermute(up, 'gx', ahead), lax.ppermute(down, 'gx', behind))]
    ppermute x1, waiting for transfers between devices: 0.91 us -> 4.83 us  [shards(): lax.ppermute(up[0], 'gx', ahead)]
    dynamic_slice x2 -> x0, local copies, waits for them, and re-layouts: 2.42 us -> none  [the longest x1 1.26 us: shards(): length = lax.dynamic_index_in_dim(lengths, own, 0, keepdims=False)]
    pallas_call x16, Pallas kernels: 21.5 us -> 23.7 us  [call(): pl.pallas_call(kernel, out_shape=out_shape, in_specs=[SMEM if x.dtype ==...]
    unnamed x24 -> x26, local copies, waits for them, and re-layouts: 9.16 us -> 7.04 us
  transfers between devices with their start and end apart: 22 -> 22, of which waited for: 17 -> 18; matrix products, arithmetic and copies ran while one was open for 4% -> 1% of each run, Pallas kernels for 13% -> 12%
where the time goes in v5:
time: 118 us
  waiting for transfers between devices  60.9 us (52%)
  Pallas kernels  23.7 us (20%)
  starting transfers between devices  22.3 us (19%)
  local copies, waits for them, and re-layouts  9.67 us (8%)
    ppermute x12, waiting for transfers between devices, shards(): up, down = (lax.ppermute(up, 'gx', ahead), lax.ppermute(down, 'gx', behind))  50.5 us
    pallas_call x16, Pallas kernels, call(): pl.pallas_call(kernel, out_shape=out_shape, in_specs=[SMEM if x.dtype ==...  23.7 us
    ppermute x12, starting transfers between devices, shards(): up, down = (lax.ppermute(up, 'gx', ahead), lax.ppermute(down, 'gx', behind))  13.5 us
    unnamed x26, local copies, waits for them, and re-layouts  7.04 us
    ppermute x1, waiting for transfers between devices, shards(): lax.ppermute(up[0], 'gx', ahead)  4.83 us
  transfers between devices with their start and end apart: 22, of which 18 were waited for; matrix products, arithmetic and copies ran while one was open for 1% of the time, Pallas kernels for 12%

profile of v5, /device:TPU:0, one launch (start us, length us, event | category | flops | bytes accessed | tf_op | source)
XLA Modules:
  0.0 117.6 jit_solution(13388128793096671936)
XLA Ops:
  2.5 3.1 %collective-permute-start.1 = (bf16[2,160,640]{2,1,0:T(8,128)(2,1)S(1)}, bf16[2,160,640]{2,1,0:T(8,128)(2,1)S(1)}, u32[]{:S(2)}, u32[]{:S(2)}) collective-permute-start(bf16[2,160,640]{2,1,0:T(8,128)(2,1)S(1)} %pad_maximum_fusion.refs_0_), channel_id=1, source_target_pairs={{0,4},{4,8},{8,12},{12,14},{14,10},{10,6},{6,2},{2,0},{1,5},{5,9},... | collective-permute-start | bytes 1228808 | tf_op jit(solution)/shard_map/ppermute | solution.py:250
  5.6 4.3 %shard_map.78 = (bf16[384,1280]{1,0:T(8,128)(2,1)}, bf16[384,1280]{1,0:T(8,128)(2,1)}, bf16[2,192,1280]{2,1,0:T(8,128)(2,1)}, f32[384,256]{1,0:T(8,128)}) custom-call(s32[8]{0:T(128)} %lengths.3, bf16[384,1280]{1,0:T(8,128)(2,1)} %bitcast.23, bf16[384,1280]{1,0:T(8,128)(2,1)} %bitcast.27, ...), custom_call_target="tpu_custom_call", output_to_operand_aliasing={{0}: (4, {}), {1}: (5, {}), {2}: (6, {}), {3}: (7, {})} | custom-call | flops 4915200 | bytes 8655904 | tf_op jit(solution)/shard_map/pallas_call | solution.py:23
  9.9 2.0 %collective-permute-start = (bf16[2,192,1280]{2,1,0:T(8,128)(2,1)}, bf16[2,192,1280]{2,1,0:T(8,128)(2,1)S(1)}, u32[]{:S(2)}, u32[]{:S(2)}) collective-permute-start(bf16[2,192,1280]{2,1,0:T(8,128)(2,1)} %get-tuple-element.53), channel_id=1, source_target_pairs={{0,16},{16,0},{1,17},{17,1},{2,18},{18,2},{3,19},{19,3},{4,20},{20... | collective-permute-start | bytes 2949128 | tf_op jit(solution)/shard_map/ppermute | solution.py:243
  13.1 2.6 %collective-permute-done.2.refs_2_ = bf16[2,160,640]{2,1,0:T(8,128)(2,1)S(1)} collective-permute-done((bf16[2,160,640]{2,1,0:T(8,128)(2,1)S(1)}, bf16[2,160,640]{2,1,0:T(8,128)(2,1)S(1)}, u32[]{:S(2)}, u32[]{:S(2)}) %collective-permute-start.2) | collective-permute-done | bytes 409632 | tf_op jit(solution)/shard_map/ppermute | solution.py:250
  15.8 1.6 %collective-permute-start.3 = (bf16[2,160,640]{2,1,0:T(8,128)(2,1)S(1)}, bf16[2,160,640]{2,1,0:T(8,128)(2,1)S(1)}, u32[]{:S(2)}, u32[]{:S(2)}) collective-permute-start(bf16[2,160,640]{2,1,0:T(8,128)(2,1)S(1)} %collective-permute-done.1.refs_1_), channel_id=1, source_target_pairs={{0,4},{4,8},{8,12},{12,14},{14,10},{10,6},{6,2},{2,0},{1,5},{5,9},... | collective-permute-start | bytes 1228808 | tf_op jit(solution)/shard_map/ppermute | solution.py:250
  19.3 7.4 %collective-permute-done.3.refs_3_ = bf16[2,160,640]{2,1,0:T(8,128)(2,1)S(1)} collective-permute-done((bf16[2,160,640]{2,1,0:T(8,128)(2,1)S(1)}, bf16[2,160,640]{2,1,0:T(8,128)(2,1)S(1)}, u32[]{:S(2)}, u32[]{:S(2)}) %collective-permute-start.3) | collective-permute-done | bytes 409632 | tf_op jit(solution)/shard_map/ppermute | solution.py:250
  26.7 2.6 %collective-permute-done.4.refs_4_ = bf16[2,160,640]{2,1,0:T(8,128)(2,1)S(1)} collective-permute-done((bf16[2,160,640]{2,1,0:T(8,128)(2,1)S(1)}, bf16[2,160,640]{2,1,0:T(8,128)(2,1)S(1)}, u32[]{:S(2)}, u32[]{:S(2)}) %collective-permute-start.4) | collective-permute-done | bytes 409632 | tf_op jit(solution)/shard_map/ppermute | solution.py:250
  29.4 1.6 %collective-permute-start.5 = (bf16[2,160,640]{2,1,0:T(8,128)(2,1)S(1)}, bf16[2,160,640]{2,1,0:T(8,128)(2,1)S(1)}, u32[]{:S(2)}, u32[]{:S(2)}) collective-permute-start(bf16[2,160,640]{2,1,0:T(8,128)(2,1)S(1)} %collective-permute-done.3.refs_3_), channel_id=1, source_target_pairs={{0,4},{4,8},{8,12},{12,14},{14,10},{10,6},{6,2},{2,0},{1,5},{5,9},... | collective-permute-start | bytes 1228808 | tf_op jit(solution)/shard_map/ppermute | solution.py:250
  32.9 8.6 %collective-permute-done.5.refs_5_ = bf16[2,160,640]{2,1,0:T(8,128)(2,1)S(1)} collective-permute-done((bf16[2,160,640]{2,1,0:T(8,128)(2,1)S(1)}, bf16[2,160,640]{2,1,0:T(8,128)(2,1)S(1)}, u32[]{:S(2)}, u32[]{:S(2)}) %collective-permute-start.5) | collective-permute-done | bytes 409632 | tf_op jit(solution)/shard_map/ppermute | solution.py:250
  41.5 2.5 %collective-permute-done.6.refs_6_ = bf16[2,160,640]{2,1,0:T(8,128)(2,1)S(1)} collective-permute-done((bf16[2,160,640]{2,1,0:T(8,128)(2,1)S(1)}, bf16[2,160,640]{2,1,0:T(8,128)(2,1)S(1)}, u32[]{:S(2)}, u32[]{:S(2)}) %collective-permute-start.6) | collective-permute-done | bytes 409632 | tf_op jit(solution)/shard_map/ppermute | solution.py:250
  47.6 4.8 %collective-permute-done.8.up_far = bf16[160,640]{1,0:T(8,128)(2,1)S(1)} collective-permute-done((bf16[160,640]{1,0:T(8,128)(2,1)}, bf16[160,640]{1,0:T(8,128)(2,1)S(1)}, u32[]{:S(2)}, u32[]{:S(2)}) %collective-permute-start.8) | collective-permute-done | bytes 204832 | tf_op jit(solution)/shard_map/ppermute | solution.py:256
  52.4 2.1 %collective-permute-done.9.down_far = bf16[160,640]{1,0:T(8,128)(2,1)} collective-permute-done((bf16[160,640]{1,0:T(8,128)(2,1)}, bf16[160,640]{1,0:T(8,128)(2,1)}, u32[]{:S(2)}, u32[]{:S(2)}) %collective-permute-start.9) | collective-permute-done | bytes 204832 | tf_op jit(solution)/shard_map/ppermute | solution.py:256
  58.5 3.9 %shard_map.79 = (bf16[384,640]{1,0:T(8,128)(2,1)S(1)}, f32[1280,640]{1,0:T(8,128)S(1)}, bf16[1280,640]{1,0:T(8,128)(2,1)S(1)}, bf16[1280,640]{1,0:T(8,128)(2,1)S(1)}) custom-call(s32[8]{0:T(128)S(1)} %stack.63.index, bf16[2,192,1280]{2,1,0:T(8,128)(2,1)S(1)} %collective-permute-done.first, bf16[2,192,1280]{2,1,0:T(8,128)(2,1)S(1)} %collective-permute-done.7.second, ...), custom_call_target="tpu_custom_call" | custom-call | flops 1887436800 | bytes 12288032 | tf_op jit(solution)/shard_map/pallas_call | solution.py:23
  62.4 2.7 %shard_map.80 = (bf16[384,640]{1,0:T(8,128)(2,1)S(1)}, f32[1280,640]{1,0:T(8,128)S(1)}) custom-call(bf16[384,1280]{1,0:T(8,128)(2,1)S(1)} %copy-done.3, bf16[384,1280]{1,0:T(8,128)(2,1)S(1)} %copy-done.1, bf16[1280,640]{1,0:T(8,128)(2,1)S(1)} %get-tuple-element.62.up, bf16[1280,640]{1,0:T(8,128)(2,1)S(1)} %get-tuple-element.63.down), custom_call_target="tpu_custom_call" | custom-call | flops 1887436800 | bytes 9011200 | tf_op jit(solution)/shard_map/pallas_call | solution.py:23
  65.7 1.6 %collective-permute-start.11 = (bf16[160,640]{1,0:T(8,128)(2,1)S(1)}, bf16[160,640]{1,0:T(8,128)(2,1)S(1)}, u32[]{:S(2)}, u32[]{:S(2)}) collective-permute-start(bf16[160,640]{1,0:T(8,128)(2,1)S(1)} %dynamic-slice_convert_fusion), channel_id=1, source_target_pairs={{4,0},{8,4},{12,8},{14,12},{10,14},{6,10},{2,6},{0,2},{5,1},{9,5},... | collective-permute-start | bytes 614408 | tf_op jit(solution)/shard_map/ppermute | solution.py:306
  67.4 2.5 %shard_map.81 = (f32[2,384,640]{2,1,0:T(8,128)S(1)}, bf16[2,384,640]{2,1,0:T(8,128)(2,1)S(1)}) custom-call(s32[3]{0:T(128)S(1)} %pad_add_fusion.meta, bf16[384,640]{1,0:T(8,128)(2,1)S(1)} %get-tuple-element.64.d_pre_own, bf16[384,640]{1,0:T(8,128)(2,1)S(1)} %get-tuple-element.65.d_pre_other, bf16[1280,640]{1,0:T(8,128)(2,1)S(1)} %get-tuple-element.62.up), custom_call_target="tpu_custom_call" | custom-call | flops 1258291200 | bytes 5570572 | tf_op jit(solution)/shard_map/pallas_call | solution.py:23
  69.9 1.6 %collective-permute-done.10.refs_2_ = bf16[160,640]{1,0:T(8,128)(2,1)S(1)} collective-permute-done((bf16[160,640]{1,0:T(8,128)(2,1)S(1)}, bf16[160,640]{1,0:T(8,128)(2,1)S(1)}, u32[]{:S(2)}, u32[]{:S(2)}) %collective-permute-start.10) | collective-permute-done | bytes 204832 | tf_op jit(solution)/shard_map/ppermute | solution.py:307
  73.5 1.6 %collective-permute-start.14 = (bf16[2,160,640]{2,1,0:T(8,128)(2,1)S(1)}, bf16[2,160,640]{2,1,0:T(8,128)(2,1)S(1)}, u32[]{:S(2)}, u32[]{:S(2)}) collective-permute-start(bf16[2,160,640]{2,1,0:T(8,128)(2,1)S(1)} %shard_map.83), channel_id=1, source_target_pairs={{4,0},{8,4},{12,8},{14,12},{10,14},{6,10},{2,6},{0,2},{5,1},{9,5},... | collective-permute-start | bytes 1228808 | tf_op jit(solution)/shard_map/ppermute | solution.py:317
  75.8 8.5 %collective-permute-done.13.refs_2_ = bf16[2,160,640]{2,1,0:T(8,128)(2,1)S(1)} collective-permute-done((bf16[2,160,640]{2,1,0:T(8,128)(2,1)S(1)}, bf16[2,160,640]{2,1,0:T(8,128)(2,1)S(1)}, u32[]{:S(2)}, u32[]{:S(2)}) %collective-permute-start.13) | collective-permute-done | bytes 409632 | tf_op jit(solution)/shard_map/ppermute | solution.py:317
  88.4 1.6 %collective-permute-start.16 = (bf16[2,160,640]{2,1,0:T(8,128)(2,1)S(1)}, bf16[2,160,640]{2,1,0:T(8,128)(2,1)S(1)}, u32[]{:S(2)}, u32[]{:S(2)}) collective-permute-start(bf16[2,160,640]{2,1,0:T(8,128)(2,1)S(1)} %shard_map.86), channel_id=1, source_target_pairs={{4,0},{8,4},{12,8},{14,12},{10,14},{6,10},{2,6},{0,2},{5,1},{9,5},... | collective-permute-start | bytes 1228808 | tf_op jit(solution)/shard_map/ppermute | solution.py:317
  90.0 7.8 %collective-permute-done.15.refs_2_ = bf16[2,160,640]{2,1,0:T(8,128)(2,1)S(1)} collective-permute-done((bf16[2,160,640]{2,1,0:T(8,128)(2,1)S(1)}, bf16[2,160,640]{2,1,0:T(8,128)(2,1)S(1)}, u32[]{:S(2)}, u32[]{:S(2)}) %collective-permute-start.15) | collective-permute-done | bytes 409632 | tf_op jit(solution)/shard_map/ppermute | solution.py:317
  100.5 1.6 %collective-permute-start.20 = (bf16[2,160,640]{2,1,0:T(8,128)(2,1)S(1)}, bf16[2,160,640]{2,1,0:T(8,128)(2,1)S(1)}, u32[]{:S(2)}, u32[]{:S(2)}) collective-permute-start(bf16[2,160,640]{2,1,0:T(8,128)(2,1)S(1)} %shard_map.90), channel_id=1, source_target_pairs={{4,0},{8,4},{12,8},{14,12},{10,14},{6,10},{2,6},{0,2},{5,1},{9,5},... | collective-permute-start | bytes 1228808 | tf_op jit(solution)/shard_map/ppermute | solution.py:317
  102.1 6.6 %collective-permute-done.19.up = bf16[2,160,640]{2,1,0:T(8,128)(2,1)S(1)} collective-permute-done((bf16[2,160,640]{2,1,0:T(8,128)(2,1)S(1)}, bf16[2,160,640]{2,1,0:T(8,128)(2,1)S(1)}, u32[]{:S(2)}, u32[]{:S(2)}) %collective-permute-start.19) | collective-permute-done | bytes 409632 | tf_op jit(solution)/shard_map/ppermute | solution.py:317
  114.0 1.9 %shard_map.88 = bf16[384,640]{1,0:T(8,128)(2,1)} custom-call(s32[3]{0:T(128)S(1)} %pad_add_fusion.meta, f32[384,640]{1,0:T(8,128)S(1)} %get-tuple-element.78.scaled, f32[384,2]{1,0:T(8,128)S(1)} %get-tuple-element.79.sums, f32[384,2]{1,0:T(8,128)S(1)} %collective-permute-done.18.came, bf16[384,1280]{1,0:T(8,128)(2,1)S(1)} %bitcast.25, ...), custom_call_target="tpu_custom_call" | custom-call | flops 1966080 | bytes 3840012 | tf_op jit(solution)/shard_map/pallas_call | solution.py:23
  (71 shorter events, 31.5 us)
Async XLA Ops:
  2.5 10.6 %collective-permute-start.1 = (bf16[2,160,640]{2,1,0:T(8,128)(2,1)S(1)}, bf16[2,160,640]{2,1,0:T(8,128)(2,1)S(1)}, u32[]{:S(2)}, u32[]{:S(2)}) collective-permute-start(bf16[2,160,640]{2,1,0:T(8,128)(2,1)S(1)} %pad_maximum_fusion.refs_0_), channel_id=1, source_target_pairs={{0,4},{4,8},{8,12},{12,14},{14,10},{10,6},{6,2},{2,0},{1,5},{5,9},... | collective-permute-start | bytes 1228808 | tf_op jit(solution)/shard_map/ppermute | solution.py:250
  5.6 10.2 %collective-permute-start.2 = (bf16[2,160,640]{2,1,0:T(8,128)(2,1)S(1)}, bf16[2,160,640]{2,1,0:T(8,128)(2,1)S(1)}, u32[]{:S(2)}, u32[]{:S(2)}) collective-permute-start(bf16[2,160,640]{2,1,0:T(8,128)(2,1)S(1)} %pad_maximum_fusion.refs_0_), channel_id=1, source_target_pairs={{4,0},{8,4},{12,8},{14,12},{10,14},{6,10},{2,6},{0,2},{5,1},{9,5},... | collective-permute-start | bytes 1228808 | tf_op jit(solution)/shard_map/ppermute | solution.py:250
  9.9 34.1 %collective-permute-start = (bf16[2,192,1280]{2,1,0:T(8,128)(2,1)}, bf16[2,192,1280]{2,1,0:T(8,128)(2,1)S(1)}, u32[]{:S(2)}, u32[]{:S(2)}) collective-permute-start(bf16[2,192,1280]{2,1,0:T(8,128)(2,1)} %get-tuple-element.53), channel_id=1, source_target_pairs={{0,16},{16,0},{1,17},{17,1},{2,18},{18,2},{3,19},{19,3},{4,20},{20... | collective-permute-start | bytes 2949128 | tf_op jit(solution)/shard_map/ppermute | solution.py:243
  15.8 11.0 %collective-permute-start.3 = (bf16[2,160,640]{2,1,0:T(8,128)(2,1)S(1)}, bf16[2,160,640]{2,1,0:T(8,128)(2,1)S(1)}, u32[]{:S(2)}, u32[]{:S(2)}) collective-permute-start(bf16[2,160,640]{2,1,0:T(8,128)(2,1)S(1)} %collective-permute-done.1.refs_1_), channel_id=1, source_target_pairs={{0,4},{4,8},{8,12},{12,14},{14,10},{10,6},{6,2},{2,0},{1,5},{5,9},... | collective-permute-start | bytes 1228808 | tf_op jit(solution)/shard_map/ppermute | solution.py:250
  18.1 11.3 %collective-permute-start.4 = (bf16[2,160,640]{2,1,0:T(8,128)(2,1)S(1)}, bf16[2,160,640]{2,1,0:T(8,128)(2,1)S(1)}, u32[]{:S(2)}, u32[]{:S(2)}) collective-permute-start(bf16[2,160,640]{2,1,0:T(8,128)(2,1)S(1)} %collective-permute-done.2.refs_2_), channel_id=1, source_target_pairs={{4,0},{8,4},{12,8},{14,12},{10,14},{6,10},{2,6},{0,2},{5,1},{9,5},... | collective-permute-start | bytes 1228808 | tf_op jit(solution)/shard_map/ppermute | solution.py:250
  29.4 12.1 %collective-permute-start.5 = (bf16[2,160,640]{2,1,0:T(8,128)(2,1)S(1)}, bf16[2,160,640]{2,1,0:T(8,128)(2,1)S(1)}, u32[]{:S(2)}, u32[]{:S(2)}) collective-permute-start(bf16[2,160,640]{2,1,0:T(8,128)(2,1)S(1)} %collective-permute-done.3.refs_3_), channel_id=1, source_target_pairs={{0,4},{4,8},{8,12},{12,14},{14,10},{10,6},{6,2},{2,0},{1,5},{5,9},... | collective-permute-start | bytes 1228808 | tf_op jit(solution)/shard_map/ppermute | solution.py:250
  31.7 12.3 %collective-permute-start.6 = (bf16[2,160,640]{2,1,0:T(8,128)(2,1)S(1)}, bf16[2,160,640]{2,1,0:T(8,128)(2,1)S(1)}, u32[]{:S(2)}, u32[]{:S(2)}) collective-permute-start(bf16[2,160,640]{2,1,0:T(8,128)(2,1)S(1)} %collective-permute-done.4.refs_4_), channel_id=1, source_target_pairs={{4,0},{8,4},{12,8},{14,12},{10,14},{6,10},{2,6},{0,2},{5,1},{9,5},... | collective-permute-start | bytes 1228808 | tf_op jit(solution)/shard_map/ppermute | solution.py:250
  44.0 10.5 %collective-permute-start.7 = (bf16[2,192,1280]{2,1,0:T(8,128)(2,1)S(1)}, bf16[2,192,1280]{2,1,0:T(8,128)(2,1)S(1)}, u32[]{:S(2)}, u32[]{:S(2)}) collective-permute-start(bf16[2,192,1280]{2,1,0:T(8,128)(2,1)S(1)} %collective-permute-done.first), channel_id=1, source_target_pairs={{0,1},{1,0},{2,3},{3,2},{4,5},{5,4},{6,7},{7,6},{8,9},{9,8},{10,11... | collective-permute-start | bytes 2949128 | tf_op jit(solution)/shard_map/ppermute | solution.py:265
  44.7 7.7 %collective-permute-start.8 = (bf16[160,640]{1,0:T(8,128)(2,1)}, bf16[160,640]{1,0:T(8,128)(2,1)S(1)}, u32[]{:S(2)}, u32[]{:S(2)}) collective-permute-start(bf16[160,640]{1,0:T(8,128)(2,1)} %slice_bitcast_fusion.1), channel_id=1, source_target_pairs={{0,4},{4,8},{8,12},{12,14},{14,10},{10,6},{6,2},{2,0},{1,5},{5,9},... | collective-permute-start | bytes 614408 | tf_op jit(solution)/shard_map/ppermute | solution.py:256
  47.0 7.5 %collective-permute-start.9 = (bf16[160,640]{1,0:T(8,128)(2,1)}, bf16[160,640]{1,0:T(8,128)(2,1)}, u32[]{:S(2)}, u32[]{:S(2)}) collective-permute-start(bf16[160,640]{1,0:T(8,128)(2,1)} %slice_bitcast_fusion), channel_id=1, source_target_pairs={{4,0},{8,4},{12,8},{14,12},{10,14},{6,10},{2,6},{0,2},{5,1},{9,5},... | collective-permute-start | bytes 614408 | tf_op jit(solution)/shard_map/ppermute | solution.py:256
  47.6 14.8 %copy-start.1 = (bf16[384,1280]{1,0:T(8,128)(2,1)S(1)}, bf16[384,1280]{1,0:T(8,128)(2,1)}, u32[]{:S(2)}) copy-start(bf16[384,1280]{1,0:T(8,128)(2,1)} %get-tuple-element.52.grads) | copy-start | bytes 2949124
  47.6 14.8 %copy-start.3 = (bf16[384,1280]{1,0:T(8,128)(2,1)S(1)}, bf16[384,1280]{1,0:T(8,128)(2,1)}, u32[]{:S(2)}) copy-start(bf16[384,1280]{1,0:T(8,128)(2,1)} %get-tuple-element.51.normed) | copy-start | bytes 2949124
  65.1 6.4 %collective-permute-start.10 = (bf16[160,640]{1,0:T(8,128)(2,1)S(1)}, bf16[160,640]{1,0:T(8,128)(2,1)S(1)}, u32[]{:S(2)}, u32[]{:S(2)}) collective-permute-start(bf16[160,640]{1,0:T(8,128)(2,1)S(1)} %dynamic-slice_convert_fusion.1), channel_id=1, source_target_pairs={{0,4},{4,8},{8,12},{12,14},{14,10},{10,6},{6,2},{2,0},{1,5},{5,9},... | collective-permute-start | bytes 614408 | tf_op jit(solution)/shard_map/ppermute | solution.py:307
  65.7 6.1 %collective-permute-start.11 = (bf16[160,640]{1,0:T(8,128)(2,1)S(1)}, bf16[160,640]{1,0:T(8,128)(2,1)S(1)}, u32[]{:S(2)}, u32[]{:S(2)}) collective-permute-start(bf16[160,640]{1,0:T(8,128)(2,1)S(1)} %dynamic-slice_convert_fusion), channel_id=1, source_target_pairs={{4,0},{8,4},{12,8},{14,12},{10,14},{6,10},{2,6},{0,2},{5,1},{9,5},... | collective-permute-start | bytes 614408 | tf_op jit(solution)/shard_map/ppermute | solution.py:306
  71.8 3.4 %collective-permute-start.12 = (bf16[2,384,640]{2,1,0:T(8,128)(2,1)S(1)}, bf16[2,384,640]{2,1,0:T(8,128)(2,1)S(1)}, u32[]{:S(2)}, u32[]{:S(2)}) collective-permute-start(bf16[2,384,640]{2,1,0:T(8,128)(2,1)S(1)} %get-tuple-element.70), channel_id=1, source_target_pairs={{0,1},{1,0},{2,3},{3,2},{4,5},{5,4},{6,7},{7,6},{8,9},{9,8},{10,11... | collective-permute-start | bytes 2949128 | tf_op jit(solution)/shard_map/ppermute | solution.py:289
  72.4 11.9 %collective-permute-start.13 = (bf16[2,160,640]{2,1,0:T(8,128)(2,1)S(1)}, bf16[2,160,640]{2,1,0:T(8,128)(2,1)S(1)}, u32[]{:S(2)}, u32[]{:S(2)}) collective-permute-start(bf16[2,160,640]{2,1,0:T(8,128)(2,1)S(1)} %shard_map.82), channel_id=1, source_target_pairs={{0,4},{4,8},{8,12},{12,14},{14,10},{10,6},{6,2},{2,0},{1,5},{5,9},... | collective-permute-start | bytes 1228808 | tf_op jit(solution)/shard_map/ppermute | solution.py:317
  73.5 11.6 %collective-permute-start.14 = (bf16[2,160,640]{2,1,0:T(8,128)(2,1)S(1)}, bf16[2,160,640]{2,1,0:T(8,128)(2,1)S(1)}, u32[]{:S(2)}, u32[]{:S(2)}) collective-permute-start(bf16[2,160,640]{2,1,0:T(8,128)(2,1)S(1)} %shard_map.83), channel_id=1, source_target_pairs={{4,0},{8,4},{12,8},{14,12},{10,14},{6,10},{2,6},{0,2},{5,1},{9,5},... | collective-permute-start | bytes 1228808 | tf_op jit(solution)/shard_map/ppermute | solution.py:317
  85.2 13.5 %collective-permute-start.17 = (bf16[384,640]{1,0:T(8,128)(2,1)S(1)}, bf16[384,640]{1,0:T(8,128)(2,1)S(1)}, u32[]{:S(2)}, u32[]{:S(2)}) collective-permute-start(bf16[384,640]{1,0:T(8,128)(2,1)S(1)} %shard_map.84), channel_id=1, source_target_pairs={{0,16},{16,0},{1,17},{17,1},{2,18},{18,2},{3,19},{19,3},{4,20},{20... | collective-permute-start | bytes 1474568 | tf_op jit(solution)/shard_map/ppermute | solution.py:321
  87.3 10.6 %collective-permute-start.15 = (bf16[2,160,640]{2,1,0:T(8,128)(2,1)S(1)}, bf16[2,160,640]{2,1,0:T(8,128)(2,1)S(1)}, u32[]{:S(2)}, u32[]{:S(2)}) collective-permute-start(bf16[2,160,640]{2,1,0:T(8,128)(2,1)S(1)} %shard_map.85), channel_id=1, source_target_pairs={{0,4},{4,8},{8,12},{12,14},{14,10},{10,6},{6,2},{2,0},{1,5},{5,9},... | collective-permute-start | bytes 1228808 | tf_op jit(solution)/shard_map/ppermute | solution.py:317
  88.4 10.3 %collective-permute-start.16 = (bf16[2,160,640]{2,1,0:T(8,128)(2,1)S(1)}, bf16[2,160,640]{2,1,0:T(8,128)(2,1)S(1)}, u32[]{:S(2)}, u32[]{:S(2)}) collective-permute-start(bf16[2,160,640]{2,1,0:T(8,128)(2,1)S(1)} %shard_map.86), channel_id=1, source_target_pairs={{4,0},{8,4},{12,8},{14,12},{10,14},{6,10},{2,6},{0,2},{5,1},{9,5},... | collective-permute-start | bytes 1228808 | tf_op jit(solution)/shard_map/ppermute | solution.py:317
  99.3 9.3 %collective-permute-start.19 = (bf16[2,160,640]{2,1,0:T(8,128)(2,1)S(1)}, bf16[2,160,640]{2,1,0:T(8,128)(2,1)S(1)}, u32[]{:S(2)}, u32[]{:S(2)}) collective-permute-start(bf16[2,160,640]{2,1,0:T(8,128)(2,1)S(1)} %shard_map.89), channel_id=1, source_target_pairs={{0,4},{4,8},{8,12},{12,14},{14,10},{10,6},{6,2},{2,0},{1,5},{5,9},... | collective-permute-start | bytes 1228808 | tf_op jit(solution)/shard_map/ppermute | solution.py:317
  100.5 9.1 %collective-permute-start.20 = (bf16[2,160,640]{2,1,0:T(8,128)(2,1)S(1)}, bf16[2,160,640]{2,1,0:T(8,128)(2,1)S(1)}, u32[]{:S(2)}, u32[]{:S(2)}) collective-permute-start(bf16[2,160,640]{2,1,0:T(8,128)(2,1)S(1)} %shard_map.90), channel_id=1, source_target_pairs={{4,0},{8,4},{12,8},{14,12},{10,14},{6,10},{2,6},{0,2},{5,1},{9,5},... | collective-permute-start | bytes 1228808 | tf_op jit(solution)/shard_map/ppermute | solution.py:317
  110.3 5.8 %collective-permute-start.21 = (bf16[160,640]{1,0:T(8,128)(2,1)S(1)}, bf16[160,640]{1,0:T(8,128)(2,1)S(1)}, u32[]{:S(2)}, u32[]{:S(2)}) collective-permute-start(bf16[160,640]{1,0:T(8,128)(2,1)S(1)} %get-tuple-element.83), channel_id=1, source_target_pairs={{0,16},{16,0},{1,17},{17,1},{2,18},{18,2},{3,19},{19,3},{4,20},{20... | collective-permute-start | bytes 614408 | tf_op jit(solution)/shard_map/ppermute | solution.py:335
  112.5 1.5 %collective-permute-start.18 = (f32[384,2]{1,0:T(8,128)S(1)}, f32[384,2]{1,0:T(8,128)S(1)}, u32[]{:S(2)}, u32[]{:S(2)}) collective-permute-start(f32[384,2]{1,0:T(8,128)S(1)} %get-tuple-element.79.sums), channel_id=1, source_target_pairs={{0,1},{1,0},{2,3},{3,2},{4,5},{5,4},{6,7},{7,6},{8,9},{9,8},{10,11... | collective-permute-start | bytes 9224 | tf_op jit(solution)/shard_map/ppermute | solution.py:347
  (11 other events, 39.6 us)

commit v6 on v3

v6 whole, which is shorter than its diff:
```python
import functools

import jax
import jax.numpy as jnp
from jax import lax
from jax.experimental import pallas as pl
from jax.experimental.pallas import tpu as pltpu
from jax.sharding import PartitionSpec as P

BF16, F32 = jnp.bfloat16, jnp.float32
VMEM = pl.BlockSpec(memory_space=pltpu.VMEM)
ANY = pl.BlockSpec(memory_space=pl.ANY)
SMEM = pl.BlockSpec(memory_space=pltpu.SMEM)


def shape(dims, kind):
    return jax.ShapeDtypeStruct(dims, kind)


def call(kernel, ins, out_shape, scratch=(), vmem=16, left=(), cost=1, ties=()):
    count = len(ins)

    def body(*refs):
        kernel(*refs[:count], *refs[count + len(ties) :])

    return pl.pallas_call(
        body if ties else kernel,
        out_shape=out_shape,
        in_specs=[
            SMEM if x.dtype == jnp.int32 else ANY if i in left else VMEM
            for i, x in enumerate(ins)
        ]
        + [ANY] * len(ties),
        out_specs=jax.tree.map(lambda _: VMEM, out_shape),
        scratch_shapes=list(scratch),
        compiler_params=pltpu.CompilerParams(vmem_limit_bytes=vmem << 20),
        cost_estimate=pl.CostEstimate(flops=1, bytes_accessed=cost, transcendentals=0),
    )(*ins, *ties)


def hold(array, *ties):
    return pl.pallas_call(
        lambda *refs: None,
        out_shape=shape(array.shape, array.dtype),
        in_specs=[ANY] * (1 + len(ties)),
        out_specs=ANY,
        input_output_aliases={0: 0},
        cost_estimate=pl.CostEstimate(flops=1, bytes_accessed=1, transcendentals=0),
    )(array, *ties)


def dot(left, right, left_dim=1, right_dim=0):
    return lax.dot_general(
        left, right, (((left_dim,), (right_dim,)), ((), ())), preferred_element_type=F32
    )


def gelu_slope(values):
    return (
        0.5 * (1.0 + lax.erf(values * 0.7071067811865476))
        + values * jnp.exp(-0.5 * values * values) * 0.3989422804014327
    )


def norm_kernel(meta, lengths, frames_from, grads_from, gain, *refs):
    normed, grads, pass_normed, pass_grads, stats, frames, out_grad, sems = refs
    copies = [
        pltpu.make_async_copy(grads_from, out_grad, sems.at[0]),
        pltpu.make_async_copy(frames_from, frames, sems.at[1]),
    ]
    for copy in copies:
        copy.start()
    half = pass_normed.shape[0]
    rows = pl.ds(pl.multiple_of(meta[1] * half, half), half)
    keep = lax.broadcasted_iota(jnp.int32, (frames.shape[0], 1), 0) < lengths[meta[0]]
    copies[0].wait()
    grads[...] = jnp.where(keep, out_grad[...].astype(F32), 0.0).astype(BF16)
    pass_grads[...] = grads[rows, :]
    copies[1].wait()
    values = frames[...].astype(F32)
    centre = jnp.mean(values, axis=-1, keepdims=True)
    shifted = values - centre
    variance = jnp.mean(shifted * shifted, axis=-1, keepdims=True)
    inv_std = lax.rsqrt(variance + 1e-05)
    normed[...] = (shifted * inv_std * gain[...][None]).astype(BF16)
    pass_normed[...] = normed[rows, :]
    stats[:, 0:1] = centre
    stats[:, 1:2] = inv_std


def back_through(normed, grads, up, down, d_pre, partial):
    pre_act = dot(normed[...], up[...])
    d_act = dot(grads[...], down[...])
    d_pre[...] = (d_act * gelu_slope(pre_act)).astype(BF16)
    partial[...] = dot(normed[...], d_pre[...], 0, 0)


def other_kernel(index, *refs):
    d_pre, partial, up, down, normed, grads, sems = refs[-7:]
    halves, blocks = refs[:4], refs[4:-7]
    half, depth = halves[0].shape[0], blocks[-1].shape[0]
    count = len(blocks) - 1
    copies = []

    def start(source, target):
        copies.append(pltpu.make_async_copy(source, target, sems.at[len(copies)]))
        copies[-1].start()

    for i in range(count):
        rows = pl.ds(pl.multiple_of(index[i] * depth, depth), depth)
        pair = (blocks[i].at[0], blocks[i].at[1]) if i < count - 1 else blocks[-2:]
        start(pair[0], up.at[rows])
        start(pair[1], down.at[rows])
    for i in range(2):
        start(halves[2 * i], normed.at[pl.ds(i * half, half)])
        start(halves[2 * i + 1], grads.at[pl.ds(i * half, half)])
    for copy in copies:
        copy.wait()
    back_through(normed, grads, up, down, d_pre, partial)


def halves_kernel(up, down, up_half, down_half, sems):
    copies = [
        pltpu.make_async_copy(up.at[0], up_half, sems.at[0]),
        pltpu.make_async_copy(down.at[1], down_half, sems.at[1]),
    ]
    for copy in copies:
        copy.start()
    for copy in copies:
        copy.wait()


def own_kernel(normed, grads, up, down, d_pre, partial):
    back_through(normed, grads, up, down, d_pre, partial)


def d_norm_kernel(meta, d_pre_own, d_pre_other, up, keep, send_own, send_other):
    core = meta[1]
    rows, width = keep.shape[1:]
    mine = up[pl.ds(pl.multiple_of(core * width, width), width), :]
    theirs = up[pl.ds(pl.multiple_of((1 - core) * width, width), width), :]
    keep[0] = dot(d_pre_own[...], mine, 1, 1)
    keep[1] = dot(d_pre_other[...], mine, 1, 1)
    send_own[...] = dot(d_pre_own[...], theirs, 1, 1).astype(BF16)
    sent = dot(d_pre_other[...], theirs, 1, 1).astype(BF16)
    send_other[rows // 2 :, :] = sent[: rows // 2]
    send_other[: rows // 2, :] = sent[rows // 2 :]


def over_kernel(meta, keep, came, over):
    half = over.shape[0] // 2
    for i in range(2):
        at = lax.rem(i + meta[1], 2) * half
        rows = slice(i * half, (i + 1) * half)
        value = keep[1, rows, :] + came[rows, :].astype(F32)
        over[pl.ds(pl.multiple_of(at, half), half), :] = value.astype(BF16)


def own_columns(meta, ref, width):
    return ref[:, pl.ds(pl.multiple_of(meta[1] * width, width), width)]


def scale_kernel(meta, keep, came, back, frames, gain, stats, scaled, sums):
    width = scaled.shape[1]
    d_norm = keep[0] + came[...].astype(F32) + back[...].astype(F32)
    value = d_norm * own_columns(meta, gain, width)
    scaled[...] = value
    rows = own_columns(meta, frames, width).astype(F32)
    centred = (rows - stats[:, 0:1]) * stats[:, 1:2]
    sums[:, 0:1] = jnp.sum(value, axis=-1, keepdims=True)
    sums[:, 1:2] = jnp.sum(value * centred, axis=-1, keepdims=True)


def input_kernel(meta, scaled, sums, came, frames, grads, stats, out):
    width = scaled.shape[1]
    means = (sums[...] + came[...]) * (0.5 / width)
    rows = own_columns(meta, frames, width).astype(F32)
    inv_std = stats[:, 1:2]
    centred = (rows - stats[:, 0:1]) * inv_std
    value = inv_std * (scaled[...] - means[:, 0:1] - centred * means[:, 1:2])
    out[...] = (own_columns(meta, grads, width).astype(F32) + value).astype(BF16)


def hop_kernel(places, index, partial, *refs):
    outs = refs[len(refs) - len(places) :]
    came = iter(refs)
    depth = outs[0].shape[0]
    for (at, summed), out in zip(places, outs):
        value = partial[pl.ds(pl.multiple_of(index[at] * depth, depth), depth), :]
        if summed:
            value = value + next(came)[...].astype(F32)
        out[...] = value.astype(BF16)


def total_kernel(index, partial, up, down, total):
    depth = total.shape[0]
    rows = pl.ds(pl.multiple_of(index[0] * depth, depth), depth)
    value = partial[rows, :] + up[...].astype(F32) + down[...].astype(F32)
    total[...] = value.astype(total.dtype)


def join_kernel(meta, index, partial, up, down, passed, out):
    depth, width = up.shape
    side = meta[2]
    rows = pl.ds(pl.multiple_of(index[0] * depth, depth), depth)
    value = partial[rows, :] + up[...].astype(F32) + down[...].astype(F32)
    out[:, pl.ds(pl.multiple_of(side * width, width), width)] = value
    other = pl.ds(pl.multiple_of((1 - side) * width, width), width)
    out[:, other] = passed[...].astype(F32)


def place_kernel(meta, own, passed, out):
    width = own.shape[1]
    side = meta[2]
    out[:, pl.ds(pl.multiple_of(side * width, width), width)] = own[...]
    other = pl.ds(pl.multiple_of((1 - side) * width, width), width)
    out[:, other] = passed[...].astype(F32)


def ring_member(place, count):
    place = place % count
    return jnp.where(place < count // 2, 2 * place, 2 * (count - 1 - place) + 1)


def shards(frames, out_grad, ln_gain, w_up, w_down, lengths):
    peers = lax.axis_size("gx")
    half = peers // 2
    own = lax.axis_index("gx")
    side = lax.axis_index("groups")
    core = lax.axis_index("gy")
    frame_len, width = frames.shape[1:]
    depth, hidden = w_up.shape
    quarter = hidden // 2
    half_width = width // 2
    half_rows = frame_len // 2
    ringed = peers <= 16 and peers % 2 == 0 and depth % 16 == 0

    order = list(range(0, peers, 2)) + list(range(peers - 1, 0, -2))
    ahead = [(order[i], order[(i + 1) % peers]) for i in range(peers)]
    behind = [(b, a) for a, b in ahead]
    place = jnp.where(own % 2 == 0, own // 2, peers - 1 - own // 2)
    swap = [(0, 1), (1, 0)]

    mine = [lax.dynamic_slice_in_dim(w, side * quarter, quarter, 1) for w in (w_up, w_down)]
    meta = jnp.stack([own, core, side]).astype(jnp.int32)
    frames, out_grad = frames[0], out_grad[0]

    rows_of, half_of = shape((frame_len, width), BF16), shape((half_rows, width), BF16)
    def norm(*ties):
        normed, grads, *passing, stats = call(
            norm_kernel,
            (meta, lengths, frames, out_grad, ln_gain),
            (rows_of, rows_of, half_of, half_of, shape((frame_len, 2), F32)),
            [pltpu.VMEM((frame_len, width), BF16)] * 2 + [pltpu.SemaphoreType.DMA((2,))],
            left=(2, 3),
            vmem=40,
            ties=ties,
        )
        return normed, grads, [lax.ppermute(part, "groups", swap) for part in passing], stats

    if ringed:
        pair = jnp.stack(mine)
        blocks = {0: pair}
        up, down = pair, pair
        for step in range(1, half):
            up, down = lax.ppermute(up, "gx", ahead), lax.ppermute(down, "gx", behind)
            blocks[-step], blocks[step] = up, down
            if step == 1:
                normed, grads, first, stats = norm(up)
        block_of = shape((depth, quarter), BF16)
        up, down = call(
            halves_kernel,
            (up, down),
            (block_of, block_of),
            [pltpu.SemaphoreType.DMA((2,))],
            left=(0, 1),
        )
        steps = list(blocks) + [half]
        index = jnp.stack([ring_member(place + step + peers, peers) for step in steps])
        blocks = [*blocks.values(), lax.ppermute(up, "gx", ahead), lax.ppermute(down, "gx", behind)]
    else:
        normed, grads, first, stats = norm()
        blocks = [lax.all_gather(w, "gx", axis=0, tiled=True) for w in mine]
        index = jnp.zeros((1,), jnp.int32)
    index = index.astype(jnp.int32)
    second = [lax.ppermute(part, "gy", swap) for part in first]

    d_pre_of, partial_of = shape((frame_len, quarter), BF16), shape((width, quarter), F32)
    weight = shape((width, quarter), BF16)
    d_pre_other, partial_other, full_up, full_down = call(
        other_kernel,
        (index, *first, *second, *blocks),
        (d_pre_of, partial_of, weight, weight),
        [pltpu.VMEM((frame_len, width), BF16)] * 2
        + [pltpu.SemaphoreType.DMA((2 * len(blocks) + 4,))],
        left=range(1, len(blocks) + 5),
    )
    d_pre_own, partial_own = call(
        own_kernel, (normed, grads, full_up, full_down), (d_pre_of, partial_of)
    )
    partial = [partial_own, partial_other]

    half_rows_of = shape((frame_len, half_width), BF16)

    def own_d_norm(*ties):
        return call(
            d_norm_kernel,
            (meta, d_pre_own, d_pre_other, full_up),
            (shape((2, frame_len, half_width), F32), half_rows_of, half_rows_of),
            ties=ties,
        )

    def over_cores(keep, came, *ties):
        return call(over_kernel, (meta, keep, came), half_rows_of, ties=ties)

    if ringed:
        place_of = {step: i for i, step in enumerate(steps)}
        place_of[-half] = place_of[half]
        came = [{}, {}]

        def hop(i, turn, *ties):
            ways = [(half - turn - (i == 1), ahead), (turn + (i == 0) - half, behind)]
            ways = [way for way in ways if way[0] != 0]
            kept = [came[i][pairs[0]] for _, pairs in ways if pairs[0] in came[i]]
            places = [(place_of[step], pairs[0] in came[i]) for step, pairs in ways]
            blocks = call(
                functools.partial(hop_kernel, tuple(places)),
                (index, partial[i], *kept),
                [block_of] * len(ways),
                ties=ties,
            )
            for block, (_, pairs) in zip(blocks, ways):
                came[i][pairs[0]] = lax.ppermute(block, "gx", pairs)
            return blocks[0]

        hop(1, 0)
        tie = hop(0, 0)
        tie = hop(1, 1, tie)
        keep, send_own, send_other = own_d_norm(tie)
        tie = hop(0, 1, tie)
        send_other = hold(send_other, tie)
        tie = hop(1, 2, tie)
        over = over_cores(keep, lax.ppermute(send_other, "gy", swap), tie)
        tie = hop(0, 2, over)
        back = lax.ppermute(over, "groups", swap)
        send_own = hold(send_own, tie)
        for turn in range(3, half):
            tie = hop(0, turn, hop(1, turn, tie))
        tail = (tie,)
        one, two = ([came[i][pairs[0]] for pairs in (ahead, behind)] for i in range(2))
        passing = call(total_kernel, (index, partial[1], *two), block_of, ties=tail)
        tail = (passing,)
        passed = lax.ppermute(passing, "groups", swap)
        up_grad = call(
            join_kernel,
            (meta, index, partial[0], *one, passed),
            shape((depth, hidden), F32),
        )
    else:
        tail = ()
        keep, send_own, send_other = own_d_norm()
        over = over_cores(keep, lax.ppermute(send_other, "gy", swap))
        back = lax.ppermute(over, "groups", swap)
        total = [lax.psum_scatter(p, "gx", scatter_dimension=0, tiled=True) for p in partial]
        passed = lax.ppermute(total[1].astype(BF16), "groups", swap)
        up_grad = call(place_kernel, (meta, total[0], passed), shape((depth, hidden), F32))
    came = lax.ppermute(send_own, "gy", swap)

    gain = ln_gain[None]
    scaled, sums = call(
        scale_kernel,
        (meta, keep, came, back, frames, gain, stats),
        (shape((frame_len, half_width), F32), shape((frame_len, 2), F32)),
        ties=tail,
    )
    input_grad = call(
        input_kernel,
        (meta, scaled, sums, lax.ppermute(sums, "gy", swap), frames, grads, stats),
        shape((frame_len, half_width), BF16),
    )
    return (input_grad[None], up_grad)


def solution(mesh):
    placed = (
        P(("groups", "gx"), None, None),
        P(("groups", "gx"), None, None),
        P(),
        P("gx", "gy"),
        P("gx", "gy"),
        P("groups"),
    )
    return jax.shard_map(
        shards,
        mesh=mesh,
        in_specs=placed,
        out_specs=(P(("groups", "gx"), None, "gy"), P(("groups", "gx"), "gy")),
        check_vma=False,
    )
```

time: 143 us -> 129 us (0.902)
  waiting for transfers between devices: 73 us -> 50.2 us
  Pallas kernels: 16.5 us -> 29.8 us
  local copies, waits for them, and re-layouts: 12.6 us -> 20.8 us
  starting transfers between devices: 34.1 us -> 26.9 us
  other arithmetic: 5.65 us -> 0.12 us
    ppermute x32 -> x29, waiting for transfers between devices: 72.5 us -> 50.2 us  [the longest x2 16.8 us: norm(): lax.ppermute(part, 'groups', swap)]
    pallas_call x7 -> x20, Pallas kernels: 16.5 us -> 29.8 us  [the longest x18 29.8 us: call(): pl.pallas_call(body if ties else kernel, out_shape=out_shape, in_specs=[S...]
    unnamed x28 -> x72, local copies, waits for them, and re-layouts: 9.41 us -> 19.6 us
    ppermute x32 -> x29, starting transfers between devices: 32.6 us -> 25.3 us  [the longest x14 13.4 us: hop(): came[i][pairs[0]] = lax.ppermute(block, 'gx', pairs)]
    convert_element_type x9 -> x0, other arithmetic: 2.6 us -> none  [the longest x8 1.84 us: shards(): way[i] = lax.ppermute(value.astype(BF16), 'gx', pairs)]
    dynamic_slice x2 -> x0, local copies, waits for them, and re-layouts: 2.31 us -> none  [the longest x1 1.24 us: shards(): length = lax.dynamic_index_in_dim(lengths, own, 0, keepdims=False)]
  transfers between devices with their start and end apart: 34 -> 31, of which waited for: 16 -> 14; matrix products, arithmetic and copies ran while one was open for 4% -> 0% of each run, Pallas kernels for 5% -> 13%
where the time goes in v6:
time: 129 us
  waiting for transfers between devices  50.2 us (39%)
  Pallas kernels  29.8 us (23%)
  starting transfers between devices  26.9 us (21%)
  local copies, waits for them, and re-layouts  20.8 us (16%)
    pallas_call x18, Pallas kernels, call(): pl.pallas_call(body if ties else kernel, out_shape=out_shape, in_specs=[S...  29.8 us
    unnamed x72, local copies, waits for them, and re-layouts  19.6 us
    ppermute x2, waiting for transfers between devices, norm(): lax.ppermute(part, 'groups', swap)  16.8 us
    ppermute x14, waiting for transfers between devices, hop(): came[i][pairs[0]] = lax.ppermute(block, 'gx', pairs)  13.7 us
    ppermute x14, starting transfers between devices, hop(): came[i][pairs[0]] = lax.ppermute(block, 'gx', pairs)  13.4 us
    ppermute x6, waiting for transfers between devices, shards(): up, down = (lax.ppermute(up, 'gx', ahead), lax.ppermute(down, 'gx', behind))  9.41 us
    ppermute x6, starting transfers between devices, shards(): up, down = (lax.ppermute(up, 'gx', ahead), lax.ppermute(down, 'gx', behind))  7.14 us
    ppermute x1, waiting for transfers between devices, shards(): lax.ppermute(up, 'gx', ahead)  5.57 us
  transfers between devices with their start and end apart: 31, of which 14 were waited for; matrix products, arithmetic and copies ran while one was open for 0% of the time, Pallas kernels for 13%

profile of v6, /device:TPU:0, one launch (start us, length us, event | category | flops | bytes accessed | tf_op | source)
XLA Modules:
  0.0 128.8 jit_solution(15520657021823633519)
XLA Ops:
  1.9 3.1 %collective-permute-start = (bf16[2,160,640]{2,1,0:T(8,128)(2,1)S(1)}, bf16[2,160,640]{2,1,0:T(8,128)(2,1)S(1)}, u32[]{:S(2)}, u32[]{:S(2)}) collective-permute-start(bf16[2,160,640]{2,1,0:T(8,128)(2,1)S(1)} %pad_maximum_fusion.refs_4_), channel_id=1, source_target_pairs={{0,4},{4,8},{8,12},{12,14},{14,10},{10,6},{6,2},{2,0},{1,5},{5,9},... | collective-permute-start | bytes 1228808 | tf_op jit(solution)/shard_map/ppermute | solution.py:266
  4.9 9.4 %collective-permute-done.refs_5_ = bf16[2,160,640]{2,1,0:T(8,128)(2,1)S(1)} collective-permute-done((bf16[2,160,640]{2,1,0:T(8,128)(2,1)S(1)}, bf16[2,160,640]{2,1,0:T(8,128)(2,1)S(1)}, u32[]{:S(2)}, u32[]{:S(2)}) %collective-permute-start) | collective-permute-done | bytes 409632 | tf_op jit(solution)/shard_map/ppermute | solution.py:266
  14.3 1.8 %collective-permute-start.6 = (bf16[2,160,640]{2,1,0:T(8,128)(2,1)S(1)}, bf16[2,160,640]{2,1,0:T(8,128)(2,1)S(1)}, u32[]{:S(2)}, u32[]{:S(2)}) collective-permute-start(bf16[2,160,640]{2,1,0:T(8,128)(2,1)S(1)} %collective-permute-done.refs_5_), channel_id=1, source_target_pairs={{0,4},{4,8},{8,12},{12,14},{14,10},{10,6},{6,2},{2,0},{1,5},{5,9},... | collective-permute-start | bytes 1228808 | tf_op jit(solution)/shard_map/ppermute | solution.py:266
  19.0 2.1 %shard_map.77 = (bf16[384,1280]{1,0:T(8,128)(2,1)S(1)}, bf16[384,1280]{1,0:T(8,128)(2,1)S(1)}, bf16[192,1280]{1,0:T(8,128)(2,1)S(1)}, bf16[192,1280]{1,0:T(8,128)(2,1)S(1)}, f32[384,2]{1,0:T(8,128)S(1)}) custom-call(s32[3]{0:T(128)S(1)} %pad_add_fusion.refs_0_.meta, s32[8]{0:T(128)S(1)} %copy-done.31, bf16[384,1280]{1,0:T(8,128)(2,1)S(1)} %bitcast.18, ...), custom_call_target="tpu_custom_call" | custom-call | flops 1 | bytes 1 | tf_op jit(solution)/shard_map/pallas_call | solution.py:26
  23.7 1.7 %collective-permute-start.1 = (bf16[192,1280]{1,0:T(8,128)(2,1)S(1)}, bf16[192,1280]{1,0:T(8,128)(2,1)S(1)}, u32[]{:S(2)}, u32[]{:S(2)}) collective-permute-start(bf16[192,1280]{1,0:T(8,128)(2,1)S(1)} %get-tuple-element.34), channel_id=1, source_target_pairs={{0,16},{16,0},{1,17},{17,1},{2,18},{18,2},{3,19},{19,3},{4,20},{20... | collective-permute-start | bytes 1474568 | tf_op jit(solution)/shard_map/ppermute | solution.py:259
  25.7 1.8 %collective-permute-start.8 = (bf16[2,160,640]{2,1,0:T(8,128)(2,1)S(1)}, bf16[2,160,640]{2,1,0:T(8,128)(2,1)S(1)}, u32[]{:S(2)}, u32[]{:S(2)}) collective-permute-start(bf16[2,160,640]{2,1,0:T(8,128)(2,1)S(1)} %collective-permute-done.6.refs_7_), channel_id=1, source_target_pairs={{0,4},{4,8},{8,12},{12,14},{14,10},{10,6},{6,2},{2,0},{1,5},{5,9},... | collective-permute-start | bytes 1228808 | tf_op jit(solution)/shard_map/ppermute | solution.py:266
  29.3 8.6 %collective-permute-done.1.refs_0_ = bf16[192,1280]{1,0:T(8,128)(2,1)S(1)} collective-permute-done((bf16[192,1280]{1,0:T(8,128)(2,1)S(1)}, bf16[192,1280]{1,0:T(8,128)(2,1)S(1)}, u32[]{:S(2)}, u32[]{:S(2)}) %collective-permute-start.1) | collective-permute-done | bytes 491552 | tf_op jit(solution)/shard_map/ppermute | solution.py:259
  37.9 8.2 %collective-permute-done.2.refs_1_ = bf16[192,1280]{1,0:T(8,128)(2,1)S(1)} collective-permute-done((bf16[192,1280]{1,0:T(8,128)(2,1)S(1)}, bf16[192,1280]{1,0:T(8,128)(2,1)S(1)}, u32[]{:S(2)}, u32[]{:S(2)}) %collective-permute-start.2) | collective-permute-done | bytes 491552 | tf_op jit(solution)/shard_map/ppermute | solution.py:259
  49.6 5.6 %collective-permute-done.10.refs_11_ = bf16[160,640]{1,0:T(8,128)(2,1)S(1)} collective-permute-done((bf16[160,640]{1,0:T(8,128)(2,1)}, bf16[160,640]{1,0:T(8,128)(2,1)S(1)}, u32[]{:S(2)}, u32[]{:S(2)}) %collective-permute-start.10) | collective-permute-done | bytes 204832 | tf_op jit(solution)/shard_map/ppermute | solution.py:280
  59.5 9.4 %shard_map.79 = (bf16[384,640]{1,0:T(8,128)(2,1)S(1)}, f32[1280,640]{1,0:T(8,128)S(1)}, bf16[1280,640]{1,0:T(8,128)(2,1)S(1)}, bf16[1280,640]{1,0:T(8,128)(2,1)S(1)}) custom-call(s32[8]{0:T(128)S(1)} %stack.63.index.refs_0_, bf16[192,1280]{1,0:T(8,128)(2,1)S(1)} %collective-permute-done.1.refs_0_, bf16[192,1280]{1,0:T(8,128)(2,1)S(1)} %collective-permute-done.2.refs_1_, ...), custom_call_target="tpu_custom_call" | custom-call | flops 1 | bytes 1 | tf_op jit(solution)/shard_map/pallas_call | solution.py:26
  69.5 1.6 %collective-permute-start.12 = (bf16[160,640]{1,0:T(8,128)(2,1)S(1)}, bf16[160,640]{1,0:T(8,128)(2,1)S(1)}, u32[]{:S(2)}, u32[]{:S(2)}) collective-permute-start(bf16[160,640]{1,0:T(8,128)(2,1)S(1)} %get-tuple-element.43), channel_id=1, source_target_pairs={{0,4},{4,8},{8,12},{12,14},{14,10},{10,6},{6,2},{2,0},{1,5},{5,9},... | collective-permute-start | bytes 614408 | tf_op jit(solution)/shard_map/ppermute | solution.py:333
  71.6 2.7 %shard_map.80 = (bf16[384,640]{1,0:T(8,128)(2,1)S(1)}, f32[1280,640]{1,0:T(8,128)S(1)}) custom-call(bf16[384,1280]{1,0:T(8,128)(2,1)S(1)} %copy-done.13, bf16[384,1280]{1,0:T(8,128)(2,1)S(1)} %copy-done.9, bf16[1280,640]{1,0:T(8,128)(2,1)S(1)} %get-tuple-element.38.up.refs_3_, bf16[1280,640]{1,0:T(8,128)(2,1)S(1)} %get-tuple-element.39.down), custom_call_target="tpu_custom_call" | custom-call | flops 1 | bytes 1 | tf_op jit(solution)/shard_map/pallas_call | solution.py:26
  74.9 1.6 %collective-permute-start.14 = (bf16[160,640]{1,0:T(8,128)(2,1)S(1)}, bf16[160,640]{1,0:T(8,128)(2,1)S(1)}, u32[]{:S(2)}, u32[]{:S(2)}) collective-permute-start(bf16[160,640]{1,0:T(8,128)(2,1)S(1)} %get-tuple-element.46.refs_4_), channel_id=1, source_target_pairs={{0,4},{4,8},{8,12},{12,14},{14,10},{10,6},{6,2},{2,0},{1,5},{5,9},... | collective-permute-start | bytes 614408 | tf_op jit(solution)/shard_map/ppermute | solution.py:333
  77.9 2.5 %shard_map.84 = (f32[2,384,640]{2,1,0:T(8,128)S(1)}, bf16[384,640]{1,0:T(8,128)(2,1)S(1)}, bf16[384,640]{1,0:T(8,128)(2,1)S(1)}) custom-call(s32[3]{0:T(128)S(1)} %pad_add_fusion.refs_0_.meta, bf16[384,640]{1,0:T(8,128)(2,1)S(1)} %get-tuple-element.40.refs_1_, bf16[384,640]{1,0:T(8,128)(2,1)S(1)} %get-tuple-element.41.refs_2_, ...), custom_call_target="tpu_custom_call" | custom-call | flops 1 | bytes 1 | tf_op jit(solution)/shard_map/pallas_call | solution.py:26
  84.7 1.6 %collective-permute-start.19 = (bf16[160,640]{1,0:T(8,128)(2,1)S(1)}, bf16[160,640]{1,0:T(8,128)(2,1)S(1)}, u32[]{:S(2)}, u32[]{:S(2)}) collective-permute-start(bf16[160,640]{1,0:T(8,128)(2,1)S(1)} %get-tuple-element.47.refs_4_), channel_id=1, source_target_pairs={{0,4},{4,8},{8,12},{12,14},{14,10},{10,6},{6,2},{2,0},{1,5},{5,9},... | collective-permute-start | bytes 614408 | tf_op jit(solution)/shard_map/ppermute | solution.py:333
  88.7 3.8 %collective-permute-done.19.refs_2_ = bf16[160,640]{1,0:T(8,128)(2,1)S(1)} collective-permute-done((bf16[160,640]{1,0:T(8,128)(2,1)S(1)}, bf16[160,640]{1,0:T(8,128)(2,1)S(1)}, u32[]{:S(2)}, u32[]{:S(2)}) %collective-permute-start.19) | collective-permute-done | bytes 204832 | tf_op jit(solution)/shard_map/ppermute | solution.py:333
  92.6 1.8 %collective-permute-done.20.refs_3_ = bf16[160,640]{1,0:T(8,128)(2,1)S(1)} collective-permute-done((bf16[160,640]{1,0:T(8,128)(2,1)}, bf16[160,640]{1,0:T(8,128)(2,1)S(1)}, u32[]{:S(2)}, u32[]{:S(2)}) %collective-permute-start.20) | collective-permute-done | bytes 204832 | tf_op jit(solution)/shard_map/ppermute | solution.py:333
  94.4 1.9 %copy-done.1 = f32[1280,640]{1,0:T(8,128)S(1)} copy-done((f32[1280,640]{1,0:T(8,128)S(1)}, f32[1280,640]{1,0:T(8,128)}, u32[]{:S(2)}) %copy-start.1) | copy-done | bytes 3276824
  103.3 1.6 %collective-permute-start.26 = (bf16[160,640]{1,0:T(8,128)(2,1)}, bf16[160,640]{1,0:T(8,128)(2,1)S(1)}, u32[]{:S(2)}, u32[]{:S(2)}) collective-permute-start(bf16[160,640]{1,0:T(8,128)(2,1)} %copy-done.17), channel_id=1, source_target_pairs={{0,4},{4,8},{8,12},{12,14},{14,10},{10,6},{6,2},{2,0},{1,5},{5,9},... | collective-permute-start | bytes 614408 | tf_op jit(solution)/shard_map/ppermute | solution.py:333
  106.4 1.9 %copy-done.2 = f32[1280,640]{1,0:T(8,128)S(1)} copy-done((f32[1280,640]{1,0:T(8,128)S(1)}, f32[1280,640]{1,0:T(8,128)}, u32[]{:S(2)}) %copy-start.2) | copy-done | bytes 3276824
  112.5 2.6 %collective-permute-done.23.refs_2_ = bf16[160,640]{1,0:T(8,128)(2,1)S(1)} collective-permute-done((bf16[160,640]{1,0:T(8,128)(2,1)S(1)}, bf16[160,640]{1,0:T(8,128)(2,1)S(1)}, u32[]{:S(2)}, u32[]{:S(2)}) %collective-permute-start.23) | collective-permute-done | bytes 204832 | tf_op jit(solution)/shard_map/ppermute | solution.py:333
  115.1 3.2 %collective-permute-done.25.refs_3_ = bf16[160,640]{1,0:T(8,128)(2,1)S(1)} collective-permute-done((bf16[160,640]{1,0:T(8,128)(2,1)S(1)}, bf16[160,640]{1,0:T(8,128)(2,1)S(1)}, u32[]{:S(2)}, u32[]{:S(2)}) %collective-permute-start.25) | collective-permute-done | bytes 204832 | tf_op jit(solution)/shard_map/ppermute | solution.py:333
  121.5 3.3 %collective-permute-done.30.passed = bf16[160,640]{1,0:T(8,128)(2,1)S(1)} collective-permute-done((bf16[160,640]{1,0:T(8,128)(2,1)S(1)}, bf16[160,640]{1,0:T(8,128)(2,1)S(1)}, u32[]{:S(2)}, u32[]{:S(2)}) %collective-permute-start.30) | collective-permute-done | bytes 204832 | tf_op jit(solution)/shard_map/ppermute | solution.py:353
  126.9 1.9 %shard_map.95 = bf16[384,640]{1,0:T(8,128)(2,1)} custom-call(s32[3]{0:T(128)S(1)} %pad_add_fusion.refs_0_.meta, f32[384,640]{1,0:T(8,128)S(1)} %get-tuple-element.59.scaled, f32[384,2]{1,0:T(8,128)S(1)} %get-tuple-element.60.sums, f32[384,2]{1,0:T(8,128)S(1)} %collective-permute-done.27.came, bf16[384,1280]{1,0:T(8,128)(2,1)S(1)} %bitcast.20, ...), custom_call_target="tpu_custom_call" | custom-call | flops 1 | bytes 1 | tf_op jit(solution)/shard_map/pallas_call | solution.py:26
  (135 shorter events, 43.9 us)
Async XLA Ops:
  1.9 12.5 %collective-permute-start = (bf16[2,160,640]{2,1,0:T(8,128)(2,1)S(1)}, bf16[2,160,640]{2,1,0:T(8,128)(2,1)S(1)}, u32[]{:S(2)}, u32[]{:S(2)}) collective-permute-start(bf16[2,160,640]{2,1,0:T(8,128)(2,1)S(1)} %pad_maximum_fusion.refs_4_), channel_id=1, source_target_pairs={{0,4},{4,8},{8,12},{12,14},{14,10},{10,6},{6,2},{2,0},{1,5},{5,9},... | collective-permute-start | bytes 1228808 | tf_op jit(solution)/shard_map/ppermute | solution.py:266
  4.9 11.2 %collective-permute-start.5 = (bf16[2,160,640]{2,1,0:T(8,128)(2,1)S(1)}, bf16[2,160,640]{2,1,0:T(8,128)(2,1)S(1)}, u32[]{:S(2)}, u32[]{:S(2)}) collective-permute-start(bf16[2,160,640]{2,1,0:T(8,128)(2,1)S(1)} %pad_maximum_fusion.refs_4_), channel_id=1, source_target_pairs={{4,0},{8,4},{12,8},{14,12},{10,14},{6,10},{2,6},{0,2},{5,1},{9,5},... | collective-permute-start | bytes 1228808 | tf_op jit(solution)/shard_map/ppermute | solution.py:266
  14.3 11.4 %collective-permute-start.6 = (bf16[2,160,640]{2,1,0:T(8,128)(2,1)S(1)}, bf16[2,160,640]{2,1,0:T(8,128)(2,1)S(1)}, u32[]{:S(2)}, u32[]{:S(2)}) collective-permute-start(bf16[2,160,640]{2,1,0:T(8,128)(2,1)S(1)} %collective-permute-done.refs_5_), channel_id=1, source_target_pairs={{0,4},{4,8},{8,12},{12,14},{14,10},{10,6},{6,2},{2,0},{1,5},{5,9},... | collective-permute-start | bytes 1228808 | tf_op jit(solution)/shard_map/ppermute | solution.py:266
  16.1 12.1 %collective-permute-start.7 = (bf16[2,160,640]{2,1,0:T(8,128)(2,1)S(1)}, bf16[2,160,640]{2,1,0:T(8,128)(2,1)S(1)}, u32[]{:S(2)}, u32[]{:S(2)}) collective-permute-start(bf16[2,160,640]{2,1,0:T(8,128)(2,1)S(1)} %collective-permute-done.5.refs_6_), channel_id=1, source_target_pairs={{4,0},{8,4},{12,8},{14,12},{10,14},{6,10},{2,6},{0,2},{5,1},{9,5},... | collective-permute-start | bytes 1228808 | tf_op jit(solution)/shard_map/ppermute | solution.py:266
  23.7 14.2 %collective-permute-start.1 = (bf16[192,1280]{1,0:T(8,128)(2,1)S(1)}, bf16[192,1280]{1,0:T(8,128)(2,1)S(1)}, u32[]{:S(2)}, u32[]{:S(2)}) collective-permute-start(bf16[192,1280]{1,0:T(8,128)(2,1)S(1)} %get-tuple-element.34), channel_id=1, source_target_pairs={{0,16},{16,0},{1,17},{17,1},{2,18},{18,2},{3,19},{19,3},{4,20},{20... | collective-permute-start | bytes 1474568 | tf_op jit(solution)/shard_map/ppermute | solution.py:259
  25.4 20.7 %collective-permute-start.2 = (bf16[192,1280]{1,0:T(8,128)(2,1)S(1)}, bf16[192,1280]{1,0:T(8,128)(2,1)S(1)}, u32[]{:S(2)}, u32[]{:S(2)}) collective-permute-start(bf16[192,1280]{1,0:T(8,128)(2,1)S(1)} %get-tuple-element.35), channel_id=1, source_target_pairs={{0,16},{16,0},{1,17},{17,1},{2,18},{18,2},{3,19},{19,3},{4,20},{20... | collective-permute-start | bytes 1474568 | tf_op jit(solution)/shard_map/ppermute | solution.py:259
  25.7 20.4 %collective-permute-start.8 = (bf16[2,160,640]{2,1,0:T(8,128)(2,1)S(1)}, bf16[2,160,640]{2,1,0:T(8,128)(2,1)S(1)}, u32[]{:S(2)}, u32[]{:S(2)}) collective-permute-start(bf16[2,160,640]{2,1,0:T(8,128)(2,1)S(1)} %collective-permute-done.6.refs_7_), channel_id=1, source_target_pairs={{0,4},{4,8},{8,12},{12,14},{14,10},{10,6},{6,2},{2,0},{1,5},{5,9},... | collective-permute-start | bytes 1228808 | tf_op jit(solution)/shard_map/ppermute | solution.py:266
  28.3 17.8 %collective-permute-start.9 = (bf16[2,160,640]{2,1,0:T(8,128)(2,1)S(1)}, bf16[2,160,640]{2,1,0:T(8,128)(2,1)S(1)}, u32[]{:S(2)}, u32[]{:S(2)}) collective-permute-start(bf16[2,160,640]{2,1,0:T(8,128)(2,1)S(1)} %collective-permute-done.7.refs_8_), channel_id=1, source_target_pairs={{4,0},{8,4},{12,8},{14,12},{10,14},{6,10},{2,6},{0,2},{5,1},{9,5},... | collective-permute-start | bytes 1228808 | tf_op jit(solution)/shard_map/ppermute | solution.py:266
  37.9 11.7 %collective-permute-start.3 = (bf16[192,1280]{1,0:T(8,128)(2,1)S(1)}, bf16[192,1280]{1,0:T(8,128)(2,1)S(1)}, u32[]{:S(2)}, u32[]{:S(2)}) collective-permute-start(bf16[192,1280]{1,0:T(8,128)(2,1)S(1)} %collective-permute-done.1.refs_0_), channel_id=1, source_target_pairs={{0,1},{1,0},{2,3},{3,2},{4,5},{5,4},{6,7},{7,6},{8,9},{9,8},{10,11... | collective-permute-start | bytes 1474568 | tf_op jit(solution)/shard_map/ppermute | solution.py:286
  47.4 7.7 %collective-permute-start.10 = (bf16[160,640]{1,0:T(8,128)(2,1)}, bf16[160,640]{1,0:T(8,128)(2,1)S(1)}, u32[]{:S(2)}, u32[]{:S(2)}) collective-permute-start(bf16[160,640]{1,0:T(8,128)(2,1)} %get-tuple-element.36), channel_id=1, source_target_pairs={{0,4},{4,8},{8,12},{12,14},{14,10},{10,6},{6,2},{2,0},{1,5},{5,9},... | collective-permute-start | bytes 614408 | tf_op jit(solution)/shard_map/ppermute | solution.py:280
  48.9 7.5 %collective-permute-start.11 = (bf16[160,640]{1,0:T(8,128)(2,1)}, bf16[160,640]{1,0:T(8,128)(2,1)}, u32[]{:S(2)}, u32[]{:S(2)}) collective-permute-start(bf16[160,640]{1,0:T(8,128)(2,1)} %get-tuple-element.37), channel_id=1, source_target_pairs={{4,0},{8,4},{12,8},{14,12},{10,14},{6,10},{2,6},{0,2},{5,1},{9,5},... | collective-permute-start | bytes 614408 | tf_op jit(solution)/shard_map/ppermute | solution.py:280
  69.5 7.5 %collective-permute-start.12 = (bf16[160,640]{1,0:T(8,128)(2,1)S(1)}, bf16[160,640]{1,0:T(8,128)(2,1)S(1)}, u32[]{:S(2)}, u32[]{:S(2)}) collective-permute-start(bf16[160,640]{1,0:T(8,128)(2,1)S(1)} %get-tuple-element.43), channel_id=1, source_target_pairs={{0,4},{4,8},{8,12},{12,14},{14,10},{10,6},{6,2},{2,0},{1,5},{5,9},... | collective-permute-start | bytes 614408 | tf_op jit(solution)/shard_map/ppermute | solution.py:333
  84.7 14.3 %collective-permute-start.18 = (bf16[384,640]{1,0:T(8,128)(2,1)}, bf16[384,640]{1,0:T(8,128)(2,1)S(1)}, u32[]{:S(2)}, u32[]{:S(2)}) collective-permute-start(bf16[384,640]{1,0:T(8,128)(2,1)} %shard_map.86), channel_id=1, source_target_pairs={{0,1},{1,0},{2,3},{3,2},{4,5},{5,4},{6,7},{7,6},{8,9},{9,8},{10,11... | collective-permute-start | bytes 1474568 | tf_op jit(solution)/shard_map/ppermute | solution.py:343
  84.7 7.9 %collective-permute-start.19 = (bf16[160,640]{1,0:T(8,128)(2,1)S(1)}, bf16[160,640]{1,0:T(8,128)(2,1)S(1)}, u32[]{:S(2)}, u32[]{:S(2)}) collective-permute-start(bf16[160,640]{1,0:T(8,128)(2,1)S(1)} %get-tuple-element.47.refs_4_), channel_id=1, source_target_pairs={{0,4},{4,8},{8,12},{12,14},{14,10},{10,6},{6,2},{2,0},{1,5},{5,9},... | collective-permute-start | bytes 614408 | tf_op jit(solution)/shard_map/ppermute | solution.py:333
  86.3 8.1 %collective-permute-start.20 = (bf16[160,640]{1,0:T(8,128)(2,1)}, bf16[160,640]{1,0:T(8,128)(2,1)S(1)}, u32[]{:S(2)}, u32[]{:S(2)}) collective-permute-start(bf16[160,640]{1,0:T(8,128)(2,1)} %copy-done.35), channel_id=1, source_target_pairs={{4,0},{8,4},{12,8},{14,12},{10,14},{6,10},{2,6},{0,2},{5,1},{9,5},... | collective-permute-start | bytes 614408 | tf_op jit(solution)/shard_map/ppermute | solution.py:333
  86.7 12.9 %collective-permute-start.16 = (bf16[160,640]{1,0:T(8,128)(2,1)}, bf16[160,640]{1,0:T(8,128)(2,1)S(1)}, u32[]{:S(2)}, u32[]{:S(2)}) collective-permute-start(bf16[160,640]{1,0:T(8,128)(2,1)} %copy-done.15), channel_id=1, source_target_pairs={{0,4},{4,8},{8,12},{12,14},{14,10},{10,6},{6,2},{2,0},{1,5},{5,9},... | collective-permute-start | bytes 614408 | tf_op jit(solution)/shard_map/ppermute | solution.py:333
  88.3 11.4 %collective-permute-start.17 = (bf16[160,640]{1,0:T(8,128)(2,1)}, bf16[160,640]{1,0:T(8,128)(2,1)S(1)}, u32[]{:S(2)}, u32[]{:S(2)}) collective-permute-start(bf16[160,640]{1,0:T(8,128)(2,1)} %copy-done.34), channel_id=1, source_target_pairs={{4,0},{8,4},{12,8},{14,12},{10,14},{6,10},{2,6},{0,2},{5,1},{9,5},... | collective-permute-start | bytes 614408 | tf_op jit(solution)/shard_map/ppermute | solution.py:333
  98.5 7.9 %collective-permute-start.24 = (bf16[160,640]{1,0:T(8,128)(2,1)}, bf16[160,640]{1,0:T(8,128)(2,1)}, u32[]{:S(2)}, u32[]{:S(2)}) collective-permute-start(bf16[160,640]{1,0:T(8,128)(2,1)} %get-tuple-element.58), channel_id=1, source_target_pairs={{4,0},{8,4},{12,8},{14,12},{10,14},{6,10},{2,6},{0,2},{5,1},{9,5},... | collective-permute-start | bytes 614408 | tf_op jit(solution)/shard_map/ppermute | solution.py:333
  101.8 18.4 %collective-permute-start.21 = (bf16[384,640]{1,0:T(8,128)(2,1)}, bf16[384,640]{1,0:T(8,128)(2,1)S(1)}, u32[]{:S(2)}, u32[]{:S(2)}) collective-permute-start(bf16[384,640]{1,0:T(8,128)(2,1)} %shard_map.90), channel_id=1, source_target_pairs={{0,1},{1,0},{2,3},{3,2},{4,5},{5,4},{6,7},{7,6},{8,9},{9,8},{10,11... | collective-permute-start | bytes 1474568 | tf_op jit(solution)/shard_map/ppermute | solution.py:367
  101.8 18.4 %collective-permute-start.22 = (bf16[384,640]{1,0:T(8,128)(2,1)}, bf16[384,640]{1,0:T(8,128)(2,1)S(1)}, u32[]{:S(2)}, u32[]{:S(2)}) collective-permute-start(bf16[384,640]{1,0:T(8,128)(2,1)} %copy-done.11), channel_id=1, source_target_pairs={{0,16},{16,0},{1,17},{17,1},{2,18},{18,2},{3,19},{19,3},{4,20},{20... | collective-permute-start | bytes 1474568 | tf_op jit(solution)/shard_map/ppermute | solution.py:345
  103.3 8.1 %collective-permute-start.26 = (bf16[160,640]{1,0:T(8,128)(2,1)}, bf16[160,640]{1,0:T(8,128)(2,1)S(1)}, u32[]{:S(2)}, u32[]{:S(2)}) collective-permute-start(bf16[160,640]{1,0:T(8,128)(2,1)} %copy-done.17), channel_id=1, source_target_pairs={{0,4},{4,8},{8,12},{12,14},{14,10},{10,6},{6,2},{2,0},{1,5},{5,9},... | collective-permute-start | bytes 614408 | tf_op jit(solution)/shard_map/ppermute | solution.py:333
  104.9 10.2 %collective-permute-start.23 = (bf16[160,640]{1,0:T(8,128)(2,1)S(1)}, bf16[160,640]{1,0:T(8,128)(2,1)S(1)}, u32[]{:S(2)}, u32[]{:S(2)}) collective-permute-start(bf16[160,640]{1,0:T(8,128)(2,1)S(1)} %get-tuple-element.55.refs_3_), channel_id=1, source_target_pairs={{0,4},{4,8},{8,12},{12,14},{14,10},{10,6},{6,2},{2,0},{1,5},{5,9},... | collective-permute-start | bytes 614408 | tf_op jit(solution)/shard_map/ppermute | solution.py:333
  110.3 8.0 %collective-permute-start.25 = (bf16[160,640]{1,0:T(8,128)(2,1)S(1)}, bf16[160,640]{1,0:T(8,128)(2,1)S(1)}, u32[]{:S(2)}, u32[]{:S(2)}) collective-permute-start(bf16[160,640]{1,0:T(8,128)(2,1)S(1)} %shard_map.91.refs_3_), channel_id=1, source_target_pairs={{4,0},{8,4},{12,8},{14,12},{10,14},{6,10},{2,6},{0,2},{5,1},{9,5},... | collective-permute-start | bytes 614408 | tf_op jit(solution)/shard_map/ppermute | solution.py:333
  111.4 10.0 %collective-permute-start.29 = (bf16[160,640]{1,0:T(8,128)(2,1)S(1)}, bf16[160,640]{1,0:T(8,128)(2,1)S(1)}, u32[]{:S(2)}, u32[]{:S(2)}) collective-permute-start(bf16[160,640]{1,0:T(8,128)(2,1)S(1)} %copy-done.33), channel_id=1, source_target_pairs={{4,0},{8,4},{12,8},{14,12},{10,14},{6,10},{2,6},{0,2},{5,1},{9,5},... | collective-permute-start | bytes 614408 | tf_op jit(solution)/shard_map/ppermute | solution.py:333
  (43 other events, 152.0 us)

commit v7 on v4

v7 whole, which is shorter than its diff:
```python
import functools

import jax
import jax.numpy as jnp
from jax import lax
from jax.experimental import pallas as pl
from jax.experimental.pallas import tpu as pltpu
from jax.sharding import PartitionSpec as P

BF16, F32 = jnp.bfloat16, jnp.float32
VMEM = pl.BlockSpec(memory_space=pltpu.VMEM)
ANY = pl.BlockSpec(memory_space=pl.ANY)
SMEM = pl.BlockSpec(memory_space=pltpu.SMEM)


def shape(dims, kind):
    return jax.ShapeDtypeStruct(dims, kind)


def call(kernel, ins, out_shape, scratch=(), vmem=4, left=(), cost=1, ties=()):
    count = len(ins)

    def body(*refs):
        kernel(*refs[:count], *refs[count + len(ties) :])

    return pl.pallas_call(
        body if ties else kernel,
        out_shape=out_shape,
        in_specs=[
            SMEM if x.dtype == jnp.int32 else ANY if i in left else VMEM
            for i, x in enumerate(ins)
        ]
        + [ANY] * len(ties),
        out_specs=jax.tree.map(lambda _: VMEM, out_shape),
        scratch_shapes=list(scratch),
        compiler_params=pltpu.CompilerParams(vmem_limit_bytes=vmem << 20),
        cost_estimate=pl.CostEstimate(flops=1, bytes_accessed=cost, transcendentals=0),
    )(*ins, *ties)


def hold(array, *ties):
    return pl.pallas_call(
        lambda *refs: None,
        out_shape=shape(array.shape, array.dtype),
        in_specs=[ANY] * (1 + len(ties)),
        out_specs=ANY,
        input_output_aliases={0: 0},
        cost_estimate=pl.CostEstimate(flops=1, bytes_accessed=1, transcendentals=0),
    )(array, *ties)


def dot(left, right, left_dim=1, right_dim=0):
    return lax.dot_general(
        left, right, (((left_dim,), (right_dim,)), ((), ())), preferred_element_type=F32
    )


def gelu_slope(values):
    return (
        0.5 * (1.0 + lax.erf(values * 0.7071067811865476))
        + values * jnp.exp(-0.5 * values * values) * 0.3989422804014327
    )


def norm_kernel(meta, lengths, frames, out_grad, gain, *refs):
    normed, grads, passing, stats = refs
    half = passing.shape[1]
    rows = pl.ds(pl.multiple_of(meta[1] * half, half), half)
    keep = lax.broadcasted_iota(jnp.int32, (frames.shape[0], 1), 0) < lengths[meta[0]]
    grads[...] = jnp.where(keep, out_grad[...].astype(F32), 0.0).astype(BF16)
    passing[1] = grads[rows, :]
    values = frames[...].astype(F32)
    centre = jnp.mean(values, axis=-1, keepdims=True)
    shifted = values - centre
    variance = jnp.mean(shifted * shifted, axis=-1, keepdims=True)
    inv_std = lax.rsqrt(variance + 1e-05)
    normed[...] = (shifted * inv_std * gain[...][None]).astype(BF16)
    passing[0] = normed[rows, :]
    stats[:, 0:1] = centre
    stats[:, 1:2] = inv_std


def back_through(normed, grads, up, down, d_pre, partial):
    pre_act = dot(normed[...], up[...])
    d_act = dot(grads[...], down[...])
    d_pre[...] = (d_act * gelu_slope(pre_act)).astype(BF16)
    partial[...] = dot(normed[...], d_pre[...], 0, 0)


def place_kernel(index, *refs):
    blocks, (up, down, sems) = refs[:-3], refs[-3:]
    depth = blocks[0].shape[1]
    copies = []
    for i, block in enumerate(blocks):
        rows = pl.ds(pl.multiple_of(index[i] * depth, depth), depth)
        copies.append(pltpu.make_async_copy(block.at[0], up.at[rows], sems.at[2 * i]))
        copies.append(pltpu.make_async_copy(block.at[1], down.at[rows], sems.at[2 * i + 1]))
    for copy in copies:
        copy.start()
    for copy in copies:
        copy.wait()


def other_kernel(index, first, second, near_up, near_down, *refs):
    d_pre, partial, up, down, normed, grads = refs[-6:]
    half = first.shape[1]
    for at, part in ((0, first), (half, second)):
        normed[at : at + half, :] = part[0]
        grads[at : at + half, :] = part[1]
    up[...] = near_up[...]
    down[...] = near_down[...]
    for ref, far in zip((up, down), refs[:-6]):
        depth = far.shape[0]
        rows = pl.ds(pl.multiple_of(index[index.shape[0] - 1] * depth, depth), depth)
        ref[rows, :] = far[...]
    back_through(normed, grads, up, down, d_pre, partial)


def own_kernel(normed, grads, up, down, d_pre, partial):
    back_through(normed, grads, up, down, d_pre, partial)


def d_norm_kernel(meta, d_pre_own, d_pre_other, up, keep, send):
    core = meta[1]
    rows, width = keep.shape[1:]
    mine = up[pl.ds(pl.multiple_of(core * width, width), width), :]
    theirs = up[pl.ds(pl.multiple_of((1 - core) * width, width), width), :]
    keep[0] = dot(d_pre_own[...], mine, 1, 1)
    keep[1] = dot(d_pre_other[...], mine, 1, 1)
    send[0] = dot(d_pre_own[...], theirs, 1, 1).astype(BF16)
    sent = dot(d_pre_other[...], theirs, 1, 1).astype(BF16)
    send[1, rows // 2 :, :] = sent[: rows // 2]
    send[1, : rows // 2, :] = sent[rows // 2 :]


def over_kernel(meta, keep, came, over):
    half = over.shape[0] // 2
    for i in range(2):
        at = lax.rem(i + meta[1], 2) * half
        rows = slice(i * half, (i + 1) * half)
        value = keep[1, rows, :] + came[1, rows, :].astype(F32)
        over[pl.ds(pl.multiple_of(at, half), half), :] = value.astype(BF16)


def own_columns(meta, ref, width):
    return ref[:, pl.ds(pl.multiple_of(meta[1] * width, width), width)]


def scale_kernel(meta, keep, came, back, frames, gain, stats, scaled, sums):
    width = scaled.shape[1]
    d_norm = keep[0] + came[0].astype(F32) + back[...].astype(F32)
    value = d_norm * own_columns(meta, gain, width)
    scaled[...] = value
    rows = own_columns(meta, frames, width).astype(F32)
    centred = (rows - stats[:, 0:1]) * stats[:, 1:2]
    sums[:, 0:1] = jnp.sum(value, axis=-1, keepdims=True)
    sums[:, 1:2] = jnp.sum(value * centred, axis=-1, keepdims=True)


def input_kernel(meta, scaled, sums, came, frames, grads, stats, out):
    width = scaled.shape[1]
    means = (sums[...] + came[...]) * (0.5 / width)
    rows = own_columns(meta, frames, width).astype(F32)
    inv_std = stats[:, 1:2]
    centred = (rows - stats[:, 0:1]) * inv_std
    value = inv_std * (scaled[...] - means[:, 0:1] - centred * means[:, 1:2])
    out[...] = (own_columns(meta, grads, width).astype(F32) + value).astype(BF16)


def hop_kernel(at, mode, index, *refs):
    windows = [i for i in range(2) if mode[i] is not None]
    partial, came, out = refs[: len(windows)], refs[len(windows) : -1], refs[-1]
    depth = out.shape[1]
    rows = pl.ds(pl.multiple_of(index[at] * depth, depth), depth)
    for k, i in enumerate(windows):
        value = partial[k][rows, :]
        if mode[i]:
            value = value + came[0][k if came[0].shape[0] == 2 else 0].astype(F32)
        out[k] = value.astype(BF16)


def own_total_kernel(index, own, other, down, total):
    depth = total.shape[1]
    rows = pl.ds(pl.multiple_of(index[0] * depth, depth), depth)
    total[0] = own[rows, :] + down[0].astype(F32)
    total[1] = other[rows, :] + down[1].astype(F32)


def total_kernel(both, up, total, passing):
    total[...] = both[0] + up[0].astype(F32)
    passing[...] = (both[1] + up[1].astype(F32)).astype(BF16)


def join_kernel(meta, own, passed, out):
    width = own.shape[1]
    side = meta[2]
    out[:, pl.ds(pl.multiple_of(side * width, width), width)] = own[...]
    other = pl.ds(pl.multiple_of((1 - side) * width, width), width)
    out[:, other] = passed[...].astype(F32)


def ring_member(place, count):
    place = place % count
    return jnp.where(place < count // 2, 2 * place, 2 * (count - 1 - place) + 1)


def shards(frames, out_grad, ln_gain, w_up, w_down, lengths):
    peers = lax.axis_size("gx")
    half = peers // 2
    own = lax.axis_index("gx")
    side = lax.axis_index("groups")
    core = lax.axis_index("gy")
    frame_len, width = frames.shape[1:]
    depth, hidden = w_up.shape
    quarter = hidden // 2
    half_width = width // 2
    half_rows = frame_len // 2
    ringed = peers <= 16 and peers % 2 == 0 and depth % 16 == 0

    order = list(range(0, peers, 2)) + list(range(peers - 1, 0, -2))
    ahead = [(order[i], order[(i + 1) % peers]) for i in range(peers)]
    behind = [(b, a) for a, b in ahead]
    place = jnp.where(own % 2 == 0, own // 2, peers - 1 - own // 2)
    swap = [(0, 1), (1, 0)]
    after = lax.optimization_barrier

    pair = jnp.stack(
        [lax.dynamic_slice_in_dim(w, side * quarter, quarter, 1) for w in (w_up, w_down)]
    )
    pair, frames, out_grad, ln_gain, lengths = after((pair, frames, out_grad, ln_gain, lengths))
    meta = jnp.stack([own, core, side]).astype(jnp.int32)
    frames, out_grad = frames[0], out_grad[0]

    rows_of = shape((frame_len, width), BF16)
    normed, grads, passing, stats = call(
        norm_kernel,
        (meta, lengths, frames, out_grad, ln_gain),
        (rows_of, rows_of, shape((2, half_rows, width), BF16), shape((frame_len, 2), F32)),
        cost=10 * frame_len * width,
    )

    weight = shape((width, quarter), BF16)
    block_of = shape((depth, quarter), BF16)
    if ringed:
        blocks = {0: pair}
        up, down = pair, pair
        for step in range(1, half):
            up, down = lax.ppermute(up, "gx", ahead), lax.ppermute(down, "gx", behind)
            blocks[-step], blocks[step] = up, down
        first = lax.ppermute(passing, "groups", swap)
        first, up, down = after((first, up, down))
        steps = list(blocks) + [half]
        index = jnp.stack([ring_member(place + step + peers, peers) for step in steps])
        index = index.astype(jnp.int32)
        near = call(
            place_kernel,
            (index, *blocks.values()),
            (weight, weight),
            [pltpu.SemaphoreType.DMA((2 * len(blocks),))],
            left=range(1, len(blocks) + 1),
        )
        far = [lax.ppermute(up[0], "gx", ahead), lax.ppermute(down[1], "gx", behind)]
    else:
        first = lax.ppermute(passing, "groups", swap)
        near = [lax.all_gather(block, "gx", axis=0, tiled=True) for block in (pair[0], pair[1])]
        index, far = jnp.zeros((1,), jnp.int32), []
    second = lax.ppermute(first, "gy", swap)

    d_pre_of, partial_of = shape((frame_len, quarter), BF16), shape((width, quarter), F32)
    d_pre_other, partial_other, full_up, full_down = call(
        other_kernel,
        (index, first, second, *near, *far),
        (d_pre_of, partial_of, weight, weight),
        [pltpu.VMEM((frame_len, width), BF16)] * 2,
        vmem=10,
    )
    d_pre_own, partial_own = call(
        own_kernel, (normed, grads, full_up, full_down), (d_pre_of, partial_of), vmem=10
    )
    partial = [partial_own, partial_other]

    half_rows_of = shape((frame_len, half_width), BF16)

    def own_d_norm(*ties):
        return call(
            d_norm_kernel,
            (meta, d_pre_own, d_pre_other, full_up),
            (shape((2, frame_len, half_width), F32), shape((2, frame_len, half_width), BF16)),
            vmem=10,
            ties=ties,
        )

    def over_cores(keep, came, *ties):
        return call(over_kernel, (meta, keep, came), half_rows_of, ties=ties)

    if ringed:
        place_of = {step: i for i, step in enumerate(steps)}
        place_of[-half] = place_of[half]

        def hop(step, mode, *given, ties=()):
            sums = [partial[i] for i in range(2) if mode[i] is not None]
            kernel = functools.partial(hop_kernel, place_of[step], mode)
            out = shape((len(sums), depth, quarter), BF16)
            block = call(kernel, (index, *sums, *given), out, ties=ties)
            return block, lax.ppermute(block, "gx", ahead if step > 0 else behind)

        _, down = hop(-half, (None, 0))
        tie, up = hop(half, (0, None))
        keep, send = own_d_norm(tie)
        for step in range(half - 1, 0, -1):
            farthest = step == half - 1
            tie, down = hop(-step, (0, 1) if farthest else (1, 1), down, ties=(tie,))
            if farthest:
                send = hold(send, tie, up)
                came = lax.ppermute(send, "gy", swap)
            tie, up = hop(step, (1, 0) if farthest else (1, 1), up, ties=(tie,))
            if step == half - 2:
                over = over_cores(keep, came, tie)
                tie = over
                back = lax.ppermute(over, "groups", swap)
        both = call(own_total_kernel, (index, *partial, down), shape((2, depth, quarter), F32))
        total, passing = call(
            total_kernel, (both, up), (shape((depth, quarter), F32), block_of), ties=(back,)
        )
        tail = (passing,)
    else:
        keep, send = own_d_norm()
        came = lax.ppermute(send, "gy", swap)
        back = lax.ppermute(over_cores(keep, came), "groups", swap)
        total, passing = [
            lax.psum_scatter(p, "gx", scatter_dimension=0, tiled=True) for p in partial
        ]
        passing, tail = passing.astype(BF16), ()
    passed = lax.ppermute(passing, "groups", swap)
    up_grad = call(join_kernel, (meta, total, passed), shape((depth, hidden), F32))

    gain = ln_gain[None]
    scaled, sums = call(
        scale_kernel,
        (meta, keep, came, back, frames, gain, stats),
        (shape((frame_len, half_width), F32), shape((frame_len, 2), F32)),
        ties=tail,
    )
    input_grad = call(
        input_kernel,
        (meta, scaled, sums, lax.ppermute(sums, "gy", swap), frames, grads, stats),
        shape((frame_len, half_width), BF16),
    )
    return (input_grad[None], up_grad)


def solution(mesh):
    placed = (
        P(("groups", "gx"), None, None),
        P(("groups", "gx"), None, None),
        P(),
        P("gx", "gy"),
        P("gx", "gy"),
        P("groups"),
    )
    return jax.shard_map(
        shards,
        mesh=mesh,
        in_specs=placed,
        out_specs=(P(("groups", "gx"), None, "gy"), P(("groups", "gx"), "gy")),
        check_vma=False,
    )
```

time: 111 us -> 115 us (1.036)
  waiting for transfers between devices: 51.8 us -> 41.9 us
  local copies, waits for them, and re-layouts: 13.8 us -> 22.9 us
  Pallas kernels: 21.5 us -> 25.7 us
  starting transfers between devices: 21.5 us -> 23.1 us
    ppermute x12 -> x6, waiting for transfers between devices: 45.4 us -> 11.7 us  [shards(): up, down = (lax.ppermute(up, 'gx', ahead), lax.ppermute(down, 'gx', behind))]
    ppermute x4 -> x10, waiting for transfers between devices: 2 us -> 28.8 us  [the longest x8 23.6 us: hop(): return (block, lax.ppermute(block, 'gx', ahead if step > 0 else behind))]
    unnamed x24 -> x68, local copies, waits for them, and re-layouts: 9.16 us -> 20.2 us
    ppermute x4 -> x10, starting transfers between devices: 4.01 us -> 10.8 us  [the longest x8 8.85 us: hop(): return (block, lax.ppermute(block, 'gx', ahead if step > 0 else behind))]
    ppermute x12 -> x6, starting transfers between devices: 13.6 us -> 7.14 us  [shards(): up, down = (lax.ppermute(up, 'gx', ahead), lax.ppermute(down, 'gx', behind))]
    pallas_call x16 -> x20, Pallas kernels: 21.5 us -> 25.7 us  [the longest x19 25.7 us: call(): pl.pallas_call(body if ties else kernel, out_shape=out_shape, in_specs=[S...]
    dynamic_slice x2 -> x0, local copies, waits for them, and re-layouts: 2.42 us -> none  [the longest x1 1.26 us: shards(): length = lax.dynamic_index_in_dim(lengths, own, 0, keepdims=False)]
    ppermute x1, waiting for transfers between devices: 1.29 us -> 0.01 us  [shards(): lax.ppermute(down[1], 'gx', behind)]
  transfers between devices with their start and end apart: 22 -> 22, of which waited for: 17 -> 13; matrix products, arithmetic and copies ran while one was open for 4% -> 1% of each run, Pallas kernels for 13% -> 17%
where the time goes in v7:
time: 115 us
  waiting for transfers between devices  41.9 us (36%)
  Pallas kernels  25.7 us (22%)
  starting transfers between devices  23.1 us (20%)
  local copies, waits for them, and re-layouts  22.9 us (20%)
    pallas_call x19, Pallas kernels, call(): pl.pallas_call(body if ties else kernel, out_shape=out_shape, in_specs=[S...  25.7 us
    ppermute x8, waiting for transfers between devices, hop(): return (block, lax.ppermute(block, 'gx', ahead if step > 0 else behind))  23.6 us
    unnamed x68, local copies, waits for them, and re-layouts  20.2 us
    ppermute x6, waiting for transfers between devices, shards(): up, down = (lax.ppermute(up, 'gx', ahead), lax.ppermute(down, 'gx', behind))  11.7 us
    ppermute x8, starting transfers between devices, hop(): return (block, lax.ppermute(block, 'gx', ahead if step > 0 else behind))  8.85 us
    ppermute x6, starting transfers between devices, shards(): up, down = (lax.ppermute(up, 'gx', ahead), lax.ppermute(down, 'gx', behind))  7.14 us
    ppermute x1, waiting for transfers between devices, shards(): first = lax.ppermute(passing, 'groups', swap)  5.17 us
  transfers between devices with their start and end apart: 22, of which 13 were waited for; matrix products, arithmetic and copies ran while one was open for 1% of the time, Pallas kernels for 17%

profile of v7, /device:TPU:0, one launch (start us, length us, event | category | flops | bytes accessed | tf_op | source)
XLA Modules:
  0.0 114.7 jit_solution(7426278665257205593)
XLA Ops:
  1.9 3.1 %collective-permute-start.1 = (bf16[2,160,640]{2,1,0:T(8,128)(2,1)S(1)}, bf16[2,160,640]{2,1,0:T(8,128)(2,1)S(1)}, u32[]{:S(2)}, u32[]{:S(2)}) collective-permute-start(bf16[2,160,640]{2,1,0:T(8,128)(2,1)S(1)} %pad_maximum_fusion.refs_0_), channel_id=1, source_target_pairs={{0,4},{4,8},{8,12},{12,14},{14,10},{10,6},{6,2},{2,0},{1,5},{5,9},... | collective-permute-start | bytes 1228808 | tf_op jit(solution)/shard_map/ppermute | solution.py:248
  6.3 1.6 %shard_map.77 = (bf16[384,1280]{1,0:T(8,128)(2,1)S(1)}, bf16[384,1280]{1,0:T(8,128)(2,1)S(1)}, bf16[2,192,1280]{2,1,0:T(8,128)(2,1)S(1)}, f32[384,2]{1,0:T(8,128)S(1)}) custom-call(s32[3]{0:T(128)S(1)} %pad_add_fusion.meta.refs_0_, s32[8]{0:T(128)S(1)} %copy-done.33, bf16[384,1280]{1,0:T(8,128)(2,1)S(1)} %bitcast.22, bf16[384,1280]{1,0:T(8,128)(2,1)S(1)} %bitcast.25, ...), custom_call_target="tpu_custom_call" | custom-call | flops 1 | bytes 4915200 | tf_op jit(solution)/shard_map/pallas_call | solution.py:26
  10.5 1.9 %collective-permute-start = (bf16[2,192,1280]{2,1,0:T(8,128)(2,1)S(1)}, bf16[2,192,1280]{2,1,0:T(8,128)(2,1)S(1)}, u32[]{:S(2)}, u32[]{:S(2)}) collective-permute-start(bf16[2,192,1280]{2,1,0:T(8,128)(2,1)S(1)} %get-tuple-element.34), channel_id=1, source_target_pairs={{0,16},{16,0},{1,17},{17,1},{2,18},{18,2},{3,19},{19,3},{4,20},{20... | collective-permute-start | bytes 2949128 | tf_op jit(solution)/shard_map/ppermute | solution.py:250
  12.5 1.9 %collective-permute-done.1.refs_1_ = bf16[2,160,640]{2,1,0:T(8,128)(2,1)S(1)} collective-permute-done((bf16[2,160,640]{2,1,0:T(8,128)(2,1)S(1)}, bf16[2,160,640]{2,1,0:T(8,128)(2,1)S(1)}, u32[]{:S(2)}, u32[]{:S(2)}) %collective-permute-start.1) | collective-permute-done | bytes 409632 | tf_op jit(solution)/shard_map/ppermute | solution.py:248
  14.4 1.8 %collective-permute-start.2 = (bf16[2,160,640]{2,1,0:T(8,128)(2,1)S(1)}, bf16[2,160,640]{2,1,0:T(8,128)(2,1)S(1)}, u32[]{:S(2)}, u32[]{:S(2)}) collective-permute-start(bf16[2,160,640]{2,1,0:T(8,128)(2,1)S(1)} %collective-permute-done.1.refs_1_), channel_id=1, source_target_pairs={{0,4},{4,8},{8,12},{12,14},{14,10},{10,6},{6,2},{2,0},{1,5},{5,9},... | collective-permute-start | bytes 1228808 | tf_op jit(solution)/shard_map/ppermute | solution.py:248
  17.9 7.1 %collective-permute-done.2.refs_3_ = bf16[2,160,640]{2,1,0:T(8,128)(2,1)S(1)} collective-permute-done((bf16[2,160,640]{2,1,0:T(8,128)(2,1)S(1)}, bf16[2,160,640]{2,1,0:T(8,128)(2,1)S(1)}, u32[]{:S(2)}, u32[]{:S(2)}) %collective-permute-start.2) | collective-permute-done | bytes 409632 | tf_op jit(solution)/shard_map/ppermute | solution.py:248
  28.6 5.2 %collective-permute-done.first = bf16[2,192,1280]{2,1,0:T(8,128)(2,1)S(1)} collective-permute-done((bf16[2,192,1280]{2,1,0:T(8,128)(2,1)S(1)}, bf16[2,192,1280]{2,1,0:T(8,128)(2,1)S(1)}, u32[]{:S(2)}, u32[]{:S(2)}) %collective-permute-start) | collective-permute-done | bytes 983072 | tf_op jit(solution)/shard_map/ppermute | solution.py:250
  34.7 1.7 %collective-permute-done.6.refs_6_ = bf16[2,160,640]{2,1,0:T(8,128)(2,1)S(1)} collective-permute-done((bf16[2,160,640]{2,1,0:T(8,128)(2,1)S(1)}, bf16[2,160,640]{2,1,0:T(8,128)(2,1)S(1)}, u32[]{:S(2)}, u32[]{:S(2)}) %collective-permute-start.6) | collective-permute-done | bytes 409632 | tf_op jit(solution)/shard_map/ppermute | solution.py:248
  37.1 1.6 %collective-permute-start.8 = (bf16[160,640]{1,0:T(8,128)(2,1)}, bf16[160,640]{1,0:T(8,128)(2,1)S(1)}, u32[]{:S(2)}, u32[]{:S(2)}) collective-permute-start(bf16[160,640]{1,0:T(8,128)(2,1)} %slice_bitcast_fusion.1), channel_id=1, source_target_pairs={{0,4},{4,8},{8,12},{12,14},{14,10},{10,6},{6,2},{2,0},{1,5},{5,9},... | collective-permute-start | bytes 614408 | tf_op jit(solution)/shard_map/ppermute | solution.py:262
  43.9 4.5 %shard_map.78 = (bf16[1280,640]{1,0:T(8,128)(2,1)S(1)}, bf16[1280,640]{1,0:T(8,128)(2,1)S(1)}) custom-call(s32[8]{0:T(128)S(1)} %stack.63.index.refs_0_, bf16[2,160,640]{2,1,0:T(8,128)(2,1)S(1)} %pad_maximum_fusion.refs_0_, bf16[2,160,640]{2,1,0:T(8,128)(2,1)S(1)} %copy-done.25, bf16[2,160,640]{2,1,0:T(8,128)(2,1)S(1)} %copy-done.27, ...), custom_call_target="tpu_custom_call" | custom-call | flops 1 | bytes 1 | tf_op jit(solution)/shard_map/pallas_call | solution.py:26
  51.8 3.8 %shard_map.79 = (bf16[384,640]{1,0:T(8,128)(2,1)S(1)}, f32[1280,640]{1,0:T(8,128)S(1)}, bf16[1280,640]{1,0:T(8,128)(2,1)S(1)}, bf16[1280,640]{1,0:T(8,128)(2,1)S(1)}) custom-call(s32[8]{0:T(128)S(1)} %stack.63.index.refs_0_, bf16[2,192,1280]{2,1,0:T(8,128)(2,1)S(1)} %copy-done.16, bf16[2,192,1280]{2,1,0:T(8,128)(2,1)S(1)} %copy-done.18, ...), custom_call_target="tpu_custom_call" | custom-call | flops 1 | bytes 1 | tf_op jit(solution)/shard_map/pallas_call | solution.py:26
  57.2 2.7 %shard_map.80 = (bf16[384,640]{1,0:T(8,128)(2,1)S(1)}, f32[1280,640]{1,0:T(8,128)S(1)}) custom-call(bf16[384,1280]{1,0:T(8,128)(2,1)S(1)} %copy-done.13, bf16[384,1280]{1,0:T(8,128)(2,1)S(1)} %copy-done.8, bf16[1280,640]{1,0:T(8,128)(2,1)S(1)} %get-tuple-element.41.up.refs_3_, bf16[1280,640]{1,0:T(8,128)(2,1)S(1)} %get-tuple-element.42.down), custom_call_target="tpu_custom_call" | custom-call | flops 1 | bytes 1 | tf_op jit(solution)/shard_map/pallas_call | solution.py:26
  60.4 1.6 %collective-permute-start.11 = (bf16[1,160,640]{2,1,0:T(8,128)(2,1)S(1)}, bf16[1,160,640]{2,1,0:T(8,128)(2,1)S(1)}, u32[]{:S(2)}, u32[]{:S(2)}) collective-permute-start(bf16[1,160,640]{2,1,0:T(8,128)(2,1)S(1)} %shard_map.81.refs_4_), channel_id=1, source_target_pairs={{0,4},{4,8},{8,12},{12,14},{14,10},{10,6},{6,2},{2,0},{1,5},{5,9},... | collective-permute-start | bytes 614408 | tf_op jit(solution)/shard_map/ppermute | solution.py:305
  62.0 2.5 %shard_map.82 = (f32[2,384,640]{2,1,0:T(8,128)S(1)}, bf16[2,384,640]{2,1,0:T(8,128)(2,1)S(1)}) custom-call(s32[3]{0:T(128)S(1)} %pad_add_fusion.meta.refs_0_, bf16[384,640]{1,0:T(8,128)(2,1)S(1)} %get-tuple-element.43.refs_1_, bf16[384,640]{1,0:T(8,128)(2,1)S(1)} %get-tuple-element.44.refs_2_, bf16[1280,640]{1,0:T(8,128)(2,1)S(1)} %get-tuple-element.41.up.refs_3_, ...), custom_call_target="tpu_custom_call" | custom-call | flops 1 | bytes 1 | tf_op jit(solution)/shard_map/pallas_call | solution.py:26
  69.0 1.9 %copy-done.1 = f32[1280,640]{1,0:T(8,128)S(1)} copy-done((f32[1280,640]{1,0:T(8,128)S(1)}, f32[1280,640]{1,0:T(8,128)}, u32[]{:S(2)}) %copy-start.1) | copy-done | bytes 3276824
  74.6 5.5 %collective-permute-done.14.refs_3_ = bf16[2,160,640]{2,1,0:T(8,128)(2,1)S(1)} collective-permute-done((bf16[2,160,640]{2,1,0:T(8,128)(2,1)}, bf16[2,160,640]{2,1,0:T(8,128)(2,1)S(1)}, u32[]{:S(2)}, u32[]{:S(2)}) %collective-permute-start.14) | collective-permute-done | bytes 409632 | tf_op jit(solution)/shard_map/ppermute | solution.py:305
  81.7 3.3 %collective-permute-done.13.refs_3_ = bf16[2,160,640]{2,1,0:T(8,128)(2,1)S(1)} collective-permute-done((bf16[2,160,640]{2,1,0:T(8,128)(2,1)S(1)}, bf16[2,160,640]{2,1,0:T(8,128)(2,1)S(1)}, u32[]{:S(2)}, u32[]{:S(2)}) %collective-permute-start.13) | collective-permute-done | bytes 409632 | tf_op jit(solution)/shard_map/ppermute | solution.py:305
  87.6 1.6 %collective-permute-start.15 = (bf16[384,640]{1,0:T(8,128)(2,1)S(1)}, bf16[384,640]{1,0:T(8,128)(2,1)S(1)}, u32[]{:S(2)}, u32[]{:S(2)}) collective-permute-start(bf16[384,640]{1,0:T(8,128)(2,1)S(1)} %shard_map.89.refs_4_), channel_id=1, source_target_pairs={{0,16},{16,0},{1,17},{17,1},{2,18},{18,2},{3,19},{19,3},{4,20},{20... | collective-permute-start | bytes 1474568 | tf_op jit(solution)/shard_map/ppermute | solution.py:320
  89.1 2.9 %collective-permute-done.16.refs_3_ = bf16[2,160,640]{2,1,0:T(8,128)(2,1)S(1)} collective-permute-done((bf16[2,160,640]{2,1,0:T(8,128)(2,1)S(1)}, bf16[2,160,640]{2,1,0:T(8,128)(2,1)S(1)}, u32[]{:S(2)}, u32[]{:S(2)}) %collective-permute-start.16) | collective-permute-done | bytes 409632 | tf_op jit(solution)/shard_map/ppermute | solution.py:305
  93.5 3.0 %collective-permute-done.18.refs_3_ = bf16[2,160,640]{2,1,0:T(8,128)(2,1)S(1)} collective-permute-done((bf16[2,160,640]{2,1,0:T(8,128)(2,1)S(1)}, bf16[2,160,640]{2,1,0:T(8,128)(2,1)S(1)}, u32[]{:S(2)}, u32[]{:S(2)}) %collective-permute-start.18) | collective-permute-done | bytes 409632 | tf_op jit(solution)/shard_map/ppermute | solution.py:305
  98.4 4.5 %collective-permute-done.17.down = bf16[2,160,640]{2,1,0:T(8,128)(2,1)S(1)} collective-permute-done((bf16[2,160,640]{2,1,0:T(8,128)(2,1)S(1)}, bf16[2,160,640]{2,1,0:T(8,128)(2,1)S(1)}, u32[]{:S(2)}, u32[]{:S(2)}) %collective-permute-start.17) | collective-permute-done | bytes 409632 | tf_op jit(solution)/shard_map/ppermute | solution.py:305
  103.5 3.5 %collective-permute-done.19.refs_1_ = bf16[2,160,640]{2,1,0:T(8,128)(2,1)S(1)} collective-permute-done((bf16[2,160,640]{2,1,0:T(8,128)(2,1)S(1)}, bf16[2,160,640]{2,1,0:T(8,128)(2,1)S(1)}, u32[]{:S(2)}, u32[]{:S(2)}) %collective-permute-start.19) | collective-permute-done | bytes 409632 | tf_op jit(solution)/shard_map/ppermute | solution.py:305
  107.2 1.5 %collective-permute-start.21 = (bf16[160,640]{1,0:T(8,128)(2,1)S(1)}, bf16[160,640]{1,0:T(8,128)(2,1)S(1)}, u32[]{:S(2)}, u32[]{:S(2)}) collective-permute-start(bf16[160,640]{1,0:T(8,128)(2,1)S(1)} %get-tuple-element.50.refs_7_), channel_id=1, source_target_pairs={{0,16},{16,0},{1,17},{17,1},{2,18},{18,2},{3,19},{19,3},{4,20},{20... | collective-permute-start | bytes 614408 | tf_op jit(solution)/shard_map/ppermute | solution.py:334
  111.3 1.9 %shard_map.95 = bf16[384,640]{1,0:T(8,128)(2,1)} custom-call(s32[3]{0:T(128)S(1)} %pad_add_fusion.meta.refs_0_, f32[384,640]{1,0:T(8,128)S(1)} %get-tuple-element.51.scaled, f32[384,2]{1,0:T(8,128)S(1)} %get-tuple-element.52.sums, f32[384,2]{1,0:T(8,128)S(1)} %collective-permute-done.20.came, bf16[384,1280]{1,0:T(8,128)(2,1)S(1)} %bitcast.24, ...), custom_call_target="tpu_custom_call" | custom-call | flops 1 | bytes 1 | tf_op jit(solution)/shard_map/pallas_call | solution.py:26
  (115 shorter events, 43.1 us)
Async XLA Ops:
  1.9 12.5 %collective-permute-start.1 = (bf16[2,160,640]{2,1,0:T(8,128)(2,1)S(1)}, bf16[2,160,640]{2,1,0:T(8,128)(2,1)S(1)}, u32[]{:S(2)}, u32[]{:S(2)}) collective-permute-start(bf16[2,160,640]{2,1,0:T(8,128)(2,1)S(1)} %pad_maximum_fusion.refs_0_), channel_id=1, source_target_pairs={{0,4},{4,8},{8,12},{12,14},{14,10},{10,6},{6,2},{2,0},{1,5},{5,9},... | collective-permute-start | bytes 1228808 | tf_op jit(solution)/shard_map/ppermute | solution.py:248
  5.0 12.0 %collective-permute-start.4 = (bf16[2,160,640]{2,1,0:T(8,128)(2,1)S(1)}, bf16[2,160,640]{2,1,0:T(8,128)(2,1)S(1)}, u32[]{:S(2)}, u32[]{:S(2)}) collective-permute-start(bf16[2,160,640]{2,1,0:T(8,128)(2,1)S(1)} %pad_maximum_fusion.refs_0_), channel_id=1, source_target_pairs={{4,0},{8,4},{12,8},{14,12},{10,14},{6,10},{2,6},{0,2},{5,1},{9,5},... | collective-permute-start | bytes 1228808 | tf_op jit(solution)/shard_map/ppermute | solution.py:248
  10.5 23.2 %collective-permute-start = (bf16[2,192,1280]{2,1,0:T(8,128)(2,1)S(1)}, bf16[2,192,1280]{2,1,0:T(8,128)(2,1)S(1)}, u32[]{:S(2)}, u32[]{:S(2)}) collective-permute-start(bf16[2,192,1280]{2,1,0:T(8,128)(2,1)S(1)} %get-tuple-element.34), channel_id=1, source_target_pairs={{0,16},{16,0},{1,17},{17,1},{2,18},{18,2},{3,19},{19,3},{4,20},{20... | collective-permute-start | bytes 2949128 | tf_op jit(solution)/shard_map/ppermute | solution.py:250
  14.4 10.7 %collective-permute-start.2 = (bf16[2,160,640]{2,1,0:T(8,128)(2,1)S(1)}, bf16[2,160,640]{2,1,0:T(8,128)(2,1)S(1)}, u32[]{:S(2)}, u32[]{:S(2)}) collective-permute-start(bf16[2,160,640]{2,1,0:T(8,128)(2,1)S(1)} %collective-permute-done.1.refs_1_), channel_id=1, source_target_pairs={{0,4},{4,8},{8,12},{12,14},{14,10},{10,6},{6,2},{2,0},{1,5},{5,9},... | collective-permute-start | bytes 1228808 | tf_op jit(solution)/shard_map/ppermute | solution.py:248
  16.9 10.4 %collective-permute-start.5 = (bf16[2,160,640]{2,1,0:T(8,128)(2,1)S(1)}, bf16[2,160,640]{2,1,0:T(8,128)(2,1)S(1)}, u32[]{:S(2)}, u32[]{:S(2)}) collective-permute-start(bf16[2,160,640]{2,1,0:T(8,128)(2,1)S(1)} %collective-permute-done.4.refs_2_), channel_id=1, source_target_pairs={{4,0},{8,4},{12,8},{14,12},{10,14},{6,10},{2,6},{0,2},{5,1},{9,5},... | collective-permute-start | bytes 1228808 | tf_op jit(solution)/shard_map/ppermute | solution.py:248
  25.0 9.7 %collective-permute-start.3 = (bf16[2,160,640]{2,1,0:T(8,128)(2,1)S(1)}, bf16[2,160,640]{2,1,0:T(8,128)(2,1)S(1)}, u32[]{:S(2)}, u32[]{:S(2)}) collective-permute-start(bf16[2,160,640]{2,1,0:T(8,128)(2,1)S(1)} %collective-permute-done.2.refs_3_), channel_id=1, source_target_pairs={{0,4},{4,8},{8,12},{12,14},{14,10},{10,6},{6,2},{2,0},{1,5},{5,9},... | collective-permute-start | bytes 1228808 | tf_op jit(solution)/shard_map/ppermute | solution.py:248
  27.3 9.1 %collective-permute-start.6 = (bf16[2,160,640]{2,1,0:T(8,128)(2,1)S(1)}, bf16[2,160,640]{2,1,0:T(8,128)(2,1)S(1)}, u32[]{:S(2)}, u32[]{:S(2)}) collective-permute-start(bf16[2,160,640]{2,1,0:T(8,128)(2,1)S(1)} %collective-permute-done.5.refs_4_), channel_id=1, source_target_pairs={{4,0},{8,4},{12,8},{14,12},{10,14},{6,10},{2,6},{0,2},{5,1},{9,5},... | collective-permute-start | bytes 1228808 | tf_op jit(solution)/shard_map/ppermute | solution.py:248
  33.8 14.7 %copy-start.15 = (bf16[2,192,1280]{2,1,0:T(8,128)(2,1)}, bf16[2,192,1280]{2,1,0:T(8,128)(2,1)S(1)}, u32[]{:S(2)}) copy-start(bf16[2,192,1280]{2,1,0:T(8,128)(2,1)S(1)} %collective-permute-done.first) | copy-start | bytes 2949124
  36.4 12.1 %collective-permute-start.7 = (bf16[2,192,1280]{2,1,0:T(8,128)(2,1)S(1)}, bf16[2,192,1280]{2,1,0:T(8,128)(2,1)S(1)}, u32[]{:S(2)}, u32[]{:S(2)}) collective-permute-start(bf16[2,192,1280]{2,1,0:T(8,128)(2,1)S(1)} %collective-permute-done.first), channel_id=1, source_target_pairs={{0,1},{1,0},{2,3},{3,2},{4,5},{5,4},{6,7},{7,6},{8,9},{9,8},{10,11... | collective-permute-start | bytes 2949128 | tf_op jit(solution)/shard_map/ppermute | solution.py:267
  37.1 11.3 %collective-permute-start.8 = (bf16[160,640]{1,0:T(8,128)(2,1)}, bf16[160,640]{1,0:T(8,128)(2,1)S(1)}, u32[]{:S(2)}, u32[]{:S(2)}) collective-permute-start(bf16[160,640]{1,0:T(8,128)(2,1)} %slice_bitcast_fusion.1), channel_id=1, source_target_pairs={{0,4},{4,8},{8,12},{12,14},{14,10},{10,6},{6,2},{2,0},{1,5},{5,9},... | collective-permute-start | bytes 614408 | tf_op jit(solution)/shard_map/ppermute | solution.py:262
  39.4 9.1 %collective-permute-start.9 = (bf16[160,640]{1,0:T(8,128)(2,1)}, bf16[160,640]{1,0:T(8,128)(2,1)}, u32[]{:S(2)}, u32[]{:S(2)}) collective-permute-start(bf16[160,640]{1,0:T(8,128)(2,1)} %slice_bitcast_fusion), channel_id=1, source_target_pairs={{4,0},{8,4},{12,8},{14,12},{10,14},{6,10},{2,6},{0,2},{5,1},{9,5},... | collective-permute-start | bytes 614408 | tf_op jit(solution)/shard_map/ppermute | solution.py:262
  56.3 8.3 %collective-permute-start.10 = (bf16[1,160,640]{2,1,0:T(8,128)(2,1)S(1)}, bf16[1,160,640]{2,1,0:T(8,128)(2,1)S(1)}, u32[]{:S(2)}, u32[]{:S(2)}) collective-permute-start(bf16[1,160,640]{2,1,0:T(8,128)(2,1)S(1)} %shard_map.83), channel_id=1, source_target_pairs={{4,0},{8,4},{12,8},{14,12},{10,14},{6,10},{2,6},{0,2},{5,1},{9,5},... | collective-permute-start | bytes 614408 | tf_op jit(solution)/shard_map/ppermute | solution.py:305
  60.4 7.0 %collective-permute-start.11 = (bf16[1,160,640]{2,1,0:T(8,128)(2,1)S(1)}, bf16[1,160,640]{2,1,0:T(8,128)(2,1)S(1)}, u32[]{:S(2)}, u32[]{:S(2)}) collective-permute-start(bf16[1,160,640]{2,1,0:T(8,128)(2,1)S(1)} %shard_map.81.refs_4_), channel_id=1, source_target_pairs={{0,4},{4,8},{8,12},{12,14},{14,10},{10,6},{6,2},{2,0},{1,5},{5,9},... | collective-permute-start | bytes 614408 | tf_op jit(solution)/shard_map/ppermute | solution.py:305
  68.1 18.8 %collective-permute-start.12 = (bf16[2,384,640]{2,1,0:T(8,128)(2,1)}, bf16[2,384,640]{2,1,0:T(8,128)(2,1)S(1)}, u32[]{:S(2)}, u32[]{:S(2)}) collective-permute-start(bf16[2,384,640]{2,1,0:T(8,128)(2,1)} %shard_map.85), channel_id=1, source_target_pairs={{0,1},{1,0},{2,3},{3,2},{4,5},{5,4},{6,7},{7,6},{8,9},{9,8},{10,11... | collective-permute-start | bytes 2949128 | tf_op jit(solution)/shard_map/ppermute | solution.py:315
  68.1 12.1 %collective-permute-start.14 = (bf16[2,160,640]{2,1,0:T(8,128)(2,1)}, bf16[2,160,640]{2,1,0:T(8,128)(2,1)S(1)}, u32[]{:S(2)}, u32[]{:S(2)}) collective-permute-start(bf16[2,160,640]{2,1,0:T(8,128)(2,1)} %copy-done.10), channel_id=1, source_target_pairs={{4,0},{8,4},{12,8},{14,12},{10,14},{6,10},{2,6},{0,2},{5,1},{9,5},... | collective-permute-start | bytes 1228808 | tf_op jit(solution)/shard_map/ppermute | solution.py:305
  73.4 11.7 %collective-permute-start.13 = (bf16[2,160,640]{2,1,0:T(8,128)(2,1)S(1)}, bf16[2,160,640]{2,1,0:T(8,128)(2,1)S(1)}, u32[]{:S(2)}, u32[]{:S(2)}) collective-permute-start(bf16[2,160,640]{2,1,0:T(8,128)(2,1)S(1)} %shard_map.86.refs_4_), channel_id=1, source_target_pairs={{0,4},{4,8},{8,12},{12,14},{14,10},{10,6},{6,2},{2,0},{1,5},{5,9},... | collective-permute-start | bytes 1228808 | tf_op jit(solution)/shard_map/ppermute | solution.py:305
  80.8 6.1 %copy-start.6 = (f32[2,384,640]{2,1,0:T(8,128)S(1)}, f32[2,384,640]{2,1,0:T(8,128)}, u32[]{:S(2)}) copy-start(f32[2,384,640]{2,1,0:T(8,128)} %copy-done.5) | copy-start | bytes 5898244
  80.8 11.1 %collective-permute-start.16 = (bf16[2,160,640]{2,1,0:T(8,128)(2,1)S(1)}, bf16[2,160,640]{2,1,0:T(8,128)(2,1)S(1)}, u32[]{:S(2)}, u32[]{:S(2)}) collective-permute-start(bf16[2,160,640]{2,1,0:T(8,128)(2,1)S(1)} %shard_map.87.refs_4_), channel_id=1, source_target_pairs={{4,0},{8,4},{12,8},{14,12},{10,14},{6,10},{2,6},{0,2},{5,1},{9,5},... | collective-permute-start | bytes 1228808 | tf_op jit(solution)/shard_map/ppermute | solution.py:305
  85.7 10.8 %collective-permute-start.18 = (bf16[2,160,640]{2,1,0:T(8,128)(2,1)S(1)}, bf16[2,160,640]{2,1,0:T(8,128)(2,1)S(1)}, u32[]{:S(2)}, u32[]{:S(2)}) collective-permute-start(bf16[2,160,640]{2,1,0:T(8,128)(2,1)S(1)} %shard_map.88.refs_3_), channel_id=1, source_target_pairs={{0,4},{4,8},{8,12},{12,14},{14,10},{10,6},{6,2},{2,0},{1,5},{5,9},... | collective-permute-start | bytes 1228808 | tf_op jit(solution)/shard_map/ppermute | solution.py:305
  87.6 19.5 %collective-permute-start.15 = (bf16[384,640]{1,0:T(8,128)(2,1)S(1)}, bf16[384,640]{1,0:T(8,128)(2,1)S(1)}, u32[]{:S(2)}, u32[]{:S(2)}) collective-permute-start(bf16[384,640]{1,0:T(8,128)(2,1)S(1)} %shard_map.89.refs_4_), channel_id=1, source_target_pairs={{0,16},{16,0},{1,17},{17,1},{2,18},{18,2},{3,19},{19,3},{4,20},{20... | collective-permute-start | bytes 1474568 | tf_op jit(solution)/shard_map/ppermute | solution.py:320
  92.6 10.3 %collective-permute-start.17 = (bf16[2,160,640]{2,1,0:T(8,128)(2,1)S(1)}, bf16[2,160,640]{2,1,0:T(8,128)(2,1)S(1)}, u32[]{:S(2)}, u32[]{:S(2)}) collective-permute-start(bf16[2,160,640]{2,1,0:T(8,128)(2,1)S(1)} %shard_map.90.refs_4_), channel_id=1, source_target_pairs={{4,0},{8,4},{12,8},{14,12},{10,14},{6,10},{2,6},{0,2},{5,1},{9,5},... | collective-permute-start | bytes 1228808 | tf_op jit(solution)/shard_map/ppermute | solution.py:305
  97.2 9.9 %collective-permute-start.19 = (bf16[2,160,640]{2,1,0:T(8,128)(2,1)S(1)}, bf16[2,160,640]{2,1,0:T(8,128)(2,1)S(1)}, u32[]{:S(2)}, u32[]{:S(2)}) collective-permute-start(bf16[2,160,640]{2,1,0:T(8,128)(2,1)S(1)} %shard_map.92), channel_id=1, source_target_pairs={{0,4},{4,8},{8,12},{12,14},{14,10},{10,6},{6,2},{2,0},{1,5},{5,9},... | collective-permute-start | bytes 1228808 | tf_op jit(solution)/shard_map/ppermute | solution.py:305
  107.2 6.0 %collective-permute-start.21 = (bf16[160,640]{1,0:T(8,128)(2,1)S(1)}, bf16[160,640]{1,0:T(8,128)(2,1)S(1)}, u32[]{:S(2)}, u32[]{:S(2)}) collective-permute-start(bf16[160,640]{1,0:T(8,128)(2,1)S(1)} %get-tuple-element.50.refs_7_), channel_id=1, source_target_pairs={{0,16},{16,0},{1,17},{17,1},{2,18},{18,2},{3,19},{19,3},{4,20},{20... | collective-permute-start | bytes 614408 | tf_op jit(solution)/shard_map/ppermute | solution.py:334
  109.8 1.5 %collective-permute-start.20 = (f32[384,2]{1,0:T(8,128)S(1)}, f32[384,2]{1,0:T(8,128)S(1)}, u32[]{:S(2)}, u32[]{:S(2)}) collective-permute-start(f32[384,2]{1,0:T(8,128)S(1)} %get-tuple-element.52.sums), channel_id=1, source_target_pairs={{0,1},{1,0},{2,3},{3,2},{4,5},{5,4},{6,7},{7,6},{8,9},{9,8},{10,11... | collective-permute-start | bytes 9224 | tf_op jit(solution)/shard_map/ppermute | solution.py:346
  (32 other events, 62.7 us)

commit v8 on v7

--- a/solution.py
+++ b/solution.py
@@ -9,6 +9,7 @@
 
 BF16, F32 = jnp.bfloat16, jnp.float32
 VMEM = pl.BlockSpec(memory_space=pltpu.VMEM)
+HBM = pl.BlockSpec(memory_space=pltpu.HBM)
 ANY = pl.BlockSpec(memory_space=pl.ANY)
 SMEM = pl.BlockSpec(memory_space=pltpu.SMEM)
 
@@ -17,24 +18,25 @@
     return jax.ShapeDtypeStruct(dims, kind)
 
 
-def call(kernel, ins, out_shape, scratch=(), vmem=4, left=(), cost=1, ties=()):
+def call(kernel, ins, out_shape, scratch=(), vmem=16, flops=1, pinned=(), ties=()):
     count = len(ins)
 
     def body(*refs):
         kernel(*refs[:count], *refs[count + len(ties) :])
 
+    moved = sum(x.size * x.dtype.itemsize for x in list(ins) + jax.tree.leaves(out_shape))
     return pl.pallas_call(
         body if ties else kernel,
         out_shape=out_shape,
         in_specs=[
-            SMEM if x.dtype == jnp.int32 else ANY if i in left else VMEM
+            SMEM if x.dtype == jnp.int32 else HBM if i in pinned else VMEM
             for i, x in enumerate(ins)
         ]
         + [ANY] * len(ties),
         out_specs=jax.tree.map(lambda _: VMEM, out_shape),
         scratch_shapes=list(scratch),
         compiler_params=pltpu.CompilerParams(vmem_limit_bytes=vmem << 20),
-        cost_estimate=pl.CostEstimate(flops=1, bytes_accessed=cost, transcendentals=0),
+        cost_estimate=pl.CostEstimate(flops=flops, bytes_accessed=moved, transcendentals=0),
     )(*ins, *ties)
 
 
@@ -89,12 +91,12 @@
 
 def place_kernel(index, *refs):
     blocks, (up, down, sems) = refs[:-3], refs[-3:]
-    depth = blocks[0].shape[1]
+    depth = blocks[0].shape[0]
     copies = []
     for i, block in enumerate(blocks):
-        rows = pl.ds(pl.multiple_of(index[i] * depth, depth), depth)
-        copies.append(pltpu.make_async_copy(block.at[0], up.at[rows], sems.at[2 * i]))
-        copies.append(pltpu.make_async_copy(block.at[1], down.at[rows], sems.at[2 * i + 1]))
+        rows = pl.ds(pl.multiple_of(index[i // 2] * depth, depth), depth)
+        target = (up, down)[i % 2].at[rows]
+        copies.append(pltpu.make_async_copy(block, target, sems.at[i]))
     for copy in copies:
         copy.start()
     for copy in copies:
@@ -167,28 +169,22 @@
     out[...] = (own_columns(meta, grads, width).astype(F32) + value).astype(BF16)
 
 
-def hop_kernel(at, mode, index, *refs):
-    windows = [i for i in range(2) if mode[i] is not None]
-    partial, came, out = refs[: len(windows)], refs[len(windows) : -1], refs[-1]
-    depth = out.shape[1]
-    rows = pl.ds(pl.multiple_of(index[at] * depth, depth), depth)
-    for k, i in enumerate(windows):
-        value = partial[k][rows, :]
-        if mode[i]:
-            value = value + came[0][k if came[0].shape[0] == 2 else 0].astype(F32)
-        out[k] = value.astype(BF16)
-
-
-def own_total_kernel(index, own, other, down, total):
-    depth = total.shape[1]
+def hop_kernel(places, index, partial, *refs):
+    outs = refs[len(refs) - len(places) :]
+    came = iter(refs)
+    depth = outs[0].shape[0]
+    for (at, summed), out in zip(places, outs):
+        value = partial[pl.ds(pl.multiple_of(index[at] * depth, depth), depth), :]
+        if summed:
+            value = value + next(came)[...].astype(F32)
+        out[...] = value.astype(BF16)
+
+
+def total_kernel(index, partial, up, down, total):
+    depth = total.shape[0]
     rows = pl.ds(pl.multiple_of(index[0] * depth, depth), depth)
-    total[0] = own[rows, :] + down[0].astype(F32)
-    total[1] = other[rows, :] + down[1].astype(F32)
-
-
-def total_kernel(both, up, total, passing):
-    total[...] = both[0] + up[0].astype(F32)
-    passing[...] = (both[1] + up[1].astype(F32)).astype(BF16)
+    value = partial[rows, :] + up[...].astype(F32) + down[...].astype(F32)
+    total[...] = value.astype(total.dtype)
 
 
 def join_kernel(meta, own, passed, out):
@@ -224,10 +220,8 @@
     swap = [(0, 1), (1, 0)]
     after = lax.optimization_barrier
 
-    pair = jnp.stack(
-        [lax.dynamic_slice_in_dim(w, side * quarter, quarter, 1) for w in (w_up, w_down)]
-    )
-    pair, frames, out_grad, ln_gain, lengths = after((pair, frames, out_grad, ln_gain, lengths))
+    mine = [lax.dynamic_slice_in_dim(w, side * quarter, quarter, 1) for w in (w_up, w_down)]
+    mine, frames, out_grad, ln_gain, lengths = after((mine, frames, out_grad, ln_gain, lengths))
     meta = jnp.stack([own, core, side]).astype(jnp.int32)
     frames, out_grad = frames[0], out_grad[0]
 
@@ -236,33 +230,37 @@
         norm_kernel,
         (meta, lengths, frames, out_grad, ln_gain),
         (rows_of, rows_of, shape((2, half_rows, width), BF16), shape((frame_len, 2), F32)),
-        cost=10 * frame_len * width,
+        flops=10 * frame_len * width,
     )
 
     weight = shape((width, quarter), BF16)
     block_of = shape((depth, quarter), BF16)
     if ringed:
-        blocks = {0: pair}
-        up, down = pair, pair
+        blocks = {0: list(mine)}
+        up, down = list(mine), list(mine)
         for step in range(1, half):
-            up, down = lax.ppermute(up, "gx", ahead), lax.ppermute(down, "gx", behind)
+            up = [lax.ppermute(block, "gx", ahead) for block in up]
+            down = [lax.ppermute(block, "gx", behind) for block in down]
             blocks[-step], blocks[step] = up, down
+            if step == 1:
+                passing = hold(passing, up[0], down[0])
         first = lax.ppermute(passing, "groups", swap)
         first, up, down = after((first, up, down))
         steps = list(blocks) + [half]
         index = jnp.stack([ring_member(place + step + peers, peers) for step in steps])
         index = index.astype(jnp.int32)
+        blocks = [block for step in blocks for block in blocks[step]]
         near = call(
             place_kernel,
-            (index, *blocks.values()),
+            (index, *blocks),
             (weight, weight),
-            [pltpu.SemaphoreType.DMA((2 * len(blocks),))],
-            left=range(1, len(blocks) + 1),
+            [pltpu.SemaphoreType.DMA((len(blocks),))],
+            pinned=range(1, len(blocks) + 1),
         )
         far = [lax.ppermute(up[0], "gx", ahead), lax.ppermute(down[1], "gx", behind)]
     else:
         first = lax.ppermute(passing, "groups", swap)
-        near = [lax.all_gather(block, "gx", axis=0, tiled=True) for block in (pair[0], pair[1])]
+        near = [lax.all_gather(block, "gx", axis=0, tiled=True) for block in mine]
         index, far = jnp.zeros((1,), jnp.int32), []
     second = lax.ppermute(first, "gy", swap)
 
@@ -272,10 +270,11 @@
         (index, first, second, *near, *far),
         (d_pre_of, partial_of, weight, weight),
         [pltpu.VMEM((frame_len, width), BF16)] * 2,
-        vmem=10,
+        flops=6 * frame_len * width * quarter,
     )
     d_pre_own, partial_own = call(
-        own_kernel, (normed, grads, full_up, full_down), (d_pre_of, partial_of), vmem=10
+        own_kernel, (normed, grads, full_up, full_down), (d_pre_of, partial_of),
+        flops=6 * frame_len * width * quarter,
     )
     partial = [partial_own, partial_other]
 
@@ -286,7 +285,7 @@
             d_norm_kernel,
             (meta, d_pre_own, d_pre_other, full_up),
             (shape((2, frame_len, half_width), F32), shape((2, frame_len, half_width), BF16)),
-            vmem=10,
+            flops=4 * frame_len * width * quarter,
             ties=ties,
         )
 
@@ -297,31 +296,41 @@
         place_of = {step: i for i, step in enumerate(steps)}
         place_of[-half] = place_of[half]
 
-        def hop(step, mode, *given, ties=()):
-            sums = [partial[i] for i in range(2) if mode[i] is not None]
-            kernel = functools.partial(hop_kernel, place_of[step], mode)
-            out = shape((len(sums), depth, quarter), BF16)
-            block = call(kernel, (index, *sums, *given), out, ties=ties)
-            return block, lax.ppermute(block, "gx", ahead if step > 0 else behind)
-
-        _, down = hop(-half, (None, 0))
-        tie, up = hop(half, (0, None))
+        came = [{}, {}]
+
+        def hop(i, turn, *ties):
+            ways = [(half - turn - (i == 1), ahead), (turn + (i == 0) - half, behind)]
+            ways = [way for way in ways if way[0] != 0]
+            kept = [came[i][pairs[0]] for _, pairs in ways if pairs[0] in came[i]]
+            places = [(place_of[step], pairs[0] in came[i]) for step, pairs in ways]
+            blocks = call(
+                functools.partial(hop_kernel, tuple(places)),
+                (index, partial[i], *kept),
+                [block_of] * len(ways),
+                ties=ties,
+            )
+            for block, (_, pairs) in zip(blocks, ways):
+                came[i][pairs[0]] = lax.ppermute(block, "gx", pairs)
+            return blocks[0]
+
+        hop(1, 0)
+        tie = hop(0, 0)
+        tie = hop(1, 1, tie)
         keep, send = own_d_norm(tie)
-        for step in range(half - 1, 0, -1):
-            farthest = step == half - 1
-            tie, down = hop(-step, (0, 1) if farthest else (1, 1), down, ties=(tie,))
-            if farthest:
-                send = hold(send, tie, up)
-                came = lax.ppermute(send, "gy", swap)
-            tie, up = hop(step, (1, 0) if farthest else (1, 1), up, ties=(tie,))
-            if step == half - 2:
-                over = over_cores(keep, came, tie)
-                tie = over
-                back = lax.ppermute(over, "groups", swap)
-        both = call(own_total_kernel, (index, *partial, down), shape((2, depth, quarter), F32))
-        total, passing = call(
-            total_kernel, (both, up), (shape((depth, quarter), F32), block_of), ties=(back,)
-        )
+        tie = hop(0, 1, send)
+        send = hold(send, tie, *came[1].values())
+        over_cores_came = lax.ppermute(send, "gy", swap)
+        tie = hop(1, 2, tie)
+        tie = hop(0, 2, tie)
+        over = over_cores(keep, over_cores_came, tie)
+        back = lax.ppermute(over, "groups", swap)
+        tie = over
+        for turn in range(3, half):
+            tie = hop(0, turn, hop(1, turn, tie))
+        one, two = ([came[i][pairs[0]] for pairs in (ahead, behind)] for i in range(2))
+        passing = call(total_kernel, (index, partial[1], *two), block_of, ties=(tie,))
+        total = call(total_kernel, (index, partial[0], *one), shape((depth, quarter), F32))
+        came = over_cores_came
         tail = (passing,)
     else:
         keep, send = own_d_norm()

time: 115 us -> 107 us (0.930)
  waiting for transfers between devices: 41.9 us -> 22.1 us
  starting transfers between devices: 23.1 us -> 37.8 us
  local copies, waits for them, and re-layouts: 22.9 us -> 17.8 us
  Pallas kernels: 25.7 us -> 27.4 us
    ppermute x15 -> x27, starting transfers between devices: 16 us -> 31.6 us  [the longest x14 17.1 us: hop(): came[i][pairs[0]] = lax.ppermute(block, 'gx', pairs)]
    ppermute x15 -> x27, waiting for transfers between devices: 35.2 us -> 19.7 us  [the longest x6 8.88 us: shards(): up = [lax.ppermute(block, 'gx', ahead) for block in up]]
    ppermute x1, waiting for transfers between devices: 5.17 us -> 0.01 us  [shards(): first = lax.ppermute(passing, 'groups', swap)]
    unnamed x68 -> x58, local copies, waits for them, and re-layouts: 20.2 us -> 16.6 us
    ppermute x1, waiting for transfers between devices: 0.01 us -> 2.42 us  [shards(): passed = lax.ppermute(passing, 'groups', swap)]
    pallas_call x19, Pallas kernels: 25.7 us -> 27.4 us  [call(): pl.pallas_call(body if ties else kernel, out_shape=out_shape, in_specs=[S...]
    ppermute x1, waiting for transfers between devices: 1.43 us -> 0.01 us  [shards(): lax.ppermute(sums, 'gy', swap)]
    squeeze x2 -> x0, local copies, waits for them, and re-layouts: 1.39 us -> none  [the longest x1 0.7 us: shards(): down[1]]
  transfers between devices with their start and end apart: 22 -> 34, of which waited for: 13 -> 12; matrix products, arithmetic and copies ran while one was open for 1% -> 0% of each run, Pallas kernels for 17% -> 19%
where the time goes in v8:
time: 107 us; the launch traced here: 106 us
  starting transfers between devices  37.8 us (35%)
  Pallas kernels  27.4 us (26%)
  waiting for transfers between devices  22.1 us (21%)
  local copies, waits for them, and re-layouts  17.8 us (17%)
    pallas_call x19, Pallas kernels, call(): pl.pallas_call(body if ties else kernel, out_shape=out_shape, in_specs=[S...  27.4 us
    ppermute x14, starting transfers between devices, hop(): came[i][pairs[0]] = lax.ppermute(block, 'gx', pairs)  17.1 us
    unnamed x58, local copies, waits for them, and re-layouts  16.6 us
    ppermute x6, waiting for transfers between devices, shards(): up = [lax.ppermute(block, 'gx', ahead) for block in up]  8.88 us
    ppermute x6, starting transfers between devices, shards(): down = [lax.ppermute(block, 'gx', behind) for block in down]  7.8 us
    ppermute x6, starting transfers between devices, shards(): up = [lax.ppermute(block, 'gx', ahead) for block in up]  6.67 us
    ppermute x14, waiting for transfers between devices, hop(): came[i][pairs[0]] = lax.ppermute(block, 'gx', pairs)  6.26 us
    ppermute x6, waiting for transfers between devices, shards(): down = [lax.ppermute(block, 'gx', behind) for block in down]  4.5 us
  transfers between devices with their start and end apart: 34, of which 12 were waited for; matrix products, arithmetic and copies ran while one was open for 0% of the time, Pallas kernels for 19%

profile of v8, /device:TPU:0, one launch (start us, length us, event | category | flops | bytes accessed | tf_op | source)
XLA Modules:
  0.0 106.1 jit_solution(6525333246759337207)
XLA Ops:
  1.7 3.1 %collective-permute-start = (bf16[160,640]{1,0:T(8,128)(2,1)S(1)}, bf16[160,640]{1,0:T(8,128)(2,1)S(1)}, u32[]{:S(2)}, u32[]{:S(2)}) collective-permute-start(bf16[160,640]{1,0:T(8,128)(2,1)S(1)} %get-tuple-element.46.refs_0_), channel_id=1, source_target_pairs={{0,4},{4,8},{8,12},{12,14},{14,10},{10,6},{6,2},{2,0},{1,5},{5,9},... | collective-permute-start | bytes 614408 | tf_op jit(solution)/shard_map/ppermute | solution.py:242
  8.6 1.6 %shard_map.77 = (bf16[384,1280]{1,0:T(8,128)(2,1)S(1)}, bf16[384,1280]{1,0:T(8,128)(2,1)S(1)}, bf16[2,192,1280]{2,1,0:T(8,128)(2,1)S(1)}, f32[384,2]{1,0:T(8,128)S(1)}) custom-call(s32[3]{0:T(128)S(1)} %pad_add_fusion.meta.refs_0_, s32[8]{0:T(128)S(1)} %copy-done.25, bf16[384,1280]{1,0:T(8,128)(2,1)S(1)} %bitcast.14, bf16[384,1280]{1,0:T(8,128)(2,1)S(1)} %bitcast.17, ...), custom_call_target="tpu_custom_call" | custom-call | flops 4915200 | bytes 4923436 | tf_op jit(solution)/shard_map/pallas_call | solution.py:28
  14.6 1.9 %collective-permute-start.2 = (bf16[2,192,1280]{2,1,0:T(8,128)(2,1)}, bf16[2,192,1280]{2,1,0:T(8,128)(2,1)S(1)}, u32[]{:S(2)}, u32[]{:S(2)}) collective-permute-start(bf16[2,192,1280]{2,1,0:T(8,128)(2,1)} %shard_map.78), channel_id=1, source_target_pairs={{0,16},{16,0},{1,17},{17,1},{2,18},{18,2},{3,19},{19,3},{4,20},{20... | collective-permute-start | bytes 2949128 | tf_op jit(solution)/shard_map/ppermute | solution.py:247
  18.5 1.6 %collective-permute-start.3 = (bf16[160,640]{1,0:T(8,128)(2,1)}, bf16[160,640]{1,0:T(8,128)(2,1)S(1)}, u32[]{:S(2)}, u32[]{:S(2)}) collective-permute-start(bf16[160,640]{1,0:T(8,128)(2,1)} %copy-done.13), channel_id=1, source_target_pairs={{0,4},{4,8},{8,12},{12,14},{14,10},{10,6},{6,2},{2,0},{1,5},{5,9},... | collective-permute-start | bytes 614408 | tf_op jit(solution)/shard_map/ppermute | solution.py:242
  20.6 3.3 %collective-permute-done.10.refs_5_ = bf16[160,640]{1,0:T(8,128)(2,1)S(1)} collective-permute-done((bf16[160,640]{1,0:T(8,128)(2,1)S(1)}, bf16[160,640]{1,0:T(8,128)(2,1)S(1)}, u32[]{:S(2)}, u32[]{:S(2)}) %collective-permute-start.10) | collective-permute-done | bytes 204832 | tf_op jit(solution)/shard_map/ppermute | solution.py:243
  23.9 2.2 %collective-permute-start.11 = (bf16[160,640]{1,0:T(8,128)(2,1)S(1)}, bf16[160,640]{1,0:T(8,128)(2,1)S(1)}, u32[]{:S(2)}, u32[]{:S(2)}) collective-permute-start(bf16[160,640]{1,0:T(8,128)(2,1)S(1)} %collective-permute-done.10.refs_5_), channel_id=1, source_target_pairs={{4,0},{8,4},{12,8},{14,12},{10,14},{6,10},{2,6},{0,2},{5,1},{9,5},... | collective-permute-start | bytes 614408 | tf_op jit(solution)/shard_map/ppermute | solution.py:243
  26.6 3.9 %collective-permute-done.3.refs_6_ = bf16[160,640]{1,0:T(8,128)(2,1)S(1)} collective-permute-done((bf16[160,640]{1,0:T(8,128)(2,1)}, bf16[160,640]{1,0:T(8,128)(2,1)S(1)}, u32[]{:S(2)}, u32[]{:S(2)}) %collective-permute-start.3) | collective-permute-done | bytes 204832 | tf_op jit(solution)/shard_map/ppermute | solution.py:242
  32.7 2.1 %collective-permute-start.12 = (bf16[160,640]{1,0:T(8,128)(2,1)S(1)}, bf16[160,640]{1,0:T(8,128)(2,1)S(1)}, u32[]{:S(2)}, u32[]{:S(2)}) collective-permute-start(bf16[160,640]{1,0:T(8,128)(2,1)S(1)} %collective-permute-done.11.refs_9_), channel_id=1, source_target_pairs={{4,0},{8,4},{12,8},{14,12},{10,14},{6,10},{2,6},{0,2},{5,1},{9,5},... | collective-permute-start | bytes 614408 | tf_op jit(solution)/shard_map/ppermute | solution.py:243
  35.3 3.8 %collective-permute-done.4.refs_10_ = bf16[160,640]{1,0:T(8,128)(2,1)S(1)} collective-permute-done((bf16[160,640]{1,0:T(8,128)(2,1)S(1)}, bf16[160,640]{1,0:T(8,128)(2,1)S(1)}, u32[]{:S(2)}, u32[]{:S(2)}) %collective-permute-start.4) | collective-permute-done | bytes 204832 | tf_op jit(solution)/shard_map/ppermute | solution.py:242
  45.3 4.8 %shard_map.79 = (bf16[1280,640]{1,0:T(8,128)(2,1)S(1)}, bf16[1280,640]{1,0:T(8,128)(2,1)S(1)}) custom-call(s32[8]{0:T(128)S(1)} %stack.51.index.refs_0_, bf16[160,640]{1,0:T(8,128)(2,1)S(1)} %get-tuple-element.46.refs_0_, bf16[160,640]{1,0:T(8,128)(2,1)S(1)} %get-tuple-element.47.refs_1_, bf16[160,640]{1,0:T(8,128)(2,1)S(1)} %copy-done.14, ...), custom_call_target="tpu_custom_call" | custom-call | flops 1 | bytes 6144032 | tf_op jit(solution)/shard_map/pallas_call | solution.py:28
  50.1 4.2 %shard_map.80 = (bf16[384,640]{1,0:T(8,128)(2,1)S(1)}, f32[1280,640]{1,0:T(8,128)S(1)}, bf16[1280,640]{1,0:T(8,128)(2,1)S(1)}, bf16[1280,640]{1,0:T(8,128)(2,1)S(1)}) custom-call(s32[8]{0:T(128)S(1)} %stack.51.index.refs_0_, bf16[2,192,1280]{2,1,0:T(8,128)(2,1)S(1)} %collective-permute-done.2.first, bf16[2,192,1280]{2,1,0:T(8,128)(2,1)} %collective-permute-done.13.second, ...), custom_call_target="tpu_custom_call" | custom-call | flops 1887436800 | bytes 12697632 | tf_op jit(solution)/shard_map/pallas_call | solution.py:28
  57.1 2.7 %shard_map.81 = (bf16[384,640]{1,0:T(8,128)(2,1)S(1)}, f32[1280,640]{1,0:T(8,128)S(1)}) custom-call(bf16[384,1280]{1,0:T(8,128)(2,1)S(1)} %copy-done.27, bf16[384,1280]{1,0:T(8,128)(2,1)S(1)} %copy-done.11, bf16[1280,640]{1,0:T(8,128)(2,1)S(1)} %get-tuple-element.53.up.refs_3_, bf16[1280,640]{1,0:T(8,128)(2,1)S(1)} %get-tuple-element.54.down), custom_call_target="tpu_custom_call" | custom-call | flops 1887436800 | bytes 9011200 | tf_op jit(solution)/shard_map/pallas_call | solution.py:28
  65.1 2.5 %shard_map.85 = (f32[2,384,640]{2,1,0:T(8,128)S(1)}, bf16[2,384,640]{2,1,0:T(8,128)(2,1)S(1)}) custom-call(s32[3]{0:T(128)S(1)} %pad_add_fusion.meta.refs_0_, bf16[384,640]{1,0:T(8,128)(2,1)S(1)} %get-tuple-element.55.refs_1_, bf16[384,640]{1,0:T(8,128)(2,1)S(1)} %get-tuple-element.56.refs_2_, bf16[1280,640]{1,0:T(8,128)(2,1)S(1)} %get-tuple-element.53.up.refs_3_, ...), custom_call_target="tpu_custom_call" | custom-call | flops 1258291200 | bytes 5570572 | tf_op jit(solution)/shard_map/pallas_call | solution.py:28
  69.9 1.8 %collective-permute-done.20.refs_2_ = bf16[160,640]{1,0:T(8,128)(2,1)S(1)} collective-permute-done((bf16[160,640]{1,0:T(8,128)(2,1)S(1)}, bf16[160,640]{1,0:T(8,128)(2,1)S(1)}, u32[]{:S(2)}, u32[]{:S(2)}) %collective-permute-start.20) | collective-permute-done | bytes 204832 | tf_op jit(solution)/shard_map/ppermute | solution.py:313
  74.4 1.9 %copy-done.1 = f32[1280,640]{1,0:T(8,128)S(1)} copy-done((f32[1280,640]{1,0:T(8,128)S(1)}, f32[1280,640]{1,0:T(8,128)}, u32[]{:S(2)}) %copy-start.1) | copy-done | bytes 3276824
  79.2 1.6 %collective-permute-start.27 = (bf16[160,640]{1,0:T(8,128)(2,1)S(1)}, bf16[160,640]{1,0:T(8,128)(2,1)S(1)}, u32[]{:S(2)}, u32[]{:S(2)}) collective-permute-start(bf16[160,640]{1,0:T(8,128)(2,1)S(1)} %get-tuple-element.72), channel_id=1, source_target_pairs={{4,0},{8,4},{12,8},{14,12},{10,14},{6,10},{2,6},{0,2},{5,1},{9,5},... | collective-permute-start | bytes 614408 | tf_op jit(solution)/shard_map/ppermute | solution.py:313
  83.8 1.6 %collective-permute-start.29 = (bf16[160,640]{1,0:T(8,128)(2,1)S(1)}, bf16[160,640]{1,0:T(8,128)(2,1)S(1)}, u32[]{:S(2)}, u32[]{:S(2)}) collective-permute-start(bf16[160,640]{1,0:T(8,128)(2,1)S(1)} %get-tuple-element.70.refs_3_), channel_id=1, source_target_pairs={{0,4},{4,8},{8,12},{12,14},{14,10},{10,6},{6,2},{2,0},{1,5},{5,9},... | collective-permute-start | bytes 614408 | tf_op jit(solution)/shard_map/ppermute | solution.py:313
  85.4 1.6 %collective-permute-start.26 = (bf16[160,640]{1,0:T(8,128)(2,1)S(1)}, bf16[160,640]{1,0:T(8,128)(2,1)S(1)}, u32[]{:S(2)}, u32[]{:S(2)}) collective-permute-start(bf16[160,640]{1,0:T(8,128)(2,1)S(1)} %get-tuple-element.69.refs_4_), channel_id=1, source_target_pairs={{0,4},{4,8},{8,12},{12,14},{14,10},{10,6},{6,2},{2,0},{1,5},{5,9},... | collective-permute-start | bytes 614408 | tf_op jit(solution)/shard_map/ppermute | solution.py:313
  88.4 1.6 %collective-permute-start.32 = (bf16[160,640]{1,0:T(8,128)(2,1)S(1)}, bf16[160,640]{1,0:T(8,128)(2,1)S(1)}, u32[]{:S(2)}, u32[]{:S(2)}) collective-permute-start(bf16[160,640]{1,0:T(8,128)(2,1)S(1)} %get-tuple-element.75), channel_id=1, source_target_pairs={{4,0},{8,4},{12,8},{14,12},{10,14},{6,10},{2,6},{0,2},{5,1},{9,5},... | collective-permute-start | bytes 614408 | tf_op jit(solution)/shard_map/ppermute | solution.py:313
  90.0 1.8 %collective-permute-done.29.refs_2_ = bf16[160,640]{1,0:T(8,128)(2,1)S(1)} collective-permute-done((bf16[160,640]{1,0:T(8,128)(2,1)S(1)}, bf16[160,640]{1,0:T(8,128)(2,1)S(1)}, u32[]{:S(2)}, u32[]{:S(2)}) %collective-permute-start.29) | collective-permute-done | bytes 204832 | tf_op jit(solution)/shard_map/ppermute | solution.py:313
  92.4 1.6 %collective-permute-start.31 = (bf16[160,640]{1,0:T(8,128)(2,1)S(1)}, bf16[160,640]{1,0:T(8,128)(2,1)S(1)}, u32[]{:S(2)}, u32[]{:S(2)}) collective-permute-start(bf16[160,640]{1,0:T(8,128)(2,1)S(1)} %shard_map.92.refs_4_), channel_id=1, source_target_pairs={{0,4},{4,8},{8,12},{12,14},{14,10},{10,6},{6,2},{2,0},{1,5},{5,9},... | collective-permute-start | bytes 614408 | tf_op jit(solution)/shard_map/ppermute | solution.py:313
  94.1 2.1 %collective-permute-done.26.refs_2_ = bf16[160,640]{1,0:T(8,128)(2,1)S(1)} collective-permute-done((bf16[160,640]{1,0:T(8,128)(2,1)S(1)}, bf16[160,640]{1,0:T(8,128)(2,1)S(1)}, u32[]{:S(2)}, u32[]{:S(2)}) %collective-permute-start.26) | collective-permute-done | bytes 204832 | tf_op jit(solution)/shard_map/ppermute | solution.py:313
  100.2 2.4 %collective-permute-done.33.passed = bf16[160,640]{1,0:T(8,128)(2,1)S(1)} collective-permute-done((bf16[160,640]{1,0:T(8,128)(2,1)S(1)}, bf16[160,640]{1,0:T(8,128)(2,1)S(1)}, u32[]{:S(2)}, u32[]{:S(2)}) %collective-permute-start.33) | collective-permute-done | bytes 204832 | tf_op jit(solution)/shard_map/ppermute | solution.py:343
  104.2 1.9 %shard_map.95 = bf16[384,640]{1,0:T(8,128)(2,1)} custom-call(s32[3]{0:T(128)S(1)} %pad_add_fusion.meta.refs_0_, f32[384,640]{1,0:T(8,128)S(1)} %get-tuple-element.73.scaled, f32[384,2]{1,0:T(8,128)S(1)} %get-tuple-element.74.sums, f32[384,2]{1,0:T(8,128)S(1)} %collective-permute-done.30.came, bf16[384,1280]{1,0:T(8,128)(2,1)S(1)} %bitcast.16, ...), custom_call_target="tpu_custom_call" | custom-call | flops 1 | bytes 3449868 | tf_op jit(solution)/shard_map/pallas_call | solution.py:28
  (127 shorter events, 47.5 us)
Async XLA Ops:
  1.7 12.1 %collective-permute-start = (bf16[160,640]{1,0:T(8,128)(2,1)S(1)}, bf16[160,640]{1,0:T(8,128)(2,1)S(1)}, u32[]{:S(2)}, u32[]{:S(2)}) collective-permute-start(bf16[160,640]{1,0:T(8,128)(2,1)S(1)} %get-tuple-element.46.refs_0_), channel_id=1, source_target_pairs={{0,4},{4,8},{8,12},{12,14},{14,10},{10,6},{6,2},{2,0},{1,5},{5,9},... | collective-permute-start | bytes 614408 | tf_op jit(solution)/shard_map/ppermute | solution.py:242
  4.8 9.1 %collective-permute-start.1 = (bf16[160,640]{1,0:T(8,128)(2,1)S(1)}, bf16[160,640]{1,0:T(8,128)(2,1)S(1)}, u32[]{:S(2)}, u32[]{:S(2)}) collective-permute-start(bf16[160,640]{1,0:T(8,128)(2,1)S(1)} %get-tuple-element.46.refs_0_), channel_id=1, source_target_pairs={{4,0},{8,4},{12,8},{14,12},{10,14},{6,10},{2,6},{0,2},{5,1},{9,5},... | collective-permute-start | bytes 614408 | tf_op jit(solution)/shard_map/ppermute | solution.py:243
  14.6 26.7 %collective-permute-start.2 = (bf16[2,192,1280]{2,1,0:T(8,128)(2,1)}, bf16[2,192,1280]{2,1,0:T(8,128)(2,1)S(1)}, u32[]{:S(2)}, u32[]{:S(2)}) collective-permute-start(bf16[2,192,1280]{2,1,0:T(8,128)(2,1)} %shard_map.78), channel_id=1, source_target_pairs={{0,16},{16,0},{1,17},{17,1},{2,18},{18,2},{3,19},{19,3},{4,20},{20... | collective-permute-start | bytes 2949128 | tf_op jit(solution)/shard_map/ppermute | solution.py:247
  18.0 8.0 %collective-permute-start.5 = (bf16[160,640]{1,0:T(8,128)(2,1)S(1)}, bf16[160,640]{1,0:T(8,128)(2,1)S(1)}, u32[]{:S(2)}, u32[]{:S(2)}) collective-permute-start(bf16[160,640]{1,0:T(8,128)(2,1)S(1)} %get-tuple-element.47.refs_1_), channel_id=1, source_target_pairs={{0,4},{4,8},{8,12},{12,14},{14,10},{10,6},{6,2},{2,0},{1,5},{5,9},... | collective-permute-start | bytes 614408 | tf_op jit(solution)/shard_map/ppermute | solution.py:242
  18.5 11.9 %collective-permute-start.3 = (bf16[160,640]{1,0:T(8,128)(2,1)}, bf16[160,640]{1,0:T(8,128)(2,1)S(1)}, u32[]{:S(2)}, u32[]{:S(2)}) collective-permute-start(bf16[160,640]{1,0:T(8,128)(2,1)} %copy-done.13), channel_id=1, source_target_pairs={{0,4},{4,8},{8,12},{12,14},{14,10},{10,6},{6,2},{2,0},{1,5},{5,9},... | collective-permute-start | bytes 614408 | tf_op jit(solution)/shard_map/ppermute | solution.py:242
  20.1 10.8 %collective-permute-start.8 = (bf16[160,640]{1,0:T(8,128)(2,1)}, bf16[160,640]{1,0:T(8,128)(2,1)S(1)}, u32[]{:S(2)}, u32[]{:S(2)}) collective-permute-start(bf16[160,640]{1,0:T(8,128)(2,1)} %copy-done.15), channel_id=1, source_target_pairs={{4,0},{8,4},{12,8},{14,12},{10,14},{6,10},{2,6},{0,2},{5,1},{9,5},... | collective-permute-start | bytes 614408 | tf_op jit(solution)/shard_map/ppermute | solution.py:243
  23.9 8.8 %collective-permute-start.11 = (bf16[160,640]{1,0:T(8,128)(2,1)S(1)}, bf16[160,640]{1,0:T(8,128)(2,1)S(1)}, u32[]{:S(2)}, u32[]{:S(2)}) collective-permute-start(bf16[160,640]{1,0:T(8,128)(2,1)S(1)} %collective-permute-done.10.refs_5_), channel_id=1, source_target_pairs={{4,0},{8,4},{12,8},{14,12},{10,14},{6,10},{2,6},{0,2},{5,1},{9,5},... | collective-permute-start | bytes 614408 | tf_op jit(solution)/shard_map/ppermute | solution.py:243
  26.1 8.8 %collective-permute-start.6 = (bf16[160,640]{1,0:T(8,128)(2,1)S(1)}, bf16[160,640]{1,0:T(8,128)(2,1)S(1)}, u32[]{:S(2)}, u32[]{:S(2)}) collective-permute-start(bf16[160,640]{1,0:T(8,128)(2,1)S(1)} %collective-permute-done.5.refs_3_), channel_id=1, source_target_pairs={{0,4},{4,8},{8,12},{12,14},{14,10},{10,6},{6,2},{2,0},{1,5},{5,9},... | collective-permute-start | bytes 614408 | tf_op jit(solution)/shard_map/ppermute | solution.py:242
  30.4 8.7 %collective-permute-start.4 = (bf16[160,640]{1,0:T(8,128)(2,1)S(1)}, bf16[160,640]{1,0:T(8,128)(2,1)S(1)}, u32[]{:S(2)}, u32[]{:S(2)}) collective-permute-start(bf16[160,640]{1,0:T(8,128)(2,1)S(1)} %collective-permute-done.3.refs_6_), channel_id=1, source_target_pairs={{0,4},{4,8},{8,12},{12,14},{14,10},{10,6},{6,2},{2,0},{1,5},{5,9},... | collective-permute-start | bytes 614408 | tf_op jit(solution)/shard_map/ppermute | solution.py:242
  31.0 8.1 %collective-permute-start.9 = (bf16[160,640]{1,0:T(8,128)(2,1)S(1)}, bf16[160,640]{1,0:T(8,128)(2,1)S(1)}, u32[]{:S(2)}, u32[]{:S(2)}) collective-permute-start(bf16[160,640]{1,0:T(8,128)(2,1)S(1)} %collective-permute-done.8.refs_8_), channel_id=1, source_target_pairs={{4,0},{8,4},{12,8},{14,12},{10,14},{6,10},{2,6},{0,2},{5,1},{9,5},... | collective-permute-start | bytes 614408 | tf_op jit(solution)/shard_map/ppermute | solution.py:243
  41.3 8.8 %collective-permute-start.13 = (bf16[2,192,1280]{2,1,0:T(8,128)(2,1)S(1)}, bf16[2,192,1280]{2,1,0:T(8,128)(2,1)}, u32[]{:S(2)}, u32[]{:S(2)}) collective-permute-start(bf16[2,192,1280]{2,1,0:T(8,128)(2,1)S(1)} %collective-permute-done.2.first), channel_id=1, source_target_pairs={{0,1},{1,0},{2,3},{3,2},{4,5},{5,4},{6,7},{7,6},{8,9},{9,8},{10,11... | collective-permute-start | bytes 2949128 | tf_op jit(solution)/shard_map/ppermute | solution.py:265
  41.3 8.8 %collective-permute-start.14 = (bf16[160,640]{1,0:T(8,128)(2,1)S(1)}, bf16[160,640]{1,0:T(8,128)(2,1)}, u32[]{:S(2)}, u32[]{:S(2)}) collective-permute-start(bf16[160,640]{1,0:T(8,128)(2,1)S(1)} %collective-permute-done.4.refs_10_), channel_id=1, source_target_pairs={{0,4},{4,8},{8,12},{12,14},{14,10},{10,6},{6,2},{2,0},{1,5},{5,9},... | collective-permute-start | bytes 614408 | tf_op jit(solution)/shard_map/ppermute | solution.py:260
  41.8 8.3 %collective-permute-start.15 = (bf16[160,640]{1,0:T(8,128)(2,1)S(1)}, bf16[160,640]{1,0:T(8,128)(2,1)}, u32[]{:S(2)}, u32[]{:S(2)}) collective-permute-start(bf16[160,640]{1,0:T(8,128)(2,1)S(1)} %collective-permute-done.12.refs_13_), channel_id=1, source_target_pairs={{4,0},{8,4},{12,8},{14,12},{10,14},{6,10},{2,6},{0,2},{5,1},{9,5},... | collective-permute-start | bytes 614408 | tf_op jit(solution)/shard_map/ppermute | solution.py:260
  60.3 8.6 %collective-permute-start.18 = (bf16[160,640]{1,0:T(8,128)(2,1)S(1)}, bf16[160,640]{1,0:T(8,128)(2,1)S(1)}, u32[]{:S(2)}, u32[]{:S(2)}) collective-permute-start(bf16[160,640]{1,0:T(8,128)(2,1)S(1)} %get-tuple-element.61.refs_4_), channel_id=1, source_target_pairs={{0,4},{4,8},{8,12},{12,14},{14,10},{10,6},{6,2},{2,0},{1,5},{5,9},... | collective-permute-start | bytes 614408 | tf_op jit(solution)/shard_map/ppermute | solution.py:313
  60.9 8.0 %collective-permute-start.19 = (bf16[160,640]{1,0:T(8,128)(2,1)S(1)}, bf16[160,640]{1,0:T(8,128)(2,1)S(1)}, u32[]{:S(2)}, u32[]{:S(2)}) collective-permute-start(bf16[160,640]{1,0:T(8,128)(2,1)S(1)} %get-tuple-element.65), channel_id=1, source_target_pairs={{4,0},{8,4},{12,8},{14,12},{10,14},{6,10},{2,6},{0,2},{5,1},{9,5},... | collective-permute-start | bytes 614408 | tf_op jit(solution)/shard_map/ppermute | solution.py:313
  63.0 8.6 %collective-permute-start.20 = (bf16[160,640]{1,0:T(8,128)(2,1)S(1)}, bf16[160,640]{1,0:T(8,128)(2,1)S(1)}, u32[]{:S(2)}, u32[]{:S(2)}) collective-permute-start(bf16[160,640]{1,0:T(8,128)(2,1)S(1)} %get-tuple-element.62.refs_4_), channel_id=1, source_target_pairs={{0,4},{4,8},{8,12},{12,14},{14,10},{10,6},{6,2},{2,0},{1,5},{5,9},... | collective-permute-start | bytes 614408 | tf_op jit(solution)/shard_map/ppermute | solution.py:313
  72.4 9.3 %collective-permute-start.22 = (bf16[2,384,640]{2,1,0:T(8,128)(2,1)}, bf16[2,384,640]{2,1,0:T(8,128)(2,1)S(1)}, u32[]{:S(2)}, u32[]{:S(2)}) collective-permute-start(bf16[2,384,640]{2,1,0:T(8,128)(2,1)} %shard_map.87), channel_id=1, source_target_pairs={{0,1},{1,0},{2,3},{3,2},{4,5},{5,4},{6,7},{7,6},{8,9},{9,8},{10,11... | collective-permute-start | bytes 2949128 | tf_op jit(solution)/shard_map/ppermute | solution.py:322
  72.4 8.5 %collective-permute-start.23 = (bf16[160,640]{1,0:T(8,128)(2,1)}, bf16[160,640]{1,0:T(8,128)(2,1)S(1)}, u32[]{:S(2)}, u32[]{:S(2)}) collective-permute-start(bf16[160,640]{1,0:T(8,128)(2,1)} %copy-done.19), channel_id=1, source_target_pairs={{0,4},{4,8},{8,12},{12,14},{14,10},{10,6},{6,2},{2,0},{1,5},{5,9},... | collective-permute-start | bytes 614408 | tf_op jit(solution)/shard_map/ppermute | solution.py:313
  79.2 7.8 %collective-permute-start.27 = (bf16[160,640]{1,0:T(8,128)(2,1)S(1)}, bf16[160,640]{1,0:T(8,128)(2,1)S(1)}, u32[]{:S(2)}, u32[]{:S(2)}) collective-permute-start(bf16[160,640]{1,0:T(8,128)(2,1)S(1)} %get-tuple-element.72), channel_id=1, source_target_pairs={{4,0},{8,4},{12,8},{14,12},{10,14},{6,10},{2,6},{0,2},{5,1},{9,5},... | collective-permute-start | bytes 614408 | tf_op jit(solution)/shard_map/ppermute | solution.py:313
  83.2 15.2 %collective-permute-start.25 = (bf16[384,640]{1,0:T(8,128)(2,1)S(1)}, bf16[384,640]{1,0:T(8,128)(2,1)S(1)}, u32[]{:S(2)}, u32[]{:S(2)}) collective-permute-start(bf16[384,640]{1,0:T(8,128)(2,1)S(1)} %shard_map.90.refs_3_), channel_id=1, source_target_pairs={{0,16},{16,0},{1,17},{17,1},{2,18},{18,2},{3,19},{19,3},{4,20},{20... | collective-permute-start | bytes 1474568 | tf_op jit(solution)/shard_map/ppermute | solution.py:326
  83.8 8.0 %collective-permute-start.29 = (bf16[160,640]{1,0:T(8,128)(2,1)S(1)}, bf16[160,640]{1,0:T(8,128)(2,1)S(1)}, u32[]{:S(2)}, u32[]{:S(2)}) collective-permute-start(bf16[160,640]{1,0:T(8,128)(2,1)S(1)} %get-tuple-element.70.refs_3_), channel_id=1, source_target_pairs={{0,4},{4,8},{8,12},{12,14},{14,10},{10,6},{6,2},{2,0},{1,5},{5,9},... | collective-permute-start | bytes 614408 | tf_op jit(solution)/shard_map/ppermute | solution.py:313
  85.4 10.8 %collective-permute-start.26 = (bf16[160,640]{1,0:T(8,128)(2,1)S(1)}, bf16[160,640]{1,0:T(8,128)(2,1)S(1)}, u32[]{:S(2)}, u32[]{:S(2)}) collective-permute-start(bf16[160,640]{1,0:T(8,128)(2,1)S(1)} %get-tuple-element.69.refs_4_), channel_id=1, source_target_pairs={{0,4},{4,8},{8,12},{12,14},{14,10},{10,6},{6,2},{2,0},{1,5},{5,9},... | collective-permute-start | bytes 614408 | tf_op jit(solution)/shard_map/ppermute | solution.py:313
  87.5 8.7 %collective-permute-start.28 = (bf16[160,640]{1,0:T(8,128)(2,1)S(1)}, bf16[160,640]{1,0:T(8,128)(2,1)S(1)}, u32[]{:S(2)}, u32[]{:S(2)}) collective-permute-start(bf16[160,640]{1,0:T(8,128)(2,1)S(1)} %shard_map.91.refs_3_), channel_id=1, source_target_pairs={{4,0},{8,4},{12,8},{14,12},{10,14},{6,10},{2,6},{0,2},{5,1},{9,5},... | collective-permute-start | bytes 614408 | tf_op jit(solution)/shard_map/ppermute | solution.py:313
  88.4 11.2 %collective-permute-start.32 = (bf16[160,640]{1,0:T(8,128)(2,1)S(1)}, bf16[160,640]{1,0:T(8,128)(2,1)S(1)}, u32[]{:S(2)}, u32[]{:S(2)}) collective-permute-start(bf16[160,640]{1,0:T(8,128)(2,1)S(1)} %get-tuple-element.75), channel_id=1, source_target_pairs={{4,0},{8,4},{12,8},{14,12},{10,14},{6,10},{2,6},{0,2},{5,1},{9,5},... | collective-permute-start | bytes 614408 | tf_op jit(solution)/shard_map/ppermute | solution.py:313
  (39 other events, 130.5 us)

commit v9 on v8

--- a/solution.py
+++ b/solution.py
@@ -64,29 +64,48 @@
     )
 
 
-def norm_kernel(meta, lengths, frames, out_grad, gain, *refs):
-    normed, grads, passing, stats = refs
-    half = passing.shape[1]
-    rows = pl.ds(pl.multiple_of(meta[1] * half, half), half)
-    keep = lax.broadcasted_iota(jnp.int32, (frames.shape[0], 1), 0) < lengths[meta[0]]
-    grads[...] = jnp.where(keep, out_grad[...].astype(F32), 0.0).astype(BF16)
-    passing[1] = grads[rows, :]
-    values = frames[...].astype(F32)
+def norm_rows(rows, gain):
+    values = rows.astype(F32)
     centre = jnp.mean(values, axis=-1, keepdims=True)
     shifted = values - centre
     variance = jnp.mean(shifted * shifted, axis=-1, keepdims=True)
     inv_std = lax.rsqrt(variance + 1e-05)
-    normed[...] = (shifted * inv_std * gain[...][None]).astype(BF16)
-    passing[0] = normed[rows, :]
+    return (shifted * inv_std * gain[...][None]).astype(BF16), centre, inv_std
+
+
+def mask_rows(rows, start, length):
+    index = start + lax.broadcasted_iota(jnp.int32, (rows.shape[0], 1), 0)
+    return jnp.where(index < length, rows.astype(F32), 0.0).astype(BF16)
+
+
+def pass_kernel(meta, lengths, frames, out_grad, gain, passing, sems, rows, grads):
+    half = rows.shape[0]
+    start = pl.multiple_of(meta[1] * half, half)
+    copies = [
+        pltpu.make_async_copy(source.at[pl.ds(start, half)], target, sems.at[i])
+        for i, (source, target) in enumerate(((frames, rows), (out_grad, grads)))
+    ]
+    for copy in copies:
+        copy.start()
+    copies[0].wait()
+    passing[0] = norm_rows(rows[...], gain)[0]
+    copies[1].wait()
+    passing[1] = mask_rows(grads[...], start, lengths[meta[0]])
+
+
+def norm_kernel(meta, lengths, frames, out_grad, gain, normed, grads, stats):
+    value, centre, inv_std = norm_rows(frames[...], gain)
+    normed[...] = value
     stats[:, 0:1] = centre
     stats[:, 1:2] = inv_std
+    grads[...] = mask_rows(out_grad[...], 0, lengths[meta[0]])
 
 
 def back_through(normed, grads, up, down, d_pre, partial):
     pre_act = dot(normed[...], up[...])
     d_act = dot(grads[...], down[...])
     d_pre[...] = (d_act * gelu_slope(pre_act)).astype(BF16)
-    partial[...] = dot(normed[...], d_pre[...], 0, 0)
+    partial[...] = dot(normed[...], d_pre[...], 0, 0).astype(BF16)
 
 
 def place_kernel(index, *refs):
@@ -103,22 +122,22 @@
         copy.wait()
 
 
-def other_kernel(index, first, second, near_up, near_down, *refs):
-    d_pre, partial, up, down, normed, grads = refs[-6:]
+def own_kernel(index, normed, grads, near_up, near_down, *refs):
+    d_pre, partial, up, down = refs[-4:]
+    up[...] = near_up[...]
+    down[...] = near_down[...]
+    for ref, far in zip((up, down), refs[:-4]):
+        depth = far.shape[0]
+        rows = pl.ds(pl.multiple_of(index[index.shape[0] - 1] * depth, depth), depth)
+        ref[rows, :] = far[...]
+    back_through(normed, grads, up, down, d_pre, partial)
+
+
+def other_kernel(first, second, up, down, d_pre, partial, normed, grads):
     half = first.shape[1]
     for at, part in ((0, first), (half, second)):
         normed[at : at + half, :] = part[0]
         grads[at : at + half, :] = part[1]
-    up[...] = near_up[...]
-    down[...] = near_down[...]
-    for ref, far in zip((up, down), refs[:-6]):
-        depth = far.shape[0]
-        rows = pl.ds(pl.multiple_of(index[index.shape[0] - 1] * depth, depth), depth)
-        ref[rows, :] = far[...]
-    back_through(normed, grads, up, down, d_pre, partial)
-
-
-def own_kernel(normed, grads, up, down, d_pre, partial):
     back_through(normed, grads, up, down, d_pre, partial)
 
 
@@ -127,8 +146,8 @@
     rows, width = keep.shape[1:]
     mine = up[pl.ds(pl.multiple_of(core * width, width), width), :]
     theirs = up[pl.ds(pl.multiple_of((1 - core) * width, width), width), :]
-    keep[0] = dot(d_pre_own[...], mine, 1, 1)
-    keep[1] = dot(d_pre_other[...], mine, 1, 1)
+    keep[0] = dot(d_pre_own[...], mine, 1, 1).astype(BF16)
+    keep[1] = dot(d_pre_other[...], mine, 1, 1).astype(BF16)
     send[0] = dot(d_pre_own[...], theirs, 1, 1).astype(BF16)
     sent = dot(d_pre_other[...], theirs, 1, 1).astype(BF16)
     send[1, rows // 2 :, :] = sent[: rows // 2]
@@ -140,7 +159,7 @@
     for i in range(2):
         at = lax.rem(i + meta[1], 2) * half
         rows = slice(i * half, (i + 1) * half)
-        value = keep[1, rows, :] + came[1, rows, :].astype(F32)
+        value = keep[1, rows, :].astype(F32) + came[1, rows, :].astype(F32)
         over[pl.ds(pl.multiple_of(at, half), half), :] = value.astype(BF16)
 
 
@@ -150,7 +169,7 @@
 
 def scale_kernel(meta, keep, came, back, frames, gain, stats, scaled, sums):
     width = scaled.shape[1]
-    d_norm = keep[0] + came[0].astype(F32) + back[...].astype(F32)
+    d_norm = keep[0].astype(F32) + came[0].astype(F32) + back[...].astype(F32)
     value = d_norm * own_columns(meta, gain, width)
     scaled[...] = value
     rows = own_columns(meta, frames, width).astype(F32)
@@ -174,25 +193,30 @@
     came = iter(refs)
     depth = outs[0].shape[0]
     for (at, summed), out in zip(places, outs):
-        value = partial[pl.ds(pl.multiple_of(index[at] * depth, depth), depth), :]
+        value = partial[pl.ds(pl.multiple_of(index[at] * depth, depth), depth), :].astype(F32)
         if summed:
             value = value + next(came)[...].astype(F32)
         out[...] = value.astype(BF16)
 
 
-def total_kernel(index, partial, up, down, total):
+def add_kernel(one, two, total):
+    total[...] = one[...].astype(F32) + two[...].astype(F32)
+
+
+def own_total_kernel(index, partial, up, down, total):
     depth = total.shape[0]
     rows = pl.ds(pl.multiple_of(index[0] * depth, depth), depth)
-    value = partial[rows, :] + up[...].astype(F32) + down[...].astype(F32)
-    total[...] = value.astype(total.dtype)
-
-
-def join_kernel(meta, own, passed, out):
-    width = own.shape[1]
+    total[...] = partial[rows, :].astype(F32) + up[...].astype(F32) + down[...].astype(F32)
+
+
+def join_kernel(meta, own, *refs):
+    width, out = own.shape[1], refs[-1]
     side = meta[2]
     out[:, pl.ds(pl.multiple_of(side * width, width), width)] = own[...]
-    other = pl.ds(pl.multiple_of((1 - side) * width, width), width)
-    out[:, other] = passed[...].astype(F32)
+    value = refs[0][...].astype(F32)
+    for ref in refs[1:-1]:
+        value = value + ref[...].astype(F32)
+    out[:, pl.ds(pl.multiple_of((1 - side) * width, width), width)] = value
 
 
 def ring_member(place, count):
@@ -226,10 +250,20 @@
     frames, out_grad = frames[0], out_grad[0]
 
     rows_of = shape((frame_len, width), BF16)
-    normed, grads, passing, stats = call(
+    operands = (meta, lengths, frames, out_grad, ln_gain)
+    passing = call(
+        pass_kernel,
+        operands,
+        shape((2, half_rows, width), BF16),
+        [pltpu.SemaphoreType.DMA((2,))] + [pltpu.VMEM((half_rows, width), BF16)] * 2,
+        flops=5 * frame_len * width,
+        pinned=(2, 3),
+    )
+    first = lax.ppermute(passing, "groups", swap)
+    normed, grads, stats = call(
         norm_kernel,
-        (meta, lengths, frames, out_grad, ln_gain),
-        (rows_of, rows_of, shape((2, half_rows, width), BF16), shape((frame_len, 2), F32)),
+        operands,
+        (rows_of, rows_of, shape((frame_len, 2), F32)),
         flops=10 * frame_len * width,
     )
 
@@ -242,10 +276,8 @@
             up = [lax.ppermute(block, "gx", ahead) for block in up]
             down = [lax.ppermute(block, "gx", behind) for block in down]
             blocks[-step], blocks[step] = up, down
-            if step == 1:
-                passing = hold(passing, up[0], down[0])
-        first = lax.ppermute(passing, "groups", swap)
         first, up, down = after((first, up, down))
+        first = hold(first, normed)
         steps = list(blocks) + [half]
         index = jnp.stack([ring_member(place + step + peers, peers) for step in steps])
         index = index.astype(jnp.int32)
@@ -259,21 +291,22 @@
         )
         far = [lax.ppermute(up[0], "gx", ahead), lax.ppermute(down[1], "gx", behind)]
     else:
-        first = lax.ppermute(passing, "groups", swap)
         near = [lax.all_gather(block, "gx", axis=0, tiled=True) for block in mine]
         index, far = jnp.zeros((1,), jnp.int32), []
     second = lax.ppermute(first, "gy", swap)
 
-    d_pre_of, partial_of = shape((frame_len, quarter), BF16), shape((width, quarter), F32)
-    d_pre_other, partial_other, full_up, full_down = call(
+    d_pre_of, partial_of = shape((frame_len, quarter), BF16), shape((width, quarter), BF16)
+    d_pre_own, partial_own, full_up, full_down = call(
+        own_kernel,
+        (index, normed, grads, *near, *far),
+        (d_pre_of, partial_of, weight, weight),
+        flops=6 * frame_len * width * quarter,
+    )
+    d_pre_other, partial_other = call(
         other_kernel,
-        (index, first, second, *near, *far),
-        (d_pre_of, partial_of, weight, weight),
+        (first, second, full_up, full_down),
+        (d_pre_of, partial_of),
         [pltpu.VMEM((frame_len, width), BF16)] * 2,
-        flops=6 * frame_len * width * quarter,
-    )
-    d_pre_own, partial_own = call(
-        own_kernel, (normed, grads, full_up, full_down), (d_pre_of, partial_of),
         flops=6 * frame_len * width * quarter,
     )
     partial = [partial_own, partial_other]
@@ -284,7 +317,7 @@
         return call(
             d_norm_kernel,
             (meta, d_pre_own, d_pre_other, full_up),
-            (shape((2, frame_len, half_width), F32), shape((2, frame_len, half_width), BF16)),
+            (shape((2, frame_len, half_width), BF16), shape((2, frame_len, half_width), BF16)),
             flops=4 * frame_len * width * quarter,
             ties=ties,
         )
@@ -292,69 +325,93 @@
     def over_cores(keep, came, *ties):
         return call(over_kernel, (meta, keep, came), half_rows_of, ties=ties)
 
+    def scale(keep, came, back, *ties):
+        return call(
+            scale_kernel,
+            (meta, keep, came, back, frames, ln_gain[None], stats),
+            (shape((frame_len, half_width), F32), shape((frame_len, 2), F32)),
+            ties=ties,
+        )
+
+    def input_gradient(scaled, sums, *ties):
+        return call(
+            input_kernel,
+            (meta, scaled, sums, lax.ppermute(sums, "gy", swap), frames, grads, stats),
+            half_rows_of,
+            ties=ties,
+        )
+
+    up_grad_of = shape((depth, hidden), F32)
     if ringed:
         place_of = {step: i for i, step in enumerate(steps)}
         place_of[-half] = place_of[half]
-
         came = [{}, {}]
+        across = {}
+        for name, pairs in (("up", ahead), ("down", behind)):
+            across[name] = [
+                (a + side_at * peers, b + (1 - side_at) * peers)
+                for side_at in range(2)
+                for a, b in pairs
+            ]
 
         def hop(i, turn, *ties):
-            ways = [(half - turn - (i == 1), ahead), (turn + (i == 0) - half, behind)]
-            ways = [way for way in ways if way[0] != 0]
-            kept = [came[i][pairs[0]] for _, pairs in ways if pairs[0] in came[i]]
-            places = [(place_of[step], pairs[0] in came[i]) for step, pairs in ways]
+            ways = [("up", half - turn - i), ("down", turn + 1 - i - half)]
+            ways = [way for way in ways if way[1] != 0]
+            kept = [came[i][name] for name, _ in ways if name in came[i]]
+            places = [(place_of[step], name in came[i]) for name, step in ways]
+            if (i, turn) == (1, 0):
+                places.append((0, False))
             blocks = call(
                 functools.partial(hop_kernel, tuple(places)),
                 (index, partial[i], *kept),
-                [block_of] * len(ways),
+                [block_of] * len(places),
                 ties=ties,
             )
-            for block, (_, pairs) in zip(blocks, ways):
-                came[i][pairs[0]] = lax.ppermute(block, "gx", pairs)
+            for block, (name, step) in zip(blocks, ways):
+                if i == 1 and abs(step) == 1:
+                    came[i][name] = lax.ppermute(block, ("groups", "gx"), across[name])
+                else:
+                    came[i][name] = lax.ppermute(block, "gx", ahead if name == "up" else behind)
+            if (i, turn) == (1, 0):
+                came[i]["own"] = lax.ppermute(blocks[-1], "groups", swap)
             return blocks[0]
 
-        hop(1, 0)
-        tie = hop(0, 0)
+        hop(0, 0)
+        tie = hop(1, 0)
+        keep, send = own_d_norm(tie)
+        send = hold(send, came[0]["up"], came[0]["down"])
+        sent = lax.ppermute(send, "gy", swap)
+        tie = hop(0, 1, send)
         tie = hop(1, 1, tie)
-        keep, send = own_d_norm(tie)
-        tie = hop(0, 1, send)
-        send = hold(send, tie, *came[1].values())
-        over_cores_came = lax.ppermute(send, "gy", swap)
+        over = over_cores(keep, sent, tie)
+        over = hold(over, came[0]["up"], came[0]["down"])
+        back = lax.ppermute(over, "groups", swap)
+        tie = hop(0, 2, over)
         tie = hop(1, 2, tie)
-        tie = hop(0, 2, tie)
-        over = over_cores(keep, over_cores_came, tie)
-        back = lax.ppermute(over, "groups", swap)
-        tie = over
         for turn in range(3, half):
-            tie = hop(0, turn, hop(1, turn, tie))
-        one, two = ([came[i][pairs[0]] for pairs in (ahead, behind)] for i in range(2))
-        passing = call(total_kernel, (index, partial[1], *two), block_of, ties=(tie,))
-        total = call(total_kernel, (index, partial[0], *one), shape((depth, quarter), F32))
-        came = over_cores_came
-        tail = (passing,)
+            tie = hop(1, turn, hop(0, turn, tie, came[1]["own"]))
+        other = call(
+            add_kernel, (came[1]["own"], came[1]["up"]), shape((depth, quarter), F32), ties=(tie,)
+        )
+        scaled, sums = scale(keep, sent, back, other)
+        input_grad = input_gradient(scaled, sums)
+        total = call(
+            own_total_kernel,
+            (index, partial[0], came[0]["up"], came[0]["down"]),
+            shape((depth, quarter), F32),
+            ties=(input_grad,),
+        )
+        up_grad = call(join_kernel, (meta, total, other, came[1]["down"]), up_grad_of)
     else:
         keep, send = own_d_norm()
-        came = lax.ppermute(send, "gy", swap)
-        back = lax.ppermute(over_cores(keep, came), "groups", swap)
+        sent = lax.ppermute(send, "gy", swap)
+        back = lax.ppermute(over_cores(keep, sent), "groups", swap)
+        input_grad = input_gradient(*scale(keep, sent, back))
         total, passing = [
-            lax.psum_scatter(p, "gx", scatter_dimension=0, tiled=True) for p in partial
+            lax.psum_scatter(p.astype(F32), "gx", scatter_dimension=0, tiled=True) for p in partial
         ]
-        passing, tail = passing.astype(BF16), ()
-    passed = lax.ppermute(passing, "groups", swap)
-    up_grad = call(join_kernel, (meta, total, passed), shape((depth, hidden), F32))
-
-    gain = ln_gain[None]
-    scaled, sums = call(
-        scale_kernel,
-        (meta, keep, came, back, frames, gain, stats),
-        (shape((frame_len, half_width), F32), shape((frame_len, 2), F32)),
-        ties=tail,
-    )
-    input_grad = call(
-        input_kernel,
-        (meta, scaled, sums, lax.ppermute(sums, "gy", swap), frames, grads, stats),
-        shape((frame_len, half_width), BF16),
-    )
+        passed = lax.ppermute(passing.astype(BF16), "groups", swap)
+        up_grad = call(join_kernel, (meta, total, passed), up_grad_of)
     return (input_grad[None], up_grad)
 
 

time: 107 us -> 119 us (1.11)
  starting transfers between devices: 37.8 us -> 42.6 us
  Pallas kernels: 27.4 us -> 30.9 us
  local copies, waits for them, and re-layouts: 17.8 us -> 21.2 us
    ppermute x6, waiting for transfers between devices: 8.88 us -> 2.15 us  [shards(): up = [lax.ppermute(block, 'gx', ahead) for block in up]]
    ppermute x6, waiting for transfers between devices: 4.5 us -> 10.5 us  [shards(): down = [lax.ppermute(block, 'gx', behind) for block in down]]
    ppermute x17, starting transfers between devices: 18.7 us -> 22.7 us  [the longest x12 17.4 us: hop(): came[i][name] = lax.ppermute(block, 'gx', ahead if name == 'up' else behind)]
    pallas_call x19 -> x20, Pallas kernels: 27.4 us -> 30.9 us  [call(): pl.pallas_call(body if ties else kernel, out_shape=out_shape, in_specs=[S...]
    unnamed x58 -> x64, local copies, waits for them, and re-layouts: 16.6 us -> 20.1 us
    ppermute x6, starting transfers between devices: 6.67 us -> 5.12 us  [shards(): up = [lax.ppermute(block, 'gx', ahead) for block in up]]
    ppermute x6, starting transfers between devices: 7.8 us -> 9.17 us  [shards(): down = [lax.ppermute(block, 'gx', behind) for block in down]]
  transfers between devices with their start and end apart: 34 -> 34, of which waited for: 12 -> 11; matrix products, arithmetic and copies ran while one was open for 0% -> 0% of each run, Pallas kernels for 19% -> 23%
where the time goes in v9:
time: 119 us
  starting transfers between devices  42.6 us (36%)
  Pallas kernels  30.9 us (26%)
  waiting for transfers between devices  22.7 us (19%)
  local copies, waits for them, and re-layouts  21.2 us (18%)
    pallas_call x20, Pallas kernels, call(): pl.pallas_call(body if ties else kernel, out_shape=out_shape, in_specs=[S...  30.9 us
    unnamed x64, local copies, waits for them, and re-layouts  20.1 us
    ppermute x12, starting transfers between devices, hop(): came[i][name] = lax.ppermute(block, 'gx', ahead if name == 'up' else behind)  17.4 us
    ppermute x6, waiting for transfers between devices, shards(): down = [lax.ppermute(block, 'gx', behind) for block in down]  10.5 us
    ppermute x6, starting transfers between devices, shards(): down = [lax.ppermute(block, 'gx', behind) for block in down]  9.17 us
    ppermute x1, waiting for transfers between devices, hop(): came[i]['own'] = lax.ppermute(blocks[-1], 'groups', swap)  6.69 us
    ppermute x6, starting transfers between devices, shards(): up = [lax.ppermute(block, 'gx', ahead) for block in up]  5.12 us
    ppermute x2, starting transfers between devices, hop(): came[i][name] = lax.ppermute(block, ('groups', 'gx'), across[name])  3.73 us
  transfers between devices with their start and end apart: 34, of which 11 were waited for; matrix products, arithmetic and copies ran while one was open for 0% of the time, Pallas kernels for 23%

profile of v9, /device:TPU:0, one launch (start us, length us, event | category | flops | bytes accessed | tf_op | source)
XLA Modules:
  0.0 118.5 jit_solution(17383775696926744785)
XLA Ops:
  5.6 1.6 %shard_map.79 = bf16[2,192,1280]{2,1,0:T(8,128)(2,1)S(1)} custom-call(s32[3]{0:T(128)S(1)} %pad_add_fusion.meta.refs_0_, s32[8]{0:T(128)S(1)} %copy-done.28, bf16[384,1280]{1,0:T(8,128)(2,1)S(1)} %bitcast.14, bf16[384,1280]{1,0:T(8,128)(2,1)S(1)} %bitcast.18, f32[1280]{0:T(1024)S(1)} %copy-done.26), custom_call_target="tpu_custom_call" | custom-call | flops 2457600 | bytes 2954284 | tf_op jit(solution)/shard_map/pallas_call | solution.py:28
  7.2 3.0 %collective-permute-start.12 = (bf16[2,192,1280]{2,1,0:T(8,128)(2,1)S(1)}, bf16[2,192,1280]{2,1,0:T(8,128)(2,1)}, u32[]{:S(2)}, u32[]{:S(2)}) collective-permute-start(bf16[2,192,1280]{2,1,0:T(8,128)(2,1)S(1)} %shard_map.79), channel_id=1, source_target_pairs={{0,16},{16,0},{1,17},{17,1},{2,18},{18,2},{3,19},{19,3},{4,20},{20... | collective-permute-start | bytes 2949128 | tf_op jit(solution)/shard_map/ppermute | solution.py:262
  10.2 1.5 %collective-permute-start.2 = (bf16[160,640]{1,0:T(8,128)(2,1)S(1)}, bf16[160,640]{1,0:T(8,128)(2,1)S(1)}, u32[]{:S(2)}, u32[]{:S(2)}) collective-permute-start(bf16[160,640]{1,0:T(8,128)(2,1)S(1)} %get-tuple-element.45.refs_0_), channel_id=1, source_target_pairs={{4,0},{8,4},{12,8},{14,12},{10,14},{6,10},{2,6},{0,2},{5,1},{9,5},... | collective-permute-start | bytes 614408 | tf_op jit(solution)/shard_map/ppermute | solution.py:277
  11.7 1.6 %collective-permute-start.3 = (bf16[160,640]{1,0:T(8,128)(2,1)S(1)}, bf16[160,640]{1,0:T(8,128)(2,1)S(1)}, u32[]{:S(2)}, u32[]{:S(2)}) collective-permute-start(bf16[160,640]{1,0:T(8,128)(2,1)S(1)} %get-tuple-element.46.refs_1_), channel_id=1, source_target_pairs={{4,0},{8,4},{12,8},{14,12},{10,14},{6,10},{2,6},{0,2},{5,1},{9,5},... | collective-permute-start | bytes 614408 | tf_op jit(solution)/shard_map/ppermute | solution.py:277
  14.2 3.9 %collective-permute-done.2.refs_4_ = bf16[160,640]{1,0:T(8,128)(2,1)S(1)} collective-permute-done((bf16[160,640]{1,0:T(8,128)(2,1)S(1)}, bf16[160,640]{1,0:T(8,128)(2,1)S(1)}, u32[]{:S(2)}, u32[]{:S(2)}) %collective-permute-start.2) | collective-permute-done | bytes 204832 | tf_op jit(solution)/shard_map/ppermute | solution.py:277
  19.7 2.9 %collective-permute-done.3.refs_5_ = bf16[160,640]{1,0:T(8,128)(2,1)S(1)} collective-permute-done((bf16[160,640]{1,0:T(8,128)(2,1)S(1)}, bf16[160,640]{1,0:T(8,128)(2,1)S(1)}, u32[]{:S(2)}, u32[]{:S(2)}) %collective-permute-start.3) | collective-permute-done | bytes 204832 | tf_op jit(solution)/shard_map/ppermute | solution.py:277
  24.6 1.6 %collective-permute-start.5 = (bf16[160,640]{1,0:T(8,128)(2,1)S(1)}, bf16[160,640]{1,0:T(8,128)(2,1)S(1)}, u32[]{:S(2)}, u32[]{:S(2)}) collective-permute-start(bf16[160,640]{1,0:T(8,128)(2,1)S(1)} %collective-permute-done.1.refs_3_), channel_id=1, source_target_pairs={{0,4},{4,8},{8,12},{12,14},{14,10},{10,6},{6,2},{2,0},{1,5},{5,9},... | collective-permute-start | bytes 614408 | tf_op jit(solution)/shard_map/ppermute | solution.py:276
  28.5 2.9 %collective-permute-done.7.refs_9_ = bf16[160,640]{1,0:T(8,128)(2,1)S(1)} collective-permute-done((bf16[160,640]{1,0:T(8,128)(2,1)S(1)}, bf16[160,640]{1,0:T(8,128)(2,1)S(1)}, u32[]{:S(2)}, u32[]{:S(2)}) %collective-permute-start.7) | collective-permute-done | bytes 204832 | tf_op jit(solution)/shard_map/ppermute | solution.py:277
  33.4 1.6 %collective-permute-start.9 = (bf16[160,640]{1,0:T(8,128)(2,1)S(1)}, bf16[160,640]{1,0:T(8,128)(2,1)S(1)}, u32[]{:S(2)}, u32[]{:S(2)}) collective-permute-start(bf16[160,640]{1,0:T(8,128)(2,1)S(1)} %collective-permute-done.5.refs_7_), channel_id=1, source_target_pairs={{0,4},{4,8},{8,12},{12,14},{14,10},{10,6},{6,2},{2,0},{1,5},{5,9},... | collective-permute-start | bytes 614408 | tf_op jit(solution)/shard_map/ppermute | solution.py:276
  39.2 2.1 %collective-permute-done.9.refs_11_ = bf16[160,640]{1,0:T(8,128)(2,1)S(1)} collective-permute-done((bf16[160,640]{1,0:T(8,128)(2,1)S(1)}, bf16[160,640]{1,0:T(8,128)(2,1)S(1)}, u32[]{:S(2)}, u32[]{:S(2)}) %collective-permute-start.9) | collective-permute-done | bytes 204832 | tf_op jit(solution)/shard_map/ppermute | solution.py:276
  45.0 4.5 %shard_map.78 = (bf16[1280,640]{1,0:T(8,128)(2,1)S(1)}, bf16[1280,640]{1,0:T(8,128)(2,1)S(1)}) custom-call(s32[8]{0:T(128)S(1)} %stack.51.index.refs_0_, bf16[160,640]{1,0:T(8,128)(2,1)S(1)} %get-tuple-element.45.refs_0_, bf16[160,640]{1,0:T(8,128)(2,1)S(1)} %get-tuple-element.46.refs_1_, bf16[160,640]{1,0:T(8,128)(2,1)S(1)} %collective-permute-done.refs_2_, ...), custom_call_target="tpu_custom_call" | custom-call | flops 1 | bytes 6144032 | tf_op jit(solution)/shard_map/pallas_call | solution.py:28
  51.0 3.9 %shard_map.80 = (bf16[384,640]{1,0:T(8,128)(2,1)S(1)}, bf16[1280,640]{1,0:T(8,128)(2,1)S(1)}, bf16[1280,640]{1,0:T(8,128)(2,1)S(1)}, bf16[1280,640]{1,0:T(8,128)(2,1)S(1)}) custom-call(s32[8]{0:T(128)S(1)} %stack.51.index.refs_0_, bf16[384,1280]{1,0:T(8,128)(2,1)S(1)} %copy-done.14, bf16[384,1280]{1,0:T(8,128)(2,1)S(1)} %copy-done.16, ...), custom_call_target="tpu_custom_call" | custom-call | flops 1887436800 | bytes 11059232 | tf_op jit(solution)/shard_map/pallas_call | solution.py:28
  55.4 1.6 %collective-permute-start.16 = (bf16[160,640]{1,0:T(8,128)(2,1)S(1)}, bf16[160,640]{1,0:T(8,128)(2,1)S(1)}, u32[]{:S(2)}, u32[]{:S(2)}) collective-permute-start(bf16[160,640]{1,0:T(8,128)(2,1)S(1)} %get-tuple-element.61), channel_id=1, source_target_pairs={{0,4},{4,8},{8,12},{12,14},{14,10},{10,6},{6,2},{2,0},{1,5},{5,9},... | collective-permute-start | bytes 614408 | tf_op jit(solution)/shard_map/ppermute | solution.py:374
  57.5 4.2 %shard_map.82 = (bf16[384,640]{1,0:T(8,128)(2,1)S(1)}, bf16[1280,640]{1,0:T(8,128)(2,1)S(1)}) custom-call(bf16[2,192,1280]{2,1,0:T(8,128)(2,1)} %shard_map.81.first, bf16[2,192,1280]{2,1,0:T(8,128)(2,1)} %collective-permute-done.15.second, bf16[1280,640]{1,0:T(8,128)(2,1)S(1)} %get-tuple-element.53.up.refs_3_, bf16[1280,640]{1,0:T(8,128)(2,1)S(1)} %get-tuple-element.54.down), custom_call_target="tpu_custom_call" | custom-call | flops 1887436800 | bytes 7372800 | tf_op jit(solution)/shard_map/pallas_call | solution.py:28
  63.7 2.5 %shard_map.84 = (bf16[2,384,640]{2,1,0:T(8,128)(2,1)S(1)}, bf16[2,384,640]{2,1,0:T(8,128)(2,1)S(1)}) custom-call(s32[3]{0:T(128)S(1)} %pad_add_fusion.meta.refs_0_, bf16[384,640]{1,0:T(8,128)(2,1)S(1)} %get-tuple-element.51.refs_1_, bf16[384,640]{1,0:T(8,128)(2,1)S(1)} %get-tuple-element.55.refs_2_, bf16[1280,640]{1,0:T(8,128)(2,1)S(1)} %get-tuple-element.53.up.refs_3_, ...), custom_call_target="tpu_custom_call" | custom-call | flops 1258291200 | bytes 4587532 | tf_op jit(solution)/shard_map/pallas_call | solution.py:28
  68.8 1.6 %collective-permute-start.19 = (bf16[160,640]{1,0:T(8,128)(2,1)}, bf16[160,640]{1,0:T(8,128)(2,1)S(1)}, u32[]{:S(2)}, u32[]{:S(2)}) collective-permute-start(bf16[160,640]{1,0:T(8,128)(2,1)} %copy-done.31), channel_id=1, source_target_pairs={{0,4},{4,8},{8,12},{12,14},{14,10},{10,6},{6,2},{2,0},{1,5},{5,9},... | collective-permute-start | bytes 614408 | tf_op jit(solution)/shard_map/ppermute | solution.py:374
  74.0 1.6 %collective-permute-start.21 = (bf16[160,640]{1,0:T(8,128)(2,1)S(1)}, bf16[160,640]{1,0:T(8,128)(2,1)S(1)}, u32[]{:S(2)}, u32[]{:S(2)}) collective-permute-start(bf16[160,640]{1,0:T(8,128)(2,1)S(1)} %get-tuple-element.64.refs_4_), channel_id=1, source_target_pairs={{0,4},{4,8},{8,12},{12,14},{14,10},{10,6},{6,2},{2,0},{1,5},{5,9},... | collective-permute-start | bytes 614408 | tf_op jit(solution)/shard_map/ppermute | solution.py:374
  79.2 1.6 %collective-permute-start.25 = (bf16[160,640]{1,0:T(8,128)(2,1)}, bf16[160,640]{1,0:T(8,128)(2,1)}, u32[]{:S(2)}, u32[]{:S(2)}) collective-permute-start(bf16[160,640]{1,0:T(8,128)(2,1)} %get-tuple-element.65.refs_3_), channel_id=1, source_target_pairs={{0,4},{4,8},{8,12},{12,14},{14,10},{10,6},{6,2},{2,0},{1,5},{5,9},... | collective-permute-start | bytes 614408 | tf_op jit(solution)/shard_map/ppermute | solution.py:374
  88.7 1.6 %collective-permute-start.29 = (bf16[160,640]{1,0:T(8,128)(2,1)S(1)}, bf16[160,640]{1,0:T(8,128)(2,1)S(1)}, u32[]{:S(2)}, u32[]{:S(2)}) collective-permute-start(bf16[160,640]{1,0:T(8,128)(2,1)S(1)} %get-tuple-element.70.refs_4_), channel_id=1, source_target_pairs={{0,4},{4,8},{8,12},{12,14},{14,10},{10,6},{6,2},{2,0},{1,5},{5,9},... | collective-permute-start | bytes 614408 | tf_op jit(solution)/shard_map/ppermute | solution.py:374
  92.0 1.6 %collective-permute-start.27 = (bf16[160,640]{1,0:T(8,128)(2,1)S(1)}, bf16[160,640]{1,0:T(8,128)(2,1)S(1)}, u32[]{:S(2)}, u32[]{:S(2)}) collective-permute-start(bf16[160,640]{1,0:T(8,128)(2,1)S(1)} %get-tuple-element.71.refs_3_), channel_id=1, source_target_pairs={{0,20},{4,24},{8,28},{12,30},{14,26},{10,22},{6,18},{2,16},{16,4},... | collective-permute-start | bytes 614408 | tf_op jit(solution)/shard_map/ppermute | solution.py:372
  93.5 6.7 %collective-permute-done.24.refs_4_.refs_0_ = bf16[160,640]{1,0:T(8,128)(2,1)S(1)} collective-permute-done((bf16[160,640]{1,0:T(8,128)(2,1)}, bf16[160,640]{1,0:T(8,128)(2,1)S(1)}, u32[]{:S(2)}, u32[]{:S(2)}) %collective-permute-start.24) | collective-permute-done | bytes 204832 | tf_op jit(solution)/shard_map/ppermute | solution.py:376
  100.2 7.0 %collective-permute-start.32 = (bf16[160,640]{1,0:T(8,128)(2,1)S(1)}, bf16[160,640]{1,0:T(8,128)(2,1)S(1)}, u32[]{:S(2)}, u32[]{:S(2)}) collective-permute-start(bf16[160,640]{1,0:T(8,128)(2,1)S(1)} %get-tuple-element.75), channel_id=1, source_target_pairs={{4,0},{8,4},{12,8},{14,12},{10,14},{6,10},{2,6},{0,2},{5,1},{9,5},... | collective-permute-start | bytes 614408 | tf_op jit(solution)/shard_map/ppermute | solution.py:374
  108.6 2.2 %collective-permute-start.33 = (bf16[160,640]{1,0:T(8,128)(2,1)S(1)}, bf16[160,640]{1,0:T(8,128)(2,1)S(1)}, u32[]{:S(2)}, u32[]{:S(2)}) collective-permute-start(bf16[160,640]{1,0:T(8,128)(2,1)S(1)} %shard_map.94.refs_2_), channel_id=1, source_target_pairs={{4,16},{8,20},{12,24},{14,28},{10,30},{6,26},{2,22},{0,18},{20,0},... | collective-permute-start | bytes 614408 | tf_op jit(solution)/shard_map/ppermute | solution.py:372
  113.5 1.9 %shard_map.97.refs_4_ = bf16[384,640]{1,0:T(8,128)(2,1)} custom-call(s32[3]{0:T(128)S(1)} %pad_add_fusion.meta.refs_0_, f32[384,640]{1,0:T(8,128)S(1)} %get-tuple-element.73.scaled, f32[384,2]{1,0:T(8,128)S(1)} %get-tuple-element.74.sums, f32[384,2]{1,0:T(8,128)S(1)} %collective-permute-done.30.came, bf16[384,1280]{1,0:T(8,128)(2,1)S(1)} %bitcast.17, ...), custom_call_target="tpu_custom_call" | custom-call | flops 1 | bytes 3449868 | tf_op jit(solution)/shard_map/pallas_call | solution.py:28
  (135 shorter events, 52.5 us)
Async XLA Ops:
  7.2 34.8 %collective-permute-start.12 = (bf16[2,192,1280]{2,1,0:T(8,128)(2,1)S(1)}, bf16[2,192,1280]{2,1,0:T(8,128)(2,1)}, u32[]{:S(2)}, u32[]{:S(2)}) collective-permute-start(bf16[2,192,1280]{2,1,0:T(8,128)(2,1)S(1)} %shard_map.79), channel_id=1, source_target_pairs={{0,16},{16,0},{1,17},{17,1},{2,18},{18,2},{3,19},{19,3},{4,20},{20... | collective-permute-start | bytes 2949128 | tf_op jit(solution)/shard_map/ppermute | solution.py:262
  10.2 8.0 %collective-permute-start.2 = (bf16[160,640]{1,0:T(8,128)(2,1)S(1)}, bf16[160,640]{1,0:T(8,128)(2,1)S(1)}, u32[]{:S(2)}, u32[]{:S(2)}) collective-permute-start(bf16[160,640]{1,0:T(8,128)(2,1)S(1)} %get-tuple-element.45.refs_0_), channel_id=1, source_target_pairs={{4,0},{8,4},{12,8},{14,12},{10,14},{6,10},{2,6},{0,2},{5,1},{9,5},... | collective-permute-start | bytes 614408 | tf_op jit(solution)/shard_map/ppermute | solution.py:277
  11.7 10.9 %collective-permute-start.3 = (bf16[160,640]{1,0:T(8,128)(2,1)S(1)}, bf16[160,640]{1,0:T(8,128)(2,1)S(1)}, u32[]{:S(2)}, u32[]{:S(2)}) collective-permute-start(bf16[160,640]{1,0:T(8,128)(2,1)S(1)} %get-tuple-element.46.refs_1_), channel_id=1, source_target_pairs={{4,0},{8,4},{12,8},{14,12},{10,14},{6,10},{2,6},{0,2},{5,1},{9,5},... | collective-permute-start | bytes 614408 | tf_op jit(solution)/shard_map/ppermute | solution.py:277
  13.3 10.8 %collective-permute-start = (bf16[160,640]{1,0:T(8,128)(2,1)S(1)}, bf16[160,640]{1,0:T(8,128)(2,1)S(1)}, u32[]{:S(2)}, u32[]{:S(2)}) collective-permute-start(bf16[160,640]{1,0:T(8,128)(2,1)S(1)} %get-tuple-element.45.refs_0_), channel_id=1, source_target_pairs={{0,4},{4,8},{8,12},{12,14},{14,10},{10,6},{6,2},{2,0},{1,5},{5,9},... | collective-permute-start | bytes 614408 | tf_op jit(solution)/shard_map/ppermute | solution.py:276
  13.7 10.9 %collective-permute-start.1 = (bf16[160,640]{1,0:T(8,128)(2,1)S(1)}, bf16[160,640]{1,0:T(8,128)(2,1)S(1)}, u32[]{:S(2)}, u32[]{:S(2)}) collective-permute-start(bf16[160,640]{1,0:T(8,128)(2,1)S(1)} %get-tuple-element.46.refs_1_), channel_id=1, source_target_pairs={{0,4},{4,8},{8,12},{12,14},{14,10},{10,6},{6,2},{2,0},{1,5},{5,9},... | collective-permute-start | bytes 614408 | tf_op jit(solution)/shard_map/ppermute | solution.py:276
  18.2 8.8 %collective-permute-start.6 = (bf16[160,640]{1,0:T(8,128)(2,1)S(1)}, bf16[160,640]{1,0:T(8,128)(2,1)S(1)}, u32[]{:S(2)}, u32[]{:S(2)}) collective-permute-start(bf16[160,640]{1,0:T(8,128)(2,1)S(1)} %collective-permute-done.2.refs_4_), channel_id=1, source_target_pairs={{4,0},{8,4},{12,8},{14,12},{10,14},{6,10},{2,6},{0,2},{5,1},{9,5},... | collective-permute-start | bytes 614408 | tf_op jit(solution)/shard_map/ppermute | solution.py:277
  22.6 8.8 %collective-permute-start.7 = (bf16[160,640]{1,0:T(8,128)(2,1)S(1)}, bf16[160,640]{1,0:T(8,128)(2,1)S(1)}, u32[]{:S(2)}, u32[]{:S(2)}) collective-permute-start(bf16[160,640]{1,0:T(8,128)(2,1)S(1)} %collective-permute-done.3.refs_5_), channel_id=1, source_target_pairs={{4,0},{8,4},{12,8},{14,12},{10,14},{6,10},{2,6},{0,2},{5,1},{9,5},... | collective-permute-start | bytes 614408 | tf_op jit(solution)/shard_map/ppermute | solution.py:277
  24.1 8.8 %collective-permute-start.4 = (bf16[160,640]{1,0:T(8,128)(2,1)S(1)}, bf16[160,640]{1,0:T(8,128)(2,1)S(1)}, u32[]{:S(2)}, u32[]{:S(2)}) collective-permute-start(bf16[160,640]{1,0:T(8,128)(2,1)S(1)} %collective-permute-done.refs_2_), channel_id=1, source_target_pairs={{0,4},{4,8},{8,12},{12,14},{14,10},{10,6},{6,2},{2,0},{1,5},{5,9},... | collective-permute-start | bytes 614408 | tf_op jit(solution)/shard_map/ppermute | solution.py:276
  24.6 8.8 %collective-permute-start.5 = (bf16[160,640]{1,0:T(8,128)(2,1)S(1)}, bf16[160,640]{1,0:T(8,128)(2,1)S(1)}, u32[]{:S(2)}, u32[]{:S(2)}) collective-permute-start(bf16[160,640]{1,0:T(8,128)(2,1)S(1)} %collective-permute-done.1.refs_3_), channel_id=1, source_target_pairs={{0,4},{4,8},{8,12},{12,14},{14,10},{10,6},{6,2},{2,0},{1,5},{5,9},... | collective-permute-start | bytes 614408 | tf_op jit(solution)/shard_map/ppermute | solution.py:276
  27.0 12.1 %collective-permute-start.10 = (bf16[160,640]{1,0:T(8,128)(2,1)S(1)}, bf16[160,640]{1,0:T(8,128)(2,1)S(1)}, u32[]{:S(2)}, u32[]{:S(2)}) collective-permute-start(bf16[160,640]{1,0:T(8,128)(2,1)S(1)} %collective-permute-done.6.refs_8_), channel_id=1, source_target_pairs={{4,0},{8,4},{12,8},{14,12},{10,14},{6,10},{2,6},{0,2},{5,1},{9,5},... | collective-permute-start | bytes 614408 | tf_op jit(solution)/shard_map/ppermute | solution.py:277
  41.9 15.6 %collective-permute-start.15 = (bf16[2,192,1280]{2,1,0:T(8,128)(2,1)}, bf16[2,192,1280]{2,1,0:T(8,128)(2,1)}, u32[]{:S(2)}, u32[]{:S(2)}) collective-permute-start(bf16[2,192,1280]{2,1,0:T(8,128)(2,1)} %shard_map.81.first), channel_id=1, source_target_pairs={{0,1},{1,0},{2,3},{3,2},{4,5},{5,4},{6,7},{7,6},{8,9},{9,8},{10,11... | collective-permute-start | bytes 2949128 | tf_op jit(solution)/shard_map/ppermute | solution.py:296
  55.4 12.7 %collective-permute-start.16 = (bf16[160,640]{1,0:T(8,128)(2,1)S(1)}, bf16[160,640]{1,0:T(8,128)(2,1)S(1)}, u32[]{:S(2)}, u32[]{:S(2)}) collective-permute-start(bf16[160,640]{1,0:T(8,128)(2,1)S(1)} %get-tuple-element.61), channel_id=1, source_target_pairs={{0,4},{4,8},{8,12},{12,14},{14,10},{10,6},{6,2},{2,0},{1,5},{5,9},... | collective-permute-start | bytes 614408 | tf_op jit(solution)/shard_map/ppermute | solution.py:374
  57.1 11.1 %collective-permute-start.17 = (bf16[160,640]{1,0:T(8,128)(2,1)S(1)}, bf16[160,640]{1,0:T(8,128)(2,1)}, u32[]{:S(2)}, u32[]{:S(2)}) collective-permute-start(bf16[160,640]{1,0:T(8,128)(2,1)S(1)} %get-tuple-element.62), channel_id=1, source_target_pairs={{4,0},{8,4},{12,8},{14,12},{10,14},{6,10},{2,6},{0,2},{5,1},{9,5},... | collective-permute-start | bytes 614408 | tf_op jit(solution)/shard_map/ppermute | solution.py:374
  68.8 12.4 %collective-permute-start.18 = (bf16[2,384,640]{2,1,0:T(8,128)(2,1)}, bf16[2,384,640]{2,1,0:T(8,128)(2,1)S(1)}, u32[]{:S(2)}, u32[]{:S(2)}) collective-permute-start(bf16[2,384,640]{2,1,0:T(8,128)(2,1)} %shard_map.86.refs_4_), channel_id=1, source_target_pairs={{0,1},{1,0},{2,3},{3,2},{4,5},{5,4},{6,7},{7,6},{8,9},{9,8},{10,11... | collective-permute-start | bytes 2949128 | tf_op jit(solution)/shard_map/ppermute | solution.py:383
  74.0 8.9 %collective-permute-start.21 = (bf16[160,640]{1,0:T(8,128)(2,1)S(1)}, bf16[160,640]{1,0:T(8,128)(2,1)S(1)}, u32[]{:S(2)}, u32[]{:S(2)}) collective-permute-start(bf16[160,640]{1,0:T(8,128)(2,1)S(1)} %get-tuple-element.64.refs_4_), channel_id=1, source_target_pairs={{0,4},{4,8},{8,12},{12,14},{14,10},{10,6},{6,2},{2,0},{1,5},{5,9},... | collective-permute-start | bytes 614408 | tf_op jit(solution)/shard_map/ppermute | solution.py:374
  79.2 11.1 %collective-permute-start.25 = (bf16[160,640]{1,0:T(8,128)(2,1)}, bf16[160,640]{1,0:T(8,128)(2,1)}, u32[]{:S(2)}, u32[]{:S(2)}) collective-permute-start(bf16[160,640]{1,0:T(8,128)(2,1)} %get-tuple-element.65.refs_3_), channel_id=1, source_target_pairs={{0,4},{4,8},{8,12},{12,14},{14,10},{10,6},{6,2},{2,0},{1,5},{5,9},... | collective-permute-start | bytes 614408 | tf_op jit(solution)/shard_map/ppermute | solution.py:374
  80.8 9.6 %collective-permute-start.26 = (bf16[160,640]{1,0:T(8,128)(2,1)}, bf16[160,640]{1,0:T(8,128)(2,1)}, u32[]{:S(2)}, u32[]{:S(2)}) collective-permute-start(bf16[160,640]{1,0:T(8,128)(2,1)} %get-tuple-element.69), channel_id=1, source_target_pairs={{4,0},{8,4},{12,8},{14,12},{10,14},{6,10},{2,6},{0,2},{5,1},{9,5},... | collective-permute-start | bytes 614408 | tf_op jit(solution)/shard_map/ppermute | solution.py:374
  83.6 27.2 %collective-permute-start.23 = (bf16[384,640]{1,0:T(8,128)(2,1)}, bf16[384,640]{1,0:T(8,128)(2,1)S(1)}, u32[]{:S(2)}, u32[]{:S(2)}) collective-permute-start(bf16[384,640]{1,0:T(8,128)(2,1)} %shard_map.90.refs_4_), channel_id=1, source_target_pairs={{0,16},{16,0},{1,17},{17,1},{2,18},{18,2},{3,19},{19,3},{4,20},{20... | collective-permute-start | bytes 1474568 | tf_op jit(solution)/shard_map/ppermute | solution.py:388
  84.2 16.0 %collective-permute-start.24 = (bf16[160,640]{1,0:T(8,128)(2,1)}, bf16[160,640]{1,0:T(8,128)(2,1)S(1)}, u32[]{:S(2)}, u32[]{:S(2)}) collective-permute-start(bf16[160,640]{1,0:T(8,128)(2,1)} %copy-done.29), channel_id=1, source_target_pairs={{0,16},{16,0},{1,17},{17,1},{2,18},{18,2},{3,19},{19,3},{4,20},{20... | collective-permute-start | bytes 614408 | tf_op jit(solution)/shard_map/ppermute | solution.py:376
  88.7 18.6 %collective-permute-start.29 = (bf16[160,640]{1,0:T(8,128)(2,1)S(1)}, bf16[160,640]{1,0:T(8,128)(2,1)S(1)}, u32[]{:S(2)}, u32[]{:S(2)}) collective-permute-start(bf16[160,640]{1,0:T(8,128)(2,1)S(1)} %get-tuple-element.70.refs_4_), channel_id=1, source_target_pairs={{0,4},{4,8},{8,12},{12,14},{14,10},{10,6},{6,2},{2,0},{1,5},{5,9},... | collective-permute-start | bytes 614408 | tf_op jit(solution)/shard_map/ppermute | solution.py:374
  91.5 16.5 %collective-permute-start.28 = (bf16[160,640]{1,0:T(8,128)(2,1)S(1)}, bf16[160,640]{1,0:T(8,128)(2,1)S(1)}, u32[]{:S(2)}, u32[]{:S(2)}) collective-permute-start(bf16[160,640]{1,0:T(8,128)(2,1)S(1)} %get-tuple-element.72), channel_id=1, source_target_pairs={{4,0},{8,4},{12,8},{14,12},{10,14},{6,10},{2,6},{0,2},{5,1},{9,5},... | collective-permute-start | bytes 614408 | tf_op jit(solution)/shard_map/ppermute | solution.py:374
  92.0 18.8 %collective-permute-start.27 = (bf16[160,640]{1,0:T(8,128)(2,1)S(1)}, bf16[160,640]{1,0:T(8,128)(2,1)S(1)}, u32[]{:S(2)}, u32[]{:S(2)}) collective-permute-start(bf16[160,640]{1,0:T(8,128)(2,1)S(1)} %get-tuple-element.71.refs_3_), channel_id=1, source_target_pairs={{0,20},{4,24},{8,28},{12,30},{14,26},{10,22},{6,18},{2,16},{16,4},... | collective-permute-start | bytes 614408 | tf_op jit(solution)/shard_map/ppermute | solution.py:372
  100.2 15.1 %collective-permute-start.32 = (bf16[160,640]{1,0:T(8,128)(2,1)S(1)}, bf16[160,640]{1,0:T(8,128)(2,1)S(1)}, u32[]{:S(2)}, u32[]{:S(2)}) collective-permute-start(bf16[160,640]{1,0:T(8,128)(2,1)S(1)} %get-tuple-element.75), channel_id=1, source_target_pairs={{4,0},{8,4},{12,8},{14,12},{10,14},{6,10},{2,6},{0,2},{5,1},{9,5},... | collective-permute-start | bytes 614408 | tf_op jit(solution)/shard_map/ppermute | solution.py:374
  108.6 8.4 %collective-permute-start.33 = (bf16[160,640]{1,0:T(8,128)(2,1)S(1)}, bf16[160,640]{1,0:T(8,128)(2,1)S(1)}, u32[]{:S(2)}, u32[]{:S(2)}) collective-permute-start(bf16[160,640]{1,0:T(8,128)(2,1)S(1)} %shard_map.94.refs_2_), channel_id=1, source_target_pairs={{4,16},{8,20},{12,24},{14,28},{10,30},{6,26},{2,22},{0,18},{20,0},... | collective-permute-start | bytes 614408 | tf_op jit(solution)/shard_map/ppermute | solution.py:372
  (42 other events, 154.4 us)

commit v10 on v9

--- a/solution.py
+++ b/solution.py
@@ -9,7 +9,6 @@
 
 BF16, F32 = jnp.bfloat16, jnp.float32
 VMEM = pl.BlockSpec(memory_space=pltpu.VMEM)
-HBM = pl.BlockSpec(memory_space=pltpu.HBM)
 ANY = pl.BlockSpec(memory_space=pl.ANY)
 SMEM = pl.BlockSpec(memory_space=pltpu.SMEM)
 
@@ -18,7 +17,7 @@
     return jax.ShapeDtypeStruct(dims, kind)
 
 
-def call(kernel, ins, out_shape, scratch=(), vmem=16, flops=1, pinned=(), ties=()):
+def call(kernel, ins, out_shape, scratch=(), vmem=16, flops=1, left=(), ties=()):
     count = len(ins)
 
     def body(*refs):
@@ -29,7 +28,7 @@
         body if ties else kernel,
         out_shape=out_shape,
         in_specs=[
-            SMEM if x.dtype == jnp.int32 else HBM if i in pinned else VMEM
+            SMEM if x.dtype == jnp.int32 else ANY if i in left else VMEM
             for i, x in enumerate(ins)
         ]
         + [ANY] * len(ties),
@@ -47,6 +46,7 @@
         in_specs=[ANY] * (1 + len(ties)),
         out_specs=ANY,
         input_output_aliases={0: 0},
+        compiler_params=pltpu.CompilerParams(vmem_limit_bytes=1 << 20),
         cost_estimate=pl.CostEstimate(flops=1, bytes_accessed=1, transcendentals=0),
     )(array, *ties)
 
@@ -108,28 +108,12 @@
     partial[...] = dot(normed[...], d_pre[...], 0, 0).astype(BF16)
 
 
-def place_kernel(index, *refs):
-    blocks, (up, down, sems) = refs[:-3], refs[-3:]
+def own_kernel(index, normed, grads, *refs):
+    blocks, (d_pre, partial, up, down) = refs[:-4], refs[-4:]
     depth = blocks[0].shape[0]
-    copies = []
     for i, block in enumerate(blocks):
         rows = pl.ds(pl.multiple_of(index[i // 2] * depth, depth), depth)
-        target = (up, down)[i % 2].at[rows]
-        copies.append(pltpu.make_async_copy(block, target, sems.at[i]))
-    for copy in copies:
-        copy.start()
-    for copy in copies:
-        copy.wait()
-
-
-def own_kernel(index, normed, grads, near_up, near_down, *refs):
-    d_pre, partial, up, down = refs[-4:]
-    up[...] = near_up[...]
-    down[...] = near_down[...]
-    for ref, far in zip((up, down), refs[:-4]):
-        depth = far.shape[0]
-        rows = pl.ds(pl.multiple_of(index[index.shape[0] - 1] * depth, depth), depth)
-        ref[rows, :] = far[...]
+        (up, down)[i % 2][rows, :] = block[...]
     back_through(normed, grads, up, down, d_pre, partial)
 
 
@@ -257,7 +241,8 @@
         shape((2, half_rows, width), BF16),
         [pltpu.SemaphoreType.DMA((2,))] + [pltpu.VMEM((half_rows, width), BF16)] * 2,
         flops=5 * frame_len * width,
-        pinned=(2, 3),
+        vmem=60,
+        left=(2, 3),
     )
     first = lax.ppermute(passing, "groups", swap)
     normed, grads, stats = call(
@@ -282,23 +267,16 @@
         index = jnp.stack([ring_member(place + step + peers, peers) for step in steps])
         index = index.astype(jnp.int32)
         blocks = [block for step in blocks for block in blocks[step]]
-        near = call(
-            place_kernel,
-            (index, *blocks),
-            (weight, weight),
-            [pltpu.SemaphoreType.DMA((len(blocks),))],
-            pinned=range(1, len(blocks) + 1),
-        )
-        far = [lax.ppermute(up[0], "gx", ahead), lax.ppermute(down[1], "gx", behind)]
+        blocks += [lax.ppermute(up[0], "gx", ahead), lax.ppermute(down[1], "gx", behind)]
     else:
-        near = [lax.all_gather(block, "gx", axis=0, tiled=True) for block in mine]
-        index, far = jnp.zeros((1,), jnp.int32), []
+        blocks = [lax.all_gather(block, "gx", axis=0, tiled=True) for block in mine]
+        index = jnp.zeros((1,), jnp.int32)
     second = lax.ppermute(first, "gy", swap)
 
     d_pre_of, partial_of = shape((frame_len, quarter), BF16), shape((width, quarter), BF16)
     d_pre_own, partial_own, full_up, full_down = call(
         own_kernel,
-        (index, normed, grads, *near, *far),
+        (index, normed, grads, *blocks),
         (d_pre_of, partial_of, weight, weight),
         flops=6 * frame_len * width * quarter,
     )
@@ -382,14 +360,14 @@
         send = hold(send, came[0]["up"], came[0]["down"])
         sent = lax.ppermute(send, "gy", swap)
         tie = hop(0, 1, send)
-        tie = hop(1, 1, tie)
+        tie = hop(1, 1, tie, came[1]["own"])
         over = over_cores(keep, sent, tie)
         over = hold(over, came[0]["up"], came[0]["down"])
         back = lax.ppermute(over, "groups", swap)
         tie = hop(0, 2, over)
         tie = hop(1, 2, tie)
         for turn in range(3, half):
-            tie = hop(1, turn, hop(0, turn, tie, came[1]["own"]))
+            tie = hop(1, turn, hop(0, turn, tie))
         other = call(
             add_kernel, (came[1]["own"], came[1]["up"]), shape((depth, quarter), F32), ties=(tie,)
         )

time: 119 us -> 116 us (0.975)
  waiting for transfers between devices: 22.7 us -> 30.8 us
  local copies, waits for them, and re-layouts: 21.2 us -> 16.4 us
  Pallas kernels: 30.9 us -> 26.4 us
  starting transfers between devices: 42.6 us -> 39.9 us
    ppermute x1, waiting for transfers between devices: 6.69 us -> 0.01 us  [hop(): came[i]['own'] = lax.ppermute(blocks[-1], 'groups', swap)]
    ppermute x12, waiting for transfers between devices: 1.73 us -> 7.27 us  [hop(): came[i][name] = lax.ppermute(block, 'gx', ahead if name == 'up' else behind)]
    unnamed x64, local copies, waits for them, and re-layouts: 20.1 us -> 14.7 us
    ppermute x1, waiting for transfers between devices: 0.2 us -> 5.08 us  [shards(): lax.ppermute(up[0], 'gx', ahead)]
    ppermute x2, waiting for transfers between devices: 0.01 us -> 4.68 us  [hop(): came[i][name] = lax.ppermute(block, ('groups', 'gx'), across[name])]
    pallas_call x20 -> x19, Pallas kernels: 30.9 us -> 26.4 us  [call(): pl.pallas_call(body if ties else kernel, out_shape=out_shape, in_specs=[S...]
    ppermute x12, starting transfers between devices: 17.4 us -> 15.4 us  [hop(): came[i][name] = lax.ppermute(block, 'gx', ahead if name == 'up' else behind)]
  transfers between devices with their start and end apart: 34 -> 34, of which waited for: 11 -> 14; matrix products, arithmetic and copies ran while one was open for 0% -> 1% of each run, Pallas kernels for 23% -> 19%
where the time goes in v10:
time: 116 us; the launch traced here: 115 us
  starting transfers between devices  39.9 us (34%)
  waiting for transfers between devices  30.8 us (27%)
  Pallas kernels  26.4 us (23%)
  local copies, waits for them, and re-layouts  16.4 us (14%)
    pallas_call x19, Pallas kernels, call(): pl.pallas_call(body if ties else kernel, out_shape=out_shape, in_specs=[S...  26.4 us
    ppermute x12, starting transfers between devices, hop(): came[i][name] = lax.ppermute(block, 'gx', ahead if name == 'up' else behind)  15.4 us
    unnamed x64, local copies, waits for them, and re-layouts  14.7 us
    ppermute x6, waiting for transfers between devices, shards(): down = [lax.ppermute(block, 'gx', behind) for block in down]  9.69 us
    ppermute x6, starting transfers between devices, shards(): down = [lax.ppermute(block, 'gx', behind) for block in down]  8.59 us
    ppermute x12, waiting for transfers between devices, hop(): came[i][name] = lax.ppermute(block, 'gx', ahead if name == 'up' else behind)  7.27 us
    ppermute x6, starting transfers between devices, shards(): up = [lax.ppermute(block, 'gx', ahead) for block in up]  5.12 us
    ppermute x1, waiting for transfers between devices, shards(): lax.ppermute(up[0], 'gx', ahead)  5.08 us
  transfers between devices with their start and end apart: 34, of which 14 were waited for; matrix products, arithmetic and copies ran while one was open for 1% of the time, Pallas kernels for 19%

profile of v10, /device:TPU:0, one launch (start us, length us, event | category | flops | bytes accessed | tf_op | source)
XLA Modules:
  0.0 115.1 jit_solution(11951916731298398667)
XLA Ops:
  2.4 3.2 %shard_map.78 = bf16[2,192,1280]{2,1,0:T(8,128)(2,1)} custom-call(s32[3]{0:T(128)} %pad_add_fusion.meta.refs_0_, s32[8]{0:T(128)} %lengths.1, bf16[384,1280]{1,0:T(8,128)(2,1)} %bitcast.14, bf16[384,1280]{1,0:T(8,128)(2,1)} %bitcast.18, f32[1280]{0:T(1024)} %gain.1), custom_call_target="tpu_custom_call" | custom-call | flops 2457600 | bytes 2954284 | tf_op jit(solution)/shard_map/pallas_call | solution.py:27
  5.6 3.0 %collective-permute-start.12 = (bf16[2,192,1280]{2,1,0:T(8,128)(2,1)}, bf16[2,192,1280]{2,1,0:T(8,128)(2,1)}, u32[]{:S(2)}, u32[]{:S(2)}) collective-permute-start(bf16[2,192,1280]{2,1,0:T(8,128)(2,1)} %shard_map.78), channel_id=1, source_target_pairs={{0,16},{16,0},{1,17},{17,1},{2,18},{18,2},{3,19},{19,3},{4,20},{20... | collective-permute-start | bytes 2949128 | tf_op jit(solution)/shard_map/ppermute | solution.py:247
  10.1 1.6 %collective-permute-start.3 = (bf16[160,640]{1,0:T(8,128)(2,1)S(1)}, bf16[160,640]{1,0:T(8,128)(2,1)S(1)}, u32[]{:S(2)}, u32[]{:S(2)}) collective-permute-start(bf16[160,640]{1,0:T(8,128)(2,1)S(1)} %get-tuple-element.44.refs_1_), channel_id=1, source_target_pairs={{4,0},{8,4},{12,8},{14,12},{10,14},{6,10},{2,6},{0,2},{5,1},{9,5},... | collective-permute-start | bytes 614408 | tf_op jit(solution)/shard_map/ppermute | solution.py:262
  12.6 3.9 %collective-permute-done.2.refs_4_ = bf16[160,640]{1,0:T(8,128)(2,1)S(1)} collective-permute-done((bf16[160,640]{1,0:T(8,128)(2,1)S(1)}, bf16[160,640]{1,0:T(8,128)(2,1)S(1)}, u32[]{:S(2)}, u32[]{:S(2)}) %collective-permute-start.2) | collective-permute-done | bytes 204832 | tf_op jit(solution)/shard_map/ppermute | solution.py:262
  16.6 1.5 %collective-permute-start.6 = (bf16[160,640]{1,0:T(8,128)(2,1)S(1)}, bf16[160,640]{1,0:T(8,128)(2,1)S(1)}, u32[]{:S(2)}, u32[]{:S(2)}) collective-permute-start(bf16[160,640]{1,0:T(8,128)(2,1)S(1)} %collective-permute-done.2.refs_4_), channel_id=1, source_target_pairs={{4,0},{8,4},{12,8},{14,12},{10,14},{6,10},{2,6},{0,2},{5,1},{9,5},... | collective-permute-start | bytes 614408 | tf_op jit(solution)/shard_map/ppermute | solution.py:262
  18.1 2.9 %collective-permute-done.3.refs_5_ = bf16[160,640]{1,0:T(8,128)(2,1)S(1)} collective-permute-done((bf16[160,640]{1,0:T(8,128)(2,1)S(1)}, bf16[160,640]{1,0:T(8,128)(2,1)S(1)}, u32[]{:S(2)}, u32[]{:S(2)}) %collective-permute-start.3) | collective-permute-done | bytes 204832 | tf_op jit(solution)/shard_map/ppermute | solution.py:262
  23.7 1.6 %collective-permute-start.5 = (bf16[160,640]{1,0:T(8,128)(2,1)S(1)}, bf16[160,640]{1,0:T(8,128)(2,1)S(1)}, u32[]{:S(2)}, u32[]{:S(2)}) collective-permute-start(bf16[160,640]{1,0:T(8,128)(2,1)S(1)} %collective-permute-done.1.refs_3_), channel_id=1, source_target_pairs={{0,4},{4,8},{8,12},{12,14},{14,10},{10,6},{6,2},{2,0},{1,5},{5,9},... | collective-permute-start | bytes 614408 | tf_op jit(solution)/shard_map/ppermute | solution.py:261
  26.9 2.9 %collective-permute-done.7.refs_9_ = bf16[160,640]{1,0:T(8,128)(2,1)S(1)} collective-permute-done((bf16[160,640]{1,0:T(8,128)(2,1)S(1)}, bf16[160,640]{1,0:T(8,128)(2,1)S(1)}, u32[]{:S(2)}, u32[]{:S(2)}) %collective-permute-start.7) | collective-permute-done | bytes 204832 | tf_op jit(solution)/shard_map/ppermute | solution.py:262
  31.8 1.6 %collective-permute-start.9 = (bf16[160,640]{1,0:T(8,128)(2,1)S(1)}, bf16[160,640]{1,0:T(8,128)(2,1)S(1)}, u32[]{:S(2)}, u32[]{:S(2)}) collective-permute-start(bf16[160,640]{1,0:T(8,128)(2,1)S(1)} %collective-permute-done.5.refs_7_), channel_id=1, source_target_pairs={{0,4},{4,8},{8,12},{12,14},{14,10},{10,6},{6,2},{2,0},{1,5},{5,9},... | collective-permute-start | bytes 614408 | tf_op jit(solution)/shard_map/ppermute | solution.py:261
  37.6 2.1 %collective-permute-done.9.refs_11_ = bf16[160,640]{1,0:T(8,128)(2,1)S(1)} collective-permute-done((bf16[160,640]{1,0:T(8,128)(2,1)S(1)}, bf16[160,640]{1,0:T(8,128)(2,1)S(1)}, u32[]{:S(2)}, u32[]{:S(2)}) %collective-permute-start.9) | collective-permute-done | bytes 204832 | tf_op jit(solution)/shard_map/ppermute | solution.py:261
  40.4 1.5 %collective-permute-start.14 = (bf16[160,640]{1,0:T(8,128)(2,1)}, bf16[160,640]{1,0:T(8,128)(2,1)}, u32[]{:S(2)}, u32[]{:S(2)}) collective-permute-start(bf16[160,640]{1,0:T(8,128)(2,1)} %collective-permute-done.11.refs_13_), channel_id=1, source_target_pairs={{4,0},{8,4},{12,8},{14,12},{10,14},{6,10},{2,6},{0,2},{5,1},{9,5},... | collective-permute-start | bytes 614408 | tf_op jit(solution)/shard_map/ppermute | solution.py:270
  42.5 5.1 %collective-permute-done.13.refs_14_ = bf16[160,640]{1,0:T(8,128)(2,1)} collective-permute-done((bf16[160,640]{1,0:T(8,128)(2,1)}, bf16[160,640]{1,0:T(8,128)(2,1)}, u32[]{:S(2)}, u32[]{:S(2)}) %collective-permute-start.13) | collective-permute-done | bytes 204832 | tf_op jit(solution)/shard_map/ppermute | solution.py:270
  57.7 4.2 %shard_map.79 = (bf16[384,640]{1,0:T(8,128)(2,1)S(1)}, bf16[1280,640]{1,0:T(8,128)(2,1)S(1)}, bf16[1280,640]{1,0:T(8,128)(2,1)S(1)}, bf16[1280,640]{1,0:T(8,128)(2,1)S(1)}) custom-call(s32[8]{0:T(128)S(1)} %copy-done.7, bf16[384,1280]{1,0:T(8,128)(2,1)S(1)} %get-tuple-element.41.normed.refs_1_, bf16[384,1280]{1,0:T(8,128)(2,1)S(1)} %copy-done.4, ...), custom_call_target="tpu_custom_call" | custom-call | flops 1887436800 | bytes 10649632 | tf_op jit(solution)/shard_map/pallas_call | solution.py:27
  62.5 1.6 %collective-permute-start.16 = (bf16[160,640]{1,0:T(8,128)(2,1)S(1)}, bf16[160,640]{1,0:T(8,128)(2,1)S(1)}, u32[]{:S(2)}, u32[]{:S(2)}) collective-permute-start(bf16[160,640]{1,0:T(8,128)(2,1)S(1)} %get-tuple-element.57), channel_id=1, source_target_pairs={{0,4},{4,8},{8,12},{12,14},{14,10},{10,6},{6,2},{2,0},{1,5},{5,9},... | collective-permute-start | bytes 614408 | tf_op jit(solution)/shard_map/ppermute | solution.py:352
  64.6 4.2 %shard_map.81 = (bf16[384,640]{1,0:T(8,128)(2,1)S(1)}, bf16[1280,640]{1,0:T(8,128)(2,1)S(1)}) custom-call(bf16[2,192,1280]{2,1,0:T(8,128)(2,1)} %shard_map.80.first, bf16[2,192,1280]{2,1,0:T(8,128)(2,1)} %collective-permute-done.15.second, bf16[1280,640]{1,0:T(8,128)(2,1)S(1)} %get-tuple-element.49.up.refs_3_, bf16[1280,640]{1,0:T(8,128)(2,1)S(1)} %get-tuple-element.50.down), custom_call_target="tpu_custom_call" | custom-call | flops 1887436800 | bytes 7372800 | tf_op jit(solution)/shard_map/pallas_call | solution.py:27
  69.4 2.5 %shard_map.83 = (bf16[2,384,640]{2,1,0:T(8,128)(2,1)S(1)}, bf16[2,384,640]{2,1,0:T(8,128)(2,1)S(1)}) custom-call(s32[3]{0:T(128)S(1)} %copy-done.10, bf16[384,640]{1,0:T(8,128)(2,1)S(1)} %get-tuple-element.47.refs_1_, bf16[384,640]{1,0:T(8,128)(2,1)S(1)} %get-tuple-element.51.refs_2_, bf16[1280,640]{1,0:T(8,128)(2,1)S(1)} %get-tuple-element.49.up.refs_3_, ...), custom_call_target="tpu_custom_call" | custom-call | flops 1258291200 | bytes 4587532 | tf_op jit(solution)/shard_map/pallas_call | solution.py:27
  72.1 1.6 %collective-permute-start.19 = (bf16[160,640]{1,0:T(8,128)(2,1)S(1)}, bf16[160,640]{1,0:T(8,128)(2,1)S(1)}, u32[]{:S(2)}, u32[]{:S(2)}) collective-permute-start(bf16[160,640]{1,0:T(8,128)(2,1)S(1)} %get-tuple-element.53.refs_4_), channel_id=1, source_target_pairs={{0,4},{4,8},{8,12},{12,14},{14,10},{10,6},{6,2},{2,0},{1,5},{5,9},... | collective-permute-start | bytes 614408 | tf_op jit(solution)/shard_map/ppermute | solution.py:352
  76.9 3.0 %collective-permute-done.19.refs_2_ = bf16[160,640]{1,0:T(8,128)(2,1)S(1)} collective-permute-done((bf16[160,640]{1,0:T(8,128)(2,1)S(1)}, bf16[160,640]{1,0:T(8,128)(2,1)S(1)}, u32[]{:S(2)}, u32[]{:S(2)}) %collective-permute-start.19) | collective-permute-done | bytes 204832 | tf_op jit(solution)/shard_map/ppermute | solution.py:352
  84.9 2.6 %collective-permute-done.23.refs_2_.refs_3_ = bf16[160,640]{1,0:T(8,128)(2,1)S(1)} collective-permute-done((bf16[160,640]{1,0:T(8,128)(2,1)S(1)}, bf16[160,640]{1,0:T(8,128)(2,1)S(1)}, u32[]{:S(2)}, u32[]{:S(2)}) %collective-permute-start.23) | collective-permute-done | bytes 204832 | tf_op jit(solution)/shard_map/ppermute | solution.py:352
  91.2 1.6 %collective-permute-start.28 = (bf16[160,640]{1,0:T(8,128)(2,1)S(1)}, bf16[160,640]{1,0:T(8,128)(2,1)S(1)}, u32[]{:S(2)}, u32[]{:S(2)}) collective-permute-start(bf16[160,640]{1,0:T(8,128)(2,1)S(1)} %get-tuple-element.68), channel_id=1, source_target_pairs={{4,0},{8,4},{12,8},{14,12},{10,14},{6,10},{2,6},{0,2},{5,1},{9,5},... | collective-permute-start | bytes 614408 | tf_op jit(solution)/shard_map/ppermute | solution.py:352
  96.2 2.5 %collective-permute-start.31 = (bf16[160,640]{1,0:T(8,128)(2,1)S(1)}, bf16[160,640]{1,0:T(8,128)(2,1)S(1)}, u32[]{:S(2)}, u32[]{:S(2)}) collective-permute-start(bf16[160,640]{1,0:T(8,128)(2,1)S(1)} %shard_map.92.refs_3_), channel_id=1, source_target_pairs={{0,4},{4,8},{8,12},{12,14},{14,10},{10,6},{6,2},{2,0},{1,5},{5,9},... | collective-permute-start | bytes 614408 | tf_op jit(solution)/shard_map/ppermute | solution.py:352
  99.9 2.8 %collective-permute-start.33 = (bf16[160,640]{1,0:T(8,128)(2,1)S(1)}, bf16[160,640]{1,0:T(8,128)(2,1)S(1)}, u32[]{:S(2)}, u32[]{:S(2)}) collective-permute-start(bf16[160,640]{1,0:T(8,128)(2,1)S(1)} %shard_map.93.refs_2_), channel_id=1, source_target_pairs={{4,16},{8,20},{12,24},{14,28},{10,30},{6,26},{2,22},{0,18},{20,0},... | collective-permute-start | bytes 614408 | tf_op jit(solution)/shard_map/ppermute | solution.py:350
  102.7 4.7 %collective-permute-done.27.refs_1_ = bf16[160,640]{1,0:T(8,128)(2,1)S(1)} collective-permute-done((bf16[160,640]{1,0:T(8,128)(2,1)S(1)}, bf16[160,640]{1,0:T(8,128)(2,1)S(1)}, u32[]{:S(2)}, u32[]{:S(2)}) %collective-permute-start.27) | collective-permute-done | bytes 204832 | tf_op jit(solution)/shard_map/ppermute | solution.py:350
  110.0 1.9 %shard_map.96.refs_4_ = bf16[384,640]{1,0:T(8,128)(2,1)} custom-call(s32[3]{0:T(128)S(1)} %copy-done.10, f32[384,640]{1,0:T(8,128)S(1)} %get-tuple-element.69.scaled, f32[384,2]{1,0:T(8,128)S(1)} %get-tuple-element.70.sums, f32[384,2]{1,0:T(8,128)S(1)} %collective-permute-done.30.came, bf16[384,1280]{1,0:T(8,128)(2,1)S(1)} %bitcast.17, ...), custom_call_target="tpu_custom_call" | custom-call | flops 1 | bytes 3449868 | tf_op jit(solution)/shard_map/pallas_call | solution.py:27
  (134 shorter events, 50.0 us)
Async XLA Ops:
  5.6 34.1 %collective-permute-start.12 = (bf16[2,192,1280]{2,1,0:T(8,128)(2,1)}, bf16[2,192,1280]{2,1,0:T(8,128)(2,1)}, u32[]{:S(2)}, u32[]{:S(2)}) collective-permute-start(bf16[2,192,1280]{2,1,0:T(8,128)(2,1)} %shard_map.78), channel_id=1, source_target_pairs={{0,16},{16,0},{1,17},{17,1},{2,18},{18,2},{3,19},{19,3},{4,20},{20... | collective-permute-start | bytes 2949128 | tf_op jit(solution)/shard_map/ppermute | solution.py:247
  8.6 8.0 %collective-permute-start.2 = (bf16[160,640]{1,0:T(8,128)(2,1)S(1)}, bf16[160,640]{1,0:T(8,128)(2,1)S(1)}, u32[]{:S(2)}, u32[]{:S(2)}) collective-permute-start(bf16[160,640]{1,0:T(8,128)(2,1)S(1)} %get-tuple-element.43.refs_0_), channel_id=1, source_target_pairs={{4,0},{8,4},{12,8},{14,12},{10,14},{6,10},{2,6},{0,2},{5,1},{9,5},... | collective-permute-start | bytes 614408 | tf_op jit(solution)/shard_map/ppermute | solution.py:262
  10.1 10.9 %collective-permute-start.3 = (bf16[160,640]{1,0:T(8,128)(2,1)S(1)}, bf16[160,640]{1,0:T(8,128)(2,1)S(1)}, u32[]{:S(2)}, u32[]{:S(2)}) collective-permute-start(bf16[160,640]{1,0:T(8,128)(2,1)S(1)} %get-tuple-element.44.refs_1_), channel_id=1, source_target_pairs={{4,0},{8,4},{12,8},{14,12},{10,14},{6,10},{2,6},{0,2},{5,1},{9,5},... | collective-permute-start | bytes 614408 | tf_op jit(solution)/shard_map/ppermute | solution.py:262
  11.7 10.8 %collective-permute-start = (bf16[160,640]{1,0:T(8,128)(2,1)S(1)}, bf16[160,640]{1,0:T(8,128)(2,1)S(1)}, u32[]{:S(2)}, u32[]{:S(2)}) collective-permute-start(bf16[160,640]{1,0:T(8,128)(2,1)S(1)} %get-tuple-element.43.refs_0_), channel_id=1, source_target_pairs={{0,4},{4,8},{8,12},{12,14},{14,10},{10,6},{6,2},{2,0},{1,5},{5,9},... | collective-permute-start | bytes 614408 | tf_op jit(solution)/shard_map/ppermute | solution.py:261
  12.1 11.6 %collective-permute-start.1 = (bf16[160,640]{1,0:T(8,128)(2,1)S(1)}, bf16[160,640]{1,0:T(8,128)(2,1)S(1)}, u32[]{:S(2)}, u32[]{:S(2)}) collective-permute-start(bf16[160,640]{1,0:T(8,128)(2,1)S(1)} %get-tuple-element.44.refs_1_), channel_id=1, source_target_pairs={{0,4},{4,8},{8,12},{12,14},{14,10},{10,6},{6,2},{2,0},{1,5},{5,9},... | collective-permute-start | bytes 614408 | tf_op jit(solution)/shard_map/ppermute | solution.py:261
  16.6 9.4 %collective-permute-start.6 = (bf16[160,640]{1,0:T(8,128)(2,1)S(1)}, bf16[160,640]{1,0:T(8,128)(2,1)S(1)}, u32[]{:S(2)}, u32[]{:S(2)}) collective-permute-start(bf16[160,640]{1,0:T(8,128)(2,1)S(1)} %collective-permute-done.2.refs_4_), channel_id=1, source_target_pairs={{4,0},{8,4},{12,8},{14,12},{10,14},{6,10},{2,6},{0,2},{5,1},{9,5},... | collective-permute-start | bytes 614408 | tf_op jit(solution)/shard_map/ppermute | solution.py:262
  21.0 8.8 %collective-permute-start.7 = (bf16[160,640]{1,0:T(8,128)(2,1)S(1)}, bf16[160,640]{1,0:T(8,128)(2,1)S(1)}, u32[]{:S(2)}, u32[]{:S(2)}) collective-permute-start(bf16[160,640]{1,0:T(8,128)(2,1)S(1)} %collective-permute-done.3.refs_5_), channel_id=1, source_target_pairs={{4,0},{8,4},{12,8},{14,12},{10,14},{6,10},{2,6},{0,2},{5,1},{9,5},... | collective-permute-start | bytes 614408 | tf_op jit(solution)/shard_map/ppermute | solution.py:262
  22.5 8.8 %collective-permute-start.4 = (bf16[160,640]{1,0:T(8,128)(2,1)S(1)}, bf16[160,640]{1,0:T(8,128)(2,1)S(1)}, u32[]{:S(2)}, u32[]{:S(2)}) collective-permute-start(bf16[160,640]{1,0:T(8,128)(2,1)S(1)} %collective-permute-done.refs_2_), channel_id=1, source_target_pairs={{0,4},{4,8},{8,12},{12,14},{14,10},{10,6},{6,2},{2,0},{1,5},{5,9},... | collective-permute-start | bytes 614408 | tf_op jit(solution)/shard_map/ppermute | solution.py:261
  23.7 8.1 %collective-permute-start.5 = (bf16[160,640]{1,0:T(8,128)(2,1)S(1)}, bf16[160,640]{1,0:T(8,128)(2,1)S(1)}, u32[]{:S(2)}, u32[]{:S(2)}) collective-permute-start(bf16[160,640]{1,0:T(8,128)(2,1)S(1)} %collective-permute-done.1.refs_3_), channel_id=1, source_target_pairs={{0,4},{4,8},{8,12},{12,14},{14,10},{10,6},{6,2},{2,0},{1,5},{5,9},... | collective-permute-start | bytes 614408 | tf_op jit(solution)/shard_map/ppermute | solution.py:261
  25.9 11.2 %collective-permute-start.10 = (bf16[160,640]{1,0:T(8,128)(2,1)S(1)}, bf16[160,640]{1,0:T(8,128)(2,1)S(1)}, u32[]{:S(2)}, u32[]{:S(2)}) collective-permute-start(bf16[160,640]{1,0:T(8,128)(2,1)S(1)} %collective-permute-done.6.refs_8_), channel_id=1, source_target_pairs={{4,0},{8,4},{12,8},{14,12},{10,14},{6,10},{2,6},{0,2},{5,1},{9,5},... | collective-permute-start | bytes 614408 | tf_op jit(solution)/shard_map/ppermute | solution.py:262
  31.8 7.9 %collective-permute-start.9 = (bf16[160,640]{1,0:T(8,128)(2,1)S(1)}, bf16[160,640]{1,0:T(8,128)(2,1)S(1)}, u32[]{:S(2)}, u32[]{:S(2)}) collective-permute-start(bf16[160,640]{1,0:T(8,128)(2,1)S(1)} %collective-permute-done.5.refs_7_), channel_id=1, source_target_pairs={{0,4},{4,8},{8,12},{12,14},{14,10},{10,6},{6,2},{2,0},{1,5},{5,9},... | collective-permute-start | bytes 614408 | tf_op jit(solution)/shard_map/ppermute | solution.py:261
  39.7 24.9 %collective-permute-start.15 = (bf16[2,192,1280]{2,1,0:T(8,128)(2,1)}, bf16[2,192,1280]{2,1,0:T(8,128)(2,1)}, u32[]{:S(2)}, u32[]{:S(2)}) collective-permute-start(bf16[2,192,1280]{2,1,0:T(8,128)(2,1)} %shard_map.80.first), channel_id=1, source_target_pairs={{0,1},{1,0},{2,3},{3,2},{4,5},{5,4},{6,7},{7,6},{8,9},{9,8},{10,11... | collective-permute-start | bytes 2949128 | tf_op jit(solution)/shard_map/ppermute | solution.py:274
  62.5 9.5 %collective-permute-start.16 = (bf16[160,640]{1,0:T(8,128)(2,1)S(1)}, bf16[160,640]{1,0:T(8,128)(2,1)S(1)}, u32[]{:S(2)}, u32[]{:S(2)}) collective-permute-start(bf16[160,640]{1,0:T(8,128)(2,1)S(1)} %get-tuple-element.57), channel_id=1, source_target_pairs={{0,4},{4,8},{8,12},{12,14},{14,10},{10,6},{6,2},{2,0},{1,5},{5,9},... | collective-permute-start | bytes 614408 | tf_op jit(solution)/shard_map/ppermute | solution.py:352
  64.1 7.8 %collective-permute-start.17 = (bf16[160,640]{1,0:T(8,128)(2,1)S(1)}, bf16[160,640]{1,0:T(8,128)(2,1)S(1)}, u32[]{:S(2)}, u32[]{:S(2)}) collective-permute-start(bf16[160,640]{1,0:T(8,128)(2,1)S(1)} %get-tuple-element.58), channel_id=1, source_target_pairs={{4,0},{8,4},{12,8},{14,12},{10,14},{6,10},{2,6},{0,2},{5,1},{9,5},... | collective-permute-start | bytes 614408 | tf_op jit(solution)/shard_map/ppermute | solution.py:352
  72.0 12.3 %collective-permute-start.18 = (bf16[2,384,640]{2,1,0:T(8,128)(2,1)S(1)}, bf16[2,384,640]{2,1,0:T(8,128)(2,1)S(1)}, u32[]{:S(2)}, u32[]{:S(2)}) collective-permute-start(bf16[2,384,640]{2,1,0:T(8,128)(2,1)S(1)} %shard_map.85.refs_4_), channel_id=1, source_target_pairs={{0,1},{1,0},{2,3},{3,2},{4,5},{5,4},{6,7},{7,6},{8,9},{9,8},{10,11... | collective-permute-start | bytes 2949128 | tf_op jit(solution)/shard_map/ppermute | solution.py:361
  72.1 7.9 %collective-permute-start.19 = (bf16[160,640]{1,0:T(8,128)(2,1)S(1)}, bf16[160,640]{1,0:T(8,128)(2,1)S(1)}, u32[]{:S(2)}, u32[]{:S(2)}) collective-permute-start(bf16[160,640]{1,0:T(8,128)(2,1)S(1)} %get-tuple-element.53.refs_4_), channel_id=1, source_target_pairs={{0,4},{4,8},{8,12},{12,14},{14,10},{10,6},{6,2},{2,0},{1,5},{5,9},... | collective-permute-start | bytes 614408 | tf_op jit(solution)/shard_map/ppermute | solution.py:352
  75.5 9.5 %collective-permute-start.22 = (bf16[160,640]{1,0:T(8,128)(2,1)S(1)}, bf16[160,640]{1,0:T(8,128)(2,1)S(1)}, u32[]{:S(2)}, u32[]{:S(2)}) collective-permute-start(bf16[160,640]{1,0:T(8,128)(2,1)S(1)} %get-tuple-element.60.refs_4_), channel_id=1, source_target_pairs={{0,4},{4,8},{8,12},{12,14},{14,10},{10,6},{6,2},{2,0},{1,5},{5,9},... | collective-permute-start | bytes 614408 | tf_op jit(solution)/shard_map/ppermute | solution.py:352
  82.2 8.2 %collective-permute-start.25 = (bf16[160,640]{1,0:T(8,128)(2,1)S(1)}, bf16[160,640]{1,0:T(8,128)(2,1)S(1)}, u32[]{:S(2)}, u32[]{:S(2)}) collective-permute-start(bf16[160,640]{1,0:T(8,128)(2,1)S(1)} %get-tuple-element.62.refs_3_), channel_id=1, source_target_pairs={{0,4},{4,8},{8,12},{12,14},{14,10},{10,6},{6,2},{2,0},{1,5},{5,9},... | collective-permute-start | bytes 614408 | tf_op jit(solution)/shard_map/ppermute | solution.py:352
  87.6 19.8 %collective-permute-start.24 = (bf16[384,640]{1,0:T(8,128)(2,1)S(1)}, bf16[384,640]{1,0:T(8,128)(2,1)S(1)}, u32[]{:S(2)}, u32[]{:S(2)}) collective-permute-start(bf16[384,640]{1,0:T(8,128)(2,1)S(1)} %shard_map.89.refs_4_), channel_id=1, source_target_pairs={{0,16},{16,0},{1,17},{17,1},{2,18},{18,2},{3,19},{19,3},{4,20},{20... | collective-permute-start | bytes 1474568 | tf_op jit(solution)/shard_map/ppermute | solution.py:366
  91.2 8.1 %collective-permute-start.28 = (bf16[160,640]{1,0:T(8,128)(2,1)S(1)}, bf16[160,640]{1,0:T(8,128)(2,1)S(1)}, u32[]{:S(2)}, u32[]{:S(2)}) collective-permute-start(bf16[160,640]{1,0:T(8,128)(2,1)S(1)} %get-tuple-element.68), channel_id=1, source_target_pairs={{4,0},{8,4},{12,8},{14,12},{10,14},{6,10},{2,6},{0,2},{5,1},{9,5},... | collective-permute-start | bytes 614408 | tf_op jit(solution)/shard_map/ppermute | solution.py:352
  92.8 14.5 %collective-permute-start.27 = (bf16[160,640]{1,0:T(8,128)(2,1)S(1)}, bf16[160,640]{1,0:T(8,128)(2,1)S(1)}, u32[]{:S(2)}, u32[]{:S(2)}) collective-permute-start(bf16[160,640]{1,0:T(8,128)(2,1)S(1)} %get-tuple-element.67.refs_3_), channel_id=1, source_target_pairs={{0,20},{4,24},{8,28},{12,30},{14,26},{10,22},{6,18},{2,16},{16,4},... | collective-permute-start | bytes 614408 | tf_op jit(solution)/shard_map/ppermute | solution.py:350
  94.0 17.9 %collective-permute-start.32 = (bf16[160,640]{1,0:T(8,128)(2,1)S(1)}, bf16[160,640]{1,0:T(8,128)(2,1)S(1)}, u32[]{:S(2)}, u32[]{:S(2)}) collective-permute-start(bf16[160,640]{1,0:T(8,128)(2,1)S(1)} %get-tuple-element.71), channel_id=1, source_target_pairs={{4,0},{8,4},{12,8},{14,12},{10,14},{6,10},{2,6},{0,2},{5,1},{9,5},... | collective-permute-start | bytes 614408 | tf_op jit(solution)/shard_map/ppermute | solution.py:352
  96.2 15.8 %collective-permute-start.31 = (bf16[160,640]{1,0:T(8,128)(2,1)S(1)}, bf16[160,640]{1,0:T(8,128)(2,1)S(1)}, u32[]{:S(2)}, u32[]{:S(2)}) collective-permute-start(bf16[160,640]{1,0:T(8,128)(2,1)S(1)} %shard_map.92.refs_3_), channel_id=1, source_target_pairs={{0,4},{4,8},{8,12},{12,14},{14,10},{10,6},{6,2},{2,0},{1,5},{5,9},... | collective-permute-start | bytes 614408 | tf_op jit(solution)/shard_map/ppermute | solution.py:352
  99.9 13.7 %collective-permute-start.33 = (bf16[160,640]{1,0:T(8,128)(2,1)S(1)}, bf16[160,640]{1,0:T(8,128)(2,1)S(1)}, u32[]{:S(2)}, u32[]{:S(2)}) collective-permute-start(bf16[160,640]{1,0:T(8,128)(2,1)S(1)} %shard_map.93.refs_2_), channel_id=1, source_target_pairs={{4,16},{8,20},{12,24},{14,28},{10,30},{6,26},{2,22},{0,18},{20,0},... | collective-permute-start | bytes 614408 | tf_op jit(solution)/shard_map/ppermute | solution.py:350
  (42 other events, 280.6 us)

commit v11 on v9

--- a/solution.py
+++ b/solution.py
@@ -9,7 +9,6 @@
 
 BF16, F32 = jnp.bfloat16, jnp.float32
 VMEM = pl.BlockSpec(memory_space=pltpu.VMEM)
-HBM = pl.BlockSpec(memory_space=pltpu.HBM)
 ANY = pl.BlockSpec(memory_space=pl.ANY)
 SMEM = pl.BlockSpec(memory_space=pltpu.SMEM)
 
@@ -18,7 +17,7 @@
     return jax.ShapeDtypeStruct(dims, kind)
 
 
-def call(kernel, ins, out_shape, scratch=(), vmem=16, flops=1, pinned=(), ties=()):
+def call(kernel, ins, out_shape, scratch=(), vmem=16, flops=1, left=(), ties=()):
     count = len(ins)
 
     def body(*refs):
@@ -29,7 +28,7 @@
         body if ties else kernel,
         out_shape=out_shape,
         in_specs=[
-            SMEM if x.dtype == jnp.int32 else HBM if i in pinned else VMEM
+            SMEM if x.dtype == jnp.int32 else ANY if i in left else VMEM
             for i, x in enumerate(ins)
         ]
         + [ANY] * len(ties),
@@ -47,6 +46,7 @@
         in_specs=[ANY] * (1 + len(ties)),
         out_specs=ANY,
         input_output_aliases={0: 0},
+        compiler_params=pltpu.CompilerParams(vmem_limit_bytes=1 << 20),
         cost_estimate=pl.CostEstimate(flops=1, bytes_accessed=1, transcendentals=0),
     )(array, *ties)
 
@@ -122,22 +122,22 @@
         copy.wait()
 
 
-def own_kernel(index, normed, grads, near_up, near_down, *refs):
-    d_pre, partial, up, down = refs[-4:]
+def other_kernel(index, first, second, near_up, near_down, *refs):
+    d_pre, partial, up, down, normed, grads = refs[-6:]
+    half = first.shape[1]
+    for at, part in ((0, first), (half, second)):
+        normed[at : at + half, :] = part[0]
+        grads[at : at + half, :] = part[1]
     up[...] = near_up[...]
     down[...] = near_down[...]
-    for ref, far in zip((up, down), refs[:-4]):
+    for ref, far in zip((up, down), refs[:-6]):
         depth = far.shape[0]
         rows = pl.ds(pl.multiple_of(index[index.shape[0] - 1] * depth, depth), depth)
         ref[rows, :] = far[...]
     back_through(normed, grads, up, down, d_pre, partial)
 
 
-def other_kernel(first, second, up, down, d_pre, partial, normed, grads):
-    half = first.shape[1]
-    for at, part in ((0, first), (half, second)):
-        normed[at : at + half, :] = part[0]
-        grads[at : at + half, :] = part[1]
+def own_kernel(normed, grads, up, down, d_pre, partial):
     back_through(normed, grads, up, down, d_pre, partial)
 
 
@@ -199,24 +199,19 @@
         out[...] = value.astype(BF16)
 
 
-def add_kernel(one, two, total):
-    total[...] = one[...].astype(F32) + two[...].astype(F32)
-
-
-def own_total_kernel(index, partial, up, down, total):
+def total_kernel(index, partial, up, down, total):
     depth = total.shape[0]
     rows = pl.ds(pl.multiple_of(index[0] * depth, depth), depth)
-    total[...] = partial[rows, :].astype(F32) + up[...].astype(F32) + down[...].astype(F32)
-
-
-def join_kernel(meta, own, *refs):
-    width, out = own.shape[1], refs[-1]
+    value = partial[rows, :].astype(F32) + up[...].astype(F32) + down[...].astype(F32)
+    total[...] = value.astype(total.dtype)
+
+
+def join_kernel(meta, own, passed, out):
+    width = own.shape[1]
     side = meta[2]
     out[:, pl.ds(pl.multiple_of(side * width, width), width)] = own[...]
-    value = refs[0][...].astype(F32)
-    for ref in refs[1:-1]:
-        value = value + ref[...].astype(F32)
-    out[:, pl.ds(pl.multiple_of((1 - side) * width, width), width)] = value
+    other = pl.ds(pl.multiple_of((1 - side) * width, width), width)
+    out[:, other] = passed[...].astype(F32)
 
 
 def ring_member(place, count):
@@ -257,7 +252,8 @@
         shape((2, half_rows, width), BF16),
         [pltpu.SemaphoreType.DMA((2,))] + [pltpu.VMEM((half_rows, width), BF16)] * 2,
         flops=5 * frame_len * width,
-        pinned=(2, 3),
+        vmem=60,
+        left=(2, 3),
     )
     first = lax.ppermute(passing, "groups", swap)
     normed, grads, stats = call(
@@ -275,9 +271,10 @@
         for step in range(1, half):
             up = [lax.ppermute(block, "gx", ahead) for block in up]
             down = [lax.ppermute(block, "gx", behind) for block in down]
+            if step == 1:
+                down[0] = hold(down[0], normed)
             blocks[-step], blocks[step] = up, down
         first, up, down = after((first, up, down))
-        first = hold(first, normed)
         steps = list(blocks) + [half]
         index = jnp.stack([ring_member(place + step + peers, peers) for step in steps])
         index = index.astype(jnp.int32)
@@ -287,7 +284,7 @@
             (index, *blocks),
             (weight, weight),
             [pltpu.SemaphoreType.DMA((len(blocks),))],
-            pinned=range(1, len(blocks) + 1),
+            left=range(1, len(blocks) + 1),
         )
         far = [lax.ppermute(up[0], "gx", ahead), lax.ppermute(down[1], "gx", behind)]
     else:
@@ -296,17 +293,17 @@
     second = lax.ppermute(first, "gy", swap)
 
     d_pre_of, partial_of = shape((frame_len, quarter), BF16), shape((width, quarter), BF16)
-    d_pre_own, partial_own, full_up, full_down = call(
+    d_pre_other, partial_other, full_up, full_down = call(
+        other_kernel,
+        (index, first, second, *near, *far),
+        (d_pre_of, partial_of, weight, weight),
+        [pltpu.VMEM((frame_len, width), BF16)] * 2,
+        flops=6 * frame_len * width * quarter,
+    )
+    d_pre_own, partial_own = call(
         own_kernel,
-        (index, normed, grads, *near, *far),
-        (d_pre_of, partial_of, weight, weight),
-        flops=6 * frame_len * width * quarter,
-    )
-    d_pre_other, partial_other = call(
-        other_kernel,
-        (first, second, full_up, full_down),
+        (normed, grads, full_up, full_down),
         (d_pre_of, partial_of),
-        [pltpu.VMEM((frame_len, width), BF16)] * 2,
         flops=6 * frame_len * width * quarter,
     )
     partial = [partial_own, partial_other]
@@ -346,62 +343,53 @@
         place_of = {step: i for i, step in enumerate(steps)}
         place_of[-half] = place_of[half]
         came = [{}, {}]
-        across = {}
-        for name, pairs in (("up", ahead), ("down", behind)):
-            across[name] = [
-                (a + side_at * peers, b + (1 - side_at) * peers)
-                for side_at in range(2)
-                for a, b in pairs
-            ]
 
         def hop(i, turn, *ties):
             ways = [("up", half - turn - i), ("down", turn + 1 - i - half)]
             ways = [way for way in ways if way[1] != 0]
             kept = [came[i][name] for name, _ in ways if name in came[i]]
+            ended = [came[i][name] for name in came[i] if name not in dict(ways)]
             places = [(place_of[step], name in came[i]) for name, step in ways]
-            if (i, turn) == (1, 0):
-                places.append((0, False))
             blocks = call(
                 functools.partial(hop_kernel, tuple(places)),
                 (index, partial[i], *kept),
                 [block_of] * len(places),
-                ties=ties,
+                ties=(*ended, *ties),
             )
-            for block, (name, step) in zip(blocks, ways):
-                if i == 1 and abs(step) == 1:
-                    came[i][name] = lax.ppermute(block, ("groups", "gx"), across[name])
-                else:
-                    came[i][name] = lax.ppermute(block, "gx", ahead if name == "up" else behind)
-            if (i, turn) == (1, 0):
-                came[i]["own"] = lax.ppermute(blocks[-1], "groups", swap)
+            for block, (name, _) in zip(blocks, ways):
+                came[i][name] = lax.ppermute(block, "gx", ahead if name == "up" else behind)
             return blocks[0]
 
-        hop(0, 0)
-        tie = hop(1, 0)
+        hop(1, 0)
+        tie = hop(0, 0)
+        tie = hop(1, 1, tie)
         keep, send = own_d_norm(tie)
-        send = hold(send, came[0]["up"], came[0]["down"])
+        tie = hop(0, 1, send)
+        send = hold(send, tie, *came[1].values())
         sent = lax.ppermute(send, "gy", swap)
-        tie = hop(0, 1, send)
-        tie = hop(1, 1, tie)
+        tie = hop(1, 2, tie)
+        tie = hop(0, 2, tie)
         over = over_cores(keep, sent, tie)
-        over = hold(over, came[0]["up"], came[0]["down"])
         back = lax.ppermute(over, "groups", swap)
-        tie = hop(0, 2, over)
-        tie = hop(1, 2, tie)
+        tie = over
         for turn in range(3, half):
-            tie = hop(1, turn, hop(0, turn, tie, came[1]["own"]))
-        other = call(
-            add_kernel, (came[1]["own"], came[1]["up"]), shape((depth, quarter), F32), ties=(tie,)
-        )
-        scaled, sums = scale(keep, sent, back, other)
+            tie = hop(0, turn, hop(1, turn, tie))
+        passing = call(
+            total_kernel,
+            (index, partial[1], came[1]["up"], came[1]["down"]),
+            block_of,
+            ties=(tie,),
+        )
+        passed = lax.ppermute(passing, "groups", swap)
+        scaled, sums = scale(keep, sent, back, passing)
         input_grad = input_gradient(scaled, sums)
         total = call(
-            own_total_kernel,
+            total_kernel,
             (index, partial[0], came[0]["up"], came[0]["down"]),
             shape((depth, quarter), F32),
             ties=(input_grad,),
         )
-        up_grad = call(join_kernel, (meta, total, other, came[1]["down"]), up_grad_of)
+        up_grad = call(join_kernel, (meta, total, passed), up_grad_of)
     else:
         keep, send = own_d_norm()
         sent = lax.ppermute(send, "gy", swap)

time: 119 us -> 109 us (0.916)
  starting transfers between devices: 42.6 us -> 34.7 us
  local copies, waits for them, and re-layouts: 21.2 us -> 15 us
  waiting for transfers between devices: 22.7 us -> 26.4 us
    ppermute x12 -> x14, waiting for transfers between devices: 1.73 us -> 13.4 us  [hop(): came[i][name] = lax.ppermute(block, 'gx', ahead if name == 'up' else behind)]
    ppermute x3 -> x1, waiting for transfers between devices: 6.69 us -> 0.01 us  [shards(): passed = lax.ppermute(passing, 'groups', swap)]
    unnamed x64 -> x50, local copies, waits for them, and re-layouts: 20.1 us -> 13.8 us
    ppermute x3 -> x1, starting transfers between devices: 5.22 us -> 1.55 us  [shards(): passed = lax.ppermute(passing, 'groups', swap)]
    ppermute x12 -> x14, starting transfers between devices: 17.4 us -> 14.6 us  [hop(): came[i][name] = lax.ppermute(block, 'gx', ahead if name == 'up' else behind)]
    ppermute x6, waiting for transfers between devices: 10.5 us -> 8.07 us  [shards(): down = [lax.ppermute(block, 'gx', behind) for block in down]]
    ppermute x6, waiting for transfers between devices: 2.15 us -> 3.54 us  [shards(): up = [lax.ppermute(block, 'gx', ahead) for block in up]]
  transfers between devices with their start and end apart: 34 -> 34, of which waited for: 11 -> 16; matrix products, arithmetic and copies ran while one was open for 0% -> 0% of each run, Pallas kernels for 23% -> 19%
where the time goes in v11:
time: 109 us
  starting transfers between devices  34.7 us (32%)
  Pallas kernels  30.9 us (28%)
  waiting for transfers between devices  26.4 us (24%)
  local copies, waits for them, and re-layouts  15 us (14%)
    pallas_call x20, Pallas kernels, call(): pl.pallas_call(body if ties else kernel, out_shape=out_shape, in_specs=[S...  30.9 us
    ppermute x14, starting transfers between devices, hop(): came[i][name] = lax.ppermute(block, 'gx', ahead if name == 'up' else behind)  14.6 us
    unnamed x50, local copies, waits for them, and re-layouts  13.8 us
    ppermute x14, waiting for transfers between devices, hop(): came[i][name] = lax.ppermute(block, 'gx', ahead if name == 'up' else behind)  13.4 us
    ppermute x6, starting transfers between devices, shards(): down = [lax.ppermute(block, 'gx', behind) for block in down]  8.1 us
    ppermute x6, waiting for transfers between devices, shards(): down = [lax.ppermute(block, 'gx', behind) for block in down]  8.07 us
    ppermute x6, starting transfers between devices, shards(): up = [lax.ppermute(block, 'gx', ahead) for block in up]  4.75 us
    ppermute x6, waiting for transfers between devices, shards(): up = [lax.ppermute(block, 'gx', ahead) for block in up]  3.54 us
  transfers between devices with their start and end apart: 34, of which 16 were waited for; matrix products, arithmetic and copies ran while one was open for 0% of the time, Pallas kernels for 19%

profile of v11, /device:TPU:0, one launch (start us, length us, event | category | flops | bytes accessed | tf_op | source)
XLA Modules:
  0.0 108.6 jit_solution(16632272848167874630)
XLA Ops:
  2.4 3.2 %shard_map.78 = bf16[2,192,1280]{2,1,0:T(8,128)(2,1)} custom-call(s32[3]{0:T(128)} %pad_add_fusion.meta.refs_0_, s32[8]{0:T(128)} %lengths.1, bf16[384,1280]{1,0:T(8,128)(2,1)} %bitcast.14, bf16[384,1280]{1,0:T(8,128)(2,1)} %bitcast.18, f32[1280]{0:T(1024)} %gain.1), custom_call_target="tpu_custom_call" | custom-call | flops 2457600 | bytes 2954284 | tf_op jit(solution)/shard_map/pallas_call | solution.py:27
  5.6 3.0 %collective-permute-start = (bf16[2,192,1280]{2,1,0:T(8,128)(2,1)}, bf16[2,192,1280]{2,1,0:T(8,128)(2,1)}, u32[]{:S(2)}, u32[]{:S(2)}) collective-permute-start(bf16[2,192,1280]{2,1,0:T(8,128)(2,1)} %shard_map.78), channel_id=1, source_target_pairs={{0,16},{16,0},{1,17},{17,1},{2,18},{18,2},{3,19},{19,3},{4,20},{20... | collective-permute-start | bytes 2949128 | tf_op jit(solution)/shard_map/ppermute | solution.py:258
  8.6 1.5 %collective-permute-start.7 = (bf16[160,640]{1,0:T(8,128)(2,1)S(1)}, bf16[160,640]{1,0:T(8,128)(2,1)S(1)}, u32[]{:S(2)}, u32[]{:S(2)}) collective-permute-start(bf16[160,640]{1,0:T(8,128)(2,1)S(1)} %get-tuple-element.44.refs_0_), channel_id=1, source_target_pairs={{4,0},{8,4},{12,8},{14,12},{10,14},{6,10},{2,6},{0,2},{5,1},{9,5},... | collective-permute-start | bytes 614408 | tf_op jit(solution)/shard_map/ppermute | solution.py:273
  10.1 1.6 %collective-permute-start.10 = (bf16[160,640]{1,0:T(8,128)(2,1)S(1)}, bf16[160,640]{1,0:T(8,128)(2,1)S(1)}, u32[]{:S(2)}, u32[]{:S(2)}) collective-permute-start(bf16[160,640]{1,0:T(8,128)(2,1)S(1)} %get-tuple-element.45.refs_1_), channel_id=1, source_target_pairs={{4,0},{8,4},{12,8},{14,12},{10,14},{6,10},{2,6},{0,2},{5,1},{9,5},... | collective-permute-start | bytes 614408 | tf_op jit(solution)/shard_map/ppermute | solution.py:273
  18.8 2.2 %collective-permute-done.10.refs_5_ = bf16[160,640]{1,0:T(8,128)(2,1)S(1)} collective-permute-done((bf16[160,640]{1,0:T(8,128)(2,1)S(1)}, bf16[160,640]{1,0:T(8,128)(2,1)S(1)}, u32[]{:S(2)}, u32[]{:S(2)}) %collective-permute-start.10) | collective-permute-done | bytes 204832 | tf_op jit(solution)/shard_map/ppermute | solution.py:273
  24.3 1.6 %collective-permute-start.5 = (bf16[160,640]{1,0:T(8,128)(2,1)S(1)}, bf16[160,640]{1,0:T(8,128)(2,1)S(1)}, u32[]{:S(2)}, u32[]{:S(2)}) collective-permute-start(bf16[160,640]{1,0:T(8,128)(2,1)S(1)} %collective-permute-done.4.refs_3_), channel_id=1, source_target_pairs={{0,4},{4,8},{8,12},{12,14},{14,10},{10,6},{6,2},{2,0},{1,5},{5,9},... | collective-permute-start | bytes 614408 | tf_op jit(solution)/shard_map/ppermute | solution.py:272
  27.0 2.7 %collective-permute-done.11.refs_9_ = bf16[160,640]{1,0:T(8,128)(2,1)S(1)} collective-permute-done((bf16[160,640]{1,0:T(8,128)(2,1)S(1)}, bf16[160,640]{1,0:T(8,128)(2,1)S(1)}, u32[]{:S(2)}, u32[]{:S(2)}) %collective-permute-start.11) | collective-permute-done | bytes 204832 | tf_op jit(solution)/shard_map/ppermute | solution.py:273
  35.3 1.8 %collective-permute-done.12.refs_13_ = bf16[160,640]{1,0:T(8,128)(2,1)} collective-permute-done((bf16[160,640]{1,0:T(8,128)(2,1)S(1)}, bf16[160,640]{1,0:T(8,128)(2,1)}, u32[]{:S(2)}, u32[]{:S(2)}) %collective-permute-start.12) | collective-permute-done | bytes 204832 | tf_op jit(solution)/shard_map/ppermute | solution.py:273
  38.2 2.1 %collective-permute-done.6.refs_11_ = bf16[160,640]{1,0:T(8,128)(2,1)S(1)} collective-permute-done((bf16[160,640]{1,0:T(8,128)(2,1)S(1)}, bf16[160,640]{1,0:T(8,128)(2,1)S(1)}, u32[]{:S(2)}, u32[]{:S(2)}) %collective-permute-start.6) | collective-permute-done | bytes 204832 | tf_op jit(solution)/shard_map/ppermute | solution.py:272
  48.7 5.1 %shard_map.80 = (bf16[1280,640]{1,0:T(8,128)(2,1)S(1)}, bf16[1280,640]{1,0:T(8,128)(2,1)S(1)}) custom-call(s32[8]{0:T(128)S(1)} %stack.51.index.refs_0_, bf16[160,640]{1,0:T(8,128)(2,1)S(1)} %get-tuple-element.44.refs_0_, bf16[160,640]{1,0:T(8,128)(2,1)S(1)} %get-tuple-element.45.refs_1_, bf16[160,640]{1,0:T(8,128)(2,1)S(1)} %copy-done.10, ...), custom_call_target="tpu_custom_call" | custom-call | flops 1 | bytes 6144032 | tf_op jit(solution)/shard_map/pallas_call | solution.py:27
  53.9 4.5 %shard_map.81 = (bf16[384,640]{1,0:T(8,128)(2,1)S(1)}, bf16[1280,640]{1,0:T(8,128)(2,1)S(1)}, bf16[1280,640]{1,0:T(8,128)(2,1)S(1)}, bf16[1280,640]{1,0:T(8,128)(2,1)S(1)}) custom-call(s32[8]{0:T(128)S(1)} %stack.51.index.refs_0_, bf16[2,192,1280]{2,1,0:T(8,128)(2,1)} %collective-permute-done.first, bf16[2,192,1280]{2,1,0:T(8,128)(2,1)} %collective-permute-done.13.second, ...), custom_call_target="tpu_custom_call" | custom-call | flops 1887436800 | bytes 11059232 | tf_op jit(solution)/shard_map/pallas_call | solution.py:27
  61.8 2.7 %shard_map.82 = (bf16[384,640]{1,0:T(8,128)(2,1)S(1)}, bf16[1280,640]{1,0:T(8,128)(2,1)S(1)}) custom-call(bf16[384,1280]{1,0:T(8,128)(2,1)S(1)} %get-tuple-element.42.refs_1_.normed, bf16[384,1280]{1,0:T(8,128)(2,1)S(1)} %copy-done.4, bf16[1280,640]{1,0:T(8,128)(2,1)S(1)} %get-tuple-element.51.up.refs_3_, bf16[1280,640]{1,0:T(8,128)(2,1)S(1)} %get-tuple-element.52.down), custom_call_target="tpu_custom_call" | custom-call | flops 1887436800 | bytes 7372800 | tf_op jit(solution)/shard_map/pallas_call | solution.py:27
  69.9 2.5 %shard_map.86 = (bf16[2,384,640]{2,1,0:T(8,128)(2,1)S(1)}, bf16[2,384,640]{2,1,0:T(8,128)(2,1)S(1)}) custom-call(s32[3]{0:T(128)S(1)} %copy-done.23, bf16[384,640]{1,0:T(8,128)(2,1)S(1)} %get-tuple-element.53.refs_1_, bf16[384,640]{1,0:T(8,128)(2,1)S(1)} %get-tuple-element.54.refs_2_, bf16[1280,640]{1,0:T(8,128)(2,1)S(1)} %get-tuple-element.51.up.refs_3_, ...), custom_call_target="tpu_custom_call" | custom-call | flops 1258291200 | bytes 4587532 | tf_op jit(solution)/shard_map/pallas_call | solution.py:27
  73.9 2.0 %collective-permute-done.20.refs_2_ = bf16[160,640]{1,0:T(8,128)(2,1)S(1)} collective-permute-done((bf16[160,640]{1,0:T(8,128)(2,1)S(1)}, bf16[160,640]{1,0:T(8,128)(2,1)S(1)}, u32[]{:S(2)}, u32[]{:S(2)}) %collective-permute-start.20) | collective-permute-done | bytes 204832 | tf_op jit(solution)/shard_map/ppermute | solution.py:360
  76.2 1.6 %collective-permute-start.23 = (bf16[160,640]{1,0:T(8,128)(2,1)S(1)}, bf16[160,640]{1,0:T(8,128)(2,1)S(1)}, u32[]{:S(2)}, u32[]{:S(2)}) collective-permute-start(bf16[160,640]{1,0:T(8,128)(2,1)S(1)} %get-tuple-element.64.refs_1_.refs_4_), channel_id=1, source_target_pairs={{0,4},{4,8},{8,12},{12,14},{14,10},{10,6},{6,2},{2,0},{1,5},{5,9},... | collective-permute-start | bytes 614408 | tf_op jit(solution)/shard_map/ppermute | solution.py:360
  78.8 1.6 %collective-permute-start.26 = (bf16[160,640]{1,0:T(8,128)(2,1)S(1)}, bf16[160,640]{1,0:T(8,128)(2,1)S(1)}, u32[]{:S(2)}, u32[]{:S(2)}) collective-permute-start(bf16[160,640]{1,0:T(8,128)(2,1)S(1)} %get-tuple-element.67.refs_4_), channel_id=1, source_target_pairs={{0,4},{4,8},{8,12},{12,14},{14,10},{10,6},{6,2},{2,0},{1,5},{5,9},... | collective-permute-start | bytes 614408 | tf_op jit(solution)/shard_map/ppermute | solution.py:360
  80.9 3.1 %collective-permute-done.23.refs_2_ = bf16[160,640]{1,0:T(8,128)(2,1)S(1)} collective-permute-done((bf16[160,640]{1,0:T(8,128)(2,1)S(1)}, bf16[160,640]{1,0:T(8,128)(2,1)S(1)}, u32[]{:S(2)}, u32[]{:S(2)}) %collective-permute-start.23) | collective-permute-done | bytes 204832 | tf_op jit(solution)/shard_map/ppermute | solution.py:360
  84.0 1.6 %collective-permute-done.24.refs_3_ = bf16[160,640]{1,0:T(8,128)(2,1)S(1)} collective-permute-done((bf16[160,640]{1,0:T(8,128)(2,1)S(1)}, bf16[160,640]{1,0:T(8,128)(2,1)S(1)}, u32[]{:S(2)}, u32[]{:S(2)}) %collective-permute-start.24) | collective-permute-done | bytes 204832 | tf_op jit(solution)/shard_map/ppermute | solution.py:360
  87.6 1.6 %collective-permute-start.29 = (bf16[160,640]{1,0:T(8,128)(2,1)S(1)}, bf16[160,640]{1,0:T(8,128)(2,1)S(1)}, u32[]{:S(2)}, u32[]{:S(2)}) collective-permute-start(bf16[160,640]{1,0:T(8,128)(2,1)S(1)} %get-tuple-element.68.refs_3_), channel_id=1, source_target_pairs={{0,4},{4,8},{8,12},{12,14},{14,10},{10,6},{6,2},{2,0},{1,5},{5,9},... | collective-permute-start | bytes 614408 | tf_op jit(solution)/shard_map/ppermute | solution.py:360
  90.9 2.5 %collective-permute-done.29.refs_2_ = bf16[160,640]{1,0:T(8,128)(2,1)S(1)} collective-permute-done((bf16[160,640]{1,0:T(8,128)(2,1)S(1)}, bf16[160,640]{1,0:T(8,128)(2,1)S(1)}, u32[]{:S(2)}, u32[]{:S(2)}) %collective-permute-start.29) | collective-permute-done | bytes 204832 | tf_op jit(solution)/shard_map/ppermute | solution.py:360
  93.4 3.1 %collective-permute-done.30.refs_3_ = bf16[160,640]{1,0:T(8,128)(2,1)S(1)} collective-permute-done((bf16[160,640]{1,0:T(8,128)(2,1)S(1)}, bf16[160,640]{1,0:T(8,128)(2,1)S(1)}, u32[]{:S(2)}, u32[]{:S(2)}) %collective-permute-start.30) | collective-permute-done | bytes 204832 | tf_op jit(solution)/shard_map/ppermute | solution.py:360
  97.1 1.6 %collective-permute-start.32 = (bf16[160,640]{1,0:T(8,128)(2,1)S(1)}, bf16[160,640]{1,0:T(8,128)(2,1)S(1)}, u32[]{:S(2)}, u32[]{:S(2)}) collective-permute-start(bf16[160,640]{1,0:T(8,128)(2,1)S(1)} %shard_map.93.refs_4_), channel_id=1, source_target_pairs={{0,4},{4,8},{8,12},{12,14},{14,10},{10,6},{6,2},{2,0},{1,5},{5,9},... | collective-permute-start | bytes 614408 | tf_op jit(solution)/shard_map/ppermute | solution.py:360
  99.4 1.5 %collective-permute-start.33 = (bf16[160,640]{1,0:T(8,128)(2,1)S(1)}, bf16[160,640]{1,0:T(8,128)(2,1)S(1)}, u32[]{:S(2)}, u32[]{:S(2)}) collective-permute-start(bf16[160,640]{1,0:T(8,128)(2,1)S(1)} %shard_map.94.refs_7_), channel_id=1, source_target_pairs={{0,16},{16,0},{1,17},{17,1},{2,18},{18,2},{3,19},{19,3},{4,20},{20... | collective-permute-start | bytes 614408 | tf_op jit(solution)/shard_map/ppermute | solution.py:383
  103.6 1.9 %shard_map.96.refs_4_ = bf16[384,640]{1,0:T(8,128)(2,1)} custom-call(s32[3]{0:T(128)S(1)} %copy-done.23, f32[384,640]{1,0:T(8,128)S(1)} %get-tuple-element.72.scaled, f32[384,2]{1,0:T(8,128)S(1)} %get-tuple-element.73.sums, f32[384,2]{1,0:T(8,128)S(1)} %collective-permute-done.31.came, bf16[384,1280]{1,0:T(8,128)(2,1)S(1)} %bitcast.17, ...), custom_call_target="tpu_custom_call" | custom-call | flops 1 | bytes 3449868 | tf_op jit(solution)/shard_map/pallas_call | solution.py:27
  (120 shorter events, 51.0 us)
Async XLA Ops:
  5.6 35.4 %collective-permute-start = (bf16[2,192,1280]{2,1,0:T(8,128)(2,1)}, bf16[2,192,1280]{2,1,0:T(8,128)(2,1)}, u32[]{:S(2)}, u32[]{:S(2)}) collective-permute-start(bf16[2,192,1280]{2,1,0:T(8,128)(2,1)} %shard_map.78), channel_id=1, source_target_pairs={{0,16},{16,0},{1,17},{17,1},{2,18},{18,2},{3,19},{19,3},{4,20},{20... | collective-permute-start | bytes 2949128 | tf_op jit(solution)/shard_map/ppermute | solution.py:258
  8.6 8.0 %collective-permute-start.7 = (bf16[160,640]{1,0:T(8,128)(2,1)S(1)}, bf16[160,640]{1,0:T(8,128)(2,1)S(1)}, u32[]{:S(2)}, u32[]{:S(2)}) collective-permute-start(bf16[160,640]{1,0:T(8,128)(2,1)S(1)} %get-tuple-element.44.refs_0_), channel_id=1, source_target_pairs={{4,0},{8,4},{12,8},{14,12},{10,14},{6,10},{2,6},{0,2},{5,1},{9,5},... | collective-permute-start | bytes 614408 | tf_op jit(solution)/shard_map/ppermute | solution.py:273
  10.1 10.9 %collective-permute-start.10 = (bf16[160,640]{1,0:T(8,128)(2,1)S(1)}, bf16[160,640]{1,0:T(8,128)(2,1)S(1)}, u32[]{:S(2)}, u32[]{:S(2)}) collective-permute-start(bf16[160,640]{1,0:T(8,128)(2,1)S(1)} %get-tuple-element.45.refs_1_), channel_id=1, source_target_pairs={{4,0},{8,4},{12,8},{14,12},{10,14},{6,10},{2,6},{0,2},{5,1},{9,5},... | collective-permute-start | bytes 614408 | tf_op jit(solution)/shard_map/ppermute | solution.py:273
  11.7 11.5 %collective-permute-start.1 = (bf16[160,640]{1,0:T(8,128)(2,1)S(1)}, bf16[160,640]{1,0:T(8,128)(2,1)S(1)}, u32[]{:S(2)}, u32[]{:S(2)}) collective-permute-start(bf16[160,640]{1,0:T(8,128)(2,1)S(1)} %get-tuple-element.44.refs_0_), channel_id=1, source_target_pairs={{0,4},{4,8},{8,12},{12,14},{14,10},{10,6},{6,2},{2,0},{1,5},{5,9},... | collective-permute-start | bytes 614408 | tf_op jit(solution)/shard_map/ppermute | solution.py:272
  12.1 12.2 %collective-permute-start.4 = (bf16[160,640]{1,0:T(8,128)(2,1)S(1)}, bf16[160,640]{1,0:T(8,128)(2,1)S(1)}, u32[]{:S(2)}, u32[]{:S(2)}) collective-permute-start(bf16[160,640]{1,0:T(8,128)(2,1)S(1)} %get-tuple-element.45.refs_1_), channel_id=1, source_target_pairs={{0,4},{4,8},{8,12},{12,14},{14,10},{10,6},{6,2},{2,0},{1,5},{5,9},... | collective-permute-start | bytes 614408 | tf_op jit(solution)/shard_map/ppermute | solution.py:272
  16.6 10.0 %collective-permute-start.8 = (bf16[160,640]{1,0:T(8,128)(2,1)S(1)}, bf16[160,640]{1,0:T(8,128)(2,1)S(1)}, u32[]{:S(2)}, u32[]{:S(2)}) collective-permute-start(bf16[160,640]{1,0:T(8,128)(2,1)S(1)} %shard_map.79.refs_4_), channel_id=1, source_target_pairs={{4,0},{8,4},{12,8},{14,12},{10,14},{6,10},{2,6},{0,2},{5,1},{9,5},... | collective-permute-start | bytes 614408 | tf_op jit(solution)/shard_map/ppermute | solution.py:273
  20.9 8.8 %collective-permute-start.11 = (bf16[160,640]{1,0:T(8,128)(2,1)S(1)}, bf16[160,640]{1,0:T(8,128)(2,1)S(1)}, u32[]{:S(2)}, u32[]{:S(2)}) collective-permute-start(bf16[160,640]{1,0:T(8,128)(2,1)S(1)} %collective-permute-done.10.refs_5_), channel_id=1, source_target_pairs={{4,0},{8,4},{12,8},{14,12},{10,14},{6,10},{2,6},{0,2},{5,1},{9,5},... | collective-permute-start | bytes 614408 | tf_op jit(solution)/shard_map/ppermute | solution.py:273
  23.1 8.1 %collective-permute-start.2 = (bf16[160,640]{1,0:T(8,128)(2,1)S(1)}, bf16[160,640]{1,0:T(8,128)(2,1)S(1)}, u32[]{:S(2)}, u32[]{:S(2)}) collective-permute-start(bf16[160,640]{1,0:T(8,128)(2,1)S(1)} %collective-permute-done.1.refs_2_), channel_id=1, source_target_pairs={{0,4},{4,8},{8,12},{12,14},{14,10},{10,6},{6,2},{2,0},{1,5},{5,9},... | collective-permute-start | bytes 614408 | tf_op jit(solution)/shard_map/ppermute | solution.py:272
  24.3 7.8 %collective-permute-start.5 = (bf16[160,640]{1,0:T(8,128)(2,1)S(1)}, bf16[160,640]{1,0:T(8,128)(2,1)S(1)}, u32[]{:S(2)}, u32[]{:S(2)}) collective-permute-start(bf16[160,640]{1,0:T(8,128)(2,1)S(1)} %collective-permute-done.4.refs_3_), channel_id=1, source_target_pairs={{0,4},{4,8},{8,12},{12,14},{14,10},{10,6},{6,2},{2,0},{1,5},{5,9},... | collective-permute-start | bytes 614408 | tf_op jit(solution)/shard_map/ppermute | solution.py:272
  26.6 8.0 %collective-permute-start.9 = (bf16[160,640]{1,0:T(8,128)(2,1)S(1)}, bf16[160,640]{1,0:T(8,128)(2,1)S(1)}, u32[]{:S(2)}, u32[]{:S(2)}) collective-permute-start(bf16[160,640]{1,0:T(8,128)(2,1)S(1)} %collective-permute-done.8.refs_8_), channel_id=1, source_target_pairs={{4,0},{8,4},{12,8},{14,12},{10,14},{6,10},{2,6},{0,2},{5,1},{9,5},... | collective-permute-start | bytes 614408 | tf_op jit(solution)/shard_map/ppermute | solution.py:273
  32.1 8.2 %collective-permute-start.6 = (bf16[160,640]{1,0:T(8,128)(2,1)S(1)}, bf16[160,640]{1,0:T(8,128)(2,1)S(1)}, u32[]{:S(2)}, u32[]{:S(2)}) collective-permute-start(bf16[160,640]{1,0:T(8,128)(2,1)S(1)} %collective-permute-done.5.refs_7_), channel_id=1, source_target_pairs={{0,4},{4,8},{8,12},{12,14},{14,10},{10,6},{6,2},{2,0},{1,5},{5,9},... | collective-permute-start | bytes 614408 | tf_op jit(solution)/shard_map/ppermute | solution.py:272
  41.0 12.8 %collective-permute-start.13 = (bf16[2,192,1280]{2,1,0:T(8,128)(2,1)}, bf16[2,192,1280]{2,1,0:T(8,128)(2,1)}, u32[]{:S(2)}, u32[]{:S(2)}) collective-permute-start(bf16[2,192,1280]{2,1,0:T(8,128)(2,1)} %collective-permute-done.first), channel_id=1, source_target_pairs={{0,1},{1,0},{2,3},{3,2},{4,5},{5,4},{6,7},{7,6},{8,9},{9,8},{10,11... | collective-permute-start | bytes 2949128 | tf_op jit(solution)/shard_map/ppermute | solution.py:293
  41.0 12.8 %collective-permute-start.14 = (bf16[160,640]{1,0:T(8,128)(2,1)}, bf16[160,640]{1,0:T(8,128)(2,1)}, u32[]{:S(2)}, u32[]{:S(2)}) collective-permute-start(bf16[160,640]{1,0:T(8,128)(2,1)} %collective-permute-done.3.refs_10_), channel_id=1, source_target_pairs={{0,4},{4,8},{8,12},{12,14},{14,10},{10,6},{6,2},{2,0},{1,5},{5,9},... | collective-permute-start | bytes 614408 | tf_op jit(solution)/shard_map/ppermute | solution.py:289
  41.5 12.3 %collective-permute-start.15 = (bf16[160,640]{1,0:T(8,128)(2,1)}, bf16[160,640]{1,0:T(8,128)(2,1)}, u32[]{:S(2)}, u32[]{:S(2)}) collective-permute-start(bf16[160,640]{1,0:T(8,128)(2,1)} %collective-permute-done.12.refs_13_), channel_id=1, source_target_pairs={{4,0},{8,4},{12,8},{14,12},{10,14},{6,10},{2,6},{0,2},{5,1},{9,5},... | collective-permute-start | bytes 614408 | tf_op jit(solution)/shard_map/ppermute | solution.py:289
  65.1 8.1 %collective-permute-start.18 = (bf16[160,640]{1,0:T(8,128)(2,1)S(1)}, bf16[160,640]{1,0:T(8,128)(2,1)S(1)}, u32[]{:S(2)}, u32[]{:S(2)}) collective-permute-start(bf16[160,640]{1,0:T(8,128)(2,1)S(1)} %get-tuple-element.59.refs_4_), channel_id=1, source_target_pairs={{0,4},{4,8},{8,12},{12,14},{14,10},{10,6},{6,2},{2,0},{1,5},{5,9},... | collective-permute-start | bytes 614408 | tf_op jit(solution)/shard_map/ppermute | solution.py:360
  67.9 8.1 %collective-permute-start.20 = (bf16[160,640]{1,0:T(8,128)(2,1)S(1)}, bf16[160,640]{1,0:T(8,128)(2,1)S(1)}, u32[]{:S(2)}, u32[]{:S(2)}) collective-permute-start(bf16[160,640]{1,0:T(8,128)(2,1)S(1)} %get-tuple-element.60.refs_4_), channel_id=1, source_target_pairs={{0,4},{4,8},{8,12},{12,14},{14,10},{10,6},{6,2},{2,0},{1,5},{5,9},... | collective-permute-start | bytes 614408 | tf_op jit(solution)/shard_map/ppermute | solution.py:360
  76.2 10.1 %collective-permute-start.22 = (bf16[2,384,640]{2,1,0:T(8,128)(2,1)S(1)}, bf16[2,384,640]{2,1,0:T(8,128)(2,1)S(1)}, u32[]{:S(2)}, u32[]{:S(2)}) collective-permute-start(bf16[2,384,640]{2,1,0:T(8,128)(2,1)S(1)} %shard_map.88), channel_id=1, source_target_pairs={{0,1},{1,0},{2,3},{3,2},{4,5},{5,4},{6,7},{7,6},{8,9},{9,8},{10,11... | collective-permute-start | bytes 2949128 | tf_op jit(solution)/shard_map/ppermute | solution.py:369
  76.2 7.9 %collective-permute-start.23 = (bf16[160,640]{1,0:T(8,128)(2,1)S(1)}, bf16[160,640]{1,0:T(8,128)(2,1)S(1)}, u32[]{:S(2)}, u32[]{:S(2)}) collective-permute-start(bf16[160,640]{1,0:T(8,128)(2,1)S(1)} %get-tuple-element.64.refs_1_.refs_4_), channel_id=1, source_target_pairs={{0,4},{4,8},{8,12},{12,14},{14,10},{10,6},{6,2},{2,0},{1,5},{5,9},... | collective-permute-start | bytes 614408 | tf_op jit(solution)/shard_map/ppermute | solution.py:360
  77.7 7.9 %collective-permute-start.24 = (bf16[160,640]{1,0:T(8,128)(2,1)S(1)}, bf16[160,640]{1,0:T(8,128)(2,1)S(1)}, u32[]{:S(2)}, u32[]{:S(2)}) collective-permute-start(bf16[160,640]{1,0:T(8,128)(2,1)S(1)} %get-tuple-element.66), channel_id=1, source_target_pairs={{4,0},{8,4},{12,8},{14,12},{10,14},{6,10},{2,6},{0,2},{5,1},{9,5},... | collective-permute-start | bytes 614408 | tf_op jit(solution)/shard_map/ppermute | solution.py:360
  78.8 10.8 %collective-permute-start.26 = (bf16[160,640]{1,0:T(8,128)(2,1)S(1)}, bf16[160,640]{1,0:T(8,128)(2,1)S(1)}, u32[]{:S(2)}, u32[]{:S(2)}) collective-permute-start(bf16[160,640]{1,0:T(8,128)(2,1)S(1)} %get-tuple-element.67.refs_4_), channel_id=1, source_target_pairs={{0,4},{4,8},{8,12},{12,14},{14,10},{10,6},{6,2},{2,0},{1,5},{5,9},... | collective-permute-start | bytes 614408 | tf_op jit(solution)/shard_map/ppermute | solution.py:360
  80.5 9.2 %collective-permute-start.27 = (bf16[160,640]{1,0:T(8,128)(2,1)S(1)}, bf16[160,640]{1,0:T(8,128)(2,1)S(1)}, u32[]{:S(2)}, u32[]{:S(2)}) collective-permute-start(bf16[160,640]{1,0:T(8,128)(2,1)S(1)} %get-tuple-element.70), channel_id=1, source_target_pairs={{4,0},{8,4},{12,8},{14,12},{10,14},{6,10},{2,6},{0,2},{5,1},{9,5},... | collective-permute-start | bytes 614408 | tf_op jit(solution)/shard_map/ppermute | solution.py:360
  87.0 13.9 %collective-permute-start.25 = (bf16[384,640]{1,0:T(8,128)(2,1)S(1)}, bf16[384,640]{1,0:T(8,128)(2,1)S(1)}, u32[]{:S(2)}, u32[]{:S(2)}) collective-permute-start(bf16[384,640]{1,0:T(8,128)(2,1)S(1)} %shard_map.91.refs_4_), channel_id=1, source_target_pairs={{0,16},{16,0},{1,17},{17,1},{2,18},{18,2},{3,19},{19,3},{4,20},{20... | collective-permute-start | bytes 1474568 | tf_op jit(solution)/shard_map/ppermute | solution.py:373
  90.2 8.5 %collective-permute-start.28 = (bf16[160,640]{1,0:T(8,128)(2,1)S(1)}, bf16[160,640]{1,0:T(8,128)(2,1)S(1)}, u32[]{:S(2)}, u32[]{:S(2)}) collective-permute-start(bf16[160,640]{1,0:T(8,128)(2,1)S(1)} %shard_map.92.refs_4_), channel_id=1, source_target_pairs={{4,0},{8,4},{12,8},{14,12},{10,14},{6,10},{2,6},{0,2},{5,1},{9,5},... | collective-permute-start | bytes 614408 | tf_op jit(solution)/shard_map/ppermute | solution.py:360
  97.1 8.4 %collective-permute-start.32 = (bf16[160,640]{1,0:T(8,128)(2,1)S(1)}, bf16[160,640]{1,0:T(8,128)(2,1)S(1)}, u32[]{:S(2)}, u32[]{:S(2)}) collective-permute-start(bf16[160,640]{1,0:T(8,128)(2,1)S(1)} %shard_map.93.refs_4_), channel_id=1, source_target_pairs={{0,4},{4,8},{8,12},{12,14},{14,10},{10,6},{6,2},{2,0},{1,5},{5,9},... | collective-permute-start | bytes 614408 | tf_op jit(solution)/shard_map/ppermute | solution.py:360
  (35 other events, 132.0 us)

commit v12 on v11

--- a/solution.py
+++ b/solution.py
@@ -9,6 +9,7 @@
 
 BF16, F32 = jnp.bfloat16, jnp.float32
 VMEM = pl.BlockSpec(memory_space=pltpu.VMEM)
+HBM = pl.BlockSpec(memory_space=pltpu.HBM)
 ANY = pl.BlockSpec(memory_space=pl.ANY)
 SMEM = pl.BlockSpec(memory_space=pltpu.SMEM)
 
@@ -17,7 +18,7 @@
     return jax.ShapeDtypeStruct(dims, kind)
 
 
-def call(kernel, ins, out_shape, scratch=(), vmem=16, flops=1, left=(), ties=()):
+def call(kernel, ins, out_shape, scratch=(), vmem=16, flops=1, left=(), pinned=(), out=VMEM, ties=()):
     count = len(ins)
 
     def body(*refs):
@@ -28,11 +29,11 @@
         body if ties else kernel,
         out_shape=out_shape,
         in_specs=[
-            SMEM if x.dtype == jnp.int32 else ANY if i in left else VMEM
+            SMEM if x.dtype == jnp.int32 else ANY if i in left else HBM if i in pinned else VMEM
             for i, x in enumerate(ins)
         ]
         + [ANY] * len(ties),
-        out_specs=jax.tree.map(lambda _: VMEM, out_shape),
+        out_specs=jax.tree.map(lambda _: out, out_shape),
         scratch_shapes=list(scratch),
         compiler_params=pltpu.CompilerParams(vmem_limit_bytes=vmem << 20),
         cost_estimate=pl.CostEstimate(flops=flops, bytes_accessed=moved, transcendentals=0),
@@ -78,9 +79,9 @@
     return jnp.where(index < length, rows.astype(F32), 0.0).astype(BF16)
 
 
-def pass_kernel(meta, lengths, frames, out_grad, gain, passing, sems, rows, grads):
+def pass_kernel(lengths, frames, out_grad, gain, passing, sems, rows, grads):
     half = rows.shape[0]
-    start = pl.multiple_of(meta[1] * half, half)
+    start = pl.multiple_of(lax.axis_index("gy") * half, half)
     copies = [
         pltpu.make_async_copy(source.at[pl.ds(start, half)], target, sems.at[i])
         for i, (source, target) in enumerate(((frames, rows), (out_grad, grads)))
@@ -90,7 +91,7 @@
     copies[0].wait()
     passing[0] = norm_rows(rows[...], gain)[0]
     copies[1].wait()
-    passing[1] = mask_rows(grads[...], start, lengths[meta[0]])
+    passing[1] = mask_rows(grads[...], start, lengths[lax.axis_index("gx")])
 
 
 def norm_kernel(meta, lengths, frames, out_grad, gain, normed, grads, stats):
@@ -167,25 +168,26 @@
     return ref[:, pl.ds(pl.multiple_of(meta[1] * width, width), width)]
 
 
-def scale_kernel(meta, keep, came, back, frames, gain, stats, scaled, sums):
-    width = scaled.shape[1]
+def scale_kernel(meta, keep, came, back, frames, gain, grads, stats, base, factor, sums):
+    width = base.shape[1]
     d_norm = keep[0].astype(F32) + came[0].astype(F32) + back[...].astype(F32)
-    value = d_norm * own_columns(meta, gain, width)
-    scaled[...] = value
-    rows = own_columns(meta, frames, width).astype(F32)
-    centred = (rows - stats[:, 0:1]) * stats[:, 1:2]
-    sums[:, 0:1] = jnp.sum(value, axis=-1, keepdims=True)
-    sums[:, 1:2] = jnp.sum(value * centred, axis=-1, keepdims=True)
-
-
-def input_kernel(meta, scaled, sums, came, frames, grads, stats, out):
-    width = scaled.shape[1]
-    means = (sums[...] + came[...]) * (0.5 / width)
+    scaled = d_norm * own_columns(meta, gain, width)
     rows = own_columns(meta, frames, width).astype(F32)
     inv_std = stats[:, 1:2]
     centred = (rows - stats[:, 0:1]) * inv_std
-    value = inv_std * (scaled[...] - means[:, 0:1] - centred * means[:, 1:2])
-    out[...] = (own_columns(meta, grads, width).astype(F32) + value).astype(BF16)
+    sums[:, 0:1] = jnp.sum(scaled, axis=-1, keepdims=True)
+    sums[:, 1:2] = jnp.sum(scaled * centred, axis=-1, keepdims=True)
+    base[...] = own_columns(meta, grads, width).astype(F32) + inv_std * scaled
+    factor[...] = inv_std * centred
+
+
+def input_kernel(base, factor, sums, came, stats, out, block, sem):
+    means = (sums[...] + came[...]) * (0.5 / base.shape[1])
+    value = base[...] - stats[:, 1:2] * means[:, 0:1] - factor[...] * means[:, 1:2]
+    block[...] = value.astype(BF16)
+    copy = pltpu.make_async_copy(block, out, sem)
+    copy.start()
+    copy.wait()
 
 
 def hop_kernel(places, index, partial, *refs):
@@ -206,7 +208,17 @@
     total[...] = value.astype(total.dtype)
 
 
-def join_kernel(meta, own, passed, out):
+def join_kernel(meta, index, partial, up, down, passed, out):
+    depth, width = passed.shape
+    side = meta[2]
+    rows = pl.ds(pl.multiple_of(index[0] * depth, depth), depth)
+    value = partial[rows, :].astype(F32) + up[...].astype(F32) + down[...].astype(F32)
+    out[:, pl.ds(pl.multiple_of(side * width, width), width)] = value
+    other = pl.ds(pl.multiple_of((1 - side) * width, width), width)
+    out[:, other] = passed[...].astype(F32)
+
+
+def place_halves_kernel(meta, own, passed, out):
     width = own.shape[1]
     side = meta[2]
     out[:, pl.ds(pl.multiple_of(side * width, width), width)] = own[...]
@@ -245,7 +257,7 @@
     frames, out_grad = frames[0], out_grad[0]
 
     rows_of = shape((frame_len, width), BF16)
-    operands = (meta, lengths, frames, out_grad, ln_gain)
+    operands = (lengths, frames, out_grad, ln_gain)
     passing = call(
         pass_kernel,
         operands,
@@ -253,12 +265,12 @@
         [pltpu.SemaphoreType.DMA((2,))] + [pltpu.VMEM((half_rows, width), BF16)] * 2,
         flops=5 * frame_len * width,
         vmem=60,
-        left=(2, 3),
+        left=(1, 2),
     )
     first = lax.ppermute(passing, "groups", swap)
     normed, grads, stats = call(
         norm_kernel,
-        operands,
+        (meta, *operands),
         (rows_of, rows_of, shape((frame_len, 2), F32)),
         flops=10 * frame_len * width,
     )
@@ -284,7 +296,7 @@
             (index, *blocks),
             (weight, weight),
             [pltpu.SemaphoreType.DMA((len(blocks),))],
-            left=range(1, len(blocks) + 1),
+            pinned=range(1, len(blocks) + 1),
         )
         far = [lax.ppermute(up[0], "gx", ahead), lax.ppermute(down[1], "gx", behind)]
     else:
@@ -325,17 +337,22 @@
     def scale(keep, came, back, *ties):
         return call(
             scale_kernel,
-            (meta, keep, came, back, frames, ln_gain[None], stats),
-            (shape((frame_len, half_width), F32), shape((frame_len, 2), F32)),
+            (meta, keep, came, back, frames, ln_gain[None], grads, stats),
+            (
+                shape((frame_len, half_width), F32),
+                shape((frame_len, half_width), F32),
+                shape((frame_len, 2), F32),
+            ),
             ties=ties,
         )
 
-    def input_gradient(scaled, sums, *ties):
+    def input_gradient(base, factor, sums):
         return call(
             input_kernel,
-            (meta, scaled, sums, lax.ppermute(sums, "gy", swap), frames, grads, stats),
+            (base, factor, sums, lax.ppermute(sums, "gy", swap), stats),
             half_rows_of,
-            ties=ties,
+            [pltpu.VMEM((frame_len, half_width), BF16), pltpu.SemaphoreType.DMA],
+            out=HBM,
         )
 
     up_grad_of = shape((depth, hidden), F32)
@@ -381,15 +398,13 @@
             ties=(tie,),
         )
         passed = lax.ppermute(passing, "groups", swap)
-        scaled, sums = scale(keep, sent, back, passing)
-        input_grad = input_gradient(scaled, sums)
-        total = call(
-            total_kernel,
-            (index, partial[0], came[0]["up"], came[0]["down"]),
-            shape((depth, quarter), F32),
+        input_grad = input_gradient(*scale(keep, sent, back, passing))
+        up_grad = call(
+            join_kernel,
+            (meta, index, partial[0], came[0]["up"], came[0]["down"], passed),
+            up_grad_of,
             ties=(input_grad,),
         )
-        up_grad = call(join_kernel, (meta, total, passed), up_grad_of)
     else:
         keep, send = own_d_norm()
         sent = lax.ppermute(send, "gy", swap)
@@ -399,7 +414,7 @@
             lax.psum_scatter(p.astype(F32), "gx", scatter_dimension=0, tiled=True) for p in partial
         ]
         passed = lax.ppermute(passing.astype(BF16), "groups", swap)
-        up_grad = call(join_kernel, (meta, total, passed), up_grad_of)
+        up_grad = call(place_halves_kernel, (meta, total, passed), up_grad_of)
     return (input_grad[None], up_grad)
 
 

time: 109 us -> 103 us (0.945)
  local copies, waits for them, and re-layouts: 15 us -> 8.48 us
  Pallas kernels: 30.9 us -> 28.6 us
  waiting for transfers between devices: 26.4 us -> 28.4 us
  starting transfers between devices: 34.7 us -> 36.1 us
    unnamed x50 -> x34, local copies, waits for them, and re-layouts: 13.8 us -> 7.33 us
    pallas_call x20 -> x19, Pallas kernels: 30.9 us -> 28.6 us  [call(): pl.pallas_call(body if ties else kernel, out_shape=out_shape, in_specs=[S...]
    ppermute x6, waiting for transfers between devices: 8.07 us -> 9.7 us  [shards(): down = [lax.ppermute(block, 'gx', behind) for block in down]]
  transfers between devices with their start and end apart: 34 -> 34, of which waited for: 16 -> 19; matrix products, arithmetic and copies ran while one was open for 0% -> 0% of each run, Pallas kernels for 19% -> 18%
where the time goes in v12:
time: 103 us
  starting transfers between devices  36.1 us (35%)
  Pallas kernels  28.6 us (28%)
  waiting for transfers between devices  28.4 us (28%)
  local copies, waits for them, and re-layouts  8.48 us (8%)
    pallas_call x19, Pallas kernels, call(): pl.pallas_call(body if ties else kernel, out_shape=out_shape, in_specs=[S...  28.6 us
    ppermute x14, starting transfers between devices, hop(): came[i][name] = lax.ppermute(block, 'gx', ahead if name == 'up' else behind)  14.5 us
    ppermute x14, waiting for transfers between devices, hop(): came[i][name] = lax.ppermute(block, 'gx', ahead if name == 'up' else behind)  14.1 us
    ppermute x6, waiting for transfers between devices, shards(): down = [lax.ppermute(block, 'gx', behind) for block in down]  9.7 us
    ppermute x6, starting transfers between devices, shards(): down = [lax.ppermute(block, 'gx', behind) for block in down]  9.17 us
    unnamed x34, local copies, waits for them, and re-layouts  7.33 us
    ppermute x6, starting transfers between devices, shards(): up = [lax.ppermute(block, 'gx', ahead) for block in up]  5.12 us
    ppermute x1, starting transfers between devices, shards(): first = lax.ppermute(passing, 'groups', swap)  3 us
  transfers between devices with their start and end apart: 34, of which 19 were waited for; matrix products, arithmetic and copies ran while one was open for 0% of the time, Pallas kernels for 18%

profile of v12, /device:TPU:0, one launch (start us, length us, event | category | flops | bytes accessed | tf_op | source)
XLA Modules:
  0.0 102.5 jit_solution(10673001653781632443)
XLA Ops:
  1.7 3.2 %shard_map.78 = bf16[2,192,1280]{2,1,0:T(8,128)(2,1)} custom-call(s32[8]{0:T(128)} %lengths.1, bf16[384,1280]{1,0:T(8,128)(2,1)} %bitcast.14, bf16[384,1280]{1,0:T(8,128)(2,1)} %bitcast.17, f32[1280]{0:T(1024)} %gain.1), custom_call_target="tpu_custom_call" | custom-call | flops 2457600 | bytes 2954272 | tf_op jit(solution)/shard_map/pallas_call | solution.py:28
  5.0 3.0 %collective-permute-start = (bf16[2,192,1280]{2,1,0:T(8,128)(2,1)}, bf16[2,192,1280]{2,1,0:T(8,128)(2,1)}, u32[]{:S(2)}, u32[]{:S(2)}) collective-permute-start(bf16[2,192,1280]{2,1,0:T(8,128)(2,1)} %shard_map.78), channel_id=1, source_target_pairs={{0,16},{16,0},{1,17},{17,1},{2,18},{18,2},{3,19},{19,3},{4,20},{20... | collective-permute-start | bytes 2949128 | tf_op jit(solution)/shard_map/ppermute | solution.py:270
  9.5 1.6 %collective-permute-start.10 = (bf16[160,640]{1,0:T(8,128)(2,1)S(1)}, bf16[160,640]{1,0:T(8,128)(2,1)}, u32[]{:S(2)}, u32[]{:S(2)}) collective-permute-start(bf16[160,640]{1,0:T(8,128)(2,1)S(1)} %get-tuple-element.46.refs_1_), channel_id=1, source_target_pairs={{4,0},{8,4},{12,8},{14,12},{10,14},{6,10},{2,6},{0,2},{5,1},{9,5},... | collective-permute-start | bytes 614408 | tf_op jit(solution)/shard_map/ppermute | solution.py:285
  18.6 1.9 %collective-permute-done.10.refs_5_ = bf16[160,640]{1,0:T(8,128)(2,1)} collective-permute-done((bf16[160,640]{1,0:T(8,128)(2,1)S(1)}, bf16[160,640]{1,0:T(8,128)(2,1)}, u32[]{:S(2)}, u32[]{:S(2)}) %collective-permute-start.10) | collective-permute-done | bytes 204832 | tf_op jit(solution)/shard_map/ppermute | solution.py:285
  22.5 1.6 %collective-permute-start.5 = (bf16[160,640]{1,0:T(8,128)(2,1)}, bf16[160,640]{1,0:T(8,128)(2,1)S(1)}, u32[]{:S(2)}, u32[]{:S(2)}) collective-permute-start(bf16[160,640]{1,0:T(8,128)(2,1)} %collective-permute-done.4.refs_3_), channel_id=1, source_target_pairs={{0,4},{4,8},{8,12},{12,14},{14,10},{10,6},{6,2},{2,0},{1,5},{5,9},... | collective-permute-start | bytes 614408 | tf_op jit(solution)/shard_map/ppermute | solution.py:284
  26.8 2.9 %collective-permute-done.11.refs_9_ = bf16[160,640]{1,0:T(8,128)(2,1)S(1)} collective-permute-done((bf16[160,640]{1,0:T(8,128)(2,1)}, bf16[160,640]{1,0:T(8,128)(2,1)S(1)}, u32[]{:S(2)}, u32[]{:S(2)}) %collective-permute-start.11) | collective-permute-done | bytes 204832 | tf_op jit(solution)/shard_map/ppermute | solution.py:285
  31.7 1.6 %collective-permute-start.6 = (bf16[160,640]{1,0:T(8,128)(2,1)S(1)}, bf16[160,640]{1,0:T(8,128)(2,1)S(1)}, u32[]{:S(2)}, u32[]{:S(2)}) collective-permute-start(bf16[160,640]{1,0:T(8,128)(2,1)S(1)} %collective-permute-done.5.refs_7_), channel_id=1, source_target_pairs={{0,4},{4,8},{8,12},{12,14},{14,10},{10,6},{6,2},{2,0},{1,5},{5,9},... | collective-permute-start | bytes 614408 | tf_op jit(solution)/shard_map/ppermute | solution.py:284
  34.7 1.8 %collective-permute-done.12.refs_13_ = bf16[160,640]{1,0:T(8,128)(2,1)} collective-permute-done((bf16[160,640]{1,0:T(8,128)(2,1)S(1)}, bf16[160,640]{1,0:T(8,128)(2,1)}, u32[]{:S(2)}, u32[]{:S(2)}) %collective-permute-start.12) | collective-permute-done | bytes 204832 | tf_op jit(solution)/shard_map/ppermute | solution.py:285
  37.2 2.1 %collective-permute-done.6.refs_11_ = bf16[160,640]{1,0:T(8,128)(2,1)S(1)} collective-permute-done((bf16[160,640]{1,0:T(8,128)(2,1)S(1)}, bf16[160,640]{1,0:T(8,128)(2,1)S(1)}, u32[]{:S(2)}, u32[]{:S(2)}) %collective-permute-start.6) | collective-permute-done | bytes 204832 | tf_op jit(solution)/shard_map/ppermute | solution.py:284
  43.9 4.1 %shard_map.80 = (bf16[1280,640]{1,0:T(8,128)(2,1)S(1)}, bf16[1280,640]{1,0:T(8,128)(2,1)S(1)}) custom-call(s32[8]{0:T(128)S(1)} %stack.51.index.refs_0_.refs_1_, bf16[160,640]{1,0:T(8,128)(2,1)S(1)} %get-tuple-element.45.refs_0_, bf16[160,640]{1,0:T(8,128)(2,1)S(1)} %get-tuple-element.46.refs_1_, bf16[160,640]{1,0:T(8,128)(2,1)} %collective-permute-done.1.refs_2_, ...), custom_call_target="tpu_custom_call" | custom-call | flops 1 | bytes 6144032 | tf_op jit(solution)/shard_map/pallas_call | solution.py:28
  48.0 4.5 %shard_map.81 = (bf16[384,640]{1,0:T(8,128)(2,1)S(1)}, bf16[1280,640]{1,0:T(8,128)(2,1)S(1)}, bf16[1280,640]{1,0:T(8,128)(2,1)S(1)}, bf16[1280,640]{1,0:T(8,128)(2,1)S(1)}) custom-call(s32[8]{0:T(128)S(1)} %stack.51.index.refs_0_.refs_1_, bf16[2,192,1280]{2,1,0:T(8,128)(2,1)} %collective-permute-done.first, ...), custom_call_target="tpu_custom_call" | custom-call | flops 1887436800 | bytes 11059232 | tf_op jit(solution)/shard_map/pallas_call | solution.py:28
  53.9 1.6 %collective-permute-start.16 = (bf16[160,640]{1,0:T(8,128)(2,1)S(1)}, bf16[160,640]{1,0:T(8,128)(2,1)S(1)}, u32[]{:S(2)}, u32[]{:S(2)}) collective-permute-start(bf16[160,640]{1,0:T(8,128)(2,1)S(1)} %get-tuple-element.57), channel_id=1, source_target_pairs={{0,4},{4,8},{8,12},{12,14},{14,10},{10,6},{6,2},{2,0},{1,5},{5,9},... | collective-permute-start | bytes 614408 | tf_op jit(solution)/shard_map/ppermute | solution.py:377
  56.0 2.7 %shard_map.82 = (bf16[384,640]{1,0:T(8,128)(2,1)S(1)}, bf16[1280,640]{1,0:T(8,128)(2,1)S(1)}) custom-call(bf16[384,1280]{1,0:T(8,128)(2,1)S(1)} %copy-done.4, bf16[384,1280]{1,0:T(8,128)(2,1)S(1)} %get-tuple-element.44.grads.refs_6_, bf16[1280,640]{1,0:T(8,128)(2,1)S(1)} %get-tuple-element.52.up.refs_3_, bf16[1280,640]{1,0:T(8,128)(2,1)S(1)} %get-tuple-element.53.down), custom_call_target="tpu_custom_call" | custom-call | flops 1887436800 | bytes 7372800 | tf_op jit(solution)/shard_map/pallas_call | solution.py:28
  59.3 1.6 %collective-permute-start.18 = (bf16[160,640]{1,0:T(8,128)(2,1)S(1)}, bf16[160,640]{1,0:T(8,128)(2,1)S(1)}, u32[]{:S(2)}, u32[]{:S(2)}) collective-permute-start(bf16[160,640]{1,0:T(8,128)(2,1)S(1)} %get-tuple-element.60.refs_4_), channel_id=1, source_target_pairs={{0,4},{4,8},{8,12},{12,14},{14,10},{10,6},{6,2},{2,0},{1,5},{5,9},... | collective-permute-start | bytes 614408 | tf_op jit(solution)/shard_map/ppermute | solution.py:377
  62.2 1.6 %collective-permute-start.20 = (bf16[160,640]{1,0:T(8,128)(2,1)S(1)}, bf16[160,640]{1,0:T(8,128)(2,1)S(1)}, u32[]{:S(2)}, u32[]{:S(2)}) collective-permute-start(bf16[160,640]{1,0:T(8,128)(2,1)S(1)} %get-tuple-element.61.refs_4_), channel_id=1, source_target_pairs={{0,4},{4,8},{8,12},{12,14},{14,10},{10,6},{6,2},{2,0},{1,5},{5,9},... | collective-permute-start | bytes 614408 | tf_op jit(solution)/shard_map/ppermute | solution.py:377
  64.3 2.5 %shard_map.86 = (bf16[2,384,640]{2,1,0:T(8,128)(2,1)S(1)}, bf16[2,384,640]{2,1,0:T(8,128)(2,1)S(1)}) custom-call(s32[3]{0:T(128)S(1)} %copy-done.15, bf16[384,640]{1,0:T(8,128)(2,1)S(1)} %get-tuple-element.54.refs_1_, bf16[384,640]{1,0:T(8,128)(2,1)S(1)} %get-tuple-element.55.refs_2_, bf16[1280,640]{1,0:T(8,128)(2,1)S(1)} %get-tuple-element.52.up.refs_3_, ...), custom_call_target="tpu_custom_call" | custom-call | flops 1258291200 | bytes 4587532 | tf_op jit(solution)/shard_map/pallas_call | solution.py:28
  71.0 1.6 %collective-permute-start.23 = (bf16[160,640]{1,0:T(8,128)(2,1)S(1)}, bf16[160,640]{1,0:T(8,128)(2,1)S(1)}, u32[]{:S(2)}, u32[]{:S(2)}) collective-permute-start(bf16[160,640]{1,0:T(8,128)(2,1)S(1)} %get-tuple-element.65.refs_1_.refs_4_), channel_id=1, source_target_pairs={{0,4},{4,8},{8,12},{12,14},{14,10},{10,6},{6,2},{2,0},{1,5},{5,9},... | collective-permute-start | bytes 614408 | tf_op jit(solution)/shard_map/ppermute | solution.py:377
  73.6 1.6 %collective-permute-start.26 = (bf16[160,640]{1,0:T(8,128)(2,1)S(1)}, bf16[160,640]{1,0:T(8,128)(2,1)S(1)}, u32[]{:S(2)}, u32[]{:S(2)}) collective-permute-start(bf16[160,640]{1,0:T(8,128)(2,1)S(1)} %get-tuple-element.68.refs_4_), channel_id=1, source_target_pairs={{0,4},{4,8},{8,12},{12,14},{14,10},{10,6},{6,2},{2,0},{1,5},{5,9},... | collective-permute-start | bytes 614408 | tf_op jit(solution)/shard_map/ppermute | solution.py:377
  75.7 3.1 %collective-permute-done.23.refs_2_ = bf16[160,640]{1,0:T(8,128)(2,1)S(1)} collective-permute-done((bf16[160,640]{1,0:T(8,128)(2,1)S(1)}, bf16[160,640]{1,0:T(8,128)(2,1)S(1)}, u32[]{:S(2)}, u32[]{:S(2)}) %collective-permute-start.23) | collective-permute-done | bytes 204832 | tf_op jit(solution)/shard_map/ppermute | solution.py:377
  78.8 1.6 %collective-permute-done.24.refs_3_ = bf16[160,640]{1,0:T(8,128)(2,1)S(1)} collective-permute-done((bf16[160,640]{1,0:T(8,128)(2,1)S(1)}, bf16[160,640]{1,0:T(8,128)(2,1)S(1)}, u32[]{:S(2)}, u32[]{:S(2)}) %collective-permute-start.24) | collective-permute-done | bytes 204832 | tf_op jit(solution)/shard_map/ppermute | solution.py:377
  85.5 2.6 %collective-permute-done.29.refs_2_ = bf16[160,640]{1,0:T(8,128)(2,1)S(1)} collective-permute-done((bf16[160,640]{1,0:T(8,128)(2,1)S(1)}, bf16[160,640]{1,0:T(8,128)(2,1)S(1)}, u32[]{:S(2)}, u32[]{:S(2)}) %collective-permute-start.29) | collective-permute-done | bytes 204832 | tf_op jit(solution)/shard_map/ppermute | solution.py:377
  88.1 3.1 %collective-permute-done.30.refs_3_.refs_4_ = bf16[160,640]{1,0:T(8,128)(2,1)S(1)} collective-permute-done((bf16[160,640]{1,0:T(8,128)(2,1)S(1)}, bf16[160,640]{1,0:T(8,128)(2,1)S(1)}, u32[]{:S(2)}, u32[]{:S(2)}) %collective-permute-start.30) | collective-permute-done | bytes 204832 | tf_op jit(solution)/shard_map/ppermute | solution.py:377
  91.8 1.7 %collective-permute-start.32 = (bf16[160,640]{1,0:T(8,128)(2,1)S(1)}, bf16[160,640]{1,0:T(8,128)(2,1)S(1)}, u32[]{:S(2)}, u32[]{:S(2)}) collective-permute-start(bf16[160,640]{1,0:T(8,128)(2,1)S(1)} %shard_map.93.refs_4_), channel_id=1, source_target_pairs={{0,4},{4,8},{8,12},{12,14},{14,10},{10,6},{6,2},{2,0},{1,5},{5,9},... | collective-permute-start | bytes 614408 | tf_op jit(solution)/shard_map/ppermute | solution.py:377
  94.1 1.6 %collective-permute-start.33 = (bf16[160,640]{1,0:T(8,128)(2,1)S(1)}, bf16[160,640]{1,0:T(8,128)(2,1)S(1)}, u32[]{:S(2)}, u32[]{:S(2)}) collective-permute-start(bf16[160,640]{1,0:T(8,128)(2,1)S(1)} %shard_map.94.refs_8_), channel_id=1, source_target_pairs={{0,16},{16,0},{1,17},{17,1},{2,18},{18,2},{3,19},{19,3},{4,20},{20... | collective-permute-start | bytes 614408 | tf_op jit(solution)/shard_map/ppermute | solution.py:400
  (103 shorter events, 46.5 us)
Async XLA Ops:
  5.0 35.0 %collective-permute-start = (bf16[2,192,1280]{2,1,0:T(8,128)(2,1)}, bf16[2,192,1280]{2,1,0:T(8,128)(2,1)}, u32[]{:S(2)}, u32[]{:S(2)}) collective-permute-start(bf16[2,192,1280]{2,1,0:T(8,128)(2,1)} %shard_map.78), channel_id=1, source_target_pairs={{0,16},{16,0},{1,17},{17,1},{2,18},{18,2},{3,19},{19,3},{4,20},{20... | collective-permute-start | bytes 2949128 | tf_op jit(solution)/shard_map/ppermute | solution.py:270
  8.0 8.1 %collective-permute-start.7 = (bf16[160,640]{1,0:T(8,128)(2,1)S(1)}, bf16[160,640]{1,0:T(8,128)(2,1)}, u32[]{:S(2)}, u32[]{:S(2)}) collective-permute-start(bf16[160,640]{1,0:T(8,128)(2,1)S(1)} %get-tuple-element.45.refs_0_), channel_id=1, source_target_pairs={{4,0},{8,4},{12,8},{14,12},{10,14},{6,10},{2,6},{0,2},{5,1},{9,5},... | collective-permute-start | bytes 614408 | tf_op jit(solution)/shard_map/ppermute | solution.py:285
  9.5 11.0 %collective-permute-start.10 = (bf16[160,640]{1,0:T(8,128)(2,1)S(1)}, bf16[160,640]{1,0:T(8,128)(2,1)}, u32[]{:S(2)}, u32[]{:S(2)}) collective-permute-start(bf16[160,640]{1,0:T(8,128)(2,1)S(1)} %get-tuple-element.46.refs_1_), channel_id=1, source_target_pairs={{4,0},{8,4},{12,8},{14,12},{10,14},{6,10},{2,6},{0,2},{5,1},{9,5},... | collective-permute-start | bytes 614408 | tf_op jit(solution)/shard_map/ppermute | solution.py:285
  11.1 10.9 %collective-permute-start.1 = (bf16[160,640]{1,0:T(8,128)(2,1)S(1)}, bf16[160,640]{1,0:T(8,128)(2,1)}, u32[]{:S(2)}, u32[]{:S(2)}) collective-permute-start(bf16[160,640]{1,0:T(8,128)(2,1)S(1)} %get-tuple-element.45.refs_0_), channel_id=1, source_target_pairs={{0,4},{4,8},{8,12},{12,14},{14,10},{10,6},{6,2},{2,0},{1,5},{5,9},... | collective-permute-start | bytes 614408 | tf_op jit(solution)/shard_map/ppermute | solution.py:284
  11.5 11.0 %collective-permute-start.4 = (bf16[160,640]{1,0:T(8,128)(2,1)S(1)}, bf16[160,640]{1,0:T(8,128)(2,1)}, u32[]{:S(2)}, u32[]{:S(2)}) collective-permute-start(bf16[160,640]{1,0:T(8,128)(2,1)S(1)} %get-tuple-element.46.refs_1_), channel_id=1, source_target_pairs={{0,4},{4,8},{8,12},{12,14},{14,10},{10,6},{6,2},{2,0},{1,5},{5,9},... | collective-permute-start | bytes 614408 | tf_op jit(solution)/shard_map/ppermute | solution.py:284
  17.0 8.2 %collective-permute-start.8 = (bf16[160,640]{1,0:T(8,128)(2,1)}, bf16[160,640]{1,0:T(8,128)(2,1)S(1)}, u32[]{:S(2)}, u32[]{:S(2)}) collective-permute-start(bf16[160,640]{1,0:T(8,128)(2,1)} %shard_map.79.refs_4_), channel_id=1, source_target_pairs={{4,0},{8,4},{12,8},{14,12},{10,14},{6,10},{2,6},{0,2},{5,1},{9,5},... | collective-permute-start | bytes 614408 | tf_op jit(solution)/shard_map/ppermute | solution.py:285
  20.5 9.2 %collective-permute-start.11 = (bf16[160,640]{1,0:T(8,128)(2,1)}, bf16[160,640]{1,0:T(8,128)(2,1)S(1)}, u32[]{:S(2)}, u32[]{:S(2)}) collective-permute-start(bf16[160,640]{1,0:T(8,128)(2,1)} %collective-permute-done.10.refs_5_), channel_id=1, source_target_pairs={{4,0},{8,4},{12,8},{14,12},{10,14},{6,10},{2,6},{0,2},{5,1},{9,5},... | collective-permute-start | bytes 614408 | tf_op jit(solution)/shard_map/ppermute | solution.py:285
  22.0 9.2 %collective-permute-start.2 = (bf16[160,640]{1,0:T(8,128)(2,1)}, bf16[160,640]{1,0:T(8,128)(2,1)S(1)}, u32[]{:S(2)}, u32[]{:S(2)}) collective-permute-start(bf16[160,640]{1,0:T(8,128)(2,1)} %collective-permute-done.1.refs_2_), channel_id=1, source_target_pairs={{0,4},{4,8},{8,12},{12,14},{14,10},{10,6},{6,2},{2,0},{1,5},{5,9},... | collective-permute-start | bytes 614408 | tf_op jit(solution)/shard_map/ppermute | solution.py:284
  22.5 9.2 %collective-permute-start.5 = (bf16[160,640]{1,0:T(8,128)(2,1)}, bf16[160,640]{1,0:T(8,128)(2,1)S(1)}, u32[]{:S(2)}, u32[]{:S(2)}) collective-permute-start(bf16[160,640]{1,0:T(8,128)(2,1)} %collective-permute-done.4.refs_3_), channel_id=1, source_target_pairs={{0,4},{4,8},{8,12},{12,14},{14,10},{10,6},{6,2},{2,0},{1,5},{5,9},... | collective-permute-start | bytes 614408 | tf_op jit(solution)/shard_map/ppermute | solution.py:284
  25.3 8.8 %collective-permute-start.9 = (bf16[160,640]{1,0:T(8,128)(2,1)S(1)}, bf16[160,640]{1,0:T(8,128)(2,1)S(1)}, u32[]{:S(2)}, u32[]{:S(2)}) collective-permute-start(bf16[160,640]{1,0:T(8,128)(2,1)S(1)} %collective-permute-done.8.refs_8_), channel_id=1, source_target_pairs={{4,0},{8,4},{12,8},{14,12},{10,14},{6,10},{2,6},{0,2},{5,1},{9,5},... | collective-permute-start | bytes 614408 | tf_op jit(solution)/shard_map/ppermute | solution.py:285
  31.7 7.6 %collective-permute-start.6 = (bf16[160,640]{1,0:T(8,128)(2,1)S(1)}, bf16[160,640]{1,0:T(8,128)(2,1)S(1)}, u32[]{:S(2)}, u32[]{:S(2)}) collective-permute-start(bf16[160,640]{1,0:T(8,128)(2,1)S(1)} %collective-permute-done.5.refs_7_), channel_id=1, source_target_pairs={{0,4},{4,8},{8,12},{12,14},{14,10},{10,6},{6,2},{2,0},{1,5},{5,9},... | collective-permute-start | bytes 614408 | tf_op jit(solution)/shard_map/ppermute | solution.py:284
  40.0 8.1 %collective-permute-start.13 = (bf16[2,192,1280]{2,1,0:T(8,128)(2,1)}, bf16[2,192,1280]{2,1,0:T(8,128)(2,1)}, u32[]{:S(2)}, u32[]{:S(2)}) collective-permute-start(bf16[2,192,1280]{2,1,0:T(8,128)(2,1)} %collective-permute-done.first), channel_id=1, source_target_pairs={{0,1},{1,0},{2,3},{3,2},{4,5},{5,4},{6,7},{7,6},{8,9},{9,8},{10,11... | collective-permute-start | bytes 2949128 | tf_op jit(solution)/shard_map/ppermute | solution.py:305
  40.0 8.1 %collective-permute-start.14 = (bf16[160,640]{1,0:T(8,128)(2,1)}, bf16[160,640]{1,0:T(8,128)(2,1)}, u32[]{:S(2)}, u32[]{:S(2)}) collective-permute-start(bf16[160,640]{1,0:T(8,128)(2,1)} %collective-permute-done.3.refs_10_), channel_id=1, source_target_pairs={{0,4},{4,8},{8,12},{12,14},{14,10},{10,6},{6,2},{2,0},{1,5},{5,9},... | collective-permute-start | bytes 614408 | tf_op jit(solution)/shard_map/ppermute | solution.py:301
  59.3 8.1 %collective-permute-start.18 = (bf16[160,640]{1,0:T(8,128)(2,1)S(1)}, bf16[160,640]{1,0:T(8,128)(2,1)S(1)}, u32[]{:S(2)}, u32[]{:S(2)}) collective-permute-start(bf16[160,640]{1,0:T(8,128)(2,1)S(1)} %get-tuple-element.60.refs_4_), channel_id=1, source_target_pairs={{0,4},{4,8},{8,12},{12,14},{14,10},{10,6},{6,2},{2,0},{1,5},{5,9},... | collective-permute-start | bytes 614408 | tf_op jit(solution)/shard_map/ppermute | solution.py:377
  60.8 7.9 %collective-permute-start.19 = (bf16[160,640]{1,0:T(8,128)(2,1)S(1)}, bf16[160,640]{1,0:T(8,128)(2,1)S(1)}, u32[]{:S(2)}, u32[]{:S(2)}) collective-permute-start(bf16[160,640]{1,0:T(8,128)(2,1)S(1)} %get-tuple-element.64), channel_id=1, source_target_pairs={{4,0},{8,4},{12,8},{14,12},{10,14},{6,10},{2,6},{0,2},{5,1},{9,5},... | collective-permute-start | bytes 614408 | tf_op jit(solution)/shard_map/ppermute | solution.py:377
  62.2 7.8 %collective-permute-start.20 = (bf16[160,640]{1,0:T(8,128)(2,1)S(1)}, bf16[160,640]{1,0:T(8,128)(2,1)S(1)}, u32[]{:S(2)}, u32[]{:S(2)}) collective-permute-start(bf16[160,640]{1,0:T(8,128)(2,1)S(1)} %get-tuple-element.61.refs_4_), channel_id=1, source_target_pairs={{0,4},{4,8},{8,12},{12,14},{14,10},{10,6},{6,2},{2,0},{1,5},{5,9},... | collective-permute-start | bytes 614408 | tf_op jit(solution)/shard_map/ppermute | solution.py:377
  71.0 10.1 %collective-permute-start.22 = (bf16[2,384,640]{2,1,0:T(8,128)(2,1)S(1)}, bf16[2,384,640]{2,1,0:T(8,128)(2,1)S(1)}, u32[]{:S(2)}, u32[]{:S(2)}) collective-permute-start(bf16[2,384,640]{2,1,0:T(8,128)(2,1)S(1)} %shard_map.88), channel_id=1, source_target_pairs={{0,1},{1,0},{2,3},{3,2},{4,5},{5,4},{6,7},{7,6},{8,9},{9,8},{10,11... | collective-permute-start | bytes 2949128 | tf_op jit(solution)/shard_map/ppermute | solution.py:386
  71.0 7.9 %collective-permute-start.23 = (bf16[160,640]{1,0:T(8,128)(2,1)S(1)}, bf16[160,640]{1,0:T(8,128)(2,1)S(1)}, u32[]{:S(2)}, u32[]{:S(2)}) collective-permute-start(bf16[160,640]{1,0:T(8,128)(2,1)S(1)} %get-tuple-element.65.refs_1_.refs_4_), channel_id=1, source_target_pairs={{0,4},{4,8},{8,12},{12,14},{14,10},{10,6},{6,2},{2,0},{1,5},{5,9},... | collective-permute-start | bytes 614408 | tf_op jit(solution)/shard_map/ppermute | solution.py:377
  72.5 7.9 %collective-permute-start.24 = (bf16[160,640]{1,0:T(8,128)(2,1)S(1)}, bf16[160,640]{1,0:T(8,128)(2,1)S(1)}, u32[]{:S(2)}, u32[]{:S(2)}) collective-permute-start(bf16[160,640]{1,0:T(8,128)(2,1)S(1)} %get-tuple-element.67), channel_id=1, source_target_pairs={{4,0},{8,4},{12,8},{14,12},{10,14},{6,10},{2,6},{0,2},{5,1},{9,5},... | collective-permute-start | bytes 614408 | tf_op jit(solution)/shard_map/ppermute | solution.py:377
  73.6 10.8 %collective-permute-start.26 = (bf16[160,640]{1,0:T(8,128)(2,1)S(1)}, bf16[160,640]{1,0:T(8,128)(2,1)S(1)}, u32[]{:S(2)}, u32[]{:S(2)}) collective-permute-start(bf16[160,640]{1,0:T(8,128)(2,1)S(1)} %get-tuple-element.68.refs_4_), channel_id=1, source_target_pairs={{0,4},{4,8},{8,12},{12,14},{14,10},{10,6},{6,2},{2,0},{1,5},{5,9},... | collective-permute-start | bytes 614408 | tf_op jit(solution)/shard_map/ppermute | solution.py:377
  75.3 9.1 %collective-permute-start.27 = (bf16[160,640]{1,0:T(8,128)(2,1)S(1)}, bf16[160,640]{1,0:T(8,128)(2,1)S(1)}, u32[]{:S(2)}, u32[]{:S(2)}) collective-permute-start(bf16[160,640]{1,0:T(8,128)(2,1)S(1)} %get-tuple-element.71), channel_id=1, source_target_pairs={{4,0},{8,4},{12,8},{14,12},{10,14},{6,10},{2,6},{0,2},{5,1},{9,5},... | collective-permute-start | bytes 614408 | tf_op jit(solution)/shard_map/ppermute | solution.py:377
  81.8 13.9 %collective-permute-start.25 = (bf16[384,640]{1,0:T(8,128)(2,1)S(1)}, bf16[384,640]{1,0:T(8,128)(2,1)S(1)}, u32[]{:S(2)}, u32[]{:S(2)}) collective-permute-start(bf16[384,640]{1,0:T(8,128)(2,1)S(1)} %shard_map.91.refs_4_), channel_id=1, source_target_pairs={{0,16},{16,0},{1,17},{17,1},{2,18},{18,2},{3,19},{19,3},{4,20},{20... | collective-permute-start | bytes 1474568 | tf_op jit(solution)/shard_map/ppermute | solution.py:390
  85.0 8.5 %collective-permute-start.28 = (bf16[160,640]{1,0:T(8,128)(2,1)S(1)}, bf16[160,640]{1,0:T(8,128)(2,1)S(1)}, u32[]{:S(2)}, u32[]{:S(2)}) collective-permute-start(bf16[160,640]{1,0:T(8,128)(2,1)S(1)} %shard_map.92.refs_4_), channel_id=1, source_target_pairs={{4,0},{8,4},{12,8},{14,12},{10,14},{6,10},{2,6},{0,2},{5,1},{9,5},... | collective-permute-start | bytes 614408 | tf_op jit(solution)/shard_map/ppermute | solution.py:377
  91.8 7.7 %collective-permute-start.32 = (bf16[160,640]{1,0:T(8,128)(2,1)S(1)}, bf16[160,640]{1,0:T(8,128)(2,1)S(1)}, u32[]{:S(2)}, u32[]{:S(2)}) collective-permute-start(bf16[160,640]{1,0:T(8,128)(2,1)S(1)} %shard_map.93.refs_4_), channel_id=1, source_target_pairs={{0,4},{4,8},{8,12},{12,14},{14,10},{10,6},{6,2},{2,0},{1,5},{5,9},... | collective-permute-start | bytes 614408 | tf_op jit(solution)/shard_map/ppermute | solution.py:377
  (27 other events, 112.2 us)

commit v13 on v12

v13 whole, which is shorter than its diff:
```python
import functools

import jax
import jax.numpy as jnp
from jax import lax
from jax.experimental import pallas as pl
from jax.experimental.pallas import tpu as pltpu
from jax.sharding import PartitionSpec as P

BF16, F32 = jnp.bfloat16, jnp.float32
VMEM = pl.BlockSpec(memory_space=pltpu.VMEM)
HBM = pl.BlockSpec(memory_space=pltpu.HBM)
ANY = pl.BlockSpec(memory_space=pl.ANY)
SMEM = pl.BlockSpec(memory_space=pltpu.SMEM)


def shape(dims, kind):
    return jax.ShapeDtypeStruct(dims, kind)


def call(kernel, ins, out_shape, scratch=(), vmem=16, flops=1, left=(), pinned=(), out=VMEM, ties=()):
    count = len(ins)

    def body(*refs):
        kernel(*refs[:count], *refs[count + len(ties) :])

    moved = sum(x.size * x.dtype.itemsize for x in list(ins) + jax.tree.leaves(out_shape))
    return pl.pallas_call(
        body if ties else kernel,
        out_shape=out_shape,
        in_specs=[
            SMEM if x.dtype == jnp.int32 else ANY if i in left else HBM if i in pinned else VMEM
            for i, x in enumerate(ins)
        ]
        + [ANY] * len(ties),
        out_specs=jax.tree.map(lambda _: out, out_shape),
        scratch_shapes=list(scratch),
        compiler_params=pltpu.CompilerParams(vmem_limit_bytes=vmem << 20),
        cost_estimate=pl.CostEstimate(flops=flops, bytes_accessed=moved, transcendentals=0),
    )(*ins, *ties)


def hold(array, *ties):
    return pl.pallas_call(
        lambda *refs: None,
        out_shape=shape(array.shape, array.dtype),
        in_specs=[ANY] * (1 + len(ties)),
        out_specs=ANY,
        input_output_aliases={0: 0},
        compiler_params=pltpu.CompilerParams(vmem_limit_bytes=1 << 20),
        cost_estimate=pl.CostEstimate(flops=1, bytes_accessed=1, transcendentals=0),
    )(array, *ties)


def dot(left, right, left_dim=1, right_dim=0):
    return lax.dot_general(
        left, right, (((left_dim,), (right_dim,)), ((), ())), preferred_element_type=F32
    )


def gelu_slope(values):
    return (
        0.5 * (1.0 + lax.erf(values * 0.7071067811865476))
        + values * jnp.exp(-0.5 * values * values) * 0.3989422804014327
    )


def block_rows(step, peers, depth):
    own = lax.axis_index("gx")
    place = jnp.where(lax.rem(own, 2) == 0, lax.div(own, 2), peers - 1 - lax.div(own, 2))
    place = lax.rem(place + (step + peers), peers)
    member = jnp.where(place < peers // 2, 2 * place, 2 * (peers - 1 - place) + 1)
    return pl.ds(pl.multiple_of(member * depth, depth), depth)


def norm_rows(rows, gain):
    values = rows.astype(F32)
    centre = jnp.mean(values, axis=-1, keepdims=True)
    shifted = values - centre
    variance = jnp.mean(shifted * shifted, axis=-1, keepdims=True)
    inv_std = lax.rsqrt(variance + 1e-05)
    return (shifted * inv_std * gain[...][None]).astype(BF16), centre, inv_std


def mask_rows(rows, start, length):
    index = start + lax.broadcasted_iota(jnp.int32, (rows.shape[0], 1), 0)
    return jnp.where(index < length, rows.astype(F32), 0.0).astype(BF16)


def first_kernel(
    lengths, frames, out_grad, gain, w_up, w_down, passing, mine_up, mine_down, sems, rows, grads
):
    half, quarter = rows.shape[0], mine_up.shape[1]
    start = pl.multiple_of(lax.axis_index("gy") * half, half)
    columns = pl.ds(pl.multiple_of(lax.axis_index("groups") * quarter, quarter), quarter)
    moves = (
        (frames.at[pl.ds(start, half)], rows),
        (out_grad.at[pl.ds(start, half)], grads),
        (w_up.at[:, columns], mine_up),
        (w_down.at[:, columns], mine_down),
    )
    copies = [pltpu.make_async_copy(*move, sems.at[i]) for i, move in enumerate(moves)]
    for copy in copies:
        copy.start()
    copies[0].wait()
    passing[0] = norm_rows(rows[...], gain)[0]
    copies[1].wait()
    passing[1] = mask_rows(grads[...], start, lengths[lax.axis_index("gx")])
    copies[2].wait()
    copies[3].wait()


def norm_kernel(lengths, frames, out_grad, gain, normed, grads, stats):
    value, centre, inv_std = norm_rows(frames[...], gain)
    normed[...] = value
    stats[:, 0:1] = centre
    stats[:, 1:2] = inv_std
    grads[...] = mask_rows(out_grad[...], 0, lengths[lax.axis_index("gx")])


def back_through(normed, grads, up, down, d_pre, partial):
    pre_act = dot(normed[...], up[...])
    d_act = dot(grads[...], down[...])
    d_pre[...] = (d_act * gelu_slope(pre_act)).astype(BF16)
    partial[...] = dot(normed[...], d_pre[...], 0, 0).astype(BF16)


def place_kernel(places, peers, *refs):
    blocks, (up, down, sems) = refs[:-3], refs[-3:]
    copies = []
    for i, ((step, which), block) in enumerate(zip(places, blocks)):
        rows = block_rows(step, peers, block.shape[0])
        copies.append(pltpu.make_async_copy(block, (up, down)[which].at[rows], sems.at[i]))
    for copy in copies:
        copy.start()
    for copy in copies:
        copy.wait()


def other_kernel(places, sends, peers, first, second, near_up, near_down, *refs):
    late, refs = refs[: len(places)], refs[len(places) :]
    (d_pre, partial, up, down), blocks, (normed, grads) = refs[:4], refs[4:-2], refs[-2:]
    half = first.shape[1]
    for at, part in ((0, first), (half, second)):
        normed[at : at + half, :] = part[0]
        grads[at : at + half, :] = part[1]
    up[...] = near_up[...]
    down[...] = near_down[...]
    for (step, which), block in zip(places, late):
        (up, down)[which][block_rows(step, peers, block.shape[0]), :] = block[...]
    back_through(normed, grads, up, down, d_pre, partial)
    for step, block in zip(sends, blocks):
        block[...] = partial[block_rows(step, peers, block.shape[0]), :]


def own_kernel(sends, peers, normed, grads, up, down, d_pre, partial, *blocks):
    back_through(normed, grads, up, down, d_pre, partial)
    for step, block in zip(sends, blocks):
        block[...] = partial[block_rows(step, peers, block.shape[0]), :]


def d_norm_kernel(d_pre_own, d_pre_other, up, keep, send):
    core = lax.axis_index("gy")
    rows, width = keep.shape[1:]
    mine = up[pl.ds(pl.multiple_of(core * width, width), width), :]
    theirs = up[pl.ds(pl.multiple_of((1 - core) * width, width), width), :]
    keep[0] = dot(d_pre_own[...], mine, 1, 1).astype(BF16)
    keep[1] = dot(d_pre_other[...], mine, 1, 1).astype(BF16)
    send[0] = dot(d_pre_own[...], theirs, 1, 1).astype(BF16)
    sent = dot(d_pre_other[...], theirs, 1, 1).astype(BF16)
    send[1, rows // 2 :, :] = sent[: rows // 2]
    send[1, : rows // 2, :] = sent[rows // 2 :]


def over_kernel(keep, came, over):
    half = over.shape[0] // 2
    for i in range(2):
        at = lax.rem(i + lax.axis_index("gy"), 2) * half
        rows = slice(i * half, (i + 1) * half)
        value = keep[1, rows, :].astype(F32) + came[1, rows, :].astype(F32)
        over[pl.ds(pl.multiple_of(at, half), half), :] = value.astype(BF16)


def own_columns(ref, width):
    return ref[:, pl.ds(pl.multiple_of(lax.axis_index("gy") * width, width), width)]


def scale_kernel(keep, came, back, frames, gain, grads, stats, base, factor, sums):
    width = base.shape[1]
    d_norm = keep[0].astype(F32) + came[0].astype(F32) + back[...].astype(F32)
    scaled = d_norm * own_columns(gain, width)
    rows = own_columns(frames, width).astype(F32)
    inv_std = stats[:, 1:2]
    centred = (rows - stats[:, 0:1]) * inv_std
    sums[:, 0:1] = jnp.sum(scaled, axis=-1, keepdims=True)
    sums[:, 1:2] = jnp.sum(scaled * centred, axis=-1, keepdims=True)
    base[...] = own_columns(grads, width).astype(F32) + inv_std * scaled
    factor[...] = inv_std * centred


def input_kernel(base, factor, sums, came, stats, out, token):
    means = (sums[...] + came[...]) * (0.5 / base.shape[1])
    value = base[...] - stats[:, 1:2] * means[:, 0:1] - factor[...] * means[:, 1:2]
    out[...] = value.astype(BF16)
    token[...] = jnp.zeros_like(token)


def hop_kernel(places, peers, partial, *refs):
    count = len(places)
    for step, came, out in zip(places, refs[:count], refs[count:]):
        value = partial[block_rows(step, peers, out.shape[0]), :].astype(F32)
        out[...] = (value + came[...].astype(F32)).astype(BF16)


def total_kernel(peers, partial, up, down, total):
    value = partial[block_rows(0, peers, total.shape[0]), :].astype(F32)
    total[...] = (value + up[...].astype(F32) + down[...].astype(F32)).astype(BF16)


def join_kernel(peers, partial, up, down, passed, out):
    depth, width = passed.shape
    side = lax.axis_index("groups")
    value = partial[block_rows(0, peers, depth), :].astype(F32)
    value = value + up[...].astype(F32) + down[...].astype(F32)
    out[:, pl.ds(pl.multiple_of(side * width, width), width)] = value
    other = pl.ds(pl.multiple_of((1 - side) * width, width), width)
    out[:, other] = passed[...].astype(F32)


def place_halves_kernel(own, passed, out):
    width = own.shape[1]
    side = lax.axis_index("groups")
    out[:, pl.ds(pl.multiple_of(side * width, width), width)] = own[...]
    other = pl.ds(pl.multiple_of((1 - side) * width, width), width)
    out[:, other] = passed[...].astype(F32)


def shards(frames, out_grad, ln_gain, w_up, w_down, lengths):
    peers = lax.axis_size("gx")
    half = peers // 2
    frame_len, width = frames.shape[1:]
    depth, hidden = w_up.shape
    quarter = hidden // 2
    half_width = width // 2
    half_rows = frame_len // 2
    ringed = peers <= 16 and peers % 2 == 0 and depth % 16 == 0

    order = list(range(0, peers, 2)) + list(range(peers - 1, 0, -2))
    ahead = [(order[i], order[(i + 1) % peers]) for i in range(peers)]
    behind = [(b, a) for a, b in ahead]
    swap = [(0, 1), (1, 0)]

    frames, out_grad = frames[0], out_grad[0]
    rows_of = shape((frame_len, width), BF16)
    block_of = shape((depth, quarter), BF16)
    passing, *mine = call(
        first_kernel,
        (lengths, frames, out_grad, ln_gain, w_up, w_down),
        (shape((2, half_rows, width), BF16), block_of, block_of),
        [pltpu.SemaphoreType.DMA((4,))] + [pltpu.VMEM((half_rows, width), BF16)] * 2,
        flops=5 * frame_len * width,
        vmem=60,
        left=(1, 2, 4, 5),
    )
    first = lax.ppermute(passing, "groups", swap)
    normed, grads, stats = call(
        norm_kernel,
        (lengths, frames, out_grad, ln_gain),
        (rows_of, rows_of, shape((frame_len, 2), F32)),
        flops=10 * frame_len * width,
    )

    weight = shape((width, quarter), BF16)
    if ringed:
        blocks = {(0, 0): mine[0], (0, 1): mine[1]}
        up, down = list(mine), list(mine)
        for step in range(1, half):
            for i in range(2):
                up[i] = lax.ppermute(up[i], "gx", ahead)
                down[i] = lax.ppermute(down[i], "gx", behind)
            if step == 1:
                up[0] = hold(up[0], normed)
            for i in range(2):
                blocks[-step, i], blocks[step, i] = up[i], down[i]
        first = hold(first, *up, *down)
        late = {
            (half - 1, 0): blocks.pop((half - 1, 0)),
            (1 - half, 1): blocks.pop((1 - half, 1)),
            (half, 0): lax.ppermute(up[0], "gx", ahead),
            (half, 1): lax.ppermute(down[1], "gx", behind),
        }
        near = call(
            functools.partial(place_kernel, tuple(blocks), peers),
            list(blocks.values()),
            (weight, weight),
            [pltpu.SemaphoreType.DMA((len(blocks),))],
            pinned=range(len(blocks)),
        )
        sends = ((half - 1, -half), (half, 1 - half))
    else:
        near = [lax.all_gather(block, "gx", axis=0, tiled=True) for block in mine]
        late, sends = {}, ((), ())
    second = lax.ppermute(first, "gy", swap)

    d_pre_of, partial_of = shape((frame_len, quarter), BF16), shape((width, quarter), BF16)
    d_pre_other, partial_other, full_up, full_down, *blocks_other = call(
        functools.partial(other_kernel, tuple(late), sends[0], peers),
        (first, second, *near, *late.values()),
        (d_pre_of, partial_of, weight, weight, *[block_of] * len(sends[0])),
        [pltpu.VMEM((frame_len, width), BF16)] * 2,
        flops=6 * frame_len * width * quarter,
    )
    d_pre_own, partial_own, *blocks_own = call(
        functools.partial(own_kernel, sends[1], peers),
        (normed, grads, full_up, full_down),
        (d_pre_of, partial_of, *[block_of] * len(sends[1])),
        flops=6 * frame_len * width * quarter,
    )
    partial = [partial_own, partial_other]

    half_rows_of = shape((frame_len, half_width), BF16)

    def own_d_norm(*ties):
        return call(
            d_norm_kernel,
            (d_pre_own, d_pre_other, full_up),
            (shape((2, frame_len, half_width), BF16), shape((2, frame_len, half_width), BF16)),
            flops=4 * frame_len * width * quarter,
            ties=ties,
        )

    def over_cores(keep, came, *ties):
        return call(over_kernel, (keep, came), half_rows_of, ties=ties)

    def scale(keep, came, back, *ties):
        return call(
            scale_kernel,
            (keep, came, back, frames, ln_gain[None], grads, stats),
            (
                shape((frame_len, half_width), F32),
                shape((frame_len, half_width), F32),
                shape((frame_len, 2), F32),
            ),
            ties=ties,
        )

    def input_gradient(base, factor, sums):
        return call(
            input_kernel,
            (base, factor, sums, lax.ppermute(sums, "gy", swap), stats),
            (half_rows_of, shape((8, 128), F32)),
        )

    up_grad_of = shape((depth, hidden), F32)
    if ringed:
        came = [{}, {}]

        def send_on(i, blocks, names):
            for block, name in zip(blocks, names):
                came[i][name] = lax.ppermute(block, "gx", ahead if name == "up" else behind)

        def hop(i, turn, *ties):
            ways = [("up", half - turn - i), ("down", turn + 1 - i - half)]
            ways = [way for way in ways if way[1] != 0]
            names = [name for name, _ in ways]
            if i == 1:
                ties += tuple(came[i][name] for name in came[i] if name not in names)
            blocks = call(
                functools.partial(hop_kernel, tuple(step for _, step in ways), peers),
                (partial[i], *[came[i][name] for name in names]),
                [block_of] * len(ways),
                ties=ties,
            )
            send_on(i, blocks, names)
            return blocks[0]

        send_on(1, blocks_other, ("up", "down"))
        send_on(0, blocks_own, ("up", "down"))
        tie = hop(1, 1, partial_own)
        keep, send = own_d_norm(tie)
        tie = hop(0, 1, send)
        send = hold(send, tie, *came[1].values())
        sent = lax.ppermute(send, "gy", swap)
        tie = hop(1, 2, tie)
        tie = hop(0, 2, tie)
        over = over_cores(keep, sent, tie)
        back = lax.ppermute(over, "groups", swap)
        tie = over
        for turn in range(3, half):
            tie = hop(0, turn, hop(1, turn, tie))
        passing = call(
            functools.partial(total_kernel, peers),
            (partial[1], came[1]["up"], came[1]["down"]),
            block_of,
            ties=(tie,),
        )
        passed = lax.ppermute(passing, "groups", swap)
        input_grad, token = input_gradient(*scale(keep, sent, back, passing))
        up_grad = call(
            functools.partial(join_kernel, peers),
            (partial[0], came[0]["up"], came[0]["down"], passed),
            up_grad_of,
            ties=(token,),
        )
    else:
        keep, send = own_d_norm()
        sent = lax.ppermute(send, "gy", swap)
        back = lax.ppermute(over_cores(keep, sent), "groups", swap)
        input_grad, _ = input_gradient(*scale(keep, sent, back))
        total, passing = [
            lax.psum_scatter(p.astype(F32), "gx", scatter_dimension=0, tiled=True) for p in partial
        ]
        passed = lax.ppermute(passing.astype(BF16), "groups", swap)
        up_grad = call(place_halves_kernel, (total, passed), up_grad_of)
    return (input_grad[None], up_grad)


def solution(mesh):
    placed = (
        P(("groups", "gx"), None, None),
        P(("groups", "gx"), None, None),
        P(),
        P("gx", "gy"),
        P("gx", "gy"),
        P("groups"),
    )
    return jax.shard_map(
        shards,
        mesh=mesh,
        in_specs=placed,
        out_specs=(P(("groups", "gx"), None, "gy"), P(("groups", "gx"), "gy")),
        check_vma=False,
    )
```

time: 103 us -> 93.7 us (0.910)
  waiting for transfers between devices: 28.4 us -> 41 us
  Pallas kernels: 28.6 us -> 19.6 us
  local copies, waits for them, and re-layouts: 8.48 us -> 0.03 us
  starting transfers between devices: 36.1 us -> 32 us
    pallas_call x19 -> x17, Pallas kernels: 28.6 us -> 19.6 us  [call(): pl.pallas_call(body if ties else kernel, out_shape=out_shape, in_specs=[S...]
    ppermute x26, waiting for transfers between devices: 26.5 us -> 34.4 us  [the longest x14 18.1 us: send_on(): came[i][name] = lax.ppermute(block, 'gx', ahead if name == 'up' else behind)]
    unnamed x34 -> x12, local copies, waits for them, and re-layouts: 7.33 us -> 0.02 us
    ppermute x26, starting transfers between devices: 28.8 us -> 25.7 us  [the longest x14 13.5 us: send_on(): came[i][name] = lax.ppermute(block, 'gx', ahead if name == 'up' else behind)]
    ppermute x1, waiting for transfers between devices: 0.01 us -> 1.85 us  [shards(): lax.ppermute(up[0], 'gx', ahead)]
    ppermute x1, waiting for transfers between devices: 0.4 us -> 1.71 us  [shards(): passed = lax.ppermute(passing, 'groups', swap)]
    ppermute x1, waiting for transfers between devices: 0.01 us -> 1.3 us  [shards(): lax.ppermute(down[1], 'gx', behind)]
    ppermute x1, starting transfers between devices: 0.51 us -> 1.62 us  [shards(): lax.ppermute(up[0], 'gx', ahead)]
  transfers between devices with their start and end apart: 34 -> 34, of which waited for: 19 -> 24; matrix products, arithmetic and copies ran while one was open for 0% -> 0% of each run, Pallas kernels for 18% -> 13%
where the time goes in v13:
time: 93.7 us; the launch traced here: 93.5 us
  waiting for transfers between devices  41 us (44%)
  starting transfers between devices  32 us (34%)
  Pallas kernels  19.6 us (21%)
    pallas_call x17, Pallas kernels, call(): pl.pallas_call(body if ties else kernel, out_shape=out_shape, in_specs=[S...  19.6 us
    ppermute x14, waiting for transfers between devices, send_on(): came[i][name] = lax.ppermute(block, 'gx', ahead if name == 'up' else behind)  18.1 us
    ppermute x14, starting transfers between devices, send_on(): came[i][name] = lax.ppermute(block, 'gx', ahead if name == 'up' else behind)  13.5 us
    ppermute x6, waiting for transfers between devices, shards(): up[i] = lax.ppermute(up[i], 'gx', ahead)  13.4 us
    ppermute x6, starting transfers between devices, shards(): up[i] = lax.ppermute(up[i], 'gx', ahead)  9.46 us
    ppermute x1, starting transfers between devices, shards(): first = lax.ppermute(passing, 'groups', swap)  3 us
    ppermute x6, waiting for transfers between devices, shards(): down[i] = lax.ppermute(down[i], 'gx', behind)  2.95 us
    ppermute x6, starting transfers between devices, shards(): down[i] = lax.ppermute(down[i], 'gx', behind)  2.7 us
  transfers between devices with their start and end apart: 34, of which 24 were waited for; matrix products, arithmetic and copies ran while one was open for 0% of the time, Pallas kernels for 13%

profile of v13, /device:TPU:0, one launch (start us, length us, event | category | flops | bytes accessed | tf_op | source)
XLA Modules:
  0.0 93.5 jit_solution(5877420365615884684)
XLA Ops:
  0.7 3.4 %shard_map.78 = (bf16[2,192,1280]{2,1,0:T(8,128)(2,1)}, bf16[160,640]{1,0:T(8,128)(2,1)}, bf16[160,640]{1,0:T(8,128)(2,1)}) custom-call(s32[8]{0:T(128)} %lengths.3, bf16[384,1280]{1,0:T(8,128)(2,1)} %bitcast.3, bf16[384,1280]{1,0:T(8,128)(2,1)} %bitcast.6, f32[1280]{0:T(1024)} %gain.3, bf16[160,1280]{1,0:T(8,128)(2,1)} %w_up.1, bf16[160,1280]{1,0:T(8,128)(2,1)} %w_down.1), custom_call_target="tpu_custom_call" | custom-call | flops 2457600 | bytes 4183072 | tf_op jit(solution)/shard_map/pallas_call | solution.py:28
  4.1 3.0 %collective-permute-start = (bf16[2,192,1280]{2,1,0:T(8,128)(2,1)}, bf16[2,192,1280]{2,1,0:T(8,128)(2,1)S(1)}, u32[]{:S(2)}, u32[]{:S(2)}) collective-permute-start(bf16[2,192,1280]{2,1,0:T(8,128)(2,1)} %get-tuple-element.37), channel_id=1, source_target_pairs={{0,16},{16,0},{1,17},{17,1},{2,18},{18,2},{3,19},{19,3},{4,20},{20... | collective-permute-start | bytes 2949128 | tf_op jit(solution)/shard_map/ppermute | solution.py:265
  7.1 1.6 %collective-permute-start.1 = (bf16[160,640]{1,0:T(8,128)(2,1)}, bf16[160,640]{1,0:T(8,128)(2,1)S(1)}, u32[]{:S(2)}, u32[]{:S(2)}) collective-permute-start(bf16[160,640]{1,0:T(8,128)(2,1)} %get-tuple-element.38.refs_0_), channel_id=1, source_target_pairs={{0,4},{4,8},{8,12},{12,14},{14,10},{10,6},{6,2},{2,0},{1,5},{5,9},... | collective-permute-start | bytes 614408 | tf_op jit(solution)/shard_map/ppermute | solution.py:279
  12.6 2.6 %collective-permute-done.1.refs_0_ = bf16[160,640]{1,0:T(8,128)(2,1)S(1)} collective-permute-done((bf16[160,640]{1,0:T(8,128)(2,1)}, bf16[160,640]{1,0:T(8,128)(2,1)S(1)}, u32[]{:S(2)}, u32[]{:S(2)}) %collective-permute-start.1) | collective-permute-done | bytes 204832 | tf_op jit(solution)/shard_map/ppermute | solution.py:279
  15.3 1.6 %collective-permute-start.2 = (bf16[160,640]{1,0:T(8,128)(2,1)S(1)}, bf16[160,640]{1,0:T(8,128)(2,1)S(1)}, u32[]{:S(2)}, u32[]{:S(2)}) collective-permute-start(bf16[160,640]{1,0:T(8,128)(2,1)S(1)} %shard_map.79.refs_2_), channel_id=1, source_target_pairs={{0,4},{4,8},{8,12},{12,14},{14,10},{10,6},{6,2},{2,0},{1,5},{5,9},... | collective-permute-start | bytes 614408 | tf_op jit(solution)/shard_map/ppermute | solution.py:279
  17.3 2.3 %collective-permute-done.4.refs_4_ = bf16[160,640]{1,0:T(8,128)(2,1)S(1)} collective-permute-done((bf16[160,640]{1,0:T(8,128)(2,1)}, bf16[160,640]{1,0:T(8,128)(2,1)S(1)}, u32[]{:S(2)}, u32[]{:S(2)}) %collective-permute-start.4) | collective-permute-done | bytes 204832 | tf_op jit(solution)/shard_map/ppermute | solution.py:279
  19.7 1.6 %collective-permute-start.5 = (bf16[160,640]{1,0:T(8,128)(2,1)S(1)}, bf16[160,640]{1,0:T(8,128)(2,1)S(1)}, u32[]{:S(2)}, u32[]{:S(2)}) collective-permute-start(bf16[160,640]{1,0:T(8,128)(2,1)S(1)} %collective-permute-done.4.refs_4_), channel_id=1, source_target_pairs={{0,4},{4,8},{8,12},{12,14},{14,10},{10,6},{6,2},{2,0},{1,5},{5,9},... | collective-permute-start | bytes 614408 | tf_op jit(solution)/shard_map/ppermute | solution.py:279
  21.7 2.3 %collective-permute-done.2.refs_6_ = bf16[160,640]{1,0:T(8,128)(2,1)S(1)} collective-permute-done((bf16[160,640]{1,0:T(8,128)(2,1)S(1)}, bf16[160,640]{1,0:T(8,128)(2,1)S(1)}, u32[]{:S(2)}, u32[]{:S(2)}) %collective-permute-start.2) | collective-permute-done | bytes 204832 | tf_op jit(solution)/shard_map/ppermute | solution.py:279
  26.1 2.3 %collective-permute-done.5.refs_8_ = bf16[160,640]{1,0:T(8,128)(2,1)S(1)} collective-permute-done((bf16[160,640]{1,0:T(8,128)(2,1)S(1)}, bf16[160,640]{1,0:T(8,128)(2,1)S(1)}, u32[]{:S(2)}, u32[]{:S(2)}) %collective-permute-start.5) | collective-permute-done | bytes 204832 | tf_op jit(solution)/shard_map/ppermute | solution.py:279
  30.5 2.3 %collective-permute-done.3.refs_1_.refs_10_ = bf16[160,640]{1,0:T(8,128)(2,1)S(1)} collective-permute-done((bf16[160,640]{1,0:T(8,128)(2,1)S(1)}, bf16[160,640]{1,0:T(8,128)(2,1)S(1)}, u32[]{:S(2)}, u32[]{:S(2)}) %collective-permute-start.3) | collective-permute-done | bytes 204832 | tf_op jit(solution)/shard_map/ppermute | solution.py:279
  32.8 1.6 %collective-permute-done.12.refs_4_.refs_11_ = bf16[160,640]{1,0:T(8,128)(2,1)S(1)} collective-permute-done((bf16[160,640]{1,0:T(8,128)(2,1)S(1)}, bf16[160,640]{1,0:T(8,128)(2,1)S(1)}, u32[]{:S(2)}, u32[]{:S(2)}) %collective-permute-start.12) | collective-permute-done | bytes 204832 | tf_op jit(solution)/shard_map/ppermute | solution.py:280
  37.1 1.6 %collective-permute-start.14 = (bf16[160,640]{1,0:T(8,128)(2,1)S(1)}, bf16[160,640]{1,0:T(8,128)(2,1)S(1)}, u32[]{:S(2)}, u32[]{:S(2)}) collective-permute-start(bf16[160,640]{1,0:T(8,128)(2,1)S(1)} %collective-permute-done.3.refs_1_.refs_10_), channel_id=1, source_target_pairs={{0,4},{4,8},{8,12},{12,14},{14,10},{10,6},{6,2},{2,0},{1,5},{5,9},... | collective-permute-start | bytes 614408 | tf_op jit(solution)/shard_map/ppermute | solution.py:289
  39.1 3.6 %shard_map.81 = (bf16[1280,640]{1,0:T(8,128)(2,1)S(1)}, bf16[1280,640]{1,0:T(8,128)(2,1)S(1)}) custom-call(bf16[160,640]{1,0:T(8,128)(2,1)S(1)} %copy-done.2, bf16[160,640]{1,0:T(8,128)(2,1)S(1)} %copy-done.3, bf16[160,640]{1,0:T(8,128)(2,1)S(1)} %shard_map.79.refs_2_, bf16[160,640]{1,0:T(8,128)(2,1)S(1)} %collective-permute-done.7.refs_3_, ...), custom_call_target="tpu_custom_call" | custom-call | flops 1 | bytes 5734400 | tf_op jit(solution)/shard_map/pallas_call | solution.py:28
  42.7 1.9 %collective-permute-done.14.refs_2_ = bf16[160,640]{1,0:T(8,128)(2,1)S(1)} collective-permute-done((bf16[160,640]{1,0:T(8,128)(2,1)S(1)}, bf16[160,640]{1,0:T(8,128)(2,1)S(1)}, u32[]{:S(2)}, u32[]{:S(2)}) %collective-permute-start.14) | collective-permute-done | bytes 204832 | tf_op jit(solution)/shard_map/ppermute | solution.py:289
  45.9 2.9 %shard_map.82 = (bf16[384,640]{1,0:T(8,128)(2,1)S(1)}, bf16[1280,640]{1,0:T(8,128)(2,1)S(1)}, bf16[1280,640]{1,0:T(8,128)(2,1)S(1)}, bf16[1280,640]{1,0:T(8,128)...) custom-call(bf16[2,192,1280]{2,1,0:T(8,128)(2,1)S(1)} %shard_map.80.first, ...), custom_call_target="tpu_custom_call" | custom-call | flops 1887436800 | bytes 11878400 | tf_op jit(solution)/shard_map/pallas_call | solution.py:28
  48.8 1.6 %collective-permute-start.16 = (bf16[160,640]{1,0:T(8,128)(2,1)S(1)}, bf16[160,640]{1,0:T(8,128)(2,1)S(1)}, u32[]{:S(2)}, u32[]{:S(2)}) collective-permute-start(bf16[160,640]{1,0:T(8,128)(2,1)S(1)} %get-tuple-element.47), channel_id=1, source_target_pairs={{0,4},{4,8},{8,12},{12,14},{14,10},{10,6},{6,2},{2,0},{1,5},{5,9},... | collective-permute-start | bytes 614408 | tf_op jit(solution)/shard_map/ppermute | solution.py:360
  50.9 2.7 %shard_map.83 = (bf16[384,640]{1,0:T(8,128)(2,1)S(1)}, bf16[1280,640]{1,0:T(8,128)(2,1)S(1)}, bf16[160,640]{1,0:T(8,128)(2,1)S(1)}, bf16[160,640]{1,0:T(8,128)(2,1)S(1)}) custom-call(bf16[384,1280]{1,0:T(8,128)(2,1)S(1)} %get-tuple-element.35.refs_1_.normed, bf16[384,1280]{1,0:T(8,128)(2,1)S(1)} %get-tuple-element.36.grads.refs_5_, ...), custom_call_target="tpu_custom_call" | custom-call | flops 1887436800 | bytes 7782400 | tf_op jit(solution)/shard_map/pallas_call | solution.py:28
  53.6 1.6 %collective-permute-start.18 = (bf16[160,640]{1,0:T(8,128)(2,1)S(1)}, bf16[160,640]{1,0:T(8,128)(2,1)S(1)}, u32[]{:S(2)}, u32[]{:S(2)}) collective-permute-start(bf16[160,640]{1,0:T(8,128)(2,1)S(1)} %get-tuple-element.53), channel_id=1, source_target_pairs={{0,4},{4,8},{8,12},{12,14},{14,10},{10,6},{6,2},{2,0},{1,5},{5,9},... | collective-permute-start | bytes 614408 | tf_op jit(solution)/shard_map/ppermute | solution.py:360
  56.7 1.6 %collective-permute-start.20 = (bf16[160,640]{1,0:T(8,128)(2,1)S(1)}, bf16[160,640]{1,0:T(8,128)(2,1)S(1)}, u32[]{:S(2)}, u32[]{:S(2)}) collective-permute-start(bf16[160,640]{1,0:T(8,128)(2,1)S(1)} %get-tuple-element.50.refs_3_), channel_id=1, source_target_pairs={{0,4},{4,8},{8,12},{12,14},{14,10},{10,6},{6,2},{2,0},{1,5},{5,9},... | collective-permute-start | bytes 614408 | tf_op jit(solution)/shard_map/ppermute | solution.py:360
  58.8 2.0 %shard_map.85 = (bf16[2,384,640]{2,1,0:T(8,128)(2,1)S(1)}, bf16[2,384,640]{2,1,0:T(8,128)(2,1)S(1)}) custom-call(bf16[384,640]{1,0:T(8,128)(2,1)S(1)} %get-tuple-element.44.refs_0_, bf16[384,640]{1,0:T(8,128)(2,1)S(1)} %get-tuple-element.45.refs_1_, bf16[1280,640]{1,0:T(8,128)(2,1)S(1)} %get-tuple-element.42.up.refs_2_, ...), custom_call_target="tpu_custom_call" | custom-call | flops 1258291200 | bytes 4587520 | tf_op jit(solution)/shard_map/pallas_call | solution.py:28
  69.5 3.6 %collective-permute-done.23.refs_1_ = bf16[160,640]{1,0:T(8,128)(2,1)S(1)} collective-permute-done((bf16[160,640]{1,0:T(8,128)(2,1)S(1)}, bf16[160,640]{1,0:T(8,128)(2,1)S(1)}, u32[]{:S(2)}, u32[]{:S(2)}) %collective-permute-start.23) | collective-permute-done | bytes 204832 | tf_op jit(solution)/shard_map/ppermute | solution.py:360
  79.5 2.0 %collective-permute-done.29.refs_1_ = bf16[160,640]{1,0:T(8,128)(2,1)S(1)} collective-permute-done((bf16[160,640]{1,0:T(8,128)(2,1)S(1)}, bf16[160,640]{1,0:T(8,128)(2,1)S(1)}, u32[]{:S(2)}, u32[]{:S(2)}) %collective-permute-start.29) | collective-permute-done | bytes 204832 | tf_op jit(solution)/shard_map/ppermute | solution.py:360
  83.2 3.3 %collective-permute-done.28.refs_2_ = bf16[160,640]{1,0:T(8,128)(2,1)S(1)} collective-permute-done((bf16[160,640]{1,0:T(8,128)(2,1)S(1)}, bf16[160,640]{1,0:T(8,128)(2,1)S(1)}, u32[]{:S(2)}, u32[]{:S(2)}) %collective-permute-start.28) | collective-permute-done | bytes 204832 | tf_op jit(solution)/shard_map/ppermute | solution.py:360
  90.7 1.7 %collective-permute-done.33.refs_3_ = bf16[160,640]{1,0:T(8,128)(2,1)S(1)} collective-permute-done((bf16[160,640]{1,0:T(8,128)(2,1)S(1)}, bf16[160,640]{1,0:T(8,128)(2,1)S(1)}, u32[]{:S(2)}, u32[]{:S(2)}) %collective-permute-start.33) | collective-permute-done | bytes 204832 | tf_op jit(solution)/shard_map/ppermute | solution.py:397
  (77 shorter events, 37.7 us)
Async XLA Ops:
  4.1 33.0 %collective-permute-start = (bf16[2,192,1280]{2,1,0:T(8,128)(2,1)}, bf16[2,192,1280]{2,1,0:T(8,128)(2,1)S(1)}, u32[]{:S(2)}, u32[]{:S(2)}) collective-permute-start(bf16[2,192,1280]{2,1,0:T(8,128)(2,1)} %get-tuple-element.37), channel_id=1, source_target_pairs={{0,16},{16,0},{1,17},{17,1},{2,18},{18,2},{3,19},{19,3},{4,20},{20... | collective-permute-start | bytes 2949128 | tf_op jit(solution)/shard_map/ppermute | solution.py:265
  7.1 8.2 %collective-permute-start.1 = (bf16[160,640]{1,0:T(8,128)(2,1)}, bf16[160,640]{1,0:T(8,128)(2,1)S(1)}, u32[]{:S(2)}, u32[]{:S(2)}) collective-permute-start(bf16[160,640]{1,0:T(8,128)(2,1)} %get-tuple-element.38.refs_0_), channel_id=1, source_target_pairs={{0,4},{4,8},{8,12},{12,14},{14,10},{10,6},{6,2},{2,0},{1,5},{5,9},... | collective-permute-start | bytes 614408 | tf_op jit(solution)/shard_map/ppermute | solution.py:279
  8.7 8.2 %collective-permute-start.10 = (bf16[160,640]{1,0:T(8,128)(2,1)}, bf16[160,640]{1,0:T(8,128)(2,1)S(1)}, u32[]{:S(2)}, u32[]{:S(2)}) collective-permute-start(bf16[160,640]{1,0:T(8,128)(2,1)} %get-tuple-element.39.refs_1_), channel_id=1, source_target_pairs={{4,0},{8,4},{12,8},{14,12},{10,14},{6,10},{2,6},{0,2},{5,1},{9,5},... | collective-permute-start | bytes 614408 | tf_op jit(solution)/shard_map/ppermute | solution.py:280
  9.1 10.6 %collective-permute-start.4 = (bf16[160,640]{1,0:T(8,128)(2,1)}, bf16[160,640]{1,0:T(8,128)(2,1)S(1)}, u32[]{:S(2)}, u32[]{:S(2)}) collective-permute-start(bf16[160,640]{1,0:T(8,128)(2,1)} %get-tuple-element.39.refs_1_), channel_id=1, source_target_pairs={{0,4},{4,8},{8,12},{12,14},{14,10},{10,6},{6,2},{2,0},{1,5},{5,9},... | collective-permute-start | bytes 614408 | tf_op jit(solution)/shard_map/ppermute | solution.py:279
  10.7 10.6 %collective-permute-start.7 = (bf16[160,640]{1,0:T(8,128)(2,1)}, bf16[160,640]{1,0:T(8,128)(2,1)S(1)}, u32[]{:S(2)}, u32[]{:S(2)}) collective-permute-start(bf16[160,640]{1,0:T(8,128)(2,1)} %get-tuple-element.38.refs_0_), channel_id=1, source_target_pairs={{4,0},{8,4},{12,8},{14,12},{10,14},{6,10},{2,6},{0,2},{5,1},{9,5},... | collective-permute-start | bytes 614408 | tf_op jit(solution)/shard_map/ppermute | solution.py:280
  15.3 8.8 %collective-permute-start.2 = (bf16[160,640]{1,0:T(8,128)(2,1)S(1)}, bf16[160,640]{1,0:T(8,128)(2,1)S(1)}, u32[]{:S(2)}, u32[]{:S(2)}) collective-permute-start(bf16[160,640]{1,0:T(8,128)(2,1)S(1)} %shard_map.79.refs_2_), channel_id=1, source_target_pairs={{0,4},{4,8},{8,12},{12,14},{14,10},{10,6},{6,2},{2,0},{1,5},{5,9},... | collective-permute-start | bytes 614408 | tf_op jit(solution)/shard_map/ppermute | solution.py:279
  16.9 8.8 %collective-permute-start.11 = (bf16[160,640]{1,0:T(8,128)(2,1)S(1)}, bf16[160,640]{1,0:T(8,128)(2,1)S(1)}, u32[]{:S(2)}, u32[]{:S(2)}) collective-permute-start(bf16[160,640]{1,0:T(8,128)(2,1)S(1)} %collective-permute-done.10.refs_5_), channel_id=1, source_target_pairs={{4,0},{8,4},{12,8},{14,12},{10,14},{6,10},{2,6},{0,2},{5,1},{9,5},... | collective-permute-start | bytes 614408 | tf_op jit(solution)/shard_map/ppermute | solution.py:280
  19.7 8.8 %collective-permute-start.5 = (bf16[160,640]{1,0:T(8,128)(2,1)S(1)}, bf16[160,640]{1,0:T(8,128)(2,1)S(1)}, u32[]{:S(2)}, u32[]{:S(2)}) collective-permute-start(bf16[160,640]{1,0:T(8,128)(2,1)S(1)} %collective-permute-done.4.refs_4_), channel_id=1, source_target_pairs={{0,4},{4,8},{8,12},{12,14},{14,10},{10,6},{6,2},{2,0},{1,5},{5,9},... | collective-permute-start | bytes 614408 | tf_op jit(solution)/shard_map/ppermute | solution.py:279
  21.3 8.8 %collective-permute-start.8 = (bf16[160,640]{1,0:T(8,128)(2,1)S(1)}, bf16[160,640]{1,0:T(8,128)(2,1)S(1)}, u32[]{:S(2)}, u32[]{:S(2)}) collective-permute-start(bf16[160,640]{1,0:T(8,128)(2,1)S(1)} %collective-permute-done.7.refs_3_), channel_id=1, source_target_pairs={{4,0},{8,4},{12,8},{14,12},{10,14},{6,10},{2,6},{0,2},{5,1},{9,5},... | collective-permute-start | bytes 614408 | tf_op jit(solution)/shard_map/ppermute | solution.py:280
  24.1 8.8 %collective-permute-start.3 = (bf16[160,640]{1,0:T(8,128)(2,1)S(1)}, bf16[160,640]{1,0:T(8,128)(2,1)S(1)}, u32[]{:S(2)}, u32[]{:S(2)}) collective-permute-start(bf16[160,640]{1,0:T(8,128)(2,1)S(1)} %collective-permute-done.2.refs_6_), channel_id=1, source_target_pairs={{0,4},{4,8},{8,12},{12,14},{14,10},{10,6},{6,2},{2,0},{1,5},{5,9},... | collective-permute-start | bytes 614408 | tf_op jit(solution)/shard_map/ppermute | solution.py:279
  25.7 8.8 %collective-permute-start.12 = (bf16[160,640]{1,0:T(8,128)(2,1)S(1)}, bf16[160,640]{1,0:T(8,128)(2,1)S(1)}, u32[]{:S(2)}, u32[]{:S(2)}) collective-permute-start(bf16[160,640]{1,0:T(8,128)(2,1)S(1)} %collective-permute-done.11.refs_9_), channel_id=1, source_target_pairs={{4,0},{8,4},{12,8},{14,12},{10,14},{6,10},{2,6},{0,2},{5,1},{9,5},... | collective-permute-start | bytes 614408 | tf_op jit(solution)/shard_map/ppermute | solution.py:280
  37.1 8.8 %collective-permute-start.13 = (bf16[2,192,1280]{2,1,0:T(8,128)(2,1)S(1)}, bf16[2,192,1280]{2,1,0:T(8,128)(2,1)S(1)}, u32[]{:S(2)}, u32[]{:S(2)}) collective-permute-start(bf16[2,192,1280]{2,1,0:T(8,128)(2,1)S(1)} %shard_map.80.first), channel_id=1, source_target_pairs={{0,1},{1,0},{2,3},{3,2},{4,5},{5,4},{6,7},{7,6},{8,9},{9,8},{10,11... | collective-permute-start | bytes 2949128 | tf_op jit(solution)/shard_map/ppermute | solution.py:303
  37.1 7.5 %collective-permute-start.14 = (bf16[160,640]{1,0:T(8,128)(2,1)S(1)}, bf16[160,640]{1,0:T(8,128)(2,1)S(1)}, u32[]{:S(2)}, u32[]{:S(2)}) collective-permute-start(bf16[160,640]{1,0:T(8,128)(2,1)S(1)} %collective-permute-done.3.refs_1_.refs_10_), channel_id=1, source_target_pairs={{0,4},{4,8},{8,12},{12,14},{14,10},{10,6},{6,2},{2,0},{1,5},{5,9},... | collective-permute-start | bytes 614408 | tf_op jit(solution)/shard_map/ppermute | solution.py:289
  53.6 8.1 %collective-permute-start.18 = (bf16[160,640]{1,0:T(8,128)(2,1)S(1)}, bf16[160,640]{1,0:T(8,128)(2,1)S(1)}, u32[]{:S(2)}, u32[]{:S(2)}) collective-permute-start(bf16[160,640]{1,0:T(8,128)(2,1)S(1)} %get-tuple-element.53), channel_id=1, source_target_pairs={{0,4},{4,8},{8,12},{12,14},{14,10},{10,6},{6,2},{2,0},{1,5},{5,9},... | collective-permute-start | bytes 614408 | tf_op jit(solution)/shard_map/ppermute | solution.py:360
  55.2 7.9 %collective-permute-start.19 = (bf16[160,640]{1,0:T(8,128)(2,1)S(1)}, bf16[160,640]{1,0:T(8,128)(2,1)S(1)}, u32[]{:S(2)}, u32[]{:S(2)}) collective-permute-start(bf16[160,640]{1,0:T(8,128)(2,1)S(1)} %get-tuple-element.54), channel_id=1, source_target_pairs={{4,0},{8,4},{12,8},{14,12},{10,14},{6,10},{2,6},{0,2},{5,1},{9,5},... | collective-permute-start | bytes 614408 | tf_op jit(solution)/shard_map/ppermute | solution.py:360
  65.3 9.6 %collective-permute-start.22 = (bf16[2,384,640]{2,1,0:T(8,128)(2,1)S(1)}, bf16[2,384,640]{2,1,0:T(8,128)(2,1)S(1)}, u32[]{:S(2)}, u32[]{:S(2)}) collective-permute-start(bf16[2,384,640]{2,1,0:T(8,128)(2,1)S(1)} %shard_map.87), channel_id=1, source_target_pairs={{0,1},{1,0},{2,3},{3,2},{4,5},{5,4},{6,7},{7,6},{8,9},{9,8},{10,11... | collective-permute-start | bytes 2949128 | tf_op jit(solution)/shard_map/ppermute | solution.py:383
  65.3 7.9 %collective-permute-start.23 = (bf16[160,640]{1,0:T(8,128)(2,1)S(1)}, bf16[160,640]{1,0:T(8,128)(2,1)S(1)}, u32[]{:S(2)}, u32[]{:S(2)}) collective-permute-start(bf16[160,640]{1,0:T(8,128)(2,1)S(1)} %get-tuple-element.55.refs_1_.refs_3_), channel_id=1, source_target_pairs={{0,4},{4,8},{8,12},{12,14},{14,10},{10,6},{6,2},{2,0},{1,5},{5,9},... | collective-permute-start | bytes 614408 | tf_op jit(solution)/shard_map/ppermute | solution.py:360
  66.8 7.9 %collective-permute-start.24 = (bf16[160,640]{1,0:T(8,128)(2,1)S(1)}, bf16[160,640]{1,0:T(8,128)(2,1)S(1)}, u32[]{:S(2)}, u32[]{:S(2)}) collective-permute-start(bf16[160,640]{1,0:T(8,128)(2,1)S(1)} %get-tuple-element.57), channel_id=1, source_target_pairs={{4,0},{8,4},{12,8},{14,12},{10,14},{6,10},{2,6},{0,2},{5,1},{9,5},... | collective-permute-start | bytes 614408 | tf_op jit(solution)/shard_map/ppermute | solution.py:360
  67.4 10.1 %collective-permute-start.26 = (bf16[160,640]{1,0:T(8,128)(2,1)S(1)}, bf16[160,640]{1,0:T(8,128)(2,1)S(1)}, u32[]{:S(2)}, u32[]{:S(2)}) collective-permute-start(bf16[160,640]{1,0:T(8,128)(2,1)S(1)} %get-tuple-element.58.refs_3_), channel_id=1, source_target_pairs={{0,4},{4,8},{8,12},{12,14},{14,10},{10,6},{6,2},{2,0},{1,5},{5,9},... | collective-permute-start | bytes 614408 | tf_op jit(solution)/shard_map/ppermute | solution.py:360
  69.0 9.4 %collective-permute-start.27 = (bf16[160,640]{1,0:T(8,128)(2,1)S(1)}, bf16[160,640]{1,0:T(8,128)(2,1)S(1)}, u32[]{:S(2)}, u32[]{:S(2)}) collective-permute-start(bf16[160,640]{1,0:T(8,128)(2,1)S(1)} %get-tuple-element.61), channel_id=1, source_target_pairs={{4,0},{8,4},{12,8},{14,12},{10,14},{6,10},{2,6},{0,2},{5,1},{9,5},... | collective-permute-start | bytes 614408 | tf_op jit(solution)/shard_map/ppermute | solution.py:360
  75.0 12.5 %collective-permute-start.25 = (bf16[384,640]{1,0:T(8,128)(2,1)S(1)}, bf16[384,640]{1,0:T(8,128)(2,1)S(1)}, u32[]{:S(2)}, u32[]{:S(2)}) collective-permute-start(bf16[384,640]{1,0:T(8,128)(2,1)S(1)} %shard_map.90.refs_2_), channel_id=1, source_target_pairs={{0,16},{16,0},{1,17},{17,1},{2,18},{18,2},{3,19},{19,3},{4,20},{20... | collective-permute-start | bytes 1474568 | tf_op jit(solution)/shard_map/ppermute | solution.py:387
  78.5 8.1 %collective-permute-start.28 = (bf16[160,640]{1,0:T(8,128)(2,1)S(1)}, bf16[160,640]{1,0:T(8,128)(2,1)S(1)}, u32[]{:S(2)}, u32[]{:S(2)}) collective-permute-start(bf16[160,640]{1,0:T(8,128)(2,1)S(1)} %shard_map.91.refs_2_), channel_id=1, source_target_pairs={{4,0},{8,4},{12,8},{14,12},{10,14},{6,10},{2,6},{0,2},{5,1},{9,5},... | collective-permute-start | bytes 614408 | tf_op jit(solution)/shard_map/ppermute | solution.py:360
  79.0 11.7 %collective-permute-start.32 = (bf16[160,640]{1,0:T(8,128)(2,1)S(1)}, bf16[160,640]{1,0:T(8,128)(2,1)S(1)}, u32[]{:S(2)}, u32[]{:S(2)}) collective-permute-start(bf16[160,640]{1,0:T(8,128)(2,1)S(1)} %get-tuple-element.66), channel_id=1, source_target_pairs={{4,0},{8,4},{12,8},{14,12},{10,14},{6,10},{2,6},{0,2},{5,1},{9,5},... | collective-permute-start | bytes 614408 | tf_op jit(solution)/shard_map/ppermute | solution.py:360
  81.6 9.1 %collective-permute-start.31 = (bf16[160,640]{1,0:T(8,128)(2,1)S(1)}, bf16[160,640]{1,0:T(8,128)(2,1)S(1)}, u32[]{:S(2)}, u32[]{:S(2)}) collective-permute-start(bf16[160,640]{1,0:T(8,128)(2,1)S(1)} %shard_map.92.refs_3_), channel_id=1, source_target_pairs={{0,4},{4,8},{8,12},{12,14},{14,10},{10,6},{6,2},{2,0},{1,5},{5,9},... | collective-permute-start | bytes 614408 | tf_op jit(solution)/shard_map/ppermute | solution.py:360
  (16 other events, 151.7 us)

commit v14 on v13

--- a/solution.py
+++ b/solution.py
@@ -137,13 +137,9 @@
         copy.wait()
 
 
-def other_kernel(places, sends, peers, first, second, near_up, near_down, *refs):
+def own_kernel(places, sends, peers, normed, grads, near_up, near_down, *refs):
     late, refs = refs[: len(places)], refs[len(places) :]
-    (d_pre, partial, up, down), blocks, (normed, grads) = refs[:4], refs[4:-2], refs[-2:]
-    half = first.shape[1]
-    for at, part in ((0, first), (half, second)):
-        normed[at : at + half, :] = part[0]
-        grads[at : at + half, :] = part[1]
+    (d_pre, partial, up, down), blocks = refs[:4], refs[4:]
     up[...] = near_up[...]
     down[...] = near_down[...]
     for (step, which), block in zip(places, late):
@@ -153,32 +149,40 @@
         block[...] = partial[block_rows(step, peers, block.shape[0]), :]
 
 
-def own_kernel(sends, peers, normed, grads, up, down, d_pre, partial, *blocks):
+def other_kernel(sends, peers, first, second, up, down, d_pre, partial, *refs):
+    blocks, (normed, grads) = refs[:-2], refs[-2:]
+    half = first.shape[1]
+    for at, part in ((0, first), (half, second)):
+        normed[at : at + half, :] = part[0]
+        grads[at : at + half, :] = part[1]
     back_through(normed, grads, up, down, d_pre, partial)
     for step, block in zip(sends, blocks):
         block[...] = partial[block_rows(step, peers, block.shape[0]), :]
 
 
-def d_norm_kernel(d_pre_own, d_pre_other, up, keep, send):
+def d_norm_kernel(d_pre_own, d_pre_other, up, keep, send_own, *sends):
     core = lax.axis_index("gy")
     rows, width = keep.shape[1:]
     mine = up[pl.ds(pl.multiple_of(core * width, width), width), :]
     theirs = up[pl.ds(pl.multiple_of((1 - core) * width, width), width), :]
     keep[0] = dot(d_pre_own[...], mine, 1, 1).astype(BF16)
     keep[1] = dot(d_pre_other[...], mine, 1, 1).astype(BF16)
-    send[0] = dot(d_pre_own[...], theirs, 1, 1).astype(BF16)
+    send_own[...] = dot(d_pre_own[...], theirs, 1, 1).astype(BF16)
     sent = dot(d_pre_other[...], theirs, 1, 1).astype(BF16)
-    send[1, rows // 2 :, :] = sent[: rows // 2]
-    send[1, : rows // 2, :] = sent[rows // 2 :]
-
-
-def over_kernel(keep, came, over):
+    sent = jnp.concatenate([sent[rows // 2 :], sent[: rows // 2]])
+    step = rows // len(sends)
+    for i, send in enumerate(sends):
+        send[...] = sent[i * step : (i + 1) * step]
+
+
+def over_kernel(keep, *refs):
+    parts, over = refs[:-1], refs[-1]
     half = over.shape[0] // 2
+    value = jnp.concatenate([part[...].astype(F32) for part in parts])
+    value = (keep[1].astype(F32) + value).astype(BF16)
     for i in range(2):
         at = lax.rem(i + lax.axis_index("gy"), 2) * half
-        rows = slice(i * half, (i + 1) * half)
-        value = keep[1, rows, :].astype(F32) + came[1, rows, :].astype(F32)
-        over[pl.ds(pl.multiple_of(at, half), half), :] = value.astype(BF16)
+        over[pl.ds(pl.multiple_of(at, half), half), :] = value[i * half : (i + 1) * half]
 
 
 def own_columns(ref, width):
@@ -187,7 +191,7 @@
 
 def scale_kernel(keep, came, back, frames, gain, grads, stats, base, factor, sums):
     width = base.shape[1]
-    d_norm = keep[0].astype(F32) + came[0].astype(F32) + back[...].astype(F32)
+    d_norm = keep[0].astype(F32) + came[...].astype(F32) + back[...].astype(F32)
     scaled = d_norm * own_columns(gain, width)
     rows = own_columns(frames, width).astype(F32)
     inv_std = stats[:, 1:2]
@@ -282,7 +286,6 @@
                 up[0] = hold(up[0], normed)
             for i in range(2):
                 blocks[-step, i], blocks[step, i] = up[i], down[i]
-        first = hold(first, *up, *down)
         late = {
             (half - 1, 0): blocks.pop((half - 1, 0)),
             (1 - half, 1): blocks.pop((1 - half, 1)),
@@ -296,6 +299,7 @@
             [pltpu.SemaphoreType.DMA((len(blocks),))],
             pinned=range(len(blocks)),
         )
+        first = hold(first, *late.values())
         sends = ((half - 1, -half), (half, 1 - half))
     else:
         near = [lax.all_gather(block, "gx", axis=0, tiled=True) for block in mine]
@@ -303,34 +307,37 @@
     second = lax.ppermute(first, "gy", swap)
 
     d_pre_of, partial_of = shape((frame_len, quarter), BF16), shape((width, quarter), BF16)
-    d_pre_other, partial_other, full_up, full_down, *blocks_other = call(
-        functools.partial(other_kernel, tuple(late), sends[0], peers),
-        (first, second, *near, *late.values()),
-        (d_pre_of, partial_of, weight, weight, *[block_of] * len(sends[0])),
+    d_pre_own, partial_own, full_up, full_down, *blocks_own = call(
+        functools.partial(own_kernel, tuple(late), sends[1], peers),
+        (normed, grads, *near, *late.values()),
+        (d_pre_of, partial_of, weight, weight, *[block_of] * len(sends[1])),
+        flops=6 * frame_len * width * quarter,
+    )
+    d_pre_other, partial_other, *blocks_other = call(
+        functools.partial(other_kernel, sends[0], peers),
+        (first, second, full_up, full_down),
+        (d_pre_of, partial_of, *[block_of] * len(sends[0])),
         [pltpu.VMEM((frame_len, width), BF16)] * 2,
         flops=6 * frame_len * width * quarter,
     )
-    d_pre_own, partial_own, *blocks_own = call(
-        functools.partial(own_kernel, sends[1], peers),
-        (normed, grads, full_up, full_down),
-        (d_pre_of, partial_of, *[block_of] * len(sends[1])),
-        flops=6 * frame_len * width * quarter,
-    )
     partial = [partial_own, partial_other]
 
     half_rows_of = shape((frame_len, half_width), BF16)
+    parts_of = [shape((frame_len // 3, half_width), BF16)] * 3
 
     def own_d_norm(*ties):
-        return call(
+        keep, send, *parts = call(
             d_norm_kernel,
             (d_pre_own, d_pre_other, full_up),
-            (shape((2, frame_len, half_width), BF16), shape((2, frame_len, half_width), BF16)),
+            (shape((2, frame_len, half_width), BF16), half_rows_of, *parts_of),
             flops=4 * frame_len * width * quarter,
             ties=ties,
         )
-
-    def over_cores(keep, came, *ties):
-        return call(over_kernel, (keep, came), half_rows_of, ties=ties)
+        return keep, send, [lax.ppermute(part, "gy", swap) for part in parts]
+
+    def over_cores(keep, parts, *ties):
+        over = call(over_kernel, (keep, *parts), half_rows_of, ties=ties)
+        return over, lax.ppermute(over, "groups", swap)
 
     def scale(keep, came, back, *ties):
         return call(
@@ -363,8 +370,7 @@
             ways = [("up", half - turn - i), ("down", turn + 1 - i - half)]
             ways = [way for way in ways if way[1] != 0]
             names = [name for name, _ in ways]
-            if i == 1:
-                ties += tuple(came[i][name] for name in came[i] if name not in names)
+            ties += tuple(came[i][name] for name in came[i] if name not in names)
             blocks = call(
                 functools.partial(hop_kernel, tuple(step for _, step in ways), peers),
                 (partial[i], *[came[i][name] for name in names]),
@@ -374,20 +380,17 @@
             send_on(i, blocks, names)
             return blocks[0]
 
+        send_on(0, blocks_own, ("up", "down"))
         send_on(1, blocks_other, ("up", "down"))
-        send_on(0, blocks_own, ("up", "down"))
-        tie = hop(1, 1, partial_own)
-        keep, send = own_d_norm(tie)
-        tie = hop(0, 1, send)
-        send = hold(send, tie, *came[1].values())
-        sent = lax.ppermute(send, "gy", swap)
-        tie = hop(1, 2, tie)
+        tie = hop(0, 1, partial_other)
+        keep, send, parts = own_d_norm(tie)
+        tie = hop(1, 1, keep)
         tie = hop(0, 2, tie)
-        over = over_cores(keep, sent, tie)
-        back = lax.ppermute(over, "groups", swap)
-        tie = over
+        over, back = over_cores(keep, parts, tie)
+        tie = hop(1, 2, over)
         for turn in range(3, half):
-            tie = hop(0, turn, hop(1, turn, tie))
+            tie = hop(1, turn, hop(0, turn, tie))
+        sent = lax.ppermute(hold(send, tie), "gy", swap)
         passing = call(
             functools.partial(total_kernel, peers),
             (partial[1], came[1]["up"], came[1]["down"]),
@@ -403,9 +406,9 @@
             ties=(token,),
         )
     else:
-        keep, send = own_d_norm()
+        keep, send, parts = own_d_norm()
         sent = lax.ppermute(send, "gy", swap)
-        back = lax.ppermute(over_cores(keep, sent), "groups", swap)
+        _, back = over_cores(keep, parts)
         input_grad, _ = input_gradient(*scale(keep, sent, back))
         total, passing = [
             lax.psum_scatter(p.astype(F32), "gx", scatter_dimension=0, tiled=True) for p in partial

time: 93.7 us -> 95.7 us (1.021)
  starting transfers between devices: 32 us -> 33 us
    ppermute x6, waiting for transfers between devices: 13.4 us -> 4.63 us  [shards(): up[i] = lax.ppermute(up[i], 'gx', ahead)]
    ppermute x6, waiting for transfers between devices: 2.95 us -> 11.4 us  [shards(): down[i] = lax.ppermute(down[i], 'gx', behind)]
    ppermute x1, waiting for transfers between devices: 1.71 us -> 2.84 us  [shards(): passed = lax.ppermute(passing, 'groups', swap)]
    ppermute x6, starting transfers between devices: 2.7 us -> 3.77 us  [shards(): down[i] = lax.ppermute(down[i], 'gx', behind)]
    ppermute x6, starting transfers between devices: 9.46 us -> 8.39 us  [shards(): up[i] = lax.ppermute(up[i], 'gx', ahead)]
    ppermute x14, starting transfers between devices: 13.5 us -> 14.5 us  [send_on(): came[i][name] = lax.ppermute(block, 'gx', ahead if name == 'up' else behind)]
  transfers between devices with their start and end apart: 34 -> 37, of which waited for: 24 -> 20; matrix products, arithmetic and copies ran while one was open for 0% -> 0% of each run, Pallas kernels for 13% -> 16%
where the time goes in v14:
time: 95.7 us; the launch traced here: 95.5 us
  waiting for transfers between devices  41.8 us (44%)
  starting transfers between devices  33 us (34%)
  Pallas kernels  19.8 us (21%)
    pallas_call x17, Pallas kernels, call(): pl.pallas_call(body if ties else kernel, out_shape=out_shape, in_specs=[S...  19.8 us
    ppermute x14, waiting for transfers between devices, send_on(): came[i][name] = lax.ppermute(block, 'gx', ahead if name == 'up' else behind)  18.9 us
    ppermute x14, starting transfers between devices, send_on(): came[i][name] = lax.ppermute(block, 'gx', ahead if name == 'up' else behind)  14.5 us
    ppermute x6, waiting for transfers between devices, shards(): down[i] = lax.ppermute(down[i], 'gx', behind)  11.4 us
    ppermute x6, starting transfers between devices, shards(): up[i] = lax.ppermute(up[i], 'gx', ahead)  8.39 us
    ppermute x6, waiting for transfers between devices, shards(): up[i] = lax.ppermute(up[i], 'gx', ahead)  4.63 us
    ppermute x6, starting transfers between devices, shards(): down[i] = lax.ppermute(down[i], 'gx', behind)  3.77 us
    ppermute x1, starting transfers between devices, shards(): first = lax.ppermute(passing, 'groups', swap)  3 us
  transfers between devices with their start and end apart: 37, of which 20 were waited for; matrix products, arithmetic and copies ran while one was open for 0% of the time, Pallas kernels for 16%

profile of v14, /device:TPU:0, one launch (start us, length us, event | category | flops | bytes accessed | tf_op | source)
XLA Modules:
  0.0 95.5 jit_solution(16932805272690697641)
XLA Ops:
  0.7 3.4 %shard_map.78 = (bf16[2,192,1280]{2,1,0:T(8,128)(2,1)}, bf16[160,640]{1,0:T(8,128)(2,1)}, bf16[160,640]{1,0:T(8,128)(2,1)}) custom-call(s32[8]{0:T(128)} %lengths.3, bf16[384,1280]{1,0:T(8,128)(2,1)} %bitcast.3, bf16[384,1280]{1,0:T(8,128)(2,1)} %bitcast.6, f32[1280]{0:T(1024)} %gain.3, bf16[160,1280]{1,0:T(8,128)(2,1)} %w_up.1, bf16[160,1280]{1,0:T(8,128)(2,1)} %w_down.1), custom_call_target="tpu_custom_call" | custom-call | flops 2457600 | bytes 4183072 | tf_op jit(solution)/shard_map/pallas_call | solution.py:28
  4.1 3.0 %collective-permute-start.14 = (bf16[2,192,1280]{2,1,0:T(8,128)(2,1)}, bf16[2,192,1280]{2,1,0:T(8,128)(2,1)S(1)}, u32[]{:S(2)}, u32[]{:S(2)}) collective-permute-start(bf16[2,192,1280]{2,1,0:T(8,128)(2,1)} %get-tuple-element.45), channel_id=1, source_target_pairs={{0,16},{16,0},{1,17},{17,1},{2,18},{18,2},{3,19},{19,3},{4,20},{20... | collective-permute-start | bytes 2949128 | tf_op jit(solution)/shard_map/ppermute | solution.py:269
  7.1 1.6 %collective-permute-start = (bf16[160,640]{1,0:T(8,128)(2,1)}, bf16[160,640]{1,0:T(8,128)(2,1)S(1)}, u32[]{:S(2)}, u32[]{:S(2)}) collective-permute-start(bf16[160,640]{1,0:T(8,128)(2,1)} %get-tuple-element.40.refs_0_), channel_id=1, source_target_pairs={{0,4},{4,8},{8,12},{12,14},{14,10},{10,6},{6,2},{2,0},{1,5},{5,9},... | collective-permute-start | bytes 614408 | tf_op jit(solution)/shard_map/ppermute | solution.py:283
  12.6 2.6 %collective-permute-done.refs_0_ = bf16[160,640]{1,0:T(8,128)(2,1)S(1)} collective-permute-done((bf16[160,640]{1,0:T(8,128)(2,1)}, bf16[160,640]{1,0:T(8,128)(2,1)S(1)}, u32[]{:S(2)}, u32[]{:S(2)}) %collective-permute-start) | collective-permute-done | bytes 204832 | tf_op jit(solution)/shard_map/ppermute | solution.py:283
  15.3 1.6 %collective-permute-start.4 = (bf16[160,640]{1,0:T(8,128)(2,1)S(1)}, bf16[160,640]{1,0:T(8,128)(2,1)S(1)}, u32[]{:S(2)}, u32[]{:S(2)}) collective-permute-start(bf16[160,640]{1,0:T(8,128)(2,1)S(1)} %shard_map.79.refs_2_), channel_id=1, source_target_pairs={{0,4},{4,8},{8,12},{12,14},{14,10},{10,6},{6,2},{2,0},{1,5},{5,9},... | collective-permute-start | bytes 614408 | tf_op jit(solution)/shard_map/ppermute | solution.py:283
  17.3 3.9 %collective-permute-done.1.refs_3_ = bf16[160,640]{1,0:T(8,128)(2,1)S(1)} collective-permute-done((bf16[160,640]{1,0:T(8,128)(2,1)}, bf16[160,640]{1,0:T(8,128)(2,1)S(1)}, u32[]{:S(2)}, u32[]{:S(2)}) %collective-permute-start.1) | collective-permute-done | bytes 204832 | tf_op jit(solution)/shard_map/ppermute | solution.py:284
  21.7 1.6 %collective-permute-start.6 = (bf16[160,640]{1,0:T(8,128)(2,1)S(1)}, bf16[160,640]{1,0:T(8,128)(2,1)S(1)}, u32[]{:S(2)}, u32[]{:S(2)}) collective-permute-start(bf16[160,640]{1,0:T(8,128)(2,1)S(1)} %collective-permute-done.2.refs_4_), channel_id=1, source_target_pairs={{0,4},{4,8},{8,12},{12,14},{14,10},{10,6},{6,2},{2,0},{1,5},{5,9},... | collective-permute-start | bytes 614408 | tf_op jit(solution)/shard_map/ppermute | solution.py:283
  24.1 1.6 %collective-permute-start.8 = (bf16[160,640]{1,0:T(8,128)(2,1)S(1)}, bf16[160,640]{1,0:T(8,128)(2,1)S(1)}, u32[]{:S(2)}, u32[]{:S(2)}) collective-permute-start(bf16[160,640]{1,0:T(8,128)(2,1)S(1)} %collective-permute-done.4.refs_6_), channel_id=1, source_target_pairs={{0,4},{4,8},{8,12},{12,14},{14,10},{10,6},{6,2},{2,0},{1,5},{5,9},... | collective-permute-start | bytes 614408 | tf_op jit(solution)/shard_map/ppermute | solution.py:283
  26.1 3.9 %collective-permute-done.5.refs_7_ = bf16[160,640]{1,0:T(8,128)(2,1)S(1)} collective-permute-done((bf16[160,640]{1,0:T(8,128)(2,1)S(1)}, bf16[160,640]{1,0:T(8,128)(2,1)S(1)}, u32[]{:S(2)}, u32[]{:S(2)}) %collective-permute-start.5) | collective-permute-done | bytes 204832 | tf_op jit(solution)/shard_map/ppermute | solution.py:284
  30.5 1.6 %collective-permute-start.11 = (bf16[160,640]{1,0:T(8,128)(2,1)S(1)}, bf16[160,640]{1,0:T(8,128)(2,1)S(1)}, u32[]{:S(2)}, u32[]{:S(2)}) collective-permute-start(bf16[160,640]{1,0:T(8,128)(2,1)S(1)} %collective-permute-done.6.refs_8_), channel_id=1, source_target_pairs={{0,4},{4,8},{8,12},{12,14},{14,10},{10,6},{6,2},{2,0},{1,5},{5,9},... | collective-permute-start | bytes 614408 | tf_op jit(solution)/shard_map/ppermute | solution.py:283
  33.3 1.6 %collective-permute-start.12 = (bf16[160,640]{1,0:T(8,128)(2,1)S(1)}, bf16[160,640]{1,0:T(8,128)(2,1)S(1)}, u32[]{:S(2)}, u32[]{:S(2)}) collective-permute-start(bf16[160,640]{1,0:T(8,128)(2,1)S(1)} %collective-permute-done.8.refs_10_), channel_id=1, source_target_pairs={{0,4},{4,8},{8,12},{12,14},{14,10},{10,6},{6,2},{2,0},{1,5},{5,9},... | collective-permute-start | bytes 614408 | tf_op jit(solution)/shard_map/ppermute | solution.py:292
  35.3 3.5 %collective-permute-done.10.refs_0_.refs_1_ = bf16[160,640]{1,0:T(8,128)(2,1)S(1)} collective-permute-done((bf16[160,640]{1,0:T(8,128)(2,1)S(1)}, bf16[160,640]{1,0:T(8,128)(2,1)S(1)}, u32[]{:S(2)}, u32[]{:S(2)}) %collective-permute-start.10) | collective-permute-done | bytes 204832 | tf_op jit(solution)/shard_map/ppermute | solution.py:284
  41.5 3.6 %shard_map.80 = (bf16[1280,640]{1,0:T(8,128)(2,1)S(1)}, bf16[1280,640]{1,0:T(8,128)(2,1)S(1)}) custom-call(bf16[160,640]{1,0:T(8,128)(2,1)S(1)} %copy-done.2, bf16[160,640]{1,0:T(8,128)(2,1)S(1)} %copy-done.3, bf16[160,640]{1,0:T(8,128)(2,1)S(1)} %shard_map.79.refs_2_, bf16[160,640]{1,0:T(8,128)(2,1)S(1)} %collective-permute-done.1.refs_3_, ...), custom_call_target="tpu_custom_call" | custom-call | flops 1 | bytes 5734400 | tf_op jit(solution)/shard_map/pallas_call | solution.py:28
  45.1 3.0 %shard_map.81 = (bf16[384,640]{1,0:T(8,128)(2,1)S(1)}, bf16[1280,640]{1,0:T(8,128)(2,1)S(1)}, bf16[1280,640]{1,0:T(8,128)(2,1)S(1)}, bf16[1280,640]{1,0:T(8,128)...) custom-call(bf16[384,1280]{1,0:T(8,128)(2,1)S(1)} %get-tuple-element.38.refs_1_.normed, ...), custom_call_target="tpu_custom_call" | custom-call | flops 1887436800 | bytes 11878400 | tf_op jit(solution)/shard_map/pallas_call | solution.py:28
  48.1 1.6 %collective-permute-start.16 = (bf16[160,640]{1,0:T(8,128)(2,1)S(1)}, bf16[160,640]{1,0:T(8,128)(2,1)S(1)}, u32[]{:S(2)}, u32[]{:S(2)}) collective-permute-start(bf16[160,640]{1,0:T(8,128)(2,1)S(1)} %get-tuple-element.50), channel_id=1, source_target_pairs={{0,4},{4,8},{8,12},{12,14},{14,10},{10,6},{6,2},{2,0},{1,5},{5,9},... | collective-permute-start | bytes 614408 | tf_op jit(solution)/shard_map/ppermute | solution.py:367
  50.1 2.7 %shard_map.83 = (bf16[384,640]{1,0:T(8,128)(2,1)S(1)}, bf16[1280,640]{1,0:T(8,128)(2,1)S(1)}, bf16[160,640]{1,0:T(8,128)(2,1)S(1)}, bf16[160,640]{1,0:T(8,128)(2,1)S(1)}) custom-call(bf16[2,192,1280]{2,1,0:T(8,128)(2,1)S(1)} %shard_map.82.first, bf16[2,192,1280]{2,1,0:T(8,128)(2,1)S(1)} %collective-permute-done.15.second, ...), custom_call_target="tpu_custom_call" | custom-call | flops 1887436800 | bytes 7782400 | tf_op jit(solution)/shard_map/pallas_call | solution.py:28
  52.9 1.6 %collective-permute-start.18 = (bf16[160,640]{1,0:T(8,128)(2,1)S(1)}, bf16[160,640]{1,0:T(8,128)(2,1)S(1)}, u32[]{:S(2)}, u32[]{:S(2)}) collective-permute-start(bf16[160,640]{1,0:T(8,128)(2,1)S(1)} %get-tuple-element.56), channel_id=1, source_target_pairs={{0,4},{4,8},{8,12},{12,14},{14,10},{10,6},{6,2},{2,0},{1,5},{5,9},... | collective-permute-start | bytes 614408 | tf_op jit(solution)/shard_map/ppermute | solution.py:367
  57.0 1.6 %collective-permute-start.25 = (bf16[160,640]{1,0:T(8,128)(2,1)S(1)}, bf16[160,640]{1,0:T(8,128)(2,1)S(1)}, u32[]{:S(2)}, u32[]{:S(2)}) collective-permute-start(bf16[160,640]{1,0:T(8,128)(2,1)S(1)} %get-tuple-element.53.refs_3_), channel_id=1, source_target_pairs={{0,4},{4,8},{8,12},{12,14},{14,10},{10,6},{6,2},{2,0},{1,5},{5,9},... | collective-permute-start | bytes 614408 | tf_op jit(solution)/shard_map/ppermute | solution.py:367
  59.1 2.0 %shard_map.85 = (bf16[2,384,640]{2,1,0:T(8,128)(2,1)S(1)}, bf16[384,640]{1,0:T(8,128)(2,1)S(1)}, bf16[128,640]{1,0:T(8,128)(2,1)S(1)}, bf16[128,640]{1,0:T(8,128)(2,1)S(1)}, bf16[128,640]{1,0:T(8,128)(2,1)S(1)}) custom-call(bf16[384,640]{1,0:T(8,128)(2,1)S(1)} %get-tuple-element.44.refs_0_, bf16[384,640]{1,0:T(8,128)(2,1)S(1)} %get-tuple-element.48.refs_1_, ...), custom_call_target="tpu_custom_call" | custom-call | flops 1258291200 | bytes 4587520 | tf_op jit(solution)/shard_map/pallas_call | solution.py:28
  62.2 1.7 %collective-permute-start.20 = (bf16[160,640]{1,0:T(8,128)(2,1)S(1)}, bf16[160,640]{1,0:T(8,128)(2,1)S(1)}, u32[]{:S(2)}, u32[]{:S(2)}) collective-permute-start(bf16[160,640]{1,0:T(8,128)(2,1)S(1)} %get-tuple-element.58.refs_3_), channel_id=1, source_target_pairs={{0,4},{4,8},{8,12},{12,14},{14,10},{10,6},{6,2},{2,0},{1,5},{5,9},... | collective-permute-start | bytes 614408 | tf_op jit(solution)/shard_map/ppermute | solution.py:367
  72.7 2.0 %collective-permute-done.28.refs_1_ = bf16[160,640]{1,0:T(8,128)(2,1)S(1)} collective-permute-done((bf16[160,640]{1,0:T(8,128)(2,1)S(1)}, bf16[160,640]{1,0:T(8,128)(2,1)S(1)}, u32[]{:S(2)}, u32[]{:S(2)}) %collective-permute-start.28) | collective-permute-done | bytes 204832 | tf_op jit(solution)/shard_map/ppermute | solution.py:367
  76.3 3.7 %collective-permute-done.27.refs_1_ = bf16[160,640]{1,0:T(8,128)(2,1)S(1)} collective-permute-done((bf16[160,640]{1,0:T(8,128)(2,1)S(1)}, bf16[160,640]{1,0:T(8,128)(2,1)S(1)}, u32[]{:S(2)}, u32[]{:S(2)}) %collective-permute-start.27) | collective-permute-done | bytes 204832 | tf_op jit(solution)/shard_map/ppermute | solution.py:367
  82.3 5.4 %collective-permute-done.33.refs_2_ = bf16[160,640]{1,0:T(8,128)(2,1)S(1)} collective-permute-done((bf16[160,640]{1,0:T(8,128)(2,1)S(1)}, bf16[160,640]{1,0:T(8,128)(2,1)S(1)}, u32[]{:S(2)}, u32[]{:S(2)}) %collective-permute-start.33) | collective-permute-done | bytes 204832 | tf_op jit(solution)/shard_map/ppermute | solution.py:367
  91.6 2.8 %collective-permute-done.36.refs_3_ = bf16[160,640]{1,0:T(8,128)(2,1)S(1)} collective-permute-done((bf16[160,640]{1,0:T(8,128)(2,1)S(1)}, bf16[160,640]{1,0:T(8,128)(2,1)S(1)}, u32[]{:S(2)}, u32[]{:S(2)}) %collective-permute-start.36) | collective-permute-done | bytes 204832 | tf_op jit(solution)/shard_map/ppermute | solution.py:400
  (83 shorter events, 32.9 us)
Async XLA Ops:
  4.1 37.4 %collective-permute-start.14 = (bf16[2,192,1280]{2,1,0:T(8,128)(2,1)}, bf16[2,192,1280]{2,1,0:T(8,128)(2,1)S(1)}, u32[]{:S(2)}, u32[]{:S(2)}) collective-permute-start(bf16[2,192,1280]{2,1,0:T(8,128)(2,1)} %get-tuple-element.45), channel_id=1, source_target_pairs={{0,16},{16,0},{1,17},{17,1},{2,18},{18,2},{3,19},{19,3},{4,20},{20... | collective-permute-start | bytes 2949128 | tf_op jit(solution)/shard_map/ppermute | solution.py:269
  7.1 8.2 %collective-permute-start = (bf16[160,640]{1,0:T(8,128)(2,1)}, bf16[160,640]{1,0:T(8,128)(2,1)S(1)}, u32[]{:S(2)}, u32[]{:S(2)}) collective-permute-start(bf16[160,640]{1,0:T(8,128)(2,1)} %get-tuple-element.40.refs_0_), channel_id=1, source_target_pairs={{0,4},{4,8},{8,12},{12,14},{14,10},{10,6},{6,2},{2,0},{1,5},{5,9},... | collective-permute-start | bytes 614408 | tf_op jit(solution)/shard_map/ppermute | solution.py:283
  8.7 8.2 %collective-permute-start.3 = (bf16[160,640]{1,0:T(8,128)(2,1)}, bf16[160,640]{1,0:T(8,128)(2,1)S(1)}, u32[]{:S(2)}, u32[]{:S(2)}) collective-permute-start(bf16[160,640]{1,0:T(8,128)(2,1)} %get-tuple-element.41.refs_1_), channel_id=1, source_target_pairs={{4,0},{8,4},{12,8},{14,12},{10,14},{6,10},{2,6},{0,2},{5,1},{9,5},... | collective-permute-start | bytes 614408 | tf_op jit(solution)/shard_map/ppermute | solution.py:284
  9.1 12.2 %collective-permute-start.1 = (bf16[160,640]{1,0:T(8,128)(2,1)}, bf16[160,640]{1,0:T(8,128)(2,1)S(1)}, u32[]{:S(2)}, u32[]{:S(2)}) collective-permute-start(bf16[160,640]{1,0:T(8,128)(2,1)} %get-tuple-element.40.refs_0_), channel_id=1, source_target_pairs={{4,0},{8,4},{12,8},{14,12},{10,14},{6,10},{2,6},{0,2},{5,1},{9,5},... | collective-permute-start | bytes 614408 | tf_op jit(solution)/shard_map/ppermute | solution.py:284
  10.6 11.1 %collective-permute-start.2 = (bf16[160,640]{1,0:T(8,128)(2,1)}, bf16[160,640]{1,0:T(8,128)(2,1)S(1)}, u32[]{:S(2)}, u32[]{:S(2)}) collective-permute-start(bf16[160,640]{1,0:T(8,128)(2,1)} %get-tuple-element.41.refs_1_), channel_id=1, source_target_pairs={{0,4},{4,8},{8,12},{12,14},{14,10},{10,6},{6,2},{2,0},{1,5},{5,9},... | collective-permute-start | bytes 614408 | tf_op jit(solution)/shard_map/ppermute | solution.py:283
  15.3 8.8 %collective-permute-start.4 = (bf16[160,640]{1,0:T(8,128)(2,1)S(1)}, bf16[160,640]{1,0:T(8,128)(2,1)S(1)}, u32[]{:S(2)}, u32[]{:S(2)}) collective-permute-start(bf16[160,640]{1,0:T(8,128)(2,1)S(1)} %shard_map.79.refs_2_), channel_id=1, source_target_pairs={{0,4},{4,8},{8,12},{12,14},{14,10},{10,6},{6,2},{2,0},{1,5},{5,9},... | collective-permute-start | bytes 614408 | tf_op jit(solution)/shard_map/ppermute | solution.py:283
  16.9 8.8 %collective-permute-start.7 = (bf16[160,640]{1,0:T(8,128)(2,1)S(1)}, bf16[160,640]{1,0:T(8,128)(2,1)S(1)}, u32[]{:S(2)}, u32[]{:S(2)}) collective-permute-start(bf16[160,640]{1,0:T(8,128)(2,1)S(1)} %collective-permute-done.3.refs_5_), channel_id=1, source_target_pairs={{4,0},{8,4},{12,8},{14,12},{10,14},{6,10},{2,6},{0,2},{5,1},{9,5},... | collective-permute-start | bytes 614408 | tf_op jit(solution)/shard_map/ppermute | solution.py:284
  21.3 8.8 %collective-permute-start.5 = (bf16[160,640]{1,0:T(8,128)(2,1)S(1)}, bf16[160,640]{1,0:T(8,128)(2,1)S(1)}, u32[]{:S(2)}, u32[]{:S(2)}) collective-permute-start(bf16[160,640]{1,0:T(8,128)(2,1)S(1)} %collective-permute-done.1.refs_3_), channel_id=1, source_target_pairs={{4,0},{8,4},{12,8},{14,12},{10,14},{6,10},{2,6},{0,2},{5,1},{9,5},... | collective-permute-start | bytes 614408 | tf_op jit(solution)/shard_map/ppermute | solution.py:284
  21.7 8.8 %collective-permute-start.6 = (bf16[160,640]{1,0:T(8,128)(2,1)S(1)}, bf16[160,640]{1,0:T(8,128)(2,1)S(1)}, u32[]{:S(2)}, u32[]{:S(2)}) collective-permute-start(bf16[160,640]{1,0:T(8,128)(2,1)S(1)} %collective-permute-done.2.refs_4_), channel_id=1, source_target_pairs={{0,4},{4,8},{8,12},{12,14},{14,10},{10,6},{6,2},{2,0},{1,5},{5,9},... | collective-permute-start | bytes 614408 | tf_op jit(solution)/shard_map/ppermute | solution.py:283
  24.1 9.2 %collective-permute-start.8 = (bf16[160,640]{1,0:T(8,128)(2,1)S(1)}, bf16[160,640]{1,0:T(8,128)(2,1)S(1)}, u32[]{:S(2)}, u32[]{:S(2)}) collective-permute-start(bf16[160,640]{1,0:T(8,128)(2,1)S(1)} %collective-permute-done.4.refs_6_), channel_id=1, source_target_pairs={{0,4},{4,8},{8,12},{12,14},{14,10},{10,6},{6,2},{2,0},{1,5},{5,9},... | collective-permute-start | bytes 614408 | tf_op jit(solution)/shard_map/ppermute | solution.py:283
  25.7 9.2 %collective-permute-start.9 = (bf16[160,640]{1,0:T(8,128)(2,1)S(1)}, bf16[160,640]{1,0:T(8,128)(2,1)S(1)}, u32[]{:S(2)}, u32[]{:S(2)}) collective-permute-start(bf16[160,640]{1,0:T(8,128)(2,1)S(1)} %collective-permute-done.7.refs_9_), channel_id=1, source_target_pairs={{4,0},{8,4},{12,8},{14,12},{10,14},{6,10},{2,6},{0,2},{5,1},{9,5},... | collective-permute-start | bytes 614408 | tf_op jit(solution)/shard_map/ppermute | solution.py:284
  30.0 8.8 %collective-permute-start.10 = (bf16[160,640]{1,0:T(8,128)(2,1)S(1)}, bf16[160,640]{1,0:T(8,128)(2,1)S(1)}, u32[]{:S(2)}, u32[]{:S(2)}) collective-permute-start(bf16[160,640]{1,0:T(8,128)(2,1)S(1)} %collective-permute-done.5.refs_7_), channel_id=1, source_target_pairs={{4,0},{8,4},{12,8},{14,12},{10,14},{6,10},{2,6},{0,2},{5,1},{9,5},... | collective-permute-start | bytes 614408 | tf_op jit(solution)/shard_map/ppermute | solution.py:284
  30.5 8.3 %collective-permute-start.11 = (bf16[160,640]{1,0:T(8,128)(2,1)S(1)}, bf16[160,640]{1,0:T(8,128)(2,1)S(1)}, u32[]{:S(2)}, u32[]{:S(2)}) collective-permute-start(bf16[160,640]{1,0:T(8,128)(2,1)S(1)} %collective-permute-done.6.refs_8_), channel_id=1, source_target_pairs={{0,4},{4,8},{8,12},{12,14},{14,10},{10,6},{6,2},{2,0},{1,5},{5,9},... | collective-permute-start | bytes 614408 | tf_op jit(solution)/shard_map/ppermute | solution.py:283
  41.5 8.7 %collective-permute-start.15 = (bf16[2,192,1280]{2,1,0:T(8,128)(2,1)S(1)}, bf16[2,192,1280]{2,1,0:T(8,128)(2,1)S(1)}, u32[]{:S(2)}, u32[]{:S(2)}) collective-permute-start(bf16[2,192,1280]{2,1,0:T(8,128)(2,1)S(1)} %shard_map.82.first), channel_id=1, source_target_pairs={{0,1},{1,0},{2,3},{3,2},{4,5},{5,4},{6,7},{7,6},{8,9},{9,8},{10,11... | collective-permute-start | bytes 2949128 | tf_op jit(solution)/shard_map/ppermute | solution.py:307
  52.9 8.3 %collective-permute-start.18 = (bf16[160,640]{1,0:T(8,128)(2,1)S(1)}, bf16[160,640]{1,0:T(8,128)(2,1)S(1)}, u32[]{:S(2)}, u32[]{:S(2)}) collective-permute-start(bf16[160,640]{1,0:T(8,128)(2,1)S(1)} %get-tuple-element.56), channel_id=1, source_target_pairs={{0,4},{4,8},{8,12},{12,14},{14,10},{10,6},{6,2},{2,0},{1,5},{5,9},... | collective-permute-start | bytes 614408 | tf_op jit(solution)/shard_map/ppermute | solution.py:367
  57.0 8.2 %collective-permute-start.25 = (bf16[160,640]{1,0:T(8,128)(2,1)S(1)}, bf16[160,640]{1,0:T(8,128)(2,1)S(1)}, u32[]{:S(2)}, u32[]{:S(2)}) collective-permute-start(bf16[160,640]{1,0:T(8,128)(2,1)S(1)} %get-tuple-element.53.refs_3_), channel_id=1, source_target_pairs={{0,4},{4,8},{8,12},{12,14},{14,10},{10,6},{6,2},{2,0},{1,5},{5,9},... | collective-permute-start | bytes 614408 | tf_op jit(solution)/shard_map/ppermute | solution.py:367
  58.7 8.0 %collective-permute-start.26 = (bf16[160,640]{1,0:T(8,128)(2,1)S(1)}, bf16[160,640]{1,0:T(8,128)(2,1)S(1)}, u32[]{:S(2)}, u32[]{:S(2)}) collective-permute-start(bf16[160,640]{1,0:T(8,128)(2,1)S(1)} %get-tuple-element.63), channel_id=1, source_target_pairs={{4,0},{8,4},{12,8},{14,12},{10,14},{6,10},{2,6},{0,2},{5,1},{9,5},... | collective-permute-start | bytes 614408 | tf_op jit(solution)/shard_map/ppermute | solution.py:367
  66.8 7.9 %collective-permute-start.28 = (bf16[160,640]{1,0:T(8,128)(2,1)S(1)}, bf16[160,640]{1,0:T(8,128)(2,1)S(1)}, u32[]{:S(2)}, u32[]{:S(2)}) collective-permute-start(bf16[160,640]{1,0:T(8,128)(2,1)S(1)} %get-tuple-element.64.refs_4_), channel_id=1, source_target_pairs={{0,4},{4,8},{8,12},{12,14},{14,10},{10,6},{6,2},{2,0},{1,5},{5,9},... | collective-permute-start | bytes 614408 | tf_op jit(solution)/shard_map/ppermute | solution.py:367
  68.4 7.9 %collective-permute-start.29 = (bf16[160,640]{1,0:T(8,128)(2,1)S(1)}, bf16[160,640]{1,0:T(8,128)(2,1)S(1)}, u32[]{:S(2)}, u32[]{:S(2)}) collective-permute-start(bf16[160,640]{1,0:T(8,128)(2,1)S(1)} %get-tuple-element.67), channel_id=1, source_target_pairs={{4,0},{8,4},{12,8},{14,12},{10,14},{6,10},{2,6},{0,2},{5,1},{9,5},... | collective-permute-start | bytes 614408 | tf_op jit(solution)/shard_map/ppermute | solution.py:367
  70.1 9.9 %collective-permute-start.27 = (bf16[160,640]{1,0:T(8,128)(2,1)S(1)}, bf16[160,640]{1,0:T(8,128)(2,1)S(1)}, u32[]{:S(2)}, u32[]{:S(2)}) collective-permute-start(bf16[160,640]{1,0:T(8,128)(2,1)S(1)} %get-tuple-element.65), channel_id=1, source_target_pairs={{4,0},{8,4},{12,8},{14,12},{10,14},{6,10},{2,6},{0,2},{5,1},{9,5},... | collective-permute-start | bytes 614408 | tf_op jit(solution)/shard_map/ppermute | solution.py:367
  70.6 9.4 %collective-permute-start.30 = (bf16[160,640]{1,0:T(8,128)(2,1)S(1)}, bf16[160,640]{1,0:T(8,128)(2,1)S(1)}, u32[]{:S(2)}, u32[]{:S(2)}) collective-permute-start(bf16[160,640]{1,0:T(8,128)(2,1)S(1)} %get-tuple-element.66.refs_2_), channel_id=1, source_target_pairs={{0,4},{4,8},{8,12},{12,14},{14,10},{10,6},{6,2},{2,0},{1,5},{5,9},... | collective-permute-start | bytes 614408 | tf_op jit(solution)/shard_map/ppermute | solution.py:367
  72.2 16.2 %collective-permute-start.32 = (bf16[384,640]{1,0:T(8,128)(2,1)S(1)}, bf16[384,640]{1,0:T(8,128)(2,1)S(1)}, u32[]{:S(2)}, u32[]{:S(2)}) collective-permute-start(bf16[384,640]{1,0:T(8,128)(2,1)S(1)} %shard_map.88.refs_3_), channel_id=1, source_target_pairs={{0,16},{16,0},{1,17},{17,1},{2,18},{18,2},{3,19},{19,3},{4,20},{20... | collective-permute-start | bytes 1474568 | tf_op jit(solution)/shard_map/ppermute | solution.py:340
  80.1 8.3 %collective-permute-start.31 = (bf16[384,640]{1,0:T(8,128)(2,1)S(1)}, bf16[384,640]{1,0:T(8,128)(2,1)S(1)}, u32[]{:S(2)}, u32[]{:S(2)}) collective-permute-start(bf16[384,640]{1,0:T(8,128)(2,1)S(1)} %shard_map.92), channel_id=1, source_target_pairs={{0,1},{1,0},{2,3},{3,2},{4,5},{5,4},{6,7},{7,6},{8,9},{9,8},{10,11... | collective-permute-start | bytes 1474568 | tf_op jit(solution)/shard_map/ppermute | solution.py:393
  80.7 10.9 %collective-permute-start.35 = (bf16[160,640]{1,0:T(8,128)(2,1)S(1)}, bf16[160,640]{1,0:T(8,128)(2,1)S(1)}, u32[]{:S(2)}, u32[]{:S(2)}) collective-permute-start(bf16[160,640]{1,0:T(8,128)(2,1)S(1)} %shard_map.90.refs_2_), channel_id=1, source_target_pairs={{0,4},{4,8},{8,12},{12,14},{14,10},{10,6},{6,2},{2,0},{1,5},{5,9},... | collective-permute-start | bytes 614408 | tf_op jit(solution)/shard_map/ppermute | solution.py:367
  (19 other events, 166.5 us)

commit v15 on v14

--- a/solution.py
+++ b/solution.py
@@ -216,9 +216,13 @@
         out[...] = (value + came[...].astype(F32)).astype(BF16)
 
 
-def total_kernel(peers, partial, up, down, total):
+def total_kernel(peers, partial, up, total):
     value = partial[block_rows(0, peers, total.shape[0]), :].astype(F32)
-    total[...] = (value + up[...].astype(F32) + down[...].astype(F32)).astype(BF16)
+    total[...] = (value + up[...].astype(F32)).astype(BF16)
+
+
+def add_kernel(one, two, total):
+    total[...] = one[...].astype(F32) + two[...].astype(F32)
 
 
 def join_kernel(peers, partial, up, down, passed, out):
@@ -228,7 +232,7 @@
     value = value + up[...].astype(F32) + down[...].astype(F32)
     out[:, pl.ds(pl.multiple_of(side * width, width), width)] = value
     other = pl.ds(pl.multiple_of((1 - side) * width, width), width)
-    out[:, other] = passed[...].astype(F32)
+    out[:, other] = passed[...]
 
 
 def place_halves_kernel(own, passed, out):
@@ -299,7 +303,7 @@
             [pltpu.SemaphoreType.DMA((len(blocks),))],
             pinned=range(len(blocks)),
         )
-        first = hold(first, *late.values())
+        first = hold(first, *late.values(), near[0])
         sends = ((half - 1, -half), (half, 1 - half))
     else:
         near = [lax.all_gather(block, "gx", axis=0, tiled=True) for block in mine]
@@ -362,9 +366,16 @@
     if ringed:
         came = [{}, {}]
 
-        def send_on(i, blocks, names):
+        across = [
+            (a + k * peers, b + (1 - k) * peers) for k in range(2) for a, b in behind
+        ]
+
+        def send_on(i, blocks, names, last=False):
             for block, name in zip(blocks, names):
-                came[i][name] = lax.ppermute(block, "gx", ahead if name == "up" else behind)
+                if last and i == 1:
+                    came[i][name] = lax.ppermute(block, ("groups", "gx"), across)
+                else:
+                    came[i][name] = lax.ppermute(block, "gx", ahead if name == "up" else behind)
 
         def hop(i, turn, *ties):
             ways = [("up", half - turn - i), ("down", turn + 1 - i - half)]
@@ -377,7 +388,7 @@
                 [block_of] * len(ways),
                 ties=ties,
             )
-            send_on(i, blocks, names)
+            send_on(i, blocks, names, turn == half - 1)
             return blocks[0]
 
         send_on(0, blocks_own, ("up", "down"))
@@ -393,17 +404,19 @@
         sent = lax.ppermute(hold(send, tie), "gy", swap)
         passing = call(
             functools.partial(total_kernel, peers),
-            (partial[1], came[1]["up"], came[1]["down"]),
+            (partial[1], came[1]["up"]),
             block_of,
             ties=(tie,),
         )
         passed = lax.ppermute(passing, "groups", swap)
         input_grad, token = input_gradient(*scale(keep, sent, back, passing))
+        passed = call(
+            add_kernel, (passed, came[1]["down"]), shape((depth, quarter), F32), ties=(token,)
+        )
         up_grad = call(
             functools.partial(join_kernel, peers),
             (partial[0], came[0]["up"], came[0]["down"], passed),
             up_grad_of,
-            ties=(token,),
         )
     else:
         keep, send, parts = own_d_norm()

time: 95.7 us -> 93.1 us (0.973)
  waiting for transfers between devices: 41.8 us -> 38 us
    ppermute x14 -> x13, waiting for transfers between devices: 18.9 us -> 13.5 us  [send_on(): came[i][name] = lax.ppermute(block, 'gx', ahead if name == 'up' else behind)]
    ppermute x6, waiting for transfers between devices: 11.4 us -> 7.92 us  [shards(): down[i] = lax.ppermute(down[i], 'gx', behind)]
    ppermute x1, waiting for transfers between devices: 2.84 us -> 5.53 us  [shards(): passed = lax.ppermute(passing, 'groups', swap)]
    ppermute x0 -> x1, waiting for transfers between devices: none -> 2.11 us  [send_on(): came[i][name] = lax.ppermute(block, ('groups', 'gx'), across)]
    ppermute x0 -> x1, starting transfers between devices: none -> 1.45 us  [send_on(): came[i][name] = lax.ppermute(block, ('groups', 'gx'), across)]
    ppermute x14 -> x13, starting transfers between devices: 14.5 us -> 14 us  [send_on(): came[i][name] = lax.ppermute(block, 'gx', ahead if name == 'up' else behind)]
    pallas_call x17 -> x18, Pallas kernels: 19.8 us -> 19.7 us  [call(): pl.pallas_call(body if ties else kernel, out_shape=out_shape, in_specs=[S...]
  transfers between devices with their start and end apart: 37 -> 37, of which waited for: 20 -> 20; matrix products, arithmetic and copies ran while one was open for 0% -> 0% of each run, Pallas kernels for 16% -> 17%
where the time goes in v15:
time: 93.1 us; the launch traced here: 92.5 us
  waiting for transfers between devices  38 us (41%)
  starting transfers between devices  33.9 us (36%)
  Pallas kernels  19.7 us (21%)
    pallas_call x18, Pallas kernels, call(): pl.pallas_call(body if ties else kernel, out_shape=out_shape, in_specs=[S...  19.7 us
    ppermute x13, starting transfers between devices, send_on(): came[i][name] = lax.ppermute(block, 'gx', ahead if name == 'up' else behind)  14 us
    ppermute x13, waiting for transfers between devices, send_on(): came[i][name] = lax.ppermute(block, 'gx', ahead if name == 'up' else behind)  13.5 us
    ppermute x6, starting transfers between devices, shards(): up[i] = lax.ppermute(up[i], 'gx', ahead)  8.39 us
    ppermute x6, waiting for transfers between devices, shards(): down[i] = lax.ppermute(down[i], 'gx', behind)  7.92 us
    ppermute x1, waiting for transfers between devices, shards(): passed = lax.ppermute(passing, 'groups', swap)  5.53 us
    ppermute x6, waiting for transfers between devices, shards(): up[i] = lax.ppermute(up[i], 'gx', ahead)  4.61 us
    ppermute x6, starting transfers between devices, shards(): down[i] = lax.ppermute(down[i], 'gx', behind)  3.77 us
  transfers between devices with their start and end apart: 37, of which 20 were waited for; matrix products, arithmetic and copies ran while one was open for 0% of the time, Pallas kernels for 17%

profile of v15, /device:TPU:0, one launch (start us, length us, event | category | flops | bytes accessed | tf_op | source)
XLA Modules:
  0.0 92.5 jit_solution(4090936258767165688)
XLA Ops:
  0.7 3.4 %shard_map.78 = (bf16[2,192,1280]{2,1,0:T(8,128)(2,1)}, bf16[160,640]{1,0:T(8,128)(2,1)}, bf16[160,640]{1,0:T(8,128)(2,1)}) custom-call(s32[8]{0:T(128)} %lengths.3, bf16[384,1280]{1,0:T(8,128)(2,1)} %bitcast.3, bf16[384,1280]{1,0:T(8,128)(2,1)} %bitcast.6, f32[1280]{0:T(1024)} %gain.3, bf16[160,1280]{1,0:T(8,128)(2,1)} %w_up.1, bf16[160,1280]{1,0:T(8,128)(2,1)} %w_down.1), custom_call_target="tpu_custom_call" | custom-call | flops 2457600 | bytes 4183072 | tf_op jit(solution)/shard_map/pallas_call | solution.py:28
  4.1 3.0 %collective-permute-start.14 = (bf16[2,192,1280]{2,1,0:T(8,128)(2,1)}, bf16[2,192,1280]{2,1,0:T(8,128)(2,1)S(1)}, u32[]{:S(2)}, u32[]{:S(2)}) collective-permute-start(bf16[2,192,1280]{2,1,0:T(8,128)(2,1)} %get-tuple-element.45), channel_id=1, source_target_pairs={{0,16},{16,0},{1,17},{17,1},{2,18},{18,2},{3,19},{19,3},{4,20},{20... | collective-permute-start | bytes 2949128 | tf_op jit(solution)/shard_map/ppermute | solution.py:273
  7.1 1.6 %collective-permute-start = (bf16[160,640]{1,0:T(8,128)(2,1)}, bf16[160,640]{1,0:T(8,128)(2,1)S(1)}, u32[]{:S(2)}, u32[]{:S(2)}) collective-permute-start(bf16[160,640]{1,0:T(8,128)(2,1)} %get-tuple-element.40.refs_0_), channel_id=1, source_target_pairs={{0,4},{4,8},{8,12},{12,14},{14,10},{10,6},{6,2},{2,0},{1,5},{5,9},... | collective-permute-start | bytes 614408 | tf_op jit(solution)/shard_map/ppermute | solution.py:287
  12.6 2.6 %collective-permute-done.refs_0_ = bf16[160,640]{1,0:T(8,128)(2,1)S(1)} collective-permute-done((bf16[160,640]{1,0:T(8,128)(2,1)}, bf16[160,640]{1,0:T(8,128)(2,1)S(1)}, u32[]{:S(2)}, u32[]{:S(2)}) %collective-permute-start) | collective-permute-done | bytes 204832 | tf_op jit(solution)/shard_map/ppermute | solution.py:287
  15.3 1.6 %collective-permute-start.4 = (bf16[160,640]{1,0:T(8,128)(2,1)S(1)}, bf16[160,640]{1,0:T(8,128)(2,1)S(1)}, u32[]{:S(2)}, u32[]{:S(2)}) collective-permute-start(bf16[160,640]{1,0:T(8,128)(2,1)S(1)} %shard_map.79.refs_2_), channel_id=1, source_target_pairs={{0,4},{4,8},{8,12},{12,14},{14,10},{10,6},{6,2},{2,0},{1,5},{5,9},... | collective-permute-start | bytes 614408 | tf_op jit(solution)/shard_map/ppermute | solution.py:287
  17.3 3.9 %collective-permute-done.1.refs_3_ = bf16[160,640]{1,0:T(8,128)(2,1)S(1)} collective-permute-done((bf16[160,640]{1,0:T(8,128)(2,1)}, bf16[160,640]{1,0:T(8,128)(2,1)S(1)}, u32[]{:S(2)}, u32[]{:S(2)}) %collective-permute-start.1) | collective-permute-done | bytes 204832 | tf_op jit(solution)/shard_map/ppermute | solution.py:288
  21.7 1.6 %collective-permute-start.6 = (bf16[160,640]{1,0:T(8,128)(2,1)S(1)}, bf16[160,640]{1,0:T(8,128)(2,1)S(1)}, u32[]{:S(2)}, u32[]{:S(2)}) collective-permute-start(bf16[160,640]{1,0:T(8,128)(2,1)S(1)} %collective-permute-done.2.refs_4_), channel_id=1, source_target_pairs={{0,4},{4,8},{8,12},{12,14},{14,10},{10,6},{6,2},{2,0},{1,5},{5,9},... | collective-permute-start | bytes 614408 | tf_op jit(solution)/shard_map/ppermute | solution.py:287
  24.1 1.6 %collective-permute-start.8 = (bf16[160,640]{1,0:T(8,128)(2,1)S(1)}, bf16[160,640]{1,0:T(8,128)(2,1)S(1)}, u32[]{:S(2)}, u32[]{:S(2)}) collective-permute-start(bf16[160,640]{1,0:T(8,128)(2,1)S(1)} %collective-permute-done.4.refs_6_), channel_id=1, source_target_pairs={{0,4},{4,8},{8,12},{12,14},{14,10},{10,6},{6,2},{2,0},{1,5},{5,9},... | collective-permute-start | bytes 614408 | tf_op jit(solution)/shard_map/ppermute | solution.py:287
  26.1 3.9 %collective-permute-done.5.refs_7_ = bf16[160,640]{1,0:T(8,128)(2,1)S(1)} collective-permute-done((bf16[160,640]{1,0:T(8,128)(2,1)S(1)}, bf16[160,640]{1,0:T(8,128)(2,1)S(1)}, u32[]{:S(2)}, u32[]{:S(2)}) %collective-permute-start.5) | collective-permute-done | bytes 204832 | tf_op jit(solution)/shard_map/ppermute | solution.py:288
  30.5 1.6 %collective-permute-start.11 = (bf16[160,640]{1,0:T(8,128)(2,1)S(1)}, bf16[160,640]{1,0:T(8,128)(2,1)S(1)}, u32[]{:S(2)}, u32[]{:S(2)}) collective-permute-start(bf16[160,640]{1,0:T(8,128)(2,1)S(1)} %collective-permute-done.6.refs_8_), channel_id=1, source_target_pairs={{0,4},{4,8},{8,12},{12,14},{14,10},{10,6},{6,2},{2,0},{1,5},{5,9},... | collective-permute-start | bytes 614408 | tf_op jit(solution)/shard_map/ppermute | solution.py:287
  33.3 1.6 %collective-permute-start.12 = (bf16[160,640]{1,0:T(8,128)(2,1)S(1)}, bf16[160,640]{1,0:T(8,128)(2,1)S(1)}, u32[]{:S(2)}, u32[]{:S(2)}) collective-permute-start(bf16[160,640]{1,0:T(8,128)(2,1)S(1)} %collective-permute-done.8.refs_10_), channel_id=1, source_target_pairs={{0,4},{4,8},{8,12},{12,14},{14,10},{10,6},{6,2},{2,0},{1,5},{5,9},... | collective-permute-start | bytes 614408 | tf_op jit(solution)/shard_map/ppermute | solution.py:296
  35.3 3.6 %shard_map.80 = (bf16[1280,640]{1,0:T(8,128)(2,1)S(1)}, bf16[1280,640]{1,0:T(8,128)(2,1)S(1)}) custom-call(bf16[160,640]{1,0:T(8,128)(2,1)S(1)} %copy-done.2, bf16[160,640]{1,0:T(8,128)(2,1)S(1)} %copy-done.3, bf16[160,640]{1,0:T(8,128)(2,1)S(1)} %shard_map.79.refs_2_, bf16[160,640]{1,0:T(8,128)(2,1)S(1)} %collective-permute-done.1.refs_3_, ...), custom_call_target="tpu_custom_call" | custom-call | flops 1 | bytes 5734400 | tf_op jit(solution)/shard_map/pallas_call | solution.py:28
  41.5 2.9 %shard_map.81 = (bf16[384,640]{1,0:T(8,128)(2,1)S(1)}, bf16[1280,640]{1,0:T(8,128)(2,1)S(1)}, bf16[1280,640]{1,0:T(8,128)(2,1)S(1)}, bf16[1280,640]{1,0:T(8,128)...) custom-call(bf16[384,1280]{1,0:T(8,128)(2,1)S(1)} %get-tuple-element.38.refs_1_.normed, ...), custom_call_target="tpu_custom_call" | custom-call | flops 1887436800 | bytes 11878400 | tf_op jit(solution)/shard_map/pallas_call | solution.py:28
  44.4 1.6 %collective-permute-start.16 = (bf16[160,640]{1,0:T(8,128)(2,1)S(1)}, bf16[160,640]{1,0:T(8,128)(2,1)S(1)}, u32[]{:S(2)}, u32[]{:S(2)}) collective-permute-start(bf16[160,640]{1,0:T(8,128)(2,1)S(1)} %get-tuple-element.50), channel_id=1, source_target_pairs={{0,4},{4,8},{8,12},{12,14},{14,10},{10,6},{6,2},{2,0},{1,5},{5,9},... | collective-permute-start | bytes 614408 | tf_op jit(solution)/shard_map/ppermute | solution.py:378
  46.5 2.7 %shard_map.83 = (bf16[384,640]{1,0:T(8,128)(2,1)S(1)}, bf16[1280,640]{1,0:T(8,128)(2,1)S(1)}, bf16[160,640]{1,0:T(8,128)(2,1)S(1)}, bf16[160,640]{1,0:T(8,128)(2,1)S(1)}) custom-call(bf16[2,192,1280]{2,1,0:T(8,128)(2,1)S(1)} %shard_map.82.first, bf16[2,192,1280]{2,1,0:T(8,128)(2,1)S(1)} %collective-permute-done.15.second, ...), custom_call_target="tpu_custom_call" | custom-call | flops 1887436800 | bytes 7782400 | tf_op jit(solution)/shard_map/pallas_call | solution.py:28
  49.2 1.6 %collective-permute-start.18 = (bf16[160,640]{1,0:T(8,128)(2,1)S(1)}, bf16[160,640]{1,0:T(8,128)(2,1)S(1)}, u32[]{:S(2)}, u32[]{:S(2)}) collective-permute-start(bf16[160,640]{1,0:T(8,128)(2,1)S(1)} %get-tuple-element.56), channel_id=1, source_target_pairs={{0,4},{4,8},{8,12},{12,14},{14,10},{10,6},{6,2},{2,0},{1,5},{5,9},... | collective-permute-start | bytes 614408 | tf_op jit(solution)/shard_map/ppermute | solution.py:378
  53.5 1.6 %collective-permute-start.25 = (bf16[160,640]{1,0:T(8,128)(2,1)S(1)}, bf16[160,640]{1,0:T(8,128)(2,1)S(1)}, u32[]{:S(2)}, u32[]{:S(2)}) collective-permute-start(bf16[160,640]{1,0:T(8,128)(2,1)S(1)} %get-tuple-element.53.refs_3_), channel_id=1, source_target_pairs={{0,4},{4,8},{8,12},{12,14},{14,10},{10,6},{6,2},{2,0},{1,5},{5,9},... | collective-permute-start | bytes 614408 | tf_op jit(solution)/shard_map/ppermute | solution.py:378
  55.5 2.0 %shard_map.85 = (bf16[2,384,640]{2,1,0:T(8,128)(2,1)S(1)}, bf16[384,640]{1,0:T(8,128)(2,1)S(1)}, bf16[128,640]{1,0:T(8,128)(2,1)S(1)}, bf16[128,640]{1,0:T(8,128)(2,1)S(1)}, bf16[128,640]{1,0:T(8,128)(2,1)S(1)}) custom-call(bf16[384,640]{1,0:T(8,128)(2,1)S(1)} %get-tuple-element.44.refs_0_, bf16[384,640]{1,0:T(8,128)(2,1)S(1)} %get-tuple-element.48.refs_1_, ...), custom_call_target="tpu_custom_call" | custom-call | flops 1258291200 | bytes 4587520 | tf_op jit(solution)/shard_map/pallas_call | solution.py:28
  58.6 1.7 %collective-permute-start.20 = (bf16[160,640]{1,0:T(8,128)(2,1)S(1)}, bf16[160,640]{1,0:T(8,128)(2,1)S(1)}, u32[]{:S(2)}, u32[]{:S(2)}) collective-permute-start(bf16[160,640]{1,0:T(8,128)(2,1)S(1)} %get-tuple-element.58.refs_3_), channel_id=1, source_target_pairs={{0,4},{4,8},{8,12},{12,14},{14,10},{10,6},{6,2},{2,0},{1,5},{5,9},... | collective-permute-start | bytes 614408 | tf_op jit(solution)/shard_map/ppermute | solution.py:378
  67.0 1.6 %collective-permute-start.30 = (bf16[160,640]{1,0:T(8,128)(2,1)S(1)}, bf16[160,640]{1,0:T(8,128)(2,1)S(1)}, u32[]{:S(2)}, u32[]{:S(2)}) collective-permute-start(bf16[160,640]{1,0:T(8,128)(2,1)S(1)} %get-tuple-element.66.refs_2_), channel_id=1, source_target_pairs={{0,4},{4,8},{8,12},{12,14},{14,10},{10,6},{6,2},{2,0},{1,5},{5,9},... | collective-permute-start | bytes 614408 | tf_op jit(solution)/shard_map/ppermute | solution.py:378
  69.2 2.0 %collective-permute-done.28.refs_1_ = bf16[160,640]{1,0:T(8,128)(2,1)S(1)} collective-permute-done((bf16[160,640]{1,0:T(8,128)(2,1)S(1)}, bf16[160,640]{1,0:T(8,128)(2,1)S(1)}, u32[]{:S(2)}, u32[]{:S(2)}) %collective-permute-start.28) | collective-permute-done | bytes 204832 | tf_op jit(solution)/shard_map/ppermute | solution.py:378
  72.8 3.6 %collective-permute-done.27.refs_1_ = bf16[160,640]{1,0:T(8,128)(2,1)S(1)} collective-permute-done((bf16[160,640]{1,0:T(8,128)(2,1)S(1)}, bf16[160,640]{1,0:T(8,128)(2,1)S(1)}, u32[]{:S(2)}, u32[]{:S(2)}) %collective-permute-start.27) | collective-permute-done | bytes 204832 | tf_op jit(solution)/shard_map/ppermute | solution.py:378
  83.8 5.5 %collective-permute-done.35.refs_0_ = bf16[160,640]{1,0:T(8,128)(2,1)S(1)} collective-permute-done((bf16[160,640]{1,0:T(8,128)(2,1)S(1)}, bf16[160,640]{1,0:T(8,128)(2,1)S(1)}, u32[]{:S(2)}, u32[]{:S(2)}) %collective-permute-start.35) | collective-permute-done | bytes 204832 | tf_op jit(solution)/shard_map/ppermute | solution.py:411
  89.3 2.1 %collective-permute-done.36.refs_1_ = bf16[160,640]{1,0:T(8,128)(2,1)S(1)} collective-permute-done((bf16[160,640]{1,0:T(8,128)(2,1)S(1)}, bf16[160,640]{1,0:T(8,128)(2,1)S(1)}, u32[]{:S(2)}, u32[]{:S(2)}) %collective-permute-start.36) | collective-permute-done | bytes 204832 | tf_op jit(solution)/shard_map/ppermute | solution.py:376
  (84 shorter events, 32.6 us)
Async XLA Ops:
  4.1 37.4 %collective-permute-start.14 = (bf16[2,192,1280]{2,1,0:T(8,128)(2,1)}, bf16[2,192,1280]{2,1,0:T(8,128)(2,1)S(1)}, u32[]{:S(2)}, u32[]{:S(2)}) collective-permute-start(bf16[2,192,1280]{2,1,0:T(8,128)(2,1)} %get-tuple-element.45), channel_id=1, source_target_pairs={{0,16},{16,0},{1,17},{17,1},{2,18},{18,2},{3,19},{19,3},{4,20},{20... | collective-permute-start | bytes 2949128 | tf_op jit(solution)/shard_map/ppermute | solution.py:273
  7.1 8.2 %collective-permute-start = (bf16[160,640]{1,0:T(8,128)(2,1)}, bf16[160,640]{1,0:T(8,128)(2,1)S(1)}, u32[]{:S(2)}, u32[]{:S(2)}) collective-permute-start(bf16[160,640]{1,0:T(8,128)(2,1)} %get-tuple-element.40.refs_0_), channel_id=1, source_target_pairs={{0,4},{4,8},{8,12},{12,14},{14,10},{10,6},{6,2},{2,0},{1,5},{5,9},... | collective-permute-start | bytes 614408 | tf_op jit(solution)/shard_map/ppermute | solution.py:287
  8.7 8.2 %collective-permute-start.3 = (bf16[160,640]{1,0:T(8,128)(2,1)}, bf16[160,640]{1,0:T(8,128)(2,1)S(1)}, u32[]{:S(2)}, u32[]{:S(2)}) collective-permute-start(bf16[160,640]{1,0:T(8,128)(2,1)} %get-tuple-element.41.refs_1_), channel_id=1, source_target_pairs={{4,0},{8,4},{12,8},{14,12},{10,14},{6,10},{2,6},{0,2},{5,1},{9,5},... | collective-permute-start | bytes 614408 | tf_op jit(solution)/shard_map/ppermute | solution.py:288
  9.1 12.2 %collective-permute-start.1 = (bf16[160,640]{1,0:T(8,128)(2,1)}, bf16[160,640]{1,0:T(8,128)(2,1)S(1)}, u32[]{:S(2)}, u32[]{:S(2)}) collective-permute-start(bf16[160,640]{1,0:T(8,128)(2,1)} %get-tuple-element.40.refs_0_), channel_id=1, source_target_pairs={{4,0},{8,4},{12,8},{14,12},{10,14},{6,10},{2,6},{0,2},{5,1},{9,5},... | collective-permute-start | bytes 614408 | tf_op jit(solution)/shard_map/ppermute | solution.py:288
  10.6 11.1 %collective-permute-start.2 = (bf16[160,640]{1,0:T(8,128)(2,1)}, bf16[160,640]{1,0:T(8,128)(2,1)S(1)}, u32[]{:S(2)}, u32[]{:S(2)}) collective-permute-start(bf16[160,640]{1,0:T(8,128)(2,1)} %get-tuple-element.41.refs_1_), channel_id=1, source_target_pairs={{0,4},{4,8},{8,12},{12,14},{14,10},{10,6},{6,2},{2,0},{1,5},{5,9},... | collective-permute-start | bytes 614408 | tf_op jit(solution)/shard_map/ppermute | solution.py:287
  15.3 8.8 %collective-permute-start.4 = (bf16[160,640]{1,0:T(8,128)(2,1)S(1)}, bf16[160,640]{1,0:T(8,128)(2,1)S(1)}, u32[]{:S(2)}, u32[]{:S(2)}) collective-permute-start(bf16[160,640]{1,0:T(8,128)(2,1)S(1)} %shard_map.79.refs_2_), channel_id=1, source_target_pairs={{0,4},{4,8},{8,12},{12,14},{14,10},{10,6},{6,2},{2,0},{1,5},{5,9},... | collective-permute-start | bytes 614408 | tf_op jit(solution)/shard_map/ppermute | solution.py:287
  16.9 8.8 %collective-permute-start.7 = (bf16[160,640]{1,0:T(8,128)(2,1)S(1)}, bf16[160,640]{1,0:T(8,128)(2,1)S(1)}, u32[]{:S(2)}, u32[]{:S(2)}) collective-permute-start(bf16[160,640]{1,0:T(8,128)(2,1)S(1)} %collective-permute-done.3.refs_5_), channel_id=1, source_target_pairs={{4,0},{8,4},{12,8},{14,12},{10,14},{6,10},{2,6},{0,2},{5,1},{9,5},... | collective-permute-start | bytes 614408 | tf_op jit(solution)/shard_map/ppermute | solution.py:288
  21.3 8.8 %collective-permute-start.5 = (bf16[160,640]{1,0:T(8,128)(2,1)S(1)}, bf16[160,640]{1,0:T(8,128)(2,1)S(1)}, u32[]{:S(2)}, u32[]{:S(2)}) collective-permute-start(bf16[160,640]{1,0:T(8,128)(2,1)S(1)} %collective-permute-done.1.refs_3_), channel_id=1, source_target_pairs={{4,0},{8,4},{12,8},{14,12},{10,14},{6,10},{2,6},{0,2},{5,1},{9,5},... | collective-permute-start | bytes 614408 | tf_op jit(solution)/shard_map/ppermute | solution.py:288
  21.7 8.8 %collective-permute-start.6 = (bf16[160,640]{1,0:T(8,128)(2,1)S(1)}, bf16[160,640]{1,0:T(8,128)(2,1)S(1)}, u32[]{:S(2)}, u32[]{:S(2)}) collective-permute-start(bf16[160,640]{1,0:T(8,128)(2,1)S(1)} %collective-permute-done.2.refs_4_), channel_id=1, source_target_pairs={{0,4},{4,8},{8,12},{12,14},{14,10},{10,6},{6,2},{2,0},{1,5},{5,9},... | collective-permute-start | bytes 614408 | tf_op jit(solution)/shard_map/ppermute | solution.py:287
  24.1 9.2 %collective-permute-start.8 = (bf16[160,640]{1,0:T(8,128)(2,1)S(1)}, bf16[160,640]{1,0:T(8,128)(2,1)S(1)}, u32[]{:S(2)}, u32[]{:S(2)}) collective-permute-start(bf16[160,640]{1,0:T(8,128)(2,1)S(1)} %collective-permute-done.4.refs_6_), channel_id=1, source_target_pairs={{0,4},{4,8},{8,12},{12,14},{14,10},{10,6},{6,2},{2,0},{1,5},{5,9},... | collective-permute-start | bytes 614408 | tf_op jit(solution)/shard_map/ppermute | solution.py:287
  25.7 9.2 %collective-permute-start.9 = (bf16[160,640]{1,0:T(8,128)(2,1)S(1)}, bf16[160,640]{1,0:T(8,128)(2,1)S(1)}, u32[]{:S(2)}, u32[]{:S(2)}) collective-permute-start(bf16[160,640]{1,0:T(8,128)(2,1)S(1)} %collective-permute-done.7.refs_9_), channel_id=1, source_target_pairs={{4,0},{8,4},{12,8},{14,12},{10,14},{6,10},{2,6},{0,2},{5,1},{9,5},... | collective-permute-start | bytes 614408 | tf_op jit(solution)/shard_map/ppermute | solution.py:288
  30.1 8.8 %collective-permute-start.10 = (bf16[160,640]{1,0:T(8,128)(2,1)S(1)}, bf16[160,640]{1,0:T(8,128)(2,1)S(1)}, u32[]{:S(2)}, u32[]{:S(2)}) collective-permute-start(bf16[160,640]{1,0:T(8,128)(2,1)S(1)} %collective-permute-done.5.refs_7_), channel_id=1, source_target_pairs={{4,0},{8,4},{12,8},{14,12},{10,14},{6,10},{2,6},{0,2},{5,1},{9,5},... | collective-permute-start | bytes 614408 | tf_op jit(solution)/shard_map/ppermute | solution.py:288
  30.5 8.4 %collective-permute-start.11 = (bf16[160,640]{1,0:T(8,128)(2,1)S(1)}, bf16[160,640]{1,0:T(8,128)(2,1)S(1)}, u32[]{:S(2)}, u32[]{:S(2)}) collective-permute-start(bf16[160,640]{1,0:T(8,128)(2,1)S(1)} %collective-permute-done.6.refs_8_), channel_id=1, source_target_pairs={{0,4},{4,8},{8,12},{12,14},{14,10},{10,6},{6,2},{2,0},{1,5},{5,9},... | collective-permute-start | bytes 614408 | tf_op jit(solution)/shard_map/ppermute | solution.py:287
  49.2 8.3 %collective-permute-start.18 = (bf16[160,640]{1,0:T(8,128)(2,1)S(1)}, bf16[160,640]{1,0:T(8,128)(2,1)S(1)}, u32[]{:S(2)}, u32[]{:S(2)}) collective-permute-start(bf16[160,640]{1,0:T(8,128)(2,1)S(1)} %get-tuple-element.56), channel_id=1, source_target_pairs={{0,4},{4,8},{8,12},{12,14},{14,10},{10,6},{6,2},{2,0},{1,5},{5,9},... | collective-permute-start | bytes 614408 | tf_op jit(solution)/shard_map/ppermute | solution.py:378
  53.5 8.1 %collective-permute-start.25 = (bf16[160,640]{1,0:T(8,128)(2,1)S(1)}, bf16[160,640]{1,0:T(8,128)(2,1)S(1)}, u32[]{:S(2)}, u32[]{:S(2)}) collective-permute-start(bf16[160,640]{1,0:T(8,128)(2,1)S(1)} %get-tuple-element.53.refs_3_), channel_id=1, source_target_pairs={{0,4},{4,8},{8,12},{12,14},{14,10},{10,6},{6,2},{2,0},{1,5},{5,9},... | collective-permute-start | bytes 614408 | tf_op jit(solution)/shard_map/ppermute | solution.py:378
  55.1 8.0 %collective-permute-start.26 = (bf16[160,640]{1,0:T(8,128)(2,1)S(1)}, bf16[160,640]{1,0:T(8,128)(2,1)S(1)}, u32[]{:S(2)}, u32[]{:S(2)}) collective-permute-start(bf16[160,640]{1,0:T(8,128)(2,1)S(1)} %get-tuple-element.63), channel_id=1, source_target_pairs={{4,0},{8,4},{12,8},{14,12},{10,14},{6,10},{2,6},{0,2},{5,1},{9,5},... | collective-permute-start | bytes 614408 | tf_op jit(solution)/shard_map/ppermute | solution.py:378
  63.2 7.9 %collective-permute-start.28 = (bf16[160,640]{1,0:T(8,128)(2,1)S(1)}, bf16[160,640]{1,0:T(8,128)(2,1)S(1)}, u32[]{:S(2)}, u32[]{:S(2)}) collective-permute-start(bf16[160,640]{1,0:T(8,128)(2,1)S(1)} %get-tuple-element.64.refs_4_), channel_id=1, source_target_pairs={{0,4},{4,8},{8,12},{12,14},{14,10},{10,6},{6,2},{2,0},{1,5},{5,9},... | collective-permute-start | bytes 614408 | tf_op jit(solution)/shard_map/ppermute | solution.py:378
  64.8 7.9 %collective-permute-start.29 = (bf16[160,640]{1,0:T(8,128)(2,1)S(1)}, bf16[160,640]{1,0:T(8,128)(2,1)S(1)}, u32[]{:S(2)}, u32[]{:S(2)}) collective-permute-start(bf16[160,640]{1,0:T(8,128)(2,1)S(1)} %get-tuple-element.67), channel_id=1, source_target_pairs={{4,0},{8,4},{12,8},{14,12},{10,14},{6,10},{2,6},{0,2},{5,1},{9,5},... | collective-permute-start | bytes 614408 | tf_op jit(solution)/shard_map/ppermute | solution.py:378
  66.5 9.9 %collective-permute-start.27 = (bf16[160,640]{1,0:T(8,128)(2,1)S(1)}, bf16[160,640]{1,0:T(8,128)(2,1)S(1)}, u32[]{:S(2)}, u32[]{:S(2)}) collective-permute-start(bf16[160,640]{1,0:T(8,128)(2,1)S(1)} %get-tuple-element.65), channel_id=1, source_target_pairs={{4,0},{8,4},{12,8},{14,12},{10,14},{6,10},{2,6},{0,2},{5,1},{9,5},... | collective-permute-start | bytes 614408 | tf_op jit(solution)/shard_map/ppermute | solution.py:378
  67.0 9.4 %collective-permute-start.30 = (bf16[160,640]{1,0:T(8,128)(2,1)S(1)}, bf16[160,640]{1,0:T(8,128)(2,1)S(1)}, u32[]{:S(2)}, u32[]{:S(2)}) collective-permute-start(bf16[160,640]{1,0:T(8,128)(2,1)S(1)} %get-tuple-element.66.refs_2_), channel_id=1, source_target_pairs={{0,4},{4,8},{8,12},{12,14},{14,10},{10,6},{6,2},{2,0},{1,5},{5,9},... | collective-permute-start | bytes 614408 | tf_op jit(solution)/shard_map/ppermute | solution.py:378
  68.6 11.9 %collective-permute-start.32 = (bf16[384,640]{1,0:T(8,128)(2,1)S(1)}, bf16[384,640]{1,0:T(8,128)(2,1)S(1)}, u32[]{:S(2)}, u32[]{:S(2)}) collective-permute-start(bf16[384,640]{1,0:T(8,128)(2,1)S(1)} %shard_map.88.refs_3_), channel_id=1, source_target_pairs={{0,16},{16,0},{1,17},{17,1},{2,18},{18,2},{3,19},{19,3},{4,20},{20... | collective-permute-start | bytes 1474568 | tf_op jit(solution)/shard_map/ppermute | solution.py:344
  76.7 12.6 %collective-permute-start.35 = (bf16[160,640]{1,0:T(8,128)(2,1)S(1)}, bf16[160,640]{1,0:T(8,128)(2,1)S(1)}, u32[]{:S(2)}, u32[]{:S(2)}) collective-permute-start(bf16[160,640]{1,0:T(8,128)(2,1)S(1)} %shard_map.93.refs_7_), channel_id=1, source_target_pairs={{0,16},{16,0},{1,17},{17,1},{2,18},{18,2},{3,19},{19,3},{4,20},{20... | collective-permute-start | bytes 614408 | tf_op jit(solution)/shard_map/ppermute | solution.py:411
  77.3 14.2 %collective-permute-start.36 = (bf16[160,640]{1,0:T(8,128)(2,1)S(1)}, bf16[160,640]{1,0:T(8,128)(2,1)S(1)}, u32[]{:S(2)}, u32[]{:S(2)}) collective-permute-start(bf16[160,640]{1,0:T(8,128)(2,1)S(1)} %shard_map.91.refs_1_.refs_2_), channel_id=1, source_target_pairs={{4,16},{8,20},{12,24},{14,28},{10,30},{6,26},{2,22},{0,18},{20,0},... | collective-permute-start | bytes 614408 | tf_op jit(solution)/shard_map/ppermute | solution.py:376
  78.7 12.8 %collective-permute-start.34 = (bf16[160,640]{1,0:T(8,128)(2,1)S(1)}, bf16[160,640]{1,0:T(8,128)(2,1)S(1)}, u32[]{:S(2)}, u32[]{:S(2)}) collective-permute-start(bf16[160,640]{1,0:T(8,128)(2,1)S(1)} %shard_map.90.refs_2_), channel_id=1, source_target_pairs={{0,4},{4,8},{8,12},{12,14},{14,10},{10,6},{6,2},{2,0},{1,5},{5,9},... | collective-permute-start | bytes 614408 | tf_op jit(solution)/shard_map/ppermute | solution.py:378
  (19 other events, 162.9 us)

commit v16 on v14

--- a/solution.py
+++ b/solution.py
@@ -87,27 +87,32 @@
     return jnp.where(index < length, rows.astype(F32), 0.0).astype(BF16)
 
 
-def first_kernel(
-    lengths, frames, out_grad, gain, w_up, w_down, passing, mine_up, mine_down, sems, rows, grads
-):
-    half, quarter = rows.shape[0], mine_up.shape[1]
+def cut_kernel(w_up, w_down, mine_up, mine_down, sems):
+    quarter = mine_up.shape[1]
+    columns = pl.ds(pl.multiple_of(lax.axis_index("groups") * quarter, quarter), quarter)
+    copies = [
+        pltpu.make_async_copy(w_up.at[:, columns], mine_up, sems.at[0]),
+        pltpu.make_async_copy(w_down.at[:, columns], mine_down, sems.at[1]),
+    ]
+    for copy in copies:
+        copy.start()
+    for copy in copies:
+        copy.wait()
+
+
+def pass_kernel(lengths, frames, out_grad, gain, passing, sems, rows, grads):
+    half = rows.shape[0]
     start = pl.multiple_of(lax.axis_index("gy") * half, half)
-    columns = pl.ds(pl.multiple_of(lax.axis_index("groups") * quarter, quarter), quarter)
-    moves = (
-        (frames.at[pl.ds(start, half)], rows),
-        (out_grad.at[pl.ds(start, half)], grads),
-        (w_up.at[:, columns], mine_up),
-        (w_down.at[:, columns], mine_down),
-    )
-    copies = [pltpu.make_async_copy(*move, sems.at[i]) for i, move in enumerate(moves)]
+    copies = [
+        pltpu.make_async_copy(source.at[pl.ds(start, half)], target, sems.at[i])
+        for i, (source, target) in enumerate(((frames, rows), (out_grad, grads)))
+    ]
     for copy in copies:
         copy.start()
     copies[0].wait()
     passing[0] = norm_rows(rows[...], gain)[0]
     copies[1].wait()
     passing[1] = mask_rows(grads[...], start, lengths[lax.axis_index("gx")])
-    copies[2].wait()
-    copies[3].wait()
 
 
 def norm_kernel(lengths, frames, out_grad, gain, normed, grads, stats):
@@ -257,16 +262,22 @@
     frames, out_grad = frames[0], out_grad[0]
     rows_of = shape((frame_len, width), BF16)
     block_of = shape((depth, quarter), BF16)
-    passing, *mine = call(
-        first_kernel,
-        (lengths, frames, out_grad, ln_gain, w_up, w_down),
-        (shape((2, half_rows, width), BF16), block_of, block_of),
-        [pltpu.SemaphoreType.DMA((4,))] + [pltpu.VMEM((half_rows, width), BF16)] * 2,
+    mine = call(
+        cut_kernel,
+        (w_up, w_down),
+        (block_of, block_of),
+        [pltpu.SemaphoreType.DMA((2,))],
+        vmem=60,
+        left=(0, 1),
+    )
+    passing = call(
+        pass_kernel,
+        (lengths, frames, out_grad, ln_gain),
+        shape((2, half_rows, width), BF16),
+        [pltpu.SemaphoreType.DMA((2,))] + [pltpu.VMEM((half_rows, width), BF16)] * 2,
         flops=5 * frame_len * width,
-        vmem=60,
-        left=(1, 2, 4, 5),
-    )
-    first = lax.ppermute(passing, "groups", swap)
+        left=(1, 2),
+    )
     normed, grads, stats = call(
         norm_kernel,
         (lengths, frames, out_grad, ln_gain),
@@ -283,6 +294,8 @@
                 up[i] = lax.ppermute(up[i], "gx", ahead)
                 down[i] = lax.ppermute(down[i], "gx", behind)
             if step == 1:
+                first = lax.ppermute(hold(passing, up[0], down[1]), "groups", swap)
+            if step == 2:
                 up[0] = hold(up[0], normed)
             for i in range(2):
                 blocks[-step, i], blocks[step, i] = up[i], down[i]
@@ -299,9 +312,10 @@
             [pltpu.SemaphoreType.DMA((len(blocks),))],
             pinned=range(len(blocks)),
         )
-        first = hold(first, *late.values())
+        first = hold(first, *late.values(), near[0])
         sends = ((half - 1, -half), (half, 1 - half))
     else:
+        first = lax.ppermute(passing, "groups", swap)
         near = [lax.all_gather(block, "gx", axis=0, tiled=True) for block in mine]
         late, sends = {}, ((), ())
     second = lax.ppermute(first, "gy", swap)
@@ -382,14 +396,14 @@
 
         send_on(0, blocks_own, ("up", "down"))
         send_on(1, blocks_other, ("up", "down"))
-        tie = hop(0, 1, partial_other)
-        keep, send, parts = own_d_norm(tie)
+        keep, send, parts = own_d_norm(*came[0].values())
         tie = hop(1, 1, keep)
-        tie = hop(0, 2, tie)
+        tie = hop(0, 1, tie)
         over, back = over_cores(keep, parts, tie)
         tie = hop(1, 2, over)
+        tie = hop(0, 2, tie)
         for turn in range(3, half):
-            tie = hop(1, turn, hop(0, turn, tie))
+            tie = hop(0, turn, hop(1, turn, tie))
         sent = lax.ppermute(hold(send, tie), "gy", swap)
         passing = call(
             functools.partial(total_kernel, peers),

time: 95.7 us -> 96.3 us (level)
  local copies, waits for them, and re-layouts: 0.03 us -> 3.78 us
  waiting for transfers between devices: 41.8 us -> 38.1 us
    ppermute x6, waiting for transfers between devices: 11.4 us -> 4.99 us  [shards(): down[i] = lax.ppermute(down[i], 'gx', behind)]
    unnamed x12 -> x16, local copies, waits for them, and re-layouts: 0.02 us -> 3.78 us
    ppermute x6, waiting for transfers between devices: 4.63 us -> 6.16 us  [shards(): up[i] = lax.ppermute(up[i], 'gx', ahead)]
    ppermute x1, starting transfers between devices: 3 us -> 1.49 us  [shards(): first = lax.ppermute(hold(passing, up[0], down[1]), 'groups', swap)]
    ppermute x6, starting transfers between devices: 8.39 us -> 9.9 us  [shards(): up[i] = lax.ppermute(up[i], 'gx', ahead)]
    ppermute x3, waiting for transfers between devices: 0.01 us -> 1.4 us  [own_d_norm(): return (keep, send, [lax.ppermute(part, 'gy', swap) for part in parts])]
    pallas_call x17 -> x18, Pallas kernels: 19.8 us -> 19.7 us  [call(): pl.pallas_call(body if ties else kernel, out_shape=out_shape, in_specs=[S...]
  transfers between devices with their start and end apart: 37 -> 37, of which waited for: 20 -> 21; matrix products, arithmetic and copies ran while one was open for 0% -> 0% of each run, Pallas kernels for 16% -> 18%
where the time goes in v16:
time: 96.3 us; the launch traced here: 96 us
  waiting for transfers between devices  38.1 us (40%)
  starting transfers between devices  33.6 us (35%)
  Pallas kernels  19.7 us (20%)
  local copies, waits for them, and re-layouts  3.78 us (4%)
    ppermute x14, waiting for transfers between devices, send_on(): came[i][name] = lax.ppermute(block, 'gx', ahead if name == 'up' else behind)  19.8 us
    pallas_call x18, Pallas kernels, call(): pl.pallas_call(body if ties else kernel, out_shape=out_shape, in_specs=[S...  19.7 us
    ppermute x14, starting transfers between devices, send_on(): came[i][name] = lax.ppermute(block, 'gx', ahead if name == 'up' else behind)  14.5 us
    ppermute x6, starting transfers between devices, shards(): up[i] = lax.ppermute(up[i], 'gx', ahead)  9.9 us
    ppermute x6, waiting for transfers between devices, shards(): up[i] = lax.ppermute(up[i], 'gx', ahead)  6.16 us
    ppermute x6, waiting for transfers between devices, shards(): down[i] = lax.ppermute(down[i], 'gx', behind)  4.99 us
    unnamed x16, local copies, waits for them, and re-layouts  3.78 us
    ppermute x6, starting transfers between devices, shards(): down[i] = lax.ppermute(down[i], 'gx', behind)  3.77 us
  transfers between devices with their start and end apart: 37, of which 21 were waited for; matrix products, arithmetic and copies ran while one was open for 0% of the time, Pallas kernels for 18%

profile of v16, /device:TPU:0, one launch (start us, length us, event | category | flops | bytes accessed | tf_op | source)
XLA Modules:
  0.0 96.0 jit_solution(2512539290600862648)
XLA Ops:
  0.6 1.8 %shard_map.78 = (bf16[160,640]{1,0:T(8,128)(2,1)}, bf16[160,640]{1,0:T(8,128)(2,1)}) custom-call(bf16[160,1280]{1,0:T(8,128)(2,1)} %w_up.1, bf16[160,1280]{1,0:T(8,128)(2,1)} %w_down.1), custom_call_target="tpu_custom_call" | custom-call | flops 1 | bytes 1228800 | tf_op jit(solution)/shard_map/pallas_call | solution.py:28
  2.4 3.1 %collective-permute-start = (bf16[160,640]{1,0:T(8,128)(2,1)}, bf16[160,640]{1,0:T(8,128)(2,1)S(1)}, u32[]{:S(2)}, u32[]{:S(2)}) collective-permute-start(bf16[160,640]{1,0:T(8,128)(2,1)} %get-tuple-element.39.refs_0_), channel_id=1, source_target_pairs={{0,4},{4,8},{8,12},{12,14},{14,10},{10,6},{6,2},{2,0},{1,5},{5,9},... | collective-permute-start | bytes 614408 | tf_op jit(solution)/shard_map/ppermute | solution.py:294
  9.3 1.6 %shard_map.82.refs_0_ = bf16[2,192,1280]{2,1,0:T(8,128)(2,1)S(1)} custom-call(s32[8]{0:T(128)S(1)} %copy-done.7, bf16[384,1280]{1,0:T(8,128)(2,1)S(1)} %bitcast.3, bf16[384,1280]{1,0:T(8,128)(2,1)S(1)} %bitcast.6, f32[1280]{0:T(1024)S(1)} %copy-done.5), custom_call_target="tpu_custom_call" | custom-call | flops 2457600 | bytes 2954272 | tf_op jit(solution)/shard_map/pallas_call | solution.py:28
  15.8 1.6 %collective-permute-start.4 = (bf16[160,640]{1,0:T(8,128)(2,1)S(1)}, bf16[160,640]{1,0:T(8,128)(2,1)S(1)}, u32[]{:S(2)}, u32[]{:S(2)}) collective-permute-start(bf16[160,640]{1,0:T(8,128)(2,1)S(1)} %collective-permute-done.refs_2_.refs_1_), channel_id=1, source_target_pairs={{0,4},{4,8},{8,12},{12,14},{14,10},{10,6},{6,2},{2,0},{1,5},{5,9},... | collective-permute-start | bytes 614408 | tf_op jit(solution)/shard_map/ppermute | solution.py:294
  19.3 2.2 %collective-permute-done.1.refs_3_ = bf16[160,640]{1,0:T(8,128)(2,1)S(1)} collective-permute-done((bf16[160,640]{1,0:T(8,128)(2,1)S(1)}, bf16[160,640]{1,0:T(8,128)(2,1)S(1)}, u32[]{:S(2)}, u32[]{:S(2)}) %collective-permute-start.1) | collective-permute-done | bytes 204832 | tf_op jit(solution)/shard_map/ppermute | solution.py:295
  23.8 3.1 %collective-permute-done.4.refs_0_ = bf16[160,640]{1,0:T(8,128)(2,1)S(1)} collective-permute-done((bf16[160,640]{1,0:T(8,128)(2,1)S(1)}, bf16[160,640]{1,0:T(8,128)(2,1)S(1)}, u32[]{:S(2)}, u32[]{:S(2)}) %collective-permute-start.4) | collective-permute-done | bytes 204832 | tf_op jit(solution)/shard_map/ppermute | solution.py:294
  32.6 3.1 %collective-permute-done.8.refs_10_ = bf16[160,640]{1,0:T(8,128)(2,1)S(1)} collective-permute-done((bf16[160,640]{1,0:T(8,128)(2,1)S(1)}, bf16[160,640]{1,0:T(8,128)(2,1)S(1)}, u32[]{:S(2)}, u32[]{:S(2)}) %collective-permute-start.8) | collective-permute-done | bytes 204832 | tf_op jit(solution)/shard_map/ppermute | solution.py:294
  37.7 3.5 %shard_map.80 = (bf16[1280,640]{1,0:T(8,128)(2,1)S(1)}, bf16[1280,640]{1,0:T(8,128)(2,1)S(1)}) custom-call(bf16[160,640]{1,0:T(8,128)(2,1)S(1)} %copy-done.3, bf16[160,640]{1,0:T(8,128)(2,1)S(1)} %copy-done.4, bf16[160,640]{1,0:T(8,128)(2,1)S(1)} %collective-permute-done.refs_2_.refs_1_, bf16[160,640]{1,0:T(8,128)(2,1)S(1)} %collective-permute-done.1.refs_3_, ...), custom_call_target="tpu_custom_call" | custom-call | flops 1 | bytes 5734400 | tf_op jit(solution)/shard_map/pallas_call | solution.py:28
  42.7 3.0 %shard_map.81 = (bf16[384,640]{1,0:T(8,128)(2,1)S(1)}, bf16[1280,640]{1,0:T(8,128)(2,1)S(1)}, bf16[1280,640]{1,0:T(8,128)(2,1)S(1)}, bf16[1280,640]{1,0:T(8,128)...) custom-call(bf16[384,1280]{1,0:T(8,128)(2,1)S(1)} %get-tuple-element.37.refs_1_.normed, ...), custom_call_target="tpu_custom_call" | custom-call | flops 1887436800 | bytes 11878400 | tf_op jit(solution)/shard_map/pallas_call | solution.py:28
  45.7 1.6 %collective-permute-start.16 = (bf16[160,640]{1,0:T(8,128)(2,1)S(1)}, bf16[160,640]{1,0:T(8,128)(2,1)S(1)}, u32[]{:S(2)}, u32[]{:S(2)}) collective-permute-start(bf16[160,640]{1,0:T(8,128)(2,1)S(1)} %get-tuple-element.47), channel_id=1, source_target_pairs={{0,4},{4,8},{8,12},{12,14},{14,10},{10,6},{6,2},{2,0},{1,5},{5,9},... | collective-permute-start | bytes 614408 | tf_op jit(solution)/shard_map/ppermute | solution.py:381
  47.8 2.7 %shard_map.85 = (bf16[384,640]{1,0:T(8,128)(2,1)S(1)}, bf16[1280,640]{1,0:T(8,128)(2,1)S(1)}, bf16[160,640]{1,0:T(8,128)(2,1)S(1)}, bf16[160,640]{1,0:T(8,128)(2,1)S(1)}) custom-call(bf16[2,192,1280]{2,1,0:T(8,128)(2,1)S(1)} %shard_map.84.first, bf16[2,192,1280]{2,1,0:T(8,128)(2,1)S(1)} %collective-permute-done.15.second, ...), custom_call_target="tpu_custom_call" | custom-call | flops 1887436800 | bytes 7782400 | tf_op jit(solution)/shard_map/pallas_call | solution.py:28
  50.5 1.6 %collective-permute-start.18 = (bf16[160,640]{1,0:T(8,128)(2,1)S(1)}, bf16[160,640]{1,0:T(8,128)(2,1)S(1)}, u32[]{:S(2)}, u32[]{:S(2)}) collective-permute-start(bf16[160,640]{1,0:T(8,128)(2,1)S(1)} %get-tuple-element.53), channel_id=1, source_target_pairs={{0,4},{4,8},{8,12},{12,14},{14,10},{10,6},{6,2},{2,0},{1,5},{5,9},... | collective-permute-start | bytes 614408 | tf_op jit(solution)/shard_map/ppermute | solution.py:381
  54.6 2.0 %shard_map.86 = (bf16[2,384,640]{2,1,0:T(8,128)(2,1)S(1)}, bf16[384,640]{1,0:T(8,128)(2,1)S(1)}, bf16[128,640]{1,0:T(8,128)(2,1)S(1)}, bf16[128,640]{1,0:T(8,128)(2,1)S(1)}, bf16[128,640]{1,0:T(8,128)(2,1)S(1)}) custom-call(bf16[384,640]{1,0:T(8,128)(2,1)S(1)} %get-tuple-element.43.refs_0_, bf16[384,640]{1,0:T(8,128)(2,1)S(1)} %get-tuple-element.46.refs_1_, ...), custom_call_target="tpu_custom_call" | custom-call | flops 1258291200 | bytes 4587520 | tf_op jit(solution)/shard_map/pallas_call | solution.py:28
  59.1 1.6 %collective-permute-start.22 = (bf16[160,640]{1,0:T(8,128)(2,1)S(1)}, bf16[160,640]{1,0:T(8,128)(2,1)S(1)}, u32[]{:S(2)}, u32[]{:S(2)}) collective-permute-start(bf16[160,640]{1,0:T(8,128)(2,1)S(1)} %get-tuple-element.55.refs_3_), channel_id=1, source_target_pairs={{0,4},{4,8},{8,12},{12,14},{14,10},{10,6},{6,2},{2,0},{1,5},{5,9},... | collective-permute-start | bytes 614408 | tf_op jit(solution)/shard_map/ppermute | solution.py:381
  61.3 1.6 %collective-permute-start.20 = (bf16[160,640]{1,0:T(8,128)(2,1)S(1)}, bf16[160,640]{1,0:T(8,128)(2,1)S(1)}, u32[]{:S(2)}, u32[]{:S(2)}) collective-permute-start(bf16[160,640]{1,0:T(8,128)(2,1)S(1)} %get-tuple-element.56.refs_4_), channel_id=1, source_target_pairs={{0,4},{4,8},{8,12},{12,14},{14,10},{10,6},{6,2},{2,0},{1,5},{5,9},... | collective-permute-start | bytes 614408 | tf_op jit(solution)/shard_map/ppermute | solution.py:381
  64.9 2.3 %collective-permute-done.22.refs_1_ = bf16[160,640]{1,0:T(8,128)(2,1)S(1)} collective-permute-done((bf16[160,640]{1,0:T(8,128)(2,1)S(1)}, bf16[160,640]{1,0:T(8,128)(2,1)S(1)}, u32[]{:S(2)}, u32[]{:S(2)}) %collective-permute-start.22) | collective-permute-done | bytes 204832 | tf_op jit(solution)/shard_map/ppermute | solution.py:381
  67.1 1.6 %collective-permute-done.23.refs_2_ = bf16[160,640]{1,0:T(8,128)(2,1)S(1)} collective-permute-done((bf16[160,640]{1,0:T(8,128)(2,1)S(1)}, bf16[160,640]{1,0:T(8,128)(2,1)S(1)}, u32[]{:S(2)}, u32[]{:S(2)}) %collective-permute-start.23) | collective-permute-done | bytes 204832 | tf_op jit(solution)/shard_map/ppermute | solution.py:381
  69.3 1.6 %collective-permute-start.29 = (bf16[160,640]{1,0:T(8,128)(2,1)S(1)}, bf16[160,640]{1,0:T(8,128)(2,1)S(1)}, u32[]{:S(2)}, u32[]{:S(2)}) collective-permute-start(bf16[160,640]{1,0:T(8,128)(2,1)S(1)} %get-tuple-element.62.refs_3_), channel_id=1, source_target_pairs={{0,4},{4,8},{8,12},{12,14},{14,10},{10,6},{6,2},{2,0},{1,5},{5,9},... | collective-permute-start | bytes 614408 | tf_op jit(solution)/shard_map/ppermute | solution.py:381
  70.9 2.2 %collective-permute-done.21.refs_2_ = bf16[160,640]{1,0:T(8,128)(2,1)S(1)} collective-permute-done((bf16[160,640]{1,0:T(8,128)(2,1)S(1)}, bf16[160,640]{1,0:T(8,128)(2,1)S(1)}, u32[]{:S(2)}, u32[]{:S(2)}) %collective-permute-start.21) | collective-permute-done | bytes 204832 | tf_op jit(solution)/shard_map/ppermute | solution.py:381
  73.2 1.6 %collective-permute-start.27 = (bf16[160,640]{1,0:T(8,128)(2,1)S(1)}, bf16[160,640]{1,0:T(8,128)(2,1)S(1)}, u32[]{:S(2)}, u32[]{:S(2)}) collective-permute-start(bf16[160,640]{1,0:T(8,128)(2,1)S(1)} %get-tuple-element.63.refs_2_), channel_id=1, source_target_pairs={{0,4},{4,8},{8,12},{12,14},{14,10},{10,6},{6,2},{2,0},{1,5},{5,9},... | collective-permute-start | bytes 614408 | tf_op jit(solution)/shard_map/ppermute | solution.py:381
  77.4 1.7 %collective-permute-done.27.refs_1_ = bf16[160,640]{1,0:T(8,128)(2,1)S(1)} collective-permute-done((bf16[160,640]{1,0:T(8,128)(2,1)S(1)}, bf16[160,640]{1,0:T(8,128)(2,1)S(1)}, u32[]{:S(2)}, u32[]{:S(2)}) %collective-permute-start.27) | collective-permute-done | bytes 204832 | tf_op jit(solution)/shard_map/ppermute | solution.py:381
  81.3 1.5 %collective-permute-start.35 = (bf16[160,640]{1,0:T(8,128)(2,1)S(1)}, bf16[160,640]{1,0:T(8,128)(2,1)S(1)}, u32[]{:S(2)}, u32[]{:S(2)}) collective-permute-start(bf16[160,640]{1,0:T(8,128)(2,1)S(1)} %shard_map.93.refs_1_.refs_3_), channel_id=1, source_target_pairs={{0,4},{4,8},{8,12},{12,14},{14,10},{10,6},{6,2},{2,0},{1,5},{5,9},... | collective-permute-start | bytes 614408 | tf_op jit(solution)/shard_map/ppermute | solution.py:381
  82.8 5.4 %collective-permute-done.33.refs_2_ = bf16[160,640]{1,0:T(8,128)(2,1)S(1)} collective-permute-done((bf16[160,640]{1,0:T(8,128)(2,1)S(1)}, bf16[160,640]{1,0:T(8,128)(2,1)S(1)}, u32[]{:S(2)}, u32[]{:S(2)}) %collective-permute-start.33) | collective-permute-done | bytes 204832 | tf_op jit(solution)/shard_map/ppermute | solution.py:381
  92.2 2.8 %collective-permute-done.36.refs_3_ = bf16[160,640]{1,0:T(8,128)(2,1)S(1)} collective-permute-done((bf16[160,640]{1,0:T(8,128)(2,1)S(1)}, bf16[160,640]{1,0:T(8,128)(2,1)S(1)}, u32[]{:S(2)}, u32[]{:S(2)}) %collective-permute-start.36) | collective-permute-done | bytes 204832 | tf_op jit(solution)/shard_map/ppermute | solution.py:414
  (89 shorter events, 40.4 us)
Async XLA Ops:
  2.4 8.5 %collective-permute-start = (bf16[160,640]{1,0:T(8,128)(2,1)}, bf16[160,640]{1,0:T(8,128)(2,1)S(1)}, u32[]{:S(2)}, u32[]{:S(2)}) collective-permute-start(bf16[160,640]{1,0:T(8,128)(2,1)} %get-tuple-element.39.refs_0_), channel_id=1, source_target_pairs={{0,4},{4,8},{8,12},{12,14},{14,10},{10,6},{6,2},{2,0},{1,5},{5,9},... | collective-permute-start | bytes 614408 | tf_op jit(solution)/shard_map/ppermute | solution.py:294
  12.3 30.5 %collective-permute-start.14 = (bf16[2,192,1280]{2,1,0:T(8,128)(2,1)S(1)}, bf16[2,192,1280]{2,1,0:T(8,128)(2,1)S(1)}, u32[]{:S(2)}, u32[]{:S(2)}) collective-permute-start(bf16[2,192,1280]{2,1,0:T(8,128)(2,1)S(1)} %shard_map.83), channel_id=1, source_target_pairs={{0,16},{16,0},{1,17},{17,1},{2,18},{18,2},{3,19},{19,3},{4,20},{20... | collective-permute-start | bytes 2949128 | tf_op jit(solution)/shard_map/ppermute | solution.py:297
  13.8 7.8 %collective-permute-start.1 = (bf16[160,640]{1,0:T(8,128)(2,1)S(1)}, bf16[160,640]{1,0:T(8,128)(2,1)S(1)}, u32[]{:S(2)}, u32[]{:S(2)}) collective-permute-start(bf16[160,640]{1,0:T(8,128)(2,1)S(1)} %copy-done.3), channel_id=1, source_target_pairs={{4,0},{8,4},{12,8},{14,12},{10,14},{6,10},{2,6},{0,2},{5,1},{9,5},... | collective-permute-start | bytes 614408 | tf_op jit(solution)/shard_map/ppermute | solution.py:295
  14.5 8.0 %collective-permute-start.2 = (bf16[160,640]{1,0:T(8,128)(2,1)S(1)}, bf16[160,640]{1,0:T(8,128)(2,1)S(1)}, u32[]{:S(2)}, u32[]{:S(2)}) collective-permute-start(bf16[160,640]{1,0:T(8,128)(2,1)S(1)} %copy-done.4), channel_id=1, source_target_pairs={{0,4},{4,8},{8,12},{12,14},{14,10},{10,6},{6,2},{2,0},{1,5},{5,9},... | collective-permute-start | bytes 614408 | tf_op jit(solution)/shard_map/ppermute | solution.py:294
  15.8 11.1 %collective-permute-start.4 = (bf16[160,640]{1,0:T(8,128)(2,1)S(1)}, bf16[160,640]{1,0:T(8,128)(2,1)S(1)}, u32[]{:S(2)}, u32[]{:S(2)}) collective-permute-start(bf16[160,640]{1,0:T(8,128)(2,1)S(1)} %collective-permute-done.refs_2_.refs_1_), channel_id=1, source_target_pairs={{0,4},{4,8},{8,12},{12,14},{14,10},{10,6},{6,2},{2,0},{1,5},{5,9},... | collective-permute-start | bytes 614408 | tf_op jit(solution)/shard_map/ppermute | solution.py:294
  17.4 10.8 %collective-permute-start.7 = (bf16[160,640]{1,0:T(8,128)(2,1)S(1)}, bf16[160,640]{1,0:T(8,128)(2,1)S(1)}, u32[]{:S(2)}, u32[]{:S(2)}) collective-permute-start(bf16[160,640]{1,0:T(8,128)(2,1)S(1)} %collective-permute-done.3.refs_5_.refs_2_), channel_id=1, source_target_pairs={{4,0},{8,4},{12,8},{14,12},{10,14},{6,10},{2,6},{0,2},{5,1},{9,5},... | collective-permute-start | bytes 614408 | tf_op jit(solution)/shard_map/ppermute | solution.py:295
  21.5 8.8 %collective-permute-start.5 = (bf16[160,640]{1,0:T(8,128)(2,1)S(1)}, bf16[160,640]{1,0:T(8,128)(2,1)S(1)}, u32[]{:S(2)}, u32[]{:S(2)}) collective-permute-start(bf16[160,640]{1,0:T(8,128)(2,1)S(1)} %collective-permute-done.1.refs_3_), channel_id=1, source_target_pairs={{4,0},{8,4},{12,8},{14,12},{10,14},{6,10},{2,6},{0,2},{5,1},{9,5},... | collective-permute-start | bytes 614408 | tf_op jit(solution)/shard_map/ppermute | solution.py:295
  22.5 8.8 %collective-permute-start.6 = (bf16[160,640]{1,0:T(8,128)(2,1)S(1)}, bf16[160,640]{1,0:T(8,128)(2,1)S(1)}, u32[]{:S(2)}, u32[]{:S(2)}) collective-permute-start(bf16[160,640]{1,0:T(8,128)(2,1)S(1)} %collective-permute-done.2.refs_4_), channel_id=1, source_target_pairs={{0,4},{4,8},{8,12},{12,14},{14,10},{10,6},{6,2},{2,0},{1,5},{5,9},... | collective-permute-start | bytes 614408 | tf_op jit(solution)/shard_map/ppermute | solution.py:294
  26.9 8.8 %collective-permute-start.8 = (bf16[160,640]{1,0:T(8,128)(2,1)S(1)}, bf16[160,640]{1,0:T(8,128)(2,1)S(1)}, u32[]{:S(2)}, u32[]{:S(2)}) collective-permute-start(bf16[160,640]{1,0:T(8,128)(2,1)S(1)} %shard_map.79.refs_6_), channel_id=1, source_target_pairs={{0,4},{4,8},{8,12},{12,14},{14,10},{10,6},{6,2},{2,0},{1,5},{5,9},... | collective-permute-start | bytes 614408 | tf_op jit(solution)/shard_map/ppermute | solution.py:294
  28.2 8.8 %collective-permute-start.9 = (bf16[160,640]{1,0:T(8,128)(2,1)S(1)}, bf16[160,640]{1,0:T(8,128)(2,1)S(1)}, u32[]{:S(2)}, u32[]{:S(2)}) collective-permute-start(bf16[160,640]{1,0:T(8,128)(2,1)S(1)} %collective-permute-done.7.refs_9_), channel_id=1, source_target_pairs={{4,0},{8,4},{12,8},{14,12},{10,14},{6,10},{2,6},{0,2},{5,1},{9,5},... | collective-permute-start | bytes 614408 | tf_op jit(solution)/shard_map/ppermute | solution.py:295
  30.3 10.9 %collective-permute-start.10 = (bf16[160,640]{1,0:T(8,128)(2,1)S(1)}, bf16[160,640]{1,0:T(8,128)(2,1)S(1)}, u32[]{:S(2)}, u32[]{:S(2)}) collective-permute-start(bf16[160,640]{1,0:T(8,128)(2,1)S(1)} %collective-permute-done.5.refs_7_), channel_id=1, source_target_pairs={{4,0},{8,4},{12,8},{14,12},{10,14},{6,10},{2,6},{0,2},{5,1},{9,5},... | collective-permute-start | bytes 614408 | tf_op jit(solution)/shard_map/ppermute | solution.py:295
  31.3 10.0 %collective-permute-start.11 = (bf16[160,640]{1,0:T(8,128)(2,1)S(1)}, bf16[160,640]{1,0:T(8,128)(2,1)S(1)}, u32[]{:S(2)}, u32[]{:S(2)}) collective-permute-start(bf16[160,640]{1,0:T(8,128)(2,1)S(1)} %collective-permute-done.6.refs_8_), channel_id=1, source_target_pairs={{0,4},{4,8},{8,12},{12,14},{14,10},{10,6},{6,2},{2,0},{1,5},{5,9},... | collective-permute-start | bytes 614408 | tf_op jit(solution)/shard_map/ppermute | solution.py:294
  45.7 7.6 %collective-permute-start.16 = (bf16[160,640]{1,0:T(8,128)(2,1)S(1)}, bf16[160,640]{1,0:T(8,128)(2,1)S(1)}, u32[]{:S(2)}, u32[]{:S(2)}) collective-permute-start(bf16[160,640]{1,0:T(8,128)(2,1)S(1)} %get-tuple-element.47), channel_id=1, source_target_pairs={{0,4},{4,8},{8,12},{12,14},{14,10},{10,6},{6,2},{2,0},{1,5},{5,9},... | collective-permute-start | bytes 614408 | tf_op jit(solution)/shard_map/ppermute | solution.py:381
  47.4 7.3 %collective-permute-start.17 = (bf16[160,640]{1,0:T(8,128)(2,1)S(1)}, bf16[160,640]{1,0:T(8,128)(2,1)S(1)}, u32[]{:S(2)}, u32[]{:S(2)}) collective-permute-start(bf16[160,640]{1,0:T(8,128)(2,1)S(1)} %get-tuple-element.48), channel_id=1, source_target_pairs={{4,0},{8,4},{12,8},{14,12},{10,14},{6,10},{2,6},{0,2},{5,1},{9,5},... | collective-permute-start | bytes 614408 | tf_op jit(solution)/shard_map/ppermute | solution.py:381
  59.1 8.1 %collective-permute-start.22 = (bf16[160,640]{1,0:T(8,128)(2,1)S(1)}, bf16[160,640]{1,0:T(8,128)(2,1)S(1)}, u32[]{:S(2)}, u32[]{:S(2)}) collective-permute-start(bf16[160,640]{1,0:T(8,128)(2,1)S(1)} %get-tuple-element.55.refs_3_), channel_id=1, source_target_pairs={{0,4},{4,8},{8,12},{12,14},{14,10},{10,6},{6,2},{2,0},{1,5},{5,9},... | collective-permute-start | bytes 614408 | tf_op jit(solution)/shard_map/ppermute | solution.py:381
  60.7 8.0 %collective-permute-start.23 = (bf16[160,640]{1,0:T(8,128)(2,1)S(1)}, bf16[160,640]{1,0:T(8,128)(2,1)S(1)}, u32[]{:S(2)}, u32[]{:S(2)}) collective-permute-start(bf16[160,640]{1,0:T(8,128)(2,1)S(1)} %get-tuple-element.58), channel_id=1, source_target_pairs={{4,0},{8,4},{12,8},{14,12},{10,14},{6,10},{2,6},{0,2},{5,1},{9,5},... | collective-permute-start | bytes 614408 | tf_op jit(solution)/shard_map/ppermute | solution.py:381
  61.3 9.6 %collective-permute-start.20 = (bf16[160,640]{1,0:T(8,128)(2,1)S(1)}, bf16[160,640]{1,0:T(8,128)(2,1)S(1)}, u32[]{:S(2)}, u32[]{:S(2)}) collective-permute-start(bf16[160,640]{1,0:T(8,128)(2,1)S(1)} %get-tuple-element.56.refs_4_), channel_id=1, source_target_pairs={{0,4},{4,8},{8,12},{12,14},{14,10},{10,6},{6,2},{2,0},{1,5},{5,9},... | collective-permute-start | bytes 614408 | tf_op jit(solution)/shard_map/ppermute | solution.py:381
  62.9 10.2 %collective-permute-start.21 = (bf16[160,640]{1,0:T(8,128)(2,1)S(1)}, bf16[160,640]{1,0:T(8,128)(2,1)S(1)}, u32[]{:S(2)}, u32[]{:S(2)}) collective-permute-start(bf16[160,640]{1,0:T(8,128)(2,1)S(1)} %get-tuple-element.57), channel_id=1, source_target_pairs={{4,0},{8,4},{12,8},{14,12},{10,14},{6,10},{2,6},{0,2},{5,1},{9,5},... | collective-permute-start | bytes 614408 | tf_op jit(solution)/shard_map/ppermute | solution.py:381
  68.8 8.4 %collective-permute-start.28 = (bf16[160,640]{1,0:T(8,128)(2,1)S(1)}, bf16[160,640]{1,0:T(8,128)(2,1)S(1)}, u32[]{:S(2)}, u32[]{:S(2)}) collective-permute-start(bf16[160,640]{1,0:T(8,128)(2,1)S(1)} %get-tuple-element.64), channel_id=1, source_target_pairs={{4,0},{8,4},{12,8},{14,12},{10,14},{6,10},{2,6},{0,2},{5,1},{9,5},... | collective-permute-start | bytes 614408 | tf_op jit(solution)/shard_map/ppermute | solution.py:381
  69.3 7.9 %collective-permute-start.29 = (bf16[160,640]{1,0:T(8,128)(2,1)S(1)}, bf16[160,640]{1,0:T(8,128)(2,1)S(1)}, u32[]{:S(2)}, u32[]{:S(2)}) collective-permute-start(bf16[160,640]{1,0:T(8,128)(2,1)S(1)} %get-tuple-element.62.refs_3_), channel_id=1, source_target_pairs={{0,4},{4,8},{8,12},{12,14},{14,10},{10,6},{6,2},{2,0},{1,5},{5,9},... | collective-permute-start | bytes 614408 | tf_op jit(solution)/shard_map/ppermute | solution.py:381
  75.3 13.6 %collective-permute-start.32 = (bf16[384,640]{1,0:T(8,128)(2,1)S(1)}, bf16[384,640]{1,0:T(8,128)(2,1)S(1)}, u32[]{:S(2)}, u32[]{:S(2)}) collective-permute-start(bf16[384,640]{1,0:T(8,128)(2,1)S(1)} %shard_map.89.refs_3_), channel_id=1, source_target_pairs={{0,16},{16,0},{1,17},{17,1},{2,18},{18,2},{3,19},{19,3},{4,20},{20... | collective-permute-start | bytes 1474568 | tf_op jit(solution)/shard_map/ppermute | solution.py:354
  80.7 8.3 %collective-permute-start.31 = (bf16[384,640]{1,0:T(8,128)(2,1)S(1)}, bf16[384,640]{1,0:T(8,128)(2,1)S(1)}, u32[]{:S(2)}, u32[]{:S(2)}) collective-permute-start(bf16[384,640]{1,0:T(8,128)(2,1)S(1)} %shard_map.94), channel_id=1, source_target_pairs={{0,1},{1,0},{2,3},{3,2},{4,5},{5,4},{6,7},{7,6},{8,9},{9,8},{10,11... | collective-permute-start | bytes 1474568 | tf_op jit(solution)/shard_map/ppermute | solution.py:407
  80.7 7.5 %collective-permute-start.33 = (bf16[160,640]{1,0:T(8,128)(2,1)S(1)}, bf16[160,640]{1,0:T(8,128)(2,1)S(1)}, u32[]{:S(2)}, u32[]{:S(2)}) collective-permute-start(bf16[160,640]{1,0:T(8,128)(2,1)S(1)} %shard_map.92.refs_2_), channel_id=1, source_target_pairs={{4,0},{8,4},{12,8},{14,12},{10,14},{6,10},{2,6},{0,2},{5,1},{9,5},... | collective-permute-start | bytes 614408 | tf_op jit(solution)/shard_map/ppermute | solution.py:381
  81.3 10.9 %collective-permute-start.35 = (bf16[160,640]{1,0:T(8,128)(2,1)S(1)}, bf16[160,640]{1,0:T(8,128)(2,1)S(1)}, u32[]{:S(2)}, u32[]{:S(2)}) collective-permute-start(bf16[160,640]{1,0:T(8,128)(2,1)S(1)} %shard_map.93.refs_1_.refs_3_), channel_id=1, source_target_pairs={{0,4},{4,8},{8,12},{12,14},{14,10},{10,6},{6,2},{2,0},{1,5},{5,9},... | collective-permute-start | bytes 614408 | tf_op jit(solution)/shard_map/ppermute | solution.py:381
  (21 other events, 98.9 us)

commit v17 on v14

--- a/solution.py
+++ b/solution.py
@@ -299,7 +299,7 @@
             [pltpu.SemaphoreType.DMA((len(blocks),))],
             pinned=range(len(blocks)),
         )
-        first = hold(first, *late.values())
+        first = hold(first, *late.values(), near[0])
         sends = ((half - 1, -half), (half, 1 - half))
     else:
         near = [lax.all_gather(block, "gx", axis=0, tiled=True) for block in mine]
@@ -323,7 +323,7 @@
     partial = [partial_own, partial_other]
 
     half_rows_of = shape((frame_len, half_width), BF16)
-    parts_of = [shape((frame_len // 3, half_width), BF16)] * 3
+    parts_of = [half_rows_of]
 
     def own_d_norm(*ties):
         keep, send, *parts = call(
@@ -382,15 +382,15 @@
 
         send_on(0, blocks_own, ("up", "down"))
         send_on(1, blocks_other, ("up", "down"))
-        tie = hop(0, 1, partial_other)
-        keep, send, parts = own_d_norm(tie)
+        keep, send, parts = own_d_norm(*came[0].values())
         tie = hop(1, 1, keep)
+        tie = hop(0, 1, tie)
+        tie = hop(1, 2, tie)
         tie = hop(0, 2, tie)
-        over, back = over_cores(keep, parts, tie)
-        tie = hop(1, 2, over)
+        tie, back = over_cores(keep, parts, tie)
         for turn in range(3, half):
-            tie = hop(1, turn, hop(0, turn, tie))
-        sent = lax.ppermute(hold(send, tie), "gy", swap)
+            tie = hop(0, turn, hop(1, turn, tie))
+        sent = lax.ppermute(send, "gy", swap)
         passing = call(
             functools.partial(total_kernel, peers),
             (partial[1], came[1]["up"], came[1]["down"]),

time: 95.7 us -> 91.1 us (0.952)
  waiting for transfers between devices: 41.8 us -> 36.8 us
    ppermute x6, waiting for transfers between devices: 11.4 us -> 7.92 us  [shards(): down[i] = lax.ppermute(down[i], 'gx', behind)]
    ppermute x1, waiting for transfers between devices: 2.84 us -> 1.01 us  [shards(): passed = lax.ppermute(passing, 'groups', swap)]
    ppermute x1, starting transfers between devices: 0.6 us -> 1.56 us  [shards(): passed = lax.ppermute(passing, 'groups', swap)]
  transfers between devices with their start and end apart: 37 -> 35, of which waited for: 20 -> 21; matrix products, arithmetic and copies ran while one was open for 0% -> 0% of each run, Pallas kernels for 16% -> 17%
where the time goes in v17:
time: 91.1 us; the launch traced here: 90.9 us
  waiting for transfers between devices  36.8 us (40%)
  starting transfers between devices  33.6 us (37%)
  Pallas kernels  19.7 us (22%)
    pallas_call x17, Pallas kernels, call(): pl.pallas_call(body if ties else kernel, out_shape=out_shape, in_specs=[S...  19.7 us
    ppermute x14, waiting for transfers between devices, send_on(): came[i][name] = lax.ppermute(block, 'gx', ahead if name == 'up' else behind)  19.3 us
    ppermute x14, starting transfers between devices, send_on(): came[i][name] = lax.ppermute(block, 'gx', ahead if name == 'up' else behind)  14.1 us
    ppermute x6, starting transfers between devices, shards(): up[i] = lax.ppermute(up[i], 'gx', ahead)  8.39 us
    ppermute x6, waiting for transfers between devices, shards(): down[i] = lax.ppermute(down[i], 'gx', behind)  7.92 us
    ppermute x6, waiting for transfers between devices, shards(): up[i] = lax.ppermute(up[i], 'gx', ahead)  4.61 us
    ppermute x6, starting transfers between devices, shards(): down[i] = lax.ppermute(down[i], 'gx', behind)  3.77 us
    ppermute x1, starting transfers between devices, shards(): first = lax.ppermute(passing, 'groups', swap)  3 us
  transfers between devices with their start and end apart: 35, of which 21 were waited for; matrix products, arithmetic and copies ran while one was open for 0% of the time, Pallas kernels for 17%

profile of v17, /device:TPU:0, one launch (start us, length us, event | category | flops | bytes accessed | tf_op | source)
XLA Modules:
  0.0 90.9 jit_solution(16560681938458649524)
XLA Ops:
  0.7 3.4 %shard_map.78 = (bf16[2,192,1280]{2,1,0:T(8,128)(2,1)}, bf16[160,640]{1,0:T(8,128)(2,1)}, bf16[160,640]{1,0:T(8,128)(2,1)}) custom-call(s32[8]{0:T(128)} %lengths.3, bf16[384,1280]{1,0:T(8,128)(2,1)} %bitcast.3, bf16[384,1280]{1,0:T(8,128)(2,1)} %bitcast.6, f32[1280]{0:T(1024)} %gain.3, bf16[160,1280]{1,0:T(8,128)(2,1)} %w_up.1, bf16[160,1280]{1,0:T(8,128)(2,1)} %w_down.1), custom_call_target="tpu_custom_call" | custom-call | flops 2457600 | bytes 4183072 | tf_op jit(solution)/shard_map/pallas_call | solution.py:28
  4.1 3.0 %collective-permute-start.14 = (bf16[2,192,1280]{2,1,0:T(8,128)(2,1)}, bf16[2,192,1280]{2,1,0:T(8,128)(2,1)S(1)}, u32[]{:S(2)}, u32[]{:S(2)}) collective-permute-start(bf16[2,192,1280]{2,1,0:T(8,128)(2,1)} %get-tuple-element.43), channel_id=1, source_target_pairs={{0,16},{16,0},{1,17},{17,1},{2,18},{18,2},{3,19},{19,3},{4,20},{20... | collective-permute-start | bytes 2949128 | tf_op jit(solution)/shard_map/ppermute | solution.py:269
  7.1 1.6 %collective-permute-start = (bf16[160,640]{1,0:T(8,128)(2,1)}, bf16[160,640]{1,0:T(8,128)(2,1)S(1)}, u32[]{:S(2)}, u32[]{:S(2)}) collective-permute-start(bf16[160,640]{1,0:T(8,128)(2,1)} %get-tuple-element.38.refs_0_), channel_id=1, source_target_pairs={{0,4},{4,8},{8,12},{12,14},{14,10},{10,6},{6,2},{2,0},{1,5},{5,9},... | collective-permute-start | bytes 614408 | tf_op jit(solution)/shard_map/ppermute | solution.py:283
  12.6 2.6 %collective-permute-done.refs_0_ = bf16[160,640]{1,0:T(8,128)(2,1)S(1)} collective-permute-done((bf16[160,640]{1,0:T(8,128)(2,1)}, bf16[160,640]{1,0:T(8,128)(2,1)S(1)}, u32[]{:S(2)}, u32[]{:S(2)}) %collective-permute-start) | collective-permute-done | bytes 204832 | tf_op jit(solution)/shard_map/ppermute | solution.py:283
  15.3 1.6 %collective-permute-start.4 = (bf16[160,640]{1,0:T(8,128)(2,1)S(1)}, bf16[160,640]{1,0:T(8,128)(2,1)S(1)}, u32[]{:S(2)}, u32[]{:S(2)}) collective-permute-start(bf16[160,640]{1,0:T(8,128)(2,1)S(1)} %shard_map.79.refs_2_), channel_id=1, source_target_pairs={{0,4},{4,8},{8,12},{12,14},{14,10},{10,6},{6,2},{2,0},{1,5},{5,9},... | collective-permute-start | bytes 614408 | tf_op jit(solution)/shard_map/ppermute | solution.py:283
  17.3 3.9 %collective-permute-done.1.refs_3_ = bf16[160,640]{1,0:T(8,128)(2,1)S(1)} collective-permute-done((bf16[160,640]{1,0:T(8,128)(2,1)}, bf16[160,640]{1,0:T(8,128)(2,1)S(1)}, u32[]{:S(2)}, u32[]{:S(2)}) %collective-permute-start.1) | collective-permute-done | bytes 204832 | tf_op jit(solution)/shard_map/ppermute | solution.py:284
  21.7 1.6 %collective-permute-start.6 = (bf16[160,640]{1,0:T(8,128)(2,1)S(1)}, bf16[160,640]{1,0:T(8,128)(2,1)S(1)}, u32[]{:S(2)}, u32[]{:S(2)}) collective-permute-start(bf16[160,640]{1,0:T(8,128)(2,1)S(1)} %collective-permute-done.2.refs_4_), channel_id=1, source_target_pairs={{0,4},{4,8},{8,12},{12,14},{14,10},{10,6},{6,2},{2,0},{1,5},{5,9},... | collective-permute-start | bytes 614408 | tf_op jit(solution)/shard_map/ppermute | solution.py:283
  24.1 1.6 %collective-permute-start.8 = (bf16[160,640]{1,0:T(8,128)(2,1)S(1)}, bf16[160,640]{1,0:T(8,128)(2,1)S(1)}, u32[]{:S(2)}, u32[]{:S(2)}) collective-permute-start(bf16[160,640]{1,0:T(8,128)(2,1)S(1)} %collective-permute-done.4.refs_6_), channel_id=1, source_target_pairs={{0,4},{4,8},{8,12},{12,14},{14,10},{10,6},{6,2},{2,0},{1,5},{5,9},... | collective-permute-start | bytes 614408 | tf_op jit(solution)/shard_map/ppermute | solution.py:283
  26.1 3.9 %collective-permute-done.5.refs_7_ = bf16[160,640]{1,0:T(8,128)(2,1)S(1)} collective-permute-done((bf16[160,640]{1,0:T(8,128)(2,1)S(1)}, bf16[160,640]{1,0:T(8,128)(2,1)S(1)}, u32[]{:S(2)}, u32[]{:S(2)}) %collective-permute-start.5) | collective-permute-done | bytes 204832 | tf_op jit(solution)/shard_map/ppermute | solution.py:284
  30.5 1.6 %collective-permute-start.11 = (bf16[160,640]{1,0:T(8,128)(2,1)S(1)}, bf16[160,640]{1,0:T(8,128)(2,1)S(1)}, u32[]{:S(2)}, u32[]{:S(2)}) collective-permute-start(bf16[160,640]{1,0:T(8,128)(2,1)S(1)} %collective-permute-done.6.refs_8_), channel_id=1, source_target_pairs={{0,4},{4,8},{8,12},{12,14},{14,10},{10,6},{6,2},{2,0},{1,5},{5,9},... | collective-permute-start | bytes 614408 | tf_op jit(solution)/shard_map/ppermute | solution.py:283
  33.3 1.6 %collective-permute-start.12 = (bf16[160,640]{1,0:T(8,128)(2,1)S(1)}, bf16[160,640]{1,0:T(8,128)(2,1)S(1)}, u32[]{:S(2)}, u32[]{:S(2)}) collective-permute-start(bf16[160,640]{1,0:T(8,128)(2,1)S(1)} %collective-permute-done.8.refs_10_), channel_id=1, source_target_pairs={{0,4},{4,8},{8,12},{12,14},{14,10},{10,6},{6,2},{2,0},{1,5},{5,9},... | collective-permute-start | bytes 614408 | tf_op jit(solution)/shard_map/ppermute | solution.py:292
  35.3 3.6 %shard_map.80 = (bf16[1280,640]{1,0:T(8,128)(2,1)S(1)}, bf16[1280,640]{1,0:T(8,128)(2,1)S(1)}) custom-call(bf16[160,640]{1,0:T(8,128)(2,1)S(1)} %copy-done.2, bf16[160,640]{1,0:T(8,128)(2,1)S(1)} %copy-done.3, bf16[160,640]{1,0:T(8,128)(2,1)S(1)} %shard_map.79.refs_2_, bf16[160,640]{1,0:T(8,128)(2,1)S(1)} %collective-permute-done.1.refs_3_, ...), custom_call_target="tpu_custom_call" | custom-call | flops 1 | bytes 5734400 | tf_op jit(solution)/shard_map/pallas_call | solution.py:28
  41.5 2.9 %shard_map.81 = (bf16[384,640]{1,0:T(8,128)(2,1)S(1)}, bf16[1280,640]{1,0:T(8,128)(2,1)S(1)}, bf16[1280,640]{1,0:T(8,128)(2,1)S(1)}, bf16[1280,640]{1,0:T(8,128)...) custom-call(bf16[384,1280]{1,0:T(8,128)(2,1)S(1)} %get-tuple-element.36.refs_1_.normed, ...), custom_call_target="tpu_custom_call" | custom-call | flops 1887436800 | bytes 11878400 | tf_op jit(solution)/shard_map/pallas_call | solution.py:28
  44.4 1.6 %collective-permute-start.16 = (bf16[160,640]{1,0:T(8,128)(2,1)S(1)}, bf16[160,640]{1,0:T(8,128)(2,1)S(1)}, u32[]{:S(2)}, u32[]{:S(2)}) collective-permute-start(bf16[160,640]{1,0:T(8,128)(2,1)S(1)} %get-tuple-element.47), channel_id=1, source_target_pairs={{0,4},{4,8},{8,12},{12,14},{14,10},{10,6},{6,2},{2,0},{1,5},{5,9},... | collective-permute-start | bytes 614408 | tf_op jit(solution)/shard_map/ppermute | solution.py:367
  46.5 2.7 %shard_map.83 = (bf16[384,640]{1,0:T(8,128)(2,1)S(1)}, bf16[1280,640]{1,0:T(8,128)(2,1)S(1)}, bf16[160,640]{1,0:T(8,128)(2,1)S(1)}, bf16[160,640]{1,0:T(8,128)(2,1)S(1)}) custom-call(bf16[2,192,1280]{2,1,0:T(8,128)(2,1)S(1)} %shard_map.82.first, bf16[2,192,1280]{2,1,0:T(8,128)(2,1)S(1)} %collective-permute-done.15.second, ...), custom_call_target="tpu_custom_call" | custom-call | flops 1887436800 | bytes 7782400 | tf_op jit(solution)/shard_map/pallas_call | solution.py:28
  49.2 1.6 %collective-permute-start.20 = (bf16[160,640]{1,0:T(8,128)(2,1)S(1)}, bf16[160,640]{1,0:T(8,128)(2,1)S(1)}, u32[]{:S(2)}, u32[]{:S(2)}) collective-permute-start(bf16[160,640]{1,0:T(8,128)(2,1)S(1)} %get-tuple-element.54), channel_id=1, source_target_pairs={{0,4},{4,8},{8,12},{12,14},{14,10},{10,6},{6,2},{2,0},{1,5},{5,9},... | collective-permute-start | bytes 614408 | tf_op jit(solution)/shard_map/ppermute | solution.py:367
  53.3 2.0 %shard_map.84 = (bf16[2,384,640]{2,1,0:T(8,128)(2,1)S(1)}, bf16[384,640]{1,0:T(8,128)(2,1)S(1)}, bf16[384,640]{1,0:T(8,128)(2,1)S(1)}) custom-call(bf16[384,640]{1,0:T(8,128)(2,1)S(1)} %get-tuple-element.42.refs_0_, bf16[384,640]{1,0:T(8,128)(2,1)S(1)} %get-tuple-element.46.refs_1_, bf16[1280,640]{1,0:T(8,128)(2,1)S(1)} %get-tuple-element.44.up.refs_2_, ...), custom_call_target="tpu_custom_call" | custom-call | flops 1258291200 | bytes 4587520 | tf_op jit(solution)/shard_map/pallas_call | solution.py:28
  57.8 1.6 %collective-permute-start.24 = (bf16[160,640]{1,0:T(8,128)(2,1)S(1)}, bf16[160,640]{1,0:T(8,128)(2,1)S(1)}, u32[]{:S(2)}, u32[]{:S(2)}) collective-permute-start(bf16[160,640]{1,0:T(8,128)(2,1)S(1)} %get-tuple-element.56.refs_3_), channel_id=1, source_target_pairs={{0,4},{4,8},{8,12},{12,14},{14,10},{10,6},{6,2},{2,0},{1,5},{5,9},... | collective-permute-start | bytes 614408 | tf_op jit(solution)/shard_map/ppermute | solution.py:367
  60.0 1.6 %collective-permute-start.22 = (bf16[160,640]{1,0:T(8,128)(2,1)S(1)}, bf16[160,640]{1,0:T(8,128)(2,1)S(1)}, u32[]{:S(2)}, u32[]{:S(2)}) collective-permute-start(bf16[160,640]{1,0:T(8,128)(2,1)S(1)} %get-tuple-element.57.refs_3_), channel_id=1, source_target_pairs={{0,4},{4,8},{8,12},{12,14},{14,10},{10,6},{6,2},{2,0},{1,5},{5,9},... | collective-permute-start | bytes 614408 | tf_op jit(solution)/shard_map/ppermute | solution.py:367
  62.0 3.8 %collective-permute-done.24.refs_1_ = bf16[160,640]{1,0:T(8,128)(2,1)S(1)} collective-permute-done((bf16[160,640]{1,0:T(8,128)(2,1)S(1)}, bf16[160,640]{1,0:T(8,128)(2,1)S(1)}, u32[]{:S(2)}, u32[]{:S(2)}) %collective-permute-start.24) | collective-permute-done | bytes 204832 | tf_op jit(solution)/shard_map/ppermute | solution.py:367
  65.8 1.6 %collective-permute-done.25.refs_2_ = bf16[160,640]{1,0:T(8,128)(2,1)S(1)} collective-permute-done((bf16[160,640]{1,0:T(8,128)(2,1)S(1)}, bf16[160,640]{1,0:T(8,128)(2,1)S(1)}, u32[]{:S(2)}, u32[]{:S(2)}) %collective-permute-start.25) | collective-permute-done | bytes 204832 | tf_op jit(solution)/shard_map/ppermute | solution.py:367
  67.5 1.6 %collective-permute-start.27 = (bf16[160,640]{1,0:T(8,128)(2,1)S(1)}, bf16[160,640]{1,0:T(8,128)(2,1)S(1)}, u32[]{:S(2)}, u32[]{:S(2)}) collective-permute-start(bf16[160,640]{1,0:T(8,128)(2,1)S(1)} %get-tuple-element.60.refs_3_), channel_id=1, source_target_pairs={{0,4},{4,8},{8,12},{12,14},{14,10},{10,6},{6,2},{2,0},{1,5},{5,9},... | collective-permute-start | bytes 614408 | tf_op jit(solution)/shard_map/ppermute | solution.py:367
  75.5 2.8 %collective-permute-done.30.refs_1_ = bf16[160,640]{1,0:T(8,128)(2,1)S(1)} collective-permute-done((bf16[160,640]{1,0:T(8,128)(2,1)S(1)}, bf16[160,640]{1,0:T(8,128)(2,1)S(1)}, u32[]{:S(2)}, u32[]{:S(2)}) %collective-permute-start.30) | collective-permute-done | bytes 204832 | tf_op jit(solution)/shard_map/ppermute | solution.py:367
  78.3 3.5 %collective-permute-done.31.refs_3_.refs_2_ = bf16[160,640]{1,0:T(8,128)(2,1)S(1)} collective-permute-done((bf16[160,640]{1,0:T(8,128)(2,1)S(1)}, bf16[160,640]{1,0:T(8,128)(2,1)S(1)}, u32[]{:S(2)}, u32[]{:S(2)}) %collective-permute-start.31) | collective-permute-done | bytes 204832 | tf_op jit(solution)/shard_map/ppermute | solution.py:367
  (78 shorter events, 32.8 us)
Async XLA Ops:
  4.1 37.4 %collective-permute-start.14 = (bf16[2,192,1280]{2,1,0:T(8,128)(2,1)}, bf16[2,192,1280]{2,1,0:T(8,128)(2,1)S(1)}, u32[]{:S(2)}, u32[]{:S(2)}) collective-permute-start(bf16[2,192,1280]{2,1,0:T(8,128)(2,1)} %get-tuple-element.43), channel_id=1, source_target_pairs={{0,16},{16,0},{1,17},{17,1},{2,18},{18,2},{3,19},{19,3},{4,20},{20... | collective-permute-start | bytes 2949128 | tf_op jit(solution)/shard_map/ppermute | solution.py:269
  7.1 8.2 %collective-permute-start = (bf16[160,640]{1,0:T(8,128)(2,1)}, bf16[160,640]{1,0:T(8,128)(2,1)S(1)}, u32[]{:S(2)}, u32[]{:S(2)}) collective-permute-start(bf16[160,640]{1,0:T(8,128)(2,1)} %get-tuple-element.38.refs_0_), channel_id=1, source_target_pairs={{0,4},{4,8},{8,12},{12,14},{14,10},{10,6},{6,2},{2,0},{1,5},{5,9},... | collective-permute-start | bytes 614408 | tf_op jit(solution)/shard_map/ppermute | solution.py:283
  8.7 8.2 %collective-permute-start.3 = (bf16[160,640]{1,0:T(8,128)(2,1)}, bf16[160,640]{1,0:T(8,128)(2,1)S(1)}, u32[]{:S(2)}, u32[]{:S(2)}) collective-permute-start(bf16[160,640]{1,0:T(8,128)(2,1)} %get-tuple-element.39.refs_1_), channel_id=1, source_target_pairs={{4,0},{8,4},{12,8},{14,12},{10,14},{6,10},{2,6},{0,2},{5,1},{9,5},... | collective-permute-start | bytes 614408 | tf_op jit(solution)/shard_map/ppermute | solution.py:284
  9.1 12.2 %collective-permute-start.1 = (bf16[160,640]{1,0:T(8,128)(2,1)}, bf16[160,640]{1,0:T(8,128)(2,1)S(1)}, u32[]{:S(2)}, u32[]{:S(2)}) collective-permute-start(bf16[160,640]{1,0:T(8,128)(2,1)} %get-tuple-element.38.refs_0_), channel_id=1, source_target_pairs={{4,0},{8,4},{12,8},{14,12},{10,14},{6,10},{2,6},{0,2},{5,1},{9,5},... | collective-permute-start | bytes 614408 | tf_op jit(solution)/shard_map/ppermute | solution.py:284
  10.6 11.1 %collective-permute-start.2 = (bf16[160,640]{1,0:T(8,128)(2,1)}, bf16[160,640]{1,0:T(8,128)(2,1)S(1)}, u32[]{:S(2)}, u32[]{:S(2)}) collective-permute-start(bf16[160,640]{1,0:T(8,128)(2,1)} %get-tuple-element.39.refs_1_), channel_id=1, source_target_pairs={{0,4},{4,8},{8,12},{12,14},{14,10},{10,6},{6,2},{2,0},{1,5},{5,9},... | collective-permute-start | bytes 614408 | tf_op jit(solution)/shard_map/ppermute | solution.py:283
  15.3 8.8 %collective-permute-start.4 = (bf16[160,640]{1,0:T(8,128)(2,1)S(1)}, bf16[160,640]{1,0:T(8,128)(2,1)S(1)}, u32[]{:S(2)}, u32[]{:S(2)}) collective-permute-start(bf16[160,640]{1,0:T(8,128)(2,1)S(1)} %shard_map.79.refs_2_), channel_id=1, source_target_pairs={{0,4},{4,8},{8,12},{12,14},{14,10},{10,6},{6,2},{2,0},{1,5},{5,9},... | collective-permute-start | bytes 614408 | tf_op jit(solution)/shard_map/ppermute | solution.py:283
  16.9 8.8 %collective-permute-start.7 = (bf16[160,640]{1,0:T(8,128)(2,1)S(1)}, bf16[160,640]{1,0:T(8,128)(2,1)S(1)}, u32[]{:S(2)}, u32[]{:S(2)}) collective-permute-start(bf16[160,640]{1,0:T(8,128)(2,1)S(1)} %collective-permute-done.3.refs_5_), channel_id=1, source_target_pairs={{4,0},{8,4},{12,8},{14,12},{10,14},{6,10},{2,6},{0,2},{5,1},{9,5},... | collective-permute-start | bytes 614408 | tf_op jit(solution)/shard_map/ppermute | solution.py:284
  21.3 8.8 %collective-permute-start.5 = (bf16[160,640]{1,0:T(8,128)(2,1)S(1)}, bf16[160,640]{1,0:T(8,128)(2,1)S(1)}, u32[]{:S(2)}, u32[]{:S(2)}) collective-permute-start(bf16[160,640]{1,0:T(8,128)(2,1)S(1)} %collective-permute-done.1.refs_3_), channel_id=1, source_target_pairs={{4,0},{8,4},{12,8},{14,12},{10,14},{6,10},{2,6},{0,2},{5,1},{9,5},... | collective-permute-start | bytes 614408 | tf_op jit(solution)/shard_map/ppermute | solution.py:284
  21.7 8.8 %collective-permute-start.6 = (bf16[160,640]{1,0:T(8,128)(2,1)S(1)}, bf16[160,640]{1,0:T(8,128)(2,1)S(1)}, u32[]{:S(2)}, u32[]{:S(2)}) collective-permute-start(bf16[160,640]{1,0:T(8,128)(2,1)S(1)} %collective-permute-done.2.refs_4_), channel_id=1, source_target_pairs={{0,4},{4,8},{8,12},{12,14},{14,10},{10,6},{6,2},{2,0},{1,5},{5,9},... | collective-permute-start | bytes 614408 | tf_op jit(solution)/shard_map/ppermute | solution.py:283
  24.1 9.2 %collective-permute-start.8 = (bf16[160,640]{1,0:T(8,128)(2,1)S(1)}, bf16[160,640]{1,0:T(8,128)(2,1)S(1)}, u32[]{:S(2)}, u32[]{:S(2)}) collective-permute-start(bf16[160,640]{1,0:T(8,128)(2,1)S(1)} %collective-permute-done.4.refs_6_), channel_id=1, source_target_pairs={{0,4},{4,8},{8,12},{12,14},{14,10},{10,6},{6,2},{2,0},{1,5},{5,9},... | collective-permute-start | bytes 614408 | tf_op jit(solution)/shard_map/ppermute | solution.py:283
  25.7 9.2 %collective-permute-start.9 = (bf16[160,640]{1,0:T(8,128)(2,1)S(1)}, bf16[160,640]{1,0:T(8,128)(2,1)S(1)}, u32[]{:S(2)}, u32[]{:S(2)}) collective-permute-start(bf16[160,640]{1,0:T(8,128)(2,1)S(1)} %collective-permute-done.7.refs_9_), channel_id=1, source_target_pairs={{4,0},{8,4},{12,8},{14,12},{10,14},{6,10},{2,6},{0,2},{5,1},{9,5},... | collective-permute-start | bytes 614408 | tf_op jit(solution)/shard_map/ppermute | solution.py:284
  30.1 8.8 %collective-permute-start.10 = (bf16[160,640]{1,0:T(8,128)(2,1)S(1)}, bf16[160,640]{1,0:T(8,128)(2,1)S(1)}, u32[]{:S(2)}, u32[]{:S(2)}) collective-permute-start(bf16[160,640]{1,0:T(8,128)(2,1)S(1)} %collective-permute-done.5.refs_7_), channel_id=1, source_target_pairs={{4,0},{8,4},{12,8},{14,12},{10,14},{6,10},{2,6},{0,2},{5,1},{9,5},... | collective-permute-start | bytes 614408 | tf_op jit(solution)/shard_map/ppermute | solution.py:284
  30.5 8.4 %collective-permute-start.11 = (bf16[160,640]{1,0:T(8,128)(2,1)S(1)}, bf16[160,640]{1,0:T(8,128)(2,1)S(1)}, u32[]{:S(2)}, u32[]{:S(2)}) collective-permute-start(bf16[160,640]{1,0:T(8,128)(2,1)S(1)} %collective-permute-done.6.refs_8_), channel_id=1, source_target_pairs={{0,4},{4,8},{8,12},{12,14},{14,10},{10,6},{6,2},{2,0},{1,5},{5,9},... | collective-permute-start | bytes 614408 | tf_op jit(solution)/shard_map/ppermute | solution.py:283
  44.4 7.6 %collective-permute-start.16 = (bf16[160,640]{1,0:T(8,128)(2,1)S(1)}, bf16[160,640]{1,0:T(8,128)(2,1)S(1)}, u32[]{:S(2)}, u32[]{:S(2)}) collective-permute-start(bf16[160,640]{1,0:T(8,128)(2,1)S(1)} %get-tuple-element.47), channel_id=1, source_target_pairs={{0,4},{4,8},{8,12},{12,14},{14,10},{10,6},{6,2},{2,0},{1,5},{5,9},... | collective-permute-start | bytes 614408 | tf_op jit(solution)/shard_map/ppermute | solution.py:367
  46.0 7.3 %collective-permute-start.17 = (bf16[160,640]{1,0:T(8,128)(2,1)S(1)}, bf16[160,640]{1,0:T(8,128)(2,1)S(1)}, u32[]{:S(2)}, u32[]{:S(2)}) collective-permute-start(bf16[160,640]{1,0:T(8,128)(2,1)S(1)} %get-tuple-element.48), channel_id=1, source_target_pairs={{4,0},{8,4},{12,8},{14,12},{10,14},{6,10},{2,6},{0,2},{5,1},{9,5},... | collective-permute-start | bytes 614408 | tf_op jit(solution)/shard_map/ppermute | solution.py:367
  55.3 16.4 %collective-permute-start.19 = (bf16[384,640]{1,0:T(8,128)(2,1)S(1)}, bf16[384,640]{1,0:T(8,128)(2,1)S(1)}, u32[]{:S(2)}, u32[]{:S(2)}) collective-permute-start(bf16[384,640]{1,0:T(8,128)(2,1)S(1)} %get-tuple-element.51), channel_id=1, source_target_pairs={{0,1},{1,0},{2,3},{3,2},{4,5},{5,4},{6,7},{7,6},{8,9},{9,8},{10,11... | collective-permute-start | bytes 1474568 | tf_op jit(solution)/shard_map/ppermute | solution.py:336
  57.8 8.1 %collective-permute-start.24 = (bf16[160,640]{1,0:T(8,128)(2,1)S(1)}, bf16[160,640]{1,0:T(8,128)(2,1)S(1)}, u32[]{:S(2)}, u32[]{:S(2)}) collective-permute-start(bf16[160,640]{1,0:T(8,128)(2,1)S(1)} %get-tuple-element.56.refs_3_), channel_id=1, source_target_pairs={{0,4},{4,8},{8,12},{12,14},{14,10},{10,6},{6,2},{2,0},{1,5},{5,9},... | collective-permute-start | bytes 614408 | tf_op jit(solution)/shard_map/ppermute | solution.py:367
  59.4 8.0 %collective-permute-start.25 = (bf16[160,640]{1,0:T(8,128)(2,1)S(1)}, bf16[160,640]{1,0:T(8,128)(2,1)S(1)}, u32[]{:S(2)}, u32[]{:S(2)}) collective-permute-start(bf16[160,640]{1,0:T(8,128)(2,1)S(1)} %get-tuple-element.59), channel_id=1, source_target_pairs={{4,0},{8,4},{12,8},{14,12},{10,14},{6,10},{2,6},{0,2},{5,1},{9,5},... | collective-permute-start | bytes 614408 | tf_op jit(solution)/shard_map/ppermute | solution.py:367
  60.0 10.3 %collective-permute-start.22 = (bf16[160,640]{1,0:T(8,128)(2,1)S(1)}, bf16[160,640]{1,0:T(8,128)(2,1)S(1)}, u32[]{:S(2)}, u32[]{:S(2)}) collective-permute-start(bf16[160,640]{1,0:T(8,128)(2,1)S(1)} %get-tuple-element.57.refs_3_), channel_id=1, source_target_pairs={{0,4},{4,8},{8,12},{12,14},{14,10},{10,6},{6,2},{2,0},{1,5},{5,9},... | collective-permute-start | bytes 614408 | tf_op jit(solution)/shard_map/ppermute | solution.py:367
  61.6 10.0 %collective-permute-start.23 = (bf16[160,640]{1,0:T(8,128)(2,1)S(1)}, bf16[160,640]{1,0:T(8,128)(2,1)S(1)}, u32[]{:S(2)}, u32[]{:S(2)}) collective-permute-start(bf16[160,640]{1,0:T(8,128)(2,1)S(1)} %get-tuple-element.58), channel_id=1, source_target_pairs={{4,0},{8,4},{12,8},{14,12},{10,14},{6,10},{2,6},{0,2},{5,1},{9,5},... | collective-permute-start | bytes 614408 | tf_op jit(solution)/shard_map/ppermute | solution.py:367
  70.2 15.4 %collective-permute-start.18 = (bf16[384,640]{1,0:T(8,128)(2,1)S(1)}, bf16[384,640]{1,0:T(8,128)(2,1)S(1)}, u32[]{:S(2)}, u32[]{:S(2)}) collective-permute-start(bf16[384,640]{1,0:T(8,128)(2,1)S(1)} %get-tuple-element.50), channel_id=1, source_target_pairs={{0,1},{1,0},{2,3},{3,2},{4,5},{5,4},{6,7},{7,6},{8,9},{9,8},{10,11... | collective-permute-start | bytes 1474568 | tf_op jit(solution)/shard_map/ppermute | solution.py:393
  71.8 13.8 %collective-permute-start.26 = (bf16[384,640]{1,0:T(8,128)(2,1)S(1)}, bf16[384,640]{1,0:T(8,128)(2,1)S(1)}, u32[]{:S(2)}, u32[]{:S(2)}) collective-permute-start(bf16[384,640]{1,0:T(8,128)(2,1)S(1)} %shard_map.89.refs_2_), channel_id=1, source_target_pairs={{0,16},{16,0},{1,17},{17,1},{2,18},{18,2},{3,19},{19,3},{4,20},{20... | collective-permute-start | bytes 1474568 | tf_op jit(solution)/shard_map/ppermute | solution.py:340
  74.0 7.8 %collective-permute-start.31 = (bf16[160,640]{1,0:T(8,128)(2,1)S(1)}, bf16[160,640]{1,0:T(8,128)(2,1)S(1)}, u32[]{:S(2)}, u32[]{:S(2)}) collective-permute-start(bf16[160,640]{1,0:T(8,128)(2,1)S(1)} %get-tuple-element.64), channel_id=1, source_target_pairs={{4,0},{8,4},{12,8},{14,12},{10,14},{6,10},{2,6},{0,2},{5,1},{9,5},... | collective-permute-start | bytes 614408 | tf_op jit(solution)/shard_map/ppermute | solution.py:367
  74.9 9.0 %collective-permute-start.29 = (bf16[160,640]{1,0:T(8,128)(2,1)S(1)}, bf16[160,640]{1,0:T(8,128)(2,1)S(1)}, u32[]{:S(2)}, u32[]{:S(2)}) collective-permute-start(bf16[160,640]{1,0:T(8,128)(2,1)S(1)} %shard_map.90.refs_2_), channel_id=1, source_target_pairs={{4,0},{8,4},{12,8},{14,12},{10,14},{6,10},{2,6},{0,2},{5,1},{9,5},... | collective-permute-start | bytes 614408 | tf_op jit(solution)/shard_map/ppermute | solution.py:367
  (17 other events, 160.1 us)

commit v18 on v17

--- a/solution.py
+++ b/solution.py
@@ -382,11 +382,11 @@
 
         send_on(0, blocks_own, ("up", "down"))
         send_on(1, blocks_other, ("up", "down"))
-        keep, send, parts = own_d_norm(*came[0].values())
+        tie = hop(0, 1, partial_other)
+        keep, send, parts = own_d_norm(tie)
         tie = hop(1, 1, keep)
-        tie = hop(0, 1, tie)
+        tie = hop(0, 2, tie)
         tie = hop(1, 2, tie)
-        tie = hop(0, 2, tie)
         tie, back = over_cores(keep, parts, tie)
         for turn in range(3, half):
             tie = hop(0, turn, hop(1, turn, tie))

time: 91.1 us -> 92.4 us (1.014)
  waiting for transfers between devices: 36.8 us -> 38.6 us
    ppermute x14, waiting for transfers between devices: 19.3 us -> 20.3 us  [send_on(): came[i][name] = lax.ppermute(block, 'gx', ahead if name == 'up' else behind)]
  transfers between devices with their start and end apart: 35 -> 35, of which waited for: 21 -> 20; matrix products, arithmetic and copies ran while one was open for 0% -> 0% of each run, Pallas kernels for 17% -> 17%
where the time goes in v18:
time: 92.4 us; the launch traced here: 92.2 us
  waiting for transfers between devices  38.6 us (42%)
  starting transfers between devices  33 us (36%)
  Pallas kernels  19.7 us (21%)
    ppermute x14, waiting for transfers between devices, send_on(): came[i][name] = lax.ppermute(block, 'gx', ahead if name == 'up' else behind)  20.3 us
    pallas_call x17, Pallas kernels, call(): pl.pallas_call(body if ties else kernel, out_shape=out_shape, in_specs=[S...  19.7 us
    ppermute x14, starting transfers between devices, send_on(): came[i][name] = lax.ppermute(block, 'gx', ahead if name == 'up' else behind)  14.3 us
    ppermute x6, starting transfers between devices, shards(): up[i] = lax.ppermute(up[i], 'gx', ahead)  8.39 us
    ppermute x6, waiting for transfers between devices, shards(): down[i] = lax.ppermute(down[i], 'gx', behind)  7.92 us
    ppermute x6, waiting for transfers between devices, shards(): up[i] = lax.ppermute(up[i], 'gx', ahead)  4.61 us
    ppermute x6, starting transfers between devices, shards(): down[i] = lax.ppermute(down[i], 'gx', behind)  3.77 us
    ppermute x1, starting transfers between devices, shards(): first = lax.ppermute(passing, 'groups', swap)  3 us
  transfers between devices with their start and end apart: 35, of which 20 were waited for; matrix products, arithmetic and copies ran while one was open for 0% of the time, Pallas kernels for 17%

profile of v18, /device:TPU:0, one launch (start us, length us, event | category | flops | bytes accessed | tf_op | source)
XLA Modules:
  0.0 92.2 jit_solution(889828039123305482)
XLA Ops:
  0.7 3.4 %shard_map.78 = (bf16[2,192,1280]{2,1,0:T(8,128)(2,1)}, bf16[160,640]{1,0:T(8,128)(2,1)}, bf16[160,640]{1,0:T(8,128)(2,1)}) custom-call(s32[8]{0:T(128)} %lengths.3, bf16[384,1280]{1,0:T(8,128)(2,1)} %bitcast.3, bf16[384,1280]{1,0:T(8,128)(2,1)} %bitcast.6, f32[1280]{0:T(1024)} %gain.3, bf16[160,1280]{1,0:T(8,128)(2,1)} %w_up.1, bf16[160,1280]{1,0:T(8,128)(2,1)} %w_down.1), custom_call_target="tpu_custom_call" | custom-call | flops 2457600 | bytes 4183072 | tf_op jit(solution)/shard_map/pallas_call | solution.py:28
  4.1 3.0 %collective-permute-start.14 = (bf16[2,192,1280]{2,1,0:T(8,128)(2,1)}, bf16[2,192,1280]{2,1,0:T(8,128)(2,1)S(1)}, u32[]{:S(2)}, u32[]{:S(2)}) collective-permute-start(bf16[2,192,1280]{2,1,0:T(8,128)(2,1)} %get-tuple-element.43), channel_id=1, source_target_pairs={{0,16},{16,0},{1,17},{17,1},{2,18},{18,2},{3,19},{19,3},{4,20},{20... | collective-permute-start | bytes 2949128 | tf_op jit(solution)/shard_map/ppermute | solution.py:269
  7.1 1.6 %collective-permute-start = (bf16[160,640]{1,0:T(8,128)(2,1)}, bf16[160,640]{1,0:T(8,128)(2,1)S(1)}, u32[]{:S(2)}, u32[]{:S(2)}) collective-permute-start(bf16[160,640]{1,0:T(8,128)(2,1)} %get-tuple-element.38.refs_0_), channel_id=1, source_target_pairs={{0,4},{4,8},{8,12},{12,14},{14,10},{10,6},{6,2},{2,0},{1,5},{5,9},... | collective-permute-start | bytes 614408 | tf_op jit(solution)/shard_map/ppermute | solution.py:283
  12.6 2.6 %collective-permute-done.refs_0_ = bf16[160,640]{1,0:T(8,128)(2,1)S(1)} collective-permute-done((bf16[160,640]{1,0:T(8,128)(2,1)}, bf16[160,640]{1,0:T(8,128)(2,1)S(1)}, u32[]{:S(2)}, u32[]{:S(2)}) %collective-permute-start) | collective-permute-done | bytes 204832 | tf_op jit(solution)/shard_map/ppermute | solution.py:283
  15.3 1.6 %collective-permute-start.4 = (bf16[160,640]{1,0:T(8,128)(2,1)S(1)}, bf16[160,640]{1,0:T(8,128)(2,1)S(1)}, u32[]{:S(2)}, u32[]{:S(2)}) collective-permute-start(bf16[160,640]{1,0:T(8,128)(2,1)S(1)} %shard_map.79.refs_2_), channel_id=1, source_target_pairs={{0,4},{4,8},{8,12},{12,14},{14,10},{10,6},{6,2},{2,0},{1,5},{5,9},... | collective-permute-start | bytes 614408 | tf_op jit(solution)/shard_map/ppermute | solution.py:283
  17.3 3.9 %collective-permute-done.1.refs_3_ = bf16[160,640]{1,0:T(8,128)(2,1)S(1)} collective-permute-done((bf16[160,640]{1,0:T(8,128)(2,1)}, bf16[160,640]{1,0:T(8,128)(2,1)S(1)}, u32[]{:S(2)}, u32[]{:S(2)}) %collective-permute-start.1) | collective-permute-done | bytes 204832 | tf_op jit(solution)/shard_map/ppermute | solution.py:284
  21.7 1.6 %collective-permute-start.6 = (bf16[160,640]{1,0:T(8,128)(2,1)S(1)}, bf16[160,640]{1,0:T(8,128)(2,1)S(1)}, u32[]{:S(2)}, u32[]{:S(2)}) collective-permute-start(bf16[160,640]{1,0:T(8,128)(2,1)S(1)} %collective-permute-done.2.refs_4_), channel_id=1, source_target_pairs={{0,4},{4,8},{8,12},{12,14},{14,10},{10,6},{6,2},{2,0},{1,5},{5,9},... | collective-permute-start | bytes 614408 | tf_op jit(solution)/shard_map/ppermute | solution.py:283
  26.1 3.9 %collective-permute-done.5.refs_7_ = bf16[160,640]{1,0:T(8,128)(2,1)S(1)} collective-permute-done((bf16[160,640]{1,0:T(8,128)(2,1)S(1)}, bf16[160,640]{1,0:T(8,128)(2,1)S(1)}, u32[]{:S(2)}, u32[]{:S(2)}) %collective-permute-start.5) | collective-permute-done | bytes 204832 | tf_op jit(solution)/shard_map/ppermute | solution.py:284
  30.5 1.6 %collective-permute-start.11 = (bf16[160,640]{1,0:T(8,128)(2,1)S(1)}, bf16[160,640]{1,0:T(8,128)(2,1)S(1)}, u32[]{:S(2)}, u32[]{:S(2)}) collective-permute-start(bf16[160,640]{1,0:T(8,128)(2,1)S(1)} %collective-permute-done.6.refs_8_), channel_id=1, source_target_pairs={{0,4},{4,8},{8,12},{12,14},{14,10},{10,6},{6,2},{2,0},{1,5},{5,9},... | collective-permute-start | bytes 614408 | tf_op jit(solution)/shard_map/ppermute | solution.py:283
  35.3 3.6 %shard_map.80 = (bf16[1280,640]{1,0:T(8,128)(2,1)S(1)}, bf16[1280,640]{1,0:T(8,128)(2,1)S(1)}) custom-call(bf16[160,640]{1,0:T(8,128)(2,1)S(1)} %copy-done.2, bf16[160,640]{1,0:T(8,128)(2,1)S(1)} %copy-done.3, bf16[160,640]{1,0:T(8,128)(2,1)S(1)} %shard_map.79.refs_2_, bf16[160,640]{1,0:T(8,128)(2,1)S(1)} %collective-permute-done.1.refs_3_, ...), custom_call_target="tpu_custom_call" | custom-call | flops 1 | bytes 5734400 | tf_op jit(solution)/shard_map/pallas_call | solution.py:28
  41.5 2.9 %shard_map.81 = (bf16[384,640]{1,0:T(8,128)(2,1)S(1)}, bf16[1280,640]{1,0:T(8,128)(2,1)S(1)}, bf16[1280,640]{1,0:T(8,128)(2,1)S(1)}, bf16[1280,640]{1,0:T(8,128)...) custom-call(bf16[384,1280]{1,0:T(8,128)(2,1)S(1)} %get-tuple-element.36.refs_1_.normed, ...), custom_call_target="tpu_custom_call" | custom-call | flops 1887436800 | bytes 11878400 | tf_op jit(solution)/shard_map/pallas_call | solution.py:28
  44.4 1.6 %collective-permute-start.16 = (bf16[160,640]{1,0:T(8,128)(2,1)S(1)}, bf16[160,640]{1,0:T(8,128)(2,1)S(1)}, u32[]{:S(2)}, u32[]{:S(2)}) collective-permute-start(bf16[160,640]{1,0:T(8,128)(2,1)S(1)} %get-tuple-element.48), channel_id=1, source_target_pairs={{0,4},{4,8},{8,12},{12,14},{14,10},{10,6},{6,2},{2,0},{1,5},{5,9},... | collective-permute-start | bytes 614408 | tf_op jit(solution)/shard_map/ppermute | solution.py:367
  46.5 2.7 %shard_map.83 = (bf16[384,640]{1,0:T(8,128)(2,1)S(1)}, bf16[1280,640]{1,0:T(8,128)(2,1)S(1)}, bf16[160,640]{1,0:T(8,128)(2,1)S(1)}, bf16[160,640]{1,0:T(8,128)(2,1)S(1)}) custom-call(bf16[2,192,1280]{2,1,0:T(8,128)(2,1)S(1)} %shard_map.82.first, bf16[2,192,1280]{2,1,0:T(8,128)(2,1)S(1)} %collective-permute-done.15.second, ...), custom_call_target="tpu_custom_call" | custom-call | flops 1887436800 | bytes 7782400 | tf_op jit(solution)/shard_map/pallas_call | solution.py:28
  49.2 1.6 %collective-permute-start.20 = (bf16[160,640]{1,0:T(8,128)(2,1)S(1)}, bf16[160,640]{1,0:T(8,128)(2,1)S(1)}, u32[]{:S(2)}, u32[]{:S(2)}) collective-permute-start(bf16[160,640]{1,0:T(8,128)(2,1)S(1)} %get-tuple-element.55), channel_id=1, source_target_pairs={{0,4},{4,8},{8,12},{12,14},{14,10},{10,6},{6,2},{2,0},{1,5},{5,9},... | collective-permute-start | bytes 614408 | tf_op jit(solution)/shard_map/ppermute | solution.py:367
  53.5 2.0 %shard_map.85 = (bf16[2,384,640]{2,1,0:T(8,128)(2,1)S(1)}, bf16[384,640]{1,0:T(8,128)(2,1)S(1)}, bf16[384,640]{1,0:T(8,128)(2,1)S(1)}) custom-call(bf16[384,640]{1,0:T(8,128)(2,1)S(1)} %get-tuple-element.42.refs_0_, bf16[384,640]{1,0:T(8,128)(2,1)S(1)} %get-tuple-element.46.refs_1_, bf16[1280,640]{1,0:T(8,128)(2,1)S(1)} %get-tuple-element.44.up.refs_2_, ...), custom_call_target="tpu_custom_call" | custom-call | flops 1258291200 | bytes 4587520 | tf_op jit(solution)/shard_map/pallas_call | solution.py:28
  55.6 1.6 %collective-permute-start.24 = (bf16[160,640]{1,0:T(8,128)(2,1)S(1)}, bf16[160,640]{1,0:T(8,128)(2,1)S(1)}, u32[]{:S(2)}, u32[]{:S(2)}) collective-permute-start(bf16[160,640]{1,0:T(8,128)(2,1)S(1)} %get-tuple-element.51.refs_3_), channel_id=1, source_target_pairs={{0,4},{4,8},{8,12},{12,14},{14,10},{10,6},{6,2},{2,0},{1,5},{5,9},... | collective-permute-start | bytes 614408 | tf_op jit(solution)/shard_map/ppermute | solution.py:367
  57.8 1.6 %collective-permute-start.22 = (bf16[160,640]{1,0:T(8,128)(2,1)S(1)}, bf16[160,640]{1,0:T(8,128)(2,1)S(1)}, u32[]{:S(2)}, u32[]{:S(2)}) collective-permute-start(bf16[160,640]{1,0:T(8,128)(2,1)S(1)} %get-tuple-element.57.refs_3_), channel_id=1, source_target_pairs={{0,4},{4,8},{8,12},{12,14},{14,10},{10,6},{6,2},{2,0},{1,5},{5,9},... | collective-permute-start | bytes 614408 | tf_op jit(solution)/shard_map/ppermute | solution.py:367
  59.8 3.6 %collective-permute-done.24.refs_1_ = bf16[160,640]{1,0:T(8,128)(2,1)S(1)} collective-permute-done((bf16[160,640]{1,0:T(8,128)(2,1)S(1)}, bf16[160,640]{1,0:T(8,128)(2,1)S(1)}, u32[]{:S(2)}, u32[]{:S(2)}) %collective-permute-start.24) | collective-permute-done | bytes 204832 | tf_op jit(solution)/shard_map/ppermute | solution.py:367
  63.5 1.6 %collective-permute-done.25.refs_2_ = bf16[160,640]{1,0:T(8,128)(2,1)S(1)} collective-permute-done((bf16[160,640]{1,0:T(8,128)(2,1)S(1)}, bf16[160,640]{1,0:T(8,128)(2,1)S(1)}, u32[]{:S(2)}, u32[]{:S(2)}) %collective-permute-start.25) | collective-permute-done | bytes 204832 | tf_op jit(solution)/shard_map/ppermute | solution.py:367
  65.2 2.2 %collective-permute-done.22.refs_1_ = bf16[160,640]{1,0:T(8,128)(2,1)S(1)} collective-permute-done((bf16[160,640]{1,0:T(8,128)(2,1)S(1)}, bf16[160,640]{1,0:T(8,128)(2,1)S(1)}, u32[]{:S(2)}, u32[]{:S(2)}) %collective-permute-start.22) | collective-permute-done | bytes 204832 | tf_op jit(solution)/shard_map/ppermute | solution.py:367
  73.2 2.7 %collective-permute-done.27.refs_3_.refs_1_ = bf16[160,640]{1,0:T(8,128)(2,1)S(1)} collective-permute-done((bf16[160,640]{1,0:T(8,128)(2,1)S(1)}, bf16[160,640]{1,0:T(8,128)(2,1)S(1)}, u32[]{:S(2)}, u32[]{:S(2)}) %collective-permute-start.27) | collective-permute-done | bytes 204832 | tf_op jit(solution)/shard_map/ppermute | solution.py:367
  77.3 2.3 %collective-permute-done.30.refs_1_ = bf16[160,640]{1,0:T(8,128)(2,1)S(1)} collective-permute-done((bf16[160,640]{1,0:T(8,128)(2,1)S(1)}, bf16[160,640]{1,0:T(8,128)(2,1)S(1)}, u32[]{:S(2)}, u32[]{:S(2)}) %collective-permute-start.30) | collective-permute-done | bytes 204832 | tf_op jit(solution)/shard_map/ppermute | solution.py:367
  79.6 3.4 %collective-permute-done.31.refs_3_.refs_2_ = bf16[160,640]{1,0:T(8,128)(2,1)S(1)} collective-permute-done((bf16[160,640]{1,0:T(8,128)(2,1)S(1)}, bf16[160,640]{1,0:T(8,128)(2,1)S(1)}, u32[]{:S(2)}, u32[]{:S(2)}) %collective-permute-start.31) | collective-permute-done | bytes 204832 | tf_op jit(solution)/shard_map/ppermute | solution.py:367
  89.4 1.8 %collective-permute-done.34.refs_3_ = bf16[160,640]{1,0:T(8,128)(2,1)S(1)} collective-permute-done((bf16[160,640]{1,0:T(8,128)(2,1)S(1)}, bf16[160,640]{1,0:T(8,128)(2,1)S(1)}, u32[]{:S(2)}, u32[]{:S(2)}) %collective-permute-start.34) | collective-permute-done | bytes 204832 | tf_op jit(solution)/shard_map/ppermute | solution.py:400
  (78 shorter events, 32.7 us)
Async XLA Ops:
  4.1 37.4 %collective-permute-start.14 = (bf16[2,192,1280]{2,1,0:T(8,128)(2,1)}, bf16[2,192,1280]{2,1,0:T(8,128)(2,1)S(1)}, u32[]{:S(2)}, u32[]{:S(2)}) collective-permute-start(bf16[2,192,1280]{2,1,0:T(8,128)(2,1)} %get-tuple-element.43), channel_id=1, source_target_pairs={{0,16},{16,0},{1,17},{17,1},{2,18},{18,2},{3,19},{19,3},{4,20},{20... | collective-permute-start | bytes 2949128 | tf_op jit(solution)/shard_map/ppermute | solution.py:269
  7.1 8.2 %collective-permute-start = (bf16[160,640]{1,0:T(8,128)(2,1)}, bf16[160,640]{1,0:T(8,128)(2,1)S(1)}, u32[]{:S(2)}, u32[]{:S(2)}) collective-permute-start(bf16[160,640]{1,0:T(8,128)(2,1)} %get-tuple-element.38.refs_0_), channel_id=1, source_target_pairs={{0,4},{4,8},{8,12},{12,14},{14,10},{10,6},{6,2},{2,0},{1,5},{5,9},... | collective-permute-start | bytes 614408 | tf_op jit(solution)/shard_map/ppermute | solution.py:283
  8.7 8.2 %collective-permute-start.3 = (bf16[160,640]{1,0:T(8,128)(2,1)}, bf16[160,640]{1,0:T(8,128)(2,1)S(1)}, u32[]{:S(2)}, u32[]{:S(2)}) collective-permute-start(bf16[160,640]{1,0:T(8,128)(2,1)} %get-tuple-element.39.refs_1_), channel_id=1, source_target_pairs={{4,0},{8,4},{12,8},{14,12},{10,14},{6,10},{2,6},{0,2},{5,1},{9,5},... | collective-permute-start | bytes 614408 | tf_op jit(solution)/shard_map/ppermute | solution.py:284
  9.1 12.2 %collective-permute-start.1 = (bf16[160,640]{1,0:T(8,128)(2,1)}, bf16[160,640]{1,0:T(8,128)(2,1)S(1)}, u32[]{:S(2)}, u32[]{:S(2)}) collective-permute-start(bf16[160,640]{1,0:T(8,128)(2,1)} %get-tuple-element.38.refs_0_), channel_id=1, source_target_pairs={{4,0},{8,4},{12,8},{14,12},{10,14},{6,10},{2,6},{0,2},{5,1},{9,5},... | collective-permute-start | bytes 614408 | tf_op jit(solution)/shard_map/ppermute | solution.py:284
  10.6 11.1 %collective-permute-start.2 = (bf16[160,640]{1,0:T(8,128)(2,1)}, bf16[160,640]{1,0:T(8,128)(2,1)S(1)}, u32[]{:S(2)}, u32[]{:S(2)}) collective-permute-start(bf16[160,640]{1,0:T(8,128)(2,1)} %get-tuple-element.39.refs_1_), channel_id=1, source_target_pairs={{0,4},{4,8},{8,12},{12,14},{14,10},{10,6},{6,2},{2,0},{1,5},{5,9},... | collective-permute-start | bytes 614408 | tf_op jit(solution)/shard_map/ppermute | solution.py:283
  15.3 8.8 %collective-permute-start.4 = (bf16[160,640]{1,0:T(8,128)(2,1)S(1)}, bf16[160,640]{1,0:T(8,128)(2,1)S(1)}, u32[]{:S(2)}, u32[]{:S(2)}) collective-permute-start(bf16[160,640]{1,0:T(8,128)(2,1)S(1)} %shard_map.79.refs_2_), channel_id=1, source_target_pairs={{0,4},{4,8},{8,12},{12,14},{14,10},{10,6},{6,2},{2,0},{1,5},{5,9},... | collective-permute-start | bytes 614408 | tf_op jit(solution)/shard_map/ppermute | solution.py:283
  16.9 8.8 %collective-permute-start.7 = (bf16[160,640]{1,0:T(8,128)(2,1)S(1)}, bf16[160,640]{1,0:T(8,128)(2,1)S(1)}, u32[]{:S(2)}, u32[]{:S(2)}) collective-permute-start(bf16[160,640]{1,0:T(8,128)(2,1)S(1)} %collective-permute-done.3.refs_5_), channel_id=1, source_target_pairs={{4,0},{8,4},{12,8},{14,12},{10,14},{6,10},{2,6},{0,2},{5,1},{9,5},... | collective-permute-start | bytes 614408 | tf_op jit(solution)/shard_map/ppermute | solution.py:284
  21.3 8.8 %collective-permute-start.5 = (bf16[160,640]{1,0:T(8,128)(2,1)S(1)}, bf16[160,640]{1,0:T(8,128)(2,1)S(1)}, u32[]{:S(2)}, u32[]{:S(2)}) collective-permute-start(bf16[160,640]{1,0:T(8,128)(2,1)S(1)} %collective-permute-done.1.refs_3_), channel_id=1, source_target_pairs={{4,0},{8,4},{12,8},{14,12},{10,14},{6,10},{2,6},{0,2},{5,1},{9,5},... | collective-permute-start | bytes 614408 | tf_op jit(solution)/shard_map/ppermute | solution.py:284
  21.7 8.8 %collective-permute-start.6 = (bf16[160,640]{1,0:T(8,128)(2,1)S(1)}, bf16[160,640]{1,0:T(8,128)(2,1)S(1)}, u32[]{:S(2)}, u32[]{:S(2)}) collective-permute-start(bf16[160,640]{1,0:T(8,128)(2,1)S(1)} %collective-permute-done.2.refs_4_), channel_id=1, source_target_pairs={{0,4},{4,8},{8,12},{12,14},{14,10},{10,6},{6,2},{2,0},{1,5},{5,9},... | collective-permute-start | bytes 614408 | tf_op jit(solution)/shard_map/ppermute | solution.py:283
  24.1 9.2 %collective-permute-start.8 = (bf16[160,640]{1,0:T(8,128)(2,1)S(1)}, bf16[160,640]{1,0:T(8,128)(2,1)S(1)}, u32[]{:S(2)}, u32[]{:S(2)}) collective-permute-start(bf16[160,640]{1,0:T(8,128)(2,1)S(1)} %collective-permute-done.4.refs_6_), channel_id=1, source_target_pairs={{0,4},{4,8},{8,12},{12,14},{14,10},{10,6},{6,2},{2,0},{1,5},{5,9},... | collective-permute-start | bytes 614408 | tf_op jit(solution)/shard_map/ppermute | solution.py:283
  25.7 9.2 %collective-permute-start.9 = (bf16[160,640]{1,0:T(8,128)(2,1)S(1)}, bf16[160,640]{1,0:T(8,128)(2,1)S(1)}, u32[]{:S(2)}, u32[]{:S(2)}) collective-permute-start(bf16[160,640]{1,0:T(8,128)(2,1)S(1)} %collective-permute-done.7.refs_9_), channel_id=1, source_target_pairs={{4,0},{8,4},{12,8},{14,12},{10,14},{6,10},{2,6},{0,2},{5,1},{9,5},... | collective-permute-start | bytes 614408 | tf_op jit(solution)/shard_map/ppermute | solution.py:284
  30.1 8.8 %collective-permute-start.10 = (bf16[160,640]{1,0:T(8,128)(2,1)S(1)}, bf16[160,640]{1,0:T(8,128)(2,1)S(1)}, u32[]{:S(2)}, u32[]{:S(2)}) collective-permute-start(bf16[160,640]{1,0:T(8,128)(2,1)S(1)} %collective-permute-done.5.refs_7_), channel_id=1, source_target_pairs={{4,0},{8,4},{12,8},{14,12},{10,14},{6,10},{2,6},{0,2},{5,1},{9,5},... | collective-permute-start | bytes 614408 | tf_op jit(solution)/shard_map/ppermute | solution.py:284
  30.5 8.4 %collective-permute-start.11 = (bf16[160,640]{1,0:T(8,128)(2,1)S(1)}, bf16[160,640]{1,0:T(8,128)(2,1)S(1)}, u32[]{:S(2)}, u32[]{:S(2)}) collective-permute-start(bf16[160,640]{1,0:T(8,128)(2,1)S(1)} %collective-permute-done.6.refs_8_), channel_id=1, source_target_pairs={{0,4},{4,8},{8,12},{12,14},{14,10},{10,6},{6,2},{2,0},{1,5},{5,9},... | collective-permute-start | bytes 614408 | tf_op jit(solution)/shard_map/ppermute | solution.py:283
  44.4 7.6 %collective-permute-start.16 = (bf16[160,640]{1,0:T(8,128)(2,1)S(1)}, bf16[160,640]{1,0:T(8,128)(2,1)S(1)}, u32[]{:S(2)}, u32[]{:S(2)}) collective-permute-start(bf16[160,640]{1,0:T(8,128)(2,1)S(1)} %get-tuple-element.48), channel_id=1, source_target_pairs={{0,4},{4,8},{8,12},{12,14},{14,10},{10,6},{6,2},{2,0},{1,5},{5,9},... | collective-permute-start | bytes 614408 | tf_op jit(solution)/shard_map/ppermute | solution.py:367
  49.2 8.4 %collective-permute-start.20 = (bf16[160,640]{1,0:T(8,128)(2,1)S(1)}, bf16[160,640]{1,0:T(8,128)(2,1)S(1)}, u32[]{:S(2)}, u32[]{:S(2)}) collective-permute-start(bf16[160,640]{1,0:T(8,128)(2,1)S(1)} %get-tuple-element.55), channel_id=1, source_target_pairs={{0,4},{4,8},{8,12},{12,14},{14,10},{10,6},{6,2},{2,0},{1,5},{5,9},... | collective-permute-start | bytes 614408 | tf_op jit(solution)/shard_map/ppermute | solution.py:367
  55.5 15.5 %collective-permute-start.19 = (bf16[384,640]{1,0:T(8,128)(2,1)S(1)}, bf16[384,640]{1,0:T(8,128)(2,1)S(1)}, u32[]{:S(2)}, u32[]{:S(2)}) collective-permute-start(bf16[384,640]{1,0:T(8,128)(2,1)S(1)} %get-tuple-element.54), channel_id=1, source_target_pairs={{0,1},{1,0},{2,3},{3,2},{4,5},{5,4},{6,7},{7,6},{8,9},{9,8},{10,11... | collective-permute-start | bytes 1474568 | tf_op jit(solution)/shard_map/ppermute | solution.py:336
  55.6 7.9 %collective-permute-start.24 = (bf16[160,640]{1,0:T(8,128)(2,1)S(1)}, bf16[160,640]{1,0:T(8,128)(2,1)S(1)}, u32[]{:S(2)}, u32[]{:S(2)}) collective-permute-start(bf16[160,640]{1,0:T(8,128)(2,1)S(1)} %get-tuple-element.51.refs_3_), channel_id=1, source_target_pairs={{0,4},{4,8},{8,12},{12,14},{14,10},{10,6},{6,2},{2,0},{1,5},{5,9},... | collective-permute-start | bytes 614408 | tf_op jit(solution)/shard_map/ppermute | solution.py:367
  57.2 7.9 %collective-permute-start.25 = (bf16[160,640]{1,0:T(8,128)(2,1)S(1)}, bf16[160,640]{1,0:T(8,128)(2,1)S(1)}, u32[]{:S(2)}, u32[]{:S(2)}) collective-permute-start(bf16[160,640]{1,0:T(8,128)(2,1)S(1)} %get-tuple-element.59), channel_id=1, source_target_pairs={{4,0},{8,4},{12,8},{14,12},{10,14},{6,10},{2,6},{0,2},{5,1},{9,5},... | collective-permute-start | bytes 614408 | tf_op jit(solution)/shard_map/ppermute | solution.py:367
  57.8 9.7 %collective-permute-start.22 = (bf16[160,640]{1,0:T(8,128)(2,1)S(1)}, bf16[160,640]{1,0:T(8,128)(2,1)S(1)}, u32[]{:S(2)}, u32[]{:S(2)}) collective-permute-start(bf16[160,640]{1,0:T(8,128)(2,1)S(1)} %get-tuple-element.57.refs_3_), channel_id=1, source_target_pairs={{0,4},{4,8},{8,12},{12,14},{14,10},{10,6},{6,2},{2,0},{1,5},{5,9},... | collective-permute-start | bytes 614408 | tf_op jit(solution)/shard_map/ppermute | solution.py:367
  59.4 9.3 %collective-permute-start.23 = (bf16[160,640]{1,0:T(8,128)(2,1)S(1)}, bf16[160,640]{1,0:T(8,128)(2,1)S(1)}, u32[]{:S(2)}, u32[]{:S(2)}) collective-permute-start(bf16[160,640]{1,0:T(8,128)(2,1)S(1)} %get-tuple-element.58), channel_id=1, source_target_pairs={{4,0},{8,4},{12,8},{14,12},{10,14},{6,10},{2,6},{0,2},{5,1},{9,5},... | collective-permute-start | bytes 614408 | tf_op jit(solution)/shard_map/ppermute | solution.py:367
  70.9 15.2 %collective-permute-start.18 = (bf16[384,640]{1,0:T(8,128)(2,1)S(1)}, bf16[384,640]{1,0:T(8,128)(2,1)S(1)}, u32[]{:S(2)}, u32[]{:S(2)}) collective-permute-start(bf16[384,640]{1,0:T(8,128)(2,1)S(1)} %get-tuple-element.53), channel_id=1, source_target_pairs={{0,1},{1,0},{2,3},{3,2},{4,5},{5,4},{6,7},{7,6},{8,9},{9,8},{10,11... | collective-permute-start | bytes 1474568 | tf_op jit(solution)/shard_map/ppermute | solution.py:393
  71.1 15.1 %collective-permute-start.26 = (bf16[384,640]{1,0:T(8,128)(2,1)S(1)}, bf16[384,640]{1,0:T(8,128)(2,1)S(1)}, u32[]{:S(2)}, u32[]{:S(2)}) collective-permute-start(bf16[384,640]{1,0:T(8,128)(2,1)S(1)} %shard_map.89.refs_2_), channel_id=1, source_target_pairs={{0,16},{16,0},{1,17},{17,1},{2,18},{18,2},{3,19},{19,3},{4,20},{20... | collective-permute-start | bytes 1474568 | tf_op jit(solution)/shard_map/ppermute | solution.py:340
  71.6 8.0 %collective-permute-start.30 = (bf16[160,640]{1,0:T(8,128)(2,1)S(1)}, bf16[160,640]{1,0:T(8,128)(2,1)S(1)}, u32[]{:S(2)}, u32[]{:S(2)}) collective-permute-start(bf16[160,640]{1,0:T(8,128)(2,1)S(1)} %get-tuple-element.60.refs_3_), channel_id=1, source_target_pairs={{0,4},{4,8},{8,12},{12,14},{14,10},{10,6},{6,2},{2,0},{1,5},{5,9},... | collective-permute-start | bytes 614408 | tf_op jit(solution)/shard_map/ppermute | solution.py:367
  76.7 8.5 %collective-permute-start.29 = (bf16[160,640]{1,0:T(8,128)(2,1)S(1)}, bf16[160,640]{1,0:T(8,128)(2,1)S(1)}, u32[]{:S(2)}, u32[]{:S(2)}) collective-permute-start(bf16[160,640]{1,0:T(8,128)(2,1)S(1)} %shard_map.90.refs_2_), channel_id=1, source_target_pairs={{4,0},{8,4},{12,8},{14,12},{10,14},{6,10},{2,6},{0,2},{5,1},{9,5},... | collective-permute-start | bytes 614408 | tf_op jit(solution)/shard_map/ppermute | solution.py:367
  (17 other events, 161.9 us)

commit v19 on v17

--- a/solution.py
+++ b/solution.py
@@ -360,7 +360,7 @@
 
     up_grad_of = shape((depth, hidden), F32)
     if ringed:
-        came = [{}, {}]
+        came, kept = [{}, {}], []
 
         def send_on(i, blocks, names):
             for block, name in zip(blocks, names):
@@ -377,6 +377,9 @@
                 [block_of] * len(ways),
                 ties=ties,
             )
+            if (i, turn) == (0, half - 2):
+                kept.append(blocks[1])
+                blocks, names = blocks[:1], names[:1]
             send_on(i, blocks, names)
             return blocks[0]
 
@@ -398,6 +401,7 @@
             ties=(tie,),
         )
         passed = lax.ppermute(passing, "groups", swap)
+        send_on(0, [hold(kept[0], passing)], ["down"])
         input_grad, token = input_gradient(*scale(keep, sent, back, passing))
         up_grad = call(
             functools.partial(join_kernel, peers),

time: 91.1 us -> 90.5 us (level)
    ppermute x1, waiting for transfers between devices: 0.01 us -> 3.94 us  [over_cores(): return (over, lax.ppermute(over, 'groups', swap))]
    ppermute x14, waiting for transfers between devices: 19.3 us -> 16.1 us  [send_on(): came[i][name] = lax.ppermute(block, 'gx', ahead if name == 'up' else behind)]
    ppermute x1, starting transfers between devices: 1.56 us -> 0.38 us  [shards(): passed = lax.ppermute(passing, 'groups', swap)]
    ppermute x1, waiting for transfers between devices: 1.01 us -> 0.01 us  [shards(): passed = lax.ppermute(passing, 'groups', swap)]
  transfers between devices with their start and end apart: 35 -> 35, of which waited for: 21 -> 20; matrix products, arithmetic and copies ran while one was open for 0% -> 0% of each run, Pallas kernels for 17% -> 17%
where the time goes in v19:
time: 90.5 us; the launch traced here: 90.3 us
  waiting for transfers between devices  36.5 us (40%)
  starting transfers between devices  33.3 us (37%)
  Pallas kernels  19.7 us (22%)
    pallas_call x17, Pallas kernels, call(): pl.pallas_call(body if ties else kernel, out_shape=out_shape, in_specs=[S...  19.7 us
    ppermute x14, waiting for transfers between devices, send_on(): came[i][name] = lax.ppermute(block, 'gx', ahead if name == 'up' else behind)  16.1 us
    ppermute x14, starting transfers between devices, send_on(): came[i][name] = lax.ppermute(block, 'gx', ahead if name == 'up' else behind)  15 us
    ppermute x6, starting transfers between devices, shards(): up[i] = lax.ppermute(up[i], 'gx', ahead)  8.39 us
    ppermute x6, waiting for transfers between devices, shards(): down[i] = lax.ppermute(down[i], 'gx', behind)  7.92 us
    ppermute x6, waiting for transfers between devices, shards(): up[i] = lax.ppermute(up[i], 'gx', ahead)  4.61 us
    ppermute x1, waiting for transfers between devices, over_cores(): return (over, lax.ppermute(over, 'groups', swap))  3.94 us
    ppermute x6, starting transfers between devices, shards(): down[i] = lax.ppermute(down[i], 'gx', behind)  3.77 us
  transfers between devices with their start and end apart: 35, of which 20 were waited for; matrix products, arithmetic and copies ran while one was open for 0% of the time, Pallas kernels for 17%

profile of v19, /device:TPU:0, one launch (start us, length us, event | category | flops | bytes accessed | tf_op | source)
XLA Modules:
  0.0 90.3 jit_solution(2807976712128215505)
XLA Ops:
  0.7 3.4 %shard_map.78 = (bf16[2,192,1280]{2,1,0:T(8,128)(2,1)}, bf16[160,640]{1,0:T(8,128)(2,1)}, bf16[160,640]{1,0:T(8,128)(2,1)}) custom-call(s32[8]{0:T(128)} %lengths.3, bf16[384,1280]{1,0:T(8,128)(2,1)} %bitcast.3, bf16[384,1280]{1,0:T(8,128)(2,1)} %bitcast.6, f32[1280]{0:T(1024)} %gain.3, bf16[160,1280]{1,0:T(8,128)(2,1)} %w_up.1, bf16[160,1280]{1,0:T(8,128)(2,1)} %w_down.1), custom_call_target="tpu_custom_call" | custom-call | flops 2457600 | bytes 4183072 | tf_op jit(solution)/shard_map/pallas_call | solution.py:28
  4.1 3.0 %collective-permute-start.14 = (bf16[2,192,1280]{2,1,0:T(8,128)(2,1)}, bf16[2,192,1280]{2,1,0:T(8,128)(2,1)S(1)}, u32[]{:S(2)}, u32[]{:S(2)}) collective-permute-start(bf16[2,192,1280]{2,1,0:T(8,128)(2,1)} %get-tuple-element.43), channel_id=1, source_target_pairs={{0,16},{16,0},{1,17},{17,1},{2,18},{18,2},{3,19},{19,3},{4,20},{20... | collective-permute-start | bytes 2949128 | tf_op jit(solution)/shard_map/ppermute | solution.py:269
  7.1 1.6 %collective-permute-start = (bf16[160,640]{1,0:T(8,128)(2,1)}, bf16[160,640]{1,0:T(8,128)(2,1)S(1)}, u32[]{:S(2)}, u32[]{:S(2)}) collective-permute-start(bf16[160,640]{1,0:T(8,128)(2,1)} %get-tuple-element.38.refs_0_), channel_id=1, source_target_pairs={{0,4},{4,8},{8,12},{12,14},{14,10},{10,6},{6,2},{2,0},{1,5},{5,9},... | collective-permute-start | bytes 614408 | tf_op jit(solution)/shard_map/ppermute | solution.py:283
  12.6 2.6 %collective-permute-done.refs_0_ = bf16[160,640]{1,0:T(8,128)(2,1)S(1)} collective-permute-done((bf16[160,640]{1,0:T(8,128)(2,1)}, bf16[160,640]{1,0:T(8,128)(2,1)S(1)}, u32[]{:S(2)}, u32[]{:S(2)}) %collective-permute-start) | collective-permute-done | bytes 204832 | tf_op jit(solution)/shard_map/ppermute | solution.py:283
  15.3 1.6 %collective-permute-start.4 = (bf16[160,640]{1,0:T(8,128)(2,1)S(1)}, bf16[160,640]{1,0:T(8,128)(2,1)S(1)}, u32[]{:S(2)}, u32[]{:S(2)}) collective-permute-start(bf16[160,640]{1,0:T(8,128)(2,1)S(1)} %shard_map.79.refs_2_), channel_id=1, source_target_pairs={{0,4},{4,8},{8,12},{12,14},{14,10},{10,6},{6,2},{2,0},{1,5},{5,9},... | collective-permute-start | bytes 614408 | tf_op jit(solution)/shard_map/ppermute | solution.py:283
  17.3 3.9 %collective-permute-done.1.refs_3_ = bf16[160,640]{1,0:T(8,128)(2,1)S(1)} collective-permute-done((bf16[160,640]{1,0:T(8,128)(2,1)}, bf16[160,640]{1,0:T(8,128)(2,1)S(1)}, u32[]{:S(2)}, u32[]{:S(2)}) %collective-permute-start.1) | collective-permute-done | bytes 204832 | tf_op jit(solution)/shard_map/ppermute | solution.py:284
  21.7 1.6 %collective-permute-start.6 = (bf16[160,640]{1,0:T(8,128)(2,1)S(1)}, bf16[160,640]{1,0:T(8,128)(2,1)S(1)}, u32[]{:S(2)}, u32[]{:S(2)}) collective-permute-start(bf16[160,640]{1,0:T(8,128)(2,1)S(1)} %collective-permute-done.2.refs_4_), channel_id=1, source_target_pairs={{0,4},{4,8},{8,12},{12,14},{14,10},{10,6},{6,2},{2,0},{1,5},{5,9},... | collective-permute-start | bytes 614408 | tf_op jit(solution)/shard_map/ppermute | solution.py:283
  24.1 1.6 %collective-permute-start.8 = (bf16[160,640]{1,0:T(8,128)(2,1)S(1)}, bf16[160,640]{1,0:T(8,128)(2,1)S(1)}, u32[]{:S(2)}, u32[]{:S(2)}) collective-permute-start(bf16[160,640]{1,0:T(8,128)(2,1)S(1)} %collective-permute-done.4.refs_6_), channel_id=1, source_target_pairs={{0,4},{4,8},{8,12},{12,14},{14,10},{10,6},{6,2},{2,0},{1,5},{5,9},... | collective-permute-start | bytes 614408 | tf_op jit(solution)/shard_map/ppermute | solution.py:283
  26.1 3.9 %collective-permute-done.5.refs_7_ = bf16[160,640]{1,0:T(8,128)(2,1)S(1)} collective-permute-done((bf16[160,640]{1,0:T(8,128)(2,1)S(1)}, bf16[160,640]{1,0:T(8,128)(2,1)S(1)}, u32[]{:S(2)}, u32[]{:S(2)}) %collective-permute-start.5) | collective-permute-done | bytes 204832 | tf_op jit(solution)/shard_map/ppermute | solution.py:284
  30.5 1.6 %collective-permute-start.11 = (bf16[160,640]{1,0:T(8,128)(2,1)S(1)}, bf16[160,640]{1,0:T(8,128)(2,1)S(1)}, u32[]{:S(2)}, u32[]{:S(2)}) collective-permute-start(bf16[160,640]{1,0:T(8,128)(2,1)S(1)} %collective-permute-done.6.refs_8_), channel_id=1, source_target_pairs={{0,4},{4,8},{8,12},{12,14},{14,10},{10,6},{6,2},{2,0},{1,5},{5,9},... | collective-permute-start | bytes 614408 | tf_op jit(solution)/shard_map/ppermute | solution.py:283
  33.3 1.6 %collective-permute-start.12 = (bf16[160,640]{1,0:T(8,128)(2,1)S(1)}, bf16[160,640]{1,0:T(8,128)(2,1)S(1)}, u32[]{:S(2)}, u32[]{:S(2)}) collective-permute-start(bf16[160,640]{1,0:T(8,128)(2,1)S(1)} %collective-permute-done.8.refs_10_), channel_id=1, source_target_pairs={{0,4},{4,8},{8,12},{12,14},{14,10},{10,6},{6,2},{2,0},{1,5},{5,9},... | collective-permute-start | bytes 614408 | tf_op jit(solution)/shard_map/ppermute | solution.py:292
  35.3 3.6 %shard_map.80 = (bf16[1280,640]{1,0:T(8,128)(2,1)S(1)}, bf16[1280,640]{1,0:T(8,128)(2,1)S(1)}) custom-call(bf16[160,640]{1,0:T(8,128)(2,1)S(1)} %copy-done.2, bf16[160,640]{1,0:T(8,128)(2,1)S(1)} %copy-done.3, bf16[160,640]{1,0:T(8,128)(2,1)S(1)} %shard_map.79.refs_2_, bf16[160,640]{1,0:T(8,128)(2,1)S(1)} %collective-permute-done.1.refs_3_, ...), custom_call_target="tpu_custom_call" | custom-call | flops 1 | bytes 5734400 | tf_op jit(solution)/shard_map/pallas_call | solution.py:28
  41.5 2.9 %shard_map.81 = (bf16[384,640]{1,0:T(8,128)(2,1)S(1)}, bf16[1280,640]{1,0:T(8,128)(2,1)S(1)}, bf16[1280,640]{1,0:T(8,128)(2,1)S(1)}, bf16[1280,640]{1,0:T(8,128)...) custom-call(bf16[384,1280]{1,0:T(8,128)(2,1)S(1)} %get-tuple-element.36.refs_1_.normed, ...), custom_call_target="tpu_custom_call" | custom-call | flops 1887436800 | bytes 11878400 | tf_op jit(solution)/shard_map/pallas_call | solution.py:28
  44.4 1.6 %collective-permute-start.16 = (bf16[160,640]{1,0:T(8,128)(2,1)S(1)}, bf16[160,640]{1,0:T(8,128)(2,1)S(1)}, u32[]{:S(2)}, u32[]{:S(2)}) collective-permute-start(bf16[160,640]{1,0:T(8,128)(2,1)S(1)} %get-tuple-element.47), channel_id=1, source_target_pairs={{0,4},{4,8},{8,12},{12,14},{14,10},{10,6},{6,2},{2,0},{1,5},{5,9},... | collective-permute-start | bytes 614408 | tf_op jit(solution)/shard_map/ppermute | solution.py:367
  46.5 2.7 %shard_map.83 = (bf16[384,640]{1,0:T(8,128)(2,1)S(1)}, bf16[1280,640]{1,0:T(8,128)(2,1)S(1)}, bf16[160,640]{1,0:T(8,128)(2,1)S(1)}, bf16[160,640]{1,0:T(8,128)(2,1)S(1)}) custom-call(bf16[2,192,1280]{2,1,0:T(8,128)(2,1)S(1)} %shard_map.82.first, bf16[2,192,1280]{2,1,0:T(8,128)(2,1)S(1)} %collective-permute-done.15.second, ...), custom_call_target="tpu_custom_call" | custom-call | flops 1887436800 | bytes 7782400 | tf_op jit(solution)/shard_map/pallas_call | solution.py:28
  49.2 1.6 %collective-permute-start.20 = (bf16[160,640]{1,0:T(8,128)(2,1)S(1)}, bf16[160,640]{1,0:T(8,128)(2,1)S(1)}, u32[]{:S(2)}, u32[]{:S(2)}) collective-permute-start(bf16[160,640]{1,0:T(8,128)(2,1)S(1)} %get-tuple-element.54), channel_id=1, source_target_pairs={{0,4},{4,8},{8,12},{12,14},{14,10},{10,6},{6,2},{2,0},{1,5},{5,9},... | collective-permute-start | bytes 614408 | tf_op jit(solution)/shard_map/ppermute | solution.py:367
  53.3 2.0 %shard_map.84 = (bf16[2,384,640]{2,1,0:T(8,128)(2,1)S(1)}, bf16[384,640]{1,0:T(8,128)(2,1)S(1)}, bf16[384,640]{1,0:T(8,128)(2,1)S(1)}) custom-call(bf16[384,640]{1,0:T(8,128)(2,1)S(1)} %get-tuple-element.42.refs_0_, bf16[384,640]{1,0:T(8,128)(2,1)S(1)} %get-tuple-element.46.refs_1_, bf16[1280,640]{1,0:T(8,128)(2,1)S(1)} %get-tuple-element.44.up.refs_2_, ...), custom_call_target="tpu_custom_call" | custom-call | flops 1258291200 | bytes 4587520 | tf_op jit(solution)/shard_map/pallas_call | solution.py:28
  57.8 1.6 %collective-permute-start.24 = (bf16[160,640]{1,0:T(8,128)(2,1)S(1)}, bf16[160,640]{1,0:T(8,128)(2,1)S(1)}, u32[]{:S(2)}, u32[]{:S(2)}) collective-permute-start(bf16[160,640]{1,0:T(8,128)(2,1)S(1)} %get-tuple-element.56.refs_3_), channel_id=1, source_target_pairs={{0,4},{4,8},{8,12},{12,14},{14,10},{10,6},{6,2},{2,0},{1,5},{5,9},... | collective-permute-start | bytes 614408 | tf_op jit(solution)/shard_map/ppermute | solution.py:367
  60.0 1.6 %collective-permute-start.22 = (bf16[160,640]{1,0:T(8,128)(2,1)S(1)}, bf16[160,640]{1,0:T(8,128)(2,1)S(1)}, u32[]{:S(2)}, u32[]{:S(2)}) collective-permute-start(bf16[160,640]{1,0:T(8,128)(2,1)S(1)} %get-tuple-element.57.refs_3_), channel_id=1, source_target_pairs={{0,4},{4,8},{8,12},{12,14},{14,10},{10,6},{6,2},{2,0},{1,5},{5,9},... | collective-permute-start | bytes 614408 | tf_op jit(solution)/shard_map/ppermute | solution.py:367
  62.0 3.8 %collective-permute-done.24.refs_1_ = bf16[160,640]{1,0:T(8,128)(2,1)S(1)} collective-permute-done((bf16[160,640]{1,0:T(8,128)(2,1)S(1)}, bf16[160,640]{1,0:T(8,128)(2,1)S(1)}, u32[]{:S(2)}, u32[]{:S(2)}) %collective-permute-start.24) | collective-permute-done | bytes 204832 | tf_op jit(solution)/shard_map/ppermute | solution.py:367
  67.5 1.6 %collective-permute-start.27 = (bf16[160,640]{1,0:T(8,128)(2,1)S(1)}, bf16[160,640]{1,0:T(8,128)(2,1)S(1)}, u32[]{:S(2)}, u32[]{:S(2)}) collective-permute-start(bf16[160,640]{1,0:T(8,128)(2,1)S(1)} %get-tuple-element.60.refs_3_), channel_id=1, source_target_pairs={{0,4},{4,8},{8,12},{12,14},{14,10},{10,6},{6,2},{2,0},{1,5},{5,9},... | collective-permute-start | bytes 614408 | tf_op jit(solution)/shard_map/ppermute | solution.py:367
  75.5 2.8 %collective-permute-done.30.refs_1_ = bf16[160,640]{1,0:T(8,128)(2,1)S(1)} collective-permute-done((bf16[160,640]{1,0:T(8,128)(2,1)S(1)}, bf16[160,640]{1,0:T(8,128)(2,1)S(1)}, u32[]{:S(2)}, u32[]{:S(2)}) %collective-permute-start.30) | collective-permute-done | bytes 204832 | tf_op jit(solution)/shard_map/ppermute | solution.py:367
  78.4 1.6 %collective-permute-start.32 = (bf16[160,640]{1,0:T(8,128)(2,1)S(1)}, bf16[160,640]{1,0:T(8,128)(2,1)S(1)}, u32[]{:S(2)}, u32[]{:S(2)}) collective-permute-start(bf16[160,640]{1,0:T(8,128)(2,1)S(1)} %shard_map.91.refs_3_), channel_id=1, source_target_pairs={{0,4},{4,8},{8,12},{12,14},{14,10},{10,6},{6,2},{2,0},{1,5},{5,9},... | collective-permute-start | bytes 614408 | tf_op jit(solution)/shard_map/ppermute | solution.py:367
  82.1 3.9 %collective-permute-done.26.refs_2_ = bf16[384,640]{1,0:T(8,128)(2,1)S(1)} collective-permute-done((bf16[384,640]{1,0:T(8,128)(2,1)S(1)}, bf16[384,640]{1,0:T(8,128)(2,1)S(1)}, u32[]{:S(2)}, u32[]{:S(2)}) %collective-permute-start.26) | collective-permute-done | bytes 491552 | tf_op jit(solution)/shard_map/ppermute | solution.py:340
  (79 shorter events, 31.7 us)
Async XLA Ops:
  4.1 37.4 %collective-permute-start.14 = (bf16[2,192,1280]{2,1,0:T(8,128)(2,1)}, bf16[2,192,1280]{2,1,0:T(8,128)(2,1)S(1)}, u32[]{:S(2)}, u32[]{:S(2)}) collective-permute-start(bf16[2,192,1280]{2,1,0:T(8,128)(2,1)} %get-tuple-element.43), channel_id=1, source_target_pairs={{0,16},{16,0},{1,17},{17,1},{2,18},{18,2},{3,19},{19,3},{4,20},{20... | collective-permute-start | bytes 2949128 | tf_op jit(solution)/shard_map/ppermute | solution.py:269
  7.1 8.2 %collective-permute-start = (bf16[160,640]{1,0:T(8,128)(2,1)}, bf16[160,640]{1,0:T(8,128)(2,1)S(1)}, u32[]{:S(2)}, u32[]{:S(2)}) collective-permute-start(bf16[160,640]{1,0:T(8,128)(2,1)} %get-tuple-element.38.refs_0_), channel_id=1, source_target_pairs={{0,4},{4,8},{8,12},{12,14},{14,10},{10,6},{6,2},{2,0},{1,5},{5,9},... | collective-permute-start | bytes 614408 | tf_op jit(solution)/shard_map/ppermute | solution.py:283
  8.7 8.2 %collective-permute-start.3 = (bf16[160,640]{1,0:T(8,128)(2,1)}, bf16[160,640]{1,0:T(8,128)(2,1)S(1)}, u32[]{:S(2)}, u32[]{:S(2)}) collective-permute-start(bf16[160,640]{1,0:T(8,128)(2,1)} %get-tuple-element.39.refs_1_), channel_id=1, source_target_pairs={{4,0},{8,4},{12,8},{14,12},{10,14},{6,10},{2,6},{0,2},{5,1},{9,5},... | collective-permute-start | bytes 614408 | tf_op jit(solution)/shard_map/ppermute | solution.py:284
  9.1 12.2 %collective-permute-start.1 = (bf16[160,640]{1,0:T(8,128)(2,1)}, bf16[160,640]{1,0:T(8,128)(2,1)S(1)}, u32[]{:S(2)}, u32[]{:S(2)}) collective-permute-start(bf16[160,640]{1,0:T(8,128)(2,1)} %get-tuple-element.38.refs_0_), channel_id=1, source_target_pairs={{4,0},{8,4},{12,8},{14,12},{10,14},{6,10},{2,6},{0,2},{5,1},{9,5},... | collective-permute-start | bytes 614408 | tf_op jit(solution)/shard_map/ppermute | solution.py:284
  10.6 11.1 %collective-permute-start.2 = (bf16[160,640]{1,0:T(8,128)(2,1)}, bf16[160,640]{1,0:T(8,128)(2,1)S(1)}, u32[]{:S(2)}, u32[]{:S(2)}) collective-permute-start(bf16[160,640]{1,0:T(8,128)(2,1)} %get-tuple-element.39.refs_1_), channel_id=1, source_target_pairs={{0,4},{4,8},{8,12},{12,14},{14,10},{10,6},{6,2},{2,0},{1,5},{5,9},... | collective-permute-start | bytes 614408 | tf_op jit(solution)/shard_map/ppermute | solution.py:283
  15.3 8.8 %collective-permute-start.4 = (bf16[160,640]{1,0:T(8,128)(2,1)S(1)}, bf16[160,640]{1,0:T(8,128)(2,1)S(1)}, u32[]{:S(2)}, u32[]{:S(2)}) collective-permute-start(bf16[160,640]{1,0:T(8,128)(2,1)S(1)} %shard_map.79.refs_2_), channel_id=1, source_target_pairs={{0,4},{4,8},{8,12},{12,14},{14,10},{10,6},{6,2},{2,0},{1,5},{5,9},... | collective-permute-start | bytes 614408 | tf_op jit(solution)/shard_map/ppermute | solution.py:283
  16.9 8.8 %collective-permute-start.7 = (bf16[160,640]{1,0:T(8,128)(2,1)S(1)}, bf16[160,640]{1,0:T(8,128)(2,1)S(1)}, u32[]{:S(2)}, u32[]{:S(2)}) collective-permute-start(bf16[160,640]{1,0:T(8,128)(2,1)S(1)} %collective-permute-done.3.refs_5_), channel_id=1, source_target_pairs={{4,0},{8,4},{12,8},{14,12},{10,14},{6,10},{2,6},{0,2},{5,1},{9,5},... | collective-permute-start | bytes 614408 | tf_op jit(solution)/shard_map/ppermute | solution.py:284
  21.3 8.8 %collective-permute-start.5 = (bf16[160,640]{1,0:T(8,128)(2,1)S(1)}, bf16[160,640]{1,0:T(8,128)(2,1)S(1)}, u32[]{:S(2)}, u32[]{:S(2)}) collective-permute-start(bf16[160,640]{1,0:T(8,128)(2,1)S(1)} %collective-permute-done.1.refs_3_), channel_id=1, source_target_pairs={{4,0},{8,4},{12,8},{14,12},{10,14},{6,10},{2,6},{0,2},{5,1},{9,5},... | collective-permute-start | bytes 614408 | tf_op jit(solution)/shard_map/ppermute | solution.py:284
  21.7 8.8 %collective-permute-start.6 = (bf16[160,640]{1,0:T(8,128)(2,1)S(1)}, bf16[160,640]{1,0:T(8,128)(2,1)S(1)}, u32[]{:S(2)}, u32[]{:S(2)}) collective-permute-start(bf16[160,640]{1,0:T(8,128)(2,1)S(1)} %collective-permute-done.2.refs_4_), channel_id=1, source_target_pairs={{0,4},{4,8},{8,12},{12,14},{14,10},{10,6},{6,2},{2,0},{1,5},{5,9},... | collective-permute-start | bytes 614408 | tf_op jit(solution)/shard_map/ppermute | solution.py:283
  24.1 9.2 %collective-permute-start.8 = (bf16[160,640]{1,0:T(8,128)(2,1)S(1)}, bf16[160,640]{1,0:T(8,128)(2,1)S(1)}, u32[]{:S(2)}, u32[]{:S(2)}) collective-permute-start(bf16[160,640]{1,0:T(8,128)(2,1)S(1)} %collective-permute-done.4.refs_6_), channel_id=1, source_target_pairs={{0,4},{4,8},{8,12},{12,14},{14,10},{10,6},{6,2},{2,0},{1,5},{5,9},... | collective-permute-start | bytes 614408 | tf_op jit(solution)/shard_map/ppermute | solution.py:283
  25.7 9.2 %collective-permute-start.9 = (bf16[160,640]{1,0:T(8,128)(2,1)S(1)}, bf16[160,640]{1,0:T(8,128)(2,1)S(1)}, u32[]{:S(2)}, u32[]{:S(2)}) collective-permute-start(bf16[160,640]{1,0:T(8,128)(2,1)S(1)} %collective-permute-done.7.refs_9_), channel_id=1, source_target_pairs={{4,0},{8,4},{12,8},{14,12},{10,14},{6,10},{2,6},{0,2},{5,1},{9,5},... | collective-permute-start | bytes 614408 | tf_op jit(solution)/shard_map/ppermute | solution.py:284
  30.1 8.8 %collective-permute-start.10 = (bf16[160,640]{1,0:T(8,128)(2,1)S(1)}, bf16[160,640]{1,0:T(8,128)(2,1)S(1)}, u32[]{:S(2)}, u32[]{:S(2)}) collective-permute-start(bf16[160,640]{1,0:T(8,128)(2,1)S(1)} %collective-permute-done.5.refs_7_), channel_id=1, source_target_pairs={{4,0},{8,4},{12,8},{14,12},{10,14},{6,10},{2,6},{0,2},{5,1},{9,5},... | collective-permute-start | bytes 614408 | tf_op jit(solution)/shard_map/ppermute | solution.py:284
  30.5 8.4 %collective-permute-start.11 = (bf16[160,640]{1,0:T(8,128)(2,1)S(1)}, bf16[160,640]{1,0:T(8,128)(2,1)S(1)}, u32[]{:S(2)}, u32[]{:S(2)}) collective-permute-start(bf16[160,640]{1,0:T(8,128)(2,1)S(1)} %collective-permute-done.6.refs_8_), channel_id=1, source_target_pairs={{0,4},{4,8},{8,12},{12,14},{14,10},{10,6},{6,2},{2,0},{1,5},{5,9},... | collective-permute-start | bytes 614408 | tf_op jit(solution)/shard_map/ppermute | solution.py:283
  44.4 7.6 %collective-permute-start.16 = (bf16[160,640]{1,0:T(8,128)(2,1)S(1)}, bf16[160,640]{1,0:T(8,128)(2,1)S(1)}, u32[]{:S(2)}, u32[]{:S(2)}) collective-permute-start(bf16[160,640]{1,0:T(8,128)(2,1)S(1)} %get-tuple-element.47), channel_id=1, source_target_pairs={{0,4},{4,8},{8,12},{12,14},{14,10},{10,6},{6,2},{2,0},{1,5},{5,9},... | collective-permute-start | bytes 614408 | tf_op jit(solution)/shard_map/ppermute | solution.py:367
  55.3 16.4 %collective-permute-start.19 = (bf16[384,640]{1,0:T(8,128)(2,1)S(1)}, bf16[384,640]{1,0:T(8,128)(2,1)S(1)}, u32[]{:S(2)}, u32[]{:S(2)}) collective-permute-start(bf16[384,640]{1,0:T(8,128)(2,1)S(1)} %get-tuple-element.51), channel_id=1, source_target_pairs={{0,1},{1,0},{2,3},{3,2},{4,5},{5,4},{6,7},{7,6},{8,9},{9,8},{10,11... | collective-permute-start | bytes 1474568 | tf_op jit(solution)/shard_map/ppermute | solution.py:336
  57.8 8.1 %collective-permute-start.24 = (bf16[160,640]{1,0:T(8,128)(2,1)S(1)}, bf16[160,640]{1,0:T(8,128)(2,1)S(1)}, u32[]{:S(2)}, u32[]{:S(2)}) collective-permute-start(bf16[160,640]{1,0:T(8,128)(2,1)S(1)} %get-tuple-element.56.refs_3_), channel_id=1, source_target_pairs={{0,4},{4,8},{8,12},{12,14},{14,10},{10,6},{6,2},{2,0},{1,5},{5,9},... | collective-permute-start | bytes 614408 | tf_op jit(solution)/shard_map/ppermute | solution.py:367
  59.4 8.0 %collective-permute-start.25 = (bf16[160,640]{1,0:T(8,128)(2,1)S(1)}, bf16[160,640]{1,0:T(8,128)(2,1)S(1)}, u32[]{:S(2)}, u32[]{:S(2)}) collective-permute-start(bf16[160,640]{1,0:T(8,128)(2,1)S(1)} %get-tuple-element.59), channel_id=1, source_target_pairs={{4,0},{8,4},{12,8},{14,12},{10,14},{6,10},{2,6},{0,2},{5,1},{9,5},... | collective-permute-start | bytes 614408 | tf_op jit(solution)/shard_map/ppermute | solution.py:367
  60.0 10.3 %collective-permute-start.22 = (bf16[160,640]{1,0:T(8,128)(2,1)S(1)}, bf16[160,640]{1,0:T(8,128)(2,1)S(1)}, u32[]{:S(2)}, u32[]{:S(2)}) collective-permute-start(bf16[160,640]{1,0:T(8,128)(2,1)S(1)} %get-tuple-element.57.refs_3_), channel_id=1, source_target_pairs={{0,4},{4,8},{8,12},{12,14},{14,10},{10,6},{6,2},{2,0},{1,5},{5,9},... | collective-permute-start | bytes 614408 | tf_op jit(solution)/shard_map/ppermute | solution.py:367
  61.6 10.0 %collective-permute-start.23 = (bf16[160,640]{1,0:T(8,128)(2,1)S(1)}, bf16[160,640]{1,0:T(8,128)(2,1)S(1)}, u32[]{:S(2)}, u32[]{:S(2)}) collective-permute-start(bf16[160,640]{1,0:T(8,128)(2,1)S(1)} %get-tuple-element.58), channel_id=1, source_target_pairs={{4,0},{8,4},{12,8},{14,12},{10,14},{6,10},{2,6},{0,2},{5,1},{9,5},... | collective-permute-start | bytes 614408 | tf_op jit(solution)/shard_map/ppermute | solution.py:367
  70.2 11.9 %collective-permute-start.18 = (bf16[384,640]{1,0:T(8,128)(2,1)S(1)}, bf16[384,640]{1,0:T(8,128)(2,1)S(1)}, u32[]{:S(2)}, u32[]{:S(2)}) collective-permute-start(bf16[384,640]{1,0:T(8,128)(2,1)S(1)} %get-tuple-element.50), channel_id=1, source_target_pairs={{0,1},{1,0},{2,3},{3,2},{4,5},{5,4},{6,7},{7,6},{8,9},{9,8},{10,11... | collective-permute-start | bytes 1474568 | tf_op jit(solution)/shard_map/ppermute | solution.py:396
  71.8 14.2 %collective-permute-start.26 = (bf16[384,640]{1,0:T(8,128)(2,1)S(1)}, bf16[384,640]{1,0:T(8,128)(2,1)S(1)}, u32[]{:S(2)}, u32[]{:S(2)}) collective-permute-start(bf16[384,640]{1,0:T(8,128)(2,1)S(1)} %shard_map.89.refs_2_), channel_id=1, source_target_pairs={{0,16},{16,0},{1,17},{17,1},{2,18},{18,2},{3,19},{19,3},{4,20},{20... | collective-permute-start | bytes 1474568 | tf_op jit(solution)/shard_map/ppermute | solution.py:340
  78.4 10.9 %collective-permute-start.32 = (bf16[160,640]{1,0:T(8,128)(2,1)S(1)}, bf16[160,640]{1,0:T(8,128)(2,1)S(1)}, u32[]{:S(2)}, u32[]{:S(2)}) collective-permute-start(bf16[160,640]{1,0:T(8,128)(2,1)S(1)} %shard_map.91.refs_3_), channel_id=1, source_target_pairs={{0,4},{4,8},{8,12},{12,14},{14,10},{10,6},{6,2},{2,0},{1,5},{5,9},... | collective-permute-start | bytes 614408 | tf_op jit(solution)/shard_map/ppermute | solution.py:367
  80.9 8.4 %collective-permute-start.33 = (bf16[160,640]{1,0:T(8,128)(2,1)S(1)}, bf16[160,640]{1,0:T(8,128)(2,1)S(1)}, u32[]{:S(2)}, u32[]{:S(2)}) collective-permute-start(bf16[160,640]{1,0:T(8,128)(2,1)S(1)} %shard_map.95), channel_id=1, source_target_pairs={{4,0},{8,4},{12,8},{14,12},{10,14},{6,10},{2,6},{0,2},{5,1},{9,5},... | collective-permute-start | bytes 614408 | tf_op jit(solution)/shard_map/ppermute | solution.py:367
  81.7 7.6 %collective-permute-start.34 = (bf16[160,640]{1,0:T(8,128)(2,1)S(1)}, bf16[160,640]{1,0:T(8,128)(2,1)S(1)}, u32[]{:S(2)}, u32[]{:S(2)}) collective-permute-start(bf16[160,640]{1,0:T(8,128)(2,1)S(1)} %shard_map.92.refs_7_.refs_1_), channel_id=1, source_target_pairs={{0,16},{16,0},{1,17},{17,1},{2,18},{18,2},{3,19},{19,3},{4,20},{20... | collective-permute-start | bytes 614408 | tf_op jit(solution)/shard_map/ppermute | solution.py:403
  (17 other events, 160.4 us)

commit v20 on v19

--- a/solution.py
+++ b/solution.py
@@ -87,27 +87,32 @@
     return jnp.where(index < length, rows.astype(F32), 0.0).astype(BF16)
 
 
-def first_kernel(
-    lengths, frames, out_grad, gain, w_up, w_down, passing, mine_up, mine_down, sems, rows, grads
-):
+def first_kernel(lengths, frames, out_grad, gain_from, w_up, w_down, *refs):
+    passing, mine_up, mine_down, rows, grads, normed, gain, sems = refs
     half, quarter = rows.shape[0], mine_up.shape[1]
     start = pl.multiple_of(lax.axis_index("gy") * half, half)
     columns = pl.ds(pl.multiple_of(lax.axis_index("groups") * quarter, quarter), quarter)
     moves = (
+        (gain_from, gain),
         (frames.at[pl.ds(start, half)], rows),
         (out_grad.at[pl.ds(start, half)], grads),
         (w_up.at[:, columns], mine_up),
         (w_down.at[:, columns], mine_down),
+        (normed, passing.at[0]),
+        (grads, passing.at[1]),
     )
     copies = [pltpu.make_async_copy(*move, sems.at[i]) for i, move in enumerate(moves)]
-    for copy in copies:
+    for copy in copies[:5]:
         copy.start()
+    copies[2].wait()
+    grads[...] = mask_rows(grads[...], start, lengths[lax.axis_index("gx")])
+    copies[6].start()
     copies[0].wait()
-    passing[0] = norm_rows(rows[...], gain)[0]
     copies[1].wait()
-    passing[1] = mask_rows(grads[...], start, lengths[lax.axis_index("gx")])
-    copies[2].wait()
-    copies[3].wait()
+    normed[...] = norm_rows(rows[...], gain)[0]
+    copies[5].start()
+    for copy in copies[3:]:
+        copy.wait()
 
 
 def norm_kernel(lengths, frames, out_grad, gain, normed, grads, stats):
@@ -202,11 +207,14 @@
     factor[...] = inv_std * centred
 
 
-def input_kernel(base, factor, sums, came, stats, out, token):
+def input_rows(base, factor, sums, came, stats):
     means = (sums[...] + came[...]) * (0.5 / base.shape[1])
     value = base[...] - stats[:, 1:2] * means[:, 0:1] - factor[...] * means[:, 1:2]
-    out[...] = value.astype(BF16)
-    token[...] = jnp.zeros_like(token)
+    return value.astype(BF16)
+
+
+def input_kernel(base, factor, sums, came, stats, out):
+    out[...] = input_rows(base, factor, sums, came, stats)
 
 
 def hop_kernel(places, peers, partial, *refs):
@@ -221,14 +229,16 @@
     total[...] = (value + up[...].astype(F32) + down[...].astype(F32)).astype(BF16)
 
 
-def join_kernel(peers, partial, up, down, passed, out):
+def last_kernel(peers, base, factor, sums, came, stats, partial, up, down, passed, *outs):
+    input_grad, up_grad = outs
+    input_grad[...] = input_rows(base, factor, sums, came, stats)
     depth, width = passed.shape
     side = lax.axis_index("groups")
     value = partial[block_rows(0, peers, depth), :].astype(F32)
     value = value + up[...].astype(F32) + down[...].astype(F32)
-    out[:, pl.ds(pl.multiple_of(side * width, width), width)] = value
+    up_grad[:, pl.ds(pl.multiple_of(side * width, width), width)] = value
     other = pl.ds(pl.multiple_of((1 - side) * width, width), width)
-    out[:, other] = passed[...].astype(F32)
+    up_grad[:, other] = passed[...].astype(F32)
 
 
 def place_halves_kernel(own, passed, out):
@@ -261,10 +271,12 @@
         first_kernel,
         (lengths, frames, out_grad, ln_gain, w_up, w_down),
         (shape((2, half_rows, width), BF16), block_of, block_of),
-        [pltpu.SemaphoreType.DMA((4,))] + [pltpu.VMEM((half_rows, width), BF16)] * 2,
+        [pltpu.VMEM((half_rows, width), BF16)] * 3
+        + [pltpu.VMEM((width,), F32), pltpu.SemaphoreType.DMA((7,))],
         flops=5 * frame_len * width,
         vmem=60,
-        left=(1, 2, 4, 5),
+        left=range(1, 6),
+        out=ANY,
     )
     first = lax.ppermute(passing, "groups", swap)
     normed, grads, stats = call(
@@ -351,13 +363,6 @@
             ties=ties,
         )
 
-    def input_gradient(base, factor, sums):
-        return call(
-            input_kernel,
-            (base, factor, sums, lax.ppermute(sums, "gy", swap), stats),
-            (half_rows_of, shape((8, 128), F32)),
-        )
-
     up_grad_of = shape((depth, hidden), F32)
     if ringed:
         came, kept = [{}, {}], []
@@ -389,8 +394,8 @@
         tie = hop(1, 1, keep)
         tie = hop(0, 1, tie)
         tie = hop(1, 2, tie)
+        tie, back = over_cores(keep, parts, tie)
         tie = hop(0, 2, tie)
-        tie, back = over_cores(keep, parts, tie)
         for turn in range(3, half):
             tie = hop(0, turn, hop(1, turn, tie))
         sent = lax.ppermute(send, "gy", swap)
@@ -402,18 +407,20 @@
         )
         passed = lax.ppermute(passing, "groups", swap)
         send_on(0, [hold(kept[0], passing)], ["down"])
-        input_grad, token = input_gradient(*scale(keep, sent, back, passing))
-        up_grad = call(
-            functools.partial(join_kernel, peers),
-            (partial[0], came[0]["up"], came[0]["down"], passed),
-            up_grad_of,
-            ties=(token,),
+        base, factor, sums = scale(keep, sent, back, passing)
+        input_grad, up_grad = call(
+            functools.partial(last_kernel, peers),
+            (base, factor, sums, lax.ppermute(sums, "gy", swap), stats)
+            + (partial[0], came[0]["up"], came[0]["down"], passed),
+            (half_rows_of, up_grad_of),
         )
     else:
         keep, send, parts = own_d_norm()
         sent = lax.ppermute(send, "gy", swap)
         _, back = over_cores(keep, parts)
-        input_grad, _ = input_gradient(*scale(keep, sent, back))
+        base, factor, sums = scale(keep, sent, back)
+        came = lax.ppermute(sums, "gy", swap)
+        input_grad = call(input_kernel, (base, factor, sums, came, stats), half_rows_of)
         total, passing = [
             lax.psum_scatter(p.astype(F32), "gx", scatter_dimension=0, tiled=True) for p in partial
         ]

time: 90.5 us -> 101 us (1.12)
  Pallas kernels: 19.7 us -> 29.9 us
    pallas_call x17 -> x16, Pallas kernels: 19.7 us -> 29.9 us  [call(): pl.pallas_call(body if ties else kernel, out_shape=out_shape, in_specs=[S...]
    ppermute x14, waiting for transfers between devices: 16.1 us -> 18.1 us  [send_on(): came[i][name] = lax.ppermute(block, 'gx', ahead if name == 'up' else behind)]
    ppermute x1, waiting for transfers between devices: 3.94 us -> 2.01 us  [over_cores(): return (over, lax.ppermute(over, 'groups', swap))]
  transfers between devices with their start and end apart: 35 -> 35, of which waited for: 20 -> 23; matrix products, arithmetic and copies ran while one was open for 0% -> 0% of each run, Pallas kernels for 17% -> 14%
where the time goes in v20:
time: 101 us; the launch traced here: 100 us
  waiting for transfers between devices  37.1 us (37%)
  starting transfers between devices  32.5 us (32%)
  Pallas kernels  29.9 us (30%)
    pallas_call x16, Pallas kernels, call(): pl.pallas_call(body if ties else kernel, out_shape=out_shape, in_specs=[S...  29.9 us
    ppermute x14, waiting for transfers between devices, send_on(): came[i][name] = lax.ppermute(block, 'gx', ahead if name == 'up' else behind)  18.1 us
    ppermute x14, starting transfers between devices, send_on(): came[i][name] = lax.ppermute(block, 'gx', ahead if name == 'up' else behind)  14.6 us
    ppermute x6, starting transfers between devices, shards(): up[i] = lax.ppermute(up[i], 'gx', ahead)  8.39 us
    ppermute x6, waiting for transfers between devices, shards(): down[i] = lax.ppermute(down[i], 'gx', behind)  7.92 us
    ppermute x6, waiting for transfers between devices, shards(): up[i] = lax.ppermute(up[i], 'gx', ahead)  4.61 us
    ppermute x6, starting transfers between devices, shards(): down[i] = lax.ppermute(down[i], 'gx', behind)  3.77 us
    ppermute x1, starting transfers between devices, shards(): first = lax.ppermute(passing, 'groups', swap)  3 us
  transfers between devices with their start and end apart: 35, of which 23 were waited for; matrix products, arithmetic and copies ran while one was open for 0% of the time, Pallas kernels for 14%

profile of v20, /device:TPU:0, one launch (start us, length us, event | category | flops | bytes accessed | tf_op | source)
XLA Modules:
  0.0 100.4 jit_solution(11217597004639680064)
XLA Ops:
  0.7 14.4 %shard_map.78 = (bf16[2,192,1280]{2,1,0:T(8,128)(2,1)}, bf16[160,640]{1,0:T(8,128)(2,1)}, bf16[160,640]{1,0:T(8,128)(2,1)}) custom-call(s32[8]{0:T(128)} %lengths.3, bf16[384,1280]{1,0:T(8,128)(2,1)} %bitcast.3, bf16[384,1280]{1,0:T(8,128)(2,1)} %bitcast.6, f32[1280]{0:T(1024)} %gain_from.1, bf16[160,1280]{1,0:T(8,128)(2,1)} %w_up.1, bf16[160,1280]{1,0:T(8,128)(2,1)} %w_down.1), custom_call_target="tpu_custom_call" | custom-call | flops 2457600 | bytes 4183072 | tf_op jit(solution)/shard_map/pallas_call | solution.py:28
  15.1 3.0 %collective-permute-start.14 = (bf16[2,192,1280]{2,1,0:T(8,128)(2,1)}, bf16[2,192,1280]{2,1,0:T(8,128)(2,1)S(1)}, u32[]{:S(2)}, u32[]{:S(2)}) collective-permute-start(bf16[2,192,1280]{2,1,0:T(8,128)(2,1)} %get-tuple-element.43), channel_id=1, source_target_pairs={{0,16},{16,0},{1,17},{17,1},{2,18},{18,2},{3,19},{19,3},{4,20},{20... | collective-permute-start | bytes 2949128 | tf_op jit(solution)/shard_map/ppermute | solution.py:281
  18.1 1.6 %collective-permute-start = (bf16[160,640]{1,0:T(8,128)(2,1)}, bf16[160,640]{1,0:T(8,128)(2,1)S(1)}, u32[]{:S(2)}, u32[]{:S(2)}) collective-permute-start(bf16[160,640]{1,0:T(8,128)(2,1)} %get-tuple-element.38.refs_0_), channel_id=1, source_target_pairs={{0,4},{4,8},{8,12},{12,14},{14,10},{10,6},{6,2},{2,0},{1,5},{5,9},... | collective-permute-start | bytes 614408 | tf_op jit(solution)/shard_map/ppermute | solution.py:295
  23.6 2.6 %collective-permute-done.refs_0_ = bf16[160,640]{1,0:T(8,128)(2,1)S(1)} collective-permute-done((bf16[160,640]{1,0:T(8,128)(2,1)}, bf16[160,640]{1,0:T(8,128)(2,1)S(1)}, u32[]{:S(2)}, u32[]{:S(2)}) %collective-permute-start) | collective-permute-done | bytes 204832 | tf_op jit(solution)/shard_map/ppermute | solution.py:295
  26.3 1.6 %collective-permute-start.4 = (bf16[160,640]{1,0:T(8,128)(2,1)S(1)}, bf16[160,640]{1,0:T(8,128)(2,1)S(1)}, u32[]{:S(2)}, u32[]{:S(2)}) collective-permute-start(bf16[160,640]{1,0:T(8,128)(2,1)S(1)} %shard_map.79.refs_2_), channel_id=1, source_target_pairs={{0,4},{4,8},{8,12},{12,14},{14,10},{10,6},{6,2},{2,0},{1,5},{5,9},... | collective-permute-start | bytes 614408 | tf_op jit(solution)/shard_map/ppermute | solution.py:295
  28.3 3.9 %collective-permute-done.1.refs_3_ = bf16[160,640]{1,0:T(8,128)(2,1)S(1)} collective-permute-done((bf16[160,640]{1,0:T(8,128)(2,1)}, bf16[160,640]{1,0:T(8,128)(2,1)S(1)}, u32[]{:S(2)}, u32[]{:S(2)}) %collective-permute-start.1) | collective-permute-done | bytes 204832 | tf_op jit(solution)/shard_map/ppermute | solution.py:296
  32.7 1.6 %collective-permute-start.6 = (bf16[160,640]{1,0:T(8,128)(2,1)S(1)}, bf16[160,640]{1,0:T(8,128)(2,1)S(1)}, u32[]{:S(2)}, u32[]{:S(2)}) collective-permute-start(bf16[160,640]{1,0:T(8,128)(2,1)S(1)} %collective-permute-done.2.refs_4_), channel_id=1, source_target_pairs={{0,4},{4,8},{8,12},{12,14},{14,10},{10,6},{6,2},{2,0},{1,5},{5,9},... | collective-permute-start | bytes 614408 | tf_op jit(solution)/shard_map/ppermute | solution.py:295
  35.1 1.6 %collective-permute-start.8 = (bf16[160,640]{1,0:T(8,128)(2,1)S(1)}, bf16[160,640]{1,0:T(8,128)(2,1)S(1)}, u32[]{:S(2)}, u32[]{:S(2)}) collective-permute-start(bf16[160,640]{1,0:T(8,128)(2,1)S(1)} %collective-permute-done.4.refs_6_), channel_id=1, source_target_pairs={{0,4},{4,8},{8,12},{12,14},{14,10},{10,6},{6,2},{2,0},{1,5},{5,9},... | collective-permute-start | bytes 614408 | tf_op jit(solution)/shard_map/ppermute | solution.py:295
  37.1 3.9 %collective-permute-done.5.refs_7_ = bf16[160,640]{1,0:T(8,128)(2,1)S(1)} collective-permute-done((bf16[160,640]{1,0:T(8,128)(2,1)S(1)}, bf16[160,640]{1,0:T(8,128)(2,1)S(1)}, u32[]{:S(2)}, u32[]{:S(2)}) %collective-permute-start.5) | collective-permute-done | bytes 204832 | tf_op jit(solution)/shard_map/ppermute | solution.py:296
  41.5 1.6 %collective-permute-start.11 = (bf16[160,640]{1,0:T(8,128)(2,1)S(1)}, bf16[160,640]{1,0:T(8,128)(2,1)S(1)}, u32[]{:S(2)}, u32[]{:S(2)}) collective-permute-start(bf16[160,640]{1,0:T(8,128)(2,1)S(1)} %collective-permute-done.6.refs_8_), channel_id=1, source_target_pairs={{0,4},{4,8},{8,12},{12,14},{14,10},{10,6},{6,2},{2,0},{1,5},{5,9},... | collective-permute-start | bytes 614408 | tf_op jit(solution)/shard_map/ppermute | solution.py:295
  46.3 3.6 %shard_map.80 = (bf16[1280,640]{1,0:T(8,128)(2,1)S(1)}, bf16[1280,640]{1,0:T(8,128)(2,1)S(1)}) custom-call(bf16[160,640]{1,0:T(8,128)(2,1)S(1)} %copy-done.2, bf16[160,640]{1,0:T(8,128)(2,1)S(1)} %copy-done.3, bf16[160,640]{1,0:T(8,128)(2,1)S(1)} %shard_map.79.refs_2_, bf16[160,640]{1,0:T(8,128)(2,1)S(1)} %collective-permute-done.1.refs_3_, ...), custom_call_target="tpu_custom_call" | custom-call | flops 1 | bytes 5734400 | tf_op jit(solution)/shard_map/pallas_call | solution.py:28
  52.5 2.9 %shard_map.81 = (bf16[384,640]{1,0:T(8,128)(2,1)S(1)}, bf16[1280,640]{1,0:T(8,128)(2,1)S(1)}, bf16[1280,640]{1,0:T(8,128)(2,1)S(1)}, bf16[1280,640]{1,0:T(8,128)...) custom-call(bf16[384,1280]{1,0:T(8,128)(2,1)S(1)} %get-tuple-element.36.refs_1_.normed, ...), custom_call_target="tpu_custom_call" | custom-call | flops 1887436800 | bytes 11878400 | tf_op jit(solution)/shard_map/pallas_call | solution.py:28
  55.4 1.6 %collective-permute-start.16 = (bf16[160,640]{1,0:T(8,128)(2,1)S(1)}, bf16[160,640]{1,0:T(8,128)(2,1)S(1)}, u32[]{:S(2)}, u32[]{:S(2)}) collective-permute-start(bf16[160,640]{1,0:T(8,128)(2,1)S(1)} %get-tuple-element.47), channel_id=1, source_target_pairs={{0,4},{4,8},{8,12},{12,14},{14,10},{10,6},{6,2},{2,0},{1,5},{5,9},... | collective-permute-start | bytes 614408 | tf_op jit(solution)/shard_map/ppermute | solution.py:372
  57.5 2.7 %shard_map.83 = (bf16[384,640]{1,0:T(8,128)(2,1)S(1)}, bf16[1280,640]{1,0:T(8,128)(2,1)S(1)}, bf16[160,640]{1,0:T(8,128)(2,1)S(1)}, bf16[160,640]{1,0:T(8,128)(2,1)S(1)}) custom-call(bf16[2,192,1280]{2,1,0:T(8,128)(2,1)S(1)} %shard_map.82.first, bf16[2,192,1280]{2,1,0:T(8,128)(2,1)S(1)} %collective-permute-done.15.second, ...), custom_call_target="tpu_custom_call" | custom-call | flops 1887436800 | bytes 7782400 | tf_op jit(solution)/shard_map/pallas_call | solution.py:28
  60.2 1.6 %collective-permute-start.20 = (bf16[160,640]{1,0:T(8,128)(2,1)S(1)}, bf16[160,640]{1,0:T(8,128)(2,1)S(1)}, u32[]{:S(2)}, u32[]{:S(2)}) collective-permute-start(bf16[160,640]{1,0:T(8,128)(2,1)S(1)} %get-tuple-element.53), channel_id=1, source_target_pairs={{0,4},{4,8},{8,12},{12,14},{14,10},{10,6},{6,2},{2,0},{1,5},{5,9},... | collective-permute-start | bytes 614408 | tf_op jit(solution)/shard_map/ppermute | solution.py:372
  64.3 2.0 %shard_map.84 = (bf16[2,384,640]{2,1,0:T(8,128)(2,1)S(1)}, bf16[384,640]{1,0:T(8,128)(2,1)S(1)}, bf16[384,640]{1,0:T(8,128)(2,1)S(1)}) custom-call(bf16[384,640]{1,0:T(8,128)(2,1)S(1)} %get-tuple-element.42.refs_0_, bf16[384,640]{1,0:T(8,128)(2,1)S(1)} %get-tuple-element.46.refs_1_, bf16[1280,640]{1,0:T(8,128)(2,1)S(1)} %get-tuple-element.44.up.refs_2_, ...), custom_call_target="tpu_custom_call" | custom-call | flops 1258291200 | bytes 4587520 | tf_op jit(solution)/shard_map/pallas_call | solution.py:28
  68.7 1.6 %collective-permute-start.22 = (bf16[160,640]{1,0:T(8,128)(2,1)S(1)}, bf16[160,640]{1,0:T(8,128)(2,1)S(1)}, u32[]{:S(2)}, u32[]{:S(2)}) collective-permute-start(bf16[160,640]{1,0:T(8,128)(2,1)S(1)} %get-tuple-element.55.refs_3_), channel_id=1, source_target_pairs={{0,4},{4,8},{8,12},{12,14},{14,10},{10,6},{6,2},{2,0},{1,5},{5,9},... | collective-permute-start | bytes 614408 | tf_op jit(solution)/shard_map/ppermute | solution.py:372
  70.9 1.6 %collective-permute-start.27 = (bf16[160,640]{1,0:T(8,128)(2,1)S(1)}, bf16[160,640]{1,0:T(8,128)(2,1)S(1)}, u32[]{:S(2)}, u32[]{:S(2)}) collective-permute-start(bf16[160,640]{1,0:T(8,128)(2,1)S(1)} %get-tuple-element.58.refs_3_), channel_id=1, source_target_pairs={{0,4},{4,8},{8,12},{12,14},{14,10},{10,6},{6,2},{2,0},{1,5},{5,9},... | collective-permute-start | bytes 614408 | tf_op jit(solution)/shard_map/ppermute | solution.py:372
  73.0 3.8 %collective-permute-done.22.refs_1_ = bf16[160,640]{1,0:T(8,128)(2,1)S(1)} collective-permute-done((bf16[160,640]{1,0:T(8,128)(2,1)S(1)}, bf16[160,640]{1,0:T(8,128)(2,1)S(1)}, u32[]{:S(2)}, u32[]{:S(2)}) %collective-permute-start.22) | collective-permute-done | bytes 204832 | tf_op jit(solution)/shard_map/ppermute | solution.py:372
  76.8 1.6 %collective-permute-done.23.refs_2_ = bf16[160,640]{1,0:T(8,128)(2,1)S(1)} collective-permute-done((bf16[160,640]{1,0:T(8,128)(2,1)S(1)}, bf16[160,640]{1,0:T(8,128)(2,1)S(1)}, u32[]{:S(2)}, u32[]{:S(2)}) %collective-permute-start.23) | collective-permute-done | bytes 204832 | tf_op jit(solution)/shard_map/ppermute | solution.py:372
  84.3 1.6 %collective-permute-done.26.refs_1_ = bf16[160,640]{1,0:T(8,128)(2,1)S(1)} collective-permute-done((bf16[160,640]{1,0:T(8,128)(2,1)S(1)}, bf16[160,640]{1,0:T(8,128)(2,1)S(1)}, u32[]{:S(2)}, u32[]{:S(2)}) %collective-permute-start.26) | collective-permute-done | bytes 204832 | tf_op jit(solution)/shard_map/ppermute | solution.py:372
  86.5 2.2 %collective-permute-done.30.refs_1_ = bf16[160,640]{1,0:T(8,128)(2,1)S(1)} collective-permute-done((bf16[160,640]{1,0:T(8,128)(2,1)S(1)}, bf16[160,640]{1,0:T(8,128)(2,1)S(1)}, u32[]{:S(2)}, u32[]{:S(2)}) %collective-permute-start.30) | collective-permute-done | bytes 204832 | tf_op jit(solution)/shard_map/ppermute | solution.py:372
  90.4 2.2 %collective-permute-done.29.refs_2_ = bf16[160,640]{1,0:T(8,128)(2,1)S(1)} collective-permute-done((bf16[160,640]{1,0:T(8,128)(2,1)S(1)}, bf16[160,640]{1,0:T(8,128)(2,1)S(1)}, u32[]{:S(2)}, u32[]{:S(2)}) %collective-permute-start.29) | collective-permute-done | bytes 204832 | tf_op jit(solution)/shard_map/ppermute | solution.py:372
  93.3 2.0 %collective-permute-done.24.refs_2_ = bf16[384,640]{1,0:T(8,128)(2,1)S(1)} collective-permute-done((bf16[384,640]{1,0:T(8,128)(2,1)S(1)}, bf16[384,640]{1,0:T(8,128)(2,1)S(1)}, u32[]{:S(2)}, u32[]{:S(2)}) %collective-permute-start.24) | collective-permute-done | bytes 491552 | tf_op jit(solution)/shard_map/ppermute | solution.py:352
  (78 shorter events, 32.7 us)
Async XLA Ops:
  15.1 37.4 %collective-permute-start.14 = (bf16[2,192,1280]{2,1,0:T(8,128)(2,1)}, bf16[2,192,1280]{2,1,0:T(8,128)(2,1)S(1)}, u32[]{:S(2)}, u32[]{:S(2)}) collective-permute-start(bf16[2,192,1280]{2,1,0:T(8,128)(2,1)} %get-tuple-element.43), channel_id=1, source_target_pairs={{0,16},{16,0},{1,17},{17,1},{2,18},{18,2},{3,19},{19,3},{4,20},{20... | collective-permute-start | bytes 2949128 | tf_op jit(solution)/shard_map/ppermute | solution.py:281
  18.1 8.2 %collective-permute-start = (bf16[160,640]{1,0:T(8,128)(2,1)}, bf16[160,640]{1,0:T(8,128)(2,1)S(1)}, u32[]{:S(2)}, u32[]{:S(2)}) collective-permute-start(bf16[160,640]{1,0:T(8,128)(2,1)} %get-tuple-element.38.refs_0_), channel_id=1, source_target_pairs={{0,4},{4,8},{8,12},{12,14},{14,10},{10,6},{6,2},{2,0},{1,5},{5,9},... | collective-permute-start | bytes 614408 | tf_op jit(solution)/shard_map/ppermute | solution.py:295
  19.6 8.2 %collective-permute-start.3 = (bf16[160,640]{1,0:T(8,128)(2,1)}, bf16[160,640]{1,0:T(8,128)(2,1)S(1)}, u32[]{:S(2)}, u32[]{:S(2)}) collective-permute-start(bf16[160,640]{1,0:T(8,128)(2,1)} %get-tuple-element.39.refs_1_), channel_id=1, source_target_pairs={{4,0},{8,4},{12,8},{14,12},{10,14},{6,10},{2,6},{0,2},{5,1},{9,5},... | collective-permute-start | bytes 614408 | tf_op jit(solution)/shard_map/ppermute | solution.py:296
  20.1 12.2 %collective-permute-start.1 = (bf16[160,640]{1,0:T(8,128)(2,1)}, bf16[160,640]{1,0:T(8,128)(2,1)S(1)}, u32[]{:S(2)}, u32[]{:S(2)}) collective-permute-start(bf16[160,640]{1,0:T(8,128)(2,1)} %get-tuple-element.38.refs_0_), channel_id=1, source_target_pairs={{4,0},{8,4},{12,8},{14,12},{10,14},{6,10},{2,6},{0,2},{5,1},{9,5},... | collective-permute-start | bytes 614408 | tf_op jit(solution)/shard_map/ppermute | solution.py:296
  21.6 11.1 %collective-permute-start.2 = (bf16[160,640]{1,0:T(8,128)(2,1)}, bf16[160,640]{1,0:T(8,128)(2,1)S(1)}, u32[]{:S(2)}, u32[]{:S(2)}) collective-permute-start(bf16[160,640]{1,0:T(8,128)(2,1)} %get-tuple-element.39.refs_1_), channel_id=1, source_target_pairs={{0,4},{4,8},{8,12},{12,14},{14,10},{10,6},{6,2},{2,0},{1,5},{5,9},... | collective-permute-start | bytes 614408 | tf_op jit(solution)/shard_map/ppermute | solution.py:295
  26.3 8.8 %collective-permute-start.4 = (bf16[160,640]{1,0:T(8,128)(2,1)S(1)}, bf16[160,640]{1,0:T(8,128)(2,1)S(1)}, u32[]{:S(2)}, u32[]{:S(2)}) collective-permute-start(bf16[160,640]{1,0:T(8,128)(2,1)S(1)} %shard_map.79.refs_2_), channel_id=1, source_target_pairs={{0,4},{4,8},{8,12},{12,14},{14,10},{10,6},{6,2},{2,0},{1,5},{5,9},... | collective-permute-start | bytes 614408 | tf_op jit(solution)/shard_map/ppermute | solution.py:295
  27.9 8.8 %collective-permute-start.7 = (bf16[160,640]{1,0:T(8,128)(2,1)S(1)}, bf16[160,640]{1,0:T(8,128)(2,1)S(1)}, u32[]{:S(2)}, u32[]{:S(2)}) collective-permute-start(bf16[160,640]{1,0:T(8,128)(2,1)S(1)} %collective-permute-done.3.refs_5_), channel_id=1, source_target_pairs={{4,0},{8,4},{12,8},{14,12},{10,14},{6,10},{2,6},{0,2},{5,1},{9,5},... | collective-permute-start | bytes 614408 | tf_op jit(solution)/shard_map/ppermute | solution.py:296
  32.3 8.8 %collective-permute-start.5 = (bf16[160,640]{1,0:T(8,128)(2,1)S(1)}, bf16[160,640]{1,0:T(8,128)(2,1)S(1)}, u32[]{:S(2)}, u32[]{:S(2)}) collective-permute-start(bf16[160,640]{1,0:T(8,128)(2,1)S(1)} %collective-permute-done.1.refs_3_), channel_id=1, source_target_pairs={{4,0},{8,4},{12,8},{14,12},{10,14},{6,10},{2,6},{0,2},{5,1},{9,5},... | collective-permute-start | bytes 614408 | tf_op jit(solution)/shard_map/ppermute | solution.py:296
  32.7 8.8 %collective-permute-start.6 = (bf16[160,640]{1,0:T(8,128)(2,1)S(1)}, bf16[160,640]{1,0:T(8,128)(2,1)S(1)}, u32[]{:S(2)}, u32[]{:S(2)}) collective-permute-start(bf16[160,640]{1,0:T(8,128)(2,1)S(1)} %collective-permute-done.2.refs_4_), channel_id=1, source_target_pairs={{0,4},{4,8},{8,12},{12,14},{14,10},{10,6},{6,2},{2,0},{1,5},{5,9},... | collective-permute-start | bytes 614408 | tf_op jit(solution)/shard_map/ppermute | solution.py:295
  35.1 9.2 %collective-permute-start.8 = (bf16[160,640]{1,0:T(8,128)(2,1)S(1)}, bf16[160,640]{1,0:T(8,128)(2,1)S(1)}, u32[]{:S(2)}, u32[]{:S(2)}) collective-permute-start(bf16[160,640]{1,0:T(8,128)(2,1)S(1)} %collective-permute-done.4.refs_6_), channel_id=1, source_target_pairs={{0,4},{4,8},{8,12},{12,14},{14,10},{10,6},{6,2},{2,0},{1,5},{5,9},... | collective-permute-start | bytes 614408 | tf_op jit(solution)/shard_map/ppermute | solution.py:295
  36.7 9.2 %collective-permute-start.9 = (bf16[160,640]{1,0:T(8,128)(2,1)S(1)}, bf16[160,640]{1,0:T(8,128)(2,1)S(1)}, u32[]{:S(2)}, u32[]{:S(2)}) collective-permute-start(bf16[160,640]{1,0:T(8,128)(2,1)S(1)} %collective-permute-done.7.refs_9_), channel_id=1, source_target_pairs={{4,0},{8,4},{12,8},{14,12},{10,14},{6,10},{2,6},{0,2},{5,1},{9,5},... | collective-permute-start | bytes 614408 | tf_op jit(solution)/shard_map/ppermute | solution.py:296
  41.0 8.8 %collective-permute-start.10 = (bf16[160,640]{1,0:T(8,128)(2,1)S(1)}, bf16[160,640]{1,0:T(8,128)(2,1)S(1)}, u32[]{:S(2)}, u32[]{:S(2)}) collective-permute-start(bf16[160,640]{1,0:T(8,128)(2,1)S(1)} %collective-permute-done.5.refs_7_), channel_id=1, source_target_pairs={{4,0},{8,4},{12,8},{14,12},{10,14},{6,10},{2,6},{0,2},{5,1},{9,5},... | collective-permute-start | bytes 614408 | tf_op jit(solution)/shard_map/ppermute | solution.py:296
  41.5 8.4 %collective-permute-start.11 = (bf16[160,640]{1,0:T(8,128)(2,1)S(1)}, bf16[160,640]{1,0:T(8,128)(2,1)S(1)}, u32[]{:S(2)}, u32[]{:S(2)}) collective-permute-start(bf16[160,640]{1,0:T(8,128)(2,1)S(1)} %collective-permute-done.6.refs_8_), channel_id=1, source_target_pairs={{0,4},{4,8},{8,12},{12,14},{14,10},{10,6},{6,2},{2,0},{1,5},{5,9},... | collective-permute-start | bytes 614408 | tf_op jit(solution)/shard_map/ppermute | solution.py:295
  55.4 7.6 %collective-permute-start.16 = (bf16[160,640]{1,0:T(8,128)(2,1)S(1)}, bf16[160,640]{1,0:T(8,128)(2,1)S(1)}, u32[]{:S(2)}, u32[]{:S(2)}) collective-permute-start(bf16[160,640]{1,0:T(8,128)(2,1)S(1)} %get-tuple-element.47), channel_id=1, source_target_pairs={{0,4},{4,8},{8,12},{12,14},{14,10},{10,6},{6,2},{2,0},{1,5},{5,9},... | collective-permute-start | bytes 614408 | tf_op jit(solution)/shard_map/ppermute | solution.py:372
  57.0 7.3 %collective-permute-start.17 = (bf16[160,640]{1,0:T(8,128)(2,1)S(1)}, bf16[160,640]{1,0:T(8,128)(2,1)S(1)}, u32[]{:S(2)}, u32[]{:S(2)}) collective-permute-start(bf16[160,640]{1,0:T(8,128)(2,1)S(1)} %get-tuple-element.48), channel_id=1, source_target_pairs={{4,0},{8,4},{12,8},{14,12},{10,14},{6,10},{2,6},{0,2},{5,1},{9,5},... | collective-permute-start | bytes 614408 | tf_op jit(solution)/shard_map/ppermute | solution.py:372
  60.2 7.1 %collective-permute-start.20 = (bf16[160,640]{1,0:T(8,128)(2,1)S(1)}, bf16[160,640]{1,0:T(8,128)(2,1)S(1)}, u32[]{:S(2)}, u32[]{:S(2)}) collective-permute-start(bf16[160,640]{1,0:T(8,128)(2,1)S(1)} %get-tuple-element.53), channel_id=1, source_target_pairs={{0,4},{4,8},{8,12},{12,14},{14,10},{10,6},{6,2},{2,0},{1,5},{5,9},... | collective-permute-start | bytes 614408 | tf_op jit(solution)/shard_map/ppermute | solution.py:372
  66.3 14.3 %collective-permute-start.19 = (bf16[384,640]{1,0:T(8,128)(2,1)S(1)}, bf16[384,640]{1,0:T(8,128)(2,1)S(1)}, u32[]{:S(2)}, u32[]{:S(2)}) collective-permute-start(bf16[384,640]{1,0:T(8,128)(2,1)S(1)} %get-tuple-element.51), channel_id=1, source_target_pairs={{0,1},{1,0},{2,3},{3,2},{4,5},{5,4},{6,7},{7,6},{8,9},{9,8},{10,11... | collective-permute-start | bytes 1474568 | tf_op jit(solution)/shard_map/ppermute | solution.py:348
  68.7 8.1 %collective-permute-start.22 = (bf16[160,640]{1,0:T(8,128)(2,1)S(1)}, bf16[160,640]{1,0:T(8,128)(2,1)S(1)}, u32[]{:S(2)}, u32[]{:S(2)}) collective-permute-start(bf16[160,640]{1,0:T(8,128)(2,1)S(1)} %get-tuple-element.55.refs_3_), channel_id=1, source_target_pairs={{0,4},{4,8},{8,12},{12,14},{14,10},{10,6},{6,2},{2,0},{1,5},{5,9},... | collective-permute-start | bytes 614408 | tf_op jit(solution)/shard_map/ppermute | solution.py:372
  70.4 8.0 %collective-permute-start.23 = (bf16[160,640]{1,0:T(8,128)(2,1)S(1)}, bf16[160,640]{1,0:T(8,128)(2,1)S(1)}, u32[]{:S(2)}, u32[]{:S(2)}) collective-permute-start(bf16[160,640]{1,0:T(8,128)(2,1)S(1)} %get-tuple-element.56), channel_id=1, source_target_pairs={{4,0},{8,4},{12,8},{14,12},{10,14},{6,10},{2,6},{0,2},{5,1},{9,5},... | collective-permute-start | bytes 614408 | tf_op jit(solution)/shard_map/ppermute | solution.py:372
  70.9 10.2 %collective-permute-start.27 = (bf16[160,640]{1,0:T(8,128)(2,1)S(1)}, bf16[160,640]{1,0:T(8,128)(2,1)S(1)}, u32[]{:S(2)}, u32[]{:S(2)}) collective-permute-start(bf16[160,640]{1,0:T(8,128)(2,1)S(1)} %get-tuple-element.58.refs_3_), channel_id=1, source_target_pairs={{0,4},{4,8},{8,12},{12,14},{14,10},{10,6},{6,2},{2,0},{1,5},{5,9},... | collective-permute-start | bytes 614408 | tf_op jit(solution)/shard_map/ppermute | solution.py:372
  72.6 10.0 %collective-permute-start.28 = (bf16[160,640]{1,0:T(8,128)(2,1)S(1)}, bf16[160,640]{1,0:T(8,128)(2,1)S(1)}, u32[]{:S(2)}, u32[]{:S(2)}) collective-permute-start(bf16[160,640]{1,0:T(8,128)(2,1)S(1)} %get-tuple-element.62), channel_id=1, source_target_pairs={{4,0},{8,4},{12,8},{14,12},{10,14},{6,10},{2,6},{0,2},{5,1},{9,5},... | collective-permute-start | bytes 614408 | tf_op jit(solution)/shard_map/ppermute | solution.py:372
  80.6 12.7 %collective-permute-start.18 = (bf16[384,640]{1,0:T(8,128)(2,1)S(1)}, bf16[384,640]{1,0:T(8,128)(2,1)S(1)}, u32[]{:S(2)}, u32[]{:S(2)}) collective-permute-start(bf16[384,640]{1,0:T(8,128)(2,1)S(1)} %get-tuple-element.50), channel_id=1, source_target_pairs={{0,1},{1,0},{2,3},{3,2},{4,5},{5,4},{6,7},{7,6},{8,9},{9,8},{10,11... | collective-permute-start | bytes 1474568 | tf_op jit(solution)/shard_map/ppermute | solution.py:401
  81.2 14.1 %collective-permute-start.24 = (bf16[384,640]{1,0:T(8,128)(2,1)S(1)}, bf16[384,640]{1,0:T(8,128)(2,1)S(1)}, u32[]{:S(2)}, u32[]{:S(2)}) collective-permute-start(bf16[384,640]{1,0:T(8,128)(2,1)S(1)} %shard_map.88.refs_3_), channel_id=1, source_target_pairs={{0,16},{16,0},{1,17},{17,1},{2,18},{18,2},{3,19},{19,3},{4,20},{20... | collective-permute-start | bytes 1474568 | tf_op jit(solution)/shard_map/ppermute | solution.py:352
  88.8 7.2 %collective-permute-start.32 = (bf16[160,640]{1,0:T(8,128)(2,1)S(1)}, bf16[160,640]{1,0:T(8,128)(2,1)S(1)}, u32[]{:S(2)}, u32[]{:S(2)}) collective-permute-start(bf16[160,640]{1,0:T(8,128)(2,1)S(1)} %shard_map.91.refs_3_), channel_id=1, source_target_pairs={{0,4},{4,8},{8,12},{12,14},{14,10},{10,6},{6,2},{2,0},{1,5},{5,9},... | collective-permute-start | bytes 614408 | tf_op jit(solution)/shard_map/ppermute | solution.py:372
  (17 other events, 201.9 us)

commit v21 on v20

--- a/solution.py
+++ b/solution.py
@@ -18,7 +18,7 @@
     return jax.ShapeDtypeStruct(dims, kind)
 
 
-def call(kernel, ins, out_shape, scratch=(), vmem=16, flops=1, left=(), pinned=(), out=VMEM, ties=()):
+def call(kernel, ins, out_shape, scratch=(), vmem=16, flops=1, left=(), pinned=(), out=None, ties=()):
     count = len(ins)
 
     def body(*refs):
@@ -33,7 +33,7 @@
             for i, x in enumerate(ins)
         ]
         + [ANY] * len(ties),
-        out_specs=jax.tree.map(lambda _: out, out_shape),
+        out_specs=out or jax.tree.map(lambda _: VMEM, out_shape),
         scratch_shapes=list(scratch),
         compiler_params=pltpu.CompilerParams(vmem_limit_bytes=vmem << 20),
         cost_estimate=pl.CostEstimate(flops=flops, bytes_accessed=moved, transcendentals=0),
@@ -276,7 +276,7 @@
         flops=5 * frame_len * width,
         vmem=60,
         left=range(1, 6),
-        out=ANY,
+        out=(ANY, VMEM, VMEM),
     )
     first = lax.ppermute(passing, "groups", swap)
     normed, grads, stats = call(

time: 101 us -> 90.2 us (0.89)
  Pallas kernels: 29.9 us -> 19.6 us
    pallas_call x16, Pallas kernels: 29.9 us -> 19.6 us  [call(): pl.pallas_call(body if ties else kernel, out_shape=out_shape, in_specs=[S...]
  transfers between devices with their start and end apart: 35 -> 35, of which waited for: 23 -> 23; matrix products, arithmetic and copies ran while one was open for 0% -> 0% of each run, Pallas kernels for 14% -> 16%
where the time goes in v21:
time: 90.2 us; the launch traced here: 90.1 us
  waiting for transfers between devices  37.1 us (41%)
  starting transfers between devices  32.6 us (36%)
  Pallas kernels  19.6 us (22%)
    pallas_call x16, Pallas kernels, call(): pl.pallas_call(body if ties else kernel, out_shape=out_shape, in_specs=[S...  19.6 us
    ppermute x14, waiting for transfers between devices, send_on(): came[i][name] = lax.ppermute(block, 'gx', ahead if name == 'up' else behind)  18 us
    ppermute x14, starting transfers between devices, send_on(): came[i][name] = lax.ppermute(block, 'gx', ahead if name == 'up' else behind)  14.7 us
    ppermute x6, starting transfers between devices, shards(): up[i] = lax.ppermute(up[i], 'gx', ahead)  8.39 us
    ppermute x6, waiting for transfers between devices, shards(): down[i] = lax.ppermute(down[i], 'gx', behind)  7.92 us
    ppermute x6, waiting for transfers between devices, shards(): up[i] = lax.ppermute(up[i], 'gx', ahead)  4.61 us
    ppermute x6, starting transfers between devices, shards(): down[i] = lax.ppermute(down[i], 'gx', behind)  3.77 us
    ppermute x1, starting transfers between devices, shards(): first = lax.ppermute(passing, 'groups', swap)  3 us
  transfers between devices with their start and end apart: 35, of which 23 were waited for; matrix products, arithmetic and copies ran while one was open for 0% of the time, Pallas kernels for 16%

profile of v21, /device:TPU:0, one launch (start us, length us, event | category | flops | bytes accessed | tf_op | source)
XLA Modules:
  0.0 90.1 jit_solution(2819242301459718848)
XLA Ops:
  0.7 4.0 %shard_map.78 = (bf16[2,192,1280]{2,1,0:T(8,128)(2,1)}, bf16[160,640]{1,0:T(8,128)(2,1)}, bf16[160,640]{1,0:T(8,128)(2,1)}) custom-call(s32[8]{0:T(128)} %lengths.3, bf16[384,1280]{1,0:T(8,128)(2,1)} %bitcast.3, bf16[384,1280]{1,0:T(8,128)(2,1)} %bitcast.6, f32[1280]{0:T(1024)} %gain_from.1, bf16[160,1280]{1,0:T(8,128)(2,1)} %w_up.1, bf16[160,1280]{1,0:T(8,128)(2,1)} %w_down.1), custom_call_target="tpu_custom_call" | custom-call | flops 2457600 | bytes 4183072 | tf_op jit(solution)/shard_map/pallas_call | solution.py:28
  4.7 3.0 %collective-permute-start.14 = (bf16[2,192,1280]{2,1,0:T(8,128)(2,1)}, bf16[2,192,1280]{2,1,0:T(8,128)(2,1)S(1)}, u32[]{:S(2)}, u32[]{:S(2)}) collective-permute-start(bf16[2,192,1280]{2,1,0:T(8,128)(2,1)} %get-tuple-element.43), channel_id=1, source_target_pairs={{0,16},{16,0},{1,17},{17,1},{2,18},{18,2},{3,19},{19,3},{4,20},{20... | collective-permute-start | bytes 2949128 | tf_op jit(solution)/shard_map/ppermute | solution.py:281
  7.7 1.6 %collective-permute-start = (bf16[160,640]{1,0:T(8,128)(2,1)}, bf16[160,640]{1,0:T(8,128)(2,1)S(1)}, u32[]{:S(2)}, u32[]{:S(2)}) collective-permute-start(bf16[160,640]{1,0:T(8,128)(2,1)} %get-tuple-element.38.refs_0_), channel_id=1, source_target_pairs={{0,4},{4,8},{8,12},{12,14},{14,10},{10,6},{6,2},{2,0},{1,5},{5,9},... | collective-permute-start | bytes 614408 | tf_op jit(solution)/shard_map/ppermute | solution.py:295
  13.3 2.6 %collective-permute-done.refs_0_ = bf16[160,640]{1,0:T(8,128)(2,1)S(1)} collective-permute-done((bf16[160,640]{1,0:T(8,128)(2,1)}, bf16[160,640]{1,0:T(8,128)(2,1)S(1)}, u32[]{:S(2)}, u32[]{:S(2)}) %collective-permute-start) | collective-permute-done | bytes 204832 | tf_op jit(solution)/shard_map/ppermute | solution.py:295
  15.9 1.6 %collective-permute-start.4 = (bf16[160,640]{1,0:T(8,128)(2,1)S(1)}, bf16[160,640]{1,0:T(8,128)(2,1)S(1)}, u32[]{:S(2)}, u32[]{:S(2)}) collective-permute-start(bf16[160,640]{1,0:T(8,128)(2,1)S(1)} %shard_map.79.refs_2_), channel_id=1, source_target_pairs={{0,4},{4,8},{8,12},{12,14},{14,10},{10,6},{6,2},{2,0},{1,5},{5,9},... | collective-permute-start | bytes 614408 | tf_op jit(solution)/shard_map/ppermute | solution.py:295
  17.9 3.9 %collective-permute-done.1.refs_3_ = bf16[160,640]{1,0:T(8,128)(2,1)S(1)} collective-permute-done((bf16[160,640]{1,0:T(8,128)(2,1)}, bf16[160,640]{1,0:T(8,128)(2,1)S(1)}, u32[]{:S(2)}, u32[]{:S(2)}) %collective-permute-start.1) | collective-permute-done | bytes 204832 | tf_op jit(solution)/shard_map/ppermute | solution.py:296
  22.3 1.6 %collective-permute-start.6 = (bf16[160,640]{1,0:T(8,128)(2,1)S(1)}, bf16[160,640]{1,0:T(8,128)(2,1)S(1)}, u32[]{:S(2)}, u32[]{:S(2)}) collective-permute-start(bf16[160,640]{1,0:T(8,128)(2,1)S(1)} %collective-permute-done.2.refs_4_), channel_id=1, source_target_pairs={{0,4},{4,8},{8,12},{12,14},{14,10},{10,6},{6,2},{2,0},{1,5},{5,9},... | collective-permute-start | bytes 614408 | tf_op jit(solution)/shard_map/ppermute | solution.py:295
  24.7 1.6 %collective-permute-start.8 = (bf16[160,640]{1,0:T(8,128)(2,1)S(1)}, bf16[160,640]{1,0:T(8,128)(2,1)S(1)}, u32[]{:S(2)}, u32[]{:S(2)}) collective-permute-start(bf16[160,640]{1,0:T(8,128)(2,1)S(1)} %collective-permute-done.4.refs_6_), channel_id=1, source_target_pairs={{0,4},{4,8},{8,12},{12,14},{14,10},{10,6},{6,2},{2,0},{1,5},{5,9},... | collective-permute-start | bytes 614408 | tf_op jit(solution)/shard_map/ppermute | solution.py:295
  26.7 3.9 %collective-permute-done.5.refs_7_ = bf16[160,640]{1,0:T(8,128)(2,1)S(1)} collective-permute-done((bf16[160,640]{1,0:T(8,128)(2,1)S(1)}, bf16[160,640]{1,0:T(8,128)(2,1)S(1)}, u32[]{:S(2)}, u32[]{:S(2)}) %collective-permute-start.5) | collective-permute-done | bytes 204832 | tf_op jit(solution)/shard_map/ppermute | solution.py:296
  31.1 1.6 %collective-permute-start.11 = (bf16[160,640]{1,0:T(8,128)(2,1)S(1)}, bf16[160,640]{1,0:T(8,128)(2,1)S(1)}, u32[]{:S(2)}, u32[]{:S(2)}) collective-permute-start(bf16[160,640]{1,0:T(8,128)(2,1)S(1)} %collective-permute-done.6.refs_8_), channel_id=1, source_target_pairs={{0,4},{4,8},{8,12},{12,14},{14,10},{10,6},{6,2},{2,0},{1,5},{5,9},... | collective-permute-start | bytes 614408 | tf_op jit(solution)/shard_map/ppermute | solution.py:295
  33.9 1.6 %collective-permute-start.12 = (bf16[160,640]{1,0:T(8,128)(2,1)S(1)}, bf16[160,640]{1,0:T(8,128)(2,1)S(1)}, u32[]{:S(2)}, u32[]{:S(2)}) collective-permute-start(bf16[160,640]{1,0:T(8,128)(2,1)S(1)} %collective-permute-done.8.refs_10_), channel_id=1, source_target_pairs={{0,4},{4,8},{8,12},{12,14},{14,10},{10,6},{6,2},{2,0},{1,5},{5,9},... | collective-permute-start | bytes 614408 | tf_op jit(solution)/shard_map/ppermute | solution.py:304
  35.9 3.6 %shard_map.80 = (bf16[1280,640]{1,0:T(8,128)(2,1)S(1)}, bf16[1280,640]{1,0:T(8,128)(2,1)S(1)}) custom-call(bf16[160,640]{1,0:T(8,128)(2,1)S(1)} %copy-done.2, bf16[160,640]{1,0:T(8,128)(2,1)S(1)} %copy-done.3, bf16[160,640]{1,0:T(8,128)(2,1)S(1)} %shard_map.79.refs_2_, bf16[160,640]{1,0:T(8,128)(2,1)S(1)} %collective-permute-done.1.refs_3_, ...), custom_call_target="tpu_custom_call" | custom-call | flops 1 | bytes 5734400 | tf_op jit(solution)/shard_map/pallas_call | solution.py:28
  42.1 2.9 %shard_map.81 = (bf16[384,640]{1,0:T(8,128)(2,1)S(1)}, bf16[1280,640]{1,0:T(8,128)(2,1)S(1)}, bf16[1280,640]{1,0:T(8,128)(2,1)S(1)}, bf16[1280,640]{1,0:T(8,128)...) custom-call(bf16[384,1280]{1,0:T(8,128)(2,1)S(1)} %get-tuple-element.36.refs_1_.normed, ...), custom_call_target="tpu_custom_call" | custom-call | flops 1887436800 | bytes 11878400 | tf_op jit(solution)/shard_map/pallas_call | solution.py:28
  45.0 1.6 %collective-permute-start.16 = (bf16[160,640]{1,0:T(8,128)(2,1)S(1)}, bf16[160,640]{1,0:T(8,128)(2,1)S(1)}, u32[]{:S(2)}, u32[]{:S(2)}) collective-permute-start(bf16[160,640]{1,0:T(8,128)(2,1)S(1)} %get-tuple-element.47), channel_id=1, source_target_pairs={{0,4},{4,8},{8,12},{12,14},{14,10},{10,6},{6,2},{2,0},{1,5},{5,9},... | collective-permute-start | bytes 614408 | tf_op jit(solution)/shard_map/ppermute | solution.py:372
  47.1 2.7 %shard_map.83 = (bf16[384,640]{1,0:T(8,128)(2,1)S(1)}, bf16[1280,640]{1,0:T(8,128)(2,1)S(1)}, bf16[160,640]{1,0:T(8,128)(2,1)S(1)}, bf16[160,640]{1,0:T(8,128)(2,1)S(1)}) custom-call(bf16[2,192,1280]{2,1,0:T(8,128)(2,1)S(1)} %shard_map.82.first, bf16[2,192,1280]{2,1,0:T(8,128)(2,1)S(1)} %collective-permute-done.15.second, ...), custom_call_target="tpu_custom_call" | custom-call | flops 1887436800 | bytes 7782400 | tf_op jit(solution)/shard_map/pallas_call | solution.py:28
  49.8 1.6 %collective-permute-start.20 = (bf16[160,640]{1,0:T(8,128)(2,1)S(1)}, bf16[160,640]{1,0:T(8,128)(2,1)S(1)}, u32[]{:S(2)}, u32[]{:S(2)}) collective-permute-start(bf16[160,640]{1,0:T(8,128)(2,1)S(1)} %get-tuple-element.53), channel_id=1, source_target_pairs={{0,4},{4,8},{8,12},{12,14},{14,10},{10,6},{6,2},{2,0},{1,5},{5,9},... | collective-permute-start | bytes 614408 | tf_op jit(solution)/shard_map/ppermute | solution.py:372
  53.9 2.0 %shard_map.84 = (bf16[2,384,640]{2,1,0:T(8,128)(2,1)S(1)}, bf16[384,640]{1,0:T(8,128)(2,1)S(1)}, bf16[384,640]{1,0:T(8,128)(2,1)S(1)}) custom-call(bf16[384,640]{1,0:T(8,128)(2,1)S(1)} %get-tuple-element.42.refs_0_, bf16[384,640]{1,0:T(8,128)(2,1)S(1)} %get-tuple-element.46.refs_1_, bf16[1280,640]{1,0:T(8,128)(2,1)S(1)} %get-tuple-element.44.up.refs_2_, ...), custom_call_target="tpu_custom_call" | custom-call | flops 1258291200 | bytes 4587520 | tf_op jit(solution)/shard_map/pallas_call | solution.py:28
  58.4 1.6 %collective-permute-start.22 = (bf16[160,640]{1,0:T(8,128)(2,1)S(1)}, bf16[160,640]{1,0:T(8,128)(2,1)S(1)}, u32[]{:S(2)}, u32[]{:S(2)}) collective-permute-start(bf16[160,640]{1,0:T(8,128)(2,1)S(1)} %get-tuple-element.55.refs_3_), channel_id=1, source_target_pairs={{0,4},{4,8},{8,12},{12,14},{14,10},{10,6},{6,2},{2,0},{1,5},{5,9},... | collective-permute-start | bytes 614408 | tf_op jit(solution)/shard_map/ppermute | solution.py:372
  60.6 1.6 %collective-permute-start.27 = (bf16[160,640]{1,0:T(8,128)(2,1)S(1)}, bf16[160,640]{1,0:T(8,128)(2,1)S(1)}, u32[]{:S(2)}, u32[]{:S(2)}) collective-permute-start(bf16[160,640]{1,0:T(8,128)(2,1)S(1)} %get-tuple-element.58.refs_3_), channel_id=1, source_target_pairs={{0,4},{4,8},{8,12},{12,14},{14,10},{10,6},{6,2},{2,0},{1,5},{5,9},... | collective-permute-start | bytes 614408 | tf_op jit(solution)/shard_map/ppermute | solution.py:372
  62.7 3.8 %collective-permute-done.22.refs_1_ = bf16[160,640]{1,0:T(8,128)(2,1)S(1)} collective-permute-done((bf16[160,640]{1,0:T(8,128)(2,1)S(1)}, bf16[160,640]{1,0:T(8,128)(2,1)S(1)}, u32[]{:S(2)}, u32[]{:S(2)}) %collective-permute-start.22) | collective-permute-done | bytes 204832 | tf_op jit(solution)/shard_map/ppermute | solution.py:372
  66.4 1.6 %collective-permute-done.23.refs_2_ = bf16[160,640]{1,0:T(8,128)(2,1)S(1)} collective-permute-done((bf16[160,640]{1,0:T(8,128)(2,1)S(1)}, bf16[160,640]{1,0:T(8,128)(2,1)S(1)}, u32[]{:S(2)}, u32[]{:S(2)}) %collective-permute-start.23) | collective-permute-done | bytes 204832 | tf_op jit(solution)/shard_map/ppermute | solution.py:372
  76.2 2.2 %collective-permute-done.30.refs_1_ = bf16[160,640]{1,0:T(8,128)(2,1)S(1)} collective-permute-done((bf16[160,640]{1,0:T(8,128)(2,1)S(1)}, bf16[160,640]{1,0:T(8,128)(2,1)S(1)}, u32[]{:S(2)}, u32[]{:S(2)}) %collective-permute-start.30) | collective-permute-done | bytes 204832 | tf_op jit(solution)/shard_map/ppermute | solution.py:372
  80.0 2.2 %collective-permute-done.29.refs_2_ = bf16[160,640]{1,0:T(8,128)(2,1)S(1)} collective-permute-done((bf16[160,640]{1,0:T(8,128)(2,1)S(1)}, bf16[160,640]{1,0:T(8,128)(2,1)S(1)}, u32[]{:S(2)}, u32[]{:S(2)}) %collective-permute-start.29) | collective-permute-done | bytes 204832 | tf_op jit(solution)/shard_map/ppermute | solution.py:372
  83.0 1.9 %collective-permute-done.24.refs_2_ = bf16[384,640]{1,0:T(8,128)(2,1)S(1)} collective-permute-done((bf16[384,640]{1,0:T(8,128)(2,1)S(1)}, bf16[384,640]{1,0:T(8,128)(2,1)S(1)}, u32[]{:S(2)}, u32[]{:S(2)}) %collective-permute-start.24) | collective-permute-done | bytes 491552 | tf_op jit(solution)/shard_map/ppermute | solution.py:352
  (78 shorter events, 32.8 us)
Async XLA Ops:
  4.7 37.4 %collective-permute-start.14 = (bf16[2,192,1280]{2,1,0:T(8,128)(2,1)}, bf16[2,192,1280]{2,1,0:T(8,128)(2,1)S(1)}, u32[]{:S(2)}, u32[]{:S(2)}) collective-permute-start(bf16[2,192,1280]{2,1,0:T(8,128)(2,1)} %get-tuple-element.43), channel_id=1, source_target_pairs={{0,16},{16,0},{1,17},{17,1},{2,18},{18,2},{3,19},{19,3},{4,20},{20... | collective-permute-start | bytes 2949128 | tf_op jit(solution)/shard_map/ppermute | solution.py:281
  7.7 8.2 %collective-permute-start = (bf16[160,640]{1,0:T(8,128)(2,1)}, bf16[160,640]{1,0:T(8,128)(2,1)S(1)}, u32[]{:S(2)}, u32[]{:S(2)}) collective-permute-start(bf16[160,640]{1,0:T(8,128)(2,1)} %get-tuple-element.38.refs_0_), channel_id=1, source_target_pairs={{0,4},{4,8},{8,12},{12,14},{14,10},{10,6},{6,2},{2,0},{1,5},{5,9},... | collective-permute-start | bytes 614408 | tf_op jit(solution)/shard_map/ppermute | solution.py:295
  9.3 8.2 %collective-permute-start.3 = (bf16[160,640]{1,0:T(8,128)(2,1)}, bf16[160,640]{1,0:T(8,128)(2,1)S(1)}, u32[]{:S(2)}, u32[]{:S(2)}) collective-permute-start(bf16[160,640]{1,0:T(8,128)(2,1)} %get-tuple-element.39.refs_1_), channel_id=1, source_target_pairs={{4,0},{8,4},{12,8},{14,12},{10,14},{6,10},{2,6},{0,2},{5,1},{9,5},... | collective-permute-start | bytes 614408 | tf_op jit(solution)/shard_map/ppermute | solution.py:296
  9.7 12.2 %collective-permute-start.1 = (bf16[160,640]{1,0:T(8,128)(2,1)}, bf16[160,640]{1,0:T(8,128)(2,1)S(1)}, u32[]{:S(2)}, u32[]{:S(2)}) collective-permute-start(bf16[160,640]{1,0:T(8,128)(2,1)} %get-tuple-element.38.refs_0_), channel_id=1, source_target_pairs={{4,0},{8,4},{12,8},{14,12},{10,14},{6,10},{2,6},{0,2},{5,1},{9,5},... | collective-permute-start | bytes 614408 | tf_op jit(solution)/shard_map/ppermute | solution.py:296
  11.2 11.1 %collective-permute-start.2 = (bf16[160,640]{1,0:T(8,128)(2,1)}, bf16[160,640]{1,0:T(8,128)(2,1)S(1)}, u32[]{:S(2)}, u32[]{:S(2)}) collective-permute-start(bf16[160,640]{1,0:T(8,128)(2,1)} %get-tuple-element.39.refs_1_), channel_id=1, source_target_pairs={{0,4},{4,8},{8,12},{12,14},{14,10},{10,6},{6,2},{2,0},{1,5},{5,9},... | collective-permute-start | bytes 614408 | tf_op jit(solution)/shard_map/ppermute | solution.py:295
  15.9 8.8 %collective-permute-start.4 = (bf16[160,640]{1,0:T(8,128)(2,1)S(1)}, bf16[160,640]{1,0:T(8,128)(2,1)S(1)}, u32[]{:S(2)}, u32[]{:S(2)}) collective-permute-start(bf16[160,640]{1,0:T(8,128)(2,1)S(1)} %shard_map.79.refs_2_), channel_id=1, source_target_pairs={{0,4},{4,8},{8,12},{12,14},{14,10},{10,6},{6,2},{2,0},{1,5},{5,9},... | collective-permute-start | bytes 614408 | tf_op jit(solution)/shard_map/ppermute | solution.py:295
  17.5 8.8 %collective-permute-start.7 = (bf16[160,640]{1,0:T(8,128)(2,1)S(1)}, bf16[160,640]{1,0:T(8,128)(2,1)S(1)}, u32[]{:S(2)}, u32[]{:S(2)}) collective-permute-start(bf16[160,640]{1,0:T(8,128)(2,1)S(1)} %collective-permute-done.3.refs_5_), channel_id=1, source_target_pairs={{4,0},{8,4},{12,8},{14,12},{10,14},{6,10},{2,6},{0,2},{5,1},{9,5},... | collective-permute-start | bytes 614408 | tf_op jit(solution)/shard_map/ppermute | solution.py:296
  21.9 8.8 %collective-permute-start.5 = (bf16[160,640]{1,0:T(8,128)(2,1)S(1)}, bf16[160,640]{1,0:T(8,128)(2,1)S(1)}, u32[]{:S(2)}, u32[]{:S(2)}) collective-permute-start(bf16[160,640]{1,0:T(8,128)(2,1)S(1)} %collective-permute-done.1.refs_3_), channel_id=1, source_target_pairs={{4,0},{8,4},{12,8},{14,12},{10,14},{6,10},{2,6},{0,2},{5,1},{9,5},... | collective-permute-start | bytes 614408 | tf_op jit(solution)/shard_map/ppermute | solution.py:296
  22.3 8.8 %collective-permute-start.6 = (bf16[160,640]{1,0:T(8,128)(2,1)S(1)}, bf16[160,640]{1,0:T(8,128)(2,1)S(1)}, u32[]{:S(2)}, u32[]{:S(2)}) collective-permute-start(bf16[160,640]{1,0:T(8,128)(2,1)S(1)} %collective-permute-done.2.refs_4_), channel_id=1, source_target_pairs={{0,4},{4,8},{8,12},{12,14},{14,10},{10,6},{6,2},{2,0},{1,5},{5,9},... | collective-permute-start | bytes 614408 | tf_op jit(solution)/shard_map/ppermute | solution.py:295
  24.7 9.2 %collective-permute-start.8 = (bf16[160,640]{1,0:T(8,128)(2,1)S(1)}, bf16[160,640]{1,0:T(8,128)(2,1)S(1)}, u32[]{:S(2)}, u32[]{:S(2)}) collective-permute-start(bf16[160,640]{1,0:T(8,128)(2,1)S(1)} %collective-permute-done.4.refs_6_), channel_id=1, source_target_pairs={{0,4},{4,8},{8,12},{12,14},{14,10},{10,6},{6,2},{2,0},{1,5},{5,9},... | collective-permute-start | bytes 614408 | tf_op jit(solution)/shard_map/ppermute | solution.py:295
  26.3 9.2 %collective-permute-start.9 = (bf16[160,640]{1,0:T(8,128)(2,1)S(1)}, bf16[160,640]{1,0:T(8,128)(2,1)S(1)}, u32[]{:S(2)}, u32[]{:S(2)}) collective-permute-start(bf16[160,640]{1,0:T(8,128)(2,1)S(1)} %collective-permute-done.7.refs_9_), channel_id=1, source_target_pairs={{4,0},{8,4},{12,8},{14,12},{10,14},{6,10},{2,6},{0,2},{5,1},{9,5},... | collective-permute-start | bytes 614408 | tf_op jit(solution)/shard_map/ppermute | solution.py:296
  30.7 8.8 %collective-permute-start.10 = (bf16[160,640]{1,0:T(8,128)(2,1)S(1)}, bf16[160,640]{1,0:T(8,128)(2,1)S(1)}, u32[]{:S(2)}, u32[]{:S(2)}) collective-permute-start(bf16[160,640]{1,0:T(8,128)(2,1)S(1)} %collective-permute-done.5.refs_7_), channel_id=1, source_target_pairs={{4,0},{8,4},{12,8},{14,12},{10,14},{6,10},{2,6},{0,2},{5,1},{9,5},... | collective-permute-start | bytes 614408 | tf_op jit(solution)/shard_map/ppermute | solution.py:296
  31.1 8.4 %collective-permute-start.11 = (bf16[160,640]{1,0:T(8,128)(2,1)S(1)}, bf16[160,640]{1,0:T(8,128)(2,1)S(1)}, u32[]{:S(2)}, u32[]{:S(2)}) collective-permute-start(bf16[160,640]{1,0:T(8,128)(2,1)S(1)} %collective-permute-done.6.refs_8_), channel_id=1, source_target_pairs={{0,4},{4,8},{8,12},{12,14},{14,10},{10,6},{6,2},{2,0},{1,5},{5,9},... | collective-permute-start | bytes 614408 | tf_op jit(solution)/shard_map/ppermute | solution.py:295
  45.0 7.6 %collective-permute-start.16 = (bf16[160,640]{1,0:T(8,128)(2,1)S(1)}, bf16[160,640]{1,0:T(8,128)(2,1)S(1)}, u32[]{:S(2)}, u32[]{:S(2)}) collective-permute-start(bf16[160,640]{1,0:T(8,128)(2,1)S(1)} %get-tuple-element.47), channel_id=1, source_target_pairs={{0,4},{4,8},{8,12},{12,14},{14,10},{10,6},{6,2},{2,0},{1,5},{5,9},... | collective-permute-start | bytes 614408 | tf_op jit(solution)/shard_map/ppermute | solution.py:372
  46.7 7.3 %collective-permute-start.17 = (bf16[160,640]{1,0:T(8,128)(2,1)S(1)}, bf16[160,640]{1,0:T(8,128)(2,1)S(1)}, u32[]{:S(2)}, u32[]{:S(2)}) collective-permute-start(bf16[160,640]{1,0:T(8,128)(2,1)S(1)} %get-tuple-element.48), channel_id=1, source_target_pairs={{4,0},{8,4},{12,8},{14,12},{10,14},{6,10},{2,6},{0,2},{5,1},{9,5},... | collective-permute-start | bytes 614408 | tf_op jit(solution)/shard_map/ppermute | solution.py:372
  49.8 7.1 %collective-permute-start.20 = (bf16[160,640]{1,0:T(8,128)(2,1)S(1)}, bf16[160,640]{1,0:T(8,128)(2,1)S(1)}, u32[]{:S(2)}, u32[]{:S(2)}) collective-permute-start(bf16[160,640]{1,0:T(8,128)(2,1)S(1)} %get-tuple-element.53), channel_id=1, source_target_pairs={{0,4},{4,8},{8,12},{12,14},{14,10},{10,6},{6,2},{2,0},{1,5},{5,9},... | collective-permute-start | bytes 614408 | tf_op jit(solution)/shard_map/ppermute | solution.py:372
  55.9 14.3 %collective-permute-start.19 = (bf16[384,640]{1,0:T(8,128)(2,1)S(1)}, bf16[384,640]{1,0:T(8,128)(2,1)S(1)}, u32[]{:S(2)}, u32[]{:S(2)}) collective-permute-start(bf16[384,640]{1,0:T(8,128)(2,1)S(1)} %get-tuple-element.51), channel_id=1, source_target_pairs={{0,1},{1,0},{2,3},{3,2},{4,5},{5,4},{6,7},{7,6},{8,9},{9,8},{10,11... | collective-permute-start | bytes 1474568 | tf_op jit(solution)/shard_map/ppermute | solution.py:348
  58.4 8.1 %collective-permute-start.22 = (bf16[160,640]{1,0:T(8,128)(2,1)S(1)}, bf16[160,640]{1,0:T(8,128)(2,1)S(1)}, u32[]{:S(2)}, u32[]{:S(2)}) collective-permute-start(bf16[160,640]{1,0:T(8,128)(2,1)S(1)} %get-tuple-element.55.refs_3_), channel_id=1, source_target_pairs={{0,4},{4,8},{8,12},{12,14},{14,10},{10,6},{6,2},{2,0},{1,5},{5,9},... | collective-permute-start | bytes 614408 | tf_op jit(solution)/shard_map/ppermute | solution.py:372
  60.0 8.0 %collective-permute-start.23 = (bf16[160,640]{1,0:T(8,128)(2,1)S(1)}, bf16[160,640]{1,0:T(8,128)(2,1)S(1)}, u32[]{:S(2)}, u32[]{:S(2)}) collective-permute-start(bf16[160,640]{1,0:T(8,128)(2,1)S(1)} %get-tuple-element.56), channel_id=1, source_target_pairs={{4,0},{8,4},{12,8},{14,12},{10,14},{6,10},{2,6},{0,2},{5,1},{9,5},... | collective-permute-start | bytes 614408 | tf_op jit(solution)/shard_map/ppermute | solution.py:372
  60.6 10.3 %collective-permute-start.27 = (bf16[160,640]{1,0:T(8,128)(2,1)S(1)}, bf16[160,640]{1,0:T(8,128)(2,1)S(1)}, u32[]{:S(2)}, u32[]{:S(2)}) collective-permute-start(bf16[160,640]{1,0:T(8,128)(2,1)S(1)} %get-tuple-element.58.refs_3_), channel_id=1, source_target_pairs={{0,4},{4,8},{8,12},{12,14},{14,10},{10,6},{6,2},{2,0},{1,5},{5,9},... | collective-permute-start | bytes 614408 | tf_op jit(solution)/shard_map/ppermute | solution.py:372
  62.2 10.0 %collective-permute-start.28 = (bf16[160,640]{1,0:T(8,128)(2,1)S(1)}, bf16[160,640]{1,0:T(8,128)(2,1)S(1)}, u32[]{:S(2)}, u32[]{:S(2)}) collective-permute-start(bf16[160,640]{1,0:T(8,128)(2,1)S(1)} %get-tuple-element.62), channel_id=1, source_target_pairs={{4,0},{8,4},{12,8},{14,12},{10,14},{6,10},{2,6},{0,2},{5,1},{9,5},... | collective-permute-start | bytes 614408 | tf_op jit(solution)/shard_map/ppermute | solution.py:372
  70.2 12.7 %collective-permute-start.18 = (bf16[384,640]{1,0:T(8,128)(2,1)S(1)}, bf16[384,640]{1,0:T(8,128)(2,1)S(1)}, u32[]{:S(2)}, u32[]{:S(2)}) collective-permute-start(bf16[384,640]{1,0:T(8,128)(2,1)S(1)} %get-tuple-element.50), channel_id=1, source_target_pairs={{0,1},{1,0},{2,3},{3,2},{4,5},{5,4},{6,7},{7,6},{8,9},{9,8},{10,11... | collective-permute-start | bytes 1474568 | tf_op jit(solution)/shard_map/ppermute | solution.py:401
  70.8 14.1 %collective-permute-start.24 = (bf16[384,640]{1,0:T(8,128)(2,1)S(1)}, bf16[384,640]{1,0:T(8,128)(2,1)S(1)}, u32[]{:S(2)}, u32[]{:S(2)}) collective-permute-start(bf16[384,640]{1,0:T(8,128)(2,1)S(1)} %shard_map.88.refs_3_), channel_id=1, source_target_pairs={{0,16},{16,0},{1,17},{17,1},{2,18},{18,2},{3,19},{19,3},{4,20},{20... | collective-permute-start | bytes 1474568 | tf_op jit(solution)/shard_map/ppermute | solution.py:352
  78.4 7.2 %collective-permute-start.32 = (bf16[160,640]{1,0:T(8,128)(2,1)S(1)}, bf16[160,640]{1,0:T(8,128)(2,1)S(1)}, u32[]{:S(2)}, u32[]{:S(2)}) collective-permute-start(bf16[160,640]{1,0:T(8,128)(2,1)S(1)} %shard_map.91.refs_3_), channel_id=1, source_target_pairs={{0,4},{4,8},{8,12},{12,14},{14,10},{10,6},{6,2},{2,0},{1,5},{5,9},... | collective-permute-start | bytes 614408 | tf_op jit(solution)/shard_map/ppermute | solution.py:372
  (17 other events, 160.3 us)

commit v22 on v21

--- a/solution.py
+++ b/solution.py
@@ -18,7 +18,7 @@
     return jax.ShapeDtypeStruct(dims, kind)
 
 
-def call(kernel, ins, out_shape, scratch=(), vmem=16, flops=1, left=(), pinned=(), out=None, ties=()):
+def call(kernel, ins, out_shape, scratch=(), vmem=16, flops=1, left=(), pinned=(), ties=()):
     count = len(ins)
 
     def body(*refs):
@@ -33,7 +33,7 @@
             for i, x in enumerate(ins)
         ]
         + [ANY] * len(ties),
-        out_specs=out or jax.tree.map(lambda _: VMEM, out_shape),
+        out_specs=jax.tree.map(lambda _: VMEM, out_shape),
         scratch_shapes=list(scratch),
         compiler_params=pltpu.CompilerParams(vmem_limit_bytes=vmem << 20),
         cost_estimate=pl.CostEstimate(flops=flops, bytes_accessed=moved, transcendentals=0),
@@ -87,32 +87,27 @@
     return jnp.where(index < length, rows.astype(F32), 0.0).astype(BF16)
 
 
-def first_kernel(lengths, frames, out_grad, gain_from, w_up, w_down, *refs):
-    passing, mine_up, mine_down, rows, grads, normed, gain, sems = refs
+def first_kernel(
+    lengths, frames, out_grad, gain, w_up, w_down, passing, mine_up, mine_down, sems, rows, grads
+):
     half, quarter = rows.shape[0], mine_up.shape[1]
     start = pl.multiple_of(lax.axis_index("gy") * half, half)
     columns = pl.ds(pl.multiple_of(lax.axis_index("groups") * quarter, quarter), quarter)
     moves = (
-        (gain_from, gain),
         (frames.at[pl.ds(start, half)], rows),
         (out_grad.at[pl.ds(start, half)], grads),
         (w_up.at[:, columns], mine_up),
         (w_down.at[:, columns], mine_down),
-        (normed, passing.at[0]),
-        (grads, passing.at[1]),
     )
     copies = [pltpu.make_async_copy(*move, sems.at[i]) for i, move in enumerate(moves)]
-    for copy in copies[:5]:
+    for copy in copies:
         copy.start()
+    copies[0].wait()
+    passing[0] = norm_rows(rows[...], gain)[0]
+    copies[1].wait()
+    passing[1] = mask_rows(grads[...], start, lengths[lax.axis_index("gx")])
     copies[2].wait()
-    grads[...] = mask_rows(grads[...], start, lengths[lax.axis_index("gx")])
-    copies[6].start()
-    copies[0].wait()
-    copies[1].wait()
-    normed[...] = norm_rows(rows[...], gain)[0]
-    copies[5].start()
-    for copy in copies[3:]:
-        copy.wait()
+    copies[3].wait()
 
 
 def norm_kernel(lengths, frames, out_grad, gain, normed, grads, stats):
@@ -271,12 +266,10 @@
         first_kernel,
         (lengths, frames, out_grad, ln_gain, w_up, w_down),
         (shape((2, half_rows, width), BF16), block_of, block_of),
-        [pltpu.VMEM((half_rows, width), BF16)] * 3
-        + [pltpu.VMEM((width,), F32), pltpu.SemaphoreType.DMA((7,))],
+        [pltpu.SemaphoreType.DMA((4,))] + [pltpu.VMEM((half_rows, width), BF16)] * 2,
         flops=5 * frame_len * width,
         vmem=60,
-        left=range(1, 6),
-        out=(ANY, VMEM, VMEM),
+        left=(1, 2, 4, 5),
     )
     first = lax.ppermute(passing, "groups", swap)
     normed, grads, stats = call(
@@ -388,9 +381,9 @@
             send_on(i, blocks, names)
             return blocks[0]
 
-        send_on(0, blocks_own, ("up", "down"))
         send_on(1, blocks_other, ("up", "down"))
-        keep, send, parts = own_d_norm(*came[0].values())
+        keep, send, parts = own_d_norm()
+        send_on(0, [hold(block, keep) for block in blocks_own], ("up", "down"))
         tie = hop(1, 1, keep)
         tie = hop(0, 1, tie)
         tie = hop(1, 2, tie)

time: 90.2 us -> 87.4 us (0.969)
  waiting for transfers between devices: 37.1 us -> 34.5 us
    ppermute x14, waiting for transfers between devices: 18 us -> 15.4 us  [send_on(): came[i][name] = lax.ppermute(block, 'gx', ahead if name == 'up' else behind)]
  transfers between devices with their start and end apart: 35 -> 35, of which waited for: 23 -> 23; matrix products, arithmetic and copies ran while one was open for 0% -> 0% of each run, Pallas kernels for 16% -> 13%
where the time goes in v22:
time: 87.4 us; the launch traced here: 87.2 us
  waiting for transfers between devices  34.5 us (39%)
  starting transfers between devices  32.9 us (38%)
  Pallas kernels  18.9 us (22%)
    pallas_call x16, Pallas kernels, call(): pl.pallas_call(body if ties else kernel, out_shape=out_shape, in_specs=[S...  18.9 us
    ppermute x14, waiting for transfers between devices, send_on(): came[i][name] = lax.ppermute(block, 'gx', ahead if name == 'up' else behind)  15.4 us
    ppermute x14, starting transfers between devices, send_on(): came[i][name] = lax.ppermute(block, 'gx', ahead if name == 'up' else behind)  14.5 us
    ppermute x6, starting transfers between devices, shards(): up[i] = lax.ppermute(up[i], 'gx', ahead)  8.39 us
    ppermute x6, waiting for transfers between devices, shards(): down[i] = lax.ppermute(down[i], 'gx', behind)  7.92 us
    ppermute x6, waiting for transfers between devices, shards(): up[i] = lax.ppermute(up[i], 'gx', ahead)  4.61 us
    ppermute x6, starting transfers between devices, shards(): down[i] = lax.ppermute(down[i], 'gx', behind)  3.77 us
    ppermute x1, starting transfers between devices, shards(): first = lax.ppermute(passing, 'groups', swap)  3 us
  transfers between devices with their start and end apart: 35, of which 23 were waited for; matrix products, arithmetic and copies ran while one was open for 0% of the time, Pallas kernels for 13%

profile of v22, /device:TPU:0, one launch (start us, length us, event | category | flops | bytes accessed | tf_op | source)
XLA Modules:
  0.0 87.2 jit_solution(17959476229794514168)
XLA Ops:
  0.7 3.4 %shard_map.78 = (bf16[2,192,1280]{2,1,0:T(8,128)(2,1)}, bf16[160,640]{1,0:T(8,128)(2,1)}, bf16[160,640]{1,0:T(8,128)(2,1)}) custom-call(s32[8]{0:T(128)} %lengths.3, bf16[384,1280]{1,0:T(8,128)(2,1)} %bitcast.3, bf16[384,1280]{1,0:T(8,128)(2,1)} %bitcast.6, f32[1280]{0:T(1024)} %gain.3, bf16[160,1280]{1,0:T(8,128)(2,1)} %w_up.1, bf16[160,1280]{1,0:T(8,128)(2,1)} %w_down.1), custom_call_target="tpu_custom_call" | custom-call | flops 2457600 | bytes 4183072 | tf_op jit(solution)/shard_map/pallas_call | solution.py:28
  4.1 3.0 %collective-permute-start.14 = (bf16[2,192,1280]{2,1,0:T(8,128)(2,1)}, bf16[2,192,1280]{2,1,0:T(8,128)(2,1)S(1)}, u32[]{:S(2)}, u32[]{:S(2)}) collective-permute-start(bf16[2,192,1280]{2,1,0:T(8,128)(2,1)} %get-tuple-element.43), channel_id=1, source_target_pairs={{0,16},{16,0},{1,17},{17,1},{2,18},{18,2},{3,19},{19,3},{4,20},{20... | collective-permute-start | bytes 2949128 | tf_op jit(solution)/shard_map/ppermute | solution.py:274
  7.1 1.6 %collective-permute-start = (bf16[160,640]{1,0:T(8,128)(2,1)}, bf16[160,640]{1,0:T(8,128)(2,1)S(1)}, u32[]{:S(2)}, u32[]{:S(2)}) collective-permute-start(bf16[160,640]{1,0:T(8,128)(2,1)} %get-tuple-element.38.refs_0_), channel_id=1, source_target_pairs={{0,4},{4,8},{8,12},{12,14},{14,10},{10,6},{6,2},{2,0},{1,5},{5,9},... | collective-permute-start | bytes 614408 | tf_op jit(solution)/shard_map/ppermute | solution.py:288
  12.6 2.6 %collective-permute-done.refs_0_ = bf16[160,640]{1,0:T(8,128)(2,1)S(1)} collective-permute-done((bf16[160,640]{1,0:T(8,128)(2,1)}, bf16[160,640]{1,0:T(8,128)(2,1)S(1)}, u32[]{:S(2)}, u32[]{:S(2)}) %collective-permute-start) | collective-permute-done | bytes 204832 | tf_op jit(solution)/shard_map/ppermute | solution.py:288
  15.3 1.6 %collective-permute-start.4 = (bf16[160,640]{1,0:T(8,128)(2,1)S(1)}, bf16[160,640]{1,0:T(8,128)(2,1)S(1)}, u32[]{:S(2)}, u32[]{:S(2)}) collective-permute-start(bf16[160,640]{1,0:T(8,128)(2,1)S(1)} %shard_map.79.refs_2_), channel_id=1, source_target_pairs={{0,4},{4,8},{8,12},{12,14},{14,10},{10,6},{6,2},{2,0},{1,5},{5,9},... | collective-permute-start | bytes 614408 | tf_op jit(solution)/shard_map/ppermute | solution.py:288
  17.3 3.9 %collective-permute-done.1.refs_3_ = bf16[160,640]{1,0:T(8,128)(2,1)S(1)} collective-permute-done((bf16[160,640]{1,0:T(8,128)(2,1)}, bf16[160,640]{1,0:T(8,128)(2,1)S(1)}, u32[]{:S(2)}, u32[]{:S(2)}) %collective-permute-start.1) | collective-permute-done | bytes 204832 | tf_op jit(solution)/shard_map/ppermute | solution.py:289
  21.7 1.6 %collective-permute-start.6 = (bf16[160,640]{1,0:T(8,128)(2,1)S(1)}, bf16[160,640]{1,0:T(8,128)(2,1)S(1)}, u32[]{:S(2)}, u32[]{:S(2)}) collective-permute-start(bf16[160,640]{1,0:T(8,128)(2,1)S(1)} %collective-permute-done.2.refs_4_), channel_id=1, source_target_pairs={{0,4},{4,8},{8,12},{12,14},{14,10},{10,6},{6,2},{2,0},{1,5},{5,9},... | collective-permute-start | bytes 614408 | tf_op jit(solution)/shard_map/ppermute | solution.py:288
  24.1 1.6 %collective-permute-start.8 = (bf16[160,640]{1,0:T(8,128)(2,1)S(1)}, bf16[160,640]{1,0:T(8,128)(2,1)S(1)}, u32[]{:S(2)}, u32[]{:S(2)}) collective-permute-start(bf16[160,640]{1,0:T(8,128)(2,1)S(1)} %collective-permute-done.4.refs_6_), channel_id=1, source_target_pairs={{0,4},{4,8},{8,12},{12,14},{14,10},{10,6},{6,2},{2,0},{1,5},{5,9},... | collective-permute-start | bytes 614408 | tf_op jit(solution)/shard_map/ppermute | solution.py:288
  26.1 3.9 %collective-permute-done.5.refs_7_ = bf16[160,640]{1,0:T(8,128)(2,1)S(1)} collective-permute-done((bf16[160,640]{1,0:T(8,128)(2,1)S(1)}, bf16[160,640]{1,0:T(8,128)(2,1)S(1)}, u32[]{:S(2)}, u32[]{:S(2)}) %collective-permute-start.5) | collective-permute-done | bytes 204832 | tf_op jit(solution)/shard_map/ppermute | solution.py:289
  30.5 1.6 %collective-permute-start.11 = (bf16[160,640]{1,0:T(8,128)(2,1)S(1)}, bf16[160,640]{1,0:T(8,128)(2,1)S(1)}, u32[]{:S(2)}, u32[]{:S(2)}) collective-permute-start(bf16[160,640]{1,0:T(8,128)(2,1)S(1)} %collective-permute-done.6.refs_8_), channel_id=1, source_target_pairs={{0,4},{4,8},{8,12},{12,14},{14,10},{10,6},{6,2},{2,0},{1,5},{5,9},... | collective-permute-start | bytes 614408 | tf_op jit(solution)/shard_map/ppermute | solution.py:288
  33.3 1.6 %collective-permute-start.12 = (bf16[160,640]{1,0:T(8,128)(2,1)S(1)}, bf16[160,640]{1,0:T(8,128)(2,1)S(1)}, u32[]{:S(2)}, u32[]{:S(2)}) collective-permute-start(bf16[160,640]{1,0:T(8,128)(2,1)S(1)} %collective-permute-done.8.refs_10_), channel_id=1, source_target_pairs={{0,4},{4,8},{8,12},{12,14},{14,10},{10,6},{6,2},{2,0},{1,5},{5,9},... | collective-permute-start | bytes 614408 | tf_op jit(solution)/shard_map/ppermute | solution.py:297
  35.3 3.6 %shard_map.80 = (bf16[1280,640]{1,0:T(8,128)(2,1)S(1)}, bf16[1280,640]{1,0:T(8,128)(2,1)S(1)}) custom-call(bf16[160,640]{1,0:T(8,128)(2,1)S(1)} %copy-done.2, bf16[160,640]{1,0:T(8,128)(2,1)S(1)} %copy-done.3, bf16[160,640]{1,0:T(8,128)(2,1)S(1)} %shard_map.79.refs_2_, bf16[160,640]{1,0:T(8,128)(2,1)S(1)} %collective-permute-done.1.refs_3_, ...), custom_call_target="tpu_custom_call" | custom-call | flops 1 | bytes 5734400 | tf_op jit(solution)/shard_map/pallas_call | solution.py:28
  41.5 2.9 %shard_map.81 = (bf16[384,640]{1,0:T(8,128)(2,1)S(1)}, bf16[1280,640]{1,0:T(8,128)(2,1)S(1)}, bf16[1280,640]{1,0:T(8,128)(2,1)S(1)}, bf16[1280,640]{1,0:T(8,128)...) custom-call(bf16[384,1280]{1,0:T(8,128)(2,1)S(1)} %get-tuple-element.36.refs_1_.normed, ...), custom_call_target="tpu_custom_call" | custom-call | flops 1887436800 | bytes 11878400 | tf_op jit(solution)/shard_map/pallas_call | solution.py:28
  44.4 2.7 %shard_map.83 = (bf16[384,640]{1,0:T(8,128)(2,1)S(1)}, bf16[1280,640]{1,0:T(8,128)(2,1)S(1)}, bf16[160,640]{1,0:T(8,128)(2,1)S(1)}, bf16[160,640]{1,0:T(8,128)(2,1)S(1)}) custom-call(bf16[2,192,1280]{2,1,0:T(8,128)(2,1)S(1)} %shard_map.82.first, bf16[2,192,1280]{2,1,0:T(8,128)(2,1)S(1)} %collective-permute-done.15.second, ...), custom_call_target="tpu_custom_call" | custom-call | flops 1887436800 | bytes 7782400 | tf_op jit(solution)/shard_map/pallas_call | solution.py:28
  47.1 1.6 %collective-permute-start.18 = (bf16[160,640]{1,0:T(8,128)(2,1)S(1)}, bf16[160,640]{1,0:T(8,128)(2,1)S(1)}, u32[]{:S(2)}, u32[]{:S(2)}) collective-permute-start(bf16[160,640]{1,0:T(8,128)(2,1)S(1)} %get-tuple-element.51), channel_id=1, source_target_pairs={{0,4},{4,8},{8,12},{12,14},{14,10},{10,6},{6,2},{2,0},{1,5},{5,9},... | collective-permute-start | bytes 614408 | tf_op jit(solution)/shard_map/ppermute | solution.py:365
  49.2 2.0 %shard_map.84 = (bf16[2,384,640]{2,1,0:T(8,128)(2,1)S(1)}, bf16[384,640]{1,0:T(8,128)(2,1)S(1)}, bf16[384,640]{1,0:T(8,128)(2,1)S(1)}) custom-call(bf16[384,640]{1,0:T(8,128)(2,1)S(1)} %get-tuple-element.42.d_pre_own, bf16[384,640]{1,0:T(8,128)(2,1)S(1)} %get-tuple-element.46.d_pre_other, bf16[1280,640]{1,0:T(8,128)(2,1)S(1)} %get-tuple-element.44.up), custom_call_target="tpu_custom_call" | custom-call | flops 1258291200 | bytes 4587520 | tf_op jit(solution)/shard_map/pallas_call | solution.py:28
  51.3 1.6 %collective-permute-start.22 = (bf16[160,640]{1,0:T(8,128)(2,1)S(1)}, bf16[160,640]{1,0:T(8,128)(2,1)S(1)}, u32[]{:S(2)}, u32[]{:S(2)}) collective-permute-start(bf16[160,640]{1,0:T(8,128)(2,1)S(1)} %shard_map.86), channel_id=1, source_target_pairs={{0,4},{4,8},{8,12},{12,14},{14,10},{10,6},{6,2},{2,0},{1,5},{5,9},... | collective-permute-start | bytes 614408 | tf_op jit(solution)/shard_map/ppermute | solution.py:365
  56.3 1.6 %collective-permute-start.20 = (bf16[160,640]{1,0:T(8,128)(2,1)S(1)}, bf16[160,640]{1,0:T(8,128)(2,1)S(1)}, u32[]{:S(2)}, u32[]{:S(2)}) collective-permute-start(bf16[160,640]{1,0:T(8,128)(2,1)S(1)} %get-tuple-element.53.refs_3_), channel_id=1, source_target_pairs={{0,4},{4,8},{8,12},{12,14},{14,10},{10,6},{6,2},{2,0},{1,5},{5,9},... | collective-permute-start | bytes 614408 | tf_op jit(solution)/shard_map/ppermute | solution.py:365
  59.3 1.6 %collective-permute-done.23.refs_2_ = bf16[160,640]{1,0:T(8,128)(2,1)S(1)} collective-permute-done((bf16[160,640]{1,0:T(8,128)(2,1)S(1)}, bf16[160,640]{1,0:T(8,128)(2,1)S(1)}, u32[]{:S(2)}, u32[]{:S(2)}) %collective-permute-start.23) | collective-permute-done | bytes 204832 | tf_op jit(solution)/shard_map/ppermute | solution.py:365
  61.0 1.6 %collective-permute-start.27 = (bf16[160,640]{1,0:T(8,128)(2,1)S(1)}, bf16[160,640]{1,0:T(8,128)(2,1)S(1)}, u32[]{:S(2)}, u32[]{:S(2)}) collective-permute-start(bf16[160,640]{1,0:T(8,128)(2,1)S(1)} %get-tuple-element.58.refs_3_), channel_id=1, source_target_pairs={{0,4},{4,8},{8,12},{12,14},{14,10},{10,6},{6,2},{2,0},{1,5},{5,9},... | collective-permute-start | bytes 614408 | tf_op jit(solution)/shard_map/ppermute | solution.py:365
  65.5 1.7 %collective-permute-start.25 = (bf16[160,640]{1,0:T(8,128)(2,1)S(1)}, bf16[160,640]{1,0:T(8,128)(2,1)S(1)}, u32[]{:S(2)}, u32[]{:S(2)}) collective-permute-start(bf16[160,640]{1,0:T(8,128)(2,1)S(1)} %get-tuple-element.59.refs_2_), channel_id=1, source_target_pairs={{0,4},{4,8},{8,12},{12,14},{14,10},{10,6},{6,2},{2,0},{1,5},{5,9},... | collective-permute-start | bytes 614408 | tf_op jit(solution)/shard_map/ppermute | solution.py:365
  74.1 2.5 %collective-permute-done.30.refs_1_ = bf16[160,640]{1,0:T(8,128)(2,1)S(1)} collective-permute-done((bf16[160,640]{1,0:T(8,128)(2,1)S(1)}, bf16[160,640]{1,0:T(8,128)(2,1)S(1)}, u32[]{:S(2)}, u32[]{:S(2)}) %collective-permute-start.30) | collective-permute-done | bytes 204832 | tf_op jit(solution)/shard_map/ppermute | solution.py:365
  76.7 1.6 %collective-permute-start.32 = (bf16[160,640]{1,0:T(8,128)(2,1)S(1)}, bf16[160,640]{1,0:T(8,128)(2,1)S(1)}, u32[]{:S(2)}, u32[]{:S(2)}) collective-permute-start(bf16[160,640]{1,0:T(8,128)(2,1)S(1)} %shard_map.93.refs_3_), channel_id=1, source_target_pairs={{0,4},{4,8},{8,12},{12,14},{14,10},{10,6},{6,2},{2,0},{1,5},{5,9},... | collective-permute-start | bytes 614408 | tf_op jit(solution)/shard_map/ppermute | solution.py:365
  80.6 2.3 %collective-permute-done.24.refs_2_ = bf16[384,640]{1,0:T(8,128)(2,1)S(1)} collective-permute-done((bf16[384,640]{1,0:T(8,128)(2,1)S(1)}, bf16[384,640]{1,0:T(8,128)(2,1)S(1)}, u32[]{:S(2)}, u32[]{:S(2)}) %collective-permute-start.24) | collective-permute-done | bytes 491552 | tf_op jit(solution)/shard_map/ppermute | solution.py:345
  (80 shorter events, 32.6 us)
Async XLA Ops:
  4.1 37.4 %collective-permute-start.14 = (bf16[2,192,1280]{2,1,0:T(8,128)(2,1)}, bf16[2,192,1280]{2,1,0:T(8,128)(2,1)S(1)}, u32[]{:S(2)}, u32[]{:S(2)}) collective-permute-start(bf16[2,192,1280]{2,1,0:T(8,128)(2,1)} %get-tuple-element.43), channel_id=1, source_target_pairs={{0,16},{16,0},{1,17},{17,1},{2,18},{18,2},{3,19},{19,3},{4,20},{20... | collective-permute-start | bytes 2949128 | tf_op jit(solution)/shard_map/ppermute | solution.py:274
  7.1 8.2 %collective-permute-start = (bf16[160,640]{1,0:T(8,128)(2,1)}, bf16[160,640]{1,0:T(8,128)(2,1)S(1)}, u32[]{:S(2)}, u32[]{:S(2)}) collective-permute-start(bf16[160,640]{1,0:T(8,128)(2,1)} %get-tuple-element.38.refs_0_), channel_id=1, source_target_pairs={{0,4},{4,8},{8,12},{12,14},{14,10},{10,6},{6,2},{2,0},{1,5},{5,9},... | collective-permute-start | bytes 614408 | tf_op jit(solution)/shard_map/ppermute | solution.py:288
  8.7 8.2 %collective-permute-start.3 = (bf16[160,640]{1,0:T(8,128)(2,1)}, bf16[160,640]{1,0:T(8,128)(2,1)S(1)}, u32[]{:S(2)}, u32[]{:S(2)}) collective-permute-start(bf16[160,640]{1,0:T(8,128)(2,1)} %get-tuple-element.39.refs_1_), channel_id=1, source_target_pairs={{4,0},{8,4},{12,8},{14,12},{10,14},{6,10},{2,6},{0,2},{5,1},{9,5},... | collective-permute-start | bytes 614408 | tf_op jit(solution)/shard_map/ppermute | solution.py:289
  9.1 12.2 %collective-permute-start.1 = (bf16[160,640]{1,0:T(8,128)(2,1)}, bf16[160,640]{1,0:T(8,128)(2,1)S(1)}, u32[]{:S(2)}, u32[]{:S(2)}) collective-permute-start(bf16[160,640]{1,0:T(8,128)(2,1)} %get-tuple-element.38.refs_0_), channel_id=1, source_target_pairs={{4,0},{8,4},{12,8},{14,12},{10,14},{6,10},{2,6},{0,2},{5,1},{9,5},... | collective-permute-start | bytes 614408 | tf_op jit(solution)/shard_map/ppermute | solution.py:289
  10.6 11.1 %collective-permute-start.2 = (bf16[160,640]{1,0:T(8,128)(2,1)}, bf16[160,640]{1,0:T(8,128)(2,1)S(1)}, u32[]{:S(2)}, u32[]{:S(2)}) collective-permute-start(bf16[160,640]{1,0:T(8,128)(2,1)} %get-tuple-element.39.refs_1_), channel_id=1, source_target_pairs={{0,4},{4,8},{8,12},{12,14},{14,10},{10,6},{6,2},{2,0},{1,5},{5,9},... | collective-permute-start | bytes 614408 | tf_op jit(solution)/shard_map/ppermute | solution.py:288
  15.3 8.8 %collective-permute-start.4 = (bf16[160,640]{1,0:T(8,128)(2,1)S(1)}, bf16[160,640]{1,0:T(8,128)(2,1)S(1)}, u32[]{:S(2)}, u32[]{:S(2)}) collective-permute-start(bf16[160,640]{1,0:T(8,128)(2,1)S(1)} %shard_map.79.refs_2_), channel_id=1, source_target_pairs={{0,4},{4,8},{8,12},{12,14},{14,10},{10,6},{6,2},{2,0},{1,5},{5,9},... | collective-permute-start | bytes 614408 | tf_op jit(solution)/shard_map/ppermute | solution.py:288
  16.9 8.8 %collective-permute-start.7 = (bf16[160,640]{1,0:T(8,128)(2,1)S(1)}, bf16[160,640]{1,0:T(8,128)(2,1)S(1)}, u32[]{:S(2)}, u32[]{:S(2)}) collective-permute-start(bf16[160,640]{1,0:T(8,128)(2,1)S(1)} %collective-permute-done.3.refs_5_), channel_id=1, source_target_pairs={{4,0},{8,4},{12,8},{14,12},{10,14},{6,10},{2,6},{0,2},{5,1},{9,5},... | collective-permute-start | bytes 614408 | tf_op jit(solution)/shard_map/ppermute | solution.py:289
  21.3 8.8 %collective-permute-start.5 = (bf16[160,640]{1,0:T(8,128)(2,1)S(1)}, bf16[160,640]{1,0:T(8,128)(2,1)S(1)}, u32[]{:S(2)}, u32[]{:S(2)}) collective-permute-start(bf16[160,640]{1,0:T(8,128)(2,1)S(1)} %collective-permute-done.1.refs_3_), channel_id=1, source_target_pairs={{4,0},{8,4},{12,8},{14,12},{10,14},{6,10},{2,6},{0,2},{5,1},{9,5},... | collective-permute-start | bytes 614408 | tf_op jit(solution)/shard_map/ppermute | solution.py:289
  21.7 8.8 %collective-permute-start.6 = (bf16[160,640]{1,0:T(8,128)(2,1)S(1)}, bf16[160,640]{1,0:T(8,128)(2,1)S(1)}, u32[]{:S(2)}, u32[]{:S(2)}) collective-permute-start(bf16[160,640]{1,0:T(8,128)(2,1)S(1)} %collective-permute-done.2.refs_4_), channel_id=1, source_target_pairs={{0,4},{4,8},{8,12},{12,14},{14,10},{10,6},{6,2},{2,0},{1,5},{5,9},... | collective-permute-start | bytes 614408 | tf_op jit(solution)/shard_map/ppermute | solution.py:288
  24.1 9.2 %collective-permute-start.8 = (bf16[160,640]{1,0:T(8,128)(2,1)S(1)}, bf16[160,640]{1,0:T(8,128)(2,1)S(1)}, u32[]{:S(2)}, u32[]{:S(2)}) collective-permute-start(bf16[160,640]{1,0:T(8,128)(2,1)S(1)} %collective-permute-done.4.refs_6_), channel_id=1, source_target_pairs={{0,4},{4,8},{8,12},{12,14},{14,10},{10,6},{6,2},{2,0},{1,5},{5,9},... | collective-permute-start | bytes 614408 | tf_op jit(solution)/shard_map/ppermute | solution.py:288
  25.7 9.2 %collective-permute-start.9 = (bf16[160,640]{1,0:T(8,128)(2,1)S(1)}, bf16[160,640]{1,0:T(8,128)(2,1)S(1)}, u32[]{:S(2)}, u32[]{:S(2)}) collective-permute-start(bf16[160,640]{1,0:T(8,128)(2,1)S(1)} %collective-permute-done.7.refs_9_), channel_id=1, source_target_pairs={{4,0},{8,4},{12,8},{14,12},{10,14},{6,10},{2,6},{0,2},{5,1},{9,5},... | collective-permute-start | bytes 614408 | tf_op jit(solution)/shard_map/ppermute | solution.py:289
  30.1 8.8 %collective-permute-start.10 = (bf16[160,640]{1,0:T(8,128)(2,1)S(1)}, bf16[160,640]{1,0:T(8,128)(2,1)S(1)}, u32[]{:S(2)}, u32[]{:S(2)}) collective-permute-start(bf16[160,640]{1,0:T(8,128)(2,1)S(1)} %collective-permute-done.5.refs_7_), channel_id=1, source_target_pairs={{4,0},{8,4},{12,8},{14,12},{10,14},{6,10},{2,6},{0,2},{5,1},{9,5},... | collective-permute-start | bytes 614408 | tf_op jit(solution)/shard_map/ppermute | solution.py:289
  30.5 8.4 %collective-permute-start.11 = (bf16[160,640]{1,0:T(8,128)(2,1)S(1)}, bf16[160,640]{1,0:T(8,128)(2,1)S(1)}, u32[]{:S(2)}, u32[]{:S(2)}) collective-permute-start(bf16[160,640]{1,0:T(8,128)(2,1)S(1)} %collective-permute-done.6.refs_8_), channel_id=1, source_target_pairs={{0,4},{4,8},{8,12},{12,14},{14,10},{10,6},{6,2},{2,0},{1,5},{5,9},... | collective-permute-start | bytes 614408 | tf_op jit(solution)/shard_map/ppermute | solution.py:288
  47.1 7.8 %collective-permute-start.18 = (bf16[160,640]{1,0:T(8,128)(2,1)S(1)}, bf16[160,640]{1,0:T(8,128)(2,1)S(1)}, u32[]{:S(2)}, u32[]{:S(2)}) collective-permute-start(bf16[160,640]{1,0:T(8,128)(2,1)S(1)} %get-tuple-element.51), channel_id=1, source_target_pairs={{0,4},{4,8},{8,12},{12,14},{14,10},{10,6},{6,2},{2,0},{1,5},{5,9},... | collective-permute-start | bytes 614408 | tf_op jit(solution)/shard_map/ppermute | solution.py:365
  48.8 7.4 %collective-permute-start.19 = (bf16[160,640]{1,0:T(8,128)(2,1)S(1)}, bf16[160,640]{1,0:T(8,128)(2,1)S(1)}, u32[]{:S(2)}, u32[]{:S(2)}) collective-permute-start(bf16[160,640]{1,0:T(8,128)(2,1)S(1)} %get-tuple-element.52), channel_id=1, source_target_pairs={{4,0},{8,4},{12,8},{14,12},{10,14},{6,10},{2,6},{0,2},{5,1},{9,5},... | collective-permute-start | bytes 614408 | tf_op jit(solution)/shard_map/ppermute | solution.py:365
  51.2 16.4 %collective-permute-start.17 = (bf16[384,640]{1,0:T(8,128)(2,1)S(1)}, bf16[384,640]{1,0:T(8,128)(2,1)S(1)}, u32[]{:S(2)}, u32[]{:S(2)}) collective-permute-start(bf16[384,640]{1,0:T(8,128)(2,1)S(1)} %get-tuple-element.49), channel_id=1, source_target_pairs={{0,1},{1,0},{2,3},{3,2},{4,5},{5,4},{6,7},{7,6},{8,9},{9,8},{10,11... | collective-permute-start | bytes 1474568 | tf_op jit(solution)/shard_map/ppermute | solution.py:341
  51.3 8.0 %collective-permute-start.22 = (bf16[160,640]{1,0:T(8,128)(2,1)S(1)}, bf16[160,640]{1,0:T(8,128)(2,1)S(1)}, u32[]{:S(2)}, u32[]{:S(2)}) collective-permute-start(bf16[160,640]{1,0:T(8,128)(2,1)S(1)} %shard_map.86), channel_id=1, source_target_pairs={{0,4},{4,8},{8,12},{12,14},{14,10},{10,6},{6,2},{2,0},{1,5},{5,9},... | collective-permute-start | bytes 614408 | tf_op jit(solution)/shard_map/ppermute | solution.py:365
  52.9 7.9 %collective-permute-start.23 = (bf16[160,640]{1,0:T(8,128)(2,1)S(1)}, bf16[160,640]{1,0:T(8,128)(2,1)S(1)}, u32[]{:S(2)}, u32[]{:S(2)}) collective-permute-start(bf16[160,640]{1,0:T(8,128)(2,1)S(1)} %shard_map.87), channel_id=1, source_target_pairs={{4,0},{8,4},{12,8},{14,12},{10,14},{6,10},{2,6},{0,2},{5,1},{9,5},... | collective-permute-start | bytes 614408 | tf_op jit(solution)/shard_map/ppermute | solution.py:365
  56.3 7.8 %collective-permute-start.20 = (bf16[160,640]{1,0:T(8,128)(2,1)S(1)}, bf16[160,640]{1,0:T(8,128)(2,1)S(1)}, u32[]{:S(2)}, u32[]{:S(2)}) collective-permute-start(bf16[160,640]{1,0:T(8,128)(2,1)S(1)} %get-tuple-element.53.refs_3_), channel_id=1, source_target_pairs={{0,4},{4,8},{8,12},{12,14},{14,10},{10,6},{6,2},{2,0},{1,5},{5,9},... | collective-permute-start | bytes 614408 | tf_op jit(solution)/shard_map/ppermute | solution.py:365
  57.9 7.5 %collective-permute-start.21 = (bf16[160,640]{1,0:T(8,128)(2,1)S(1)}, bf16[160,640]{1,0:T(8,128)(2,1)S(1)}, u32[]{:S(2)}, u32[]{:S(2)}) collective-permute-start(bf16[160,640]{1,0:T(8,128)(2,1)S(1)} %get-tuple-element.54), channel_id=1, source_target_pairs={{4,0},{8,4},{12,8},{14,12},{10,14},{6,10},{2,6},{0,2},{5,1},{9,5},... | collective-permute-start | bytes 614408 | tf_op jit(solution)/shard_map/ppermute | solution.py:365
  61.0 8.1 %collective-permute-start.27 = (bf16[160,640]{1,0:T(8,128)(2,1)S(1)}, bf16[160,640]{1,0:T(8,128)(2,1)S(1)}, u32[]{:S(2)}, u32[]{:S(2)}) collective-permute-start(bf16[160,640]{1,0:T(8,128)(2,1)S(1)} %get-tuple-element.58.refs_3_), channel_id=1, source_target_pairs={{0,4},{4,8},{8,12},{12,14},{14,10},{10,6},{6,2},{2,0},{1,5},{5,9},... | collective-permute-start | bytes 614408 | tf_op jit(solution)/shard_map/ppermute | solution.py:365
  65.5 7.5 %collective-permute-start.25 = (bf16[160,640]{1,0:T(8,128)(2,1)S(1)}, bf16[160,640]{1,0:T(8,128)(2,1)S(1)}, u32[]{:S(2)}, u32[]{:S(2)}) collective-permute-start(bf16[160,640]{1,0:T(8,128)(2,1)S(1)} %get-tuple-element.59.refs_2_), channel_id=1, source_target_pairs={{0,4},{4,8},{8,12},{12,14},{14,10},{10,6},{6,2},{2,0},{1,5},{5,9},... | collective-permute-start | bytes 614408 | tf_op jit(solution)/shard_map/ppermute | solution.py:365
  67.6 13.0 %collective-permute-start.16 = (bf16[384,640]{1,0:T(8,128)(2,1)S(1)}, bf16[384,640]{1,0:T(8,128)(2,1)S(1)}, u32[]{:S(2)}, u32[]{:S(2)}) collective-permute-start(bf16[384,640]{1,0:T(8,128)(2,1)S(1)} %get-tuple-element.48), channel_id=1, source_target_pairs={{0,1},{1,0},{2,3},{3,2},{4,5},{5,4},{6,7},{7,6},{8,9},{9,8},{10,11... | collective-permute-start | bytes 1474568 | tf_op jit(solution)/shard_map/ppermute | solution.py:394
  69.1 13.8 %collective-permute-start.24 = (bf16[384,640]{1,0:T(8,128)(2,1)S(1)}, bf16[384,640]{1,0:T(8,128)(2,1)S(1)}, u32[]{:S(2)}, u32[]{:S(2)}) collective-permute-start(bf16[384,640]{1,0:T(8,128)(2,1)S(1)} %shard_map.90.refs_3_), channel_id=1, source_target_pairs={{0,16},{16,0},{1,17},{17,1},{2,18},{18,2},{3,19},{19,3},{4,20},{20... | collective-permute-start | bytes 1474568 | tf_op jit(solution)/shard_map/ppermute | solution.py:345
  (17 other events, 157.9 us)

commit v23 on v22

--- a/solution.py
+++ b/solution.py
@@ -160,26 +160,25 @@
         block[...] = partial[block_rows(step, peers, block.shape[0]), :]
 
 
-def d_norm_kernel(d_pre_own, d_pre_other, up, keep, send_own, *sends):
+def d_norm_kernel(d_pre_own, d_pre_other, up, keep, send_other, *sends):
     core = lax.axis_index("gy")
     rows, width = keep.shape[1:]
     mine = up[pl.ds(pl.multiple_of(core * width, width), width), :]
     theirs = up[pl.ds(pl.multiple_of((1 - core) * width, width), width), :]
     keep[0] = dot(d_pre_own[...], mine, 1, 1).astype(BF16)
     keep[1] = dot(d_pre_other[...], mine, 1, 1).astype(BF16)
-    send_own[...] = dot(d_pre_own[...], theirs, 1, 1).astype(BF16)
     sent = dot(d_pre_other[...], theirs, 1, 1).astype(BF16)
-    sent = jnp.concatenate([sent[rows // 2 :], sent[: rows // 2]])
+    send_other[: rows // 2, :] = sent[rows // 2 :]
+    send_other[rows // 2 :, :] = sent[: rows // 2]
+    sent = dot(d_pre_own[...], theirs, 1, 1).astype(BF16)
     step = rows // len(sends)
     for i, send in enumerate(sends):
         send[...] = sent[i * step : (i + 1) * step]
 
 
-def over_kernel(keep, *refs):
-    parts, over = refs[:-1], refs[-1]
+def over_kernel(keep, came, over):
     half = over.shape[0] // 2
-    value = jnp.concatenate([part[...].astype(F32) for part in parts])
-    value = (keep[1].astype(F32) + value).astype(BF16)
+    value = (keep[1].astype(F32) + came[...].astype(F32)).astype(BF16)
     for i in range(2):
         at = lax.rem(i + lax.axis_index("gy"), 2) * half
         over[pl.ds(pl.multiple_of(at, half), half), :] = value[i * half : (i + 1) * half]
@@ -189,9 +188,11 @@
     return ref[:, pl.ds(pl.multiple_of(lax.axis_index("gy") * width, width), width)]
 
 
-def scale_kernel(keep, came, back, frames, gain, grads, stats, base, factor, sums):
+def scale_kernel(keep, back, frames, gain, grads, stats, *refs):
+    came, (base, factor, sums) = refs[:-3], refs[-3:]
     width = base.shape[1]
-    d_norm = keep[0].astype(F32) + came[...].astype(F32) + back[...].astype(F32)
+    d_norm = jnp.concatenate([part[...].astype(F32) for part in came])
+    d_norm = keep[0].astype(F32) + d_norm + back[...].astype(F32)
     scaled = d_norm * own_columns(gain, width)
     rows = own_columns(frames, width).astype(F32)
     inv_std = stats[:, 1:2]
@@ -328,7 +329,7 @@
     partial = [partial_own, partial_other]
 
     half_rows_of = shape((frame_len, half_width), BF16)
-    parts_of = [half_rows_of]
+    parts_of = [shape((frame_len // 3, half_width), BF16)] * 3
 
     def own_d_norm(*ties):
         keep, send, *parts = call(
@@ -338,16 +339,17 @@
             flops=4 * frame_len * width * quarter,
             ties=ties,
         )
-        return keep, send, [lax.ppermute(part, "gy", swap) for part in parts]
-
-    def over_cores(keep, parts, *ties):
-        over = call(over_kernel, (keep, *parts), half_rows_of, ties=ties)
+        sent = [lax.ppermute(part, "gy", swap) for part in parts]
+        return keep, lax.ppermute(send, "gy", swap), sent
+
+    def over_cores(keep, came, *ties):
+        over = call(over_kernel, (keep, came), half_rows_of, ties=ties)
         return over, lax.ppermute(over, "groups", swap)
 
     def scale(keep, came, back, *ties):
         return call(
             scale_kernel,
-            (keep, came, back, frames, ln_gain[None], grads, stats),
+            (keep, back, frames, ln_gain[None], grads, stats, *came),
             (
                 shape((frame_len, half_width), F32),
                 shape((frame_len, half_width), F32),
@@ -382,16 +384,15 @@
             return blocks[0]
 
         send_on(1, blocks_other, ("up", "down"))
-        keep, send, parts = own_d_norm()
+        keep, came_other, sent = own_d_norm()
         send_on(0, [hold(block, keep) for block in blocks_own], ("up", "down"))
         tie = hop(1, 1, keep)
         tie = hop(0, 1, tie)
         tie = hop(1, 2, tie)
-        tie, back = over_cores(keep, parts, tie)
+        tie, back = over_cores(keep, came_other, tie)
         tie = hop(0, 2, tie)
         for turn in range(3, half):
             tie = hop(0, turn, hop(1, turn, tie))
-        sent = lax.ppermute(send, "gy", swap)
         passing = call(
             functools.partial(total_kernel, peers),
             (partial[1], came[1]["up"], came[1]["down"]),
@@ -408,9 +409,8 @@
             (half_rows_of, up_grad_of),
         )
     else:
-        keep, send, parts = own_d_norm()
-        sent = lax.ppermute(send, "gy", swap)
-        _, back = over_cores(keep, parts)
+        keep, came_other, sent = own_d_norm()
+        _, back = over_cores(keep, came_other)
         base, factor, sums = scale(keep, sent, back)
         came = lax.ppermute(sums, "gy", swap)
         input_grad = call(input_kernel, (base, factor, sums, came, stats), half_rows_of)

time: 87.4 us -> 87.4 us (level)
    ppermute x1, waiting for transfers between devices: 2.28 us -> 0.01 us  [over_cores(): return (over, lax.ppermute(over, 'groups', swap))]
    ppermute x2 -> x4, waiting for transfers between devices: 0.01 us -> 1.39 us  [the longest x3 1.39 us: own_d_norm(): sent = [lax.ppermute(part, 'gy', swap) for part in parts]]
  transfers between devices with their start and end apart: 35 -> 37, of which waited for: 23 -> 22; matrix products, arithmetic and copies ran while one was open for 0% -> 0% of each run, Pallas kernels for 13% -> 13%
where the time goes in v23:
time: 87.4 us; the launch traced here: 87.2 us
  waiting for transfers between devices  33.8 us (39%)
  starting transfers between devices  33.6 us (38%)
  Pallas kernels  18.9 us (22%)
    pallas_call x16, Pallas kernels, call(): pl.pallas_call(body if ties else kernel, out_shape=out_shape, in_specs=[S...  18.9 us
    ppermute x14, waiting for transfers between devices, send_on(): came[i][name] = lax.ppermute(block, 'gx', ahead if name == 'up' else behind)  15.7 us
    ppermute x14, starting transfers between devices, send_on(): came[i][name] = lax.ppermute(block, 'gx', ahead if name == 'up' else behind)  14.5 us
    ppermute x6, starting transfers between devices, shards(): up[i] = lax.ppermute(up[i], 'gx', ahead)  8.39 us
    ppermute x6, waiting for transfers between devices, shards(): down[i] = lax.ppermute(down[i], 'gx', behind)  7.92 us
    ppermute x6, waiting for transfers between devices, shards(): up[i] = lax.ppermute(up[i], 'gx', ahead)  4.61 us
    ppermute x6, starting transfers between devices, shards(): down[i] = lax.ppermute(down[i], 'gx', behind)  3.77 us
    ppermute x1, starting transfers between devices, shards(): first = lax.ppermute(passing, 'groups', swap)  3 us
  transfers between devices with their start and end apart: 37, of which 22 were waited for; matrix products, arithmetic and copies ran while one was open for 0% of the time, Pallas kernels for 13%

profile of v23, /device:TPU:0, one launch (start us, length us, event | category | flops | bytes accessed | tf_op | source)
XLA Modules:
  0.0 87.2 jit_solution(13317105107208516250)
XLA Ops:
  0.7 3.4 %shard_map.78 = (bf16[2,192,1280]{2,1,0:T(8,128)(2,1)}, bf16[160,640]{1,0:T(8,128)(2,1)}, bf16[160,640]{1,0:T(8,128)(2,1)}) custom-call(s32[8]{0:T(128)} %lengths.3, bf16[384,1280]{1,0:T(8,128)(2,1)} %bitcast.3, bf16[384,1280]{1,0:T(8,128)(2,1)} %bitcast.6, f32[1280]{0:T(1024)} %gain.3, bf16[160,1280]{1,0:T(8,128)(2,1)} %w_up.1, bf16[160,1280]{1,0:T(8,128)(2,1)} %w_down.1), custom_call_target="tpu_custom_call" | custom-call | flops 2457600 | bytes 4183072 | tf_op jit(solution)/shard_map/pallas_call | solution.py:28
  4.1 3.0 %collective-permute-start.14 = (bf16[2,192,1280]{2,1,0:T(8,128)(2,1)}, bf16[2,192,1280]{2,1,0:T(8,128)(2,1)S(1)}, u32[]{:S(2)}, u32[]{:S(2)}) collective-permute-start(bf16[2,192,1280]{2,1,0:T(8,128)(2,1)} %get-tuple-element.45), channel_id=1, source_target_pairs={{0,16},{16,0},{1,17},{17,1},{2,18},{18,2},{3,19},{19,3},{4,20},{20... | collective-permute-start | bytes 2949128 | tf_op jit(solution)/shard_map/ppermute | solution.py:275
  7.1 1.6 %collective-permute-start = (bf16[160,640]{1,0:T(8,128)(2,1)}, bf16[160,640]{1,0:T(8,128)(2,1)S(1)}, u32[]{:S(2)}, u32[]{:S(2)}) collective-permute-start(bf16[160,640]{1,0:T(8,128)(2,1)} %get-tuple-element.40.refs_0_), channel_id=1, source_target_pairs={{0,4},{4,8},{8,12},{12,14},{14,10},{10,6},{6,2},{2,0},{1,5},{5,9},... | collective-permute-start | bytes 614408 | tf_op jit(solution)/shard_map/ppermute | solution.py:289
  12.6 2.6 %collective-permute-done.refs_0_ = bf16[160,640]{1,0:T(8,128)(2,1)S(1)} collective-permute-done((bf16[160,640]{1,0:T(8,128)(2,1)}, bf16[160,640]{1,0:T(8,128)(2,1)S(1)}, u32[]{:S(2)}, u32[]{:S(2)}) %collective-permute-start) | collective-permute-done | bytes 204832 | tf_op jit(solution)/shard_map/ppermute | solution.py:289
  15.3 1.6 %collective-permute-start.4 = (bf16[160,640]{1,0:T(8,128)(2,1)S(1)}, bf16[160,640]{1,0:T(8,128)(2,1)S(1)}, u32[]{:S(2)}, u32[]{:S(2)}) collective-permute-start(bf16[160,640]{1,0:T(8,128)(2,1)S(1)} %shard_map.79.refs_2_), channel_id=1, source_target_pairs={{0,4},{4,8},{8,12},{12,14},{14,10},{10,6},{6,2},{2,0},{1,5},{5,9},... | collective-permute-start | bytes 614408 | tf_op jit(solution)/shard_map/ppermute | solution.py:289
  17.3 3.9 %collective-permute-done.1.refs_3_ = bf16[160,640]{1,0:T(8,128)(2,1)S(1)} collective-permute-done((bf16[160,640]{1,0:T(8,128)(2,1)}, bf16[160,640]{1,0:T(8,128)(2,1)S(1)}, u32[]{:S(2)}, u32[]{:S(2)}) %collective-permute-start.1) | collective-permute-done | bytes 204832 | tf_op jit(solution)/shard_map/ppermute | solution.py:290
  21.7 1.6 %collective-permute-start.6 = (bf16[160,640]{1,0:T(8,128)(2,1)S(1)}, bf16[160,640]{1,0:T(8,128)(2,1)S(1)}, u32[]{:S(2)}, u32[]{:S(2)}) collective-permute-start(bf16[160,640]{1,0:T(8,128)(2,1)S(1)} %collective-permute-done.2.refs_4_), channel_id=1, source_target_pairs={{0,4},{4,8},{8,12},{12,14},{14,10},{10,6},{6,2},{2,0},{1,5},{5,9},... | collective-permute-start | bytes 614408 | tf_op jit(solution)/shard_map/ppermute | solution.py:289
  24.1 1.6 %collective-permute-start.8 = (bf16[160,640]{1,0:T(8,128)(2,1)S(1)}, bf16[160,640]{1,0:T(8,128)(2,1)S(1)}, u32[]{:S(2)}, u32[]{:S(2)}) collective-permute-start(bf16[160,640]{1,0:T(8,128)(2,1)S(1)} %collective-permute-done.4.refs_6_), channel_id=1, source_target_pairs={{0,4},{4,8},{8,12},{12,14},{14,10},{10,6},{6,2},{2,0},{1,5},{5,9},... | collective-permute-start | bytes 614408 | tf_op jit(solution)/shard_map/ppermute | solution.py:289
  26.1 3.9 %collective-permute-done.5.refs_7_ = bf16[160,640]{1,0:T(8,128)(2,1)S(1)} collective-permute-done((bf16[160,640]{1,0:T(8,128)(2,1)S(1)}, bf16[160,640]{1,0:T(8,128)(2,1)S(1)}, u32[]{:S(2)}, u32[]{:S(2)}) %collective-permute-start.5) | collective-permute-done | bytes 204832 | tf_op jit(solution)/shard_map/ppermute | solution.py:290
  30.5 1.6 %collective-permute-start.11 = (bf16[160,640]{1,0:T(8,128)(2,1)S(1)}, bf16[160,640]{1,0:T(8,128)(2,1)S(1)}, u32[]{:S(2)}, u32[]{:S(2)}) collective-permute-start(bf16[160,640]{1,0:T(8,128)(2,1)S(1)} %collective-permute-done.6.refs_8_), channel_id=1, source_target_pairs={{0,4},{4,8},{8,12},{12,14},{14,10},{10,6},{6,2},{2,0},{1,5},{5,9},... | collective-permute-start | bytes 614408 | tf_op jit(solution)/shard_map/ppermute | solution.py:289
  33.3 1.6 %collective-permute-start.12 = (bf16[160,640]{1,0:T(8,128)(2,1)S(1)}, bf16[160,640]{1,0:T(8,128)(2,1)S(1)}, u32[]{:S(2)}, u32[]{:S(2)}) collective-permute-start(bf16[160,640]{1,0:T(8,128)(2,1)S(1)} %collective-permute-done.8.refs_10_), channel_id=1, source_target_pairs={{0,4},{4,8},{8,12},{12,14},{14,10},{10,6},{6,2},{2,0},{1,5},{5,9},... | collective-permute-start | bytes 614408 | tf_op jit(solution)/shard_map/ppermute | solution.py:298
  35.3 3.6 %shard_map.80 = (bf16[1280,640]{1,0:T(8,128)(2,1)S(1)}, bf16[1280,640]{1,0:T(8,128)(2,1)S(1)}) custom-call(bf16[160,640]{1,0:T(8,128)(2,1)S(1)} %copy-done.2, bf16[160,640]{1,0:T(8,128)(2,1)S(1)} %copy-done.3, bf16[160,640]{1,0:T(8,128)(2,1)S(1)} %shard_map.79.refs_2_, bf16[160,640]{1,0:T(8,128)(2,1)S(1)} %collective-permute-done.1.refs_3_, ...), custom_call_target="tpu_custom_call" | custom-call | flops 1 | bytes 5734400 | tf_op jit(solution)/shard_map/pallas_call | solution.py:28
  41.5 2.9 %shard_map.81 = (bf16[384,640]{1,0:T(8,128)(2,1)S(1)}, bf16[1280,640]{1,0:T(8,128)(2,1)S(1)}, bf16[1280,640]{1,0:T(8,128)(2,1)S(1)}, bf16[1280,640]{1,0:T(8,128)...) custom-call(bf16[384,1280]{1,0:T(8,128)(2,1)S(1)} %get-tuple-element.38.refs_1_.normed, ...), custom_call_target="tpu_custom_call" | custom-call | flops 1887436800 | bytes 11878400 | tf_op jit(solution)/shard_map/pallas_call | solution.py:28
  44.4 2.7 %shard_map.83 = (bf16[384,640]{1,0:T(8,128)(2,1)S(1)}, bf16[1280,640]{1,0:T(8,128)(2,1)S(1)}, bf16[160,640]{1,0:T(8,128)(2,1)S(1)}, bf16[160,640]{1,0:T(8,128)(2,1)S(1)}) custom-call(bf16[2,192,1280]{2,1,0:T(8,128)(2,1)S(1)} %shard_map.82.first, bf16[2,192,1280]{2,1,0:T(8,128)(2,1)S(1)} %collective-permute-done.15.second, ...), custom_call_target="tpu_custom_call" | custom-call | flops 1887436800 | bytes 7782400 | tf_op jit(solution)/shard_map/pallas_call | solution.py:28
  47.1 1.6 %collective-permute-start.17 = (bf16[160,640]{1,0:T(8,128)(2,1)S(1)}, bf16[160,640]{1,0:T(8,128)(2,1)S(1)}, u32[]{:S(2)}, u32[]{:S(2)}) collective-permute-start(bf16[160,640]{1,0:T(8,128)(2,1)S(1)} %get-tuple-element.52), channel_id=1, source_target_pairs={{0,4},{4,8},{8,12},{12,14},{14,10},{10,6},{6,2},{2,0},{1,5},{5,9},... | collective-permute-start | bytes 614408 | tf_op jit(solution)/shard_map/ppermute | solution.py:367
  49.2 2.0 %shard_map.84 = (bf16[2,384,640]{2,1,0:T(8,128)(2,1)S(1)}, bf16[384,640]{1,0:T(8,128)(2,1)S(1)}, bf16[128,640]{1,0:T(8,128)(2,1)S(1)}, bf16[128,640]{1,0:T(8,128)(2,1)S(1)}, bf16[128,640]{1,0:T(8,128)(2,1)S(1)}) custom-call(bf16[384,640]{1,0:T(8,128)(2,1)S(1)} %get-tuple-element.44.d_pre_own, bf16[384,640]{1,0:T(8,128)(2,1)S(1)} %get-tuple-element.48.d_pre_other, ...), custom_call_target="tpu_custom_call" | custom-call | flops 1258291200 | bytes 4587520 | tf_op jit(solution)/shard_map/pallas_call | solution.py:28
  51.3 1.6 %collective-permute-start.21 = (bf16[160,640]{1,0:T(8,128)(2,1)S(1)}, bf16[160,640]{1,0:T(8,128)(2,1)S(1)}, u32[]{:S(2)}, u32[]{:S(2)}) collective-permute-start(bf16[160,640]{1,0:T(8,128)(2,1)S(1)} %shard_map.86), channel_id=1, source_target_pairs={{0,4},{4,8},{8,12},{12,14},{14,10},{10,6},{6,2},{2,0},{1,5},{5,9},... | collective-permute-start | bytes 614408 | tf_op jit(solution)/shard_map/ppermute | solution.py:367
  56.3 1.6 %collective-permute-start.19 = (bf16[160,640]{1,0:T(8,128)(2,1)S(1)}, bf16[160,640]{1,0:T(8,128)(2,1)S(1)}, u32[]{:S(2)}, u32[]{:S(2)}) collective-permute-start(bf16[160,640]{1,0:T(8,128)(2,1)S(1)} %get-tuple-element.54.refs_3_), channel_id=1, source_target_pairs={{0,4},{4,8},{8,12},{12,14},{14,10},{10,6},{6,2},{2,0},{1,5},{5,9},... | collective-permute-start | bytes 614408 | tf_op jit(solution)/shard_map/ppermute | solution.py:367
  59.3 1.6 %collective-permute-done.22.refs_2_ = bf16[160,640]{1,0:T(8,128)(2,1)S(1)} collective-permute-done((bf16[160,640]{1,0:T(8,128)(2,1)S(1)}, bf16[160,640]{1,0:T(8,128)(2,1)S(1)}, u32[]{:S(2)}, u32[]{:S(2)}) %collective-permute-start.22) | collective-permute-done | bytes 204832 | tf_op jit(solution)/shard_map/ppermute | solution.py:367
  61.0 1.6 %collective-permute-start.29 = (bf16[160,640]{1,0:T(8,128)(2,1)S(1)}, bf16[160,640]{1,0:T(8,128)(2,1)S(1)}, u32[]{:S(2)}, u32[]{:S(2)}) collective-permute-start(bf16[160,640]{1,0:T(8,128)(2,1)S(1)} %get-tuple-element.59.refs_3_), channel_id=1, source_target_pairs={{0,4},{4,8},{8,12},{12,14},{14,10},{10,6},{6,2},{2,0},{1,5},{5,9},... | collective-permute-start | bytes 614408 | tf_op jit(solution)/shard_map/ppermute | solution.py:367
  65.5 1.7 %collective-permute-start.27 = (bf16[160,640]{1,0:T(8,128)(2,1)S(1)}, bf16[160,640]{1,0:T(8,128)(2,1)S(1)}, u32[]{:S(2)}, u32[]{:S(2)}) collective-permute-start(bf16[160,640]{1,0:T(8,128)(2,1)S(1)} %get-tuple-element.60.refs_2_), channel_id=1, source_target_pairs={{0,4},{4,8},{8,12},{12,14},{14,10},{10,6},{6,2},{2,0},{1,5},{5,9},... | collective-permute-start | bytes 614408 | tf_op jit(solution)/shard_map/ppermute | solution.py:367
  71.6 2.0 %collective-permute-done.27.refs_3_.refs_1_ = bf16[160,640]{1,0:T(8,128)(2,1)S(1)} collective-permute-done((bf16[160,640]{1,0:T(8,128)(2,1)S(1)}, bf16[160,640]{1,0:T(8,128)(2,1)S(1)}, u32[]{:S(2)}, u32[]{:S(2)}) %collective-permute-start.27) | collective-permute-done | bytes 204832 | tf_op jit(solution)/shard_map/ppermute | solution.py:367
  74.7 1.9 %collective-permute-done.32.refs_1_ = bf16[160,640]{1,0:T(8,128)(2,1)S(1)} collective-permute-done((bf16[160,640]{1,0:T(8,128)(2,1)S(1)}, bf16[160,640]{1,0:T(8,128)(2,1)S(1)}, u32[]{:S(2)}, u32[]{:S(2)}) %collective-permute-start.32) | collective-permute-done | bytes 204832 | tf_op jit(solution)/shard_map/ppermute | solution.py:367
  76.7 1.6 %collective-permute-start.34 = (bf16[160,640]{1,0:T(8,128)(2,1)S(1)}, bf16[160,640]{1,0:T(8,128)(2,1)S(1)}, u32[]{:S(2)}, u32[]{:S(2)}) collective-permute-start(bf16[160,640]{1,0:T(8,128)(2,1)S(1)} %shard_map.93.refs_3_), channel_id=1, source_target_pairs={{0,4},{4,8},{8,12},{12,14},{14,10},{10,6},{6,2},{2,0},{1,5},{5,9},... | collective-permute-start | bytes 614408 | tf_op jit(solution)/shard_map/ppermute | solution.py:367
  (84 shorter events, 33.5 us)
Async XLA Ops:
  4.1 37.4 %collective-permute-start.14 = (bf16[2,192,1280]{2,1,0:T(8,128)(2,1)}, bf16[2,192,1280]{2,1,0:T(8,128)(2,1)S(1)}, u32[]{:S(2)}, u32[]{:S(2)}) collective-permute-start(bf16[2,192,1280]{2,1,0:T(8,128)(2,1)} %get-tuple-element.45), channel_id=1, source_target_pairs={{0,16},{16,0},{1,17},{17,1},{2,18},{18,2},{3,19},{19,3},{4,20},{20... | collective-permute-start | bytes 2949128 | tf_op jit(solution)/shard_map/ppermute | solution.py:275
  7.1 8.2 %collective-permute-start = (bf16[160,640]{1,0:T(8,128)(2,1)}, bf16[160,640]{1,0:T(8,128)(2,1)S(1)}, u32[]{:S(2)}, u32[]{:S(2)}) collective-permute-start(bf16[160,640]{1,0:T(8,128)(2,1)} %get-tuple-element.40.refs_0_), channel_id=1, source_target_pairs={{0,4},{4,8},{8,12},{12,14},{14,10},{10,6},{6,2},{2,0},{1,5},{5,9},... | collective-permute-start | bytes 614408 | tf_op jit(solution)/shard_map/ppermute | solution.py:289
  8.7 8.2 %collective-permute-start.3 = (bf16[160,640]{1,0:T(8,128)(2,1)}, bf16[160,640]{1,0:T(8,128)(2,1)S(1)}, u32[]{:S(2)}, u32[]{:S(2)}) collective-permute-start(bf16[160,640]{1,0:T(8,128)(2,1)} %get-tuple-element.41.refs_1_), channel_id=1, source_target_pairs={{4,0},{8,4},{12,8},{14,12},{10,14},{6,10},{2,6},{0,2},{5,1},{9,5},... | collective-permute-start | bytes 614408 | tf_op jit(solution)/shard_map/ppermute | solution.py:290
  9.1 12.2 %collective-permute-start.1 = (bf16[160,640]{1,0:T(8,128)(2,1)}, bf16[160,640]{1,0:T(8,128)(2,1)S(1)}, u32[]{:S(2)}, u32[]{:S(2)}) collective-permute-start(bf16[160,640]{1,0:T(8,128)(2,1)} %get-tuple-element.40.refs_0_), channel_id=1, source_target_pairs={{4,0},{8,4},{12,8},{14,12},{10,14},{6,10},{2,6},{0,2},{5,1},{9,5},... | collective-permute-start | bytes 614408 | tf_op jit(solution)/shard_map/ppermute | solution.py:290
  10.6 11.1 %collective-permute-start.2 = (bf16[160,640]{1,0:T(8,128)(2,1)}, bf16[160,640]{1,0:T(8,128)(2,1)S(1)}, u32[]{:S(2)}, u32[]{:S(2)}) collective-permute-start(bf16[160,640]{1,0:T(8,128)(2,1)} %get-tuple-element.41.refs_1_), channel_id=1, source_target_pairs={{0,4},{4,8},{8,12},{12,14},{14,10},{10,6},{6,2},{2,0},{1,5},{5,9},... | collective-permute-start | bytes 614408 | tf_op jit(solution)/shard_map/ppermute | solution.py:289
  15.3 8.8 %collective-permute-start.4 = (bf16[160,640]{1,0:T(8,128)(2,1)S(1)}, bf16[160,640]{1,0:T(8,128)(2,1)S(1)}, u32[]{:S(2)}, u32[]{:S(2)}) collective-permute-start(bf16[160,640]{1,0:T(8,128)(2,1)S(1)} %shard_map.79.refs_2_), channel_id=1, source_target_pairs={{0,4},{4,8},{8,12},{12,14},{14,10},{10,6},{6,2},{2,0},{1,5},{5,9},... | collective-permute-start | bytes 614408 | tf_op jit(solution)/shard_map/ppermute | solution.py:289
  16.9 8.8 %collective-permute-start.7 = (bf16[160,640]{1,0:T(8,128)(2,1)S(1)}, bf16[160,640]{1,0:T(8,128)(2,1)S(1)}, u32[]{:S(2)}, u32[]{:S(2)}) collective-permute-start(bf16[160,640]{1,0:T(8,128)(2,1)S(1)} %collective-permute-done.3.refs_5_), channel_id=1, source_target_pairs={{4,0},{8,4},{12,8},{14,12},{10,14},{6,10},{2,6},{0,2},{5,1},{9,5},... | collective-permute-start | bytes 614408 | tf_op jit(solution)/shard_map/ppermute | solution.py:290
  21.3 8.8 %collective-permute-start.5 = (bf16[160,640]{1,0:T(8,128)(2,1)S(1)}, bf16[160,640]{1,0:T(8,128)(2,1)S(1)}, u32[]{:S(2)}, u32[]{:S(2)}) collective-permute-start(bf16[160,640]{1,0:T(8,128)(2,1)S(1)} %collective-permute-done.1.refs_3_), channel_id=1, source_target_pairs={{4,0},{8,4},{12,8},{14,12},{10,14},{6,10},{2,6},{0,2},{5,1},{9,5},... | collective-permute-start | bytes 614408 | tf_op jit(solution)/shard_map/ppermute | solution.py:290
  21.7 8.8 %collective-permute-start.6 = (bf16[160,640]{1,0:T(8,128)(2,1)S(1)}, bf16[160,640]{1,0:T(8,128)(2,1)S(1)}, u32[]{:S(2)}, u32[]{:S(2)}) collective-permute-start(bf16[160,640]{1,0:T(8,128)(2,1)S(1)} %collective-permute-done.2.refs_4_), channel_id=1, source_target_pairs={{0,4},{4,8},{8,12},{12,14},{14,10},{10,6},{6,2},{2,0},{1,5},{5,9},... | collective-permute-start | bytes 614408 | tf_op jit(solution)/shard_map/ppermute | solution.py:289
  24.1 9.2 %collective-permute-start.8 = (bf16[160,640]{1,0:T(8,128)(2,1)S(1)}, bf16[160,640]{1,0:T(8,128)(2,1)S(1)}, u32[]{:S(2)}, u32[]{:S(2)}) collective-permute-start(bf16[160,640]{1,0:T(8,128)(2,1)S(1)} %collective-permute-done.4.refs_6_), channel_id=1, source_target_pairs={{0,4},{4,8},{8,12},{12,14},{14,10},{10,6},{6,2},{2,0},{1,5},{5,9},... | collective-permute-start | bytes 614408 | tf_op jit(solution)/shard_map/ppermute | solution.py:289
  25.7 9.2 %collective-permute-start.9 = (bf16[160,640]{1,0:T(8,128)(2,1)S(1)}, bf16[160,640]{1,0:T(8,128)(2,1)S(1)}, u32[]{:S(2)}, u32[]{:S(2)}) collective-permute-start(bf16[160,640]{1,0:T(8,128)(2,1)S(1)} %collective-permute-done.7.refs_9_), channel_id=1, source_target_pairs={{4,0},{8,4},{12,8},{14,12},{10,14},{6,10},{2,6},{0,2},{5,1},{9,5},... | collective-permute-start | bytes 614408 | tf_op jit(solution)/shard_map/ppermute | solution.py:290
  30.1 8.8 %collective-permute-start.10 = (bf16[160,640]{1,0:T(8,128)(2,1)S(1)}, bf16[160,640]{1,0:T(8,128)(2,1)S(1)}, u32[]{:S(2)}, u32[]{:S(2)}) collective-permute-start(bf16[160,640]{1,0:T(8,128)(2,1)S(1)} %collective-permute-done.5.refs_7_), channel_id=1, source_target_pairs={{4,0},{8,4},{12,8},{14,12},{10,14},{6,10},{2,6},{0,2},{5,1},{9,5},... | collective-permute-start | bytes 614408 | tf_op jit(solution)/shard_map/ppermute | solution.py:290
  30.5 8.4 %collective-permute-start.11 = (bf16[160,640]{1,0:T(8,128)(2,1)S(1)}, bf16[160,640]{1,0:T(8,128)(2,1)S(1)}, u32[]{:S(2)}, u32[]{:S(2)}) collective-permute-start(bf16[160,640]{1,0:T(8,128)(2,1)S(1)} %collective-permute-done.6.refs_8_), channel_id=1, source_target_pairs={{0,4},{4,8},{8,12},{12,14},{14,10},{10,6},{6,2},{2,0},{1,5},{5,9},... | collective-permute-start | bytes 614408 | tf_op jit(solution)/shard_map/ppermute | solution.py:289
  47.1 7.8 %collective-permute-start.17 = (bf16[160,640]{1,0:T(8,128)(2,1)S(1)}, bf16[160,640]{1,0:T(8,128)(2,1)S(1)}, u32[]{:S(2)}, u32[]{:S(2)}) collective-permute-start(bf16[160,640]{1,0:T(8,128)(2,1)S(1)} %get-tuple-element.52), channel_id=1, source_target_pairs={{0,4},{4,8},{8,12},{12,14},{14,10},{10,6},{6,2},{2,0},{1,5},{5,9},... | collective-permute-start | bytes 614408 | tf_op jit(solution)/shard_map/ppermute | solution.py:367
  48.8 7.4 %collective-permute-start.18 = (bf16[160,640]{1,0:T(8,128)(2,1)S(1)}, bf16[160,640]{1,0:T(8,128)(2,1)S(1)}, u32[]{:S(2)}, u32[]{:S(2)}) collective-permute-start(bf16[160,640]{1,0:T(8,128)(2,1)S(1)} %get-tuple-element.53), channel_id=1, source_target_pairs={{4,0},{8,4},{12,8},{14,12},{10,14},{6,10},{2,6},{0,2},{5,1},{9,5},... | collective-permute-start | bytes 614408 | tf_op jit(solution)/shard_map/ppermute | solution.py:367
  51.2 16.4 %collective-permute-start.16 = (bf16[384,640]{1,0:T(8,128)(2,1)S(1)}, bf16[384,640]{1,0:T(8,128)(2,1)S(1)}, u32[]{:S(2)}, u32[]{:S(2)}) collective-permute-start(bf16[384,640]{1,0:T(8,128)(2,1)S(1)} %get-tuple-element.50), channel_id=1, source_target_pairs={{0,1},{1,0},{2,3},{3,2},{4,5},{5,4},{6,7},{7,6},{8,9},{9,8},{10,11... | collective-permute-start | bytes 1474568 | tf_op jit(solution)/shard_map/ppermute | solution.py:343
  51.3 8.0 %collective-permute-start.21 = (bf16[160,640]{1,0:T(8,128)(2,1)S(1)}, bf16[160,640]{1,0:T(8,128)(2,1)S(1)}, u32[]{:S(2)}, u32[]{:S(2)}) collective-permute-start(bf16[160,640]{1,0:T(8,128)(2,1)S(1)} %shard_map.86), channel_id=1, source_target_pairs={{0,4},{4,8},{8,12},{12,14},{14,10},{10,6},{6,2},{2,0},{1,5},{5,9},... | collective-permute-start | bytes 614408 | tf_op jit(solution)/shard_map/ppermute | solution.py:367
  52.9 7.9 %collective-permute-start.22 = (bf16[160,640]{1,0:T(8,128)(2,1)S(1)}, bf16[160,640]{1,0:T(8,128)(2,1)S(1)}, u32[]{:S(2)}, u32[]{:S(2)}) collective-permute-start(bf16[160,640]{1,0:T(8,128)(2,1)S(1)} %shard_map.87), channel_id=1, source_target_pairs={{4,0},{8,4},{12,8},{14,12},{10,14},{6,10},{2,6},{0,2},{5,1},{9,5},... | collective-permute-start | bytes 614408 | tf_op jit(solution)/shard_map/ppermute | solution.py:367
  56.3 7.8 %collective-permute-start.19 = (bf16[160,640]{1,0:T(8,128)(2,1)S(1)}, bf16[160,640]{1,0:T(8,128)(2,1)S(1)}, u32[]{:S(2)}, u32[]{:S(2)}) collective-permute-start(bf16[160,640]{1,0:T(8,128)(2,1)S(1)} %get-tuple-element.54.refs_3_), channel_id=1, source_target_pairs={{0,4},{4,8},{8,12},{12,14},{14,10},{10,6},{6,2},{2,0},{1,5},{5,9},... | collective-permute-start | bytes 614408 | tf_op jit(solution)/shard_map/ppermute | solution.py:367
  57.9 7.5 %collective-permute-start.20 = (bf16[160,640]{1,0:T(8,128)(2,1)S(1)}, bf16[160,640]{1,0:T(8,128)(2,1)S(1)}, u32[]{:S(2)}, u32[]{:S(2)}) collective-permute-start(bf16[160,640]{1,0:T(8,128)(2,1)S(1)} %get-tuple-element.55), channel_id=1, source_target_pairs={{4,0},{8,4},{12,8},{14,12},{10,14},{6,10},{2,6},{0,2},{5,1},{9,5},... | collective-permute-start | bytes 614408 | tf_op jit(solution)/shard_map/ppermute | solution.py:367
  61.0 8.1 %collective-permute-start.29 = (bf16[160,640]{1,0:T(8,128)(2,1)S(1)}, bf16[160,640]{1,0:T(8,128)(2,1)S(1)}, u32[]{:S(2)}, u32[]{:S(2)}) collective-permute-start(bf16[160,640]{1,0:T(8,128)(2,1)S(1)} %get-tuple-element.59.refs_3_), channel_id=1, source_target_pairs={{0,4},{4,8},{8,12},{12,14},{14,10},{10,6},{6,2},{2,0},{1,5},{5,9},... | collective-permute-start | bytes 614408 | tf_op jit(solution)/shard_map/ppermute | solution.py:367
  62.6 7.4 %collective-permute-start.30 = (bf16[160,640]{1,0:T(8,128)(2,1)S(1)}, bf16[160,640]{1,0:T(8,128)(2,1)S(1)}, u32[]{:S(2)}, u32[]{:S(2)}) collective-permute-start(bf16[160,640]{1,0:T(8,128)(2,1)S(1)} %get-tuple-element.66), channel_id=1, source_target_pairs={{4,0},{8,4},{12,8},{14,12},{10,14},{6,10},{2,6},{0,2},{5,1},{9,5},... | collective-permute-start | bytes 614408 | tf_op jit(solution)/shard_map/ppermute | solution.py:367
  65.5 8.1 %collective-permute-start.27 = (bf16[160,640]{1,0:T(8,128)(2,1)S(1)}, bf16[160,640]{1,0:T(8,128)(2,1)S(1)}, u32[]{:S(2)}, u32[]{:S(2)}) collective-permute-start(bf16[160,640]{1,0:T(8,128)(2,1)S(1)} %get-tuple-element.60.refs_2_), channel_id=1, source_target_pairs={{0,4},{4,8},{8,12},{12,14},{14,10},{10,6},{6,2},{2,0},{1,5},{5,9},... | collective-permute-start | bytes 614408 | tf_op jit(solution)/shard_map/ppermute | solution.py:367
  67.7 14.3 %collective-permute-start.23 = (bf16[384,640]{1,0:T(8,128)(2,1)S(1)}, bf16[384,640]{1,0:T(8,128)(2,1)S(1)}, u32[]{:S(2)}, u32[]{:S(2)}) collective-permute-start(bf16[384,640]{1,0:T(8,128)(2,1)S(1)} %shard_map.90.refs_3_), channel_id=1, source_target_pairs={{0,16},{16,0},{1,17},{17,1},{2,18},{18,2},{3,19},{19,3},{4,20},{20... | collective-permute-start | bytes 1474568 | tf_op jit(solution)/shard_map/ppermute | solution.py:347
  (19 other events, 163.6 us)

commit v24 on v23

--- a/solution.py
+++ b/solution.py
@@ -119,9 +119,12 @@
 
 
 def back_through(normed, grads, up, down, d_pre, partial):
-    pre_act = dot(normed[...], up[...])
-    d_act = dot(grads[...], down[...])
-    d_pre[...] = (d_act * gelu_slope(pre_act)).astype(BF16)
+    tile = 256
+    for at in range(0, d_pre.shape[1], tile):
+        columns = slice(at, min(at + tile, d_pre.shape[1]))
+        pre_act = dot(normed[...], up[:, columns])
+        d_act = dot(grads[...], down[:, columns])
+        d_pre[:, columns] = (d_act * gelu_slope(pre_act)).astype(BF16)
     partial[...] = dot(normed[...], d_pre[...], 0, 0).astype(BF16)
 
 

time: 87.4 us -> 87.5 us (level)
  no operation moved by 1% of the time
where the time goes in v24:
time: 87.5 us; the launch traced here: 87.3 us
  waiting for transfers between devices  33.8 us (39%)
  starting transfers between devices  33.6 us (38%)
  Pallas kernels  19 us (22%)
    pallas_call x16, Pallas kernels, call(): pl.pallas_call(body if ties else kernel, out_shape=out_shape, in_specs=[S...  19 us
    ppermute x14, waiting for transfers between devices, send_on(): came[i][name] = lax.ppermute(block, 'gx', ahead if name == 'up' else behind)  15.7 us
    ppermute x14, starting transfers between devices, send_on(): came[i][name] = lax.ppermute(block, 'gx', ahead if name == 'up' else behind)  14.5 us
    ppermute x6, starting transfers between devices, shards(): up[i] = lax.ppermute(up[i], 'gx', ahead)  8.39 us
    ppermute x6, waiting for transfers between devices, shards(): down[i] = lax.ppermute(down[i], 'gx', behind)  7.92 us
    ppermute x6, waiting for transfers between devices, shards(): up[i] = lax.ppermute(up[i], 'gx', ahead)  4.61 us
    ppermute x6, starting transfers between devices, shards(): down[i] = lax.ppermute(down[i], 'gx', behind)  3.77 us
    ppermute x1, starting transfers between devices, shards(): first = lax.ppermute(passing, 'groups', swap)  3 us
  transfers between devices with their start and end apart: 37, of which 22 were waited for; matrix products, arithmetic and copies ran while one was open for 0% of the time, Pallas kernels for 13%

profile of v24, /device:TPU:0, one launch (start us, length us, event | category | flops | bytes accessed | tf_op | source)
XLA Modules:
  0.0 87.3 jit_solution(15704912226609313272)
XLA Ops:
  0.7 3.4 %shard_map.78 = (bf16[2,192,1280]{2,1,0:T(8,128)(2,1)}, bf16[160,640]{1,0:T(8,128)(2,1)}, bf16[160,640]{1,0:T(8,128)(2,1)}) custom-call(s32[8]{0:T(128)} %lengths.3, bf16[384,1280]{1,0:T(8,128)(2,1)} %bitcast.3, bf16[384,1280]{1,0:T(8,128)(2,1)} %bitcast.6, f32[1280]{0:T(1024)} %gain.3, bf16[160,1280]{1,0:T(8,128)(2,1)} %w_up.1, bf16[160,1280]{1,0:T(8,128)(2,1)} %w_down.1), custom_call_target="tpu_custom_call" | custom-call | flops 2457600 | bytes 4183072 | tf_op jit(solution)/shard_map/pallas_call | solution.py:28
  4.1 3.0 %collective-permute-start.14 = (bf16[2,192,1280]{2,1,0:T(8,128)(2,1)}, bf16[2,192,1280]{2,1,0:T(8,128)(2,1)S(1)}, u32[]{:S(2)}, u32[]{:S(2)}) collective-permute-start(bf16[2,192,1280]{2,1,0:T(8,128)(2,1)} %get-tuple-element.45), channel_id=1, source_target_pairs={{0,16},{16,0},{1,17},{17,1},{2,18},{18,2},{3,19},{19,3},{4,20},{20... | collective-permute-start | bytes 2949128 | tf_op jit(solution)/shard_map/ppermute | solution.py:278
  7.1 1.6 %collective-permute-start = (bf16[160,640]{1,0:T(8,128)(2,1)}, bf16[160,640]{1,0:T(8,128)(2,1)S(1)}, u32[]{:S(2)}, u32[]{:S(2)}) collective-permute-start(bf16[160,640]{1,0:T(8,128)(2,1)} %get-tuple-element.40.refs_0_), channel_id=1, source_target_pairs={{0,4},{4,8},{8,12},{12,14},{14,10},{10,6},{6,2},{2,0},{1,5},{5,9},... | collective-permute-start | bytes 614408 | tf_op jit(solution)/shard_map/ppermute | solution.py:292
  12.6 2.6 %collective-permute-done.refs_0_ = bf16[160,640]{1,0:T(8,128)(2,1)S(1)} collective-permute-done((bf16[160,640]{1,0:T(8,128)(2,1)}, bf16[160,640]{1,0:T(8,128)(2,1)S(1)}, u32[]{:S(2)}, u32[]{:S(2)}) %collective-permute-start) | collective-permute-done | bytes 204832 | tf_op jit(solution)/shard_map/ppermute | solution.py:292
  15.3 1.6 %collective-permute-start.4 = (bf16[160,640]{1,0:T(8,128)(2,1)S(1)}, bf16[160,640]{1,0:T(8,128)(2,1)S(1)}, u32[]{:S(2)}, u32[]{:S(2)}) collective-permute-start(bf16[160,640]{1,0:T(8,128)(2,1)S(1)} %shard_map.79.refs_2_), channel_id=1, source_target_pairs={{0,4},{4,8},{8,12},{12,14},{14,10},{10,6},{6,2},{2,0},{1,5},{5,9},... | collective-permute-start | bytes 614408 | tf_op jit(solution)/shard_map/ppermute | solution.py:292
  17.3 3.9 %collective-permute-done.1.refs_3_ = bf16[160,640]{1,0:T(8,128)(2,1)S(1)} collective-permute-done((bf16[160,640]{1,0:T(8,128)(2,1)}, bf16[160,640]{1,0:T(8,128)(2,1)S(1)}, u32[]{:S(2)}, u32[]{:S(2)}) %collective-permute-start.1) | collective-permute-done | bytes 204832 | tf_op jit(solution)/shard_map/ppermute | solution.py:293
  21.7 1.6 %collective-permute-start.6 = (bf16[160,640]{1,0:T(8,128)(2,1)S(1)}, bf16[160,640]{1,0:T(8,128)(2,1)S(1)}, u32[]{:S(2)}, u32[]{:S(2)}) collective-permute-start(bf16[160,640]{1,0:T(8,128)(2,1)S(1)} %collective-permute-done.2.refs_4_), channel_id=1, source_target_pairs={{0,4},{4,8},{8,12},{12,14},{14,10},{10,6},{6,2},{2,0},{1,5},{5,9},... | collective-permute-start | bytes 614408 | tf_op jit(solution)/shard_map/ppermute | solution.py:292
  24.1 1.6 %collective-permute-start.8 = (bf16[160,640]{1,0:T(8,128)(2,1)S(1)}, bf16[160,640]{1,0:T(8,128)(2,1)S(1)}, u32[]{:S(2)}, u32[]{:S(2)}) collective-permute-start(bf16[160,640]{1,0:T(8,128)(2,1)S(1)} %collective-permute-done.4.refs_6_), channel_id=1, source_target_pairs={{0,4},{4,8},{8,12},{12,14},{14,10},{10,6},{6,2},{2,0},{1,5},{5,9},... | collective-permute-start | bytes 614408 | tf_op jit(solution)/shard_map/ppermute | solution.py:292
  26.1 3.9 %collective-permute-done.5.refs_7_ = bf16[160,640]{1,0:T(8,128)(2,1)S(1)} collective-permute-done((bf16[160,640]{1,0:T(8,128)(2,1)S(1)}, bf16[160,640]{1,0:T(8,128)(2,1)S(1)}, u32[]{:S(2)}, u32[]{:S(2)}) %collective-permute-start.5) | collective-permute-done | bytes 204832 | tf_op jit(solution)/shard_map/ppermute | solution.py:293
  30.5 1.6 %collective-permute-start.11 = (bf16[160,640]{1,0:T(8,128)(2,1)S(1)}, bf16[160,640]{1,0:T(8,128)(2,1)S(1)}, u32[]{:S(2)}, u32[]{:S(2)}) collective-permute-start(bf16[160,640]{1,0:T(8,128)(2,1)S(1)} %collective-permute-done.6.refs_8_), channel_id=1, source_target_pairs={{0,4},{4,8},{8,12},{12,14},{14,10},{10,6},{6,2},{2,0},{1,5},{5,9},... | collective-permute-start | bytes 614408 | tf_op jit(solution)/shard_map/ppermute | solution.py:292
  33.3 1.6 %collective-permute-start.12 = (bf16[160,640]{1,0:T(8,128)(2,1)S(1)}, bf16[160,640]{1,0:T(8,128)(2,1)S(1)}, u32[]{:S(2)}, u32[]{:S(2)}) collective-permute-start(bf16[160,640]{1,0:T(8,128)(2,1)S(1)} %collective-permute-done.8.refs_10_), channel_id=1, source_target_pairs={{0,4},{4,8},{8,12},{12,14},{14,10},{10,6},{6,2},{2,0},{1,5},{5,9},... | collective-permute-start | bytes 614408 | tf_op jit(solution)/shard_map/ppermute | solution.py:301
  35.3 3.6 %shard_map.80 = (bf16[1280,640]{1,0:T(8,128)(2,1)S(1)}, bf16[1280,640]{1,0:T(8,128)(2,1)S(1)}) custom-call(bf16[160,640]{1,0:T(8,128)(2,1)S(1)} %copy-done.2, bf16[160,640]{1,0:T(8,128)(2,1)S(1)} %copy-done.3, bf16[160,640]{1,0:T(8,128)(2,1)S(1)} %shard_map.79.refs_2_, bf16[160,640]{1,0:T(8,128)(2,1)S(1)} %collective-permute-done.1.refs_3_, ...), custom_call_target="tpu_custom_call" | custom-call | flops 1 | bytes 5734400 | tf_op jit(solution)/shard_map/pallas_call | solution.py:28
  41.5 3.0 %shard_map.81 = (bf16[384,640]{1,0:T(8,128)(2,1)S(1)}, bf16[1280,640]{1,0:T(8,128)(2,1)S(1)}, bf16[1280,640]{1,0:T(8,128)(2,1)S(1)}, bf16[1280,640]{1,0:T(8,128)...) custom-call(bf16[384,1280]{1,0:T(8,128)(2,1)S(1)} %get-tuple-element.38.refs_1_.normed, ...), custom_call_target="tpu_custom_call" | custom-call | flops 1887436800 | bytes 11878400 | tf_op jit(solution)/shard_map/pallas_call | solution.py:28
  44.5 2.7 %shard_map.83 = (bf16[384,640]{1,0:T(8,128)(2,1)S(1)}, bf16[1280,640]{1,0:T(8,128)(2,1)S(1)}, bf16[160,640]{1,0:T(8,128)(2,1)S(1)}, bf16[160,640]{1,0:T(8,128)(2,1)S(1)}) custom-call(bf16[2,192,1280]{2,1,0:T(8,128)(2,1)S(1)} %shard_map.82.first, bf16[2,192,1280]{2,1,0:T(8,128)(2,1)S(1)} %collective-permute-done.15.second, ...), custom_call_target="tpu_custom_call" | custom-call | flops 1887436800 | bytes 7782400 | tf_op jit(solution)/shard_map/pallas_call | solution.py:28
  47.2 1.6 %collective-permute-start.17 = (bf16[160,640]{1,0:T(8,128)(2,1)S(1)}, bf16[160,640]{1,0:T(8,128)(2,1)S(1)}, u32[]{:S(2)}, u32[]{:S(2)}) collective-permute-start(bf16[160,640]{1,0:T(8,128)(2,1)S(1)} %get-tuple-element.52), channel_id=1, source_target_pairs={{0,4},{4,8},{8,12},{12,14},{14,10},{10,6},{6,2},{2,0},{1,5},{5,9},... | collective-permute-start | bytes 614408 | tf_op jit(solution)/shard_map/ppermute | solution.py:370
  49.3 2.0 %shard_map.84 = (bf16[2,384,640]{2,1,0:T(8,128)(2,1)S(1)}, bf16[384,640]{1,0:T(8,128)(2,1)S(1)}, bf16[128,640]{1,0:T(8,128)(2,1)S(1)}, bf16[128,640]{1,0:T(8,128)(2,1)S(1)}, bf16[128,640]{1,0:T(8,128)(2,1)S(1)}) custom-call(bf16[384,640]{1,0:T(8,128)(2,1)S(1)} %get-tuple-element.44.d_pre_own, bf16[384,640]{1,0:T(8,128)(2,1)S(1)} %get-tuple-element.48.d_pre_other, ...), custom_call_target="tpu_custom_call" | custom-call | flops 1258291200 | bytes 4587520 | tf_op jit(solution)/shard_map/pallas_call | solution.py:28
  51.4 1.6 %collective-permute-start.21 = (bf16[160,640]{1,0:T(8,128)(2,1)S(1)}, bf16[160,640]{1,0:T(8,128)(2,1)S(1)}, u32[]{:S(2)}, u32[]{:S(2)}) collective-permute-start(bf16[160,640]{1,0:T(8,128)(2,1)S(1)} %shard_map.86), channel_id=1, source_target_pairs={{0,4},{4,8},{8,12},{12,14},{14,10},{10,6},{6,2},{2,0},{1,5},{5,9},... | collective-permute-start | bytes 614408 | tf_op jit(solution)/shard_map/ppermute | solution.py:370
  56.4 1.6 %collective-permute-start.19 = (bf16[160,640]{1,0:T(8,128)(2,1)S(1)}, bf16[160,640]{1,0:T(8,128)(2,1)S(1)}, u32[]{:S(2)}, u32[]{:S(2)}) collective-permute-start(bf16[160,640]{1,0:T(8,128)(2,1)S(1)} %get-tuple-element.54.refs_3_), channel_id=1, source_target_pairs={{0,4},{4,8},{8,12},{12,14},{14,10},{10,6},{6,2},{2,0},{1,5},{5,9},... | collective-permute-start | bytes 614408 | tf_op jit(solution)/shard_map/ppermute | solution.py:370
  59.4 1.5 %collective-permute-done.22.refs_2_ = bf16[160,640]{1,0:T(8,128)(2,1)S(1)} collective-permute-done((bf16[160,640]{1,0:T(8,128)(2,1)S(1)}, bf16[160,640]{1,0:T(8,128)(2,1)S(1)}, u32[]{:S(2)}, u32[]{:S(2)}) %collective-permute-start.22) | collective-permute-done | bytes 204832 | tf_op jit(solution)/shard_map/ppermute | solution.py:370
  61.1 1.6 %collective-permute-start.29 = (bf16[160,640]{1,0:T(8,128)(2,1)S(1)}, bf16[160,640]{1,0:T(8,128)(2,1)S(1)}, u32[]{:S(2)}, u32[]{:S(2)}) collective-permute-start(bf16[160,640]{1,0:T(8,128)(2,1)S(1)} %get-tuple-element.59.refs_3_), channel_id=1, source_target_pairs={{0,4},{4,8},{8,12},{12,14},{14,10},{10,6},{6,2},{2,0},{1,5},{5,9},... | collective-permute-start | bytes 614408 | tf_op jit(solution)/shard_map/ppermute | solution.py:370
  65.6 1.7 %collective-permute-start.27 = (bf16[160,640]{1,0:T(8,128)(2,1)S(1)}, bf16[160,640]{1,0:T(8,128)(2,1)S(1)}, u32[]{:S(2)}, u32[]{:S(2)}) collective-permute-start(bf16[160,640]{1,0:T(8,128)(2,1)S(1)} %get-tuple-element.60.refs_2_), channel_id=1, source_target_pairs={{0,4},{4,8},{8,12},{12,14},{14,10},{10,6},{6,2},{2,0},{1,5},{5,9},... | collective-permute-start | bytes 614408 | tf_op jit(solution)/shard_map/ppermute | solution.py:370
  71.7 2.0 %collective-permute-done.27.refs_3_.refs_1_ = bf16[160,640]{1,0:T(8,128)(2,1)S(1)} collective-permute-done((bf16[160,640]{1,0:T(8,128)(2,1)S(1)}, bf16[160,640]{1,0:T(8,128)(2,1)S(1)}, u32[]{:S(2)}, u32[]{:S(2)}) %collective-permute-start.27) | collective-permute-done | bytes 204832 | tf_op jit(solution)/shard_map/ppermute | solution.py:370
  74.8 1.9 %collective-permute-done.32.refs_1_ = bf16[160,640]{1,0:T(8,128)(2,1)S(1)} collective-permute-done((bf16[160,640]{1,0:T(8,128)(2,1)S(1)}, bf16[160,640]{1,0:T(8,128)(2,1)S(1)}, u32[]{:S(2)}, u32[]{:S(2)}) %collective-permute-start.32) | collective-permute-done | bytes 204832 | tf_op jit(solution)/shard_map/ppermute | solution.py:370
  76.8 1.6 %collective-permute-start.34 = (bf16[160,640]{1,0:T(8,128)(2,1)S(1)}, bf16[160,640]{1,0:T(8,128)(2,1)S(1)}, u32[]{:S(2)}, u32[]{:S(2)}) collective-permute-start(bf16[160,640]{1,0:T(8,128)(2,1)S(1)} %shard_map.93.refs_3_), channel_id=1, source_target_pairs={{0,4},{4,8},{8,12},{12,14},{14,10},{10,6},{6,2},{2,0},{1,5},{5,9},... | collective-permute-start | bytes 614408 | tf_op jit(solution)/shard_map/ppermute | solution.py:370
  (84 shorter events, 33.5 us)
Async XLA Ops:
  4.1 37.4 %collective-permute-start.14 = (bf16[2,192,1280]{2,1,0:T(8,128)(2,1)}, bf16[2,192,1280]{2,1,0:T(8,128)(2,1)S(1)}, u32[]{:S(2)}, u32[]{:S(2)}) collective-permute-start(bf16[2,192,1280]{2,1,0:T(8,128)(2,1)} %get-tuple-element.45), channel_id=1, source_target_pairs={{0,16},{16,0},{1,17},{17,1},{2,18},{18,2},{3,19},{19,3},{4,20},{20... | collective-permute-start | bytes 2949128 | tf_op jit(solution)/shard_map/ppermute | solution.py:278
  7.1 8.2 %collective-permute-start = (bf16[160,640]{1,0:T(8,128)(2,1)}, bf16[160,640]{1,0:T(8,128)(2,1)S(1)}, u32[]{:S(2)}, u32[]{:S(2)}) collective-permute-start(bf16[160,640]{1,0:T(8,128)(2,1)} %get-tuple-element.40.refs_0_), channel_id=1, source_target_pairs={{0,4},{4,8},{8,12},{12,14},{14,10},{10,6},{6,2},{2,0},{1,5},{5,9},... | collective-permute-start | bytes 614408 | tf_op jit(solution)/shard_map/ppermute | solution.py:292
  8.7 8.2 %collective-permute-start.3 = (bf16[160,640]{1,0:T(8,128)(2,1)}, bf16[160,640]{1,0:T(8,128)(2,1)S(1)}, u32[]{:S(2)}, u32[]{:S(2)}) collective-permute-start(bf16[160,640]{1,0:T(8,128)(2,1)} %get-tuple-element.41.refs_1_), channel_id=1, source_target_pairs={{4,0},{8,4},{12,8},{14,12},{10,14},{6,10},{2,6},{0,2},{5,1},{9,5},... | collective-permute-start | bytes 614408 | tf_op jit(solution)/shard_map/ppermute | solution.py:293
  9.1 12.2 %collective-permute-start.1 = (bf16[160,640]{1,0:T(8,128)(2,1)}, bf16[160,640]{1,0:T(8,128)(2,1)S(1)}, u32[]{:S(2)}, u32[]{:S(2)}) collective-permute-start(bf16[160,640]{1,0:T(8,128)(2,1)} %get-tuple-element.40.refs_0_), channel_id=1, source_target_pairs={{4,0},{8,4},{12,8},{14,12},{10,14},{6,10},{2,6},{0,2},{5,1},{9,5},... | collective-permute-start | bytes 614408 | tf_op jit(solution)/shard_map/ppermute | solution.py:293
  10.6 11.1 %collective-permute-start.2 = (bf16[160,640]{1,0:T(8,128)(2,1)}, bf16[160,640]{1,0:T(8,128)(2,1)S(1)}, u32[]{:S(2)}, u32[]{:S(2)}) collective-permute-start(bf16[160,640]{1,0:T(8,128)(2,1)} %get-tuple-element.41.refs_1_), channel_id=1, source_target_pairs={{0,4},{4,8},{8,12},{12,14},{14,10},{10,6},{6,2},{2,0},{1,5},{5,9},... | collective-permute-start | bytes 614408 | tf_op jit(solution)/shard_map/ppermute | solution.py:292
  15.3 8.8 %collective-permute-start.4 = (bf16[160,640]{1,0:T(8,128)(2,1)S(1)}, bf16[160,640]{1,0:T(8,128)(2,1)S(1)}, u32[]{:S(2)}, u32[]{:S(2)}) collective-permute-start(bf16[160,640]{1,0:T(8,128)(2,1)S(1)} %shard_map.79.refs_2_), channel_id=1, source_target_pairs={{0,4},{4,8},{8,12},{12,14},{14,10},{10,6},{6,2},{2,0},{1,5},{5,9},... | collective-permute-start | bytes 614408 | tf_op jit(solution)/shard_map/ppermute | solution.py:292
  16.9 8.8 %collective-permute-start.7 = (bf16[160,640]{1,0:T(8,128)(2,1)S(1)}, bf16[160,640]{1,0:T(8,128)(2,1)S(1)}, u32[]{:S(2)}, u32[]{:S(2)}) collective-permute-start(bf16[160,640]{1,0:T(8,128)(2,1)S(1)} %collective-permute-done.3.refs_5_), channel_id=1, source_target_pairs={{4,0},{8,4},{12,8},{14,12},{10,14},{6,10},{2,6},{0,2},{5,1},{9,5},... | collective-permute-start | bytes 614408 | tf_op jit(solution)/shard_map/ppermute | solution.py:293
  21.3 8.8 %collective-permute-start.5 = (bf16[160,640]{1,0:T(8,128)(2,1)S(1)}, bf16[160,640]{1,0:T(8,128)(2,1)S(1)}, u32[]{:S(2)}, u32[]{:S(2)}) collective-permute-start(bf16[160,640]{1,0:T(8,128)(2,1)S(1)} %collective-permute-done.1.refs_3_), channel_id=1, source_target_pairs={{4,0},{8,4},{12,8},{14,12},{10,14},{6,10},{2,6},{0,2},{5,1},{9,5},... | collective-permute-start | bytes 614408 | tf_op jit(solution)/shard_map/ppermute | solution.py:293
  21.7 8.8 %collective-permute-start.6 = (bf16[160,640]{1,0:T(8,128)(2,1)S(1)}, bf16[160,640]{1,0:T(8,128)(2,1)S(1)}, u32[]{:S(2)}, u32[]{:S(2)}) collective-permute-start(bf16[160,640]{1,0:T(8,128)(2,1)S(1)} %collective-permute-done.2.refs_4_), channel_id=1, source_target_pairs={{0,4},{4,8},{8,12},{12,14},{14,10},{10,6},{6,2},{2,0},{1,5},{5,9},... | collective-permute-start | bytes 614408 | tf_op jit(solution)/shard_map/ppermute | solution.py:292
  24.1 9.2 %collective-permute-start.8 = (bf16[160,640]{1,0:T(8,128)(2,1)S(1)}, bf16[160,640]{1,0:T(8,128)(2,1)S(1)}, u32[]{:S(2)}, u32[]{:S(2)}) collective-permute-start(bf16[160,640]{1,0:T(8,128)(2,1)S(1)} %collective-permute-done.4.refs_6_), channel_id=1, source_target_pairs={{0,4},{4,8},{8,12},{12,14},{14,10},{10,6},{6,2},{2,0},{1,5},{5,9},... | collective-permute-start | bytes 614408 | tf_op jit(solution)/shard_map/ppermute | solution.py:292
  25.7 9.2 %collective-permute-start.9 = (bf16[160,640]{1,0:T(8,128)(2,1)S(1)}, bf16[160,640]{1,0:T(8,128)(2,1)S(1)}, u32[]{:S(2)}, u32[]{:S(2)}) collective-permute-start(bf16[160,640]{1,0:T(8,128)(2,1)S(1)} %collective-permute-done.7.refs_9_), channel_id=1, source_target_pairs={{4,0},{8,4},{12,8},{14,12},{10,14},{6,10},{2,6},{0,2},{5,1},{9,5},... | collective-permute-start | bytes 614408 | tf_op jit(solution)/shard_map/ppermute | solution.py:293
  30.1 8.8 %collective-permute-start.10 = (bf16[160,640]{1,0:T(8,128)(2,1)S(1)}, bf16[160,640]{1,0:T(8,128)(2,1)S(1)}, u32[]{:S(2)}, u32[]{:S(2)}) collective-permute-start(bf16[160,640]{1,0:T(8,128)(2,1)S(1)} %collective-permute-done.5.refs_7_), channel_id=1, source_target_pairs={{4,0},{8,4},{12,8},{14,12},{10,14},{6,10},{2,6},{0,2},{5,1},{9,5},... | collective-permute-start | bytes 614408 | tf_op jit(solution)/shard_map/ppermute | solution.py:293
  30.5 8.4 %collective-permute-start.11 = (bf16[160,640]{1,0:T(8,128)(2,1)S(1)}, bf16[160,640]{1,0:T(8,128)(2,1)S(1)}, u32[]{:S(2)}, u32[]{:S(2)}) collective-permute-start(bf16[160,640]{1,0:T(8,128)(2,1)S(1)} %collective-permute-done.6.refs_8_), channel_id=1, source_target_pairs={{0,4},{4,8},{8,12},{12,14},{14,10},{10,6},{6,2},{2,0},{1,5},{5,9},... | collective-permute-start | bytes 614408 | tf_op jit(solution)/shard_map/ppermute | solution.py:292
  47.2 7.8 %collective-permute-start.17 = (bf16[160,640]{1,0:T(8,128)(2,1)S(1)}, bf16[160,640]{1,0:T(8,128)(2,1)S(1)}, u32[]{:S(2)}, u32[]{:S(2)}) collective-permute-start(bf16[160,640]{1,0:T(8,128)(2,1)S(1)} %get-tuple-element.52), channel_id=1, source_target_pairs={{0,4},{4,8},{8,12},{12,14},{14,10},{10,6},{6,2},{2,0},{1,5},{5,9},... | collective-permute-start | bytes 614408 | tf_op jit(solution)/shard_map/ppermute | solution.py:370
  48.8 7.4 %collective-permute-start.18 = (bf16[160,640]{1,0:T(8,128)(2,1)S(1)}, bf16[160,640]{1,0:T(8,128)(2,1)S(1)}, u32[]{:S(2)}, u32[]{:S(2)}) collective-permute-start(bf16[160,640]{1,0:T(8,128)(2,1)S(1)} %get-tuple-element.53), channel_id=1, source_target_pairs={{4,0},{8,4},{12,8},{14,12},{10,14},{6,10},{2,6},{0,2},{5,1},{9,5},... | collective-permute-start | bytes 614408 | tf_op jit(solution)/shard_map/ppermute | solution.py:370
  51.3 16.4 %collective-permute-start.16 = (bf16[384,640]{1,0:T(8,128)(2,1)S(1)}, bf16[384,640]{1,0:T(8,128)(2,1)S(1)}, u32[]{:S(2)}, u32[]{:S(2)}) collective-permute-start(bf16[384,640]{1,0:T(8,128)(2,1)S(1)} %get-tuple-element.50), channel_id=1, source_target_pairs={{0,1},{1,0},{2,3},{3,2},{4,5},{5,4},{6,7},{7,6},{8,9},{9,8},{10,11... | collective-permute-start | bytes 1474568 | tf_op jit(solution)/shard_map/ppermute | solution.py:346
  51.4 8.0 %collective-permute-start.21 = (bf16[160,640]{1,0:T(8,128)(2,1)S(1)}, bf16[160,640]{1,0:T(8,128)(2,1)S(1)}, u32[]{:S(2)}, u32[]{:S(2)}) collective-permute-start(bf16[160,640]{1,0:T(8,128)(2,1)S(1)} %shard_map.86), channel_id=1, source_target_pairs={{0,4},{4,8},{8,12},{12,14},{14,10},{10,6},{6,2},{2,0},{1,5},{5,9},... | collective-permute-start | bytes 614408 | tf_op jit(solution)/shard_map/ppermute | solution.py:370
  53.0 7.9 %collective-permute-start.22 = (bf16[160,640]{1,0:T(8,128)(2,1)S(1)}, bf16[160,640]{1,0:T(8,128)(2,1)S(1)}, u32[]{:S(2)}, u32[]{:S(2)}) collective-permute-start(bf16[160,640]{1,0:T(8,128)(2,1)S(1)} %shard_map.87), channel_id=1, source_target_pairs={{4,0},{8,4},{12,8},{14,12},{10,14},{6,10},{2,6},{0,2},{5,1},{9,5},... | collective-permute-start | bytes 614408 | tf_op jit(solution)/shard_map/ppermute | solution.py:370
  56.4 7.8 %collective-permute-start.19 = (bf16[160,640]{1,0:T(8,128)(2,1)S(1)}, bf16[160,640]{1,0:T(8,128)(2,1)S(1)}, u32[]{:S(2)}, u32[]{:S(2)}) collective-permute-start(bf16[160,640]{1,0:T(8,128)(2,1)S(1)} %get-tuple-element.54.refs_3_), channel_id=1, source_target_pairs={{0,4},{4,8},{8,12},{12,14},{14,10},{10,6},{6,2},{2,0},{1,5},{5,9},... | collective-permute-start | bytes 614408 | tf_op jit(solution)/shard_map/ppermute | solution.py:370
  58.0 7.4 %collective-permute-start.20 = (bf16[160,640]{1,0:T(8,128)(2,1)S(1)}, bf16[160,640]{1,0:T(8,128)(2,1)S(1)}, u32[]{:S(2)}, u32[]{:S(2)}) collective-permute-start(bf16[160,640]{1,0:T(8,128)(2,1)S(1)} %get-tuple-element.55), channel_id=1, source_target_pairs={{4,0},{8,4},{12,8},{14,12},{10,14},{6,10},{2,6},{0,2},{5,1},{9,5},... | collective-permute-start | bytes 614408 | tf_op jit(solution)/shard_map/ppermute | solution.py:370
  61.1 8.1 %collective-permute-start.29 = (bf16[160,640]{1,0:T(8,128)(2,1)S(1)}, bf16[160,640]{1,0:T(8,128)(2,1)S(1)}, u32[]{:S(2)}, u32[]{:S(2)}) collective-permute-start(bf16[160,640]{1,0:T(8,128)(2,1)S(1)} %get-tuple-element.59.refs_3_), channel_id=1, source_target_pairs={{0,4},{4,8},{8,12},{12,14},{14,10},{10,6},{6,2},{2,0},{1,5},{5,9},... | collective-permute-start | bytes 614408 | tf_op jit(solution)/shard_map/ppermute | solution.py:370
  62.7 7.4 %collective-permute-start.30 = (bf16[160,640]{1,0:T(8,128)(2,1)S(1)}, bf16[160,640]{1,0:T(8,128)(2,1)S(1)}, u32[]{:S(2)}, u32[]{:S(2)}) collective-permute-start(bf16[160,640]{1,0:T(8,128)(2,1)S(1)} %get-tuple-element.66), channel_id=1, source_target_pairs={{4,0},{8,4},{12,8},{14,12},{10,14},{6,10},{2,6},{0,2},{5,1},{9,5},... | collective-permute-start | bytes 614408 | tf_op jit(solution)/shard_map/ppermute | solution.py:370
  65.6 8.1 %collective-permute-start.27 = (bf16[160,640]{1,0:T(8,128)(2,1)S(1)}, bf16[160,640]{1,0:T(8,128)(2,1)S(1)}, u32[]{:S(2)}, u32[]{:S(2)}) collective-permute-start(bf16[160,640]{1,0:T(8,128)(2,1)S(1)} %get-tuple-element.60.refs_2_), channel_id=1, source_target_pairs={{0,4},{4,8},{8,12},{12,14},{14,10},{10,6},{6,2},{2,0},{1,5},{5,9},... | collective-permute-start | bytes 614408 | tf_op jit(solution)/shard_map/ppermute | solution.py:370
  67.8 14.3 %collective-permute-start.23 = (bf16[384,640]{1,0:T(8,128)(2,1)S(1)}, bf16[384,640]{1,0:T(8,128)(2,1)S(1)}, u32[]{:S(2)}, u32[]{:S(2)}) collective-permute-start(bf16[384,640]{1,0:T(8,128)(2,1)S(1)} %shard_map.90.refs_3_), channel_id=1, source_target_pairs={{0,16},{16,0},{1,17},{17,1},{2,18},{18,2},{3,19},{19,3},{4,20},{20... | collective-permute-start | bytes 1474568 | tf_op jit(solution)/shard_map/ppermute | solution.py:350
  (19 other events, 163.7 us)

commit v25 on v24

--- a/solution.py
+++ b/solution.py
@@ -212,8 +212,9 @@
     return value.astype(BF16)
 
 
-def input_kernel(base, factor, sums, came, stats, out):
+def input_kernel(base, factor, sums, came, stats, out, token):
     out[...] = input_rows(base, factor, sums, came, stats)
+    token[...] = jnp.zeros_like(token)
 
 
 def hop_kernel(places, peers, partial, *refs):
@@ -228,9 +229,7 @@
     total[...] = (value + up[...].astype(F32) + down[...].astype(F32)).astype(BF16)
 
 
-def last_kernel(peers, base, factor, sums, came, stats, partial, up, down, passed, *outs):
-    input_grad, up_grad = outs
-    input_grad[...] = input_rows(base, factor, sums, came, stats)
+def last_kernel(peers, partial, up, down, passed, up_grad):
     depth, width = passed.shape
     side = lax.axis_index("groups")
     value = partial[block_rows(0, peers, depth), :].astype(F32)
@@ -361,6 +360,13 @@
             ties=ties,
         )
 
+    def input_gradient(base, factor, sums):
+        return call(
+            input_kernel,
+            (base, factor, sums, lax.ppermute(sums, "gy", swap), stats),
+            (half_rows_of, shape((8, 128), F32)),
+        )
+
     up_grad_of = shape((depth, hidden), F32)
     if ringed:
         came, kept = [{}, {}], []
@@ -404,19 +410,17 @@
         )
         passed = lax.ppermute(passing, "groups", swap)
         send_on(0, [hold(kept[0], passing)], ["down"])
-        base, factor, sums = scale(keep, sent, back, passing)
-        input_grad, up_grad = call(
+        input_grad, token = input_gradient(*scale(keep, sent, back, passing))
+        up_grad = call(
             functools.partial(last_kernel, peers),
-            (base, factor, sums, lax.ppermute(sums, "gy", swap), stats)
-            + (partial[0], came[0]["up"], came[0]["down"], passed),
-            (half_rows_of, up_grad_of),
+            (partial[0], came[0]["up"], came[0]["down"], passed),
+            up_grad_of,
+            ties=(token,),
         )
     else:
         keep, came_other, sent = own_d_norm()
         _, back = over_cores(keep, came_other)
-        base, factor, sums = scale(keep, sent, back)
-        came = lax.ppermute(sums, "gy", swap)
-        input_grad = call(input_kernel, (base, factor, sums, came, stats), half_rows_of)
+        input_grad, _ = input_gradient(*scale(keep, sent, back))
         total, passing = [
             lax.psum_scatter(p.astype(F32), "gx", scatter_dimension=0, tiled=True) for p in partial
         ]

time: 87.5 us -> 87.1 us (level)
  waiting for transfers between devices: 33.8 us -> 32.7 us
    ppermute x14, waiting for transfers between devices: 15.7 us -> 14.6 us  [send_on(): came[i][name] = lax.ppermute(block, 'gx', ahead if name == 'up' else behind)]
    pallas_call x16 -> x17, Pallas kernels: 19 us -> 19.8 us  [call(): pl.pallas_call(body if ties else kernel, out_shape=out_shape, in_specs=[S...]
  transfers between devices with their start and end apart: 37 -> 37, of which waited for: 22 -> 22; matrix products, arithmetic and copies ran while one was open for 0% -> 0% of each run, Pallas kernels for 13% -> 15%
where the time goes in v25:
time: 87.1 us; the launch traced here: 87 us
  starting transfers between devices  33.6 us (39%)
  waiting for transfers between devices  32.7 us (38%)
  Pallas kernels  19.8 us (23%)
    pallas_call x17, Pallas kernels, call(): pl.pallas_call(body if ties else kernel, out_shape=out_shape, in_specs=[S...  19.8 us
    ppermute x14, waiting for transfers between devices, send_on(): came[i][name] = lax.ppermute(block, 'gx', ahead if name == 'up' else behind)  14.6 us
    ppermute x14, starting transfers between devices, send_on(): came[i][name] = lax.ppermute(block, 'gx', ahead if name == 'up' else behind)  14.5 us
    ppermute x6, starting transfers between devices, shards(): up[i] = lax.ppermute(up[i], 'gx', ahead)  8.39 us
    ppermute x6, waiting for transfers between devices, shards(): down[i] = lax.ppermute(down[i], 'gx', behind)  7.92 us
    ppermute x6, waiting for transfers between devices, shards(): up[i] = lax.ppermute(up[i], 'gx', ahead)  4.61 us
    ppermute x6, starting transfers between devices, shards(): down[i] = lax.ppermute(down[i], 'gx', behind)  3.77 us
    ppermute x1, starting transfers between devices, shards(): first = lax.ppermute(passing, 'groups', swap)  3 us
  transfers between devices with their start and end apart: 37, of which 22 were waited for; matrix products, arithmetic and copies ran while one was open for 0% of the time, Pallas kernels for 15%

profile of v25, /device:TPU:0, one launch (start us, length us, event | category | flops | bytes accessed | tf_op | source)
XLA Modules:
  0.0 87.0 jit_solution(11091179507605431483)
XLA Ops:
  0.7 3.4 %shard_map.78 = (bf16[2,192,1280]{2,1,0:T(8,128)(2,1)}, bf16[160,640]{1,0:T(8,128)(2,1)}, bf16[160,640]{1,0:T(8,128)(2,1)}) custom-call(s32[8]{0:T(128)} %lengths.3, bf16[384,1280]{1,0:T(8,128)(2,1)} %bitcast.3, bf16[384,1280]{1,0:T(8,128)(2,1)} %bitcast.6, f32[1280]{0:T(1024)} %gain.3, bf16[160,1280]{1,0:T(8,128)(2,1)} %w_up.1, bf16[160,1280]{1,0:T(8,128)(2,1)} %w_down.1), custom_call_target="tpu_custom_call" | custom-call | flops 2457600 | bytes 4183072 | tf_op jit(solution)/shard_map/pallas_call | solution.py:28
  4.1 3.0 %collective-permute-start.14 = (bf16[2,192,1280]{2,1,0:T(8,128)(2,1)}, bf16[2,192,1280]{2,1,0:T(8,128)(2,1)S(1)}, u32[]{:S(2)}, u32[]{:S(2)}) collective-permute-start(bf16[2,192,1280]{2,1,0:T(8,128)(2,1)} %get-tuple-element.45), channel_id=1, source_target_pairs={{0,16},{16,0},{1,17},{17,1},{2,18},{18,2},{3,19},{19,3},{4,20},{20... | collective-permute-start | bytes 2949128 | tf_op jit(solution)/shard_map/ppermute | solution.py:277
  7.1 1.6 %collective-permute-start = (bf16[160,640]{1,0:T(8,128)(2,1)}, bf16[160,640]{1,0:T(8,128)(2,1)S(1)}, u32[]{:S(2)}, u32[]{:S(2)}) collective-permute-start(bf16[160,640]{1,0:T(8,128)(2,1)} %get-tuple-element.40.refs_0_), channel_id=1, source_target_pairs={{0,4},{4,8},{8,12},{12,14},{14,10},{10,6},{6,2},{2,0},{1,5},{5,9},... | collective-permute-start | bytes 614408 | tf_op jit(solution)/shard_map/ppermute | solution.py:291
  12.6 2.6 %collective-permute-done.refs_0_ = bf16[160,640]{1,0:T(8,128)(2,1)S(1)} collective-permute-done((bf16[160,640]{1,0:T(8,128)(2,1)}, bf16[160,640]{1,0:T(8,128)(2,1)S(1)}, u32[]{:S(2)}, u32[]{:S(2)}) %collective-permute-start) | collective-permute-done | bytes 204832 | tf_op jit(solution)/shard_map/ppermute | solution.py:291
  15.3 1.6 %collective-permute-start.4 = (bf16[160,640]{1,0:T(8,128)(2,1)S(1)}, bf16[160,640]{1,0:T(8,128)(2,1)S(1)}, u32[]{:S(2)}, u32[]{:S(2)}) collective-permute-start(bf16[160,640]{1,0:T(8,128)(2,1)S(1)} %shard_map.79.refs_2_), channel_id=1, source_target_pairs={{0,4},{4,8},{8,12},{12,14},{14,10},{10,6},{6,2},{2,0},{1,5},{5,9},... | collective-permute-start | bytes 614408 | tf_op jit(solution)/shard_map/ppermute | solution.py:291
  17.3 3.9 %collective-permute-done.1.refs_3_ = bf16[160,640]{1,0:T(8,128)(2,1)S(1)} collective-permute-done((bf16[160,640]{1,0:T(8,128)(2,1)}, bf16[160,640]{1,0:T(8,128)(2,1)S(1)}, u32[]{:S(2)}, u32[]{:S(2)}) %collective-permute-start.1) | collective-permute-done | bytes 204832 | tf_op jit(solution)/shard_map/ppermute | solution.py:292
  21.7 1.6 %collective-permute-start.6 = (bf16[160,640]{1,0:T(8,128)(2,1)S(1)}, bf16[160,640]{1,0:T(8,128)(2,1)S(1)}, u32[]{:S(2)}, u32[]{:S(2)}) collective-permute-start(bf16[160,640]{1,0:T(8,128)(2,1)S(1)} %collective-permute-done.2.refs_4_), channel_id=1, source_target_pairs={{0,4},{4,8},{8,12},{12,14},{14,10},{10,6},{6,2},{2,0},{1,5},{5,9},... | collective-permute-start | bytes 614408 | tf_op jit(solution)/shard_map/ppermute | solution.py:291
  24.1 1.6 %collective-permute-start.8 = (bf16[160,640]{1,0:T(8,128)(2,1)S(1)}, bf16[160,640]{1,0:T(8,128)(2,1)S(1)}, u32[]{:S(2)}, u32[]{:S(2)}) collective-permute-start(bf16[160,640]{1,0:T(8,128)(2,1)S(1)} %collective-permute-done.4.refs_6_), channel_id=1, source_target_pairs={{0,4},{4,8},{8,12},{12,14},{14,10},{10,6},{6,2},{2,0},{1,5},{5,9},... | collective-permute-start | bytes 614408 | tf_op jit(solution)/shard_map/ppermute | solution.py:291
  26.1 3.9 %collective-permute-done.5.refs_7_ = bf16[160,640]{1,0:T(8,128)(2,1)S(1)} collective-permute-done((bf16[160,640]{1,0:T(8,128)(2,1)S(1)}, bf16[160,640]{1,0:T(8,128)(2,1)S(1)}, u32[]{:S(2)}, u32[]{:S(2)}) %collective-permute-start.5) | collective-permute-done | bytes 204832 | tf_op jit(solution)/shard_map/ppermute | solution.py:292
  30.5 1.6 %collective-permute-start.11 = (bf16[160,640]{1,0:T(8,128)(2,1)S(1)}, bf16[160,640]{1,0:T(8,128)(2,1)S(1)}, u32[]{:S(2)}, u32[]{:S(2)}) collective-permute-start(bf16[160,640]{1,0:T(8,128)(2,1)S(1)} %collective-permute-done.6.refs_8_), channel_id=1, source_target_pairs={{0,4},{4,8},{8,12},{12,14},{14,10},{10,6},{6,2},{2,0},{1,5},{5,9},... | collective-permute-start | bytes 614408 | tf_op jit(solution)/shard_map/ppermute | solution.py:291
  33.3 1.6 %collective-permute-start.12 = (bf16[160,640]{1,0:T(8,128)(2,1)S(1)}, bf16[160,640]{1,0:T(8,128)(2,1)S(1)}, u32[]{:S(2)}, u32[]{:S(2)}) collective-permute-start(bf16[160,640]{1,0:T(8,128)(2,1)S(1)} %collective-permute-done.8.refs_10_), channel_id=1, source_target_pairs={{0,4},{4,8},{8,12},{12,14},{14,10},{10,6},{6,2},{2,0},{1,5},{5,9},... | collective-permute-start | bytes 614408 | tf_op jit(solution)/shard_map/ppermute | solution.py:300
  35.3 3.6 %shard_map.80 = (bf16[1280,640]{1,0:T(8,128)(2,1)S(1)}, bf16[1280,640]{1,0:T(8,128)(2,1)S(1)}) custom-call(bf16[160,640]{1,0:T(8,128)(2,1)S(1)} %copy-done.2, bf16[160,640]{1,0:T(8,128)(2,1)S(1)} %copy-done.3, bf16[160,640]{1,0:T(8,128)(2,1)S(1)} %shard_map.79.refs_2_, bf16[160,640]{1,0:T(8,128)(2,1)S(1)} %collective-permute-done.1.refs_3_, ...), custom_call_target="tpu_custom_call" | custom-call | flops 1 | bytes 5734400 | tf_op jit(solution)/shard_map/pallas_call | solution.py:28
  41.5 3.0 %shard_map.81 = (bf16[384,640]{1,0:T(8,128)(2,1)S(1)}, bf16[1280,640]{1,0:T(8,128)(2,1)S(1)}, bf16[1280,640]{1,0:T(8,128)(2,1)S(1)}, bf16[1280,640]{1,0:T(8,128)...) custom-call(bf16[384,1280]{1,0:T(8,128)(2,1)S(1)} %get-tuple-element.38.refs_1_.normed, ...), custom_call_target="tpu_custom_call" | custom-call | flops 1887436800 | bytes 11878400 | tf_op jit(solution)/shard_map/pallas_call | solution.py:28
  44.5 2.7 %shard_map.83 = (bf16[384,640]{1,0:T(8,128)(2,1)S(1)}, bf16[1280,640]{1,0:T(8,128)(2,1)S(1)}, bf16[160,640]{1,0:T(8,128)(2,1)S(1)}, bf16[160,640]{1,0:T(8,128)(2,1)S(1)}) custom-call(bf16[2,192,1280]{2,1,0:T(8,128)(2,1)S(1)} %shard_map.82.first, bf16[2,192,1280]{2,1,0:T(8,128)(2,1)S(1)} %collective-permute-done.15.second, ...), custom_call_target="tpu_custom_call" | custom-call | flops 1887436800 | bytes 7782400 | tf_op jit(solution)/shard_map/pallas_call | solution.py:28
  47.2 1.6 %collective-permute-start.17 = (bf16[160,640]{1,0:T(8,128)(2,1)S(1)}, bf16[160,640]{1,0:T(8,128)(2,1)S(1)}, u32[]{:S(2)}, u32[]{:S(2)}) collective-permute-start(bf16[160,640]{1,0:T(8,128)(2,1)S(1)} %get-tuple-element.52), channel_id=1, source_target_pairs={{0,4},{4,8},{8,12},{12,14},{14,10},{10,6},{6,2},{2,0},{1,5},{5,9},... | collective-permute-start | bytes 614408 | tf_op jit(solution)/shard_map/ppermute | solution.py:376
  49.3 2.0 %shard_map.84 = (bf16[2,384,640]{2,1,0:T(8,128)(2,1)S(1)}, bf16[384,640]{1,0:T(8,128)(2,1)S(1)}, bf16[128,640]{1,0:T(8,128)(2,1)S(1)}, bf16[128,640]{1,0:T(8,128)(2,1)S(1)}, bf16[128,640]{1,0:T(8,128)(2,1)S(1)}) custom-call(bf16[384,640]{1,0:T(8,128)(2,1)S(1)} %get-tuple-element.44.d_pre_own, bf16[384,640]{1,0:T(8,128)(2,1)S(1)} %get-tuple-element.48.d_pre_other, ...), custom_call_target="tpu_custom_call" | custom-call | flops 1258291200 | bytes 4587520 | tf_op jit(solution)/shard_map/pallas_call | solution.py:28
  51.4 1.6 %collective-permute-start.21 = (bf16[160,640]{1,0:T(8,128)(2,1)S(1)}, bf16[160,640]{1,0:T(8,128)(2,1)S(1)}, u32[]{:S(2)}, u32[]{:S(2)}) collective-permute-start(bf16[160,640]{1,0:T(8,128)(2,1)S(1)} %shard_map.86), channel_id=1, source_target_pairs={{0,4},{4,8},{8,12},{12,14},{14,10},{10,6},{6,2},{2,0},{1,5},{5,9},... | collective-permute-start | bytes 614408 | tf_op jit(solution)/shard_map/ppermute | solution.py:376
  56.4 1.6 %collective-permute-start.19 = (bf16[160,640]{1,0:T(8,128)(2,1)S(1)}, bf16[160,640]{1,0:T(8,128)(2,1)S(1)}, u32[]{:S(2)}, u32[]{:S(2)}) collective-permute-start(bf16[160,640]{1,0:T(8,128)(2,1)S(1)} %get-tuple-element.54.refs_3_), channel_id=1, source_target_pairs={{0,4},{4,8},{8,12},{12,14},{14,10},{10,6},{6,2},{2,0},{1,5},{5,9},... | collective-permute-start | bytes 614408 | tf_op jit(solution)/shard_map/ppermute | solution.py:376
  59.4 1.5 %collective-permute-done.22.refs_2_ = bf16[160,640]{1,0:T(8,128)(2,1)S(1)} collective-permute-done((bf16[160,640]{1,0:T(8,128)(2,1)S(1)}, bf16[160,640]{1,0:T(8,128)(2,1)S(1)}, u32[]{:S(2)}, u32[]{:S(2)}) %collective-permute-start.22) | collective-permute-done | bytes 204832 | tf_op jit(solution)/shard_map/ppermute | solution.py:376
  61.1 1.6 %collective-permute-start.29 = (bf16[160,640]{1,0:T(8,128)(2,1)S(1)}, bf16[160,640]{1,0:T(8,128)(2,1)S(1)}, u32[]{:S(2)}, u32[]{:S(2)}) collective-permute-start(bf16[160,640]{1,0:T(8,128)(2,1)S(1)} %get-tuple-element.59.refs_3_), channel_id=1, source_target_pairs={{0,4},{4,8},{8,12},{12,14},{14,10},{10,6},{6,2},{2,0},{1,5},{5,9},... | collective-permute-start | bytes 614408 | tf_op jit(solution)/shard_map/ppermute | solution.py:376
  65.6 1.7 %collective-permute-start.27 = (bf16[160,640]{1,0:T(8,128)(2,1)S(1)}, bf16[160,640]{1,0:T(8,128)(2,1)S(1)}, u32[]{:S(2)}, u32[]{:S(2)}) collective-permute-start(bf16[160,640]{1,0:T(8,128)(2,1)S(1)} %get-tuple-element.60.refs_2_), channel_id=1, source_target_pairs={{0,4},{4,8},{8,12},{12,14},{14,10},{10,6},{6,2},{2,0},{1,5},{5,9},... | collective-permute-start | bytes 614408 | tf_op jit(solution)/shard_map/ppermute | solution.py:376
  71.7 2.0 %collective-permute-done.27.refs_3_.refs_1_ = bf16[160,640]{1,0:T(8,128)(2,1)S(1)} collective-permute-done((bf16[160,640]{1,0:T(8,128)(2,1)S(1)}, bf16[160,640]{1,0:T(8,128)(2,1)S(1)}, u32[]{:S(2)}, u32[]{:S(2)}) %collective-permute-start.27) | collective-permute-done | bytes 204832 | tf_op jit(solution)/shard_map/ppermute | solution.py:376
  74.8 1.9 %collective-permute-done.32.refs_1_ = bf16[160,640]{1,0:T(8,128)(2,1)S(1)} collective-permute-done((bf16[160,640]{1,0:T(8,128)(2,1)S(1)}, bf16[160,640]{1,0:T(8,128)(2,1)S(1)}, u32[]{:S(2)}, u32[]{:S(2)}) %collective-permute-start.32) | collective-permute-done | bytes 204832 | tf_op jit(solution)/shard_map/ppermute | solution.py:376
  76.8 1.6 %collective-permute-start.34 = (bf16[160,640]{1,0:T(8,128)(2,1)S(1)}, bf16[160,640]{1,0:T(8,128)(2,1)S(1)}, u32[]{:S(2)}, u32[]{:S(2)}) collective-permute-start(bf16[160,640]{1,0:T(8,128)(2,1)S(1)} %shard_map.93.refs_3_), channel_id=1, source_target_pairs={{0,4},{4,8},{8,12},{12,14},{14,10},{10,6},{6,2},{2,0},{1,5},{5,9},... | collective-permute-start | bytes 614408 | tf_op jit(solution)/shard_map/ppermute | solution.py:376
  (85 shorter events, 33.1 us)
Async XLA Ops:
  4.1 37.4 %collective-permute-start.14 = (bf16[2,192,1280]{2,1,0:T(8,128)(2,1)}, bf16[2,192,1280]{2,1,0:T(8,128)(2,1)S(1)}, u32[]{:S(2)}, u32[]{:S(2)}) collective-permute-start(bf16[2,192,1280]{2,1,0:T(8,128)(2,1)} %get-tuple-element.45), channel_id=1, source_target_pairs={{0,16},{16,0},{1,17},{17,1},{2,18},{18,2},{3,19},{19,3},{4,20},{20... | collective-permute-start | bytes 2949128 | tf_op jit(solution)/shard_map/ppermute | solution.py:277
  7.1 8.2 %collective-permute-start = (bf16[160,640]{1,0:T(8,128)(2,1)}, bf16[160,640]{1,0:T(8,128)(2,1)S(1)}, u32[]{:S(2)}, u32[]{:S(2)}) collective-permute-start(bf16[160,640]{1,0:T(8,128)(2,1)} %get-tuple-element.40.refs_0_), channel_id=1, source_target_pairs={{0,4},{4,8},{8,12},{12,14},{14,10},{10,6},{6,2},{2,0},{1,5},{5,9},... | collective-permute-start | bytes 614408 | tf_op jit(solution)/shard_map/ppermute | solution.py:291
  8.7 8.2 %collective-permute-start.3 = (bf16[160,640]{1,0:T(8,128)(2,1)}, bf16[160,640]{1,0:T(8,128)(2,1)S(1)}, u32[]{:S(2)}, u32[]{:S(2)}) collective-permute-start(bf16[160,640]{1,0:T(8,128)(2,1)} %get-tuple-element.41.refs_1_), channel_id=1, source_target_pairs={{4,0},{8,4},{12,8},{14,12},{10,14},{6,10},{2,6},{0,2},{5,1},{9,5},... | collective-permute-start | bytes 614408 | tf_op jit(solution)/shard_map/ppermute | solution.py:292
  9.1 12.2 %collective-permute-start.1 = (bf16[160,640]{1,0:T(8,128)(2,1)}, bf16[160,640]{1,0:T(8,128)(2,1)S(1)}, u32[]{:S(2)}, u32[]{:S(2)}) collective-permute-start(bf16[160,640]{1,0:T(8,128)(2,1)} %get-tuple-element.40.refs_0_), channel_id=1, source_target_pairs={{4,0},{8,4},{12,8},{14,12},{10,14},{6,10},{2,6},{0,2},{5,1},{9,5},... | collective-permute-start | bytes 614408 | tf_op jit(solution)/shard_map/ppermute | solution.py:292
  10.6 11.1 %collective-permute-start.2 = (bf16[160,640]{1,0:T(8,128)(2,1)}, bf16[160,640]{1,0:T(8,128)(2,1)S(1)}, u32[]{:S(2)}, u32[]{:S(2)}) collective-permute-start(bf16[160,640]{1,0:T(8,128)(2,1)} %get-tuple-element.41.refs_1_), channel_id=1, source_target_pairs={{0,4},{4,8},{8,12},{12,14},{14,10},{10,6},{6,2},{2,0},{1,5},{5,9},... | collective-permute-start | bytes 614408 | tf_op jit(solution)/shard_map/ppermute | solution.py:291
  15.3 8.8 %collective-permute-start.4 = (bf16[160,640]{1,0:T(8,128)(2,1)S(1)}, bf16[160,640]{1,0:T(8,128)(2,1)S(1)}, u32[]{:S(2)}, u32[]{:S(2)}) collective-permute-start(bf16[160,640]{1,0:T(8,128)(2,1)S(1)} %shard_map.79.refs_2_), channel_id=1, source_target_pairs={{0,4},{4,8},{8,12},{12,14},{14,10},{10,6},{6,2},{2,0},{1,5},{5,9},... | collective-permute-start | bytes 614408 | tf_op jit(solution)/shard_map/ppermute | solution.py:291
  16.9 8.8 %collective-permute-start.7 = (bf16[160,640]{1,0:T(8,128)(2,1)S(1)}, bf16[160,640]{1,0:T(8,128)(2,1)S(1)}, u32[]{:S(2)}, u32[]{:S(2)}) collective-permute-start(bf16[160,640]{1,0:T(8,128)(2,1)S(1)} %collective-permute-done.3.refs_5_), channel_id=1, source_target_pairs={{4,0},{8,4},{12,8},{14,12},{10,14},{6,10},{2,6},{0,2},{5,1},{9,5},... | collective-permute-start | bytes 614408 | tf_op jit(solution)/shard_map/ppermute | solution.py:292
  21.3 8.8 %collective-permute-start.5 = (bf16[160,640]{1,0:T(8,128)(2,1)S(1)}, bf16[160,640]{1,0:T(8,128)(2,1)S(1)}, u32[]{:S(2)}, u32[]{:S(2)}) collective-permute-start(bf16[160,640]{1,0:T(8,128)(2,1)S(1)} %collective-permute-done.1.refs_3_), channel_id=1, source_target_pairs={{4,0},{8,4},{12,8},{14,12},{10,14},{6,10},{2,6},{0,2},{5,1},{9,5},... | collective-permute-start | bytes 614408 | tf_op jit(solution)/shard_map/ppermute | solution.py:292
  21.7 8.8 %collective-permute-start.6 = (bf16[160,640]{1,0:T(8,128)(2,1)S(1)}, bf16[160,640]{1,0:T(8,128)(2,1)S(1)}, u32[]{:S(2)}, u32[]{:S(2)}) collective-permute-start(bf16[160,640]{1,0:T(8,128)(2,1)S(1)} %collective-permute-done.2.refs_4_), channel_id=1, source_target_pairs={{0,4},{4,8},{8,12},{12,14},{14,10},{10,6},{6,2},{2,0},{1,5},{5,9},... | collective-permute-start | bytes 614408 | tf_op jit(solution)/shard_map/ppermute | solution.py:291
  24.1 9.2 %collective-permute-start.8 = (bf16[160,640]{1,0:T(8,128)(2,1)S(1)}, bf16[160,640]{1,0:T(8,128)(2,1)S(1)}, u32[]{:S(2)}, u32[]{:S(2)}) collective-permute-start(bf16[160,640]{1,0:T(8,128)(2,1)S(1)} %collective-permute-done.4.refs_6_), channel_id=1, source_target_pairs={{0,4},{4,8},{8,12},{12,14},{14,10},{10,6},{6,2},{2,0},{1,5},{5,9},... | collective-permute-start | bytes 614408 | tf_op jit(solution)/shard_map/ppermute | solution.py:291
  25.7 9.2 %collective-permute-start.9 = (bf16[160,640]{1,0:T(8,128)(2,1)S(1)}, bf16[160,640]{1,0:T(8,128)(2,1)S(1)}, u32[]{:S(2)}, u32[]{:S(2)}) collective-permute-start(bf16[160,640]{1,0:T(8,128)(2,1)S(1)} %collective-permute-done.7.refs_9_), channel_id=1, source_target_pairs={{4,0},{8,4},{12,8},{14,12},{10,14},{6,10},{2,6},{0,2},{5,1},{9,5},... | collective-permute-start | bytes 614408 | tf_op jit(solution)/shard_map/ppermute | solution.py:292
  30.1 8.8 %collective-permute-start.10 = (bf16[160,640]{1,0:T(8,128)(2,1)S(1)}, bf16[160,640]{1,0:T(8,128)(2,1)S(1)}, u32[]{:S(2)}, u32[]{:S(2)}) collective-permute-start(bf16[160,640]{1,0:T(8,128)(2,1)S(1)} %collective-permute-done.5.refs_7_), channel_id=1, source_target_pairs={{4,0},{8,4},{12,8},{14,12},{10,14},{6,10},{2,6},{0,2},{5,1},{9,5},... | collective-permute-start | bytes 614408 | tf_op jit(solution)/shard_map/ppermute | solution.py:292
  30.5 8.4 %collective-permute-start.11 = (bf16[160,640]{1,0:T(8,128)(2,1)S(1)}, bf16[160,640]{1,0:T(8,128)(2,1)S(1)}, u32[]{:S(2)}, u32[]{:S(2)}) collective-permute-start(bf16[160,640]{1,0:T(8,128)(2,1)S(1)} %collective-permute-done.6.refs_8_), channel_id=1, source_target_pairs={{0,4},{4,8},{8,12},{12,14},{14,10},{10,6},{6,2},{2,0},{1,5},{5,9},... | collective-permute-start | bytes 614408 | tf_op jit(solution)/shard_map/ppermute | solution.py:291
  47.2 7.8 %collective-permute-start.17 = (bf16[160,640]{1,0:T(8,128)(2,1)S(1)}, bf16[160,640]{1,0:T(8,128)(2,1)S(1)}, u32[]{:S(2)}, u32[]{:S(2)}) collective-permute-start(bf16[160,640]{1,0:T(8,128)(2,1)S(1)} %get-tuple-element.52), channel_id=1, source_target_pairs={{0,4},{4,8},{8,12},{12,14},{14,10},{10,6},{6,2},{2,0},{1,5},{5,9},... | collective-permute-start | bytes 614408 | tf_op jit(solution)/shard_map/ppermute | solution.py:376
  48.8 7.4 %collective-permute-start.18 = (bf16[160,640]{1,0:T(8,128)(2,1)S(1)}, bf16[160,640]{1,0:T(8,128)(2,1)S(1)}, u32[]{:S(2)}, u32[]{:S(2)}) collective-permute-start(bf16[160,640]{1,0:T(8,128)(2,1)S(1)} %get-tuple-element.53), channel_id=1, source_target_pairs={{4,0},{8,4},{12,8},{14,12},{10,14},{6,10},{2,6},{0,2},{5,1},{9,5},... | collective-permute-start | bytes 614408 | tf_op jit(solution)/shard_map/ppermute | solution.py:376
  51.3 16.4 %collective-permute-start.16 = (bf16[384,640]{1,0:T(8,128)(2,1)S(1)}, bf16[384,640]{1,0:T(8,128)(2,1)S(1)}, u32[]{:S(2)}, u32[]{:S(2)}) collective-permute-start(bf16[384,640]{1,0:T(8,128)(2,1)S(1)} %get-tuple-element.50), channel_id=1, source_target_pairs={{0,1},{1,0},{2,3},{3,2},{4,5},{5,4},{6,7},{7,6},{8,9},{9,8},{10,11... | collective-permute-start | bytes 1474568 | tf_op jit(solution)/shard_map/ppermute | solution.py:345
  51.4 8.0 %collective-permute-start.21 = (bf16[160,640]{1,0:T(8,128)(2,1)S(1)}, bf16[160,640]{1,0:T(8,128)(2,1)S(1)}, u32[]{:S(2)}, u32[]{:S(2)}) collective-permute-start(bf16[160,640]{1,0:T(8,128)(2,1)S(1)} %shard_map.86), channel_id=1, source_target_pairs={{0,4},{4,8},{8,12},{12,14},{14,10},{10,6},{6,2},{2,0},{1,5},{5,9},... | collective-permute-start | bytes 614408 | tf_op jit(solution)/shard_map/ppermute | solution.py:376
  53.0 7.9 %collective-permute-start.22 = (bf16[160,640]{1,0:T(8,128)(2,1)S(1)}, bf16[160,640]{1,0:T(8,128)(2,1)S(1)}, u32[]{:S(2)}, u32[]{:S(2)}) collective-permute-start(bf16[160,640]{1,0:T(8,128)(2,1)S(1)} %shard_map.87), channel_id=1, source_target_pairs={{4,0},{8,4},{12,8},{14,12},{10,14},{6,10},{2,6},{0,2},{5,1},{9,5},... | collective-permute-start | bytes 614408 | tf_op jit(solution)/shard_map/ppermute | solution.py:376
  56.4 7.8 %collective-permute-start.19 = (bf16[160,640]{1,0:T(8,128)(2,1)S(1)}, bf16[160,640]{1,0:T(8,128)(2,1)S(1)}, u32[]{:S(2)}, u32[]{:S(2)}) collective-permute-start(bf16[160,640]{1,0:T(8,128)(2,1)S(1)} %get-tuple-element.54.refs_3_), channel_id=1, source_target_pairs={{0,4},{4,8},{8,12},{12,14},{14,10},{10,6},{6,2},{2,0},{1,5},{5,9},... | collective-permute-start | bytes 614408 | tf_op jit(solution)/shard_map/ppermute | solution.py:376
  58.0 7.4 %collective-permute-start.20 = (bf16[160,640]{1,0:T(8,128)(2,1)S(1)}, bf16[160,640]{1,0:T(8,128)(2,1)S(1)}, u32[]{:S(2)}, u32[]{:S(2)}) collective-permute-start(bf16[160,640]{1,0:T(8,128)(2,1)S(1)} %get-tuple-element.55), channel_id=1, source_target_pairs={{4,0},{8,4},{12,8},{14,12},{10,14},{6,10},{2,6},{0,2},{5,1},{9,5},... | collective-permute-start | bytes 614408 | tf_op jit(solution)/shard_map/ppermute | solution.py:376
  61.1 8.1 %collective-permute-start.29 = (bf16[160,640]{1,0:T(8,128)(2,1)S(1)}, bf16[160,640]{1,0:T(8,128)(2,1)S(1)}, u32[]{:S(2)}, u32[]{:S(2)}) collective-permute-start(bf16[160,640]{1,0:T(8,128)(2,1)S(1)} %get-tuple-element.59.refs_3_), channel_id=1, source_target_pairs={{0,4},{4,8},{8,12},{12,14},{14,10},{10,6},{6,2},{2,0},{1,5},{5,9},... | collective-permute-start | bytes 614408 | tf_op jit(solution)/shard_map/ppermute | solution.py:376
  65.6 8.1 %collective-permute-start.27 = (bf16[160,640]{1,0:T(8,128)(2,1)S(1)}, bf16[160,640]{1,0:T(8,128)(2,1)S(1)}, u32[]{:S(2)}, u32[]{:S(2)}) collective-permute-start(bf16[160,640]{1,0:T(8,128)(2,1)S(1)} %get-tuple-element.60.refs_2_), channel_id=1, source_target_pairs={{0,4},{4,8},{8,12},{12,14},{14,10},{10,6},{6,2},{2,0},{1,5},{5,9},... | collective-permute-start | bytes 614408 | tf_op jit(solution)/shard_map/ppermute | solution.py:376
  67.8 14.3 %collective-permute-start.23 = (bf16[384,640]{1,0:T(8,128)(2,1)S(1)}, bf16[384,640]{1,0:T(8,128)(2,1)S(1)}, u32[]{:S(2)}, u32[]{:S(2)}) collective-permute-start(bf16[384,640]{1,0:T(8,128)(2,1)S(1)} %shard_map.90.refs_3_), channel_id=1, source_target_pairs={{0,16},{16,0},{1,17},{17,1},{2,18},{18,2},{3,19},{19,3},{4,20},{20... | collective-permute-start | bytes 1474568 | tf_op jit(solution)/shard_map/ppermute | solution.py:349
  76.8 8.6 %collective-permute-start.34 = (bf16[160,640]{1,0:T(8,128)(2,1)S(1)}, bf16[160,640]{1,0:T(8,128)(2,1)S(1)}, u32[]{:S(2)}, u32[]{:S(2)}) collective-permute-start(bf16[160,640]{1,0:T(8,128)(2,1)S(1)} %shard_map.93.refs_3_), channel_id=1, source_target_pairs={{0,4},{4,8},{8,12},{12,14},{14,10},{10,6},{6,2},{2,0},{1,5},{5,9},... | collective-permute-start | bytes 614408 | tf_op jit(solution)/shard_map/ppermute | solution.py:376
  (19 other events, 164.9 us)

commit v26 on v25

--- a/solution.py
+++ b/solution.py
@@ -379,7 +379,6 @@
             ways = [("up", half - turn - i), ("down", turn + 1 - i - half)]
             ways = [way for way in ways if way[1] != 0]
             names = [name for name, _ in ways]
-            ties += tuple(came[i][name] for name in came[i] if name not in names)
             blocks = call(
                 functools.partial(hop_kernel, tuple(step for _, step in ways), peers),
                 (partial[i], *[came[i][name] for name in names]),
@@ -401,7 +400,7 @@
         tie, back = over_cores(keep, came_other, tie)
         tie = hop(0, 2, tie)
         for turn in range(3, half):
-            tie = hop(0, turn, hop(1, turn, tie))
+            tie = hop(0, turn, hop(1, turn, tie), came[1]["up"])
         passing = call(
             functools.partial(total_kernel, peers),
             (partial[1], came[1]["up"], came[1]["down"]),

time: 87.1 us -> 87.1 us (level)
  no operation moved by 1% of the time
where the time goes in v26:
time: 87.1 us; the launch traced here: 86.9 us
  starting transfers between devices  33.7 us (39%)
  waiting for transfers between devices  32.5 us (37%)
  Pallas kernels  19.8 us (23%)
    pallas_call x17, Pallas kernels, call(): pl.pallas_call(body if ties else kernel, out_shape=out_shape, in_specs=[S...  19.8 us
    ppermute x14, starting transfers between devices, send_on(): came[i][name] = lax.ppermute(block, 'gx', ahead if name == 'up' else behind)  14.6 us
    ppermute x14, waiting for transfers between devices, send_on(): came[i][name] = lax.ppermute(block, 'gx', ahead if name == 'up' else behind)  14.5 us
    ppermute x6, starting transfers between devices, shards(): up[i] = lax.ppermute(up[i], 'gx', ahead)  8.39 us
    ppermute x6, waiting for transfers between devices, shards(): down[i] = lax.ppermute(down[i], 'gx', behind)  7.92 us
    ppermute x6, waiting for transfers between devices, shards(): up[i] = lax.ppermute(up[i], 'gx', ahead)  4.61 us
    ppermute x6, starting transfers between devices, shards(): down[i] = lax.ppermute(down[i], 'gx', behind)  3.77 us
    ppermute x1, starting transfers between devices, shards(): first = lax.ppermute(passing, 'groups', swap)  3 us
  transfers between devices with their start and end apart: 37, of which 22 were waited for; matrix products, arithmetic and copies ran while one was open for 0% of the time, Pallas kernels for 15%

profile of v26, /device:TPU:0, one launch (start us, length us, event | category | flops | bytes accessed | tf_op | source)
XLA Modules:
  0.0 86.9 jit_solution(4456222643559744142)
XLA Ops:
  0.7 3.4 %shard_map.78 = (bf16[2,192,1280]{2,1,0:T(8,128)(2,1)}, bf16[160,640]{1,0:T(8,128)(2,1)}, bf16[160,640]{1,0:T(8,128)(2,1)}) custom-call(s32[8]{0:T(128)} %lengths.3, bf16[384,1280]{1,0:T(8,128)(2,1)} %bitcast.3, bf16[384,1280]{1,0:T(8,128)(2,1)} %bitcast.6, f32[1280]{0:T(1024)} %gain.3, bf16[160,1280]{1,0:T(8,128)(2,1)} %w_up.1, bf16[160,1280]{1,0:T(8,128)(2,1)} %w_down.1), custom_call_target="tpu_custom_call" | custom-call | flops 2457600 | bytes 4183072 | tf_op jit(solution)/shard_map/pallas_call | solution.py:28
  4.1 3.0 %collective-permute-start.14 = (bf16[2,192,1280]{2,1,0:T(8,128)(2,1)}, bf16[2,192,1280]{2,1,0:T(8,128)(2,1)S(1)}, u32[]{:S(2)}, u32[]{:S(2)}) collective-permute-start(bf16[2,192,1280]{2,1,0:T(8,128)(2,1)} %get-tuple-element.45), channel_id=1, source_target_pairs={{0,16},{16,0},{1,17},{17,1},{2,18},{18,2},{3,19},{19,3},{4,20},{20... | collective-permute-start | bytes 2949128 | tf_op jit(solution)/shard_map/ppermute | solution.py:277
  7.1 1.6 %collective-permute-start = (bf16[160,640]{1,0:T(8,128)(2,1)}, bf16[160,640]{1,0:T(8,128)(2,1)S(1)}, u32[]{:S(2)}, u32[]{:S(2)}) collective-permute-start(bf16[160,640]{1,0:T(8,128)(2,1)} %get-tuple-element.40.refs_0_), channel_id=1, source_target_pairs={{0,4},{4,8},{8,12},{12,14},{14,10},{10,6},{6,2},{2,0},{1,5},{5,9},... | collective-permute-start | bytes 614408 | tf_op jit(solution)/shard_map/ppermute | solution.py:291
  12.6 2.6 %collective-permute-done.refs_0_ = bf16[160,640]{1,0:T(8,128)(2,1)S(1)} collective-permute-done((bf16[160,640]{1,0:T(8,128)(2,1)}, bf16[160,640]{1,0:T(8,128)(2,1)S(1)}, u32[]{:S(2)}, u32[]{:S(2)}) %collective-permute-start) | collective-permute-done | bytes 204832 | tf_op jit(solution)/shard_map/ppermute | solution.py:291
  15.3 1.6 %collective-permute-start.4 = (bf16[160,640]{1,0:T(8,128)(2,1)S(1)}, bf16[160,640]{1,0:T(8,128)(2,1)S(1)}, u32[]{:S(2)}, u32[]{:S(2)}) collective-permute-start(bf16[160,640]{1,0:T(8,128)(2,1)S(1)} %shard_map.79.refs_2_), channel_id=1, source_target_pairs={{0,4},{4,8},{8,12},{12,14},{14,10},{10,6},{6,2},{2,0},{1,5},{5,9},... | collective-permute-start | bytes 614408 | tf_op jit(solution)/shard_map/ppermute | solution.py:291
  17.3 3.9 %collective-permute-done.1.refs_3_ = bf16[160,640]{1,0:T(8,128)(2,1)S(1)} collective-permute-done((bf16[160,640]{1,0:T(8,128)(2,1)}, bf16[160,640]{1,0:T(8,128)(2,1)S(1)}, u32[]{:S(2)}, u32[]{:S(2)}) %collective-permute-start.1) | collective-permute-done | bytes 204832 | tf_op jit(solution)/shard_map/ppermute | solution.py:292
  21.7 1.6 %collective-permute-start.6 = (bf16[160,640]{1,0:T(8,128)(2,1)S(1)}, bf16[160,640]{1,0:T(8,128)(2,1)S(1)}, u32[]{:S(2)}, u32[]{:S(2)}) collective-permute-start(bf16[160,640]{1,0:T(8,128)(2,1)S(1)} %collective-permute-done.2.refs_4_), channel_id=1, source_target_pairs={{0,4},{4,8},{8,12},{12,14},{14,10},{10,6},{6,2},{2,0},{1,5},{5,9},... | collective-permute-start | bytes 614408 | tf_op jit(solution)/shard_map/ppermute | solution.py:291
  24.1 1.6 %collective-permute-start.8 = (bf16[160,640]{1,0:T(8,128)(2,1)S(1)}, bf16[160,640]{1,0:T(8,128)(2,1)S(1)}, u32[]{:S(2)}, u32[]{:S(2)}) collective-permute-start(bf16[160,640]{1,0:T(8,128)(2,1)S(1)} %collective-permute-done.4.refs_6_), channel_id=1, source_target_pairs={{0,4},{4,8},{8,12},{12,14},{14,10},{10,6},{6,2},{2,0},{1,5},{5,9},... | collective-permute-start | bytes 614408 | tf_op jit(solution)/shard_map/ppermute | solution.py:291
  26.1 3.9 %collective-permute-done.5.refs_7_ = bf16[160,640]{1,0:T(8,128)(2,1)S(1)} collective-permute-done((bf16[160,640]{1,0:T(8,128)(2,1)S(1)}, bf16[160,640]{1,0:T(8,128)(2,1)S(1)}, u32[]{:S(2)}, u32[]{:S(2)}) %collective-permute-start.5) | collective-permute-done | bytes 204832 | tf_op jit(solution)/shard_map/ppermute | solution.py:292
  30.5 1.6 %collective-permute-start.11 = (bf16[160,640]{1,0:T(8,128)(2,1)S(1)}, bf16[160,640]{1,0:T(8,128)(2,1)S(1)}, u32[]{:S(2)}, u32[]{:S(2)}) collective-permute-start(bf16[160,640]{1,0:T(8,128)(2,1)S(1)} %collective-permute-done.6.refs_8_), channel_id=1, source_target_pairs={{0,4},{4,8},{8,12},{12,14},{14,10},{10,6},{6,2},{2,0},{1,5},{5,9},... | collective-permute-start | bytes 614408 | tf_op jit(solution)/shard_map/ppermute | solution.py:291
  33.3 1.6 %collective-permute-start.12 = (bf16[160,640]{1,0:T(8,128)(2,1)S(1)}, bf16[160,640]{1,0:T(8,128)(2,1)S(1)}, u32[]{:S(2)}, u32[]{:S(2)}) collective-permute-start(bf16[160,640]{1,0:T(8,128)(2,1)S(1)} %collective-permute-done.8.refs_10_), channel_id=1, source_target_pairs={{0,4},{4,8},{8,12},{12,14},{14,10},{10,6},{6,2},{2,0},{1,5},{5,9},... | collective-permute-start | bytes 614408 | tf_op jit(solution)/shard_map/ppermute | solution.py:300
  35.3 3.6 %shard_map.80 = (bf16[1280,640]{1,0:T(8,128)(2,1)S(1)}, bf16[1280,640]{1,0:T(8,128)(2,1)S(1)}) custom-call(bf16[160,640]{1,0:T(8,128)(2,1)S(1)} %copy-done.2, bf16[160,640]{1,0:T(8,128)(2,1)S(1)} %copy-done.3, bf16[160,640]{1,0:T(8,128)(2,1)S(1)} %shard_map.79.refs_2_, bf16[160,640]{1,0:T(8,128)(2,1)S(1)} %collective-permute-done.1.refs_3_, ...), custom_call_target="tpu_custom_call" | custom-call | flops 1 | bytes 5734400 | tf_op jit(solution)/shard_map/pallas_call | solution.py:28
  41.5 3.0 %shard_map.81 = (bf16[384,640]{1,0:T(8,128)(2,1)S(1)}, bf16[1280,640]{1,0:T(8,128)(2,1)S(1)}, bf16[1280,640]{1,0:T(8,128)(2,1)S(1)}, bf16[1280,640]{1,0:T(8,128)...) custom-call(bf16[384,1280]{1,0:T(8,128)(2,1)S(1)} %get-tuple-element.38.refs_1_.normed, ...), custom_call_target="tpu_custom_call" | custom-call | flops 1887436800 | bytes 11878400 | tf_op jit(solution)/shard_map/pallas_call | solution.py:28
  44.5 2.7 %shard_map.83 = (bf16[384,640]{1,0:T(8,128)(2,1)S(1)}, bf16[1280,640]{1,0:T(8,128)(2,1)S(1)}, bf16[160,640]{1,0:T(8,128)(2,1)S(1)}, bf16[160,640]{1,0:T(8,128)(2,1)S(1)}) custom-call(bf16[2,192,1280]{2,1,0:T(8,128)(2,1)S(1)} %shard_map.82.first, bf16[2,192,1280]{2,1,0:T(8,128)(2,1)S(1)} %collective-permute-done.15.second, ...), custom_call_target="tpu_custom_call" | custom-call | flops 1887436800 | bytes 7782400 | tf_op jit(solution)/shard_map/pallas_call | solution.py:28
  47.2 1.6 %collective-permute-start.17 = (bf16[160,640]{1,0:T(8,128)(2,1)S(1)}, bf16[160,640]{1,0:T(8,128)(2,1)S(1)}, u32[]{:S(2)}, u32[]{:S(2)}) collective-permute-start(bf16[160,640]{1,0:T(8,128)(2,1)S(1)} %get-tuple-element.52), channel_id=1, source_target_pairs={{0,4},{4,8},{8,12},{12,14},{14,10},{10,6},{6,2},{2,0},{1,5},{5,9},... | collective-permute-start | bytes 614408 | tf_op jit(solution)/shard_map/ppermute | solution.py:376
  49.3 2.0 %shard_map.84 = (bf16[2,384,640]{2,1,0:T(8,128)(2,1)S(1)}, bf16[384,640]{1,0:T(8,128)(2,1)S(1)}, bf16[128,640]{1,0:T(8,128)(2,1)S(1)}, bf16[128,640]{1,0:T(8,128)(2,1)S(1)}, bf16[128,640]{1,0:T(8,128)(2,1)S(1)}) custom-call(bf16[384,640]{1,0:T(8,128)(2,1)S(1)} %get-tuple-element.44.d_pre_own, bf16[384,640]{1,0:T(8,128)(2,1)S(1)} %get-tuple-element.48.d_pre_other, ...), custom_call_target="tpu_custom_call" | custom-call | flops 1258291200 | bytes 4587520 | tf_op jit(solution)/shard_map/pallas_call | solution.py:28
  51.4 1.6 %collective-permute-start.21 = (bf16[160,640]{1,0:T(8,128)(2,1)S(1)}, bf16[160,640]{1,0:T(8,128)(2,1)S(1)}, u32[]{:S(2)}, u32[]{:S(2)}) collective-permute-start(bf16[160,640]{1,0:T(8,128)(2,1)S(1)} %shard_map.86), channel_id=1, source_target_pairs={{0,4},{4,8},{8,12},{12,14},{14,10},{10,6},{6,2},{2,0},{1,5},{5,9},... | collective-permute-start | bytes 614408 | tf_op jit(solution)/shard_map/ppermute | solution.py:376
  56.4 1.6 %collective-permute-start.19 = (bf16[160,640]{1,0:T(8,128)(2,1)S(1)}, bf16[160,640]{1,0:T(8,128)(2,1)S(1)}, u32[]{:S(2)}, u32[]{:S(2)}) collective-permute-start(bf16[160,640]{1,0:T(8,128)(2,1)S(1)} %get-tuple-element.54.refs_3_), channel_id=1, source_target_pairs={{0,4},{4,8},{8,12},{12,14},{14,10},{10,6},{6,2},{2,0},{1,5},{5,9},... | collective-permute-start | bytes 614408 | tf_op jit(solution)/shard_map/ppermute | solution.py:376
  61.1 1.6 %collective-permute-start.29 = (bf16[160,640]{1,0:T(8,128)(2,1)S(1)}, bf16[160,640]{1,0:T(8,128)(2,1)S(1)}, u32[]{:S(2)}, u32[]{:S(2)}) collective-permute-start(bf16[160,640]{1,0:T(8,128)(2,1)S(1)} %get-tuple-element.59.refs_3_), channel_id=1, source_target_pairs={{0,4},{4,8},{8,12},{12,14},{14,10},{10,6},{6,2},{2,0},{1,5},{5,9},... | collective-permute-start | bytes 614408 | tf_op jit(solution)/shard_map/ppermute | solution.py:376
  66.1 1.6 %collective-permute-start.27 = (bf16[160,640]{1,0:T(8,128)(2,1)S(1)}, bf16[160,640]{1,0:T(8,128)(2,1)S(1)}, u32[]{:S(2)}, u32[]{:S(2)}) collective-permute-start(bf16[160,640]{1,0:T(8,128)(2,1)S(1)} %get-tuple-element.60.refs_2_), channel_id=1, source_target_pairs={{0,4},{4,8},{8,12},{12,14},{14,10},{10,6},{6,2},{2,0},{1,5},{5,9},... | collective-permute-start | bytes 614408 | tf_op jit(solution)/shard_map/ppermute | solution.py:376
  69.1 1.6 %collective-permute-done.30.refs_2_ = bf16[160,640]{1,0:T(8,128)(2,1)S(1)} collective-permute-done((bf16[160,640]{1,0:T(8,128)(2,1)S(1)}, bf16[160,640]{1,0:T(8,128)(2,1)S(1)}, u32[]{:S(2)}, u32[]{:S(2)}) %collective-permute-start.30) | collective-permute-done | bytes 204832 | tf_op jit(solution)/shard_map/ppermute | solution.py:376
  70.8 1.6 %collective-permute-start.32 = (bf16[160,640]{1,0:T(8,128)(2,1)S(1)}, bf16[160,640]{1,0:T(8,128)(2,1)S(1)}, u32[]{:S(2)}, u32[]{:S(2)}) collective-permute-start(bf16[160,640]{1,0:T(8,128)(2,1)S(1)} %get-tuple-element.67.refs_2_), channel_id=1, source_target_pairs={{0,4},{4,8},{8,12},{12,14},{14,10},{10,6},{6,2},{2,0},{1,5},{5,9},... | collective-permute-start | bytes 614408 | tf_op jit(solution)/shard_map/ppermute | solution.py:376
  74.7 2.0 %collective-permute-done.32.refs_1_ = bf16[160,640]{1,0:T(8,128)(2,1)S(1)} collective-permute-done((bf16[160,640]{1,0:T(8,128)(2,1)S(1)}, bf16[160,640]{1,0:T(8,128)(2,1)S(1)}, u32[]{:S(2)}, u32[]{:S(2)}) %collective-permute-start.32) | collective-permute-done | bytes 204832 | tf_op jit(solution)/shard_map/ppermute | solution.py:376
  76.8 1.6 %collective-permute-start.34 = (bf16[160,640]{1,0:T(8,128)(2,1)S(1)}, bf16[160,640]{1,0:T(8,128)(2,1)S(1)}, u32[]{:S(2)}, u32[]{:S(2)}) collective-permute-start(bf16[160,640]{1,0:T(8,128)(2,1)S(1)} %shard_map.93.refs_3_), channel_id=1, source_target_pairs={{0,4},{4,8},{8,12},{12,14},{14,10},{10,6},{6,2},{2,0},{1,5},{5,9},... | collective-permute-start | bytes 614408 | tf_op jit(solution)/shard_map/ppermute | solution.py:376
  (85 shorter events, 33.5 us)
Async XLA Ops:
  4.1 37.4 %collective-permute-start.14 = (bf16[2,192,1280]{2,1,0:T(8,128)(2,1)}, bf16[2,192,1280]{2,1,0:T(8,128)(2,1)S(1)}, u32[]{:S(2)}, u32[]{:S(2)}) collective-permute-start(bf16[2,192,1280]{2,1,0:T(8,128)(2,1)} %get-tuple-element.45), channel_id=1, source_target_pairs={{0,16},{16,0},{1,17},{17,1},{2,18},{18,2},{3,19},{19,3},{4,20},{20... | collective-permute-start | bytes 2949128 | tf_op jit(solution)/shard_map/ppermute | solution.py:277
  7.1 8.2 %collective-permute-start = (bf16[160,640]{1,0:T(8,128)(2,1)}, bf16[160,640]{1,0:T(8,128)(2,1)S(1)}, u32[]{:S(2)}, u32[]{:S(2)}) collective-permute-start(bf16[160,640]{1,0:T(8,128)(2,1)} %get-tuple-element.40.refs_0_), channel_id=1, source_target_pairs={{0,4},{4,8},{8,12},{12,14},{14,10},{10,6},{6,2},{2,0},{1,5},{5,9},... | collective-permute-start | bytes 614408 | tf_op jit(solution)/shard_map/ppermute | solution.py:291
  8.7 8.2 %collective-permute-start.3 = (bf16[160,640]{1,0:T(8,128)(2,1)}, bf16[160,640]{1,0:T(8,128)(2,1)S(1)}, u32[]{:S(2)}, u32[]{:S(2)}) collective-permute-start(bf16[160,640]{1,0:T(8,128)(2,1)} %get-tuple-element.41.refs_1_), channel_id=1, source_target_pairs={{4,0},{8,4},{12,8},{14,12},{10,14},{6,10},{2,6},{0,2},{5,1},{9,5},... | collective-permute-start | bytes 614408 | tf_op jit(solution)/shard_map/ppermute | solution.py:292
  9.1 12.2 %collective-permute-start.1 = (bf16[160,640]{1,0:T(8,128)(2,1)}, bf16[160,640]{1,0:T(8,128)(2,1)S(1)}, u32[]{:S(2)}, u32[]{:S(2)}) collective-permute-start(bf16[160,640]{1,0:T(8,128)(2,1)} %get-tuple-element.40.refs_0_), channel_id=1, source_target_pairs={{4,0},{8,4},{12,8},{14,12},{10,14},{6,10},{2,6},{0,2},{5,1},{9,5},... | collective-permute-start | bytes 614408 | tf_op jit(solution)/shard_map/ppermute | solution.py:292
  10.6 11.1 %collective-permute-start.2 = (bf16[160,640]{1,0:T(8,128)(2,1)}, bf16[160,640]{1,0:T(8,128)(2,1)S(1)}, u32[]{:S(2)}, u32[]{:S(2)}) collective-permute-start(bf16[160,640]{1,0:T(8,128)(2,1)} %get-tuple-element.41.refs_1_), channel_id=1, source_target_pairs={{0,4},{4,8},{8,12},{12,14},{14,10},{10,6},{6,2},{2,0},{1,5},{5,9},... | collective-permute-start | bytes 614408 | tf_op jit(solution)/shard_map/ppermute | solution.py:291
  15.3 8.8 %collective-permute-start.4 = (bf16[160,640]{1,0:T(8,128)(2,1)S(1)}, bf16[160,640]{1,0:T(8,128)(2,1)S(1)}, u32[]{:S(2)}, u32[]{:S(2)}) collective-permute-start(bf16[160,640]{1,0:T(8,128)(2,1)S(1)} %shard_map.79.refs_2_), channel_id=1, source_target_pairs={{0,4},{4,8},{8,12},{12,14},{14,10},{10,6},{6,2},{2,0},{1,5},{5,9},... | collective-permute-start | bytes 614408 | tf_op jit(solution)/shard_map/ppermute | solution.py:291
  16.9 8.8 %collective-permute-start.7 = (bf16[160,640]{1,0:T(8,128)(2,1)S(1)}, bf16[160,640]{1,0:T(8,128)(2,1)S(1)}, u32[]{:S(2)}, u32[]{:S(2)}) collective-permute-start(bf16[160,640]{1,0:T(8,128)(2,1)S(1)} %collective-permute-done.3.refs_5_), channel_id=1, source_target_pairs={{4,0},{8,4},{12,8},{14,12},{10,14},{6,10},{2,6},{0,2},{5,1},{9,5},... | collective-permute-start | bytes 614408 | tf_op jit(solution)/shard_map/ppermute | solution.py:292
  21.3 8.8 %collective-permute-start.5 = (bf16[160,640]{1,0:T(8,128)(2,1)S(1)}, bf16[160,640]{1,0:T(8,128)(2,1)S(1)}, u32[]{:S(2)}, u32[]{:S(2)}) collective-permute-start(bf16[160,640]{1,0:T(8,128)(2,1)S(1)} %collective-permute-done.1.refs_3_), channel_id=1, source_target_pairs={{4,0},{8,4},{12,8},{14,12},{10,14},{6,10},{2,6},{0,2},{5,1},{9,5},... | collective-permute-start | bytes 614408 | tf_op jit(solution)/shard_map/ppermute | solution.py:292
  21.7 8.8 %collective-permute-start.6 = (bf16[160,640]{1,0:T(8,128)(2,1)S(1)}, bf16[160,640]{1,0:T(8,128)(2,1)S(1)}, u32[]{:S(2)}, u32[]{:S(2)}) collective-permute-start(bf16[160,640]{1,0:T(8,128)(2,1)S(1)} %collective-permute-done.2.refs_4_), channel_id=1, source_target_pairs={{0,4},{4,8},{8,12},{12,14},{14,10},{10,6},{6,2},{2,0},{1,5},{5,9},... | collective-permute-start | bytes 614408 | tf_op jit(solution)/shard_map/ppermute | solution.py:291
  24.1 9.2 %collective-permute-start.8 = (bf16[160,640]{1,0:T(8,128)(2,1)S(1)}, bf16[160,640]{1,0:T(8,128)(2,1)S(1)}, u32[]{:S(2)}, u32[]{:S(2)}) collective-permute-start(bf16[160,640]{1,0:T(8,128)(2,1)S(1)} %collective-permute-done.4.refs_6_), channel_id=1, source_target_pairs={{0,4},{4,8},{8,12},{12,14},{14,10},{10,6},{6,2},{2,0},{1,5},{5,9},... | collective-permute-start | bytes 614408 | tf_op jit(solution)/shard_map/ppermute | solution.py:291
  25.7 9.2 %collective-permute-start.9 = (bf16[160,640]{1,0:T(8,128)(2,1)S(1)}, bf16[160,640]{1,0:T(8,128)(2,1)S(1)}, u32[]{:S(2)}, u32[]{:S(2)}) collective-permute-start(bf16[160,640]{1,0:T(8,128)(2,1)S(1)} %collective-permute-done.7.refs_9_), channel_id=1, source_target_pairs={{4,0},{8,4},{12,8},{14,12},{10,14},{6,10},{2,6},{0,2},{5,1},{9,5},... | collective-permute-start | bytes 614408 | tf_op jit(solution)/shard_map/ppermute | solution.py:292
  30.1 8.8 %collective-permute-start.10 = (bf16[160,640]{1,0:T(8,128)(2,1)S(1)}, bf16[160,640]{1,0:T(8,128)(2,1)S(1)}, u32[]{:S(2)}, u32[]{:S(2)}) collective-permute-start(bf16[160,640]{1,0:T(8,128)(2,1)S(1)} %collective-permute-done.5.refs_7_), channel_id=1, source_target_pairs={{4,0},{8,4},{12,8},{14,12},{10,14},{6,10},{2,6},{0,2},{5,1},{9,5},... | collective-permute-start | bytes 614408 | tf_op jit(solution)/shard_map/ppermute | solution.py:292
  30.5 8.4 %collective-permute-start.11 = (bf16[160,640]{1,0:T(8,128)(2,1)S(1)}, bf16[160,640]{1,0:T(8,128)(2,1)S(1)}, u32[]{:S(2)}, u32[]{:S(2)}) collective-permute-start(bf16[160,640]{1,0:T(8,128)(2,1)S(1)} %collective-permute-done.6.refs_8_), channel_id=1, source_target_pairs={{0,4},{4,8},{8,12},{12,14},{14,10},{10,6},{6,2},{2,0},{1,5},{5,9},... | collective-permute-start | bytes 614408 | tf_op jit(solution)/shard_map/ppermute | solution.py:291
  47.2 7.8 %collective-permute-start.17 = (bf16[160,640]{1,0:T(8,128)(2,1)S(1)}, bf16[160,640]{1,0:T(8,128)(2,1)S(1)}, u32[]{:S(2)}, u32[]{:S(2)}) collective-permute-start(bf16[160,640]{1,0:T(8,128)(2,1)S(1)} %get-tuple-element.52), channel_id=1, source_target_pairs={{0,4},{4,8},{8,12},{12,14},{14,10},{10,6},{6,2},{2,0},{1,5},{5,9},... | collective-permute-start | bytes 614408 | tf_op jit(solution)/shard_map/ppermute | solution.py:376
  51.3 16.4 %collective-permute-start.16 = (bf16[384,640]{1,0:T(8,128)(2,1)S(1)}, bf16[384,640]{1,0:T(8,128)(2,1)S(1)}, u32[]{:S(2)}, u32[]{:S(2)}) collective-permute-start(bf16[384,640]{1,0:T(8,128)(2,1)S(1)} %get-tuple-element.50), channel_id=1, source_target_pairs={{0,1},{1,0},{2,3},{3,2},{4,5},{5,4},{6,7},{7,6},{8,9},{9,8},{10,11... | collective-permute-start | bytes 1474568 | tf_op jit(solution)/shard_map/ppermute | solution.py:345
  51.4 8.0 %collective-permute-start.21 = (bf16[160,640]{1,0:T(8,128)(2,1)S(1)}, bf16[160,640]{1,0:T(8,128)(2,1)S(1)}, u32[]{:S(2)}, u32[]{:S(2)}) collective-permute-start(bf16[160,640]{1,0:T(8,128)(2,1)S(1)} %shard_map.86), channel_id=1, source_target_pairs={{0,4},{4,8},{8,12},{12,14},{14,10},{10,6},{6,2},{2,0},{1,5},{5,9},... | collective-permute-start | bytes 614408 | tf_op jit(solution)/shard_map/ppermute | solution.py:376
  53.0 7.9 %collective-permute-start.22 = (bf16[160,640]{1,0:T(8,128)(2,1)S(1)}, bf16[160,640]{1,0:T(8,128)(2,1)S(1)}, u32[]{:S(2)}, u32[]{:S(2)}) collective-permute-start(bf16[160,640]{1,0:T(8,128)(2,1)S(1)} %shard_map.87), channel_id=1, source_target_pairs={{4,0},{8,4},{12,8},{14,12},{10,14},{6,10},{2,6},{0,2},{5,1},{9,5},... | collective-permute-start | bytes 614408 | tf_op jit(solution)/shard_map/ppermute | solution.py:376
  56.4 7.8 %collective-permute-start.19 = (bf16[160,640]{1,0:T(8,128)(2,1)S(1)}, bf16[160,640]{1,0:T(8,128)(2,1)S(1)}, u32[]{:S(2)}, u32[]{:S(2)}) collective-permute-start(bf16[160,640]{1,0:T(8,128)(2,1)S(1)} %get-tuple-element.54.refs_3_), channel_id=1, source_target_pairs={{0,4},{4,8},{8,12},{12,14},{14,10},{10,6},{6,2},{2,0},{1,5},{5,9},... | collective-permute-start | bytes 614408 | tf_op jit(solution)/shard_map/ppermute | solution.py:376
  61.1 8.1 %collective-permute-start.29 = (bf16[160,640]{1,0:T(8,128)(2,1)S(1)}, bf16[160,640]{1,0:T(8,128)(2,1)S(1)}, u32[]{:S(2)}, u32[]{:S(2)}) collective-permute-start(bf16[160,640]{1,0:T(8,128)(2,1)S(1)} %get-tuple-element.59.refs_3_), channel_id=1, source_target_pairs={{0,4},{4,8},{8,12},{12,14},{14,10},{10,6},{6,2},{2,0},{1,5},{5,9},... | collective-permute-start | bytes 614408 | tf_op jit(solution)/shard_map/ppermute | solution.py:376
  62.7 8.0 %collective-permute-start.30 = (bf16[160,640]{1,0:T(8,128)(2,1)S(1)}, bf16[160,640]{1,0:T(8,128)(2,1)S(1)}, u32[]{:S(2)}, u32[]{:S(2)}) collective-permute-start(bf16[160,640]{1,0:T(8,128)(2,1)S(1)} %get-tuple-element.66), channel_id=1, source_target_pairs={{4,0},{8,4},{12,8},{14,12},{10,14},{6,10},{2,6},{0,2},{5,1},{9,5},... | collective-permute-start | bytes 614408 | tf_op jit(solution)/shard_map/ppermute | solution.py:376
  65.6 8.0 %collective-permute-start.28 = (bf16[160,640]{1,0:T(8,128)(2,1)S(1)}, bf16[160,640]{1,0:T(8,128)(2,1)S(1)}, u32[]{:S(2)}, u32[]{:S(2)}) collective-permute-start(bf16[160,640]{1,0:T(8,128)(2,1)S(1)} %get-tuple-element.65), channel_id=1, source_target_pairs={{4,0},{8,4},{12,8},{14,12},{10,14},{6,10},{2,6},{0,2},{5,1},{9,5},... | collective-permute-start | bytes 614408 | tf_op jit(solution)/shard_map/ppermute | solution.py:376
  66.1 8.1 %collective-permute-start.27 = (bf16[160,640]{1,0:T(8,128)(2,1)S(1)}, bf16[160,640]{1,0:T(8,128)(2,1)S(1)}, u32[]{:S(2)}, u32[]{:S(2)}) collective-permute-start(bf16[160,640]{1,0:T(8,128)(2,1)S(1)} %get-tuple-element.60.refs_2_), channel_id=1, source_target_pairs={{0,4},{4,8},{8,12},{12,14},{14,10},{10,6},{6,2},{2,0},{1,5},{5,9},... | collective-permute-start | bytes 614408 | tf_op jit(solution)/shard_map/ppermute | solution.py:376
  67.8 14.3 %collective-permute-start.23 = (bf16[384,640]{1,0:T(8,128)(2,1)S(1)}, bf16[384,640]{1,0:T(8,128)(2,1)S(1)}, u32[]{:S(2)}, u32[]{:S(2)}) collective-permute-start(bf16[384,640]{1,0:T(8,128)(2,1)S(1)} %shard_map.90.refs_3_), channel_id=1, source_target_pairs={{0,16},{16,0},{1,17},{17,1},{2,18},{18,2},{3,19},{19,3},{4,20},{20... | collective-permute-start | bytes 1474568 | tf_op jit(solution)/shard_map/ppermute | solution.py:349
  76.8 8.5 %collective-permute-start.34 = (bf16[160,640]{1,0:T(8,128)(2,1)S(1)}, bf16[160,640]{1,0:T(8,128)(2,1)S(1)}, u32[]{:S(2)}, u32[]{:S(2)}) collective-permute-start(bf16[160,640]{1,0:T(8,128)(2,1)S(1)} %shard_map.93.refs_3_), channel_id=1, source_target_pairs={{0,4},{4,8},{8,12},{12,14},{14,10},{10,6},{6,2},{2,0},{1,5},{5,9},... | collective-permute-start | bytes 614408 | tf_op jit(solution)/shard_map/ppermute | solution.py:376
  (19 other events, 165.4 us)

commit v27 on v26

--- a/solution.py
+++ b/solution.py
@@ -408,7 +408,7 @@
             ties=(tie,),
         )
         passed = lax.ppermute(passing, "groups", swap)
-        send_on(0, [hold(kept[0], passing)], ["down"])
+        send_on(0, [hold(kept[0], passing, sent[0], sent[1])], ["down"])
         input_grad, token = input_gradient(*scale(keep, sent, back, passing))
         up_grad = call(
             functools.partial(last_kernel, peers),

time: 87.1 us -> 87.1 us (level)
  no operation moved by 1% of the time
where the time goes in v27:
time: 87.1 us; the launch traced here: 86.9 us
  starting transfers between devices  33.7 us (39%)
  waiting for transfers between devices  32.5 us (37%)
  Pallas kernels  19.8 us (23%)
    pallas_call x17, Pallas kernels, call(): pl.pallas_call(body if ties else kernel, out_shape=out_shape, in_specs=[S...  19.8 us
    ppermute x14, starting transfers between devices, send_on(): came[i][name] = lax.ppermute(block, 'gx', ahead if name == 'up' else behind)  14.6 us
    ppermute x14, waiting for transfers between devices, send_on(): came[i][name] = lax.ppermute(block, 'gx', ahead if name == 'up' else behind)  14.5 us
    ppermute x6, starting transfers between devices, shards(): up[i] = lax.ppermute(up[i], 'gx', ahead)  8.39 us
    ppermute x6, waiting for transfers between devices, shards(): down[i] = lax.ppermute(down[i], 'gx', behind)  7.92 us
    ppermute x6, waiting for transfers between devices, shards(): up[i] = lax.ppermute(up[i], 'gx', ahead)  4.61 us
    ppermute x6, starting transfers between devices, shards(): down[i] = lax.ppermute(down[i], 'gx', behind)  3.77 us
    ppermute x1, starting transfers between devices, shards(): first = lax.ppermute(passing, 'groups', swap)  3 us
  transfers between devices with their start and end apart: 37, of which 22 were waited for; matrix products, arithmetic and copies ran while one was open for 0% of the time, Pallas kernels for 15%

profile of v27, /device:TPU:0, one launch (start us, length us, event | category | flops | bytes accessed | tf_op | source)
XLA Modules:
  0.0 86.9 jit_solution(667893187453819355)
XLA Ops:
  0.7 3.4 %shard_map.78 = (bf16[2,192,1280]{2,1,0:T(8,128)(2,1)}, bf16[160,640]{1,0:T(8,128)(2,1)}, bf16[160,640]{1,0:T(8,128)(2,1)}) custom-call(s32[8]{0:T(128)} %lengths.3, bf16[384,1280]{1,0:T(8,128)(2,1)} %bitcast.3, bf16[384,1280]{1,0:T(8,128)(2,1)} %bitcast.6, f32[1280]{0:T(1024)} %gain.3, bf16[160,1280]{1,0:T(8,128)(2,1)} %w_up.1, bf16[160,1280]{1,0:T(8,128)(2,1)} %w_down.1), custom_call_target="tpu_custom_call" | custom-call | flops 2457600 | bytes 4183072 | tf_op jit(solution)/shard_map/pallas_call | solution.py:28
  4.1 3.0 %collective-permute-start.14 = (bf16[2,192,1280]{2,1,0:T(8,128)(2,1)}, bf16[2,192,1280]{2,1,0:T(8,128)(2,1)S(1)}, u32[]{:S(2)}, u32[]{:S(2)}) collective-permute-start(bf16[2,192,1280]{2,1,0:T(8,128)(2,1)} %get-tuple-element.45), channel_id=1, source_target_pairs={{0,16},{16,0},{1,17},{17,1},{2,18},{18,2},{3,19},{19,3},{4,20},{20... | collective-permute-start | bytes 2949128 | tf_op jit(solution)/shard_map/ppermute | solution.py:277
  7.1 1.6 %collective-permute-start = (bf16[160,640]{1,0:T(8,128)(2,1)}, bf16[160,640]{1,0:T(8,128)(2,1)S(1)}, u32[]{:S(2)}, u32[]{:S(2)}) collective-permute-start(bf16[160,640]{1,0:T(8,128)(2,1)} %get-tuple-element.40.refs_0_), channel_id=1, source_target_pairs={{0,4},{4,8},{8,12},{12,14},{14,10},{10,6},{6,2},{2,0},{1,5},{5,9},... | collective-permute-start | bytes 614408 | tf_op jit(solution)/shard_map/ppermute | solution.py:291
  12.6 2.6 %collective-permute-done.refs_0_ = bf16[160,640]{1,0:T(8,128)(2,1)S(1)} collective-permute-done((bf16[160,640]{1,0:T(8,128)(2,1)}, bf16[160,640]{1,0:T(8,128)(2,1)S(1)}, u32[]{:S(2)}, u32[]{:S(2)}) %collective-permute-start) | collective-permute-done | bytes 204832 | tf_op jit(solution)/shard_map/ppermute | solution.py:291
  15.3 1.6 %collective-permute-start.4 = (bf16[160,640]{1,0:T(8,128)(2,1)S(1)}, bf16[160,640]{1,0:T(8,128)(2,1)S(1)}, u32[]{:S(2)}, u32[]{:S(2)}) collective-permute-start(bf16[160,640]{1,0:T(8,128)(2,1)S(1)} %shard_map.79.refs_2_), channel_id=1, source_target_pairs={{0,4},{4,8},{8,12},{12,14},{14,10},{10,6},{6,2},{2,0},{1,5},{5,9},... | collective-permute-start | bytes 614408 | tf_op jit(solution)/shard_map/ppermute | solution.py:291
  17.3 3.9 %collective-permute-done.1.refs_3_ = bf16[160,640]{1,0:T(8,128)(2,1)S(1)} collective-permute-done((bf16[160,640]{1,0:T(8,128)(2,1)}, bf16[160,640]{1,0:T(8,128)(2,1)S(1)}, u32[]{:S(2)}, u32[]{:S(2)}) %collective-permute-start.1) | collective-permute-done | bytes 204832 | tf_op jit(solution)/shard_map/ppermute | solution.py:292
  21.7 1.6 %collective-permute-start.6 = (bf16[160,640]{1,0:T(8,128)(2,1)S(1)}, bf16[160,640]{1,0:T(8,128)(2,1)S(1)}, u32[]{:S(2)}, u32[]{:S(2)}) collective-permute-start(bf16[160,640]{1,0:T(8,128)(2,1)S(1)} %collective-permute-done.2.refs_4_), channel_id=1, source_target_pairs={{0,4},{4,8},{8,12},{12,14},{14,10},{10,6},{6,2},{2,0},{1,5},{5,9},... | collective-permute-start | bytes 614408 | tf_op jit(solution)/shard_map/ppermute | solution.py:291
  24.1 1.6 %collective-permute-start.8 = (bf16[160,640]{1,0:T(8,128)(2,1)S(1)}, bf16[160,640]{1,0:T(8,128)(2,1)S(1)}, u32[]{:S(2)}, u32[]{:S(2)}) collective-permute-start(bf16[160,640]{1,0:T(8,128)(2,1)S(1)} %collective-permute-done.4.refs_6_), channel_id=1, source_target_pairs={{0,4},{4,8},{8,12},{12,14},{14,10},{10,6},{6,2},{2,0},{1,5},{5,9},... | collective-permute-start | bytes 614408 | tf_op jit(solution)/shard_map/ppermute | solution.py:291
  26.1 3.9 %collective-permute-done.5.refs_7_ = bf16[160,640]{1,0:T(8,128)(2,1)S(1)} collective-permute-done((bf16[160,640]{1,0:T(8,128)(2,1)S(1)}, bf16[160,640]{1,0:T(8,128)(2,1)S(1)}, u32[]{:S(2)}, u32[]{:S(2)}) %collective-permute-start.5) | collective-permute-done | bytes 204832 | tf_op jit(solution)/shard_map/ppermute | solution.py:292
  30.5 1.6 %collective-permute-start.11 = (bf16[160,640]{1,0:T(8,128)(2,1)S(1)}, bf16[160,640]{1,0:T(8,128)(2,1)S(1)}, u32[]{:S(2)}, u32[]{:S(2)}) collective-permute-start(bf16[160,640]{1,0:T(8,128)(2,1)S(1)} %collective-permute-done.6.refs_8_), channel_id=1, source_target_pairs={{0,4},{4,8},{8,12},{12,14},{14,10},{10,6},{6,2},{2,0},{1,5},{5,9},... | collective-permute-start | bytes 614408 | tf_op jit(solution)/shard_map/ppermute | solution.py:291
  33.3 1.6 %collective-permute-start.12 = (bf16[160,640]{1,0:T(8,128)(2,1)S(1)}, bf16[160,640]{1,0:T(8,128)(2,1)S(1)}, u32[]{:S(2)}, u32[]{:S(2)}) collective-permute-start(bf16[160,640]{1,0:T(8,128)(2,1)S(1)} %collective-permute-done.8.refs_10_), channel_id=1, source_target_pairs={{0,4},{4,8},{8,12},{12,14},{14,10},{10,6},{6,2},{2,0},{1,5},{5,9},... | collective-permute-start | bytes 614408 | tf_op jit(solution)/shard_map/ppermute | solution.py:300
  35.3 3.6 %shard_map.80 = (bf16[1280,640]{1,0:T(8,128)(2,1)S(1)}, bf16[1280,640]{1,0:T(8,128)(2,1)S(1)}) custom-call(bf16[160,640]{1,0:T(8,128)(2,1)S(1)} %copy-done.2, bf16[160,640]{1,0:T(8,128)(2,1)S(1)} %copy-done.3, bf16[160,640]{1,0:T(8,128)(2,1)S(1)} %shard_map.79.refs_2_, bf16[160,640]{1,0:T(8,128)(2,1)S(1)} %collective-permute-done.1.refs_3_, ...), custom_call_target="tpu_custom_call" | custom-call | flops 1 | bytes 5734400 | tf_op jit(solution)/shard_map/pallas_call | solution.py:28
  41.5 3.0 %shard_map.81 = (bf16[384,640]{1,0:T(8,128)(2,1)S(1)}, bf16[1280,640]{1,0:T(8,128)(2,1)S(1)}, bf16[1280,640]{1,0:T(8,128)(2,1)S(1)}, bf16[1280,640]{1,0:T(8,128)...) custom-call(bf16[384,1280]{1,0:T(8,128)(2,1)S(1)} %get-tuple-element.38.refs_1_.normed, ...), custom_call_target="tpu_custom_call" | custom-call | flops 1887436800 | bytes 11878400 | tf_op jit(solution)/shard_map/pallas_call | solution.py:28
  44.5 2.7 %shard_map.83 = (bf16[384,640]{1,0:T(8,128)(2,1)S(1)}, bf16[1280,640]{1,0:T(8,128)(2,1)S(1)}, bf16[160,640]{1,0:T(8,128)(2,1)S(1)}, bf16[160,640]{1,0:T(8,128)(2,1)S(1)}) custom-call(bf16[2,192,1280]{2,1,0:T(8,128)(2,1)S(1)} %shard_map.82.first, bf16[2,192,1280]{2,1,0:T(8,128)(2,1)S(1)} %collective-permute-done.15.second, ...), custom_call_target="tpu_custom_call" | custom-call | flops 1887436800 | bytes 7782400 | tf_op jit(solution)/shard_map/pallas_call | solution.py:28
  47.2 1.6 %collective-permute-start.17 = (bf16[160,640]{1,0:T(8,128)(2,1)S(1)}, bf16[160,640]{1,0:T(8,128)(2,1)S(1)}, u32[]{:S(2)}, u32[]{:S(2)}) collective-permute-start(bf16[160,640]{1,0:T(8,128)(2,1)S(1)} %get-tuple-element.52), channel_id=1, source_target_pairs={{0,4},{4,8},{8,12},{12,14},{14,10},{10,6},{6,2},{2,0},{1,5},{5,9},... | collective-permute-start | bytes 614408 | tf_op jit(solution)/shard_map/ppermute | solution.py:376
  49.3 2.0 %shard_map.84 = (bf16[2,384,640]{2,1,0:T(8,128)(2,1)S(1)}, bf16[384,640]{1,0:T(8,128)(2,1)S(1)}, bf16[128,640]{1,0:T(8,128)(2,1)S(1)}, bf16[128,640]{1,0:T(8,128)(2,1)S(1)}, bf16[128,640]{1,0:T(8,128)(2,1)S(1)}) custom-call(bf16[384,640]{1,0:T(8,128)(2,1)S(1)} %get-tuple-element.44.d_pre_own, bf16[384,640]{1,0:T(8,128)(2,1)S(1)} %get-tuple-element.48.d_pre_other, ...), custom_call_target="tpu_custom_call" | custom-call | flops 1258291200 | bytes 4587520 | tf_op jit(solution)/shard_map/pallas_call | solution.py:28
  51.4 1.6 %collective-permute-start.21 = (bf16[160,640]{1,0:T(8,128)(2,1)S(1)}, bf16[160,640]{1,0:T(8,128)(2,1)S(1)}, u32[]{:S(2)}, u32[]{:S(2)}) collective-permute-start(bf16[160,640]{1,0:T(8,128)(2,1)S(1)} %shard_map.86), channel_id=1, source_target_pairs={{0,4},{4,8},{8,12},{12,14},{14,10},{10,6},{6,2},{2,0},{1,5},{5,9},... | collective-permute-start | bytes 614408 | tf_op jit(solution)/shard_map/ppermute | solution.py:376
  56.4 1.6 %collective-permute-start.19 = (bf16[160,640]{1,0:T(8,128)(2,1)S(1)}, bf16[160,640]{1,0:T(8,128)(2,1)S(1)}, u32[]{:S(2)}, u32[]{:S(2)}) collective-permute-start(bf16[160,640]{1,0:T(8,128)(2,1)S(1)} %get-tuple-element.54.refs_3_), channel_id=1, source_target_pairs={{0,4},{4,8},{8,12},{12,14},{14,10},{10,6},{6,2},{2,0},{1,5},{5,9},... | collective-permute-start | bytes 614408 | tf_op jit(solution)/shard_map/ppermute | solution.py:376
  61.1 1.6 %collective-permute-start.29 = (bf16[160,640]{1,0:T(8,128)(2,1)S(1)}, bf16[160,640]{1,0:T(8,128)(2,1)S(1)}, u32[]{:S(2)}, u32[]{:S(2)}) collective-permute-start(bf16[160,640]{1,0:T(8,128)(2,1)S(1)} %get-tuple-element.59.refs_3_), channel_id=1, source_target_pairs={{0,4},{4,8},{8,12},{12,14},{14,10},{10,6},{6,2},{2,0},{1,5},{5,9},... | collective-permute-start | bytes 614408 | tf_op jit(solution)/shard_map/ppermute | solution.py:376
  66.1 1.6 %collective-permute-start.27 = (bf16[160,640]{1,0:T(8,128)(2,1)S(1)}, bf16[160,640]{1,0:T(8,128)(2,1)S(1)}, u32[]{:S(2)}, u32[]{:S(2)}) collective-permute-start(bf16[160,640]{1,0:T(8,128)(2,1)S(1)} %get-tuple-element.60.refs_2_), channel_id=1, source_target_pairs={{0,4},{4,8},{8,12},{12,14},{14,10},{10,6},{6,2},{2,0},{1,5},{5,9},... | collective-permute-start | bytes 614408 | tf_op jit(solution)/shard_map/ppermute | solution.py:376
  69.1 1.6 %collective-permute-done.30.refs_2_ = bf16[160,640]{1,0:T(8,128)(2,1)S(1)} collective-permute-done((bf16[160,640]{1,0:T(8,128)(2,1)S(1)}, bf16[160,640]{1,0:T(8,128)(2,1)S(1)}, u32[]{:S(2)}, u32[]{:S(2)}) %collective-permute-start.30) | collective-permute-done | bytes 204832 | tf_op jit(solution)/shard_map/ppermute | solution.py:376
  70.8 1.6 %collective-permute-start.32 = (bf16[160,640]{1,0:T(8,128)(2,1)S(1)}, bf16[160,640]{1,0:T(8,128)(2,1)S(1)}, u32[]{:S(2)}, u32[]{:S(2)}) collective-permute-start(bf16[160,640]{1,0:T(8,128)(2,1)S(1)} %get-tuple-element.67.refs_2_), channel_id=1, source_target_pairs={{0,4},{4,8},{8,12},{12,14},{14,10},{10,6},{6,2},{2,0},{1,5},{5,9},... | collective-permute-start | bytes 614408 | tf_op jit(solution)/shard_map/ppermute | solution.py:376
  74.7 2.0 %collective-permute-done.32.refs_1_ = bf16[160,640]{1,0:T(8,128)(2,1)S(1)} collective-permute-done((bf16[160,640]{1,0:T(8,128)(2,1)S(1)}, bf16[160,640]{1,0:T(8,128)(2,1)S(1)}, u32[]{:S(2)}, u32[]{:S(2)}) %collective-permute-start.32) | collective-permute-done | bytes 204832 | tf_op jit(solution)/shard_map/ppermute | solution.py:376
  76.8 1.6 %collective-permute-start.34 = (bf16[160,640]{1,0:T(8,128)(2,1)S(1)}, bf16[160,640]{1,0:T(8,128)(2,1)S(1)}, u32[]{:S(2)}, u32[]{:S(2)}) collective-permute-start(bf16[160,640]{1,0:T(8,128)(2,1)S(1)} %shard_map.93.refs_3_), channel_id=1, source_target_pairs={{0,4},{4,8},{8,12},{12,14},{14,10},{10,6},{6,2},{2,0},{1,5},{5,9},... | collective-permute-start | bytes 614408 | tf_op jit(solution)/shard_map/ppermute | solution.py:376
  (85 shorter events, 33.6 us)
Async XLA Ops:
  4.1 37.4 %collective-permute-start.14 = (bf16[2,192,1280]{2,1,0:T(8,128)(2,1)}, bf16[2,192,1280]{2,1,0:T(8,128)(2,1)S(1)}, u32[]{:S(2)}, u32[]{:S(2)}) collective-permute-start(bf16[2,192,1280]{2,1,0:T(8,128)(2,1)} %get-tuple-element.45), channel_id=1, source_target_pairs={{0,16},{16,0},{1,17},{17,1},{2,18},{18,2},{3,19},{19,3},{4,20},{20... | collective-permute-start | bytes 2949128 | tf_op jit(solution)/shard_map/ppermute | solution.py:277
  7.1 8.2 %collective-permute-start = (bf16[160,640]{1,0:T(8,128)(2,1)}, bf16[160,640]{1,0:T(8,128)(2,1)S(1)}, u32[]{:S(2)}, u32[]{:S(2)}) collective-permute-start(bf16[160,640]{1,0:T(8,128)(2,1)} %get-tuple-element.40.refs_0_), channel_id=1, source_target_pairs={{0,4},{4,8},{8,12},{12,14},{14,10},{10,6},{6,2},{2,0},{1,5},{5,9},... | collective-permute-start | bytes 614408 | tf_op jit(solution)/shard_map/ppermute | solution.py:291
  8.7 8.2 %collective-permute-start.3 = (bf16[160,640]{1,0:T(8,128)(2,1)}, bf16[160,640]{1,0:T(8,128)(2,1)S(1)}, u32[]{:S(2)}, u32[]{:S(2)}) collective-permute-start(bf16[160,640]{1,0:T(8,128)(2,1)} %get-tuple-element.41.refs_1_), channel_id=1, source_target_pairs={{4,0},{8,4},{12,8},{14,12},{10,14},{6,10},{2,6},{0,2},{5,1},{9,5},... | collective-permute-start | bytes 614408 | tf_op jit(solution)/shard_map/ppermute | solution.py:292
  9.1 12.2 %collective-permute-start.1 = (bf16[160,640]{1,0:T(8,128)(2,1)}, bf16[160,640]{1,0:T(8,128)(2,1)S(1)}, u32[]{:S(2)}, u32[]{:S(2)}) collective-permute-start(bf16[160,640]{1,0:T(8,128)(2,1)} %get-tuple-element.40.refs_0_), channel_id=1, source_target_pairs={{4,0},{8,4},{12,8},{14,12},{10,14},{6,10},{2,6},{0,2},{5,1},{9,5},... | collective-permute-start | bytes 614408 | tf_op jit(solution)/shard_map/ppermute | solution.py:292
  10.6 11.1 %collective-permute-start.2 = (bf16[160,640]{1,0:T(8,128)(2,1)}, bf16[160,640]{1,0:T(8,128)(2,1)S(1)}, u32[]{:S(2)}, u32[]{:S(2)}) collective-permute-start(bf16[160,640]{1,0:T(8,128)(2,1)} %get-tuple-element.41.refs_1_), channel_id=1, source_target_pairs={{0,4},{4,8},{8,12},{12,14},{14,10},{10,6},{6,2},{2,0},{1,5},{5,9},... | collective-permute-start | bytes 614408 | tf_op jit(solution)/shard_map/ppermute | solution.py:291
  15.3 8.8 %collective-permute-start.4 = (bf16[160,640]{1,0:T(8,128)(2,1)S(1)}, bf16[160,640]{1,0:T(8,128)(2,1)S(1)}, u32[]{:S(2)}, u32[]{:S(2)}) collective-permute-start(bf16[160,640]{1,0:T(8,128)(2,1)S(1)} %shard_map.79.refs_2_), channel_id=1, source_target_pairs={{0,4},{4,8},{8,12},{12,14},{14,10},{10,6},{6,2},{2,0},{1,5},{5,9},... | collective-permute-start | bytes 614408 | tf_op jit(solution)/shard_map/ppermute | solution.py:291
  16.9 8.8 %collective-permute-start.7 = (bf16[160,640]{1,0:T(8,128)(2,1)S(1)}, bf16[160,640]{1,0:T(8,128)(2,1)S(1)}, u32[]{:S(2)}, u32[]{:S(2)}) collective-permute-start(bf16[160,640]{1,0:T(8,128)(2,1)S(1)} %collective-permute-done.3.refs_5_), channel_id=1, source_target_pairs={{4,0},{8,4},{12,8},{14,12},{10,14},{6,10},{2,6},{0,2},{5,1},{9,5},... | collective-permute-start | bytes 614408 | tf_op jit(solution)/shard_map/ppermute | solution.py:292
  21.3 8.8 %collective-permute-start.5 = (bf16[160,640]{1,0:T(8,128)(2,1)S(1)}, bf16[160,640]{1,0:T(8,128)(2,1)S(1)}, u32[]{:S(2)}, u32[]{:S(2)}) collective-permute-start(bf16[160,640]{1,0:T(8,128)(2,1)S(1)} %collective-permute-done.1.refs_3_), channel_id=1, source_target_pairs={{4,0},{8,4},{12,8},{14,12},{10,14},{6,10},{2,6},{0,2},{5,1},{9,5},... | collective-permute-start | bytes 614408 | tf_op jit(solution)/shard_map/ppermute | solution.py:292
  21.7 8.8 %collective-permute-start.6 = (bf16[160,640]{1,0:T(8,128)(2,1)S(1)}, bf16[160,640]{1,0:T(8,128)(2,1)S(1)}, u32[]{:S(2)}, u32[]{:S(2)}) collective-permute-start(bf16[160,640]{1,0:T(8,128)(2,1)S(1)} %collective-permute-done.2.refs_4_), channel_id=1, source_target_pairs={{0,4},{4,8},{8,12},{12,14},{14,10},{10,6},{6,2},{2,0},{1,5},{5,9},... | collective-permute-start | bytes 614408 | tf_op jit(solution)/shard_map/ppermute | solution.py:291
  24.1 9.2 %collective-permute-start.8 = (bf16[160,640]{1,0:T(8,128)(2,1)S(1)}, bf16[160,640]{1,0:T(8,128)(2,1)S(1)}, u32[]{:S(2)}, u32[]{:S(2)}) collective-permute-start(bf16[160,640]{1,0:T(8,128)(2,1)S(1)} %collective-permute-done.4.refs_6_), channel_id=1, source_target_pairs={{0,4},{4,8},{8,12},{12,14},{14,10},{10,6},{6,2},{2,0},{1,5},{5,9},... | collective-permute-start | bytes 614408 | tf_op jit(solution)/shard_map/ppermute | solution.py:291
  25.7 9.2 %collective-permute-start.9 = (bf16[160,640]{1,0:T(8,128)(2,1)S(1)}, bf16[160,640]{1,0:T(8,128)(2,1)S(1)}, u32[]{:S(2)}, u32[]{:S(2)}) collective-permute-start(bf16[160,640]{1,0:T(8,128)(2,1)S(1)} %collective-permute-done.7.refs_9_), channel_id=1, source_target_pairs={{4,0},{8,4},{12,8},{14,12},{10,14},{6,10},{2,6},{0,2},{5,1},{9,5},... | collective-permute-start | bytes 614408 | tf_op jit(solution)/shard_map/ppermute | solution.py:292
  30.1 8.8 %collective-permute-start.10 = (bf16[160,640]{1,0:T(8,128)(2,1)S(1)}, bf16[160,640]{1,0:T(8,128)(2,1)S(1)}, u32[]{:S(2)}, u32[]{:S(2)}) collective-permute-start(bf16[160,640]{1,0:T(8,128)(2,1)S(1)} %collective-permute-done.5.refs_7_), channel_id=1, source_target_pairs={{4,0},{8,4},{12,8},{14,12},{10,14},{6,10},{2,6},{0,2},{5,1},{9,5},... | collective-permute-start | bytes 614408 | tf_op jit(solution)/shard_map/ppermute | solution.py:292
  30.5 8.4 %collective-permute-start.11 = (bf16[160,640]{1,0:T(8,128)(2,1)S(1)}, bf16[160,640]{1,0:T(8,128)(2,1)S(1)}, u32[]{:S(2)}, u32[]{:S(2)}) collective-permute-start(bf16[160,640]{1,0:T(8,128)(2,1)S(1)} %collective-permute-done.6.refs_8_), channel_id=1, source_target_pairs={{0,4},{4,8},{8,12},{12,14},{14,10},{10,6},{6,2},{2,0},{1,5},{5,9},... | collective-permute-start | bytes 614408 | tf_op jit(solution)/shard_map/ppermute | solution.py:291
  47.2 7.8 %collective-permute-start.17 = (bf16[160,640]{1,0:T(8,128)(2,1)S(1)}, bf16[160,640]{1,0:T(8,128)(2,1)S(1)}, u32[]{:S(2)}, u32[]{:S(2)}) collective-permute-start(bf16[160,640]{1,0:T(8,128)(2,1)S(1)} %get-tuple-element.52), channel_id=1, source_target_pairs={{0,4},{4,8},{8,12},{12,14},{14,10},{10,6},{6,2},{2,0},{1,5},{5,9},... | collective-permute-start | bytes 614408 | tf_op jit(solution)/shard_map/ppermute | solution.py:376
  51.3 16.4 %collective-permute-start.16 = (bf16[384,640]{1,0:T(8,128)(2,1)S(1)}, bf16[384,640]{1,0:T(8,128)(2,1)S(1)}, u32[]{:S(2)}, u32[]{:S(2)}) collective-permute-start(bf16[384,640]{1,0:T(8,128)(2,1)S(1)} %get-tuple-element.50), channel_id=1, source_target_pairs={{0,1},{1,0},{2,3},{3,2},{4,5},{5,4},{6,7},{7,6},{8,9},{9,8},{10,11... | collective-permute-start | bytes 1474568 | tf_op jit(solution)/shard_map/ppermute | solution.py:345
  51.4 8.0 %collective-permute-start.21 = (bf16[160,640]{1,0:T(8,128)(2,1)S(1)}, bf16[160,640]{1,0:T(8,128)(2,1)S(1)}, u32[]{:S(2)}, u32[]{:S(2)}) collective-permute-start(bf16[160,640]{1,0:T(8,128)(2,1)S(1)} %shard_map.86), channel_id=1, source_target_pairs={{0,4},{4,8},{8,12},{12,14},{14,10},{10,6},{6,2},{2,0},{1,5},{5,9},... | collective-permute-start | bytes 614408 | tf_op jit(solution)/shard_map/ppermute | solution.py:376
  53.0 7.9 %collective-permute-start.22 = (bf16[160,640]{1,0:T(8,128)(2,1)S(1)}, bf16[160,640]{1,0:T(8,128)(2,1)S(1)}, u32[]{:S(2)}, u32[]{:S(2)}) collective-permute-start(bf16[160,640]{1,0:T(8,128)(2,1)S(1)} %shard_map.87), channel_id=1, source_target_pairs={{4,0},{8,4},{12,8},{14,12},{10,14},{6,10},{2,6},{0,2},{5,1},{9,5},... | collective-permute-start | bytes 614408 | tf_op jit(solution)/shard_map/ppermute | solution.py:376
  56.4 7.8 %collective-permute-start.19 = (bf16[160,640]{1,0:T(8,128)(2,1)S(1)}, bf16[160,640]{1,0:T(8,128)(2,1)S(1)}, u32[]{:S(2)}, u32[]{:S(2)}) collective-permute-start(bf16[160,640]{1,0:T(8,128)(2,1)S(1)} %get-tuple-element.54.refs_3_), channel_id=1, source_target_pairs={{0,4},{4,8},{8,12},{12,14},{14,10},{10,6},{6,2},{2,0},{1,5},{5,9},... | collective-permute-start | bytes 614408 | tf_op jit(solution)/shard_map/ppermute | solution.py:376
  61.1 8.1 %collective-permute-start.29 = (bf16[160,640]{1,0:T(8,128)(2,1)S(1)}, bf16[160,640]{1,0:T(8,128)(2,1)S(1)}, u32[]{:S(2)}, u32[]{:S(2)}) collective-permute-start(bf16[160,640]{1,0:T(8,128)(2,1)S(1)} %get-tuple-element.59.refs_3_), channel_id=1, source_target_pairs={{0,4},{4,8},{8,12},{12,14},{14,10},{10,6},{6,2},{2,0},{1,5},{5,9},... | collective-permute-start | bytes 614408 | tf_op jit(solution)/shard_map/ppermute | solution.py:376
  62.7 8.0 %collective-permute-start.30 = (bf16[160,640]{1,0:T(8,128)(2,1)S(1)}, bf16[160,640]{1,0:T(8,128)(2,1)S(1)}, u32[]{:S(2)}, u32[]{:S(2)}) collective-permute-start(bf16[160,640]{1,0:T(8,128)(2,1)S(1)} %get-tuple-element.66), channel_id=1, source_target_pairs={{4,0},{8,4},{12,8},{14,12},{10,14},{6,10},{2,6},{0,2},{5,1},{9,5},... | collective-permute-start | bytes 614408 | tf_op jit(solution)/shard_map/ppermute | solution.py:376
  65.6 8.0 %collective-permute-start.28 = (bf16[160,640]{1,0:T(8,128)(2,1)S(1)}, bf16[160,640]{1,0:T(8,128)(2,1)S(1)}, u32[]{:S(2)}, u32[]{:S(2)}) collective-permute-start(bf16[160,640]{1,0:T(8,128)(2,1)S(1)} %get-tuple-element.65), channel_id=1, source_target_pairs={{4,0},{8,4},{12,8},{14,12},{10,14},{6,10},{2,6},{0,2},{5,1},{9,5},... | collective-permute-start | bytes 614408 | tf_op jit(solution)/shard_map/ppermute | solution.py:376
  66.1 8.1 %collective-permute-start.27 = (bf16[160,640]{1,0:T(8,128)(2,1)S(1)}, bf16[160,640]{1,0:T(8,128)(2,1)S(1)}, u32[]{:S(2)}, u32[]{:S(2)}) collective-permute-start(bf16[160,640]{1,0:T(8,128)(2,1)S(1)} %get-tuple-element.60.refs_2_), channel_id=1, source_target_pairs={{0,4},{4,8},{8,12},{12,14},{14,10},{10,6},{6,2},{2,0},{1,5},{5,9},... | collective-permute-start | bytes 614408 | tf_op jit(solution)/shard_map/ppermute | solution.py:376
  67.8 14.3 %collective-permute-start.23 = (bf16[384,640]{1,0:T(8,128)(2,1)S(1)}, bf16[384,640]{1,0:T(8,128)(2,1)S(1)}, u32[]{:S(2)}, u32[]{:S(2)}) collective-permute-start(bf16[384,640]{1,0:T(8,128)(2,1)S(1)} %shard_map.90.refs_3_), channel_id=1, source_target_pairs={{0,16},{16,0},{1,17},{17,1},{2,18},{18,2},{3,19},{19,3},{4,20},{20... | collective-permute-start | bytes 1474568 | tf_op jit(solution)/shard_map/ppermute | solution.py:349
  76.8 8.5 %collective-permute-start.34 = (bf16[160,640]{1,0:T(8,128)(2,1)S(1)}, bf16[160,640]{1,0:T(8,128)(2,1)S(1)}, u32[]{:S(2)}, u32[]{:S(2)}) collective-permute-start(bf16[160,640]{1,0:T(8,128)(2,1)S(1)} %shard_map.93.refs_3_), channel_id=1, source_target_pairs={{0,4},{4,8},{8,12},{12,14},{14,10},{10,6},{6,2},{2,0},{1,5},{5,9},... | collective-permute-start | bytes 614408 | tf_op jit(solution)/shard_map/ppermute | solution.py:376
  (19 other events, 163.8 us)
